TPU v7x, 32 devices: a whole 2x2x4 slice. The times are simulated.
32 devices in a mesh: groups: 2 (over y), tok: 4 (over z), ch: 2 (over x), sub: 2 (over core).
Axes of the slice: x: 2, y: 2, z: 4, core: 2. Of those that a mesh axis runs over, the one named last changes fastest.
Arguments:
- weather: float32 [128, 128, 128], P('groups', 'tok', ('ch', 'sub')), parts along dimension 0, may hold values from -6 to 6
- conv_first: float32 [9, 64, 64], replicated, may hold values from -0.25 to 0.25
- conv_second: float32 [9, 64, 64], replicated, may hold values from -0.25 to 0.25
- patch_embed: bfloat16 [256, 384], replicated, may hold values from -0.375 to 0.375
- token_mixing: bfloat16 [4096, 16384], P('tok', ('ch', 'sub')), may hold values from -0.09375 to 0.09375
Outputs:
- lifted: bfloat16 [768, 16384], P(('groups', 'tok'), ('ch', 'sub')), parts along dimension 0
There are 2 independent parts, one for each index of `groups`. A program takes and returns all parts, laid end to end along the dimension named above; an argument that names none is the same for every part. Nothing has to cross between parts.
All inputs are finite; a program needn't handle non-finite values.
Results may differ from a plain program's by a relative error of at most 0.0058.
Values may be sent and summed in bfloat16 or wider, within the bound.
No kernel may reach another device: no remote copies, remote signals or barrier semaphores. Data moves between devices by JAX's collectives and lax.ppermute only.
A program may use at most 64 MiB of HBM per device.

v0:
```python
import jax
import jax.numpy as jnp
from jax import lax
from jax.sharding import PartitionSpec as P


def padded_2(block, sides, width, periodic):
    for axis, dim in sides:
        count = lax.axis_size(axis)
        forward = [(i, i + 1) for i in range(count - 1)]
        if periodic:
            forward.append((count - 1, 0))
        backward = [(target, source) for source, target in forward]
        low = lax.ppermute(
            lax.slice_in_dim(block, block.shape[dim] - width, None, axis=dim), axis, forward
        )
        high = lax.ppermute(lax.slice_in_dim(block, 0, width, axis=dim), axis, backward)
        block = jnp.concatenate([low, block, high], axis=dim)
    return block


def valid_conv(padded, kernel):
    width_lon = padded.shape[1] - 2
    width_lat = padded.shape[2] - 2
    stacked = jnp.stack(
        [
            padded[:, row_shift : row_shift + width_lon, col_shift : col_shift + width_lat]
            for row_shift in range(3)
            for col_shift in range(3)
        ],
        0,
    )
    return jnp.einsum("toi,tixy->oxy", kernel, stacked, precision=lax.Precision.HIGHEST)


def embed_patches(field_in, patch_embed):
    chans, width_lon, width_lat = field_in.shape
    blocks = field_in.reshape(chans, width_lon // 2, 2, width_lat // 2, 2)
    embed_four = patch_embed.reshape(chans, 2, 2, patch_embed.shape[1])
    return jnp.einsum(
        "cpaqb,cabo->pqo", blocks, embed_four, preferred_element_type=jnp.float32
    ).astype(jnp.bfloat16)


def local(weather, conv_first, conv_second, patch_embed, token_mixing):
    widened = padded_2(weather, (("tok", 1),), 2, True)
    padded = padded_2(widened, ((("ch", "sub"), 2),), 2, False)
    hidden_one = jax.nn.gelu(valid_conv(padded, conv_first), approximate=False)
    width_lat = weather.shape[2]
    lat_index = (
        jnp.arange(width_lat + 2, dtype=jnp.int32) - 1 + lax.axis_index(("ch", "sub")) * width_lat
    )
    inside = (lat_index >= 0) & (lat_index < width_lat * lax.axis_size(("ch", "sub")))
    hidden_one = jnp.where(inside[None, None, :], hidden_one, jnp.float32(0.0))
    field_two = valid_conv(hidden_one, conv_second)
    field_two = field_two.astype(jnp.bfloat16)
    local_tokens = embed_patches(field_two, patch_embed)
    gathered = lax.all_gather(local_tokens, ("ch", "sub"), axis=1, tiled=True)
    tokens = gathered.reshape(-1, gathered.shape[2])
    summed = lax.psum_scatter(
        lax.dot_general(
            tokens, token_mixing, (((0,), (0,)), ((), ())), preferred_element_type=jnp.float32
        ),
        "tok",
        scatter_dimension=0,
        tiled=True,
    )
    return jax.nn.gelu(summed, approximate=False).astype(jnp.bfloat16)


def solution(mesh):
    placed = (P("groups", "tok", ("ch", "sub")), P(), P(), P(), P("tok", ("ch", "sub")))
    return jax.shard_map(
        local,
        mesh=mesh,
        in_specs=placed,
        out_specs=P(("groups", "tok"), ("ch", "sub")),
        check_vma=False,
    )
```

profile of v0, /device:TPU:0, one launch (start us, length us, event | category | flops | bytes accessed | tf_op | source)
XLA Modules:
  0.0 174.0 jit_solution(14999862905189932922)
XLA Ops:
  6.5 0.0 copy-start
  6.5 0.0 reduce-scatter.2.cloned.1.call-start
  6.5 0.8 fusion.64
  7.4 3.0 %collective-permute-start = (f32[64,2,32]{0,2,1:T(8,128)S(1)}, f32[64,2,32]{0,2,1:T(8,128)S(1)}, u32[]{:S(2)}, u32[]{:S(2)}) collective-permute-start(f32[64,2,32]{0,2,1:T(8,128)S(1)} %get-tuple-element.8), channel_id=1, source_target_pairs={{0,4},{4,8},{8,12},{12,0},{1,5},{5,9},{9,13},{13,1},{2,6},{6,10},{... | collective-permute-start | bytes 49160 | tf_op jit(solution)/shard_map/ppermute | solution.py:14
  10.4 2.1 %collective-permute-start.1 = (f32[64,2,32]{0,2,1:T(8,128)S(1)}, f32[64,2,32]{0,2,1:T(8,128)S(1)}, u32[]{:S(2)}, u32[]{:S(2)}) collective-permute-start(f32[64,2,32]{0,2,1:T(8,128)S(1)} %get-tuple-element.7), channel_id=1, source_target_pairs={{4,0},{8,4},{12,8},{0,12},{5,1},{9,5},{13,9},{1,13},{6,2},{10,6},{... | collective-permute-start | bytes 49160 | tf_op jit(solution)/shard_map/ppermute | solution.py:17
  12.5 1.9 %collective-permute-done = f32[64,2,32]{0,2,1:T(8,128)S(1)} collective-permute-done((f32[64,2,32]{0,2,1:T(8,128)S(1)}, f32[64,2,32]{0,2,1:T(8,128)S(1)}, u32[]{:S(2)}, u32[]{:S(2)}) %collective-permute-start) | collective-permute-done | bytes 16416 | tf_op jit(solution)/shard_map/ppermute | solution.py:14
  14.4 1.1 constant_dynamic-update-slice_fusion.1
  15.5 0.0 collective-permute-done.1
  15.6 1.3 collective-permute-start.2
  16.9 0.0 copy-done.2
  16.9 0.1 reshape.18
  17.0 1.3 collective-permute-start.3
  18.3 0.0 collective-permute-done.2
  18.3 0.1 fusion.23
  18.4 3.6 %collective-permute-done.3 = f32[64,36,2]{0,2,1:T(2,128)S(1)} collective-permute-done((f32[64,36,2]{0,2,1:T(2,128)S(1)}, f32[64,36,2]{0,2,1:T(2,128)S(1)}, u32[]{:S(2)}, u32[]{:S(2)}) %collective-permute-start.3) | collective-permute-done | bytes 18464 | tf_op jit(solution)/shard_map/ppermute | solution.py:17
  22.0 0.1 pad_maximum_fusion
  22.1 0.1 fusion.33
  22.2 0.1 fusion.17
  22.3 0.1 fusion.20
  22.4 0.1 fusion.32
  22.4 0.1 fusion.14
  22.5 0.1 fusion.31
  22.6 0.1 fusion.29
  22.6 0.1 fusion.28
  22.7 0.0 copy-done
  22.7 6.9 %fusion.26 = f32[64,34,34]{0,2,1:T(8,128)S(1)} fusion(f32[9,64,34,34]{1,3,0,2:T(8,128)S(1)} %fusion.28, pred[34]{0:T(512)(128)(4,1)S(1)} %compare_and_fusion, f32[9,64,64]{2,1,0:T(8,128)S(1)} %copy-done), kind=kOutput, calls=%fused_computation.48 | convolution fusion | flops 516186368 | bytes 3106850 | tf_op jit(solution)/shard_map/toi,tixy->oxy/dot_general | solution.py:33
  29.6 0.1 fusion.57
  29.6 0.0 slice-start
  29.7 0.1 fusion.56
  29.7 0.1 fusion.55
  29.8 0.1 fusion.54
  29.9 0.1 fusion.53
  29.9 0.1 fusion.52
  30.0 0.0 copy-start.1
  30.0 0.1 fusion.51
  30.1 0.1 fusion.50
  30.2 0.0 slice-start.1
  30.2 0.1 fusion.49
  30.2 0.9 copy-done.1
  31.2 3.9 %fusion.10 = bf16[32,32,64]{2,1,0:T(8,128)(2,1)S(1)} fusion(f32[9,64,32,32]{1,3,2,0:T(8,128)S(1)} %fusion.49, f32[9,64,64]{2,1,0:T(8,128)S(1)} %copy-done.1), kind=kOutput, calls=%fused_computation.21 | convolution fusion | flops 453050368 | bytes 2637824 | tf_op jit(solution)/shard_map/toi,tixy->oxy/dot_general | solution.py:33
  35.1 0.4 fusion.11
  35.5 9.5 %all_gather.3 = bf16[16,64,384]{2,1,0:T(8,128)(2,1)S(1)} all-gather(bf16[16,16,384]{2,1,0:T(8,128)(2,1)S(1)} %fusion.11), channel_id=1, replica_groups=mesh['groups'=2,'tok'=4,'ch'=2,'sub'=2] {'ch','sub'}, dimensions={1}, use_global_device_ids=true | all-gather | bytes 983040 | tf_op jit(solution)/shard_map/all_gather | solution.py:58
  45.1 0.0 slice-done
  45.1 0.0 slice-done.1
  45.1 5.3 %fusion.65 = f32[384,4096]{1,0:T(8,128)} fusion(bf16[1024,384]{1,0:T(8,128)(2,1)S(1)} %bitcast.187, bf16[1024,4096]{1,0:T(8,128)(2,1)S(1)} %bitcast.186), kind=kOutput, calls=%fused_computation.110 | convolution fusion | flops 3221225472 | bytes 15466496 | tf_op jit(solution)/shard_map/dot_general | solution.py:61
  50.4 0.0 reduce-scatter.2.cloned.1.call-update
  50.4 111.5 %reduce-scatter.2.cloned.1.call-done = f32[96,4096]{1,0:T(8,128)} async-done(((f32[384,4096]{1,0:T(8,128)}), f32[96,4096]{1,0:T(8,128)}) %reduce-scatter.2.cloned.1.call-update) | async-done | bytes 1572880 | tf_op jit(solution)/shard_map/reduce_scatter | solution.py:60
  161.9 5.2 %fusion.2 = bf16[96,4096]{1,0:T(8,128)(2,1)} fusion(f32[96,4096]{1,0:T(8,128)} %reduce-scatter.2.cloned.1.call-done), kind=kLoop, calls=%fused_computation.3 | loop fusion | flops 25559040 | bytes 2359296 | tf_op jit(solution)/shard_map/convert_element_type | solution.py:68
  (6 shorter events, 0.0 us)
Async XLA Ops:
  6.5 16.2 %copy-start = (f32[9,64,64]{2,1,0:T(8,128)S(1)}, f32[9,64,64]{2,1,0:T(8,128)}, u32[]{:S(2)}) copy-start(f32[9,64,64]{2,1,0:T(8,128)} %param.6) | copy-start | bytes 442372
  6.5 10.3 %copy-start.2 = (bf16[256,384]{1,0:T(8,128)(2,1)S(1)}, bf16[256,384]{1,0:T(8,128)(2,1)}, u32[]{:S(2)}) copy-start(bf16[256,384]{1,0:T(8,128)(2,1)} %param.8) | copy-start | bytes 589828
  6.5 155.4 %reduce-scatter.2.cloned.1.call-start = ((), (), s32[]{:S(2)}) async-start(), calls=%async_computation.1 | async-start | bytes 7864320 | tf_op jit(solution)/shard_map/reduce_scatter | solution.py:60
  7.4 7.0 %collective-permute-start = (f32[64,2,32]{0,2,1:T(8,128)S(1)}, f32[64,2,32]{0,2,1:T(8,128)S(1)}, u32[]{:S(2)}, u32[]{:S(2)}) collective-permute-start(f32[64,2,32]{0,2,1:T(8,128)S(1)} %get-tuple-element.8), channel_id=1, source_target_pairs={{0,4},{4,8},{8,12},{12,0},{1,5},{5,9},{9,13},{13,1},{2,6},{6,10},{... | collective-permute-start | bytes 49160 | tf_op jit(solution)/shard_map/ppermute | solution.py:14
  10.4 5.1 %collective-permute-start.1 = (f32[64,2,32]{0,2,1:T(8,128)S(1)}, f32[64,2,32]{0,2,1:T(8,128)S(1)}, u32[]{:S(2)}, u32[]{:S(2)}) collective-permute-start(f32[64,2,32]{0,2,1:T(8,128)S(1)} %get-tuple-element.7), channel_id=1, source_target_pairs={{4,0},{8,4},{12,8},{0,12},{5,1},{9,5},{13,9},{1,13},{6,2},{10,6},{... | collective-permute-start | bytes 49160 | tf_op jit(solution)/shard_map/ppermute | solution.py:17
  15.6 2.7 %collective-permute-start.2 = (f32[64,36,2]{0,2,1:T(2,128)S(1)}, f32[64,36,2]{0,2,1:T(2,128)S(1)}, u32[]{:S(2)}, u32[]{:S(2)}) collective-permute-start(f32[64,36,2]{0,2,1:T(2,128)S(1)} %get-tuple-element.6), channel_id=1, source_target_pairs={{0,1},{1,2},{2,3},{4,5},{5,6},{6,7},{8,9},{9,10},{10,11},{12,13},{... | collective-permute-start | bytes 55304 | tf_op jit(solution)/shard_map/ppermute | solution.py:14
  17.0 5.1 %collective-permute-start.3 = (f32[64,36,2]{0,2,1:T(2,128)S(1)}, f32[64,36,2]{0,2,1:T(2,128)S(1)}, u32[]{:S(2)}, u32[]{:S(2)}) collective-permute-start(f32[64,36,2]{0,2,1:T(2,128)S(1)} %get-tuple-element.5), channel_id=1, source_target_pairs={{1,0},{2,1},{3,2},{5,4},{6,5},{7,6},{9,8},{10,9},{11,10},{13,12},{... | collective-permute-start | bytes 55304 | tf_op jit(solution)/shard_map/ppermute | solution.py:17
  29.6 15.4 %slice-start = ((s8[8388608]{0:T(1024)(128)(4,1)}), s8[4194304]{0:T(1024)(128)(4,1)S(1)}, s32[]{:S(2)}) async-start(s8[8388608]{0:T(1024)(128)(4,1)} %bitcast.185), calls=%async_computation.2 | async-start | bytes 8388608
  30.0 1.1 copy-start.1
  30.2 14.9 %slice-start.1 = ((s8[8388608]{0:T(1024)(128)(4,1)}), s8[4194304]{0:T(1024)(128)(4,1)S(1)}, s32[]{:S(2)}) async-start(s8[8388608]{0:T(1024)(128)(4,1)} %bitcast.185), calls=%async_computation.3 | async-start | bytes 8388608
Sparse Core Ops, SparseCore 0:
  50.6 111.3 reduce-scatter.1
where the time goes:
time: 174 us
  waiting for transfers between devices  117 us (67%)
  matrix products  16.6 us (10%)
  between operations  13.7 us (8%)
  blocking collectives  9.54 us (5%)
  starting transfers between devices  7.69 us (4%)
  other arithmetic  5.78 us (3%)
  local copies, waits for them, and re-layouts  3.67 us (2%)
    reduce_scatter x1, waiting for transfers between devices, local(): lax.psum_scatter(lax.dot_general(tokens, token_mixing, (((0,), (0,)), (()...  111 us
    dot_general x2, matrix products, valid_conv(): jnp.einsum('toi,tixy->oxy', kernel, stacked, precision=lax.Precision.HIGH...  10.8 us
    all_gather x1, blocking collectives, local(): gathered = lax.all_gather(local_tokens, ('ch', 'sub'), axis=1, tiled=True)  9.54 us
    dot_general x1, matrix products, local(): lax.dot_general(tokens, token_mixing, (((0,), (0,)), ((), ())), preferred...  5.32 us
    convert_element_type x1, other arithmetic, local(): return jax.nn.gelu(summed, approximate=False).astype(jnp.bfloat16)  5.23 us
    ppermute x2, starting transfers between devices, padded_2(): lax.ppermute(lax.slice_in_dim(block, block.shape[dim] - width, None, axis...  4.32 us
    ppermute x2, waiting for transfers between devices, padded_2(): lax.ppermute(lax.slice_in_dim(block, 0, width, axis=dim), axis, backward)  3.65 us
  transfers between devices with their start and end apart: 5, of which 3 were waited for; matrix products, arithmetic and copies ran while one was open for 1% of the time, Pallas kernels for 0%

commit v1 on v0

--- a/solution.py
+++ b/solution.py
@@ -42,7 +42,39 @@
     ).astype(jnp.bfloat16)
 
 
+def lift(tokens, token_mixing, pieces):
+    count = lax.axis_size("tok")
+    rows = tokens.shape[1] // count
+    width = token_mixing.shape[1] // pieces
+    down = [(i, (i - 1) % count) for i in range(count)]
+    partials = []
+    for piece in range(pieces):
+        partials.append(
+            lax.dot_general(
+                tokens,
+                token_mixing[:, piece * width : (piece + 1) * width],
+                (((0,), (0,)), ((), ())),
+                preferred_element_type=jnp.float32,
+            )
+        )
+    travelling = [part[:rows].astype(jnp.bfloat16) for part in partials]
+    for step in range(1, count):
+        for piece in range(pieces):
+            arrived = lax.ppermute(travelling[piece], "tok", down).astype(jnp.float32)
+            summed = arrived + partials[piece][step * rows : (step + 1) * rows]
+            if step == count - 1:
+                summed = jax.nn.gelu(summed, approximate=False)
+            travelling[piece] = summed.astype(jnp.bfloat16)
+    return jnp.concatenate(travelling, axis=1)
+
+
 def local(weather, conv_first, conv_second, patch_embed, token_mixing):
+    count = lax.axis_size("tok")
+    rows = patch_embed.shape[1] // count
+    turn = ((lax.axis_index("tok") + 1) % count) * rows
+    rolled = lax.dynamic_slice_in_dim(
+        jnp.concatenate([patch_embed, patch_embed], axis=1), turn, patch_embed.shape[1], axis=1
+    )
     widened = padded_2(weather, (("tok", 1),), 2, True)
     padded = padded_2(widened, ((("ch", "sub"), 2),), 2, False)
     hidden_one = jax.nn.gelu(valid_conv(padded, conv_first), approximate=False)
@@ -54,18 +86,10 @@
     hidden_one = jnp.where(inside[None, None, :], hidden_one, jnp.float32(0.0))
     field_two = valid_conv(hidden_one, conv_second)
     field_two = field_two.astype(jnp.bfloat16)
-    local_tokens = embed_patches(field_two, patch_embed)
+    local_tokens = embed_patches(field_two, rolled)
     gathered = lax.all_gather(local_tokens, ("ch", "sub"), axis=1, tiled=True)
     tokens = gathered.reshape(-1, gathered.shape[2])
-    summed = lax.psum_scatter(
-        lax.dot_general(
-            tokens, token_mixing, (((0,), (0,)), ((), ())), preferred_element_type=jnp.float32
-        ),
-        "tok",
-        scatter_dimension=0,
-        tiled=True,
-    )
-    return jax.nn.gelu(summed, approximate=False).astype(jnp.bfloat16)
+    return lift(tokens, token_mixing, 4)
 
 
 def solution(mesh):

time: 174 us -> 96.5 us (0.55)
  waiting for transfers between devices: 117 us -> 15.2 us
  starting transfers between devices: 7.69 us -> 46.3 us
  between operations: 13.7 us -> 0.39 us
    reduce_scatter x1 -> x0, waiting for transfers between devices: 111 us -> none  [local(): lax.psum_scatter(lax.dot_general(tokens, token_mixing, (((0,), (0,)), (()...]
    ppermute x0 -> x12, starting transfers between devices: none -> 38.6 us  [lift(): arrived = lax.ppermute(travelling[piece], 'tok', down).astype(jnp.float32)]
    ppermute x0 -> x12, waiting for transfers between devices: none -> 10.8 us  [lift(): arrived = lax.ppermute(travelling[piece], 'tok', down).astype(jnp.float32)]
    concatenate x0 -> x2, other arithmetic: none -> 2.06 us  [the longest x1 1.12 us: local(): jnp.concatenate([patch_embed, patch_embed], axis=1)]
    convert_element_type x1 -> x12, other arithmetic: 5.23 us -> 3.86 us  [lift(): travelling[piece] = summed.astype(jnp.bfloat16)]
    dot_general x1 -> x4, matrix products: 5.32 us -> 4.06 us  [lift(): lax.dot_general(tokens, token_mixing[:, piece * width:(piece + 1) * width...]
  transfers between devices with their start and end apart: 5 -> 16, of which waited for: 3 -> 6; matrix products, arithmetic and copies ran while one was open for 1% -> 7% of each run, Pallas kernels for 0% -> 0%
where the time goes in v1:
time: 96.5 us; the launch traced here: 96.3 us
  starting transfers between devices  46.3 us (48%)
  waiting for transfers between devices  15.2 us (16%)
  matrix products  15.2 us (16%)
  blocking collectives  9.54 us (10%)
  other arithmetic  6.46 us (7%)
  local copies, waits for them, and re-layouts  3.15 us (3%)
    ppermute x12, starting transfers between devices, lift(): arrived = lax.ppermute(travelling[piece], 'tok', down).astype(jnp.float32)  38.6 us
    ppermute x12, waiting for transfers between devices, lift(): arrived = lax.ppermute(travelling[piece], 'tok', down).astype(jnp.float32)  10.8 us
    dot_general x2, matrix products, valid_conv(): jnp.einsum('toi,tixy->oxy', kernel, stacked, precision=lax.Precision.HIGH...  10.7 us
    all_gather x1, blocking collectives, local(): gathered = lax.all_gather(local_tokens, ('ch', 'sub'), axis=1, tiled=True)  9.54 us
    ppermute x2, starting transfers between devices, padded_2(): lax.ppermute(lax.slice_in_dim(block, block.shape[dim] - width, None, axis...  4.32 us
    dot_general x4, matrix products, lift(): lax.dot_general(tokens, token_mixing[:, piece * width:(piece + 1) * width...  4.06 us
    convert_element_type x12, other arithmetic, lift(): travelling[piece] = summed.astype(jnp.bfloat16)  3.86 us
    ppermute x2, waiting for transfers between devices, padded_2(): lax.ppermute(lax.slice_in_dim(block, 0, width, axis=dim), axis, backward)  3.65 us
  transfers between devices with their start and end apart: 16, of which 6 were waited for; matrix products, arithmetic and copies ran while one was open for 7% of the time, Pallas kernels for 0%

profile of v1, /device:TPU:0, one launch (start us, length us, event | category | flops | bytes accessed | tf_op | source)
XLA Modules:
  0.0 96.3 jit_solution(10206521769113980332)
XLA Ops:
  0.0 0.8 fusion.111
  0.8 3.0 %collective-permute-start = (f32[64,2,32]{0,2,1:T(8,128)S(1)}, f32[64,2,32]{0,2,1:T(8,128)S(1)}, u32[]{:S(2)}, u32[]{:S(2)}) collective-permute-start(f32[64,2,32]{0,2,1:T(8,128)S(1)} %get-tuple-element.8), channel_id=1, source_target_pairs={{0,4},{4,8},{8,12},{12,0},{1,5},{5,9},{9,13},{13,1},{2,6},{6,10},{... | collective-permute-start | bytes 49160 | tf_op jit(solution)/shard_map/ppermute | solution.py:14
  3.9 2.1 %collective-permute-start.1 = (f32[64,2,32]{0,2,1:T(8,128)S(1)}, f32[64,2,32]{0,2,1:T(8,128)S(1)}, u32[]{:S(2)}, u32[]{:S(2)}) collective-permute-start(f32[64,2,32]{0,2,1:T(8,128)S(1)} %get-tuple-element.7), channel_id=1, source_target_pairs={{4,0},{8,4},{12,8},{0,12},{5,1},{9,5},{13,9},{1,13},{6,2},{10,6},{... | collective-permute-start | bytes 49160 | tf_op jit(solution)/shard_map/ppermute | solution.py:17
  5.9 1.1 %fusion.107 = bf16[256,384]{1,0:T(8,128)(2,1)S(1)} fusion(s32[]{:T(128)S(6)} %select_n.16, bf16[256,384]{1,0:T(8,128)(2,1)} %param.8), kind=kLoop, calls=%fused_computation.194 | loop fusion | flops 393216 | bytes 393220 | tf_op jit(solution)/shard_map/concatenate | solution.py:76
  7.1 0.8 collective-permute-done
  7.9 1.1 %constant_dynamic-update-slice_fusion.1 = f32[64,36,32]{0,2,1:T(8,128)S(1)} fusion(f32[64,36,32]{0,2,1:T(8,128)S(1)} %constant_dynamic-update-slice_fusion.2, f32[64,32,32]{0,2,1:T(8,128)} %param.5), kind=kLoop, calls=%fused_computation.198 | loop fusion | bytes 786432
  9.0 1.3 %collective-permute-start.2 = (f32[64,36,2]{0,2,1:T(2,128)S(1)}, f32[64,36,2]{0,2,1:T(2,128)S(1)}, u32[]{:S(2)}, u32[]{:S(2)}) collective-permute-start(f32[64,36,2]{0,2,1:T(2,128)S(1)} %get-tuple-element.6), channel_id=1, source_target_pairs={{0,1},{1,2},{2,3},{4,5},{5,6},{6,7},{8,9},{9,10},{10,11},{12,13},{... | collective-permute-start | bytes 55304 | tf_op jit(solution)/shard_map/ppermute | solution.py:14
  10.3 0.1 reshape.18
  10.4 1.3 %collective-permute-start.3 = (f32[64,36,2]{0,2,1:T(2,128)S(1)}, f32[64,36,2]{0,2,1:T(2,128)S(1)}, u32[]{:S(2)}, u32[]{:S(2)}) collective-permute-start(f32[64,36,2]{0,2,1:T(2,128)S(1)} %get-tuple-element.5), channel_id=1, source_target_pairs={{1,0},{2,1},{3,2},{5,4},{6,5},{7,6},{9,8},{10,9},{11,10},{13,12},{... | collective-permute-start | bytes 55304 | tf_op jit(solution)/shard_map/ppermute | solution.py:17
  11.7 0.1 fusion.21
  11.8 3.6 %collective-permute-done.3 = f32[64,36,2]{0,2,1:T(2,128)S(1)} collective-permute-done((f32[64,36,2]{0,2,1:T(2,128)S(1)}, f32[64,36,2]{0,2,1:T(2,128)S(1)}, u32[]{:S(2)}, u32[]{:S(2)}) %collective-permute-start.3) | collective-permute-done | bytes 18464 | tf_op jit(solution)/shard_map/ppermute | solution.py:17
  15.5 0.1 pad_maximum_fusion.1
  15.7 0.1 fusion.18
  15.9 0.1 fusion.29
  16.2 6.9 %fusion.24 = f32[64,34,34]{0,2,1:T(8,128)S(1)} fusion(f32[9,64,34,34]{1,3,0,2:T(8,128)S(1)} %fusion.26, pred[34]{0:T(512)(128)(4,1)S(1)} %compare_and_fusion, f32[9,64,64]{2,1,0:T(8,128)S(1)} %copy-done), kind=kOutput, calls=%fused_computation.38 | convolution fusion | flops 516186368 | bytes 3106850 | tf_op jit(solution)/shard_map/toi,tixy->oxy/dot_general | solution.py:33
  23.2 0.1 fusion.53
  23.3 0.1 fusion.51
  23.4 0.1 fusion.50
  23.5 0.1 fusion.48
  23.6 0.1 fusion.47
  23.7 0.3 copy-done.1
  24.0 3.9 %fusion.8 = bf16[32,32,64]{2,1,0:T(8,128)(2,1)S(1)} fusion(f32[9,64,32,32]{1,3,2,0:T(8,128)S(1)} %fusion.47, f32[9,64,64]{2,1,0:T(8,128)S(1)} %copy-done.1), kind=kOutput, calls=%fused_computation.10 | convolution fusion | flops 453050368 | bytes 2637824 | tf_op jit(solution)/shard_map/toi,tixy->oxy/dot_general | solution.py:33
  27.9 0.4 fusion.9
  28.3 9.5 %all_gather.3 = bf16[16,64,384]{2,1,0:T(8,128)(2,1)S(1)} all-gather(bf16[16,16,384]{2,1,0:T(8,128)(2,1)S(1)} %fusion.9), channel_id=1, replica_groups=mesh['groups'=2,'tok'=4,'ch'=2,'sub'=2] {'ch','sub'}, dimensions={1}, use_global_device_ids=true | all-gather | bytes 983040 | tf_op jit(solution)/shard_map/all_gather | solution.py:90
  37.9 1.0 %fusion.6 = f32[384,1024]{1,0:T(8,128)S(1)} fusion(bf16[1024,384]{1,0:T(8,128)(2,1)S(1)} %bitcast.187, bf16[1024,4096]{1,0:T(8,128)(2,1)S(1)} %bitcast.192), kind=kOutput, calls=%fused_computation.6 | convolution fusion | flops 805306368 | bytes 4456448 | tf_op jit(solution)/shard_map/dot_general | solution.py:53
  38.9 1.0 %fusion.4 = f32[384,1024]{1,0:T(8,128)S(1)} fusion(bf16[1024,384]{1,0:T(8,128)(2,1)S(1)} %bitcast.188, bf16[1024,4096]{1,0:T(8,128)(2,1)S(1)} %bitcast.192), kind=kOutput, calls=%fused_computation.4 | convolution fusion | flops 805306368 | bytes 4456448 | tf_op jit(solution)/shard_map/dot_general | solution.py:53
  39.9 1.0 %fusion.2 = f32[384,1024]{1,0:T(8,128)S(1)} fusion(bf16[1024,384]{1,0:T(8,128)(2,1)S(1)} %bitcast.189, bf16[1024,4096]{1,0:T(8,128)(2,1)S(1)} %bitcast.192), kind=kOutput, calls=%fused_computation.2 | convolution fusion | flops 805306368 | bytes 4456448 | tf_op jit(solution)/shard_map/dot_general | solution.py:53
  41.0 2.7 %collective-permute-start.4 = (bf16[96,1024]{1,0:T(8,128)(2,1)S(1)}, bf16[96,1024]{1,0:T(8,128)(2,1)S(1)}, u32[]{:S(2)}, u32[]{:S(2)}) collective-permute-start(bf16[96,1024]{1,0:T(8,128)(2,1)S(1)} %slice.343), channel_id=1, source_target_pairs={{0,12},{4,0},{8,4},{12,8},{1,13},{5,1},{9,5},{13,9},{2,14},{6,2},{... | collective-permute-start | bytes 589832 | tf_op jit(solution)/shard_map/ppermute | solution.py:63
  43.8 0.5 collective-permute-start.10
  44.2 1.0 %fusion = f32[384,1024]{1,0:T(8,128)S(1)} fusion(bf16[1024,384]{1,0:T(8,128)(2,1)S(1)} %bitcast.190, bf16[1024,4096]{1,0:T(8,128)(2,1)S(1)} %bitcast.192), kind=kOutput, calls=%fused_computation | convolution fusion | flops 805306368 | bytes 4456448 | tf_op jit(solution)/shard_map/dot_general | solution.py:53
  45.3 1.9 %collective-permute-start.13 = (bf16[96,1024]{1,0:T(8,128)(2,1)S(1)}, bf16[96,1024]{1,0:T(8,128)(2,1)S(1)}, u32[]{:S(2)}, u32[]{:S(2)}) collective-permute-start(bf16[96,1024]{1,0:T(8,128)(2,1)S(1)} %slice.340), channel_id=1, source_target_pairs={{0,12},{4,0},{8,4},{12,8},{1,13},{5,1},{9,5},{13,9},{2,14},{6,2},{... | collective-permute-start | bytes 589832 | tf_op jit(solution)/shard_map/ppermute | solution.py:63
  47.2 1.7 %collective-permute-done.4 = bf16[96,1024]{1,0:T(8,128)(2,1)S(1)} collective-permute-done((bf16[96,1024]{1,0:T(8,128)(2,1)S(1)}, bf16[96,1024]{1,0:T(8,128)(2,1)S(1)}, u32[]{:S(2)}, u32[]{:S(2)}) %collective-permute-start.4) | collective-permute-done | bytes 196640 | tf_op jit(solution)/shard_map/ppermute | solution.py:63
  49.0 4.3 %collective-permute-start.5 = (bf16[96,1024]{1,0:T(8,128)(2,1)S(1)}, bf16[96,1024]{1,0:T(8,128)(2,1)S(1)}, u32[]{:S(2)}, u32[]{:S(2)}) collective-permute-start(bf16[96,1024]{1,0:T(8,128)(2,1)S(1)} %fusion.75), channel_id=1, source_target_pairs={{0,12},{4,0},{8,4},{12,8},{1,13},{5,1},{9,5},{13,9},{2,14},{6,2},{... | collective-permute-start | bytes 589832 | tf_op jit(solution)/shard_map/ppermute | solution.py:63
  53.4 4.2 %collective-permute-start.8 = (bf16[96,1024]{1,0:T(8,128)(2,1)S(1)}, bf16[96,1024]{1,0:T(8,128)(2,1)S(1)}, u32[]{:S(2)}, u32[]{:S(2)}) collective-permute-start(bf16[96,1024]{1,0:T(8,128)(2,1)S(1)} %fusion.73), channel_id=1, source_target_pairs={{0,12},{4,0},{8,4},{12,8},{1,13},{5,1},{9,5},{13,9},{2,14},{6,2},{... | collective-permute-start | bytes 589832 | tf_op jit(solution)/shard_map/ppermute | solution.py:63
  57.6 4.2 %collective-permute-start.11 = (bf16[96,1024]{1,0:T(8,128)(2,1)S(1)}, bf16[96,1024]{1,0:T(8,128)(2,1)S(1)}, u32[]{:S(2)}, u32[]{:S(2)}) collective-permute-start(bf16[96,1024]{1,0:T(8,128)(2,1)S(1)} %fusion.71), channel_id=1, source_target_pairs={{0,12},{4,0},{8,4},{12,8},{1,13},{5,1},{9,5},{13,9},{2,14},{6,2},{... | collective-permute-start | bytes 589832 | tf_op jit(solution)/shard_map/ppermute | solution.py:63
  61.8 4.2 %collective-permute-start.14 = (bf16[96,1024]{1,0:T(8,128)(2,1)S(1)}, bf16[96,1024]{1,0:T(8,128)(2,1)S(1)}, u32[]{:S(2)}, u32[]{:S(2)}) collective-permute-start(bf16[96,1024]{1,0:T(8,128)(2,1)S(1)} %fusion.69), channel_id=1, source_target_pairs={{0,12},{4,0},{8,4},{12,8},{1,13},{5,1},{9,5},{13,9},{2,14},{6,2},{... | collective-permute-start | bytes 589832 | tf_op jit(solution)/shard_map/ppermute | solution.py:63
  66.0 4.2 %collective-permute-start.6 = (bf16[96,1024]{1,0:T(8,128)(2,1)S(1)}, bf16[96,1024]{1,0:T(8,128)(2,1)S(1)}, u32[]{:S(2)}, u32[]{:S(2)}) collective-permute-start(bf16[96,1024]{1,0:T(8,128)(2,1)S(1)} %fusion.74), channel_id=1, source_target_pairs={{0,12},{4,0},{8,4},{12,8},{1,13},{5,1},{9,5},{13,9},{2,14},{6,2},{... | collective-permute-start | bytes 589832 | tf_op jit(solution)/shard_map/ppermute | solution.py:63
  70.2 4.2 %collective-permute-start.9 = (bf16[96,1024]{1,0:T(8,128)(2,1)S(1)}, bf16[96,1024]{1,0:T(8,128)(2,1)S(1)}, u32[]{:S(2)}, u32[]{:S(2)}) collective-permute-start(bf16[96,1024]{1,0:T(8,128)(2,1)S(1)} %fusion.72), channel_id=1, source_target_pairs={{0,12},{4,0},{8,4},{12,8},{1,13},{5,1},{9,5},{13,9},{2,14},{6,2},{... | collective-permute-start | bytes 589832 | tf_op jit(solution)/shard_map/ppermute | solution.py:63
  74.4 4.2 %collective-permute-start.12 = (bf16[96,1024]{1,0:T(8,128)(2,1)S(1)}, bf16[96,1024]{1,0:T(8,128)(2,1)S(1)}, u32[]{:S(2)}, u32[]{:S(2)}) collective-permute-start(bf16[96,1024]{1,0:T(8,128)(2,1)S(1)} %fusion.70), channel_id=1, source_target_pairs={{0,12},{4,0},{8,4},{12,8},{1,13},{5,1},{9,5},{13,9},{2,14},{6,2},{... | collective-permute-start | bytes 589832 | tf_op jit(solution)/shard_map/ppermute | solution.py:63
  78.6 4.2 %collective-permute-start.15 = (bf16[96,1024]{1,0:T(8,128)(2,1)S(1)}, bf16[96,1024]{1,0:T(8,128)(2,1)S(1)}, u32[]{:S(2)}, u32[]{:S(2)}) collective-permute-start(bf16[96,1024]{1,0:T(8,128)(2,1)S(1)} %fusion.68), channel_id=1, source_target_pairs={{0,12},{4,0},{8,4},{12,8},{1,13},{5,1},{9,5},{13,9},{2,14},{6,2},{... | collective-permute-start | bytes 589832 | tf_op jit(solution)/shard_map/ppermute | solution.py:63
  82.8 0.9 fusion.58
  83.7 3.2 %collective-permute-done.9 = bf16[96,1024]{1,0:T(8,128)(2,1)S(1)} collective-permute-done((bf16[96,1024]{1,0:T(8,128)(2,1)S(1)}, bf16[96,1024]{1,0:T(8,128)(2,1)S(1)}, u32[]{:S(2)}, u32[]{:S(2)}) %collective-permute-start.9) | collective-permute-done | bytes 196640 | tf_op jit(solution)/shard_map/ppermute | solution.py:63
  86.8 0.9 fusion.61
  87.7 3.3 %collective-permute-done.12 = bf16[96,1024]{1,0:T(8,128)(2,1)S(1)} collective-permute-done((bf16[96,1024]{1,0:T(8,128)(2,1)S(1)}, bf16[96,1024]{1,0:T(8,128)(2,1)S(1)}, u32[]{:S(2)}, u32[]{:S(2)}) %collective-permute-start.12) | collective-permute-done | bytes 196640 | tf_op jit(solution)/shard_map/ppermute | solution.py:63
  91.0 0.9 fusion.64
  91.9 2.6 %collective-permute-done.15 = bf16[96,1024]{1,0:T(8,128)(2,1)S(1)} collective-permute-done((bf16[96,1024]{1,0:T(8,128)(2,1)S(1)}, bf16[96,1024]{1,0:T(8,128)(2,1)S(1)}, u32[]{:S(2)}, u32[]{:S(2)}) %collective-permute-start.15) | collective-permute-done | bytes 196640 | tf_op jit(solution)/shard_map/ppermute | solution.py:63
  94.5 0.9 fusion.67
  95.3 0.9 pad_maximum_fusion
  (45 shorter events, 1.2 us)
Async XLA Ops:
  0.0 16.2 %copy-start = (f32[9,64,64]{2,1,0:T(8,128)S(1)}, f32[9,64,64]{2,1,0:T(8,128)}, u32[]{:S(2)}) copy-start(f32[9,64,64]{2,1,0:T(8,128)} %param.6) | copy-start | bytes 442372
  0.8 7.0 %collective-permute-start = (f32[64,2,32]{0,2,1:T(8,128)S(1)}, f32[64,2,32]{0,2,1:T(8,128)S(1)}, u32[]{:S(2)}, u32[]{:S(2)}) collective-permute-start(f32[64,2,32]{0,2,1:T(8,128)S(1)} %get-tuple-element.8), channel_id=1, source_target_pairs={{0,4},{4,8},{8,12},{12,0},{1,5},{5,9},{9,13},{13,1},{2,6},{6,10},{... | collective-permute-start | bytes 49160 | tf_op jit(solution)/shard_map/ppermute | solution.py:14
  3.9 5.1 %collective-permute-start.1 = (f32[64,2,32]{0,2,1:T(8,128)S(1)}, f32[64,2,32]{0,2,1:T(8,128)S(1)}, u32[]{:S(2)}, u32[]{:S(2)}) collective-permute-start(f32[64,2,32]{0,2,1:T(8,128)S(1)} %get-tuple-element.7), channel_id=1, source_target_pairs={{4,0},{8,4},{12,8},{0,12},{5,1},{9,5},{13,9},{1,13},{6,2},{10,6},{... | collective-permute-start | bytes 49160 | tf_op jit(solution)/shard_map/ppermute | solution.py:17
  9.0 2.7 %collective-permute-start.2 = (f32[64,36,2]{0,2,1:T(2,128)S(1)}, f32[64,36,2]{0,2,1:T(2,128)S(1)}, u32[]{:S(2)}, u32[]{:S(2)}) collective-permute-start(f32[64,36,2]{0,2,1:T(2,128)S(1)} %get-tuple-element.6), channel_id=1, source_target_pairs={{0,1},{1,2},{2,3},{4,5},{5,6},{6,7},{8,9},{9,10},{10,11},{12,13},{... | collective-permute-start | bytes 55304 | tf_op jit(solution)/shard_map/ppermute | solution.py:14
  10.4 5.1 %collective-permute-start.3 = (f32[64,36,2]{0,2,1:T(2,128)S(1)}, f32[64,36,2]{0,2,1:T(2,128)S(1)}, u32[]{:S(2)}, u32[]{:S(2)}) collective-permute-start(f32[64,36,2]{0,2,1:T(2,128)S(1)} %get-tuple-element.5), channel_id=1, source_target_pairs={{1,0},{2,1},{3,2},{5,4},{6,5},{7,6},{9,8},{10,9},{11,10},{13,12},{... | collective-permute-start | bytes 55304 | tf_op jit(solution)/shard_map/ppermute | solution.py:17
  23.0 1.0 %copy-start.1 = (f32[9,64,64]{2,1,0:T(8,128)S(1)}, f32[9,64,64]{2,1,0:T(8,128)}, u32[]{:S(2)}) copy-start(f32[9,64,64]{2,1,0:T(8,128)} %param.7) | copy-start | bytes 442372
  23.1 14.8 %slice-start = ((s8[8388608]{0:T(1024)(128)(4,1)}), s8[4194304]{0:T(1024)(128)(4,1)S(1)}, s32[]{:S(2)}) async-start(s8[8388608]{0:T(1024)(128)(4,1)} %bitcast.191), calls=%async_computation | async-start | bytes 8388608
  23.6 14.3 %slice-start.1 = ((s8[8388608]{0:T(1024)(128)(4,1)}), s8[4194304]{0:T(1024)(128)(4,1)S(1)}, s32[]{:S(2)}) async-start(s8[8388608]{0:T(1024)(128)(4,1)} %bitcast.191), calls=%async_computation.1 | async-start | bytes 8388608
  41.0 7.9 %collective-permute-start.4 = (bf16[96,1024]{1,0:T(8,128)(2,1)S(1)}, bf16[96,1024]{1,0:T(8,128)(2,1)S(1)}, u32[]{:S(2)}, u32[]{:S(2)}) collective-permute-start(bf16[96,1024]{1,0:T(8,128)(2,1)S(1)} %slice.343), channel_id=1, source_target_pairs={{0,12},{4,0},{8,4},{12,8},{1,13},{5,1},{9,5},{13,9},{2,14},{6,2},{... | collective-permute-start | bytes 589832 | tf_op jit(solution)/shard_map/ppermute | solution.py:63
  43.7 9.6 %collective-permute-start.7 = (bf16[96,1024]{1,0:T(8,128)(2,1)S(1)}, bf16[96,1024]{1,0:T(8,128)(2,1)S(1)}, u32[]{:S(2)}, u32[]{:S(2)}) collective-permute-start(bf16[96,1024]{1,0:T(8,128)(2,1)S(1)} %slice.342), channel_id=1, source_target_pairs={{0,12},{4,0},{8,4},{12,8},{1,13},{5,1},{9,5},{13,9},{2,14},{6,2},{... | collective-permute-start | bytes 589832 | tf_op jit(solution)/shard_map/ppermute | solution.py:63
  43.8 13.7 %collective-permute-start.10 = (bf16[96,1024]{1,0:T(8,128)(2,1)S(1)}, bf16[96,1024]{1,0:T(8,128)(2,1)S(1)}, u32[]{:S(2)}, u32[]{:S(2)}) collective-permute-start(bf16[96,1024]{1,0:T(8,128)(2,1)S(1)} %slice.341), channel_id=1, source_target_pairs={{0,12},{4,0},{8,4},{12,8},{1,13},{5,1},{9,5},{13,9},{2,14},{6,2},{... | collective-permute-start | bytes 589832 | tf_op jit(solution)/shard_map/ppermute | solution.py:63
  45.3 16.4 %collective-permute-start.13 = (bf16[96,1024]{1,0:T(8,128)(2,1)S(1)}, bf16[96,1024]{1,0:T(8,128)(2,1)S(1)}, u32[]{:S(2)}, u32[]{:S(2)}) collective-permute-start(bf16[96,1024]{1,0:T(8,128)(2,1)S(1)} %slice.340), channel_id=1, source_target_pairs={{0,12},{4,0},{8,4},{12,8},{1,13},{5,1},{9,5},{13,9},{2,14},{6,2},{... | collective-permute-start | bytes 589832 | tf_op jit(solution)/shard_map/ppermute | solution.py:63
  49.0 17.0 %collective-permute-start.5 = (bf16[96,1024]{1,0:T(8,128)(2,1)S(1)}, bf16[96,1024]{1,0:T(8,128)(2,1)S(1)}, u32[]{:S(2)}, u32[]{:S(2)}) collective-permute-start(bf16[96,1024]{1,0:T(8,128)(2,1)S(1)} %fusion.75), channel_id=1, source_target_pairs={{0,12},{4,0},{8,4},{12,8},{1,13},{5,1},{9,5},{13,9},{2,14},{6,2},{... | collective-permute-start | bytes 589832 | tf_op jit(solution)/shard_map/ppermute | solution.py:63
  53.4 16.8 %collective-permute-start.8 = (bf16[96,1024]{1,0:T(8,128)(2,1)S(1)}, bf16[96,1024]{1,0:T(8,128)(2,1)S(1)}, u32[]{:S(2)}, u32[]{:S(2)}) collective-permute-start(bf16[96,1024]{1,0:T(8,128)(2,1)S(1)} %fusion.73), channel_id=1, source_target_pairs={{0,12},{4,0},{8,4},{12,8},{1,13},{5,1},{9,5},{13,9},{2,14},{6,2},{... | collective-permute-start | bytes 589832 | tf_op jit(solution)/shard_map/ppermute | solution.py:63
  57.6 16.8 %collective-permute-start.11 = (bf16[96,1024]{1,0:T(8,128)(2,1)S(1)}, bf16[96,1024]{1,0:T(8,128)(2,1)S(1)}, u32[]{:S(2)}, u32[]{:S(2)}) collective-permute-start(bf16[96,1024]{1,0:T(8,128)(2,1)S(1)} %fusion.71), channel_id=1, source_target_pairs={{0,12},{4,0},{8,4},{12,8},{1,13},{5,1},{9,5},{13,9},{2,14},{6,2},{... | collective-permute-start | bytes 589832 | tf_op jit(solution)/shard_map/ppermute | solution.py:63
  61.8 16.8 %collective-permute-start.14 = (bf16[96,1024]{1,0:T(8,128)(2,1)S(1)}, bf16[96,1024]{1,0:T(8,128)(2,1)S(1)}, u32[]{:S(2)}, u32[]{:S(2)}) collective-permute-start(bf16[96,1024]{1,0:T(8,128)(2,1)S(1)} %fusion.69), channel_id=1, source_target_pairs={{0,12},{4,0},{8,4},{12,8},{1,13},{5,1},{9,5},{13,9},{2,14},{6,2},{... | collective-permute-start | bytes 589832 | tf_op jit(solution)/shard_map/ppermute | solution.py:63
  66.0 16.8 %collective-permute-start.6 = (bf16[96,1024]{1,0:T(8,128)(2,1)S(1)}, bf16[96,1024]{1,0:T(8,128)(2,1)S(1)}, u32[]{:S(2)}, u32[]{:S(2)}) collective-permute-start(bf16[96,1024]{1,0:T(8,128)(2,1)S(1)} %fusion.74), channel_id=1, source_target_pairs={{0,12},{4,0},{8,4},{12,8},{1,13},{5,1},{9,5},{13,9},{2,14},{6,2},{... | collective-permute-start | bytes 589832 | tf_op jit(solution)/shard_map/ppermute | solution.py:63
  70.2 16.6 %collective-permute-start.9 = (bf16[96,1024]{1,0:T(8,128)(2,1)S(1)}, bf16[96,1024]{1,0:T(8,128)(2,1)S(1)}, u32[]{:S(2)}, u32[]{:S(2)}) collective-permute-start(bf16[96,1024]{1,0:T(8,128)(2,1)S(1)} %fusion.72), channel_id=1, source_target_pairs={{0,12},{4,0},{8,4},{12,8},{1,13},{5,1},{9,5},{13,9},{2,14},{6,2},{... | collective-permute-start | bytes 589832 | tf_op jit(solution)/shard_map/ppermute | solution.py:63
  74.4 16.6 %collective-permute-start.12 = (bf16[96,1024]{1,0:T(8,128)(2,1)S(1)}, bf16[96,1024]{1,0:T(8,128)(2,1)S(1)}, u32[]{:S(2)}, u32[]{:S(2)}) collective-permute-start(bf16[96,1024]{1,0:T(8,128)(2,1)S(1)} %fusion.70), channel_id=1, source_target_pairs={{0,12},{4,0},{8,4},{12,8},{1,13},{5,1},{9,5},{13,9},{2,14},{6,2},{... | collective-permute-start | bytes 589832 | tf_op jit(solution)/shard_map/ppermute | solution.py:63
  78.6 15.8 %collective-permute-start.15 = (bf16[96,1024]{1,0:T(8,128)(2,1)S(1)}, bf16[96,1024]{1,0:T(8,128)(2,1)S(1)}, u32[]{:S(2)}, u32[]{:S(2)}) collective-permute-start(bf16[96,1024]{1,0:T(8,128)(2,1)S(1)} %fusion.68), channel_id=1, source_target_pairs={{0,12},{4,0},{8,4},{12,8},{1,13},{5,1},{9,5},{13,9},{2,14},{6,2},{... | collective-permute-start | bytes 589832 | tf_op jit(solution)/shard_map/ppermute | solution.py:63

commit v2 on v1

v2 whole, which is shorter than its diff:
```python
import functools

import jax
import jax.numpy as jnp
from jax import lax
from jax.experimental import pallas as pl
from jax.experimental.pallas import tpu as pltpu
from jax.sharding import PartitionSpec as P

PIECES = 4
LANES = 128
VMEM_BYTES = 24 * 1024 * 1024
ROWS_AT_ONCE = 768


def pack_kernel(field_ref, low_ref, high_ref, packed_ref):
    lon, lat, chans = field_ref.shape
    pairs = field_ref[...].reshape(lon // 2, 2, lat, chans)
    joined = jnp.concatenate([pairs[:, 0], pairs[:, 1]], axis=-1).astype(packed_ref.dtype)
    packed_ref[pl.ds(1, lon // 2)] = joined
    low_ref[...] = joined[:1]
    high_ref[...] = joined[-1:]


def split_two(value):
    upper = value.astype(jnp.bfloat16)
    return upper, (value - upper.astype(jnp.float32)).astype(jnp.bfloat16)


def spread_taps(kernel_ref):
    chans = kernel_ref.shape[1]
    nothing = jnp.zeros((chans, kernel_ref.shape[2]), jnp.float32)
    rows = []
    for tap in range(3):
        taps = [kernel_ref[3 * turn + tap] for turn in range(3)]
        rows.append(jnp.concatenate([taps[1], taps[2], nothing, taps[0]], axis=-1))
        rows.append(jnp.concatenate([taps[0], taps[1], taps[2], nothing], axis=-1))
    return jnp.concatenate(rows, axis=0).T


def weights_kernel(first_ref, second_ref, embed_ref, taps_one_ref, taps_two_ref, embed_out_ref, scratch):
    for source, target in ((first_ref, taps_one_ref), (second_ref, taps_two_ref)):
        upper, lower = split_two(spread_taps(source))
        target[0] = upper
        target[1] = lower
    chans = embed_ref.shape[0] // 4
    for first in range(0, embed_ref.shape[1], LANES):
        scratch[...] = embed_ref[:, pl.ds(first, LANES)].astype(jnp.float32)
        ordered = [scratch[pl.ds(2 * a + b, chans, stride=4), :] for b in range(2) for a in range(2)]
        turned = jnp.concatenate(ordered, axis=0).T
        embed_out_ref[pl.ds(first, LANES), :] = turned.astype(embed_out_ref.dtype)


def pairs_at_once(pairs, lat):
    best = 1
    for size in range(1, pairs + 1):
        if pairs % size == 0 and size * lat <= ROWS_AT_ONCE:
            best = size
    return best


def window(pairs_of, first, size, last):
    rows = []
    for pair in range(first, first + size):
        here = pairs_of(pair)
        after = pairs_of(min(pair + 1, last))
        before = pairs_of(max(pair - 1, 0))
        lane = lax.broadcasted_iota(jnp.int32, here.shape, 1)
        rows.append(jnp.concatenate([here, jnp.where(lane < here.shape[1] // 2, after, before)], axis=-1))
    return jnp.concatenate(rows, axis=0)


def add_lat_taps(products, lat):
    wide = products.shape[1] // 3
    count = products.shape[0]
    row = lax.broadcasted_iota(jnp.int32, (count, wide), 0) % lat
    below = pltpu.roll(products[:, :wide], 1, axis=0)
    above = pltpu.roll(products[:, 2 * wide :], count - 1, axis=0)
    return (
        products[:, wide : 2 * wide]
        + jnp.where(row == 0, 0.0, below)
        + jnp.where(row == lat - 1, 0.0, above)
    )


def gelu(value):
    return 0.5 * value * (1.0 + lax.erf(value * (0.5**0.5)))


def encode_kernel(field_ref, taps_one_ref, taps_two_ref, embed_ref, tokens_ref, upper_ref, lower_ref, two_ref):
    parts, pairs, width, wide = field_ref.shape
    lat = parts * width
    last = pairs - 1

    def field_of(pair):
        return field_ref[:, pair].reshape(lat, wide)

    def dot(left, right):
        return jnp.dot(left, right, preferred_element_type=jnp.float32)

    size = pairs_at_once(pairs, lat)
    for first in range(0, pairs, size):
        rows = window(field_of, first, size, last)
        products = dot(rows, taps_one_ref[0]) + dot(rows, taps_one_ref[1])
        upper, lower = split_two(gelu(add_lat_taps(products, lat)))
        upper_ref[pl.ds(first, size)] = upper.reshape(size, lat, wide)
        lower_ref[pl.ds(first, size)] = lower.reshape(size, lat, wide)
    size = pairs_at_once(pairs - 2, lat)
    for first in range(1, pairs - 1, size):
        rows_upper = window(lambda pair: upper_ref[pair], first, size, last)
        rows_lower = window(lambda pair: lower_ref[pair], first, size, last)
        products = dot(rows_upper, taps_two_ref[0]) + dot(rows_upper, taps_two_ref[1])
        products = products + dot(rows_lower, taps_two_ref[0])
        rounded = add_lat_taps(products, lat).astype(jnp.bfloat16).astype(jnp.float32)
        two_ref[pl.ds((first - 1) * lat, size * lat), :] = rounded
    half = two_ref.shape[0] // 2
    patches = jnp.concatenate(
        [two_ref[pl.ds(b, half, stride=2), :].astype(jnp.bfloat16) for b in range(2)], axis=-1
    )
    tokens_ref[...] = lax.dot_general(
        embed_ref[...], patches, (((1,), (1,)), ((), ())), preferred_element_type=jnp.float32
    ).astype(tokens_ref.dtype)


def call(kernel, out_shape, inputs, scratch=(), flops=0, moved=0):
    return pl.pallas_call(
        kernel,
        out_shape=out_shape,
        in_specs=[pl.BlockSpec(memory_space=pltpu.VMEM)] * len(inputs),
        out_specs=jax.tree.map(lambda unused: pl.BlockSpec(memory_space=pltpu.VMEM), out_shape),
        scratch_shapes=list(scratch),
        compiler_params=pltpu.CompilerParams(vmem_limit_bytes=VMEM_BYTES),
        cost_estimate=pl.CostEstimate(flops=flops, bytes_accessed=moved, transcendentals=0),
    )(*inputs)


def encode(weather, conv_first, conv_second, patch_embed):
    chans, lon, lat = weather.shape
    pairs, wide = lon // 2, 2 * chans
    embed = patch_embed.shape[1]
    shape = functools.partial(jax.ShapeDtypeStruct, dtype=jnp.bfloat16)
    low, high, packed = call(
        pack_kernel,
        (shape((1, lat, wide)), shape((1, lat, wide)), shape((pairs + 2, lat, wide))),
        (jnp.transpose(weather, (1, 2, 0)),),
        moved=weather.size * 10,
    )
    count = lax.axis_size("tok")
    up = [(i, (i + 1) % count) for i in range(count)]
    down = [(target, source) for source, target in up]
    before = lax.ppermute(high, "tok", up)
    after = lax.ppermute(low, "tok", down)
    taps = shape((2, 4 * chans, 6 * chans))
    taps_one, taps_two, embed_rows = call(
        weights_kernel,
        (taps, taps, shape((embed, 4 * chans))),
        (conv_first, conv_second, patch_embed),
        scratch=[pltpu.VMEM((patch_embed.shape[0], LANES), jnp.float32)],
        moved=conv_first.size * 20,
    )
    packed = lax.dynamic_update_slice_in_dim(packed, before, 0, 0)
    packed = lax.dynamic_update_slice_in_dim(packed, after, pairs + 1, 0)
    gathered = lax.all_gather(packed, ("ch", "sub"), axis=0)
    full_lat = gathered.shape[0] * lat
    held = pltpu.VMEM((pairs + 2, full_lat, wide), jnp.bfloat16)
    return call(
        encode_kernel,
        shape((embed, pairs * full_lat // 2)),
        (gathered, taps_one, taps_two, embed_rows),
        scratch=[held, held, pltpu.VMEM((pairs * full_lat, wide), jnp.float32)],
        flops=2 * (pairs + 1) * full_lat * 4 * chans * 6 * chans * 5,
        moved=gathered.size * 2,
    )


def lift(tokens, token_mixing, pieces):
    count = lax.axis_size("tok")
    rows = tokens.shape[0] // count
    width = token_mixing.shape[1] // pieces
    down = [(i, (i - 1) % count) for i in range(count)]
    partials = [
        jnp.dot(
            tokens,
            token_mixing[:, piece * width : (piece + 1) * width],
            preferred_element_type=jnp.float32,
        )
        for piece in range(pieces)
    ]
    travelling = [part[:rows].astype(jnp.bfloat16) for part in partials]
    for step in range(1, count):
        for piece in range(pieces):
            arrived = lax.ppermute(travelling[piece], "tok", down).astype(jnp.float32)
            summed = arrived + partials[piece][step * rows : (step + 1) * rows]
            if step == count - 1:
                summed = jax.nn.gelu(summed, approximate=False)
            travelling[piece] = summed.astype(jnp.bfloat16)
    return jnp.concatenate(travelling, axis=1)


def local(weather, conv_first, conv_second, patch_embed, token_mixing):
    count = lax.axis_size("tok")
    embed = patch_embed.shape[1]
    turn = ((lax.axis_index("tok") + 1) % count) * (embed // count)
    rolled = lax.dynamic_slice_in_dim(
        jnp.concatenate([patch_embed, patch_embed], axis=1), turn, embed, axis=1
    )
    tokens = encode(weather, conv_first, conv_second, rolled)
    return lift(tokens, token_mixing, PIECES)


def solution(mesh):
    placed = (P("groups", "tok", ("ch", "sub")), P(), P(), P(), P("tok", ("ch", "sub")))
    return jax.shard_map(
        local,
        mesh=mesh,
        in_specs=placed,
        out_specs=P(("groups", "tok"), ("ch", "sub")),
        check_vma=False,
    )
```

time: 96.5 us -> 79.7 us (0.83)
  matrix products: 15.2 us -> 3.9 us
  starting transfers between devices: 46.3 us -> 39.8 us
  Pallas kernels: 0 us -> 3.96 us
  blocking collectives: 9.54 us -> 7.82 us
    dot_general x7 -> x4, matrix products: 15.2 us -> 3.9 us  [lift(): jnp.dot(tokens, token_mixing[:, piece * width:(piece + 1) * width], prefe...]
    ppermute x4 -> x2, waiting for transfers between devices: 4.46 us -> 0.01 us  [the longest x1 0.01 us: encode(): before = lax.ppermute(high, 'tok', up)]
    ppermute x12, waiting for transfers between devices: 10.8 us -> 14.8 us  [lift(): arrived = lax.ppermute(travelling[piece], 'tok', down).astype(jnp.float32)]
    pallas_call x0 -> x3, Pallas kernels: none -> 3.96 us  [call(): pl.pallas_call(kernel, out_shape=out_shape, in_specs=[pl.BlockSpec(memory...]
    ppermute x12, starting transfers between devices: 38.6 us -> 34.6 us  [lift(): arrived = lax.ppermute(travelling[piece], 'tok', down).astype(jnp.float32)]
    ppermute x4 -> x2, starting transfers between devices: 7.69 us -> 5.17 us  [the longest x1 3.08 us: encode(): before = lax.ppermute(high, 'tok', up)]
    all_gather x1, blocking collectives: 9.54 us -> 7.82 us  [encode(): gathered = lax.all_gather(packed, ('ch', 'sub'), axis=0)]
    unnamed x21 -> x8, local copies, waits for them, and re-layouts: 2.06 us -> 2.97 us
  transfers between devices with their start and end apart: 16 -> 14, of which waited for: 6 -> 12; matrix products, arithmetic and copies ran while one was open for 7% -> 6% of each run, Pallas kernels for 0% -> 1%
where the time goes in v2:
time: 79.7 us; the launch traced here: 79.5 us
  starting transfers between devices  39.8 us (50%)
  waiting for transfers between devices  14.8 us (19%)
  blocking collectives  7.82 us (10%)
  other arithmetic  5.91 us (7%)
  Pallas kernels  3.96 us (5%)
  matrix products  3.9 us (5%)
  local copies, waits for them, and re-layouts  3.08 us (4%)
    ppermute x12, starting transfers between devices, lift(): arrived = lax.ppermute(travelling[piece], 'tok', down).astype(jnp.float32)  34.6 us
    ppermute x12, waiting for transfers between devices, lift(): arrived = lax.ppermute(travelling[piece], 'tok', down).astype(jnp.float32)  14.8 us
    all_gather x1, blocking collectives, encode(): gathered = lax.all_gather(packed, ('ch', 'sub'), axis=0)  7.82 us
    pallas_call x3, Pallas kernels, call(): pl.pallas_call(kernel, out_shape=out_shape, in_specs=[pl.BlockSpec(memory...  3.96 us
    dot_general x4, matrix products, lift(): jnp.dot(tokens, token_mixing[:, piece * width:(piece + 1) * width], prefe...  3.9 us
    convert_element_type x12, other arithmetic, lift(): travelling[piece] = summed.astype(jnp.bfloat16)  3.85 us
    ppermute x1, starting transfers between devices, encode(): before = lax.ppermute(high, 'tok', up)  3.08 us
    unnamed x8, local copies, waits for them, and re-layouts  2.97 us
  transfers between devices with their start and end apart: 14, of which 12 were waited for; matrix products, arithmetic and copies ran while one was open for 6% of the time, Pallas kernels for 1%

profile of v2, /device:TPU:0, one launch (start us, length us, event | category | flops | bytes accessed | tf_op | source)
XLA Modules:
  0.0 79.5 jit_solution(12169146096508973372)
XLA Ops:
  0.0 1.0 %copy-done = f32[64,32,32]{0,2,1:T(8,128)S(1)} copy-done((f32[64,32,32]{0,2,1:T(8,128)S(1)}, f32[64,32,32]{0,2,1:T(8,128)}, u32[]{:S(2)}) %copy-start) | copy-done | bytes 262168
  1.0 0.1 shard_map.55
  1.2 3.1 %collective-permute-start = (bf16[1,32,128]{2,1,0:T(8,128)(2,1)S(1)}, bf16[1,32,128]{2,1,0:T(8,128)(2,1)S(1)}, u32[]{:S(2)}, u32[]{:S(2)}) collective-permute-start(bf16[1,32,128]{2,1,0:T(8,128)(2,1)S(1)} %get-tuple-element.12), channel_id=1, source_target_pairs={{0,4},{4,8},{8,12},{12,0},{1,5},{5,9},{9,13},{13,1},{2,6},{6,10},{... | collective-permute-start | bytes 24584 | tf_op jit(solution)/shard_map/ppermute | solution.py:151
  4.2 2.1 %collective-permute-start.1 = (bf16[1,32,128]{2,1,0:T(8,128)(2,1)S(1)}, bf16[1,32,128]{2,1,0:T(8,128)(2,1)S(1)}, u32[]{:S(2)}, u32[]{:S(2)}) collective-permute-start(bf16[1,32,128]{2,1,0:T(8,128)(2,1)S(1)} %get-tuple-element.13), channel_id=1, source_target_pairs={{4,0},{8,4},{12,8},{0,12},{5,1},{9,5},{13,9},{1,13},{6,2},{10,6},{... | collective-permute-start | bytes 24584 | tf_op jit(solution)/shard_map/ppermute | solution.py:152
  6.3 1.1 %fusion.56.embed_ref = bf16[256,384]{1,0:T(8,128)(2,1)S(1)} fusion(s32[]{:T(128)S(6)} %select_n.11, bf16[256,384]{1,0:T(8,128)(2,1)} %param.8), kind=kLoop, calls=%fused_computation.111 | loop fusion | flops 393216 | bytes 393220 | tf_op jit(solution)/shard_map/concatenate | solution.py:205
  7.5 1.0 %copy-done.1 = f32[9,64,64]{2,1,0:T(8,128)S(1)} copy-done((f32[9,64,64]{2,1,0:T(8,128)S(1)}, f32[9,64,64]{2,1,0:T(8,128)}, u32[]{:S(2)}) %copy-start.1) | copy-done | bytes 147480
  8.4 1.0 %copy-done.2 = f32[9,64,64]{2,1,0:T(8,128)S(1)} copy-done((f32[9,64,64]{2,1,0:T(8,128)S(1)}, f32[9,64,64]{2,1,0:T(8,128)}, u32[]{:S(2)}) %copy-start.2) | copy-done | bytes 147480
  9.4 0.5 shard_map.56
  10.0 7.8 %all_gather.13.field_ref = bf16[4,18,32,128]{3,2,1,0:T(8,128)(2,1)S(1)} all-gather(bf16[1,18,32,128]{3,2,1,0:T(8,128)(2,1)S(1)} %bitcast_dynamic-update-slice_fusion), channel_id=1, replica_groups=mesh['groups'=2,'tok'=4,'ch'=2,'sub'=2] {'ch','sub'}, dimensions={0}, use_global_device_ids=true | all-gather | bytes 737280 | tf_op jit(solution)/shard_map/all_gather | solution.py:163
  17.8 3.3 %shard_map.57 = bf16[384,1024]{1,0:T(8,128)(2,1)S(1)} custom-call(bf16[4,18,32,128]{3,2,1,0:T(8,128)(2,1)S(1)} %all_gather.13.field_ref, bf16[2,256,384]{2,1,0:T(8,128)(2,1)S(1)} %get-tuple-element.14.taps_one_ref, bf16[2,256,384]{2,1,0:T(8,128)(2,1)S(1)} %get-tuple-element.15.taps_two_ref, bf16[384,256]{1,0:T(8,128)(2,1)S(1)} %get-tuple-element.16.embed_ref), custom_call_target="tpu_custom_call" | custom-call | flops 2139095040 | bytes 589824 | tf_op jit(solution)/shard_map/pallas_call | solution.py:126
  21.1 1.0 %fusion = f32[384,1024]{1,0:T(8,128)S(1)} fusion(bf16[384,1024]{1,0:T(8,128)(2,1)S(1)} %shard_map.57, bf16[1024,4096]{1,0:T(8,128)(2,1)S(1)} %copy-done.3), kind=kOutput, calls=%fused_computation | convolution fusion | flops 805306368 | bytes 4456448 | tf_op jit(solution)/shard_map/dot_general | solution.py:182
  22.1 1.0 %fusion.2 = f32[384,1024]{1,0:T(8,128)S(1)} fusion(bf16[384,1024]{1,0:T(8,128)(2,1)S(1)} %shard_map.57, bf16[1024,4096]{1,0:T(8,128)(2,1)S(1)} %copy-done.3), kind=kOutput, calls=%fused_computation.2 | convolution fusion | flops 805306368 | bytes 4456448 | tf_op jit(solution)/shard_map/dot_general | solution.py:182
  23.1 1.0 %fusion.4 = f32[384,1024]{1,0:T(8,128)S(1)} fusion(bf16[384,1024]{1,0:T(8,128)(2,1)S(1)} %shard_map.57, bf16[1024,4096]{1,0:T(8,128)(2,1)S(1)} %copy-done.3), kind=kOutput, calls=%fused_computation.4 | convolution fusion | flops 805306368 | bytes 4456448 | tf_op jit(solution)/shard_map/dot_general | solution.py:182
  24.1 1.9 %collective-permute-start.11 = (bf16[96,1024]{1,0:T(8,128)(2,1)S(1)}, bf16[96,1024]{1,0:T(8,128)(2,1)S(1)}, u32[]{:S(2)}, u32[]{:S(2)}) collective-permute-start(bf16[96,1024]{1,0:T(8,128)(2,1)S(1)} %slice.148), channel_id=1, source_target_pairs={{0,12},{4,0},{8,4},{12,8},{1,13},{5,1},{9,5},{13,9},{2,14},{6,2},{... | collective-permute-start | bytes 589832 | tf_op jit(solution)/shard_map/ppermute | solution.py:192
  26.0 0.6 collective-permute-start.8
  26.6 0.5 collective-permute-start.5
  27.1 1.0 %fusion.6 = f32[384,1024]{1,0:T(8,128)S(1)} fusion(bf16[384,1024]{1,0:T(8,128)(2,1)S(1)} %shard_map.57, bf16[1024,4096]{1,0:T(8,128)(2,1)S(1)} %copy-done.3), kind=kOutput, calls=%fused_computation.6 | convolution fusion | flops 805306368 | bytes 4456448 | tf_op jit(solution)/shard_map/dot_general | solution.py:182
  28.1 2.3 %collective-permute-start.2 = (bf16[96,1024]{1,0:T(8,128)(2,1)S(1)}, bf16[96,1024]{1,0:T(8,128)(2,1)S(1)}, u32[]{:S(2)}, u32[]{:S(2)}) collective-permute-start(bf16[96,1024]{1,0:T(8,128)(2,1)S(1)} %slice.151), channel_id=1, source_target_pairs={{0,12},{4,0},{8,4},{12,8},{1,13},{5,1},{9,5},{13,9},{2,14},{6,2},{... | collective-permute-start | bytes 589832 | tf_op jit(solution)/shard_map/ppermute | solution.py:192
  30.3 1.5 %collective-permute-done.11 = bf16[96,1024]{1,0:T(8,128)(2,1)S(1)} collective-permute-done((bf16[96,1024]{1,0:T(8,128)(2,1)S(1)}, bf16[96,1024]{1,0:T(8,128)(2,1)S(1)}, u32[]{:S(2)}, u32[]{:S(2)}) %collective-permute-start.11) | collective-permute-done | bytes 196640 | tf_op jit(solution)/shard_map/ppermute | solution.py:192
  31.9 3.7 %collective-permute-start.12 = (bf16[96,1024]{1,0:T(8,128)(2,1)S(1)}, bf16[96,1024]{1,0:T(8,128)(2,1)S(1)}, u32[]{:S(2)}, u32[]{:S(2)}) collective-permute-start(bf16[96,1024]{1,0:T(8,128)(2,1)S(1)} %fusion.21), channel_id=1, source_target_pairs={{0,12},{4,0},{8,4},{12,8},{1,13},{5,1},{9,5},{13,9},{2,14},{6,2},{... | collective-permute-start | bytes 589832 | tf_op jit(solution)/shard_map/ppermute | solution.py:192
  35.6 0.5 collective-permute-done.8
  36.1 3.7 %collective-permute-start.9 = (bf16[96,1024]{1,0:T(8,128)(2,1)S(1)}, bf16[96,1024]{1,0:T(8,128)(2,1)S(1)}, u32[]{:S(2)}, u32[]{:S(2)}) collective-permute-start(bf16[96,1024]{1,0:T(8,128)(2,1)S(1)} %fusion.23), channel_id=1, source_target_pairs={{0,12},{4,0},{8,4},{12,8},{1,13},{5,1},{9,5},{13,9},{2,14},{6,2},{... | collective-permute-start | bytes 589832 | tf_op jit(solution)/shard_map/ppermute | solution.py:192
  39.8 0.5 collective-permute-done.5
  40.3 3.7 %collective-permute-start.6 = (bf16[96,1024]{1,0:T(8,128)(2,1)S(1)}, bf16[96,1024]{1,0:T(8,128)(2,1)S(1)}, u32[]{:S(2)}, u32[]{:S(2)}) collective-permute-start(bf16[96,1024]{1,0:T(8,128)(2,1)S(1)} %fusion.25), channel_id=1, source_target_pairs={{0,12},{4,0},{8,4},{12,8},{1,13},{5,1},{9,5},{13,9},{2,14},{6,2},{... | collective-permute-start | bytes 589832 | tf_op jit(solution)/shard_map/ppermute | solution.py:192
  44.0 0.5 collective-permute-done.2
  44.5 0.1 fusion.27
  44.6 3.7 %collective-permute-start.3 = (bf16[96,1024]{1,0:T(8,128)(2,1)S(1)}, bf16[96,1024]{1,0:T(8,128)(2,1)S(1)}, u32[]{:S(2)}, u32[]{:S(2)}) collective-permute-start(bf16[96,1024]{1,0:T(8,128)(2,1)S(1)} %fusion.27), channel_id=1, source_target_pairs={{0,12},{4,0},{8,4},{12,8},{1,13},{5,1},{9,5},{13,9},{2,14},{6,2},{... | collective-permute-start | bytes 589832 | tf_op jit(solution)/shard_map/ppermute | solution.py:192
  48.2 0.5 collective-permute-done.12
  48.7 0.1 fusion.20
  48.8 3.7 %collective-permute-start.13 = (bf16[96,1024]{1,0:T(8,128)(2,1)S(1)}, bf16[96,1024]{1,0:T(8,128)(2,1)S(1)}, u32[]{:S(2)}, u32[]{:S(2)}) collective-permute-start(bf16[96,1024]{1,0:T(8,128)(2,1)S(1)} %fusion.20), channel_id=1, source_target_pairs={{0,12},{4,0},{8,4},{12,8},{1,13},{5,1},{9,5},{13,9},{2,14},{6,2},{... | collective-permute-start | bytes 589832 | tf_op jit(solution)/shard_map/ppermute | solution.py:192
  52.4 0.5 collective-permute-done.9
  52.9 0.1 fusion.22
  53.0 3.7 %collective-permute-start.10 = (bf16[96,1024]{1,0:T(8,128)(2,1)S(1)}, bf16[96,1024]{1,0:T(8,128)(2,1)S(1)}, u32[]{:S(2)}, u32[]{:S(2)}) collective-permute-start(bf16[96,1024]{1,0:T(8,128)(2,1)S(1)} %fusion.22), channel_id=1, source_target_pairs={{0,12},{4,0},{8,4},{12,8},{1,13},{5,1},{9,5},{13,9},{2,14},{6,2},{... | collective-permute-start | bytes 589832 | tf_op jit(solution)/shard_map/ppermute | solution.py:192
  56.7 0.5 collective-permute-done.6
  57.2 0.1 fusion.24
  57.2 3.7 %collective-permute-start.7 = (bf16[96,1024]{1,0:T(8,128)(2,1)S(1)}, bf16[96,1024]{1,0:T(8,128)(2,1)S(1)}, u32[]{:S(2)}, u32[]{:S(2)}) collective-permute-start(bf16[96,1024]{1,0:T(8,128)(2,1)S(1)} %fusion.24), channel_id=1, source_target_pairs={{0,12},{4,0},{8,4},{12,8},{1,13},{5,1},{9,5},{13,9},{2,14},{6,2},{... | collective-permute-start | bytes 589832 | tf_op jit(solution)/shard_map/ppermute | solution.py:192
  60.9 0.5 collective-permute-done.3
  61.4 0.1 fusion.26
  61.4 3.8 %collective-permute-start.4 = (bf16[96,1024]{1,0:T(8,128)(2,1)S(1)}, bf16[96,1024]{1,0:T(8,128)(2,1)S(1)}, u32[]{:S(2)}, u32[]{:S(2)}) collective-permute-start(bf16[96,1024]{1,0:T(8,128)(2,1)S(1)} %fusion.26), channel_id=1, source_target_pairs={{0,12},{4,0},{8,4},{12,8},{1,13},{5,1},{9,5},{13,9},{2,14},{6,2},{... | collective-permute-start | bytes 589832 | tf_op jit(solution)/shard_map/ppermute | solution.py:192
  65.3 0.3 collective-permute-done.13
  65.6 0.9 %fusion.19 = bf16[96,1024]{1,0:T(8,128)(2,1)S(1)} fusion(f32[384,1024]{1,0:T(8,128)S(1)} %fusion, bf16[96,1024]{1,0:T(8,128)(2,1)S(1)} %collective-permute-done.13), kind=kLoop, calls=%fused_computation.24 | loop fusion | flops 6586368 | bytes 786432 | tf_op jit(solution)/shard_map/convert_element_type | solution.py:196
  66.4 3.3 %collective-permute-done.10 = bf16[96,1024]{1,0:T(8,128)(2,1)S(1)} collective-permute-done((bf16[96,1024]{1,0:T(8,128)(2,1)S(1)}, bf16[96,1024]{1,0:T(8,128)(2,1)S(1)}, u32[]{:S(2)}, u32[]{:S(2)}) %collective-permute-start.10) | collective-permute-done | bytes 196640 | tf_op jit(solution)/shard_map/ppermute | solution.py:192
  69.8 0.9 %fusion.16 = bf16[96,1024]{1,0:T(8,128)(2,1)S(1)} fusion(f32[384,1024]{1,0:T(8,128)S(1)} %fusion.2, bf16[96,1024]{1,0:T(8,128)(2,1)S(1)} %collective-permute-done.10), kind=kLoop, calls=%fused_computation.21 | loop fusion | flops 6586368 | bytes 786432 | tf_op jit(solution)/shard_map/convert_element_type | solution.py:196
  70.7 3.3 %collective-permute-done.7 = bf16[96,1024]{1,0:T(8,128)(2,1)S(1)} collective-permute-done((bf16[96,1024]{1,0:T(8,128)(2,1)S(1)}, bf16[96,1024]{1,0:T(8,128)(2,1)S(1)}, u32[]{:S(2)}, u32[]{:S(2)}) %collective-permute-start.7) | collective-permute-done | bytes 196640 | tf_op jit(solution)/shard_map/ppermute | solution.py:192
  74.0 0.9 %fusion.13 = bf16[96,1024]{1,0:T(8,128)(2,1)S(1)} fusion(f32[384,1024]{1,0:T(8,128)S(1)} %fusion.4, bf16[96,1024]{1,0:T(8,128)(2,1)S(1)} %collective-permute-done.7), kind=kLoop, calls=%fused_computation.18 | loop fusion | flops 6586368 | bytes 786432 | tf_op jit(solution)/shard_map/convert_element_type | solution.py:196
  74.9 2.8 %collective-permute-done.4 = bf16[96,1024]{1,0:T(8,128)(2,1)S(1)} collective-permute-done((bf16[96,1024]{1,0:T(8,128)(2,1)S(1)}, bf16[96,1024]{1,0:T(8,128)(2,1)S(1)}, u32[]{:S(2)}, u32[]{:S(2)}) %collective-permute-start.4) | collective-permute-done | bytes 196640 | tf_op jit(solution)/shard_map/ppermute | solution.py:192
  77.7 0.9 %fusion.10 = bf16[96,1024]{1,0:T(8,128)(2,1)S(1)} fusion(f32[384,1024]{1,0:T(8,128)S(1)} %fusion.6, bf16[96,1024]{1,0:T(8,128)(2,1)S(1)} %collective-permute-done.4), kind=kLoop, calls=%fused_computation.15 | loop fusion | flops 6586368 | bytes 786432 | tf_op jit(solution)/shard_map/convert_element_type | solution.py:196
  78.5 0.9 %pad_maximum_fusion = bf16[96,4096]{1,0:T(8,128)(2,1)} fusion(bf16[96,1024]{1,0:T(8,128)(2,1)S(1)} %fusion.19, bf16[96,1024]{1,0:T(8,128)(2,1)S(1)} %fusion.16, bf16[96,1024]{1,0:T(8,128)(2,1)S(1)} %fusion.13, bf16[96,1024]{1,0:T(8,128)(2,1)S(1)} %fusion.10), kind=kLoop, calls=%fused_computation.8 | loop fusion | flops 3145728 | bytes 1572864 | tf_op jit(solution)/shard_map/concatenate | solution.py:197
  (16 shorter events, 0.2 us)
Async XLA Ops:
  0.0 1.0 %copy-start = (f32[64,32,32]{0,2,1:T(8,128)S(1)}, f32[64,32,32]{0,2,1:T(8,128)}, u32[]{:S(2)}) copy-start(f32[64,32,32]{0,2,1:T(8,128)} %param.5) | copy-start | bytes 786436
  1.2 8.8 %collective-permute-start = (bf16[1,32,128]{2,1,0:T(8,128)(2,1)S(1)}, bf16[1,32,128]{2,1,0:T(8,128)(2,1)S(1)}, u32[]{:S(2)}, u32[]{:S(2)}) collective-permute-start(bf16[1,32,128]{2,1,0:T(8,128)(2,1)S(1)} %get-tuple-element.12), channel_id=1, source_target_pairs={{0,4},{4,8},{8,12},{12,0},{1,5},{5,9},{9,13},{13,1},{2,6},{6,10},{... | collective-permute-start | bytes 24584 | tf_op jit(solution)/shard_map/ppermute | solution.py:151
  4.2 5.7 %collective-permute-start.1 = (bf16[1,32,128]{2,1,0:T(8,128)(2,1)S(1)}, bf16[1,32,128]{2,1,0:T(8,128)(2,1)S(1)}, u32[]{:S(2)}, u32[]{:S(2)}) collective-permute-start(bf16[1,32,128]{2,1,0:T(8,128)(2,1)S(1)} %get-tuple-element.13), channel_id=1, source_target_pairs={{4,0},{8,4},{12,8},{0,12},{5,1},{9,5},{13,9},{1,13},{6,2},{10,6},{... | collective-permute-start | bytes 24584 | tf_op jit(solution)/shard_map/ppermute | solution.py:152
  7.4 1.0 %copy-start.1 = (f32[9,64,64]{2,1,0:T(8,128)S(1)}, f32[9,64,64]{2,1,0:T(8,128)}, u32[]{:S(2)}) copy-start(f32[9,64,64]{2,1,0:T(8,128)} %first_ref.1) | copy-start | bytes 442372
  8.4 1.0 %copy-start.2 = (f32[9,64,64]{2,1,0:T(8,128)S(1)}, f32[9,64,64]{2,1,0:T(8,128)}, u32[]{:S(2)}) copy-start(f32[9,64,64]{2,1,0:T(8,128)} %second_ref.1) | copy-start | bytes 442372
  9.9 11.2 %copy-start.3 = (bf16[1024,4096]{1,0:T(8,128)(2,1)S(1)}, bf16[1024,4096]{1,0:T(8,128)(2,1)}, u32[]{:S(2)}) copy-start(bf16[1024,4096]{1,0:T(8,128)(2,1)} %param.9) | copy-start | bytes 25165828
  24.1 7.8 %collective-permute-start.11 = (bf16[96,1024]{1,0:T(8,128)(2,1)S(1)}, bf16[96,1024]{1,0:T(8,128)(2,1)S(1)}, u32[]{:S(2)}, u32[]{:S(2)}) collective-permute-start(bf16[96,1024]{1,0:T(8,128)(2,1)S(1)} %slice.148), channel_id=1, source_target_pairs={{0,12},{4,0},{8,4},{12,8},{1,13},{5,1},{9,5},{13,9},{2,14},{6,2},{... | collective-permute-start | bytes 589832 | tf_op jit(solution)/shard_map/ppermute | solution.py:192
  26.0 10.1 %collective-permute-start.8 = (bf16[96,1024]{1,0:T(8,128)(2,1)S(1)}, bf16[96,1024]{1,0:T(8,128)(2,1)S(1)}, u32[]{:S(2)}, u32[]{:S(2)}) collective-permute-start(bf16[96,1024]{1,0:T(8,128)(2,1)S(1)} %slice.149), channel_id=1, source_target_pairs={{0,12},{4,0},{8,4},{12,8},{1,13},{5,1},{9,5},{13,9},{2,14},{6,2},{... | collective-permute-start | bytes 589832 | tf_op jit(solution)/shard_map/ppermute | solution.py:192
  26.6 13.7 %collective-permute-start.5 = (bf16[96,1024]{1,0:T(8,128)(2,1)S(1)}, bf16[96,1024]{1,0:T(8,128)(2,1)S(1)}, u32[]{:S(2)}, u32[]{:S(2)}) collective-permute-start(bf16[96,1024]{1,0:T(8,128)(2,1)S(1)} %slice.150), channel_id=1, source_target_pairs={{0,12},{4,0},{8,4},{12,8},{1,13},{5,1},{9,5},{13,9},{2,14},{6,2},{... | collective-permute-start | bytes 589832 | tf_op jit(solution)/shard_map/ppermute | solution.py:192
  28.1 16.4 %collective-permute-start.2 = (bf16[96,1024]{1,0:T(8,128)(2,1)S(1)}, bf16[96,1024]{1,0:T(8,128)(2,1)S(1)}, u32[]{:S(2)}, u32[]{:S(2)}) collective-permute-start(bf16[96,1024]{1,0:T(8,128)(2,1)S(1)} %slice.151), channel_id=1, source_target_pairs={{0,12},{4,0},{8,4},{12,8},{1,13},{5,1},{9,5},{13,9},{2,14},{6,2},{... | collective-permute-start | bytes 589832 | tf_op jit(solution)/shard_map/ppermute | solution.py:192
  31.9 16.8 %collective-permute-start.12 = (bf16[96,1024]{1,0:T(8,128)(2,1)S(1)}, bf16[96,1024]{1,0:T(8,128)(2,1)S(1)}, u32[]{:S(2)}, u32[]{:S(2)}) collective-permute-start(bf16[96,1024]{1,0:T(8,128)(2,1)S(1)} %fusion.21), channel_id=1, source_target_pairs={{0,12},{4,0},{8,4},{12,8},{1,13},{5,1},{9,5},{13,9},{2,14},{6,2},{... | collective-permute-start | bytes 589832 | tf_op jit(solution)/shard_map/ppermute | solution.py:192
  36.1 16.8 %collective-permute-start.9 = (bf16[96,1024]{1,0:T(8,128)(2,1)S(1)}, bf16[96,1024]{1,0:T(8,128)(2,1)S(1)}, u32[]{:S(2)}, u32[]{:S(2)}) collective-permute-start(bf16[96,1024]{1,0:T(8,128)(2,1)S(1)} %fusion.23), channel_id=1, source_target_pairs={{0,12},{4,0},{8,4},{12,8},{1,13},{5,1},{9,5},{13,9},{2,14},{6,2},{... | collective-permute-start | bytes 589832 | tf_op jit(solution)/shard_map/ppermute | solution.py:192
  40.3 16.8 %collective-permute-start.6 = (bf16[96,1024]{1,0:T(8,128)(2,1)S(1)}, bf16[96,1024]{1,0:T(8,128)(2,1)S(1)}, u32[]{:S(2)}, u32[]{:S(2)}) collective-permute-start(bf16[96,1024]{1,0:T(8,128)(2,1)S(1)} %fusion.25), channel_id=1, source_target_pairs={{0,12},{4,0},{8,4},{12,8},{1,13},{5,1},{9,5},{13,9},{2,14},{6,2},{... | collective-permute-start | bytes 589832 | tf_op jit(solution)/shard_map/ppermute | solution.py:192
  44.6 16.8 %collective-permute-start.3 = (bf16[96,1024]{1,0:T(8,128)(2,1)S(1)}, bf16[96,1024]{1,0:T(8,128)(2,1)S(1)}, u32[]{:S(2)}, u32[]{:S(2)}) collective-permute-start(bf16[96,1024]{1,0:T(8,128)(2,1)S(1)} %fusion.27), channel_id=1, source_target_pairs={{0,12},{4,0},{8,4},{12,8},{1,13},{5,1},{9,5},{13,9},{2,14},{6,2},{... | collective-permute-start | bytes 589832 | tf_op jit(solution)/shard_map/ppermute | solution.py:192
  48.8 16.8 %collective-permute-start.13 = (bf16[96,1024]{1,0:T(8,128)(2,1)S(1)}, bf16[96,1024]{1,0:T(8,128)(2,1)S(1)}, u32[]{:S(2)}, u32[]{:S(2)}) collective-permute-start(bf16[96,1024]{1,0:T(8,128)(2,1)S(1)} %fusion.20), channel_id=1, source_target_pairs={{0,12},{4,0},{8,4},{12,8},{1,13},{5,1},{9,5},{13,9},{2,14},{6,2},{... | collective-permute-start | bytes 589832 | tf_op jit(solution)/shard_map/ppermute | solution.py:192
  53.0 16.8 %collective-permute-start.10 = (bf16[96,1024]{1,0:T(8,128)(2,1)S(1)}, bf16[96,1024]{1,0:T(8,128)(2,1)S(1)}, u32[]{:S(2)}, u32[]{:S(2)}) collective-permute-start(bf16[96,1024]{1,0:T(8,128)(2,1)S(1)} %fusion.22), channel_id=1, source_target_pairs={{0,12},{4,0},{8,4},{12,8},{1,13},{5,1},{9,5},{13,9},{2,14},{6,2},{... | collective-permute-start | bytes 589832 | tf_op jit(solution)/shard_map/ppermute | solution.py:192
  57.2 16.8 %collective-permute-start.7 = (bf16[96,1024]{1,0:T(8,128)(2,1)S(1)}, bf16[96,1024]{1,0:T(8,128)(2,1)S(1)}, u32[]{:S(2)}, u32[]{:S(2)}) collective-permute-start(bf16[96,1024]{1,0:T(8,128)(2,1)S(1)} %fusion.24), channel_id=1, source_target_pairs={{0,12},{4,0},{8,4},{12,8},{1,13},{5,1},{9,5},{13,9},{2,14},{6,2},{... | collective-permute-start | bytes 589832 | tf_op jit(solution)/shard_map/ppermute | solution.py:192
  61.4 16.2 %collective-permute-start.4 = (bf16[96,1024]{1,0:T(8,128)(2,1)S(1)}, bf16[96,1024]{1,0:T(8,128)(2,1)S(1)}, u32[]{:S(2)}, u32[]{:S(2)}) collective-permute-start(bf16[96,1024]{1,0:T(8,128)(2,1)S(1)} %fusion.26), channel_id=1, source_target_pairs={{0,12},{4,0},{8,4},{12,8},{1,13},{5,1},{9,5},{13,9},{2,14},{6,2},{... | collective-permute-start | bytes 589832 | tf_op jit(solution)/shard_map/ppermute | solution.py:192

commit v3 on v2

--- a/solution.py
+++ b/solution.py
@@ -8,6 +8,7 @@
 from jax.sharding import PartitionSpec as P
 
 PIECES = 4
+STEP = 256
 LANES = 128
 VMEM_BYTES = 24 * 1024 * 1024
 ROWS_AT_ONCE = 768
@@ -87,13 +88,22 @@
     return 0.5 * value * (1.0 + lax.erf(value * (0.5**0.5)))
 
 
-def encode_kernel(field_ref, taps_one_ref, taps_two_ref, embed_ref, tokens_ref, upper_ref, lower_ref, two_ref):
-    parts, pairs, width, wide = field_ref.shape
-    lat = parts * width
+def encode_kernel(count_ch, count_sub, *refs):
+    count = count_ch * count_sub
+    blocks = refs[:count]
+    taps_one_ref, taps_two_ref, embed_ref, tokens_ref, field_ref, upper_ref, lower_ref, two_ref = refs[count:]
+    pairs, lat, wide = field_ref.shape
+    width = lat // count
     last = pairs - 1
+    for away_ch in range(count_ch):
+        for away_sub in range(count_sub):
+            at_ch = lax.rem(lax.axis_index("ch") + count_ch - away_ch, count_ch)
+            at_sub = lax.rem(lax.axis_index("sub") + count_sub - away_sub, count_sub)
+            start = pl.multiple_of((at_ch * count_sub + at_sub) * width, width)
+            field_ref[:, pl.ds(start, width), :] = blocks[away_ch * count_sub + away_sub][...]
 
     def field_of(pair):
-        return field_ref[:, pair].reshape(lat, wide)
+        return field_ref[pair]
 
     def dot(left, right):
         return jnp.dot(left, right, preferred_element_type=jnp.float32)
@@ -134,6 +144,23 @@
     )(*inputs)
 
 
+def turned(value, axis, away):
+    count = lax.axis_size(axis)
+    return lax.ppermute(value, axis, [(i, (i + away) % count) for i in range(count)])
+
+
+def gather_blocks(block):
+    rows = [block]
+    for away in range(1, lax.axis_size("ch")):
+        rows.append(turned(block, "ch", away))
+    blocks = []
+    for row in rows:
+        blocks.append(row)
+        for away in range(1, lax.axis_size("sub")):
+            blocks.append(turned(row, "sub", away))
+    return blocks
+
+
 def encode(weather, conv_first, conv_second, patch_embed):
     chans, lon, lat = weather.shape
     pairs, wide = lon // 2, 2 * chans
@@ -145,11 +172,8 @@
         (jnp.transpose(weather, (1, 2, 0)),),
         moved=weather.size * 10,
     )
-    count = lax.axis_size("tok")
-    up = [(i, (i + 1) % count) for i in range(count)]
-    down = [(target, source) for source, target in up]
-    before = lax.ppermute(high, "tok", up)
-    after = lax.ppermute(low, "tok", down)
+    before = turned(high, "tok", 1)
+    after = turned(low, "tok", -1)
     taps = shape((2, 4 * chans, 6 * chans))
     taps_one, taps_two, embed_rows = call(
         weights_kernel,
@@ -160,39 +184,64 @@
     )
     packed = lax.dynamic_update_slice_in_dim(packed, before, 0, 0)
     packed = lax.dynamic_update_slice_in_dim(packed, after, pairs + 1, 0)
-    gathered = lax.all_gather(packed, ("ch", "sub"), axis=0)
-    full_lat = gathered.shape[0] * lat
+    blocks = gather_blocks(packed)
+    full_lat = len(blocks) * lat
     held = pltpu.VMEM((pairs + 2, full_lat, wide), jnp.bfloat16)
     return call(
-        encode_kernel,
+        functools.partial(encode_kernel, lax.axis_size("ch"), lax.axis_size("sub")),
         shape((embed, pairs * full_lat // 2)),
-        (gathered, taps_one, taps_two, embed_rows),
-        scratch=[held, held, pltpu.VMEM((pairs * full_lat, wide), jnp.float32)],
+        (*blocks, taps_one, taps_two, embed_rows),
+        scratch=[held, held, held, pltpu.VMEM((pairs * full_lat, wide), jnp.float32)],
         flops=2 * (pairs + 1) * full_lat * 4 * chans * 6 * chans * 5,
-        moved=gathered.size * 2,
-    )
+        moved=packed.size * 2 * len(blocks),
+    )
+
+
+def partial_kernel(tokens_ref, mixing_ref, sent_ref, kept_ref):
+    product = jnp.dot(tokens_ref[...], mixing_ref[...], preferred_element_type=jnp.float32)
+    rows = sent_ref.shape[0]
+    sent_ref[...] = product[:rows].astype(sent_ref.dtype)
+    kept_ref[...] = product[rows:]
+
+
+def partial(tokens, token_mixing, first, width, rows):
+    embed, count = tokens.shape
+    step = STEP if width % STEP == 0 else width
+    return pl.pallas_call(
+        partial_kernel,
+        out_shape=(
+            jax.ShapeDtypeStruct((rows, width), jnp.bfloat16),
+            jax.ShapeDtypeStruct((embed - rows, width), jnp.float32),
+        ),
+        grid=(width // step,),
+        in_specs=[
+            pl.BlockSpec(memory_space=pltpu.VMEM),
+            pl.BlockSpec((count, step), lambda i: (0, first // step + i)),
+        ],
+        out_specs=(
+            pl.BlockSpec((rows, step), lambda i: (0, i)),
+            pl.BlockSpec((embed - rows, step), lambda i: (0, i)),
+        ),
+        compiler_params=pltpu.CompilerParams(vmem_limit_bytes=VMEM_BYTES),
+        cost_estimate=pl.CostEstimate(flops=0, bytes_accessed=0, transcendentals=0),
+    )(tokens, token_mixing)
 
 
 def lift(tokens, token_mixing, pieces):
     count = lax.axis_size("tok")
     rows = tokens.shape[0] // count
     width = token_mixing.shape[1] // pieces
-    down = [(i, (i - 1) % count) for i in range(count)]
-    partials = [
-        jnp.dot(
-            tokens,
-            token_mixing[:, piece * width : (piece + 1) * width],
-            preferred_element_type=jnp.float32,
-        )
-        for piece in range(pieces)
-    ]
-    travelling = [part[:rows].astype(jnp.bfloat16) for part in partials]
+    travelling, kept = [], []
+    for piece in range(pieces):
+        sent, others = partial(tokens, token_mixing, piece * width, width, rows)
+        travelling.append(sent)
+        kept.append(others)
     for step in range(1, count):
         for piece in range(pieces):
-            arrived = lax.ppermute(travelling[piece], "tok", down).astype(jnp.float32)
-            summed = arrived + partials[piece][step * rows : (step + 1) * rows]
+            arrived = turned(travelling[piece], "tok", -1).astype(jnp.float32)
+            summed = arrived + kept[piece][(step - 1) * rows : step * rows]
             if step == count - 1:
-                summed = jax.nn.gelu(summed, approximate=False)
+                summed = gelu(summed)
             travelling[piece] = summed.astype(jnp.bfloat16)
     return jnp.concatenate(travelling, axis=1)
 

time: 79.7 us -> 80.3 us (level)
  waiting for transfers between devices: 14.8 us -> 33.9 us
  starting transfers between devices: 39.8 us -> 30.4 us
  Pallas kernels: 3.96 us -> 11.8 us
  blocking collectives: 7.82 us -> 0 us
  matrix products: 3.9 us -> 0 us
  other arithmetic: 5.91 us -> 2.77 us
  local copies, waits for them, and re-layouts: 3.08 us -> 1.07 us
    ppermute x14 -> x17, waiting for transfers between devices: 14.8 us -> 33.9 us  [turned(): lax.ppermute(value, axis, [(i, (i + away) % count) for i in range(count)])]
    ppermute x14 -> x17, starting transfers between devices: 39.8 us -> 30.4 us  [turned(): lax.ppermute(value, axis, [(i, (i + away) % count) for i in range(count)])]
    all_gather x1 -> x0, blocking collectives: 7.82 us -> none  [encode(): gathered = lax.all_gather(packed, ('ch', 'sub'), axis=0)]
    pallas_call x0 -> x4, Pallas kernels: none -> 7.76 us  [partial(): pl.pallas_call(partial_kernel, out_shape=(jax.ShapeDtypeStruct((rows, wid...]
    dot_general x4 -> x0, matrix products: 3.9 us -> none  [lift(): jnp.dot(tokens, token_mixing[:, piece * width:(piece + 1) * width], prefe...]
    convert_element_type x12, other arithmetic: 3.85 us -> 0.72 us  [lift(): travelling[piece] = summed.astype(jnp.bfloat16)]
    unnamed x8, local copies, waits for them, and re-layouts: 2.97 us -> 1.05 us
  transfers between devices with their start and end apart: 14 -> 17, of which waited for: 12 -> 13; matrix products, arithmetic and copies ran while one was open for 6% -> 2% of each run, Pallas kernels for 1% -> 8%
where the time goes in v3:
time: 80.3 us; the launch traced here: 80.2 us
  waiting for transfers between devices  33.9 us (42%)
  starting transfers between devices  30.4 us (38%)
  Pallas kernels  11.8 us (15%)
  other arithmetic  2.77 us (3%)
  local copies, waits for them, and re-layouts  1.07 us (1%)
    ppermute x17, waiting for transfers between devices, turned(): lax.ppermute(value, axis, [(i, (i + away) % count) for i in range(count)])  33.9 us
    ppermute x17, starting transfers between devices, turned(): lax.ppermute(value, axis, [(i, (i + away) % count) for i in range(count)])  30.4 us
    pallas_call x4, Pallas kernels, partial(): pl.pallas_call(partial_kernel, out_shape=(jax.ShapeDtypeStruct((rows, wid...  7.76 us
    pallas_call x3, Pallas kernels, call(): pl.pallas_call(kernel, out_shape=out_shape, in_specs=[pl.BlockSpec(memory...  4.05 us
  transfers between devices with their start and end apart: 17, of which 13 were waited for; matrix products, arithmetic and copies ran while one was open for 2% of the time, Pallas kernels for 8%

profile of v3, /device:TPU:0, one launch (start us, length us, event | category | flops | bytes accessed | tf_op | source)
XLA Modules:
  0.0 80.2 jit_solution(9408512894041165488)
XLA Ops:
  0.0 1.0 %copy-done.1 = f32[64,32,32]{0,2,1:T(8,128)S(1)} copy-done((f32[64,32,32]{0,2,1:T(8,128)S(1)}, f32[64,32,32]{0,2,1:T(8,128)}, u32[]{:S(2)}) %copy-start.1) | copy-done | bytes 262168
  1.0 0.1 shard_map.55
  1.2 3.1 %collective-permute-start = (bf16[1,32,128]{2,1,0:T(8,128)(2,1)S(1)}, bf16[1,32,128]{2,1,0:T(8,128)(2,1)S(1)}, u32[]{:S(2)}, u32[]{:S(2)}) collective-permute-start(bf16[1,32,128]{2,1,0:T(8,128)(2,1)S(1)} %get-tuple-element.20), channel_id=1, source_target_pairs={{0,4},{4,8},{8,12},{12,0},{1,5},{5,9},{9,13},{13,1},{2,6},{6,10},{... | collective-permute-start | bytes 24584 | tf_op jit(solution)/shard_map/ppermute | solution.py:149
  4.2 2.1 %collective-permute-start.1 = (bf16[1,32,128]{2,1,0:T(8,128)(2,1)S(1)}, bf16[1,32,128]{2,1,0:T(8,128)(2,1)S(1)}, u32[]{:S(2)}, u32[]{:S(2)}) collective-permute-start(bf16[1,32,128]{2,1,0:T(8,128)(2,1)S(1)} %get-tuple-element.21), channel_id=1, source_target_pairs={{0,12},{4,0},{8,4},{12,8},{1,13},{5,1},{9,5},{13,9},{2,14},{6,2},{... | collective-permute-start | bytes 24584 | tf_op jit(solution)/shard_map/ppermute | solution.py:149
  6.3 1.6 %collective-permute-done = bf16[1,32,128]{2,1,0:T(8,128)(2,1)S(1)} collective-permute-done((bf16[1,32,128]{2,1,0:T(8,128)(2,1)S(1)}, bf16[1,32,128]{2,1,0:T(8,128)(2,1)S(1)}, u32[]{:S(2)}, u32[]{:S(2)}) %collective-permute-start) | collective-permute-done | bytes 8224 | tf_op jit(solution)/shard_map/ppermute | solution.py:149
  8.0 0.0 collective-permute-done.1
  8.0 1.7 %collective-permute-start.3 = (bf16[18,32,128]{2,1,0:T(8,128)(2,1)S(1)}, bf16[18,32,128]{2,1,0:T(8,128)(2,1)S(1)}, u32[]{:S(2)}, u32[]{:S(2)}) collective-permute-start(bf16[18,32,128]{2,1,0:T(8,128)(2,1)S(1)} %constant_dynamic-update-slice_fusion.refs_0_), channel_id=1, source_target_pairs={{0,2},{2,0},{1,3},{3,1},{4,6},{6,4},{5,7},{7,5},{8,10},{10,8},{9,1... | collective-permute-start | bytes 442376 | tf_op jit(solution)/shard_map/ppermute | solution.py:149
  9.7 0.0 collective-permute-start.2
  9.7 3.5 %collective-permute-done.3.refs_2_ = bf16[18,32,128]{2,1,0:T(8,128)(2,1)S(1)} collective-permute-done((bf16[18,32,128]{2,1,0:T(8,128)(2,1)S(1)}, bf16[18,32,128]{2,1,0:T(8,128)(2,1)S(1)}, u32[]{:S(2)}, u32[]{:S(2)}) %collective-permute-start.3) | collective-permute-done | bytes 147488 | tf_op jit(solution)/shard_map/ppermute | solution.py:149
  13.2 0.0 collective-permute-start.4
  13.2 1.1 %fusion.embed_ref = bf16[256,384]{1,0:T(8,128)(2,1)S(1)} fusion(s32[]{:T(128)S(6)} %select_n.11, bf16[256,384]{1,0:T(8,128)(2,1)} %param.8), kind=kLoop, calls=%fused_computation.15 | loop fusion | flops 393216 | bytes 393220 | tf_op jit(solution)/shard_map/concatenate | solution.py:254
  14.3 0.0 copy-start
  14.4 0.5 shard_map.56
  14.9 0.0 collective-permute-done.4.refs_3_
  14.9 3.4 %shard_map.57.tokens_ref = bf16[384,1024]{1,0:T(8,128)(2,1)S(1)} custom-call(bf16[18,32,128]{2,1,0:T(8,128)(2,1)S(1)} %constant_dynamic-update-slice_fusion.refs_0_, bf16[18,32,128]{2,1,0:T(8,128)(2,1)S(1)} %collective-permute-done.2.refs_1_, bf16[18,32,128]{2,1,0:T(8,128)(2,1)S(1)} %collective-permute-done.3.refs_2_, ...), custom_call_target="tpu_custom_call" | custom-call | flops 2139095040 | bytes 589824 | tf_op jit(solution)/shard_map/pallas_call | solution.py:136
  18.3 1.9 %shard_map.61 = (bf16[96,1024]{1,0:T(8,128)(2,1)S(1)}, f32[288,1024]{1,0:T(8,128)S(1)}) custom-call(bf16[384,1024]{1,0:T(8,128)(2,1)S(1)} %shard_map.57.tokens_ref, bf16[1024,4096]{1,0:T(8,128)(2,1)S(1)} %copy-done), custom_call_target="tpu_custom_call" | custom-call | tf_op jit(solution)/shard_map/pallas_call | solution.py:210
  20.3 3.8 %collective-permute-start.14 = (bf16[96,1024]{1,0:T(8,128)(2,1)S(1)}, bf16[96,1024]{1,0:T(8,128)(2,1)S(1)}, u32[]{:S(2)}, u32[]{:S(2)}) collective-permute-start(bf16[96,1024]{1,0:T(8,128)(2,1)S(1)} %get-tuple-element.31), channel_id=1, source_target_pairs={{0,12},{4,0},{8,4},{12,8},{1,13},{5,1},{9,5},{13,9},{2,14},{6,2},{... | collective-permute-start | bytes 589832 | tf_op jit(solution)/shard_map/ppermute | solution.py:149
  24.1 1.9 %shard_map.60 = (bf16[96,1024]{1,0:T(8,128)(2,1)S(1)}, f32[288,1024]{1,0:T(8,128)S(1)}) custom-call(bf16[384,1024]{1,0:T(8,128)(2,1)S(1)} %shard_map.57.tokens_ref, bf16[1024,4096]{1,0:T(8,128)(2,1)S(1)} %copy-done), custom_call_target="tpu_custom_call" | custom-call | tf_op jit(solution)/shard_map/pallas_call | solution.py:210
  26.0 1.9 %shard_map.59 = (bf16[96,1024]{1,0:T(8,128)(2,1)S(1)}, f32[288,1024]{1,0:T(8,128)S(1)}) custom-call(bf16[384,1024]{1,0:T(8,128)(2,1)S(1)} %shard_map.57.tokens_ref, bf16[1024,4096]{1,0:T(8,128)(2,1)S(1)} %copy-done), custom_call_target="tpu_custom_call" | custom-call | tf_op jit(solution)/shard_map/pallas_call | solution.py:210
  28.0 1.9 %shard_map.58 = (bf16[96,1024]{1,0:T(8,128)(2,1)S(1)}, f32[288,1024]{1,0:T(8,128)S(1)}) custom-call(bf16[384,1024]{1,0:T(8,128)(2,1)S(1)} %shard_map.57.tokens_ref, bf16[1024,4096]{1,0:T(8,128)(2,1)S(1)} %copy-done), custom_call_target="tpu_custom_call" | custom-call | tf_op jit(solution)/shard_map/pallas_call | solution.py:210
  29.9 0.3 collective-permute-start.11
  30.2 0.4 collective-permute-start.8
  30.6 0.6 collective-permute-start.5
  31.2 0.0 collective-permute-done.14
  31.2 3.8 %collective-permute-start.15 = (bf16[96,1024]{1,0:T(8,128)(2,1)S(1)}, bf16[96,1024]{1,0:T(8,128)(2,1)S(1)}, u32[]{:S(2)}, u32[]{:S(2)}) collective-permute-start(bf16[96,1024]{1,0:T(8,128)(2,1)S(1)} %add_convert_fusion.1), channel_id=1, source_target_pairs={{0,12},{4,0},{8,4},{12,8},{1,13},{5,1},{9,5},{13,9},{2,14},{6,2},{... | collective-permute-start | bytes 589832 | tf_op jit(solution)/shard_map/ppermute | solution.py:149
  35.0 2.7 %collective-permute-done.11 = bf16[96,1024]{1,0:T(8,128)(2,1)S(1)} collective-permute-done((bf16[96,1024]{1,0:T(8,128)(2,1)S(1)}, bf16[96,1024]{1,0:T(8,128)(2,1)S(1)}, u32[]{:S(2)}, u32[]{:S(2)}) %collective-permute-start.11) | collective-permute-done | bytes 196640 | tf_op jit(solution)/shard_map/ppermute | solution.py:149
  37.7 2.1 %collective-permute-start.12 = (bf16[96,1024]{1,0:T(8,128)(2,1)S(1)}, bf16[96,1024]{1,0:T(8,128)(2,1)S(1)}, u32[]{:S(2)}, u32[]{:S(2)}) collective-permute-start(bf16[96,1024]{1,0:T(8,128)(2,1)S(1)} %add_convert_fusion.3), channel_id=1, source_target_pairs={{0,12},{4,0},{8,4},{12,8},{1,13},{5,1},{9,5},{13,9},{2,14},{6,2},{... | collective-permute-start | bytes 589832 | tf_op jit(solution)/shard_map/ppermute | solution.py:149
  39.8 2.1 %collective-permute-done.8 = bf16[96,1024]{1,0:T(8,128)(2,1)S(1)} collective-permute-done((bf16[96,1024]{1,0:T(8,128)(2,1)S(1)}, bf16[96,1024]{1,0:T(8,128)(2,1)S(1)}, u32[]{:S(2)}, u32[]{:S(2)}) %collective-permute-start.8) | collective-permute-done | bytes 196640 | tf_op jit(solution)/shard_map/ppermute | solution.py:149
  42.0 2.1 %collective-permute-start.9 = (bf16[96,1024]{1,0:T(8,128)(2,1)S(1)}, bf16[96,1024]{1,0:T(8,128)(2,1)S(1)}, u32[]{:S(2)}, u32[]{:S(2)}) collective-permute-start(bf16[96,1024]{1,0:T(8,128)(2,1)S(1)} %add_convert_fusion.5), channel_id=1, source_target_pairs={{0,12},{4,0},{8,4},{12,8},{1,13},{5,1},{9,5},{13,9},{2,14},{6,2},{... | collective-permute-start | bytes 589832 | tf_op jit(solution)/shard_map/ppermute | solution.py:149
  44.1 2.1 %collective-permute-done.5 = bf16[96,1024]{1,0:T(8,128)(2,1)S(1)} collective-permute-done((bf16[96,1024]{1,0:T(8,128)(2,1)S(1)}, bf16[96,1024]{1,0:T(8,128)(2,1)S(1)}, u32[]{:S(2)}, u32[]{:S(2)}) %collective-permute-start.5) | collective-permute-done | bytes 196640 | tf_op jit(solution)/shard_map/ppermute | solution.py:149
  46.2 2.1 %collective-permute-start.6 = (bf16[96,1024]{1,0:T(8,128)(2,1)S(1)}, bf16[96,1024]{1,0:T(8,128)(2,1)S(1)}, u32[]{:S(2)}, u32[]{:S(2)}) collective-permute-start(bf16[96,1024]{1,0:T(8,128)(2,1)S(1)} %add_convert_fusion.7), channel_id=1, source_target_pairs={{0,12},{4,0},{8,4},{12,8},{1,13},{5,1},{9,5},{13,9},{2,14},{6,2},{... | collective-permute-start | bytes 589832 | tf_op jit(solution)/shard_map/ppermute | solution.py:149
  48.3 2.1 %collective-permute-done.15 = bf16[96,1024]{1,0:T(8,128)(2,1)S(1)} collective-permute-done((bf16[96,1024]{1,0:T(8,128)(2,1)S(1)}, bf16[96,1024]{1,0:T(8,128)(2,1)S(1)}, u32[]{:S(2)}, u32[]{:S(2)}) %collective-permute-start.15) | collective-permute-done | bytes 196640 | tf_op jit(solution)/shard_map/ppermute | solution.py:149
  50.4 2.1 %collective-permute-start.16 = (bf16[96,1024]{1,0:T(8,128)(2,1)S(1)}, bf16[96,1024]{1,0:T(8,128)(2,1)S(1)}, u32[]{:S(2)}, u32[]{:S(2)}) collective-permute-start(bf16[96,1024]{1,0:T(8,128)(2,1)S(1)} %add_convert_fusion), channel_id=1, source_target_pairs={{0,12},{4,0},{8,4},{12,8},{1,13},{5,1},{9,5},{13,9},{2,14},{6,2},{... | collective-permute-start | bytes 589832 | tf_op jit(solution)/shard_map/ppermute | solution.py:149
  52.5 2.1 %collective-permute-done.12 = bf16[96,1024]{1,0:T(8,128)(2,1)S(1)} collective-permute-done((bf16[96,1024]{1,0:T(8,128)(2,1)S(1)}, bf16[96,1024]{1,0:T(8,128)(2,1)S(1)}, u32[]{:S(2)}, u32[]{:S(2)}) %collective-permute-start.12) | collective-permute-done | bytes 196640 | tf_op jit(solution)/shard_map/ppermute | solution.py:149
  54.6 2.1 %collective-permute-start.13 = (bf16[96,1024]{1,0:T(8,128)(2,1)S(1)}, bf16[96,1024]{1,0:T(8,128)(2,1)S(1)}, u32[]{:S(2)}, u32[]{:S(2)}) collective-permute-start(bf16[96,1024]{1,0:T(8,128)(2,1)S(1)} %add_convert_fusion.2), channel_id=1, source_target_pairs={{0,12},{4,0},{8,4},{12,8},{1,13},{5,1},{9,5},{13,9},{2,14},{6,2},{... | collective-permute-start | bytes 589832 | tf_op jit(solution)/shard_map/ppermute | solution.py:149
  56.7 2.1 %collective-permute-done.9 = bf16[96,1024]{1,0:T(8,128)(2,1)S(1)} collective-permute-done((bf16[96,1024]{1,0:T(8,128)(2,1)S(1)}, bf16[96,1024]{1,0:T(8,128)(2,1)S(1)}, u32[]{:S(2)}, u32[]{:S(2)}) %collective-permute-start.9) | collective-permute-done | bytes 196640 | tf_op jit(solution)/shard_map/ppermute | solution.py:149
  58.8 2.1 %collective-permute-start.10 = (bf16[96,1024]{1,0:T(8,128)(2,1)S(1)}, bf16[96,1024]{1,0:T(8,128)(2,1)S(1)}, u32[]{:S(2)}, u32[]{:S(2)}) collective-permute-start(bf16[96,1024]{1,0:T(8,128)(2,1)S(1)} %add_convert_fusion.4), channel_id=1, source_target_pairs={{0,12},{4,0},{8,4},{12,8},{1,13},{5,1},{9,5},{13,9},{2,14},{6,2},{... | collective-permute-start | bytes 589832 | tf_op jit(solution)/shard_map/ppermute | solution.py:149
  60.9 2.1 %collective-permute-done.6 = bf16[96,1024]{1,0:T(8,128)(2,1)S(1)} collective-permute-done((bf16[96,1024]{1,0:T(8,128)(2,1)S(1)}, bf16[96,1024]{1,0:T(8,128)(2,1)S(1)}, u32[]{:S(2)}, u32[]{:S(2)}) %collective-permute-start.6) | collective-permute-done | bytes 196640 | tf_op jit(solution)/shard_map/ppermute | solution.py:149
  63.0 2.1 %collective-permute-start.7 = (bf16[96,1024]{1,0:T(8,128)(2,1)S(1)}, bf16[96,1024]{1,0:T(8,128)(2,1)S(1)}, u32[]{:S(2)}, u32[]{:S(2)}) collective-permute-start(bf16[96,1024]{1,0:T(8,128)(2,1)S(1)} %add_convert_fusion.6), channel_id=1, source_target_pairs={{0,12},{4,0},{8,4},{12,8},{1,13},{5,1},{9,5},{13,9},{2,14},{6,2},{... | collective-permute-start | bytes 589832 | tf_op jit(solution)/shard_map/ppermute | solution.py:149
  65.1 2.1 %collective-permute-done.16 = bf16[96,1024]{1,0:T(8,128)(2,1)S(1)} collective-permute-done((bf16[96,1024]{1,0:T(8,128)(2,1)S(1)}, bf16[96,1024]{1,0:T(8,128)(2,1)S(1)}, u32[]{:S(2)}, u32[]{:S(2)}) %collective-permute-start.16) | collective-permute-done | bytes 196640 | tf_op jit(solution)/shard_map/ppermute | solution.py:149
  67.2 0.1 multiply_convert_fusion
  67.3 4.1 %collective-permute-done.13 = bf16[96,1024]{1,0:T(8,128)(2,1)S(1)} collective-permute-done((bf16[96,1024]{1,0:T(8,128)(2,1)S(1)}, bf16[96,1024]{1,0:T(8,128)(2,1)S(1)}, u32[]{:S(2)}, u32[]{:S(2)}) %collective-permute-start.13) | collective-permute-done | bytes 196640 | tf_op jit(solution)/shard_map/ppermute | solution.py:149
  71.4 0.1 multiply_convert_fusion.1
  71.5 4.1 %collective-permute-done.10 = bf16[96,1024]{1,0:T(8,128)(2,1)S(1)} collective-permute-done((bf16[96,1024]{1,0:T(8,128)(2,1)S(1)}, bf16[96,1024]{1,0:T(8,128)(2,1)S(1)}, u32[]{:S(2)}, u32[]{:S(2)}) %collective-permute-start.10) | collective-permute-done | bytes 196640 | tf_op jit(solution)/shard_map/ppermute | solution.py:149
  75.6 0.1 multiply_convert_fusion.2
  75.7 3.4 %collective-permute-done.7 = bf16[96,1024]{1,0:T(8,128)(2,1)S(1)} collective-permute-done((bf16[96,1024]{1,0:T(8,128)(2,1)S(1)}, bf16[96,1024]{1,0:T(8,128)(2,1)S(1)}, u32[]{:S(2)}, u32[]{:S(2)}) %collective-permute-start.7) | collective-permute-done | bytes 196640 | tf_op jit(solution)/shard_map/ppermute | solution.py:149
  79.1 0.1 multiply_convert_fusion.3
  79.2 0.9 %pad_maximum_fusion = bf16[96,4096]{1,0:T(8,128)(2,1)} fusion(bf16[96,1024]{1,0:T(8,128)(2,1)S(1)} %multiply_convert_fusion, bf16[96,1024]{1,0:T(8,128)(2,1)S(1)} %multiply_convert_fusion.1, bf16[96,1024]{1,0:T(8,128)(2,1)S(1)} %multiply_convert_fusion.2, bf16[96,1024]{1,0:T(8,128)(2,1)S(1)} %multiply_convert_fusion.3), kind=kLoop, calls=%fused_computation | loop fusion | flops 3145728 | bytes 1572864 | tf_op jit(solution)/shard_map/concatenate | solution.py:246
  (17 shorter events, 0.3 us)
Async XLA Ops:
  0.0 1.0 %copy-start.1 = (f32[64,32,32]{0,2,1:T(8,128)S(1)}, f32[64,32,32]{0,2,1:T(8,128)}, u32[]{:S(2)}) copy-start(f32[64,32,32]{0,2,1:T(8,128)} %param.5) | copy-start | bytes 786436
  1.0 13.3 %copy-start.2 = (f32[9,64,64]{2,1,0:T(8,128)S(1)}, f32[9,64,64]{2,1,0:T(8,128)}, u32[]{:S(2)}) copy-start(f32[9,64,64]{2,1,0:T(8,128)} %first_ref.1) | copy-start | bytes 442372
  1.0 13.3 %copy-start.3 = (f32[9,64,64]{2,1,0:T(8,128)S(1)}, f32[9,64,64]{2,1,0:T(8,128)}, u32[]{:S(2)}) copy-start(f32[9,64,64]{2,1,0:T(8,128)} %second_ref.1) | copy-start | bytes 442372
  1.2 6.8 %collective-permute-start = (bf16[1,32,128]{2,1,0:T(8,128)(2,1)S(1)}, bf16[1,32,128]{2,1,0:T(8,128)(2,1)S(1)}, u32[]{:S(2)}, u32[]{:S(2)}) collective-permute-start(bf16[1,32,128]{2,1,0:T(8,128)(2,1)S(1)} %get-tuple-element.20), channel_id=1, source_target_pairs={{0,4},{4,8},{8,12},{12,0},{1,5},{5,9},{9,13},{13,1},{2,6},{6,10},{... | collective-permute-start | bytes 24584 | tf_op jit(solution)/shard_map/ppermute | solution.py:149
  4.2 3.8 %collective-permute-start.1 = (bf16[1,32,128]{2,1,0:T(8,128)(2,1)S(1)}, bf16[1,32,128]{2,1,0:T(8,128)(2,1)S(1)}, u32[]{:S(2)}, u32[]{:S(2)}) collective-permute-start(bf16[1,32,128]{2,1,0:T(8,128)(2,1)S(1)} %get-tuple-element.21), channel_id=1, source_target_pairs={{0,12},{4,0},{8,4},{12,8},{1,13},{5,1},{9,5},{13,9},{2,14},{6,2},{... | collective-permute-start | bytes 24584 | tf_op jit(solution)/shard_map/ppermute | solution.py:149
  8.0 5.2 %collective-permute-start.3 = (bf16[18,32,128]{2,1,0:T(8,128)(2,1)S(1)}, bf16[18,32,128]{2,1,0:T(8,128)(2,1)S(1)}, u32[]{:S(2)}, u32[]{:S(2)}) collective-permute-start(bf16[18,32,128]{2,1,0:T(8,128)(2,1)S(1)} %constant_dynamic-update-slice_fusion.refs_0_), channel_id=1, source_target_pairs={{0,2},{2,0},{1,3},{3,1},{4,6},{6,4},{5,7},{7,5},{8,10},{10,8},{9,1... | collective-permute-start | bytes 442376 | tf_op jit(solution)/shard_map/ppermute | solution.py:149
  9.7 5.2 %collective-permute-start.2 = (bf16[18,32,128]{2,1,0:T(8,128)(2,1)S(1)}, bf16[18,32,128]{2,1,0:T(8,128)(2,1)S(1)}, u32[]{:S(2)}, u32[]{:S(2)}) collective-permute-start(bf16[18,32,128]{2,1,0:T(8,128)(2,1)S(1)} %constant_dynamic-update-slice_fusion.refs_0_), channel_id=1, source_target_pairs={{0,1},{1,0},{2,3},{3,2},{4,5},{5,4},{6,7},{7,6},{8,9},{9,8},{10,11... | collective-permute-start | bytes 442376 | tf_op jit(solution)/shard_map/ppermute | solution.py:149
  13.2 1.7 %collective-permute-start.4 = (bf16[18,32,128]{2,1,0:T(8,128)(2,1)S(1)}, bf16[18,32,128]{2,1,0:T(8,128)(2,1)S(1)}, u32[]{:S(2)}, u32[]{:S(2)}) collective-permute-start(bf16[18,32,128]{2,1,0:T(8,128)(2,1)S(1)} %collective-permute-done.3.refs_2_), channel_id=1, source_target_pairs={{0,1},{1,0},{2,3},{3,2},{4,5},{5,4},{6,7},{7,6},{8,9},{9,8},{10,11... | collective-permute-start | bytes 442376 | tf_op jit(solution)/shard_map/ppermute | solution.py:149
  14.3 4.0 %copy-start = (bf16[1024,4096]{1,0:T(8,128)(2,1)S(1)}, bf16[1024,4096]{1,0:T(8,128)(2,1)}, u32[]{:S(2)}) copy-start(bf16[1024,4096]{1,0:T(8,128)(2,1)} %mixing_ref.7) | copy-start | bytes 25165828
  20.3 10.9 %collective-permute-start.14 = (bf16[96,1024]{1,0:T(8,128)(2,1)S(1)}, bf16[96,1024]{1,0:T(8,128)(2,1)S(1)}, u32[]{:S(2)}, u32[]{:S(2)}) collective-permute-start(bf16[96,1024]{1,0:T(8,128)(2,1)S(1)} %get-tuple-element.31), channel_id=1, source_target_pairs={{0,12},{4,0},{8,4},{12,8},{1,13},{5,1},{9,5},{13,9},{2,14},{6,2},{... | collective-permute-start | bytes 589832 | tf_op jit(solution)/shard_map/ppermute | solution.py:149
  29.9 7.8 %collective-permute-start.11 = (bf16[96,1024]{1,0:T(8,128)(2,1)S(1)}, bf16[96,1024]{1,0:T(8,128)(2,1)S(1)}, u32[]{:S(2)}, u32[]{:S(2)}) collective-permute-start(bf16[96,1024]{1,0:T(8,128)(2,1)S(1)} %get-tuple-element.29), channel_id=1, source_target_pairs={{0,12},{4,0},{8,4},{12,8},{1,13},{5,1},{9,5},{13,9},{2,14},{6,2},{... | collective-permute-start | bytes 589832 | tf_op jit(solution)/shard_map/ppermute | solution.py:149
  30.2 11.7 %collective-permute-start.8 = (bf16[96,1024]{1,0:T(8,128)(2,1)S(1)}, bf16[96,1024]{1,0:T(8,128)(2,1)S(1)}, u32[]{:S(2)}, u32[]{:S(2)}) collective-permute-start(bf16[96,1024]{1,0:T(8,128)(2,1)S(1)} %get-tuple-element.27), channel_id=1, source_target_pairs={{0,12},{4,0},{8,4},{12,8},{1,13},{5,1},{9,5},{13,9},{2,14},{6,2},{... | collective-permute-start | bytes 589832 | tf_op jit(solution)/shard_map/ppermute | solution.py:149
  30.6 15.5 %collective-permute-start.5 = (bf16[96,1024]{1,0:T(8,128)(2,1)S(1)}, bf16[96,1024]{1,0:T(8,128)(2,1)S(1)}, u32[]{:S(2)}, u32[]{:S(2)}) collective-permute-start(bf16[96,1024]{1,0:T(8,128)(2,1)S(1)} %get-tuple-element.25), channel_id=1, source_target_pairs={{0,12},{4,0},{8,4},{12,8},{1,13},{5,1},{9,5},{13,9},{2,14},{6,2},{... | collective-permute-start | bytes 589832 | tf_op jit(solution)/shard_map/ppermute | solution.py:149
  31.2 19.1 %collective-permute-start.15 = (bf16[96,1024]{1,0:T(8,128)(2,1)S(1)}, bf16[96,1024]{1,0:T(8,128)(2,1)S(1)}, u32[]{:S(2)}, u32[]{:S(2)}) collective-permute-start(bf16[96,1024]{1,0:T(8,128)(2,1)S(1)} %add_convert_fusion.1), channel_id=1, source_target_pairs={{0,12},{4,0},{8,4},{12,8},{1,13},{5,1},{9,5},{13,9},{2,14},{6,2},{... | collective-permute-start | bytes 589832 | tf_op jit(solution)/shard_map/ppermute | solution.py:149
  37.7 16.8 %collective-permute-start.12 = (bf16[96,1024]{1,0:T(8,128)(2,1)S(1)}, bf16[96,1024]{1,0:T(8,128)(2,1)S(1)}, u32[]{:S(2)}, u32[]{:S(2)}) collective-permute-start(bf16[96,1024]{1,0:T(8,128)(2,1)S(1)} %add_convert_fusion.3), channel_id=1, source_target_pairs={{0,12},{4,0},{8,4},{12,8},{1,13},{5,1},{9,5},{13,9},{2,14},{6,2},{... | collective-permute-start | bytes 589832 | tf_op jit(solution)/shard_map/ppermute | solution.py:149
  42.0 16.8 %collective-permute-start.9 = (bf16[96,1024]{1,0:T(8,128)(2,1)S(1)}, bf16[96,1024]{1,0:T(8,128)(2,1)S(1)}, u32[]{:S(2)}, u32[]{:S(2)}) collective-permute-start(bf16[96,1024]{1,0:T(8,128)(2,1)S(1)} %add_convert_fusion.5), channel_id=1, source_target_pairs={{0,12},{4,0},{8,4},{12,8},{1,13},{5,1},{9,5},{13,9},{2,14},{6,2},{... | collective-permute-start | bytes 589832 | tf_op jit(solution)/shard_map/ppermute | solution.py:149
  46.2 16.8 %collective-permute-start.6 = (bf16[96,1024]{1,0:T(8,128)(2,1)S(1)}, bf16[96,1024]{1,0:T(8,128)(2,1)S(1)}, u32[]{:S(2)}, u32[]{:S(2)}) collective-permute-start(bf16[96,1024]{1,0:T(8,128)(2,1)S(1)} %add_convert_fusion.7), channel_id=1, source_target_pairs={{0,12},{4,0},{8,4},{12,8},{1,13},{5,1},{9,5},{13,9},{2,14},{6,2},{... | collective-permute-start | bytes 589832 | tf_op jit(solution)/shard_map/ppermute | solution.py:149
  50.4 16.8 %collective-permute-start.16 = (bf16[96,1024]{1,0:T(8,128)(2,1)S(1)}, bf16[96,1024]{1,0:T(8,128)(2,1)S(1)}, u32[]{:S(2)}, u32[]{:S(2)}) collective-permute-start(bf16[96,1024]{1,0:T(8,128)(2,1)S(1)} %add_convert_fusion), channel_id=1, source_target_pairs={{0,12},{4,0},{8,4},{12,8},{1,13},{5,1},{9,5},{13,9},{2,14},{6,2},{... | collective-permute-start | bytes 589832 | tf_op jit(solution)/shard_map/ppermute | solution.py:149
  54.6 16.8 %collective-permute-start.13 = (bf16[96,1024]{1,0:T(8,128)(2,1)S(1)}, bf16[96,1024]{1,0:T(8,128)(2,1)S(1)}, u32[]{:S(2)}, u32[]{:S(2)}) collective-permute-start(bf16[96,1024]{1,0:T(8,128)(2,1)S(1)} %add_convert_fusion.2), channel_id=1, source_target_pairs={{0,12},{4,0},{8,4},{12,8},{1,13},{5,1},{9,5},{13,9},{2,14},{6,2},{... | collective-permute-start | bytes 589832 | tf_op jit(solution)/shard_map/ppermute | solution.py:149
  58.8 16.8 %collective-permute-start.10 = (bf16[96,1024]{1,0:T(8,128)(2,1)S(1)}, bf16[96,1024]{1,0:T(8,128)(2,1)S(1)}, u32[]{:S(2)}, u32[]{:S(2)}) collective-permute-start(bf16[96,1024]{1,0:T(8,128)(2,1)S(1)} %add_convert_fusion.4), channel_id=1, source_target_pairs={{0,12},{4,0},{8,4},{12,8},{1,13},{5,1},{9,5},{13,9},{2,14},{6,2},{... | collective-permute-start | bytes 589832 | tf_op jit(solution)/shard_map/ppermute | solution.py:149
  63.0 16.1 %collective-permute-start.7 = (bf16[96,1024]{1,0:T(8,128)(2,1)S(1)}, bf16[96,1024]{1,0:T(8,128)(2,1)S(1)}, u32[]{:S(2)}, u32[]{:S(2)}) collective-permute-start(bf16[96,1024]{1,0:T(8,128)(2,1)S(1)} %add_convert_fusion.6), channel_id=1, source_target_pairs={{0,12},{4,0},{8,4},{12,8},{1,13},{5,1},{9,5},{13,9},{2,14},{6,2},{... | collective-permute-start | bytes 589832 | tf_op jit(solution)/shard_map/ppermute | solution.py:149

commit v4 on v3

--- a/solution.py
+++ b/solution.py
@@ -1,4 +1,5 @@
 import functools
+import itertools
 
 import jax
 import jax.numpy as jnp
@@ -18,7 +19,7 @@
     lon, lat, chans = field_ref.shape
     pairs = field_ref[...].reshape(lon // 2, 2, lat, chans)
     joined = jnp.concatenate([pairs[:, 0], pairs[:, 1]], axis=-1).astype(packed_ref.dtype)
-    packed_ref[pl.ds(1, lon // 2)] = joined
+    packed_ref[...] = joined
     low_ref[...] = joined[:1]
     high_ref[...] = joined[-1:]
 
@@ -45,11 +46,15 @@
         target[0] = upper
         target[1] = lower
     chans = embed_ref.shape[0] // 4
-    for first in range(0, embed_ref.shape[1], LANES):
-        scratch[...] = embed_ref[:, pl.ds(first, LANES)].astype(jnp.float32)
+    embed = embed_ref.shape[1]
+    count = lax.axis_size("tok")
+    turn = lax.rem(lax.axis_index("tok") + 1, count) * (embed // count)
+    turned_embed = pltpu.roll(embed_ref[...].astype(jnp.float32), lax.rem(embed - turn, embed), axis=1)
+    for first in range(0, embed, LANES):
+        scratch[...] = turned_embed[:, first : first + LANES]
         ordered = [scratch[pl.ds(2 * a + b, chans, stride=4), :] for b in range(2) for a in range(2)]
-        turned = jnp.concatenate(ordered, axis=0).T
-        embed_out_ref[pl.ds(first, LANES), :] = turned.astype(embed_out_ref.dtype)
+        rows = jnp.concatenate(ordered, axis=0).T
+        embed_out_ref[pl.ds(first, LANES), :] = rows.astype(embed_out_ref.dtype)
 
 
 def pairs_at_once(pairs, lat):
@@ -90,8 +95,8 @@
 
 def encode_kernel(count_ch, count_sub, *refs):
     count = count_ch * count_sub
-    blocks = refs[:count]
-    taps_one_ref, taps_two_ref, embed_ref, tokens_ref, field_ref, upper_ref, lower_ref, two_ref = refs[count:]
+    blocks, befores, afters = refs[:count], refs[count : 2 * count], refs[2 * count : 3 * count]
+    taps_one_ref, taps_two_ref, embed_ref, tokens_ref, field_ref, upper_ref, lower_ref, two_ref = refs[3 * count :]
     pairs, lat, wide = field_ref.shape
     width = lat // count
     last = pairs - 1
@@ -100,7 +105,10 @@
             at_ch = lax.rem(lax.axis_index("ch") + count_ch - away_ch, count_ch)
             at_sub = lax.rem(lax.axis_index("sub") + count_sub - away_sub, count_sub)
             start = pl.multiple_of((at_ch * count_sub + at_sub) * width, width)
-            field_ref[:, pl.ds(start, width), :] = blocks[away_ch * count_sub + away_sub][...]
+            away = away_ch * count_sub + away_sub
+            field_ref[pl.ds(1, pairs - 2), pl.ds(start, width), :] = blocks[away][...]
+            field_ref[pl.ds(0, 1), pl.ds(start, width), :] = befores[away][...]
+            field_ref[pl.ds(pairs - 1, 1), pl.ds(start, width), :] = afters[away][...]
 
     def field_of(pair):
         return field_ref[pair]
@@ -144,20 +152,25 @@
     )(*inputs)
 
 
-def turned(value, axis, away):
-    count = lax.axis_size(axis)
-    return lax.ppermute(value, axis, [(i, (i + away) % count) for i in range(count)])
-
-
-def gather_blocks(block):
-    rows = [block]
-    for away in range(1, lax.axis_size("ch")):
-        rows.append(turned(block, "ch", away))
+def turned(value, steps):
+    axes = tuple(steps)
+    sizes = [lax.axis_size(axis) for axis in axes]
+    sources = list(itertools.product(*[range(size) for size in sizes]))
+    place = {source: number for number, source in enumerate(sources)}
+    route = []
+    for source in sources:
+        target = tuple((at + steps[axis]) % size for at, axis, size in zip(source, axes, sizes))
+        route.append((place[source], place[target]))
+    return lax.ppermute(value, axes, route)
+
+
+def band_blocks(block, steps):
     blocks = []
-    for row in rows:
-        blocks.append(row)
-        for away in range(1, lax.axis_size("sub")):
-            blocks.append(turned(row, "sub", away))
+    for away_ch in range(lax.axis_size("ch")):
+        for away_sub in range(lax.axis_size("sub")):
+            moves = dict(steps, ch=away_ch, sub=away_sub)
+            moves = {axis: step for axis, step in moves.items() if step != 0}
+            blocks.append(turned(block, moves) if moves else block)
     return blocks
 
 
@@ -168,12 +181,10 @@
     shape = functools.partial(jax.ShapeDtypeStruct, dtype=jnp.bfloat16)
     low, high, packed = call(
         pack_kernel,
-        (shape((1, lat, wide)), shape((1, lat, wide)), shape((pairs + 2, lat, wide))),
+        (shape((1, lat, wide)), shape((1, lat, wide)), shape((pairs, lat, wide))),
         (jnp.transpose(weather, (1, 2, 0)),),
         moved=weather.size * 10,
     )
-    before = turned(high, "tok", 1)
-    after = turned(low, "tok", -1)
     taps = shape((2, 4 * chans, 6 * chans))
     taps_one, taps_two, embed_rows = call(
         weights_kernel,
@@ -182,49 +193,40 @@
         scratch=[pltpu.VMEM((patch_embed.shape[0], LANES), jnp.float32)],
         moved=conv_first.size * 20,
     )
-    packed = lax.dynamic_update_slice_in_dim(packed, before, 0, 0)
-    packed = lax.dynamic_update_slice_in_dim(packed, after, pairs + 1, 0)
-    blocks = gather_blocks(packed)
+    blocks = band_blocks(packed, {})
+    befores = band_blocks(high, {"tok": 1})
+    afters = band_blocks(low, {"tok": -1})
     full_lat = len(blocks) * lat
     held = pltpu.VMEM((pairs + 2, full_lat, wide), jnp.bfloat16)
     return call(
         functools.partial(encode_kernel, lax.axis_size("ch"), lax.axis_size("sub")),
         shape((embed, pairs * full_lat // 2)),
-        (*blocks, taps_one, taps_two, embed_rows),
+        (*blocks, *befores, *afters, taps_one, taps_two, embed_rows),
         scratch=[held, held, held, pltpu.VMEM((pairs * full_lat, wide), jnp.float32)],
         flops=2 * (pairs + 1) * full_lat * 4 * chans * 6 * chans * 5,
         moved=packed.size * 2 * len(blocks),
     )
 
 
-def partial_kernel(tokens_ref, mixing_ref, sent_ref, kept_ref):
-    product = jnp.dot(tokens_ref[...], mixing_ref[...], preferred_element_type=jnp.float32)
-    rows = sent_ref.shape[0]
-    sent_ref[...] = product[:rows].astype(sent_ref.dtype)
-    kept_ref[...] = product[rows:]
+def partial_kernel(first, tokens_ref, mixing_ref, sent_ref, kept_ref):
+    rows, width = sent_ref.shape
+    step = STEP if width % STEP == 0 else width
+    tokens = tokens_ref[...]
+    for at in range(0, width, step):
+        product = jnp.dot(tokens, mixing_ref[:, pl.ds(first + at, step)], preferred_element_type=jnp.float32)
+        sent_ref[:, pl.ds(at, step)] = product[:rows].astype(sent_ref.dtype)
+        kept_ref[:, pl.ds(at, step)] = product[rows:]
 
 
 def partial(tokens, token_mixing, first, width, rows):
-    embed, count = tokens.shape
-    step = STEP if width % STEP == 0 else width
-    return pl.pallas_call(
-        partial_kernel,
-        out_shape=(
+    return call(
+        functools.partial(partial_kernel, first),
+        (
             jax.ShapeDtypeStruct((rows, width), jnp.bfloat16),
-            jax.ShapeDtypeStruct((embed - rows, width), jnp.float32),
+            jax.ShapeDtypeStruct((tokens.shape[0] - rows, width), jnp.float32),
         ),
-        grid=(width // step,),
-        in_specs=[
-            pl.BlockSpec(memory_space=pltpu.VMEM),
-            pl.BlockSpec((count, step), lambda i: (0, first // step + i)),
-        ],
-        out_specs=(
-            pl.BlockSpec((rows, step), lambda i: (0, i)),
-            pl.BlockSpec((embed - rows, step), lambda i: (0, i)),
-        ),
-        compiler_params=pltpu.CompilerParams(vmem_limit_bytes=VMEM_BYTES),
-        cost_estimate=pl.CostEstimate(flops=0, bytes_accessed=0, transcendentals=0),
-    )(tokens, token_mixing)
+        (tokens, token_mixing),
+    )
 
 
 def lift(tokens, token_mixing, pieces):
@@ -238,7 +240,7 @@
         kept.append(others)
     for step in range(1, count):
         for piece in range(pieces):
-            arrived = turned(travelling[piece], "tok", -1).astype(jnp.float32)
+            arrived = turned(travelling[piece], {"tok": -1}).astype(jnp.float32)
             summed = arrived + kept[piece][(step - 1) * rows : step * rows]
             if step == count - 1:
                 summed = gelu(summed)
@@ -247,13 +249,7 @@
 
 
 def local(weather, conv_first, conv_second, patch_embed, token_mixing):
-    count = lax.axis_size("tok")
-    embed = patch_embed.shape[1]
-    turn = ((lax.axis_index("tok") + 1) % count) * (embed // count)
-    rolled = lax.dynamic_slice_in_dim(
-        jnp.concatenate([patch_embed, patch_embed], axis=1), turn, embed, axis=1
-    )
-    tokens = encode(weather, conv_first, conv_second, rolled)
+    tokens = encode(weather, conv_first, conv_second, patch_embed)
     return lift(tokens, token_mixing, PIECES)
 
 

time: 80.3 us -> 85.9 us (1.070)
  starting transfers between devices: 30.4 us -> 40.9 us
  Pallas kernels: 11.8 us -> 8.01 us
  local copies, waits for them, and re-layouts: 1.07 us -> 3.89 us
  waiting for transfers between devices: 33.9 us -> 31.1 us
  other arithmetic: 2.77 us -> 1.65 us
    ppermute x17 -> x23, starting transfers between devices: 30.4 us -> 40.9 us  [turned(): return lax.ppermute(value, axes, route)]
    pallas_call x4 -> x0, Pallas kernels: 7.76 us -> none  [partial(): pl.pallas_call(partial_kernel, out_shape=(jax.ShapeDtypeStruct((rows, wid...]
    pallas_call x3 -> x7, Pallas kernels: 4.05 us -> 8.01 us  [call(): pl.pallas_call(kernel, out_shape=out_shape, in_specs=[pl.BlockSpec(memory...]
    ppermute x17 -> x23, waiting for transfers between devices: 33.9 us -> 31.1 us  [turned(): return lax.ppermute(value, axes, route)]
    unnamed x8 -> x10, local copies, waits for them, and re-layouts: 1.05 us -> 3.89 us
    concatenate x1 -> x0, other arithmetic: 1.12 us -> none  [local(): jnp.concatenate([patch_embed, patch_embed], axis=1)]
  transfers between devices with their start and end apart: 17 -> 23, of which waited for: 13 -> 17; matrix products, arithmetic and copies ran while one was open for 2% -> 1% of each run, Pallas kernels for 8% -> 4%
where the time goes in v4:
time: 85.9 us; the launch traced here: 85.7 us
  starting transfers between devices  40.9 us (48%)
  waiting for transfers between devices  31.1 us (36%)
  Pallas kernels  8.01 us (9%)
  local copies, waits for them, and re-layouts  3.89 us (5%)
  other arithmetic  1.65 us (2%)
    ppermute x23, starting transfers between devices, turned(): return lax.ppermute(value, axes, route)  40.9 us
    ppermute x23, waiting for transfers between devices, turned(): return lax.ppermute(value, axes, route)  31.1 us
    pallas_call x7, Pallas kernels, call(): pl.pallas_call(kernel, out_shape=out_shape, in_specs=[pl.BlockSpec(memory...  8.01 us
    unnamed x10, local copies, waits for them, and re-layouts  3.89 us
  transfers between devices with their start and end apart: 23, of which 17 were waited for; matrix products, arithmetic and copies ran while one was open for 1% of the time, Pallas kernels for 4%

profile of v4, /device:TPU:0, one launch (start us, length us, event | category | flops | bytes accessed | tf_op | source)
XLA Modules:
  0.0 85.7 jit_solution(594006471849185498)
XLA Ops:
  0.0 1.0 %copy-done.1 = f32[64,32,32]{0,2,1:T(8,128)S(1)} copy-done((f32[64,32,32]{0,2,1:T(8,128)S(1)}, f32[64,32,32]{0,2,1:T(8,128)}, u32[]{:S(2)}) %copy-start.1) | copy-done | bytes 262168
  1.2 2.4 %collective-permute-start.2 = (bf16[16,32,128]{2,1,0:T(8,128)(2,1)S(1)}, bf16[16,32,128]{2,1,0:T(8,128)(2,1)S(1)}, u32[]{:S(2)}, u32[]{:S(2)}) collective-permute-start(bf16[16,32,128]{2,1,0:T(8,128)(2,1)S(1)} %get-tuple-element.19.refs_0_), channel_id=1, source_target_pairs={{0,3},{1,2},{2,1},{3,0},{4,7},{5,6},{6,5},{7,4},{8,11},{9,10},{10,... | collective-permute-start | bytes 393224 | tf_op jit(solution)/shard_map/ppermute | solution.py:164
  3.6 0.6 collective-permute-start.1
  4.3 2.5 %collective-permute-start.6 = (bf16[1,32,128]{2,1,0:T(8,128)(2,1)S(1)}, bf16[1,32,128]{2,1,0:T(8,128)(2,1)S(1)}, u32[]{:S(2)}, u32[]{:S(2)}) collective-permute-start(bf16[1,32,128]{2,1,0:T(8,128)(2,1)S(1)} %get-tuple-element.20), channel_id=1, source_target_pairs={{0,7},{1,6},{2,5},{3,4},{4,11},{5,10},{6,9},{7,8},{8,15},{9,14},{1... | collective-permute-start | bytes 24584 | tf_op jit(solution)/shard_map/ppermute | solution.py:164
  6.7 1.7 %collective-permute-start.5 = (bf16[1,32,128]{2,1,0:T(8,128)(2,1)S(1)}, bf16[1,32,128]{2,1,0:T(8,128)(2,1)S(1)}, u32[]{:S(2)}, u32[]{:S(2)}) collective-permute-start(bf16[1,32,128]{2,1,0:T(8,128)(2,1)S(1)} %get-tuple-element.20), channel_id=1, source_target_pairs={{0,6},{2,4},{4,10},{6,8},{8,14},{10,12},{12,2},{14,0},{1,7},{3,5},... | collective-permute-start | bytes 24584 | tf_op jit(solution)/shard_map/ppermute | solution.py:164
  8.4 1.8 %collective-permute-done.6.refs_7_ = bf16[1,32,128]{2,1,0:T(8,128)(2,1)S(1)} collective-permute-done((bf16[1,32,128]{2,1,0:T(8,128)(2,1)S(1)}, bf16[1,32,128]{2,1,0:T(8,128)(2,1)S(1)}, u32[]{:S(2)}, u32[]{:S(2)}) %collective-permute-start.6) | collective-permute-done | bytes 8224 | tf_op jit(solution)/shard_map/ppermute | solution.py:164
  10.2 2.9 %collective-permute-done.5.refs_6_ = bf16[1,32,128]{2,1,0:T(8,128)(2,1)S(1)} collective-permute-done((bf16[1,32,128]{2,1,0:T(8,128)(2,1)S(1)}, bf16[1,32,128]{2,1,0:T(8,128)(2,1)S(1)}, u32[]{:S(2)}, u32[]{:S(2)}) %collective-permute-start.5) | collective-permute-done | bytes 8224 | tf_op jit(solution)/shard_map/ppermute | solution.py:164
  13.1 2.0 %collective-permute-done.4.refs_5_ = bf16[1,32,128]{2,1,0:T(8,128)(2,1)S(1)} collective-permute-done((bf16[1,32,128]{2,1,0:T(8,128)(2,1)S(1)}, bf16[1,32,128]{2,1,0:T(8,128)(2,1)S(1)}, u32[]{:S(2)}, u32[]{:S(2)}) %collective-permute-start.4) | collective-permute-done | bytes 8224 | tf_op jit(solution)/shard_map/ppermute | solution.py:164
  15.1 0.8 collective-permute-start.10
  15.9 2.6 %collective-permute-done.3.refs_4_ = bf16[1,32,128]{2,1,0:T(8,128)(2,1)S(1)} collective-permute-done((bf16[1,32,128]{2,1,0:T(8,128)(2,1)S(1)}, bf16[1,32,128]{2,1,0:T(8,128)(2,1)S(1)}, u32[]{:S(2)}, u32[]{:S(2)}) %collective-permute-start.3) | collective-permute-done | bytes 8224 | tf_op jit(solution)/shard_map/ppermute | solution.py:164
  18.6 0.5 collective-permute-done.10.refs_11_
  19.1 2.2 %collective-permute-start.8 = (bf16[1,32,128]{2,1,0:T(8,128)(2,1)S(1)}, bf16[1,32,128]{2,1,0:T(8,128)(2,1)S(1)}, u32[]{:S(2)}, u32[]{:S(2)}) collective-permute-start(bf16[1,32,128]{2,1,0:T(8,128)(2,1)S(1)} %get-tuple-element.21), channel_id=1, source_target_pairs={{0,13},{1,12},{4,1},{5,0},{8,5},{9,4},{12,9},{13,8},{2,15},{3,14},... | collective-permute-start | bytes 24584 | tf_op jit(solution)/shard_map/ppermute | solution.py:164
  21.3 1.8 %collective-permute-done.9.refs_10_ = bf16[1,32,128]{2,1,0:T(8,128)(2,1)S(1)} collective-permute-done((bf16[1,32,128]{2,1,0:T(8,128)(2,1)S(1)}, bf16[1,32,128]{2,1,0:T(8,128)(2,1)S(1)}, u32[]{:S(2)}, u32[]{:S(2)}) %collective-permute-start.9) | collective-permute-done | bytes 8224 | tf_op jit(solution)/shard_map/ppermute | solution.py:164
  23.1 1.5 %collective-permute-start.7 = (bf16[1,32,128]{2,1,0:T(8,128)(2,1)S(1)}, bf16[1,32,128]{2,1,0:T(8,128)(2,1)S(1)}, u32[]{:S(2)}, u32[]{:S(2)}) collective-permute-start(bf16[1,32,128]{2,1,0:T(8,128)(2,1)S(1)} %get-tuple-element.21), channel_id=1, source_target_pairs={{0,12},{4,0},{8,4},{12,8},{1,13},{5,1},{9,5},{13,9},{2,14},{6,2},{... | collective-permute-start | bytes 24584 | tf_op jit(solution)/shard_map/ppermute | solution.py:164
  24.6 1.0 %copy-done.2 = f32[9,64,64]{2,1,0:T(8,128)S(1)} copy-done((f32[9,64,64]{2,1,0:T(8,128)S(1)}, f32[9,64,64]{2,1,0:T(8,128)}, u32[]{:S(2)}) %copy-start.2) | copy-done | bytes 147480
  25.6 1.0 %copy-done.3 = f32[9,64,64]{2,1,0:T(8,128)S(1)} copy-done((f32[9,64,64]{2,1,0:T(8,128)S(1)}, f32[9,64,64]{2,1,0:T(8,128)}, u32[]{:S(2)}) %copy-start.3) | copy-done | bytes 147480
  26.6 0.9 %copy-done.4 = bf16[256,384]{1,0:T(8,128)(2,1)S(1)} copy-done((bf16[256,384]{1,0:T(8,128)(2,1)S(1)}, bf16[256,384]{1,0:T(8,128)(2,1)}, u32[]{:S(2)}) %copy-start.4) | copy-done | bytes 196632
  27.5 0.6 shard_map.56
  28.1 3.4 %shard_map.57.tokens_ref = bf16[384,1024]{1,0:T(8,128)(2,1)S(1)} custom-call(bf16[16,32,128]{2,1,0:T(8,128)(2,1)S(1)} %get-tuple-element.19.refs_0_, bf16[16,32,128]{2,1,0:T(8,128)(2,1)S(1)} %collective-permute-done.refs_1_, bf16[16,32,128]{2,1,0:T(8,128)(2,1)S(1)} %collective-permute-done.1.refs_2_, ...), custom_call_target="tpu_custom_call" | custom-call | flops 2139095040 | bytes 524288 | tf_op jit(solution)/shard_map/pallas_call | solution.py:144
  31.6 1.0 %shard_map.61 = (bf16[96,1024]{1,0:T(8,128)(2,1)S(1)}, f32[288,1024]{1,0:T(8,128)S(1)}) custom-call(bf16[384,1024]{1,0:T(8,128)(2,1)S(1)} %shard_map.57.tokens_ref, bf16[1024,4096]{1,0:T(8,128)(2,1)S(1)} %copy-done), custom_call_target="tpu_custom_call" | custom-call | tf_op jit(solution)/shard_map/pallas_call | solution.py:144
  32.6 2.0 %collective-permute-start.20 = (bf16[96,1024]{1,0:T(8,128)(2,1)S(1)}, bf16[96,1024]{1,0:T(8,128)(2,1)S(1)}, u32[]{:S(2)}, u32[]{:S(2)}) collective-permute-start(bf16[96,1024]{1,0:T(8,128)(2,1)S(1)} %get-tuple-element.31), channel_id=1, source_target_pairs={{0,12},{4,0},{8,4},{12,8},{1,13},{5,1},{9,5},{13,9},{2,14},{6,2},{... | collective-permute-start | bytes 589832 | tf_op jit(solution)/shard_map/ppermute | solution.py:164
  34.6 1.0 %shard_map.60 = (bf16[96,1024]{1,0:T(8,128)(2,1)S(1)}, f32[288,1024]{1,0:T(8,128)S(1)}) custom-call(bf16[384,1024]{1,0:T(8,128)(2,1)S(1)} %shard_map.57.tokens_ref, bf16[1024,4096]{1,0:T(8,128)(2,1)S(1)} %copy-done), custom_call_target="tpu_custom_call" | custom-call | tf_op jit(solution)/shard_map/pallas_call | solution.py:144
  35.5 1.0 %shard_map.59 = (bf16[96,1024]{1,0:T(8,128)(2,1)S(1)}, f32[288,1024]{1,0:T(8,128)S(1)}) custom-call(bf16[384,1024]{1,0:T(8,128)(2,1)S(1)} %shard_map.57.tokens_ref, bf16[1024,4096]{1,0:T(8,128)(2,1)S(1)} %copy-done), custom_call_target="tpu_custom_call" | custom-call | tf_op jit(solution)/shard_map/pallas_call | solution.py:144
  36.5 1.0 %shard_map.58 = (bf16[96,1024]{1,0:T(8,128)(2,1)S(1)}, f32[288,1024]{1,0:T(8,128)S(1)}) custom-call(bf16[384,1024]{1,0:T(8,128)(2,1)S(1)} %shard_map.57.tokens_ref, bf16[1024,4096]{1,0:T(8,128)(2,1)S(1)} %copy-done), custom_call_target="tpu_custom_call" | custom-call | tf_op jit(solution)/shard_map/pallas_call | solution.py:144
  37.6 1.4 %collective-permute-start.14 = (bf16[96,1024]{1,0:T(8,128)(2,1)S(1)}, bf16[96,1024]{1,0:T(8,128)(2,1)S(1)}, u32[]{:S(2)}, u32[]{:S(2)}) collective-permute-start(bf16[96,1024]{1,0:T(8,128)(2,1)S(1)} %get-tuple-element.27), channel_id=1, source_target_pairs={{0,12},{4,0},{8,4},{12,8},{1,13},{5,1},{9,5},{13,9},{2,14},{6,2},{... | collective-permute-start | bytes 589832 | tf_op jit(solution)/shard_map/ppermute | solution.py:164
  39.0 1.5 %collective-permute-start.11 = (bf16[96,1024]{1,0:T(8,128)(2,1)S(1)}, bf16[96,1024]{1,0:T(8,128)(2,1)S(1)}, u32[]{:S(2)}, u32[]{:S(2)}) collective-permute-start(bf16[96,1024]{1,0:T(8,128)(2,1)S(1)} %get-tuple-element.25), channel_id=1, source_target_pairs={{0,12},{4,0},{8,4},{12,8},{1,13},{5,1},{9,5},{13,9},{2,14},{6,2},{... | collective-permute-start | bytes 589832 | tf_op jit(solution)/shard_map/ppermute | solution.py:164
  40.6 3.5 %collective-permute-start.21 = (bf16[96,1024]{1,0:T(8,128)(2,1)S(1)}, bf16[96,1024]{1,0:T(8,128)(2,1)S(1)}, u32[]{:S(2)}, u32[]{:S(2)}) collective-permute-start(bf16[96,1024]{1,0:T(8,128)(2,1)S(1)} %add_convert_fusion.1), channel_id=1, source_target_pairs={{0,12},{4,0},{8,4},{12,8},{1,13},{5,1},{9,5},{13,9},{2,14},{6,2},{... | collective-permute-start | bytes 589832 | tf_op jit(solution)/shard_map/ppermute | solution.py:164
  44.1 1.3 %collective-permute-done.17 = bf16[96,1024]{1,0:T(8,128)(2,1)S(1)} collective-permute-done((bf16[96,1024]{1,0:T(8,128)(2,1)S(1)}, bf16[96,1024]{1,0:T(8,128)(2,1)S(1)}, u32[]{:S(2)}, u32[]{:S(2)}) %collective-permute-start.17) | collective-permute-done | bytes 196640 | tf_op jit(solution)/shard_map/ppermute | solution.py:164
  45.4 2.9 %collective-permute-start.18 = (bf16[96,1024]{1,0:T(8,128)(2,1)S(1)}, bf16[96,1024]{1,0:T(8,128)(2,1)S(1)}, u32[]{:S(2)}, u32[]{:S(2)}) collective-permute-start(bf16[96,1024]{1,0:T(8,128)(2,1)S(1)} %add_convert_fusion.3), channel_id=1, source_target_pairs={{0,12},{4,0},{8,4},{12,8},{1,13},{5,1},{9,5},{13,9},{2,14},{6,2},{... | collective-permute-start | bytes 589832 | tf_op jit(solution)/shard_map/ppermute | solution.py:164
  48.4 1.3 %collective-permute-done.14 = bf16[96,1024]{1,0:T(8,128)(2,1)S(1)} collective-permute-done((bf16[96,1024]{1,0:T(8,128)(2,1)S(1)}, bf16[96,1024]{1,0:T(8,128)(2,1)S(1)}, u32[]{:S(2)}, u32[]{:S(2)}) %collective-permute-start.14) | collective-permute-done | bytes 196640 | tf_op jit(solution)/shard_map/ppermute | solution.py:164
  49.7 2.9 %collective-permute-start.15 = (bf16[96,1024]{1,0:T(8,128)(2,1)S(1)}, bf16[96,1024]{1,0:T(8,128)(2,1)S(1)}, u32[]{:S(2)}, u32[]{:S(2)}) collective-permute-start(bf16[96,1024]{1,0:T(8,128)(2,1)S(1)} %add_convert_fusion.5), channel_id=1, source_target_pairs={{0,12},{4,0},{8,4},{12,8},{1,13},{5,1},{9,5},{13,9},{2,14},{6,2},{... | collective-permute-start | bytes 589832 | tf_op jit(solution)/shard_map/ppermute | solution.py:164
  52.6 1.3 %collective-permute-done.11 = bf16[96,1024]{1,0:T(8,128)(2,1)S(1)} collective-permute-done((bf16[96,1024]{1,0:T(8,128)(2,1)S(1)}, bf16[96,1024]{1,0:T(8,128)(2,1)S(1)}, u32[]{:S(2)}, u32[]{:S(2)}) %collective-permute-start.11) | collective-permute-done | bytes 196640 | tf_op jit(solution)/shard_map/ppermute | solution.py:164
  53.9 2.9 %collective-permute-start.12 = (bf16[96,1024]{1,0:T(8,128)(2,1)S(1)}, bf16[96,1024]{1,0:T(8,128)(2,1)S(1)}, u32[]{:S(2)}, u32[]{:S(2)}) collective-permute-start(bf16[96,1024]{1,0:T(8,128)(2,1)S(1)} %add_convert_fusion.7), channel_id=1, source_target_pairs={{0,12},{4,0},{8,4},{12,8},{1,13},{5,1},{9,5},{13,9},{2,14},{6,2},{... | collective-permute-start | bytes 589832 | tf_op jit(solution)/shard_map/ppermute | solution.py:164
  56.8 1.3 %collective-permute-done.21 = bf16[96,1024]{1,0:T(8,128)(2,1)S(1)} collective-permute-done((bf16[96,1024]{1,0:T(8,128)(2,1)S(1)}, bf16[96,1024]{1,0:T(8,128)(2,1)S(1)}, u32[]{:S(2)}, u32[]{:S(2)}) %collective-permute-start.21) | collective-permute-done | bytes 196640 | tf_op jit(solution)/shard_map/ppermute | solution.py:164
  58.1 2.9 %collective-permute-start.22 = (bf16[96,1024]{1,0:T(8,128)(2,1)S(1)}, bf16[96,1024]{1,0:T(8,128)(2,1)S(1)}, u32[]{:S(2)}, u32[]{:S(2)}) collective-permute-start(bf16[96,1024]{1,0:T(8,128)(2,1)S(1)} %add_convert_fusion), channel_id=1, source_target_pairs={{0,12},{4,0},{8,4},{12,8},{1,13},{5,1},{9,5},{13,9},{2,14},{6,2},{... | collective-permute-start | bytes 589832 | tf_op jit(solution)/shard_map/ppermute | solution.py:164
  61.0 1.3 %collective-permute-done.18 = bf16[96,1024]{1,0:T(8,128)(2,1)S(1)} collective-permute-done((bf16[96,1024]{1,0:T(8,128)(2,1)S(1)}, bf16[96,1024]{1,0:T(8,128)(2,1)S(1)}, u32[]{:S(2)}, u32[]{:S(2)}) %collective-permute-start.18) | collective-permute-done | bytes 196640 | tf_op jit(solution)/shard_map/ppermute | solution.py:164
  62.3 2.9 %collective-permute-start.19 = (bf16[96,1024]{1,0:T(8,128)(2,1)S(1)}, bf16[96,1024]{1,0:T(8,128)(2,1)S(1)}, u32[]{:S(2)}, u32[]{:S(2)}) collective-permute-start(bf16[96,1024]{1,0:T(8,128)(2,1)S(1)} %add_convert_fusion.2), channel_id=1, source_target_pairs={{0,12},{4,0},{8,4},{12,8},{1,13},{5,1},{9,5},{13,9},{2,14},{6,2},{... | collective-permute-start | bytes 589832 | tf_op jit(solution)/shard_map/ppermute | solution.py:164
  65.2 1.3 %collective-permute-done.15 = bf16[96,1024]{1,0:T(8,128)(2,1)S(1)} collective-permute-done((bf16[96,1024]{1,0:T(8,128)(2,1)S(1)}, bf16[96,1024]{1,0:T(8,128)(2,1)S(1)}, u32[]{:S(2)}, u32[]{:S(2)}) %collective-permute-start.15) | collective-permute-done | bytes 196640 | tf_op jit(solution)/shard_map/ppermute | solution.py:164
  66.5 2.9 %collective-permute-start.16 = (bf16[96,1024]{1,0:T(8,128)(2,1)S(1)}, bf16[96,1024]{1,0:T(8,128)(2,1)S(1)}, u32[]{:S(2)}, u32[]{:S(2)}) collective-permute-start(bf16[96,1024]{1,0:T(8,128)(2,1)S(1)} %add_convert_fusion.4), channel_id=1, source_target_pairs={{0,12},{4,0},{8,4},{12,8},{1,13},{5,1},{9,5},{13,9},{2,14},{6,2},{... | collective-permute-start | bytes 589832 | tf_op jit(solution)/shard_map/ppermute | solution.py:164
  69.4 1.3 %collective-permute-done.12 = bf16[96,1024]{1,0:T(8,128)(2,1)S(1)} collective-permute-done((bf16[96,1024]{1,0:T(8,128)(2,1)S(1)}, bf16[96,1024]{1,0:T(8,128)(2,1)S(1)}, u32[]{:S(2)}, u32[]{:S(2)}) %collective-permute-start.12) | collective-permute-done | bytes 196640 | tf_op jit(solution)/shard_map/ppermute | solution.py:164
  70.7 2.9 %collective-permute-start.13 = (bf16[96,1024]{1,0:T(8,128)(2,1)S(1)}, bf16[96,1024]{1,0:T(8,128)(2,1)S(1)}, u32[]{:S(2)}, u32[]{:S(2)}) collective-permute-start(bf16[96,1024]{1,0:T(8,128)(2,1)S(1)} %add_convert_fusion.6), channel_id=1, source_target_pairs={{0,12},{4,0},{8,4},{12,8},{1,13},{5,1},{9,5},{13,9},{2,14},{6,2},{... | collective-permute-start | bytes 589832 | tf_op jit(solution)/shard_map/ppermute | solution.py:164
  73.6 1.3 %collective-permute-done.22 = bf16[96,1024]{1,0:T(8,128)(2,1)S(1)} collective-permute-done((bf16[96,1024]{1,0:T(8,128)(2,1)S(1)}, bf16[96,1024]{1,0:T(8,128)(2,1)S(1)}, u32[]{:S(2)}, u32[]{:S(2)}) %collective-permute-start.22) | collective-permute-done | bytes 196640 | tf_op jit(solution)/shard_map/ppermute | solution.py:164
  74.9 0.1 multiply_convert_fusion
  75.0 4.1 %collective-permute-done.19 = bf16[96,1024]{1,0:T(8,128)(2,1)S(1)} collective-permute-done((bf16[96,1024]{1,0:T(8,128)(2,1)S(1)}, bf16[96,1024]{1,0:T(8,128)(2,1)S(1)}, u32[]{:S(2)}, u32[]{:S(2)}) %collective-permute-start.19) | collective-permute-done | bytes 196640 | tf_op jit(solution)/shard_map/ppermute | solution.py:164
  79.1 0.1 multiply_convert_fusion.1
  79.2 3.3 %collective-permute-done.16 = bf16[96,1024]{1,0:T(8,128)(2,1)S(1)} collective-permute-done((bf16[96,1024]{1,0:T(8,128)(2,1)S(1)}, bf16[96,1024]{1,0:T(8,128)(2,1)S(1)}, u32[]{:S(2)}, u32[]{:S(2)}) %collective-permute-start.16) | collective-permute-done | bytes 196640 | tf_op jit(solution)/shard_map/ppermute | solution.py:164
  82.6 2.0 %collective-permute-done.13 = bf16[96,1024]{1,0:T(8,128)(2,1)S(1)} collective-permute-done((bf16[96,1024]{1,0:T(8,128)(2,1)S(1)}, bf16[96,1024]{1,0:T(8,128)(2,1)S(1)}, u32[]{:S(2)}, u32[]{:S(2)}) %collective-permute-start.13) | collective-permute-done | bytes 196640 | tf_op jit(solution)/shard_map/ppermute | solution.py:164
  84.7 0.9 %pad_maximum_fusion = bf16[96,4096]{1,0:T(8,128)(2,1)} fusion(bf16[96,1024]{1,0:T(8,128)(2,1)S(1)} %multiply_convert_fusion, bf16[96,1024]{1,0:T(8,128)(2,1)S(1)} %multiply_convert_fusion.1, bf16[96,1024]{1,0:T(8,128)(2,1)S(1)} %multiply_convert_fusion.2, bf16[96,1024]{1,0:T(8,128)(2,1)S(1)} %multiply_convert_fusion.3), kind=kLoop, calls=%fused_computation | loop fusion | flops 3145728 | bytes 1572864 | tf_op jit(solution)/shard_map/concatenate | solution.py:248
  (28 shorter events, 0.8 us)
Async XLA Ops:
  0.0 1.0 %copy-start.1 = (f32[64,32,32]{0,2,1:T(8,128)S(1)}, f32[64,32,32]{0,2,1:T(8,128)}, u32[]{:S(2)}) copy-start(f32[64,32,32]{0,2,1:T(8,128)} %param.5) | copy-start | bytes 786436
  1.2 27.0 %collective-permute-start.2 = (bf16[16,32,128]{2,1,0:T(8,128)(2,1)S(1)}, bf16[16,32,128]{2,1,0:T(8,128)(2,1)S(1)}, u32[]{:S(2)}, u32[]{:S(2)}) collective-permute-start(bf16[16,32,128]{2,1,0:T(8,128)(2,1)S(1)} %get-tuple-element.19.refs_0_), channel_id=1, source_target_pairs={{0,3},{1,2},{2,1},{3,0},{4,7},{5,6},{6,5},{7,4},{8,11},{9,10},{10,... | collective-permute-start | bytes 393224 | tf_op jit(solution)/shard_map/ppermute | solution.py:164
  3.6 24.5 %collective-permute-start.1 = (bf16[16,32,128]{2,1,0:T(8,128)(2,1)S(1)}, bf16[16,32,128]{2,1,0:T(8,128)(2,1)S(1)}, u32[]{:S(2)}, u32[]{:S(2)}) collective-permute-start(bf16[16,32,128]{2,1,0:T(8,128)(2,1)S(1)} %get-tuple-element.19.refs_0_), channel_id=1, source_target_pairs={{0,2},{2,0},{1,3},{3,1},{4,6},{6,4},{5,7},{7,5},{8,10},{10,8},{9,1... | collective-permute-start | bytes 393224 | tf_op jit(solution)/shard_map/ppermute | solution.py:164
  4.2 23.9 %collective-permute-start = (bf16[16,32,128]{2,1,0:T(8,128)(2,1)S(1)}, bf16[16,32,128]{2,1,0:T(8,128)(2,1)S(1)}, u32[]{:S(2)}, u32[]{:S(2)}) collective-permute-start(bf16[16,32,128]{2,1,0:T(8,128)(2,1)S(1)} %get-tuple-element.19.refs_0_), channel_id=1, source_target_pairs={{0,1},{1,0},{2,3},{3,2},{4,5},{5,4},{6,7},{7,6},{8,9},{9,8},{10,11... | collective-permute-start | bytes 393224 | tf_op jit(solution)/shard_map/ppermute | solution.py:164
  4.3 5.9 %collective-permute-start.6 = (bf16[1,32,128]{2,1,0:T(8,128)(2,1)S(1)}, bf16[1,32,128]{2,1,0:T(8,128)(2,1)S(1)}, u32[]{:S(2)}, u32[]{:S(2)}) collective-permute-start(bf16[1,32,128]{2,1,0:T(8,128)(2,1)S(1)} %get-tuple-element.20), channel_id=1, source_target_pairs={{0,7},{1,6},{2,5},{3,4},{4,11},{5,10},{6,9},{7,8},{8,15},{9,14},{1... | collective-permute-start | bytes 24584 | tf_op jit(solution)/shard_map/ppermute | solution.py:164
  6.7 6.3 %collective-permute-start.5 = (bf16[1,32,128]{2,1,0:T(8,128)(2,1)S(1)}, bf16[1,32,128]{2,1,0:T(8,128)(2,1)S(1)}, u32[]{:S(2)}, u32[]{:S(2)}) collective-permute-start(bf16[1,32,128]{2,1,0:T(8,128)(2,1)S(1)} %get-tuple-element.20), channel_id=1, source_target_pairs={{0,6},{2,4},{4,10},{6,8},{8,14},{10,12},{12,2},{14,0},{1,7},{3,5},... | collective-permute-start | bytes 24584 | tf_op jit(solution)/shard_map/ppermute | solution.py:164
  10.2 4.9 %collective-permute-start.4 = (bf16[1,32,128]{2,1,0:T(8,128)(2,1)S(1)}, bf16[1,32,128]{2,1,0:T(8,128)(2,1)S(1)}, u32[]{:S(2)}, u32[]{:S(2)}) collective-permute-start(bf16[1,32,128]{2,1,0:T(8,128)(2,1)S(1)} %get-tuple-element.20), channel_id=1, source_target_pairs={{0,5},{1,4},{4,9},{5,8},{8,13},{9,12},{12,1},{13,0},{2,7},{3,6},{6... | collective-permute-start | bytes 24584 | tf_op jit(solution)/shard_map/ppermute | solution.py:164
  13.1 5.4 %collective-permute-start.3 = (bf16[1,32,128]{2,1,0:T(8,128)(2,1)S(1)}, bf16[1,32,128]{2,1,0:T(8,128)(2,1)S(1)}, u32[]{:S(2)}, u32[]{:S(2)}) collective-permute-start(bf16[1,32,128]{2,1,0:T(8,128)(2,1)S(1)} %get-tuple-element.20), channel_id=1, source_target_pairs={{0,4},{4,8},{8,12},{12,0},{1,5},{5,9},{9,13},{13,1},{2,6},{6,10},{... | collective-permute-start | bytes 24584 | tf_op jit(solution)/shard_map/ppermute | solution.py:164
  15.1 4.0 %collective-permute-start.10 = (bf16[1,32,128]{2,1,0:T(8,128)(2,1)S(1)}, bf16[1,32,128]{2,1,0:T(8,128)(2,1)S(1)}, u32[]{:S(2)}, u32[]{:S(2)}) collective-permute-start(bf16[1,32,128]{2,1,0:T(8,128)(2,1)S(1)} %get-tuple-element.21), channel_id=1, source_target_pairs={{0,15},{1,14},{2,13},{3,12},{4,3},{5,2},{6,1},{7,0},{8,7},{9,6},{1... | collective-permute-start | bytes 24584 | tf_op jit(solution)/shard_map/ppermute | solution.py:164
  18.5 4.5 %collective-permute-start.9 = (bf16[1,32,128]{2,1,0:T(8,128)(2,1)S(1)}, bf16[1,32,128]{2,1,0:T(8,128)(2,1)S(1)}, u32[]{:S(2)}, u32[]{:S(2)}) collective-permute-start(bf16[1,32,128]{2,1,0:T(8,128)(2,1)S(1)} %get-tuple-element.21), channel_id=1, source_target_pairs={{0,14},{2,12},{4,2},{6,0},{8,6},{10,4},{12,10},{14,8},{1,15},{3,13... | collective-permute-start | bytes 24584 | tf_op jit(solution)/shard_map/ppermute | solution.py:164
  19.1 9.0 %collective-permute-start.8 = (bf16[1,32,128]{2,1,0:T(8,128)(2,1)S(1)}, bf16[1,32,128]{2,1,0:T(8,128)(2,1)S(1)}, u32[]{:S(2)}, u32[]{:S(2)}) collective-permute-start(bf16[1,32,128]{2,1,0:T(8,128)(2,1)S(1)} %get-tuple-element.21), channel_id=1, source_target_pairs={{0,13},{1,12},{4,1},{5,0},{8,5},{9,4},{12,9},{13,8},{2,15},{3,14},... | collective-permute-start | bytes 24584 | tf_op jit(solution)/shard_map/ppermute | solution.py:164
  23.1 5.0 %collective-permute-start.7 = (bf16[1,32,128]{2,1,0:T(8,128)(2,1)S(1)}, bf16[1,32,128]{2,1,0:T(8,128)(2,1)S(1)}, u32[]{:S(2)}, u32[]{:S(2)}) collective-permute-start(bf16[1,32,128]{2,1,0:T(8,128)(2,1)S(1)} %get-tuple-element.21), channel_id=1, source_target_pairs={{0,12},{4,0},{8,4},{12,8},{1,13},{5,1},{9,5},{13,9},{2,14},{6,2},{... | collective-permute-start | bytes 24584 | tf_op jit(solution)/shard_map/ppermute | solution.py:164
  24.6 1.0 %copy-start.2 = (f32[9,64,64]{2,1,0:T(8,128)S(1)}, f32[9,64,64]{2,1,0:T(8,128)}, u32[]{:S(2)}) copy-start(f32[9,64,64]{2,1,0:T(8,128)} %first_ref.1) | copy-start | bytes 442372
  25.6 1.0 %copy-start.3 = (f32[9,64,64]{2,1,0:T(8,128)S(1)}, f32[9,64,64]{2,1,0:T(8,128)}, u32[]{:S(2)}) copy-start(f32[9,64,64]{2,1,0:T(8,128)} %second_ref.1) | copy-start | bytes 442372
  26.6 0.9 %copy-start.4 = (bf16[256,384]{1,0:T(8,128)(2,1)S(1)}, bf16[256,384]{1,0:T(8,128)(2,1)}, u32[]{:S(2)}) copy-start(bf16[256,384]{1,0:T(8,128)(2,1)} %embed_ref.1) | copy-start | bytes 589828
  27.5 4.1 %copy-start = (bf16[1024,4096]{1,0:T(8,128)(2,1)S(1)}, bf16[1024,4096]{1,0:T(8,128)(2,1)}, u32[]{:S(2)}) copy-start(bf16[1024,4096]{1,0:T(8,128)(2,1)} %mixing_ref.7) | copy-start | bytes 25165828
  32.6 8.0 %collective-permute-start.20 = (bf16[96,1024]{1,0:T(8,128)(2,1)S(1)}, bf16[96,1024]{1,0:T(8,128)(2,1)S(1)}, u32[]{:S(2)}, u32[]{:S(2)}) collective-permute-start(bf16[96,1024]{1,0:T(8,128)(2,1)S(1)} %get-tuple-element.31), channel_id=1, source_target_pairs={{0,12},{4,0},{8,4},{12,8},{1,13},{5,1},{9,5},{13,9},{2,14},{6,2},{... | collective-permute-start | bytes 589832 | tf_op jit(solution)/shard_map/ppermute | solution.py:164
  37.5 7.9 %collective-permute-start.17 = (bf16[96,1024]{1,0:T(8,128)(2,1)S(1)}, bf16[96,1024]{1,0:T(8,128)(2,1)S(1)}, u32[]{:S(2)}, u32[]{:S(2)}) collective-permute-start(bf16[96,1024]{1,0:T(8,128)(2,1)S(1)} %get-tuple-element.29), channel_id=1, source_target_pairs={{0,12},{4,0},{8,4},{12,8},{1,13},{5,1},{9,5},{13,9},{2,14},{6,2},{... | collective-permute-start | bytes 589832 | tf_op jit(solution)/shard_map/ppermute | solution.py:164
  37.6 12.0 %collective-permute-start.14 = (bf16[96,1024]{1,0:T(8,128)(2,1)S(1)}, bf16[96,1024]{1,0:T(8,128)(2,1)S(1)}, u32[]{:S(2)}, u32[]{:S(2)}) collective-permute-start(bf16[96,1024]{1,0:T(8,128)(2,1)S(1)} %get-tuple-element.27), channel_id=1, source_target_pairs={{0,12},{4,0},{8,4},{12,8},{1,13},{5,1},{9,5},{13,9},{2,14},{6,2},{... | collective-permute-start | bytes 589832 | tf_op jit(solution)/shard_map/ppermute | solution.py:164
  39.0 14.8 %collective-permute-start.11 = (bf16[96,1024]{1,0:T(8,128)(2,1)S(1)}, bf16[96,1024]{1,0:T(8,128)(2,1)S(1)}, u32[]{:S(2)}, u32[]{:S(2)}) collective-permute-start(bf16[96,1024]{1,0:T(8,128)(2,1)S(1)} %get-tuple-element.25), channel_id=1, source_target_pairs={{0,12},{4,0},{8,4},{12,8},{1,13},{5,1},{9,5},{13,9},{2,14},{6,2},{... | collective-permute-start | bytes 589832 | tf_op jit(solution)/shard_map/ppermute | solution.py:164
  40.6 17.4 %collective-permute-start.21 = (bf16[96,1024]{1,0:T(8,128)(2,1)S(1)}, bf16[96,1024]{1,0:T(8,128)(2,1)S(1)}, u32[]{:S(2)}, u32[]{:S(2)}) collective-permute-start(bf16[96,1024]{1,0:T(8,128)(2,1)S(1)} %add_convert_fusion.1), channel_id=1, source_target_pairs={{0,12},{4,0},{8,4},{12,8},{1,13},{5,1},{9,5},{13,9},{2,14},{6,2},{... | collective-permute-start | bytes 589832 | tf_op jit(solution)/shard_map/ppermute | solution.py:164
  45.4 16.8 %collective-permute-start.18 = (bf16[96,1024]{1,0:T(8,128)(2,1)S(1)}, bf16[96,1024]{1,0:T(8,128)(2,1)S(1)}, u32[]{:S(2)}, u32[]{:S(2)}) collective-permute-start(bf16[96,1024]{1,0:T(8,128)(2,1)S(1)} %add_convert_fusion.3), channel_id=1, source_target_pairs={{0,12},{4,0},{8,4},{12,8},{1,13},{5,1},{9,5},{13,9},{2,14},{6,2},{... | collective-permute-start | bytes 589832 | tf_op jit(solution)/shard_map/ppermute | solution.py:164
  49.7 16.8 %collective-permute-start.15 = (bf16[96,1024]{1,0:T(8,128)(2,1)S(1)}, bf16[96,1024]{1,0:T(8,128)(2,1)S(1)}, u32[]{:S(2)}, u32[]{:S(2)}) collective-permute-start(bf16[96,1024]{1,0:T(8,128)(2,1)S(1)} %add_convert_fusion.5), channel_id=1, source_target_pairs={{0,12},{4,0},{8,4},{12,8},{1,13},{5,1},{9,5},{13,9},{2,14},{6,2},{... | collective-permute-start | bytes 589832 | tf_op jit(solution)/shard_map/ppermute | solution.py:164
  53.9 16.8 %collective-permute-start.12 = (bf16[96,1024]{1,0:T(8,128)(2,1)S(1)}, bf16[96,1024]{1,0:T(8,128)(2,1)S(1)}, u32[]{:S(2)}, u32[]{:S(2)}) collective-permute-start(bf16[96,1024]{1,0:T(8,128)(2,1)S(1)} %add_convert_fusion.7), channel_id=1, source_target_pairs={{0,12},{4,0},{8,4},{12,8},{1,13},{5,1},{9,5},{13,9},{2,14},{6,2},{... | collective-permute-start | bytes 589832 | tf_op jit(solution)/shard_map/ppermute | solution.py:164
  58.1 16.8 %collective-permute-start.22 = (bf16[96,1024]{1,0:T(8,128)(2,1)S(1)}, bf16[96,1024]{1,0:T(8,128)(2,1)S(1)}, u32[]{:S(2)}, u32[]{:S(2)}) collective-permute-start(bf16[96,1024]{1,0:T(8,128)(2,1)S(1)} %add_convert_fusion), channel_id=1, source_target_pairs={{0,12},{4,0},{8,4},{12,8},{1,13},{5,1},{9,5},{13,9},{2,14},{6,2},{... | collective-permute-start | bytes 589832 | tf_op jit(solution)/shard_map/ppermute | solution.py:164
  62.3 16.8 %collective-permute-start.19 = (bf16[96,1024]{1,0:T(8,128)(2,1)S(1)}, bf16[96,1024]{1,0:T(8,128)(2,1)S(1)}, u32[]{:S(2)}, u32[]{:S(2)}) collective-permute-start(bf16[96,1024]{1,0:T(8,128)(2,1)S(1)} %add_convert_fusion.2), channel_id=1, source_target_pairs={{0,12},{4,0},{8,4},{12,8},{1,13},{5,1},{9,5},{13,9},{2,14},{6,2},{... | collective-permute-start | bytes 589832 | tf_op jit(solution)/shard_map/ppermute | solution.py:164
  66.5 16.0 %collective-permute-start.16 = (bf16[96,1024]{1,0:T(8,128)(2,1)S(1)}, bf16[96,1024]{1,0:T(8,128)(2,1)S(1)}, u32[]{:S(2)}, u32[]{:S(2)}) collective-permute-start(bf16[96,1024]{1,0:T(8,128)(2,1)S(1)} %add_convert_fusion.4), channel_id=1, source_target_pairs={{0,12},{4,0},{8,4},{12,8},{1,13},{5,1},{9,5},{13,9},{2,14},{6,2},{... | collective-permute-start | bytes 589832 | tf_op jit(solution)/shard_map/ppermute | solution.py:164
  70.7 13.9 %collective-permute-start.13 = (bf16[96,1024]{1,0:T(8,128)(2,1)S(1)}, bf16[96,1024]{1,0:T(8,128)(2,1)S(1)}, u32[]{:S(2)}, u32[]{:S(2)}) collective-permute-start(bf16[96,1024]{1,0:T(8,128)(2,1)S(1)} %add_convert_fusion.6), channel_id=1, source_target_pairs={{0,12},{4,0},{8,4},{12,8},{1,13},{5,1},{9,5},{13,9},{2,14},{6,2},{... | collective-permute-start | bytes 589832 | tf_op jit(solution)/shard_map/ppermute | solution.py:164

commit v5 on v4

--- a/solution.py
+++ b/solution.py
@@ -1,5 +1,4 @@
 import functools
-import itertools
 
 import jax
 import jax.numpy as jnp
@@ -19,7 +18,7 @@
     lon, lat, chans = field_ref.shape
     pairs = field_ref[...].reshape(lon // 2, 2, lat, chans)
     joined = jnp.concatenate([pairs[:, 0], pairs[:, 1]], axis=-1).astype(packed_ref.dtype)
-    packed_ref[...] = joined
+    packed_ref[pl.ds(1, lon // 2)] = joined
     low_ref[...] = joined[:1]
     high_ref[...] = joined[-1:]
 
@@ -95,8 +94,8 @@
 
 def encode_kernel(count_ch, count_sub, *refs):
     count = count_ch * count_sub
-    blocks, befores, afters = refs[:count], refs[count : 2 * count], refs[2 * count : 3 * count]
-    taps_one_ref, taps_two_ref, embed_ref, tokens_ref, field_ref, upper_ref, lower_ref, two_ref = refs[3 * count :]
+    blocks = refs[:count]
+    taps_one_ref, taps_two_ref, embed_ref, tokens_ref, field_ref, upper_ref, lower_ref, two_ref = refs[count:]
     pairs, lat, wide = field_ref.shape
     width = lat // count
     last = pairs - 1
@@ -105,10 +104,7 @@
             at_ch = lax.rem(lax.axis_index("ch") + count_ch - away_ch, count_ch)
             at_sub = lax.rem(lax.axis_index("sub") + count_sub - away_sub, count_sub)
             start = pl.multiple_of((at_ch * count_sub + at_sub) * width, width)
-            away = away_ch * count_sub + away_sub
-            field_ref[pl.ds(1, pairs - 2), pl.ds(start, width), :] = blocks[away][...]
-            field_ref[pl.ds(0, 1), pl.ds(start, width), :] = befores[away][...]
-            field_ref[pl.ds(pairs - 1, 1), pl.ds(start, width), :] = afters[away][...]
+            field_ref[:, pl.ds(start, width), :] = blocks[away_ch * count_sub + away_sub][...]
 
     def field_of(pair):
         return field_ref[pair]
@@ -152,26 +148,19 @@
     )(*inputs)
 
 
-def turned(value, steps):
-    axes = tuple(steps)
-    sizes = [lax.axis_size(axis) for axis in axes]
-    sources = list(itertools.product(*[range(size) for size in sizes]))
-    place = {source: number for number, source in enumerate(sources)}
-    route = []
-    for source in sources:
-        target = tuple((at + steps[axis]) % size for at, axis, size in zip(source, axes, sizes))
-        route.append((place[source], place[target]))
-    return lax.ppermute(value, axes, route)
-
-
-def band_blocks(block, steps):
+def turned(value, axis, away):
+    count = lax.axis_size(axis)
+    return lax.ppermute(value, axis, [(i, (i + away) % count) for i in range(count)])
+
+
+def band_blocks(block, beside):
+    rows = [block] + [turned(block, "ch", away) for away in range(1, lax.axis_size("ch"))]
+    rows[1:], beside = lax.optimization_barrier((rows[1:], beside))
     blocks = []
-    for away_ch in range(lax.axis_size("ch")):
-        for away_sub in range(lax.axis_size("sub")):
-            moves = dict(steps, ch=away_ch, sub=away_sub)
-            moves = {axis: step for axis, step in moves.items() if step != 0}
-            blocks.append(turned(block, moves) if moves else block)
-    return blocks
+    for row in rows:
+        blocks.append(row)
+        blocks.extend(turned(row, "sub", away) for away in range(1, lax.axis_size("sub")))
+    return blocks, beside
 
 
 def encode(weather, conv_first, conv_second, patch_embed):
@@ -181,27 +170,29 @@
     shape = functools.partial(jax.ShapeDtypeStruct, dtype=jnp.bfloat16)
     low, high, packed = call(
         pack_kernel,
-        (shape((1, lat, wide)), shape((1, lat, wide)), shape((pairs, lat, wide))),
+        (shape((1, lat, wide)), shape((1, lat, wide)), shape((pairs + 2, lat, wide))),
         (jnp.transpose(weather, (1, 2, 0)),),
         moved=weather.size * 10,
     )
+    before = turned(high, "tok", 1)
+    after = turned(low, "tok", -1)
     taps = shape((2, 4 * chans, 6 * chans))
-    taps_one, taps_two, embed_rows = call(
+    weights = call(
         weights_kernel,
         (taps, taps, shape((embed, 4 * chans))),
         (conv_first, conv_second, patch_embed),
         scratch=[pltpu.VMEM((patch_embed.shape[0], LANES), jnp.float32)],
         moved=conv_first.size * 20,
     )
-    blocks = band_blocks(packed, {})
-    befores = band_blocks(high, {"tok": 1})
-    afters = band_blocks(low, {"tok": -1})
+    packed = lax.dynamic_update_slice_in_dim(packed, before, 0, 0)
+    packed = lax.dynamic_update_slice_in_dim(packed, after, pairs + 1, 0)
+    blocks, weights = band_blocks(packed, weights)
     full_lat = len(blocks) * lat
     held = pltpu.VMEM((pairs + 2, full_lat, wide), jnp.bfloat16)
     return call(
         functools.partial(encode_kernel, lax.axis_size("ch"), lax.axis_size("sub")),
         shape((embed, pairs * full_lat // 2)),
-        (*blocks, *befores, *afters, taps_one, taps_two, embed_rows),
+        (*blocks, *weights),
         scratch=[held, held, held, pltpu.VMEM((pairs * full_lat, wide), jnp.float32)],
         flops=2 * (pairs + 1) * full_lat * 4 * chans * 6 * chans * 5,
         moved=packed.size * 2 * len(blocks),
@@ -240,7 +231,7 @@
         kept.append(others)
     for step in range(1, count):
         for piece in range(pieces):
-            arrived = turned(travelling[piece], {"tok": -1}).astype(jnp.float32)
+            arrived = turned(travelling[piece], "tok", -1).astype(jnp.float32)
             summed = arrived + kept[piece][(step - 1) * rows : step * rows]
             if step == count - 1:
                 summed = gelu(summed)

time: 85.9 us -> 76.2 us (0.89)
  waiting for transfers between devices: 31.1 us -> 24.2 us
  starting transfers between devices: 40.9 us -> 38.1 us
    ppermute x23 -> x17, waiting for transfers between devices: 31.1 us -> 24.2 us  [turned(): lax.ppermute(value, axis, [(i, (i + away) % count) for i in range(count)])]
    ppermute x23 -> x17, starting transfers between devices: 40.9 us -> 38.1 us  [turned(): lax.ppermute(value, axis, [(i, (i + away) % count) for i in range(count)])]
  transfers between devices with their start and end apart: 23 -> 17, of which waited for: 17 -> 15; matrix products, arithmetic and copies ran while one was open for 1% -> 1% of each run, Pallas kernels for 4% -> 5%
where the time goes in v5:
time: 76.2 us; the launch traced here: 76 us
  starting transfers between devices  38.1 us (50%)
  waiting for transfers between devices  24.2 us (32%)
  Pallas kernels  8 us (10%)
  local copies, waits for them, and re-layouts  3.91 us (5%)
  other arithmetic  1.65 us (2%)
    ppermute x17, starting transfers between devices, turned(): lax.ppermute(value, axis, [(i, (i + away) % count) for i in range(count)])  38.1 us
    ppermute x17, waiting for transfers between devices, turned(): lax.ppermute(value, axis, [(i, (i + away) % count) for i in range(count)])  24.2 us
    pallas_call x7, Pallas kernels, call(): pl.pallas_call(kernel, out_shape=out_shape, in_specs=[pl.BlockSpec(memory...  8 us
    unnamed x10, local copies, waits for them, and re-layouts  3.89 us
  transfers between devices with their start and end apart: 17, of which 15 were waited for; matrix products, arithmetic and copies ran while one was open for 1% of the time, Pallas kernels for 5%

profile of v5, /device:TPU:0, one launch (start us, length us, event | category | flops | bytes accessed | tf_op | source)
XLA Modules:
  0.0 76.0 jit_solution(9769204930356025613)
XLA Ops:
  0.0 1.0 %copy-done.1 = f32[64,32,32]{0,2,1:T(8,128)S(1)} copy-done((f32[64,32,32]{0,2,1:T(8,128)S(1)}, f32[64,32,32]{0,2,1:T(8,128)}, u32[]{:S(2)}) %copy-start.1) | copy-done | bytes 262168
  1.0 0.1 shard_map.55
  1.2 3.1 %collective-permute-start = (bf16[1,32,128]{2,1,0:T(8,128)(2,1)S(1)}, bf16[1,32,128]{2,1,0:T(8,128)(2,1)S(1)}, u32[]{:S(2)}, u32[]{:S(2)}) collective-permute-start(bf16[1,32,128]{2,1,0:T(8,128)(2,1)S(1)} %get-tuple-element.24), channel_id=1, source_target_pairs={{0,4},{4,8},{8,12},{12,0},{1,5},{5,9},{9,13},{13,1},{2,6},{6,10},{... | collective-permute-start | bytes 24584 | tf_op jit(solution)/shard_map/ppermute | solution.py:153
  4.2 2.1 %collective-permute-start.1 = (bf16[1,32,128]{2,1,0:T(8,128)(2,1)S(1)}, bf16[1,32,128]{2,1,0:T(8,128)(2,1)S(1)}, u32[]{:S(2)}, u32[]{:S(2)}) collective-permute-start(bf16[1,32,128]{2,1,0:T(8,128)(2,1)S(1)} %get-tuple-element.25), channel_id=1, source_target_pairs={{0,12},{4,0},{8,4},{12,8},{1,13},{5,1},{9,5},{13,9},{2,14},{6,2},{... | collective-permute-start | bytes 24584 | tf_op jit(solution)/shard_map/ppermute | solution.py:153
  6.3 1.6 %collective-permute-done = bf16[1,32,128]{2,1,0:T(8,128)(2,1)S(1)} collective-permute-done((bf16[1,32,128]{2,1,0:T(8,128)(2,1)S(1)}, bf16[1,32,128]{2,1,0:T(8,128)(2,1)S(1)}, u32[]{:S(2)}, u32[]{:S(2)}) %collective-permute-start) | collective-permute-done | bytes 8224 | tf_op jit(solution)/shard_map/ppermute | solution.py:153
  8.0 1.7 %collective-permute-start.3 = (bf16[18,32,128]{2,1,0:T(8,128)(2,1)S(1)}, bf16[18,32,128]{2,1,0:T(8,128)(2,1)S(1)}, u32[]{:S(2)}, u32[]{:S(2)}) collective-permute-start(bf16[18,32,128]{2,1,0:T(8,128)(2,1)S(1)} %constant_dynamic-update-slice_fusion.refs_0_), channel_id=1, source_target_pairs={{0,2},{2,0},{1,3},{3,1},{4,6},{6,4},{5,7},{7,5},{8,10},{10,8},{9,1... | collective-permute-start | bytes 442376 | tf_op jit(solution)/shard_map/ppermute | solution.py:153
  9.7 1.0 %copy-done.2 = f32[9,64,64]{2,1,0:T(8,128)S(1)} copy-done((f32[9,64,64]{2,1,0:T(8,128)S(1)}, f32[9,64,64]{2,1,0:T(8,128)}, u32[]{:S(2)}) %copy-start.2) | copy-done | bytes 147480
  10.6 1.0 %copy-done.3 = f32[9,64,64]{2,1,0:T(8,128)S(1)} copy-done((f32[9,64,64]{2,1,0:T(8,128)S(1)}, f32[9,64,64]{2,1,0:T(8,128)}, u32[]{:S(2)}) %copy-start.3) | copy-done | bytes 147480
  11.6 0.9 %copy-done.4 = bf16[256,384]{1,0:T(8,128)(2,1)S(1)} copy-done((bf16[256,384]{1,0:T(8,128)(2,1)S(1)}, bf16[256,384]{1,0:T(8,128)(2,1)}, u32[]{:S(2)}) %copy-start.4) | copy-done | bytes 196632
  12.5 0.6 shard_map.56
  13.1 0.1 collective-permute-start.2
  13.2 0.5 collective-permute-start.4
  13.7 0.9 %collective-permute-done.2.refs_1_ = bf16[18,32,128]{2,1,0:T(8,128)(2,1)S(1)} collective-permute-done((bf16[18,32,128]{2,1,0:T(8,128)(2,1)S(1)}, bf16[18,32,128]{2,1,0:T(8,128)(2,1)S(1)}, u32[]{:S(2)}, u32[]{:S(2)}) %collective-permute-start.2) | collective-permute-done | bytes 147488 | tf_op jit(solution)/shard_map/ppermute | solution.py:153
  14.6 0.2 collective-permute-done.4.refs_3_
  14.8 3.4 %shard_map.57.tokens_ref = bf16[384,1024]{1,0:T(8,128)(2,1)S(1)} custom-call(bf16[18,32,128]{2,1,0:T(8,128)(2,1)S(1)} %constant_dynamic-update-slice_fusion.refs_0_, bf16[18,32,128]{2,1,0:T(8,128)(2,1)S(1)} %collective-permute-done.2.refs_1_, bf16[18,32,128]{2,1,0:T(8,128)(2,1)S(1)} %collective-permute-done.3.refs_2_, ...), custom_call_target="tpu_custom_call" | custom-call | flops 2139095040 | bytes 589824 | tf_op jit(solution)/shard_map/pallas_call | solution.py:140
  18.2 1.0 %shard_map.61 = (bf16[96,1024]{1,0:T(8,128)(2,1)S(1)}, f32[288,1024]{1,0:T(8,128)S(1)}) custom-call(bf16[384,1024]{1,0:T(8,128)(2,1)S(1)} %shard_map.57.tokens_ref, bf16[1024,4096]{1,0:T(8,128)(2,1)S(1)} %copy-done), custom_call_target="tpu_custom_call" | custom-call | tf_op jit(solution)/shard_map/pallas_call | solution.py:140
  19.2 3.8 %collective-permute-start.14 = (bf16[96,1024]{1,0:T(8,128)(2,1)S(1)}, bf16[96,1024]{1,0:T(8,128)(2,1)S(1)}, u32[]{:S(2)}, u32[]{:S(2)}) collective-permute-start(bf16[96,1024]{1,0:T(8,128)(2,1)S(1)} %get-tuple-element.39), channel_id=1, source_target_pairs={{0,12},{4,0},{8,4},{12,8},{1,13},{5,1},{9,5},{13,9},{2,14},{6,2},{... | collective-permute-start | bytes 589832 | tf_op jit(solution)/shard_map/ppermute | solution.py:153
  23.0 1.0 %shard_map.60 = (bf16[96,1024]{1,0:T(8,128)(2,1)S(1)}, f32[288,1024]{1,0:T(8,128)S(1)}) custom-call(bf16[384,1024]{1,0:T(8,128)(2,1)S(1)} %shard_map.57.tokens_ref, bf16[1024,4096]{1,0:T(8,128)(2,1)S(1)} %copy-done), custom_call_target="tpu_custom_call" | custom-call | tf_op jit(solution)/shard_map/pallas_call | solution.py:140
  24.0 1.0 %shard_map.59 = (bf16[96,1024]{1,0:T(8,128)(2,1)S(1)}, f32[288,1024]{1,0:T(8,128)S(1)}) custom-call(bf16[384,1024]{1,0:T(8,128)(2,1)S(1)} %shard_map.57.tokens_ref, bf16[1024,4096]{1,0:T(8,128)(2,1)S(1)} %copy-done), custom_call_target="tpu_custom_call" | custom-call | tf_op jit(solution)/shard_map/pallas_call | solution.py:140
  24.9 1.0 %shard_map.58 = (bf16[96,1024]{1,0:T(8,128)(2,1)S(1)}, f32[288,1024]{1,0:T(8,128)S(1)}) custom-call(bf16[384,1024]{1,0:T(8,128)(2,1)S(1)} %shard_map.57.tokens_ref, bf16[1024,4096]{1,0:T(8,128)(2,1)S(1)} %copy-done), custom_call_target="tpu_custom_call" | custom-call | tf_op jit(solution)/shard_map/pallas_call | solution.py:140
  25.9 0.1 collective-permute-start.11
  26.0 0.4 collective-permute-start.8
  26.4 0.7 collective-permute-start.5
  27.2 1.1 %collective-permute-done.14 = bf16[96,1024]{1,0:T(8,128)(2,1)S(1)} collective-permute-done((bf16[96,1024]{1,0:T(8,128)(2,1)S(1)}, bf16[96,1024]{1,0:T(8,128)(2,1)S(1)}, u32[]{:S(2)}, u32[]{:S(2)}) %collective-permute-start.14) | collective-permute-done | bytes 196640 | tf_op jit(solution)/shard_map/ppermute | solution.py:153
  28.3 4.3 %collective-permute-start.15 = (bf16[96,1024]{1,0:T(8,128)(2,1)S(1)}, bf16[96,1024]{1,0:T(8,128)(2,1)S(1)}, u32[]{:S(2)}, u32[]{:S(2)}) collective-permute-start(bf16[96,1024]{1,0:T(8,128)(2,1)S(1)} %add_convert_fusion.1), channel_id=1, source_target_pairs={{0,12},{4,0},{8,4},{12,8},{1,13},{5,1},{9,5},{13,9},{2,14},{6,2},{... | collective-permute-start | bytes 589832 | tf_op jit(solution)/shard_map/ppermute | solution.py:153
  32.6 1.1 %collective-permute-done.11 = bf16[96,1024]{1,0:T(8,128)(2,1)S(1)} collective-permute-done((bf16[96,1024]{1,0:T(8,128)(2,1)S(1)}, bf16[96,1024]{1,0:T(8,128)(2,1)S(1)}, u32[]{:S(2)}, u32[]{:S(2)}) %collective-permute-start.11) | collective-permute-done | bytes 196640 | tf_op jit(solution)/shard_map/ppermute | solution.py:153
  33.8 3.0 %collective-permute-start.12 = (bf16[96,1024]{1,0:T(8,128)(2,1)S(1)}, bf16[96,1024]{1,0:T(8,128)(2,1)S(1)}, u32[]{:S(2)}, u32[]{:S(2)}) collective-permute-start(bf16[96,1024]{1,0:T(8,128)(2,1)S(1)} %add_convert_fusion.3), channel_id=1, source_target_pairs={{0,12},{4,0},{8,4},{12,8},{1,13},{5,1},{9,5},{13,9},{2,14},{6,2},{... | collective-permute-start | bytes 589832 | tf_op jit(solution)/shard_map/ppermute | solution.py:153
  36.8 1.1 %collective-permute-done.8 = bf16[96,1024]{1,0:T(8,128)(2,1)S(1)} collective-permute-done((bf16[96,1024]{1,0:T(8,128)(2,1)S(1)}, bf16[96,1024]{1,0:T(8,128)(2,1)S(1)}, u32[]{:S(2)}, u32[]{:S(2)}) %collective-permute-start.8) | collective-permute-done | bytes 196640 | tf_op jit(solution)/shard_map/ppermute | solution.py:153
  38.0 3.0 %collective-permute-start.9 = (bf16[96,1024]{1,0:T(8,128)(2,1)S(1)}, bf16[96,1024]{1,0:T(8,128)(2,1)S(1)}, u32[]{:S(2)}, u32[]{:S(2)}) collective-permute-start(bf16[96,1024]{1,0:T(8,128)(2,1)S(1)} %add_convert_fusion.5), channel_id=1, source_target_pairs={{0,12},{4,0},{8,4},{12,8},{1,13},{5,1},{9,5},{13,9},{2,14},{6,2},{... | collective-permute-start | bytes 589832 | tf_op jit(solution)/shard_map/ppermute | solution.py:153
  41.0 1.1 %collective-permute-done.5 = bf16[96,1024]{1,0:T(8,128)(2,1)S(1)} collective-permute-done((bf16[96,1024]{1,0:T(8,128)(2,1)S(1)}, bf16[96,1024]{1,0:T(8,128)(2,1)S(1)}, u32[]{:S(2)}, u32[]{:S(2)}) %collective-permute-start.5) | collective-permute-done | bytes 196640 | tf_op jit(solution)/shard_map/ppermute | solution.py:153
  42.2 3.0 %collective-permute-start.6 = (bf16[96,1024]{1,0:T(8,128)(2,1)S(1)}, bf16[96,1024]{1,0:T(8,128)(2,1)S(1)}, u32[]{:S(2)}, u32[]{:S(2)}) collective-permute-start(bf16[96,1024]{1,0:T(8,128)(2,1)S(1)} %add_convert_fusion.7), channel_id=1, source_target_pairs={{0,12},{4,0},{8,4},{12,8},{1,13},{5,1},{9,5},{13,9},{2,14},{6,2},{... | collective-permute-start | bytes 589832 | tf_op jit(solution)/shard_map/ppermute | solution.py:153
  45.2 1.1 %collective-permute-done.15 = bf16[96,1024]{1,0:T(8,128)(2,1)S(1)} collective-permute-done((bf16[96,1024]{1,0:T(8,128)(2,1)S(1)}, bf16[96,1024]{1,0:T(8,128)(2,1)S(1)}, u32[]{:S(2)}, u32[]{:S(2)}) %collective-permute-start.15) | collective-permute-done | bytes 196640 | tf_op jit(solution)/shard_map/ppermute | solution.py:153
  46.4 3.0 %collective-permute-start.16 = (bf16[96,1024]{1,0:T(8,128)(2,1)S(1)}, bf16[96,1024]{1,0:T(8,128)(2,1)S(1)}, u32[]{:S(2)}, u32[]{:S(2)}) collective-permute-start(bf16[96,1024]{1,0:T(8,128)(2,1)S(1)} %add_convert_fusion), channel_id=1, source_target_pairs={{0,12},{4,0},{8,4},{12,8},{1,13},{5,1},{9,5},{13,9},{2,14},{6,2},{... | collective-permute-start | bytes 589832 | tf_op jit(solution)/shard_map/ppermute | solution.py:153
  49.5 1.1 %collective-permute-done.12 = bf16[96,1024]{1,0:T(8,128)(2,1)S(1)} collective-permute-done((bf16[96,1024]{1,0:T(8,128)(2,1)S(1)}, bf16[96,1024]{1,0:T(8,128)(2,1)S(1)}, u32[]{:S(2)}, u32[]{:S(2)}) %collective-permute-start.12) | collective-permute-done | bytes 196640 | tf_op jit(solution)/shard_map/ppermute | solution.py:153
  50.6 3.0 %collective-permute-start.13 = (bf16[96,1024]{1,0:T(8,128)(2,1)S(1)}, bf16[96,1024]{1,0:T(8,128)(2,1)S(1)}, u32[]{:S(2)}, u32[]{:S(2)}) collective-permute-start(bf16[96,1024]{1,0:T(8,128)(2,1)S(1)} %add_convert_fusion.2), channel_id=1, source_target_pairs={{0,12},{4,0},{8,4},{12,8},{1,13},{5,1},{9,5},{13,9},{2,14},{6,2},{... | collective-permute-start | bytes 589832 | tf_op jit(solution)/shard_map/ppermute | solution.py:153
  53.7 1.1 %collective-permute-done.9 = bf16[96,1024]{1,0:T(8,128)(2,1)S(1)} collective-permute-done((bf16[96,1024]{1,0:T(8,128)(2,1)S(1)}, bf16[96,1024]{1,0:T(8,128)(2,1)S(1)}, u32[]{:S(2)}, u32[]{:S(2)}) %collective-permute-start.9) | collective-permute-done | bytes 196640 | tf_op jit(solution)/shard_map/ppermute | solution.py:153
  54.8 3.0 %collective-permute-start.10 = (bf16[96,1024]{1,0:T(8,128)(2,1)S(1)}, bf16[96,1024]{1,0:T(8,128)(2,1)S(1)}, u32[]{:S(2)}, u32[]{:S(2)}) collective-permute-start(bf16[96,1024]{1,0:T(8,128)(2,1)S(1)} %add_convert_fusion.4), channel_id=1, source_target_pairs={{0,12},{4,0},{8,4},{12,8},{1,13},{5,1},{9,5},{13,9},{2,14},{6,2},{... | collective-permute-start | bytes 589832 | tf_op jit(solution)/shard_map/ppermute | solution.py:153
  57.9 1.1 %collective-permute-done.6 = bf16[96,1024]{1,0:T(8,128)(2,1)S(1)} collective-permute-done((bf16[96,1024]{1,0:T(8,128)(2,1)S(1)}, bf16[96,1024]{1,0:T(8,128)(2,1)S(1)}, u32[]{:S(2)}, u32[]{:S(2)}) %collective-permute-start.6) | collective-permute-done | bytes 196640 | tf_op jit(solution)/shard_map/ppermute | solution.py:153
  59.1 3.0 %collective-permute-start.7 = (bf16[96,1024]{1,0:T(8,128)(2,1)S(1)}, bf16[96,1024]{1,0:T(8,128)(2,1)S(1)}, u32[]{:S(2)}, u32[]{:S(2)}) collective-permute-start(bf16[96,1024]{1,0:T(8,128)(2,1)S(1)} %add_convert_fusion.6), channel_id=1, source_target_pairs={{0,12},{4,0},{8,4},{12,8},{1,13},{5,1},{9,5},{13,9},{2,14},{6,2},{... | collective-permute-start | bytes 589832 | tf_op jit(solution)/shard_map/ppermute | solution.py:153
  62.1 1.1 %collective-permute-done.16 = bf16[96,1024]{1,0:T(8,128)(2,1)S(1)} collective-permute-done((bf16[96,1024]{1,0:T(8,128)(2,1)S(1)}, bf16[96,1024]{1,0:T(8,128)(2,1)S(1)}, u32[]{:S(2)}, u32[]{:S(2)}) %collective-permute-start.16) | collective-permute-done | bytes 196640 | tf_op jit(solution)/shard_map/ppermute | solution.py:153
  63.2 0.1 multiply_convert_fusion
  63.3 4.1 %collective-permute-done.13 = bf16[96,1024]{1,0:T(8,128)(2,1)S(1)} collective-permute-done((bf16[96,1024]{1,0:T(8,128)(2,1)S(1)}, bf16[96,1024]{1,0:T(8,128)(2,1)S(1)}, u32[]{:S(2)}, u32[]{:S(2)}) %collective-permute-start.13) | collective-permute-done | bytes 196640 | tf_op jit(solution)/shard_map/ppermute | solution.py:153
  67.4 0.1 multiply_convert_fusion.1
  67.5 4.1 %collective-permute-done.10 = bf16[96,1024]{1,0:T(8,128)(2,1)S(1)} collective-permute-done((bf16[96,1024]{1,0:T(8,128)(2,1)S(1)}, bf16[96,1024]{1,0:T(8,128)(2,1)S(1)}, u32[]{:S(2)}, u32[]{:S(2)}) %collective-permute-start.10) | collective-permute-done | bytes 196640 | tf_op jit(solution)/shard_map/ppermute | solution.py:153
  71.7 0.1 multiply_convert_fusion.2
  71.8 3.2 %collective-permute-done.7 = bf16[96,1024]{1,0:T(8,128)(2,1)S(1)} collective-permute-done((bf16[96,1024]{1,0:T(8,128)(2,1)S(1)}, bf16[96,1024]{1,0:T(8,128)(2,1)S(1)}, u32[]{:S(2)}, u32[]{:S(2)}) %collective-permute-start.7) | collective-permute-done | bytes 196640 | tf_op jit(solution)/shard_map/ppermute | solution.py:153
  75.0 0.1 multiply_convert_fusion.3
  75.1 0.9 %pad_maximum_fusion = bf16[96,4096]{1,0:T(8,128)(2,1)} fusion(bf16[96,1024]{1,0:T(8,128)(2,1)S(1)} %multiply_convert_fusion, bf16[96,1024]{1,0:T(8,128)(2,1)S(1)} %multiply_convert_fusion.1, bf16[96,1024]{1,0:T(8,128)(2,1)S(1)} %multiply_convert_fusion.2, bf16[96,1024]{1,0:T(8,128)(2,1)S(1)} %multiply_convert_fusion.3), kind=kLoop, calls=%fused_computation | loop fusion | flops 3145728 | bytes 1572864 | tf_op jit(solution)/shard_map/concatenate | solution.py:239
  (18 shorter events, 0.3 us)
Async XLA Ops:
  0.0 1.0 %copy-start.1 = (f32[64,32,32]{0,2,1:T(8,128)S(1)}, f32[64,32,32]{0,2,1:T(8,128)}, u32[]{:S(2)}) copy-start(f32[64,32,32]{0,2,1:T(8,128)} %param.5) | copy-start | bytes 786436
  1.2 6.8 %collective-permute-start = (bf16[1,32,128]{2,1,0:T(8,128)(2,1)S(1)}, bf16[1,32,128]{2,1,0:T(8,128)(2,1)S(1)}, u32[]{:S(2)}, u32[]{:S(2)}) collective-permute-start(bf16[1,32,128]{2,1,0:T(8,128)(2,1)S(1)} %get-tuple-element.24), channel_id=1, source_target_pairs={{0,4},{4,8},{8,12},{12,0},{1,5},{5,9},{9,13},{13,1},{2,6},{6,10},{... | collective-permute-start | bytes 24584 | tf_op jit(solution)/shard_map/ppermute | solution.py:153
  4.2 3.8 %collective-permute-start.1 = (bf16[1,32,128]{2,1,0:T(8,128)(2,1)S(1)}, bf16[1,32,128]{2,1,0:T(8,128)(2,1)S(1)}, u32[]{:S(2)}, u32[]{:S(2)}) collective-permute-start(bf16[1,32,128]{2,1,0:T(8,128)(2,1)S(1)} %get-tuple-element.25), channel_id=1, source_target_pairs={{0,12},{4,0},{8,4},{12,8},{1,13},{5,1},{9,5},{13,9},{2,14},{6,2},{... | collective-permute-start | bytes 24584 | tf_op jit(solution)/shard_map/ppermute | solution.py:153
  8.0 5.2 %collective-permute-start.3 = (bf16[18,32,128]{2,1,0:T(8,128)(2,1)S(1)}, bf16[18,32,128]{2,1,0:T(8,128)(2,1)S(1)}, u32[]{:S(2)}, u32[]{:S(2)}) collective-permute-start(bf16[18,32,128]{2,1,0:T(8,128)(2,1)S(1)} %constant_dynamic-update-slice_fusion.refs_0_), channel_id=1, source_target_pairs={{0,2},{2,0},{1,3},{3,1},{4,6},{6,4},{5,7},{7,5},{8,10},{10,8},{9,1... | collective-permute-start | bytes 442376 | tf_op jit(solution)/shard_map/ppermute | solution.py:153
  9.7 1.0 %copy-start.2 = (f32[9,64,64]{2,1,0:T(8,128)S(1)}, f32[9,64,64]{2,1,0:T(8,128)}, u32[]{:S(2)}) copy-start(f32[9,64,64]{2,1,0:T(8,128)} %first_ref.1) | copy-start | bytes 442372
  10.6 1.0 %copy-start.3 = (f32[9,64,64]{2,1,0:T(8,128)S(1)}, f32[9,64,64]{2,1,0:T(8,128)}, u32[]{:S(2)}) copy-start(f32[9,64,64]{2,1,0:T(8,128)} %second_ref.1) | copy-start | bytes 442372
  11.6 0.9 %copy-start.4 = (bf16[256,384]{1,0:T(8,128)(2,1)S(1)}, bf16[256,384]{1,0:T(8,128)(2,1)}, u32[]{:S(2)}) copy-start(bf16[256,384]{1,0:T(8,128)(2,1)} %embed_ref.1) | copy-start | bytes 589828
  12.5 5.7 %copy-start = (bf16[1024,4096]{1,0:T(8,128)(2,1)S(1)}, bf16[1024,4096]{1,0:T(8,128)(2,1)}, u32[]{:S(2)}) copy-start(bf16[1024,4096]{1,0:T(8,128)(2,1)} %mixing_ref.7) | copy-start | bytes 25165828
  13.1 1.4 %collective-permute-start.2 = (bf16[18,32,128]{2,1,0:T(8,128)(2,1)S(1)}, bf16[18,32,128]{2,1,0:T(8,128)(2,1)S(1)}, u32[]{:S(2)}, u32[]{:S(2)}) collective-permute-start(bf16[18,32,128]{2,1,0:T(8,128)(2,1)S(1)} %constant_dynamic-update-slice_fusion.refs_0_), channel_id=1, source_target_pairs={{0,1},{1,0},{2,3},{3,2},{4,5},{5,4},{6,7},{7,6},{8,9},{9,8},{10,11... | collective-permute-start | bytes 442376 | tf_op jit(solution)/shard_map/ppermute | solution.py:153
  13.2 1.6 %collective-permute-start.4 = (bf16[18,32,128]{2,1,0:T(8,128)(2,1)S(1)}, bf16[18,32,128]{2,1,0:T(8,128)(2,1)S(1)}, u32[]{:S(2)}, u32[]{:S(2)}) collective-permute-start(bf16[18,32,128]{2,1,0:T(8,128)(2,1)S(1)} %collective-permute-done.3.refs_2_), channel_id=1, source_target_pairs={{0,1},{1,0},{2,3},{3,2},{4,5},{5,4},{6,7},{7,6},{8,9},{9,8},{10,11... | collective-permute-start | bytes 442376 | tf_op jit(solution)/shard_map/ppermute | solution.py:153
  19.2 9.1 %collective-permute-start.14 = (bf16[96,1024]{1,0:T(8,128)(2,1)S(1)}, bf16[96,1024]{1,0:T(8,128)(2,1)S(1)}, u32[]{:S(2)}, u32[]{:S(2)}) collective-permute-start(bf16[96,1024]{1,0:T(8,128)(2,1)S(1)} %get-tuple-element.39), channel_id=1, source_target_pairs={{0,12},{4,0},{8,4},{12,8},{1,13},{5,1},{9,5},{13,9},{2,14},{6,2},{... | collective-permute-start | bytes 589832 | tf_op jit(solution)/shard_map/ppermute | solution.py:153
  25.9 7.8 %collective-permute-start.11 = (bf16[96,1024]{1,0:T(8,128)(2,1)S(1)}, bf16[96,1024]{1,0:T(8,128)(2,1)S(1)}, u32[]{:S(2)}, u32[]{:S(2)}) collective-permute-start(bf16[96,1024]{1,0:T(8,128)(2,1)S(1)} %get-tuple-element.37), channel_id=1, source_target_pairs={{0,12},{4,0},{8,4},{12,8},{1,13},{5,1},{9,5},{13,9},{2,14},{6,2},{... | collective-permute-start | bytes 589832 | tf_op jit(solution)/shard_map/ppermute | solution.py:153
  26.0 11.9 %collective-permute-start.8 = (bf16[96,1024]{1,0:T(8,128)(2,1)S(1)}, bf16[96,1024]{1,0:T(8,128)(2,1)S(1)}, u32[]{:S(2)}, u32[]{:S(2)}) collective-permute-start(bf16[96,1024]{1,0:T(8,128)(2,1)S(1)} %get-tuple-element.35), channel_id=1, source_target_pairs={{0,12},{4,0},{8,4},{12,8},{1,13},{5,1},{9,5},{13,9},{2,14},{6,2},{... | collective-permute-start | bytes 589832 | tf_op jit(solution)/shard_map/ppermute | solution.py:153
  26.4 15.7 %collective-permute-start.5 = (bf16[96,1024]{1,0:T(8,128)(2,1)S(1)}, bf16[96,1024]{1,0:T(8,128)(2,1)S(1)}, u32[]{:S(2)}, u32[]{:S(2)}) collective-permute-start(bf16[96,1024]{1,0:T(8,128)(2,1)S(1)} %get-tuple-element.33), channel_id=1, source_target_pairs={{0,12},{4,0},{8,4},{12,8},{1,13},{5,1},{9,5},{13,9},{2,14},{6,2},{... | collective-permute-start | bytes 589832 | tf_op jit(solution)/shard_map/ppermute | solution.py:153
  28.3 18.1 %collective-permute-start.15 = (bf16[96,1024]{1,0:T(8,128)(2,1)S(1)}, bf16[96,1024]{1,0:T(8,128)(2,1)S(1)}, u32[]{:S(2)}, u32[]{:S(2)}) collective-permute-start(bf16[96,1024]{1,0:T(8,128)(2,1)S(1)} %add_convert_fusion.1), channel_id=1, source_target_pairs={{0,12},{4,0},{8,4},{12,8},{1,13},{5,1},{9,5},{13,9},{2,14},{6,2},{... | collective-permute-start | bytes 589832 | tf_op jit(solution)/shard_map/ppermute | solution.py:153
  33.8 16.8 %collective-permute-start.12 = (bf16[96,1024]{1,0:T(8,128)(2,1)S(1)}, bf16[96,1024]{1,0:T(8,128)(2,1)S(1)}, u32[]{:S(2)}, u32[]{:S(2)}) collective-permute-start(bf16[96,1024]{1,0:T(8,128)(2,1)S(1)} %add_convert_fusion.3), channel_id=1, source_target_pairs={{0,12},{4,0},{8,4},{12,8},{1,13},{5,1},{9,5},{13,9},{2,14},{6,2},{... | collective-permute-start | bytes 589832 | tf_op jit(solution)/shard_map/ppermute | solution.py:153
  38.0 16.8 %collective-permute-start.9 = (bf16[96,1024]{1,0:T(8,128)(2,1)S(1)}, bf16[96,1024]{1,0:T(8,128)(2,1)S(1)}, u32[]{:S(2)}, u32[]{:S(2)}) collective-permute-start(bf16[96,1024]{1,0:T(8,128)(2,1)S(1)} %add_convert_fusion.5), channel_id=1, source_target_pairs={{0,12},{4,0},{8,4},{12,8},{1,13},{5,1},{9,5},{13,9},{2,14},{6,2},{... | collective-permute-start | bytes 589832 | tf_op jit(solution)/shard_map/ppermute | solution.py:153
  42.2 16.8 %collective-permute-start.6 = (bf16[96,1024]{1,0:T(8,128)(2,1)S(1)}, bf16[96,1024]{1,0:T(8,128)(2,1)S(1)}, u32[]{:S(2)}, u32[]{:S(2)}) collective-permute-start(bf16[96,1024]{1,0:T(8,128)(2,1)S(1)} %add_convert_fusion.7), channel_id=1, source_target_pairs={{0,12},{4,0},{8,4},{12,8},{1,13},{5,1},{9,5},{13,9},{2,14},{6,2},{... | collective-permute-start | bytes 589832 | tf_op jit(solution)/shard_map/ppermute | solution.py:153
  46.4 16.8 %collective-permute-start.16 = (bf16[96,1024]{1,0:T(8,128)(2,1)S(1)}, bf16[96,1024]{1,0:T(8,128)(2,1)S(1)}, u32[]{:S(2)}, u32[]{:S(2)}) collective-permute-start(bf16[96,1024]{1,0:T(8,128)(2,1)S(1)} %add_convert_fusion), channel_id=1, source_target_pairs={{0,12},{4,0},{8,4},{12,8},{1,13},{5,1},{9,5},{13,9},{2,14},{6,2},{... | collective-permute-start | bytes 589832 | tf_op jit(solution)/shard_map/ppermute | solution.py:153
  50.6 16.8 %collective-permute-start.13 = (bf16[96,1024]{1,0:T(8,128)(2,1)S(1)}, bf16[96,1024]{1,0:T(8,128)(2,1)S(1)}, u32[]{:S(2)}, u32[]{:S(2)}) collective-permute-start(bf16[96,1024]{1,0:T(8,128)(2,1)S(1)} %add_convert_fusion.2), channel_id=1, source_target_pairs={{0,12},{4,0},{8,4},{12,8},{1,13},{5,1},{9,5},{13,9},{2,14},{6,2},{... | collective-permute-start | bytes 589832 | tf_op jit(solution)/shard_map/ppermute | solution.py:153
  54.8 16.8 %collective-permute-start.10 = (bf16[96,1024]{1,0:T(8,128)(2,1)S(1)}, bf16[96,1024]{1,0:T(8,128)(2,1)S(1)}, u32[]{:S(2)}, u32[]{:S(2)}) collective-permute-start(bf16[96,1024]{1,0:T(8,128)(2,1)S(1)} %add_convert_fusion.4), channel_id=1, source_target_pairs={{0,12},{4,0},{8,4},{12,8},{1,13},{5,1},{9,5},{13,9},{2,14},{6,2},{... | collective-permute-start | bytes 589832 | tf_op jit(solution)/shard_map/ppermute | solution.py:153
  59.1 15.9 %collective-permute-start.7 = (bf16[96,1024]{1,0:T(8,128)(2,1)S(1)}, bf16[96,1024]{1,0:T(8,128)(2,1)S(1)}, u32[]{:S(2)}, u32[]{:S(2)}) collective-permute-start(bf16[96,1024]{1,0:T(8,128)(2,1)S(1)} %add_convert_fusion.6), channel_id=1, source_target_pairs={{0,12},{4,0},{8,4},{12,8},{1,13},{5,1},{9,5},{13,9},{2,14},{6,2},{... | collective-permute-start | bytes 589832 | tf_op jit(solution)/shard_map/ppermute | solution.py:153

commit v6 on v5

--- a/solution.py
+++ b/solution.py
@@ -47,7 +47,7 @@
     chans = embed_ref.shape[0] // 4
     embed = embed_ref.shape[1]
     count = lax.axis_size("tok")
-    turn = lax.rem(lax.axis_index("tok") + 1, count) * (embed // count)
+    turn = lax.axis_index("tok") * (embed // count)
     turned_embed = pltpu.roll(embed_ref[...].astype(jnp.float32), lax.rem(embed - turn, embed), axis=1)
     for first in range(0, embed, LANES):
         scratch[...] = turned_embed[:, first : first + LANES]
@@ -200,13 +200,13 @@
 
 
 def partial_kernel(first, tokens_ref, mixing_ref, sent_ref, kept_ref):
-    rows, width = sent_ref.shape
+    width = sent_ref.shape[1]
     step = STEP if width % STEP == 0 else width
     tokens = tokens_ref[...]
     for at in range(0, width, step):
         product = jnp.dot(tokens, mixing_ref[:, pl.ds(first + at, step)], preferred_element_type=jnp.float32)
-        sent_ref[:, pl.ds(at, step)] = product[:rows].astype(sent_ref.dtype)
-        kept_ref[:, pl.ds(at, step)] = product[rows:]
+        kept_ref[:, pl.ds(at, step)] = product[: kept_ref.shape[0]]
+        sent_ref[:, pl.ds(at, step)] = product[kept_ref.shape[0] :].astype(sent_ref.dtype)
 
 
 def partial(tokens, token_mixing, first, width, rows):
@@ -231,8 +231,9 @@
         kept.append(others)
     for step in range(1, count):
         for piece in range(pieces):
-            arrived = turned(travelling[piece], "tok", -1).astype(jnp.float32)
-            summed = arrived + kept[piece][(step - 1) * rows : step * rows]
+            arrived = turned(travelling[piece], "tok", 1).astype(jnp.float32)
+            at = (count - 1 - step) * rows
+            summed = arrived + kept[piece][at : at + rows]
             if step == count - 1:
                 summed = gelu(summed)
             travelling[piece] = summed.astype(jnp.bfloat16)

time: 76.2 us -> 76 us (level)
  starting transfers between devices: 38.1 us -> 12.9 us
  waiting for transfers between devices: 24.2 us -> 49 us
    ppermute x17, starting transfers between devices: 38.1 us -> 12.9 us  [turned(): lax.ppermute(value, axis, [(i, (i + away) % count) for i in range(count)])]
    ppermute x17, waiting for transfers between devices: 24.2 us -> 49 us  [turned(): lax.ppermute(value, axis, [(i, (i + away) % count) for i in range(count)])]
where the time goes in v6:
time: 76 us; the launch traced here: 75.8 us
  waiting for transfers between devices  49 us (64%)
  starting transfers between devices  12.9 us (17%)
  Pallas kernels  8.01 us (11%)
  local copies, waits for them, and re-layouts  3.91 us (5%)
  other arithmetic  1.65 us (2%)
    ppermute x17, waiting for transfers between devices, turned(): lax.ppermute(value, axis, [(i, (i + away) % count) for i in range(count)])  49 us
    ppermute x17, starting transfers between devices, turned(): lax.ppermute(value, axis, [(i, (i + away) % count) for i in range(count)])  12.9 us
    pallas_call x7, Pallas kernels, call(): pl.pallas_call(kernel, out_shape=out_shape, in_specs=[pl.BlockSpec(memory...  8.01 us
    unnamed x10, local copies, waits for them, and re-layouts  3.89 us
  transfers between devices with their start and end apart: 17, of which 15 were waited for; matrix products, arithmetic and copies ran while one was open for 1% of the time, Pallas kernels for 5%

profile of v6, /device:TPU:0, one launch (start us, length us, event | category | flops | bytes accessed | tf_op | source)
XLA Modules:
  0.0 75.8 jit_solution(14955082056458860097)
XLA Ops:
  0.0 1.0 %copy-done.1 = f32[64,32,32]{0,2,1:T(8,128)S(1)} copy-done((f32[64,32,32]{0,2,1:T(8,128)S(1)}, f32[64,32,32]{0,2,1:T(8,128)}, u32[]{:S(2)}) %copy-start.1) | copy-done | bytes 262168
  1.0 0.1 shard_map.55
  1.2 3.1 %collective-permute-start = (bf16[1,32,128]{2,1,0:T(8,128)(2,1)S(1)}, bf16[1,32,128]{2,1,0:T(8,128)(2,1)S(1)}, u32[]{:S(2)}, u32[]{:S(2)}) collective-permute-start(bf16[1,32,128]{2,1,0:T(8,128)(2,1)S(1)} %get-tuple-element.24), channel_id=1, source_target_pairs={{0,4},{4,8},{8,12},{12,0},{1,5},{5,9},{9,13},{13,1},{2,6},{6,10},{... | collective-permute-start | bytes 24584 | tf_op jit(solution)/shard_map/ppermute | solution.py:153
  4.2 2.1 %collective-permute-start.1 = (bf16[1,32,128]{2,1,0:T(8,128)(2,1)S(1)}, bf16[1,32,128]{2,1,0:T(8,128)(2,1)S(1)}, u32[]{:S(2)}, u32[]{:S(2)}) collective-permute-start(bf16[1,32,128]{2,1,0:T(8,128)(2,1)S(1)} %get-tuple-element.25), channel_id=1, source_target_pairs={{0,12},{4,0},{8,4},{12,8},{1,13},{5,1},{9,5},{13,9},{2,14},{6,2},{... | collective-permute-start | bytes 24584 | tf_op jit(solution)/shard_map/ppermute | solution.py:153
  6.3 1.6 %collective-permute-done = bf16[1,32,128]{2,1,0:T(8,128)(2,1)S(1)} collective-permute-done((bf16[1,32,128]{2,1,0:T(8,128)(2,1)S(1)}, bf16[1,32,128]{2,1,0:T(8,128)(2,1)S(1)}, u32[]{:S(2)}, u32[]{:S(2)}) %collective-permute-start) | collective-permute-done | bytes 8224 | tf_op jit(solution)/shard_map/ppermute | solution.py:153
  8.0 1.7 %collective-permute-start.3 = (bf16[18,32,128]{2,1,0:T(8,128)(2,1)S(1)}, bf16[18,32,128]{2,1,0:T(8,128)(2,1)S(1)}, u32[]{:S(2)}, u32[]{:S(2)}) collective-permute-start(bf16[18,32,128]{2,1,0:T(8,128)(2,1)S(1)} %constant_dynamic-update-slice_fusion.refs_0_), channel_id=1, source_target_pairs={{0,2},{2,0},{1,3},{3,1},{4,6},{6,4},{5,7},{7,5},{8,10},{10,8},{9,1... | collective-permute-start | bytes 442376 | tf_op jit(solution)/shard_map/ppermute | solution.py:153
  9.7 1.0 %copy-done.2 = f32[9,64,64]{2,1,0:T(8,128)S(1)} copy-done((f32[9,64,64]{2,1,0:T(8,128)S(1)}, f32[9,64,64]{2,1,0:T(8,128)}, u32[]{:S(2)}) %copy-start.2) | copy-done | bytes 147480
  10.6 1.0 %copy-done.3 = f32[9,64,64]{2,1,0:T(8,128)S(1)} copy-done((f32[9,64,64]{2,1,0:T(8,128)S(1)}, f32[9,64,64]{2,1,0:T(8,128)}, u32[]{:S(2)}) %copy-start.3) | copy-done | bytes 147480
  11.6 0.9 %copy-done.4 = bf16[256,384]{1,0:T(8,128)(2,1)S(1)} copy-done((bf16[256,384]{1,0:T(8,128)(2,1)S(1)}, bf16[256,384]{1,0:T(8,128)(2,1)}, u32[]{:S(2)}) %copy-start.4) | copy-done | bytes 196632
  12.5 0.6 shard_map.56
  13.1 0.1 collective-permute-start.2
  13.2 0.5 collective-permute-start.4
  13.7 0.9 %collective-permute-done.2.refs_1_ = bf16[18,32,128]{2,1,0:T(8,128)(2,1)S(1)} collective-permute-done((bf16[18,32,128]{2,1,0:T(8,128)(2,1)S(1)}, bf16[18,32,128]{2,1,0:T(8,128)(2,1)S(1)}, u32[]{:S(2)}, u32[]{:S(2)}) %collective-permute-start.2) | collective-permute-done | bytes 147488 | tf_op jit(solution)/shard_map/ppermute | solution.py:153
  14.6 0.2 collective-permute-done.4.refs_3_
  14.8 3.4 %shard_map.57.tokens_ref = bf16[384,1024]{1,0:T(8,128)(2,1)S(1)} custom-call(bf16[18,32,128]{2,1,0:T(8,128)(2,1)S(1)} %constant_dynamic-update-slice_fusion.refs_0_, bf16[18,32,128]{2,1,0:T(8,128)(2,1)S(1)} %collective-permute-done.2.refs_1_, bf16[18,32,128]{2,1,0:T(8,128)(2,1)S(1)} %collective-permute-done.3.refs_2_, ...), custom_call_target="tpu_custom_call" | custom-call | flops 2139095040 | bytes 589824 | tf_op jit(solution)/shard_map/pallas_call | solution.py:140
  18.2 1.0 %shard_map.61 = (bf16[96,1024]{1,0:T(8,128)(2,1)S(1)}, f32[288,1024]{1,0:T(8,128)S(1)}) custom-call(bf16[384,1024]{1,0:T(8,128)(2,1)S(1)} %shard_map.57.tokens_ref, bf16[1024,4096]{1,0:T(8,128)(2,1)S(1)} %copy-done), custom_call_target="tpu_custom_call" | custom-call | tf_op jit(solution)/shard_map/pallas_call | solution.py:140
  19.2 1.3 %collective-permute-start.14 = (bf16[96,1024]{1,0:T(8,128)(2,1)S(1)}, bf16[96,1024]{1,0:T(8,128)(2,1)S(1)}, u32[]{:S(2)}, u32[]{:S(2)}) collective-permute-start(bf16[96,1024]{1,0:T(8,128)(2,1)S(1)} %get-tuple-element.39), channel_id=1, source_target_pairs={{0,4},{4,8},{8,12},{12,0},{1,5},{5,9},{9,13},{13,1},{2,6},{6,10},{... | collective-permute-start | bytes 589832 | tf_op jit(solution)/shard_map/ppermute | solution.py:153
  20.5 1.0 %shard_map.60 = (bf16[96,1024]{1,0:T(8,128)(2,1)S(1)}, f32[288,1024]{1,0:T(8,128)S(1)}) custom-call(bf16[384,1024]{1,0:T(8,128)(2,1)S(1)} %shard_map.57.tokens_ref, bf16[1024,4096]{1,0:T(8,128)(2,1)S(1)} %copy-done), custom_call_target="tpu_custom_call" | custom-call | tf_op jit(solution)/shard_map/pallas_call | solution.py:140
  21.5 1.0 %shard_map.59 = (bf16[96,1024]{1,0:T(8,128)(2,1)S(1)}, f32[288,1024]{1,0:T(8,128)S(1)}) custom-call(bf16[384,1024]{1,0:T(8,128)(2,1)S(1)} %shard_map.57.tokens_ref, bf16[1024,4096]{1,0:T(8,128)(2,1)S(1)} %copy-done), custom_call_target="tpu_custom_call" | custom-call | tf_op jit(solution)/shard_map/pallas_call | solution.py:140
  22.5 1.0 %shard_map.58 = (bf16[96,1024]{1,0:T(8,128)(2,1)S(1)}, f32[288,1024]{1,0:T(8,128)S(1)}) custom-call(bf16[384,1024]{1,0:T(8,128)(2,1)S(1)} %shard_map.57.tokens_ref, bf16[1024,4096]{1,0:T(8,128)(2,1)S(1)} %copy-done), custom_call_target="tpu_custom_call" | custom-call | tf_op jit(solution)/shard_map/pallas_call | solution.py:140
  23.5 1.6 %collective-permute-start.11 = (bf16[96,1024]{1,0:T(8,128)(2,1)S(1)}, bf16[96,1024]{1,0:T(8,128)(2,1)S(1)}, u32[]{:S(2)}, u32[]{:S(2)}) collective-permute-start(bf16[96,1024]{1,0:T(8,128)(2,1)S(1)} %get-tuple-element.37), channel_id=1, source_target_pairs={{0,4},{4,8},{8,12},{12,0},{1,5},{5,9},{9,13},{13,1},{2,6},{6,10},{... | collective-permute-start | bytes 589832 | tf_op jit(solution)/shard_map/ppermute | solution.py:153
  25.1 2.0 %collective-permute-start.8 = (bf16[96,1024]{1,0:T(8,128)(2,1)S(1)}, bf16[96,1024]{1,0:T(8,128)(2,1)S(1)}, u32[]{:S(2)}, u32[]{:S(2)}) collective-permute-start(bf16[96,1024]{1,0:T(8,128)(2,1)S(1)} %get-tuple-element.35), channel_id=1, source_target_pairs={{0,4},{4,8},{8,12},{12,0},{1,5},{5,9},{9,13},{13,1},{2,6},{6,10},{... | collective-permute-start | bytes 589832 | tf_op jit(solution)/shard_map/ppermute | solution.py:153
  27.1 0.1 collective-permute-start.5
  27.2 1.5 %collective-permute-done.14 = bf16[96,1024]{1,0:T(8,128)(2,1)S(1)} collective-permute-done((bf16[96,1024]{1,0:T(8,128)(2,1)S(1)}, bf16[96,1024]{1,0:T(8,128)(2,1)S(1)}, u32[]{:S(2)}, u32[]{:S(2)}) %collective-permute-start.14) | collective-permute-done | bytes 196640 | tf_op jit(solution)/shard_map/ppermute | solution.py:153
  28.8 0.1 collective-permute-start.15
  28.8 4.3 %collective-permute-done.11 = bf16[96,1024]{1,0:T(8,128)(2,1)S(1)} collective-permute-done((bf16[96,1024]{1,0:T(8,128)(2,1)S(1)}, bf16[96,1024]{1,0:T(8,128)(2,1)S(1)}, u32[]{:S(2)}, u32[]{:S(2)}) %collective-permute-start.11) | collective-permute-done | bytes 196640 | tf_op jit(solution)/shard_map/ppermute | solution.py:153
  33.2 0.1 collective-permute-start.12
  33.3 4.1 %collective-permute-done.8 = bf16[96,1024]{1,0:T(8,128)(2,1)S(1)} collective-permute-done((bf16[96,1024]{1,0:T(8,128)(2,1)S(1)}, bf16[96,1024]{1,0:T(8,128)(2,1)S(1)}, u32[]{:S(2)}, u32[]{:S(2)}) %collective-permute-start.8) | collective-permute-done | bytes 196640 | tf_op jit(solution)/shard_map/ppermute | solution.py:153
  37.4 0.1 collective-permute-start.9
  37.5 4.1 %collective-permute-done.5 = bf16[96,1024]{1,0:T(8,128)(2,1)S(1)} collective-permute-done((bf16[96,1024]{1,0:T(8,128)(2,1)S(1)}, bf16[96,1024]{1,0:T(8,128)(2,1)S(1)}, u32[]{:S(2)}, u32[]{:S(2)}) %collective-permute-start.5) | collective-permute-done | bytes 196640 | tf_op jit(solution)/shard_map/ppermute | solution.py:153
  41.6 0.1 collective-permute-start.6
  41.7 4.1 %collective-permute-done.15 = bf16[96,1024]{1,0:T(8,128)(2,1)S(1)} collective-permute-done((bf16[96,1024]{1,0:T(8,128)(2,1)S(1)}, bf16[96,1024]{1,0:T(8,128)(2,1)S(1)}, u32[]{:S(2)}, u32[]{:S(2)}) %collective-permute-start.15) | collective-permute-done | bytes 196640 | tf_op jit(solution)/shard_map/ppermute | solution.py:153
  45.9 0.1 collective-permute-start.16
  45.9 4.1 %collective-permute-done.12 = bf16[96,1024]{1,0:T(8,128)(2,1)S(1)} collective-permute-done((bf16[96,1024]{1,0:T(8,128)(2,1)S(1)}, bf16[96,1024]{1,0:T(8,128)(2,1)S(1)}, u32[]{:S(2)}, u32[]{:S(2)}) %collective-permute-start.12) | collective-permute-done | bytes 196640 | tf_op jit(solution)/shard_map/ppermute | solution.py:153
  50.1 0.1 collective-permute-start.13
  50.1 4.1 %collective-permute-done.9 = bf16[96,1024]{1,0:T(8,128)(2,1)S(1)} collective-permute-done((bf16[96,1024]{1,0:T(8,128)(2,1)S(1)}, bf16[96,1024]{1,0:T(8,128)(2,1)S(1)}, u32[]{:S(2)}, u32[]{:S(2)}) %collective-permute-start.9) | collective-permute-done | bytes 196640 | tf_op jit(solution)/shard_map/ppermute | solution.py:153
  54.3 0.1 collective-permute-start.10
  54.3 4.1 %collective-permute-done.6 = bf16[96,1024]{1,0:T(8,128)(2,1)S(1)} collective-permute-done((bf16[96,1024]{1,0:T(8,128)(2,1)S(1)}, bf16[96,1024]{1,0:T(8,128)(2,1)S(1)}, u32[]{:S(2)}, u32[]{:S(2)}) %collective-permute-start.6) | collective-permute-done | bytes 196640 | tf_op jit(solution)/shard_map/ppermute | solution.py:153
  58.5 0.1 collective-permute-start.7
  58.6 4.1 %collective-permute-done.16 = bf16[96,1024]{1,0:T(8,128)(2,1)S(1)} collective-permute-done((bf16[96,1024]{1,0:T(8,128)(2,1)S(1)}, bf16[96,1024]{1,0:T(8,128)(2,1)S(1)}, u32[]{:S(2)}, u32[]{:S(2)}) %collective-permute-start.16) | collective-permute-done | bytes 196640 | tf_op jit(solution)/shard_map/ppermute | solution.py:153
  62.7 0.1 multiply_convert_fusion
  62.8 4.1 %collective-permute-done.13 = bf16[96,1024]{1,0:T(8,128)(2,1)S(1)} collective-permute-done((bf16[96,1024]{1,0:T(8,128)(2,1)S(1)}, bf16[96,1024]{1,0:T(8,128)(2,1)S(1)}, u32[]{:S(2)}, u32[]{:S(2)}) %collective-permute-start.13) | collective-permute-done | bytes 196640 | tf_op jit(solution)/shard_map/ppermute | solution.py:153
  66.9 0.1 multiply_convert_fusion.1
  67.0 4.1 %collective-permute-done.10 = bf16[96,1024]{1,0:T(8,128)(2,1)S(1)} collective-permute-done((bf16[96,1024]{1,0:T(8,128)(2,1)S(1)}, bf16[96,1024]{1,0:T(8,128)(2,1)S(1)}, u32[]{:S(2)}, u32[]{:S(2)}) %collective-permute-start.10) | collective-permute-done | bytes 196640 | tf_op jit(solution)/shard_map/ppermute | solution.py:153
  71.1 0.1 multiply_convert_fusion.2
  71.2 3.5 %collective-permute-done.7 = bf16[96,1024]{1,0:T(8,128)(2,1)S(1)} collective-permute-done((bf16[96,1024]{1,0:T(8,128)(2,1)S(1)}, bf16[96,1024]{1,0:T(8,128)(2,1)S(1)}, u32[]{:S(2)}, u32[]{:S(2)}) %collective-permute-start.7) | collective-permute-done | bytes 196640 | tf_op jit(solution)/shard_map/ppermute | solution.py:153
  74.7 0.1 multiply_convert_fusion.3
  74.8 0.9 %pad_maximum_fusion = bf16[96,4096]{1,0:T(8,128)(2,1)} fusion(bf16[96,1024]{1,0:T(8,128)(2,1)S(1)} %multiply_convert_fusion, bf16[96,1024]{1,0:T(8,128)(2,1)S(1)} %multiply_convert_fusion.1, bf16[96,1024]{1,0:T(8,128)(2,1)S(1)} %multiply_convert_fusion.2, bf16[96,1024]{1,0:T(8,128)(2,1)S(1)} %multiply_convert_fusion.3), kind=kLoop, calls=%fused_computation | loop fusion | flops 3145728 | bytes 1572864 | tf_op jit(solution)/shard_map/concatenate | solution.py:240
  (18 shorter events, 0.3 us)
Async XLA Ops:
  0.0 1.0 %copy-start.1 = (f32[64,32,32]{0,2,1:T(8,128)S(1)}, f32[64,32,32]{0,2,1:T(8,128)}, u32[]{:S(2)}) copy-start(f32[64,32,32]{0,2,1:T(8,128)} %param.5) | copy-start | bytes 786436
  1.2 6.8 %collective-permute-start = (bf16[1,32,128]{2,1,0:T(8,128)(2,1)S(1)}, bf16[1,32,128]{2,1,0:T(8,128)(2,1)S(1)}, u32[]{:S(2)}, u32[]{:S(2)}) collective-permute-start(bf16[1,32,128]{2,1,0:T(8,128)(2,1)S(1)} %get-tuple-element.24), channel_id=1, source_target_pairs={{0,4},{4,8},{8,12},{12,0},{1,5},{5,9},{9,13},{13,1},{2,6},{6,10},{... | collective-permute-start | bytes 24584 | tf_op jit(solution)/shard_map/ppermute | solution.py:153
  4.2 3.8 %collective-permute-start.1 = (bf16[1,32,128]{2,1,0:T(8,128)(2,1)S(1)}, bf16[1,32,128]{2,1,0:T(8,128)(2,1)S(1)}, u32[]{:S(2)}, u32[]{:S(2)}) collective-permute-start(bf16[1,32,128]{2,1,0:T(8,128)(2,1)S(1)} %get-tuple-element.25), channel_id=1, source_target_pairs={{0,12},{4,0},{8,4},{12,8},{1,13},{5,1},{9,5},{13,9},{2,14},{6,2},{... | collective-permute-start | bytes 24584 | tf_op jit(solution)/shard_map/ppermute | solution.py:153
  8.0 5.2 %collective-permute-start.3 = (bf16[18,32,128]{2,1,0:T(8,128)(2,1)S(1)}, bf16[18,32,128]{2,1,0:T(8,128)(2,1)S(1)}, u32[]{:S(2)}, u32[]{:S(2)}) collective-permute-start(bf16[18,32,128]{2,1,0:T(8,128)(2,1)S(1)} %constant_dynamic-update-slice_fusion.refs_0_), channel_id=1, source_target_pairs={{0,2},{2,0},{1,3},{3,1},{4,6},{6,4},{5,7},{7,5},{8,10},{10,8},{9,1... | collective-permute-start | bytes 442376 | tf_op jit(solution)/shard_map/ppermute | solution.py:153
  9.7 1.0 %copy-start.2 = (f32[9,64,64]{2,1,0:T(8,128)S(1)}, f32[9,64,64]{2,1,0:T(8,128)}, u32[]{:S(2)}) copy-start(f32[9,64,64]{2,1,0:T(8,128)} %first_ref.1) | copy-start | bytes 442372
  10.6 1.0 %copy-start.3 = (f32[9,64,64]{2,1,0:T(8,128)S(1)}, f32[9,64,64]{2,1,0:T(8,128)}, u32[]{:S(2)}) copy-start(f32[9,64,64]{2,1,0:T(8,128)} %second_ref.1) | copy-start | bytes 442372
  11.6 0.9 %copy-start.4 = (bf16[256,384]{1,0:T(8,128)(2,1)S(1)}, bf16[256,384]{1,0:T(8,128)(2,1)}, u32[]{:S(2)}) copy-start(bf16[256,384]{1,0:T(8,128)(2,1)} %embed_ref.1) | copy-start | bytes 589828
  12.5 5.7 %copy-start = (bf16[1024,4096]{1,0:T(8,128)(2,1)S(1)}, bf16[1024,4096]{1,0:T(8,128)(2,1)}, u32[]{:S(2)}) copy-start(bf16[1024,4096]{1,0:T(8,128)(2,1)} %mixing_ref.7) | copy-start | bytes 25165828
  13.1 1.4 %collective-permute-start.2 = (bf16[18,32,128]{2,1,0:T(8,128)(2,1)S(1)}, bf16[18,32,128]{2,1,0:T(8,128)(2,1)S(1)}, u32[]{:S(2)}, u32[]{:S(2)}) collective-permute-start(bf16[18,32,128]{2,1,0:T(8,128)(2,1)S(1)} %constant_dynamic-update-slice_fusion.refs_0_), channel_id=1, source_target_pairs={{0,1},{1,0},{2,3},{3,2},{4,5},{5,4},{6,7},{7,6},{8,9},{9,8},{10,11... | collective-permute-start | bytes 442376 | tf_op jit(solution)/shard_map/ppermute | solution.py:153
  13.2 1.6 %collective-permute-start.4 = (bf16[18,32,128]{2,1,0:T(8,128)(2,1)S(1)}, bf16[18,32,128]{2,1,0:T(8,128)(2,1)S(1)}, u32[]{:S(2)}, u32[]{:S(2)}) collective-permute-start(bf16[18,32,128]{2,1,0:T(8,128)(2,1)S(1)} %collective-permute-done.3.refs_2_), channel_id=1, source_target_pairs={{0,1},{1,0},{2,3},{3,2},{4,5},{5,4},{6,7},{7,6},{8,9},{9,8},{10,11... | collective-permute-start | bytes 442376 | tf_op jit(solution)/shard_map/ppermute | solution.py:153
  19.2 9.5 %collective-permute-start.14 = (bf16[96,1024]{1,0:T(8,128)(2,1)S(1)}, bf16[96,1024]{1,0:T(8,128)(2,1)S(1)}, u32[]{:S(2)}, u32[]{:S(2)}) collective-permute-start(bf16[96,1024]{1,0:T(8,128)(2,1)S(1)} %get-tuple-element.39), channel_id=1, source_target_pairs={{0,4},{4,8},{8,12},{12,0},{1,5},{5,9},{9,13},{13,1},{2,6},{6,10},{... | collective-permute-start | bytes 589832 | tf_op jit(solution)/shard_map/ppermute | solution.py:153
  23.5 9.7 %collective-permute-start.11 = (bf16[96,1024]{1,0:T(8,128)(2,1)S(1)}, bf16[96,1024]{1,0:T(8,128)(2,1)S(1)}, u32[]{:S(2)}, u32[]{:S(2)}) collective-permute-start(bf16[96,1024]{1,0:T(8,128)(2,1)S(1)} %get-tuple-element.37), channel_id=1, source_target_pairs={{0,4},{4,8},{8,12},{12,0},{1,5},{5,9},{9,13},{13,1},{2,6},{6,10},{... | collective-permute-start | bytes 589832 | tf_op jit(solution)/shard_map/ppermute | solution.py:153
  25.1 12.3 %collective-permute-start.8 = (bf16[96,1024]{1,0:T(8,128)(2,1)S(1)}, bf16[96,1024]{1,0:T(8,128)(2,1)S(1)}, u32[]{:S(2)}, u32[]{:S(2)}) collective-permute-start(bf16[96,1024]{1,0:T(8,128)(2,1)S(1)} %get-tuple-element.35), channel_id=1, source_target_pairs={{0,4},{4,8},{8,12},{12,0},{1,5},{5,9},{9,13},{13,1},{2,6},{6,10},{... | collective-permute-start | bytes 589832 | tf_op jit(solution)/shard_map/ppermute | solution.py:153
  27.1 14.5 %collective-permute-start.5 = (bf16[96,1024]{1,0:T(8,128)(2,1)S(1)}, bf16[96,1024]{1,0:T(8,128)(2,1)S(1)}, u32[]{:S(2)}, u32[]{:S(2)}) collective-permute-start(bf16[96,1024]{1,0:T(8,128)(2,1)S(1)} %get-tuple-element.33), channel_id=1, source_target_pairs={{0,4},{4,8},{8,12},{12,0},{1,5},{5,9},{9,13},{13,1},{2,6},{6,10},{... | collective-permute-start | bytes 589832 | tf_op jit(solution)/shard_map/ppermute | solution.py:153
  28.8 17.0 %collective-permute-start.15 = (bf16[96,1024]{1,0:T(8,128)(2,1)S(1)}, bf16[96,1024]{1,0:T(8,128)(2,1)S(1)}, u32[]{:S(2)}, u32[]{:S(2)}) collective-permute-start(bf16[96,1024]{1,0:T(8,128)(2,1)S(1)} %add_convert_fusion.1), channel_id=1, source_target_pairs={{0,4},{4,8},{8,12},{12,0},{1,5},{5,9},{9,13},{13,1},{2,6},{6,10},{... | collective-permute-start | bytes 589832 | tf_op jit(solution)/shard_map/ppermute | solution.py:153
  33.2 16.8 %collective-permute-start.12 = (bf16[96,1024]{1,0:T(8,128)(2,1)S(1)}, bf16[96,1024]{1,0:T(8,128)(2,1)S(1)}, u32[]{:S(2)}, u32[]{:S(2)}) collective-permute-start(bf16[96,1024]{1,0:T(8,128)(2,1)S(1)} %add_convert_fusion.3), channel_id=1, source_target_pairs={{0,4},{4,8},{8,12},{12,0},{1,5},{5,9},{9,13},{13,1},{2,6},{6,10},{... | collective-permute-start | bytes 589832 | tf_op jit(solution)/shard_map/ppermute | solution.py:153
  37.4 16.8 %collective-permute-start.9 = (bf16[96,1024]{1,0:T(8,128)(2,1)S(1)}, bf16[96,1024]{1,0:T(8,128)(2,1)S(1)}, u32[]{:S(2)}, u32[]{:S(2)}) collective-permute-start(bf16[96,1024]{1,0:T(8,128)(2,1)S(1)} %add_convert_fusion.5), channel_id=1, source_target_pairs={{0,4},{4,8},{8,12},{12,0},{1,5},{5,9},{9,13},{13,1},{2,6},{6,10},{... | collective-permute-start | bytes 589832 | tf_op jit(solution)/shard_map/ppermute | solution.py:153
  41.6 16.8 %collective-permute-start.6 = (bf16[96,1024]{1,0:T(8,128)(2,1)S(1)}, bf16[96,1024]{1,0:T(8,128)(2,1)S(1)}, u32[]{:S(2)}, u32[]{:S(2)}) collective-permute-start(bf16[96,1024]{1,0:T(8,128)(2,1)S(1)} %add_convert_fusion.7), channel_id=1, source_target_pairs={{0,4},{4,8},{8,12},{12,0},{1,5},{5,9},{9,13},{13,1},{2,6},{6,10},{... | collective-permute-start | bytes 589832 | tf_op jit(solution)/shard_map/ppermute | solution.py:153
  45.9 16.8 %collective-permute-start.16 = (bf16[96,1024]{1,0:T(8,128)(2,1)S(1)}, bf16[96,1024]{1,0:T(8,128)(2,1)S(1)}, u32[]{:S(2)}, u32[]{:S(2)}) collective-permute-start(bf16[96,1024]{1,0:T(8,128)(2,1)S(1)} %add_convert_fusion), channel_id=1, source_target_pairs={{0,4},{4,8},{8,12},{12,0},{1,5},{5,9},{9,13},{13,1},{2,6},{6,10},{... | collective-permute-start | bytes 589832 | tf_op jit(solution)/shard_map/ppermute | solution.py:153
  50.1 16.8 %collective-permute-start.13 = (bf16[96,1024]{1,0:T(8,128)(2,1)S(1)}, bf16[96,1024]{1,0:T(8,128)(2,1)S(1)}, u32[]{:S(2)}, u32[]{:S(2)}) collective-permute-start(bf16[96,1024]{1,0:T(8,128)(2,1)S(1)} %add_convert_fusion.2), channel_id=1, source_target_pairs={{0,4},{4,8},{8,12},{12,0},{1,5},{5,9},{9,13},{13,1},{2,6},{6,10},{... | collective-permute-start | bytes 589832 | tf_op jit(solution)/shard_map/ppermute | solution.py:153
  54.3 16.8 %collective-permute-start.10 = (bf16[96,1024]{1,0:T(8,128)(2,1)S(1)}, bf16[96,1024]{1,0:T(8,128)(2,1)S(1)}, u32[]{:S(2)}, u32[]{:S(2)}) collective-permute-start(bf16[96,1024]{1,0:T(8,128)(2,1)S(1)} %add_convert_fusion.4), channel_id=1, source_target_pairs={{0,4},{4,8},{8,12},{12,0},{1,5},{5,9},{9,13},{13,1},{2,6},{6,10},{... | collective-permute-start | bytes 589832 | tf_op jit(solution)/shard_map/ppermute | solution.py:153
  58.5 16.2 %collective-permute-start.7 = (bf16[96,1024]{1,0:T(8,128)(2,1)S(1)}, bf16[96,1024]{1,0:T(8,128)(2,1)S(1)}, u32[]{:S(2)}, u32[]{:S(2)}) collective-permute-start(bf16[96,1024]{1,0:T(8,128)(2,1)S(1)} %add_convert_fusion.6), channel_id=1, source_target_pairs={{0,4},{4,8},{8,12},{12,0},{1,5},{5,9},{9,13},{13,1},{2,6},{6,10},{... | collective-permute-start | bytes 589832 | tf_op jit(solution)/shard_map/ppermute | solution.py:153

commit v7 on v6

--- a/solution.py
+++ b/solution.py
@@ -11,16 +11,28 @@
 STEP = 256
 LANES = 128
 VMEM_BYTES = 24 * 1024 * 1024
-ROWS_AT_ONCE = 768
-
-
-def pack_kernel(field_ref, low_ref, high_ref, packed_ref):
+ROWS_AT_ONCE = 1024
+
+
+def pack_kernel(field_ref, packed_ref):
     lon, lat, chans = field_ref.shape
     pairs = field_ref[...].reshape(lon // 2, 2, lat, chans)
-    joined = jnp.concatenate([pairs[:, 0], pairs[:, 1]], axis=-1).astype(packed_ref.dtype)
-    packed_ref[pl.ds(1, lon // 2)] = joined
-    low_ref[...] = joined[:1]
-    high_ref[...] = joined[-1:]
+    packed_ref[...] = jnp.concatenate([pairs[:, 0], pairs[:, 1]], axis=-1).astype(packed_ref.dtype)
+
+
+def join_kernel(count_ch, count_sub, *refs):
+    blocks, (field_ref, low_ref, high_ref) = refs[:-3], refs[-3:]
+    pairs, lat, wide = field_ref.shape
+    width = lat // (count_ch * count_sub)
+    for away_ch in range(count_ch):
+        for away_sub in range(count_sub):
+            at_ch = lax.rem(lax.axis_index("ch") + count_ch - away_ch, count_ch)
+            at_sub = lax.rem(lax.axis_index("sub") + count_sub - away_sub, count_sub)
+            here = pl.ds(pl.multiple_of((at_ch * count_sub + at_sub) * width, width), width)
+            block = blocks[away_ch * count_sub + away_sub][...]
+            field_ref[:, here, :] = block
+            low_ref[:, here, :] = block[:1]
+            high_ref[:, here, :] = block[pairs - 1 :]
 
 
 def split_two(value):
@@ -64,14 +76,13 @@
     return best
 
 
-def window(pairs_of, first, size, last):
+def window(pair_at, pairs):
     rows = []
-    for pair in range(first, first + size):
-        here = pairs_of(pair)
-        after = pairs_of(min(pair + 1, last))
-        before = pairs_of(max(pair - 1, 0))
+    for pair in pairs:
+        here = pair_at(pair)
         lane = lax.broadcasted_iota(jnp.int32, here.shape, 1)
-        rows.append(jnp.concatenate([here, jnp.where(lane < here.shape[1] // 2, after, before)], axis=-1))
+        beside = jnp.where(lane < here.shape[1] // 2, pair_at(pair + 1), pair_at(pair - 1))
+        rows.append(jnp.concatenate([here, beside], axis=-1))
     return jnp.concatenate(rows, axis=0)
 
 
@@ -92,48 +103,87 @@
     return 0.5 * value * (1.0 + lax.erf(value * (0.5**0.5)))
 
 
-def encode_kernel(count_ch, count_sub, *refs):
-    count = count_ch * count_sub
-    blocks = refs[:count]
-    taps_one_ref, taps_two_ref, embed_ref, tokens_ref, field_ref, upper_ref, lower_ref, two_ref = refs[count:]
-    pairs, lat, wide = field_ref.shape
-    width = lat // count
-    last = pairs - 1
-    for away_ch in range(count_ch):
-        for away_sub in range(count_sub):
-            at_ch = lax.rem(lax.axis_index("ch") + count_ch - away_ch, count_ch)
-            at_sub = lax.rem(lax.axis_index("sub") + count_sub - away_sub, count_sub)
-            start = pl.multiple_of((at_ch * count_sub + at_sub) * width, width)
-            field_ref[:, pl.ds(start, width), :] = blocks[away_ch * count_sub + away_sub][...]
-
-    def field_of(pair):
-        return field_ref[pair]
-
-    def dot(left, right):
-        return jnp.dot(left, right, preferred_element_type=jnp.float32)
-
-    size = pairs_at_once(pairs, lat)
-    for first in range(0, pairs, size):
-        rows = window(field_of, first, size, last)
-        products = dot(rows, taps_one_ref[0]) + dot(rows, taps_one_ref[1])
-        upper, lower = split_two(gelu(add_lat_taps(products, lat)))
-        upper_ref[pl.ds(first, size)] = upper.reshape(size, lat, wide)
-        lower_ref[pl.ds(first, size)] = lower.reshape(size, lat, wide)
-    size = pairs_at_once(pairs - 2, lat)
-    for first in range(1, pairs - 1, size):
-        rows_upper = window(lambda pair: upper_ref[pair], first, size, last)
-        rows_lower = window(lambda pair: lower_ref[pair], first, size, last)
-        products = dot(rows_upper, taps_two_ref[0]) + dot(rows_upper, taps_two_ref[1])
-        products = products + dot(rows_lower, taps_two_ref[0])
-        rounded = add_lat_taps(products, lat).astype(jnp.bfloat16).astype(jnp.float32)
-        two_ref[pl.ds((first - 1) * lat, size * lat), :] = rounded
+def dot(left, right):
+    return jnp.dot(left, right, preferred_element_type=jnp.float32)
+
+
+def first_conv(field_at, pairs, taps_ref, lat):
+    rows = window(field_at, pairs)
+    products = dot(rows, taps_ref[0]) + dot(rows, taps_ref[1])
+    parts = split_two(gelu(add_lat_taps(products, lat)))
+    return [part.reshape(len(pairs), lat, part.shape[1]) for part in parts]
+
+
+def second_conv(upper_at, lower_at, pairs, taps_ref, lat):
+    upper, lower = window(upper_at, pairs), window(lower_at, pairs)
+    products = dot(upper, taps_ref[0]) + dot(upper, taps_ref[1]) + dot(lower, taps_ref[0])
+    return add_lat_taps(products, lat).astype(jnp.bfloat16).astype(jnp.float32)
+
+
+def embed_patches(two_ref, embed_ref):
     half = two_ref.shape[0] // 2
     patches = jnp.concatenate(
         [two_ref[pl.ds(b, half, stride=2), :].astype(jnp.bfloat16) for b in range(2)], axis=-1
     )
-    tokens_ref[...] = lax.dot_general(
+    return lax.dot_general(
         embed_ref[...], patches, (((1,), (1,)), ((), ())), preferred_element_type=jnp.float32
-    ).astype(tokens_ref.dtype)
+    ).astype(jnp.bfloat16)
+
+
+def runs(first, last, lat):
+    size = pairs_at_once(last - first, lat)
+    return [list(range(at, at + size)) for at in range(first, last, size)]
+
+
+def inner_kernel(
+    field_ref, taps_one_ref, taps_two_ref, embed_ref, tokens_ref, upper_edge_ref, lower_edge_ref, upper_ref, lower_ref, two_ref
+):
+    pairs, lat, wide = field_ref.shape
+    for run in runs(1, pairs - 1, lat):
+        upper, lower = first_conv(lambda pair: field_ref[pair], run, taps_one_ref, lat)
+        upper_ref[pl.ds(run[0], len(run))] = upper
+        lower_ref[pl.ds(run[0], len(run))] = lower
+    for inside, edge in ((upper_ref, upper_edge_ref), (lower_ref, lower_edge_ref)):
+        edge[pl.ds(0, 2)] = inside[pl.ds(1, 2)]
+        edge[pl.ds(2, 2)] = inside[pl.ds(pairs - 3, 2)]
+    for run in runs(2, pairs - 2, lat):
+        two = second_conv(lambda pair: upper_ref[pair], lambda pair: lower_ref[pair], run, taps_two_ref, lat)
+        two_ref[pl.ds((run[0] - 2) * lat, len(run) * lat), :] = two
+    tokens_ref[...] = embed_patches(two_ref, embed_ref)
+
+
+def outer_kernel(
+    field_ref, before_ref, after_ref, upper_edge_ref, lower_edge_ref, taps_one_ref, taps_two_ref, embed_ref, inner_ref, tokens_ref, two_ref
+):
+    pairs, lat, wide = field_ref.shape
+
+    def field_at(pair):
+        if pair < 0:
+            return before_ref[0]
+        if pair >= pairs:
+            return after_ref[0]
+        return field_ref[pair]
+
+    outermost = [-1, 0, pairs - 1, pairs]
+    next_inside = [1, 2, pairs - 3, pairs - 2]
+    upper, lower = first_conv(field_at, outermost, taps_one_ref, lat)
+
+    def hidden_at(found, edge_ref):
+        def at(pair):
+            if pair in outermost:
+                return found[outermost.index(pair)]
+            return edge_ref[next_inside.index(pair)]
+
+        return at
+
+    two_ref[...] = second_conv(
+        hidden_at(upper, upper_edge_ref), hidden_at(lower, lower_edge_ref), [0, 1, pairs - 2, pairs - 1], taps_two_ref, lat
+    )
+    outer = embed_patches(two_ref, embed_ref)
+    inner = inner_ref.shape[1]
+    tokens_ref[:, :lat] = outer[:, :lat]
+    tokens_ref[:, pl.ds(lat, inner)] = inner_ref[...]
+    tokens_ref[:, pl.ds(lat + inner, lat)] = outer[:, lat:]
 
 
 def call(kernel, out_shape, inputs, scratch=(), flops=0, moved=0):
@@ -168,14 +218,9 @@
     pairs, wide = lon // 2, 2 * chans
     embed = patch_embed.shape[1]
     shape = functools.partial(jax.ShapeDtypeStruct, dtype=jnp.bfloat16)
-    low, high, packed = call(
-        pack_kernel,
-        (shape((1, lat, wide)), shape((1, lat, wide)), shape((pairs + 2, lat, wide))),
-        (jnp.transpose(weather, (1, 2, 0)),),
-        moved=weather.size * 10,
-    )
-    before = turned(high, "tok", 1)
-    after = turned(low, "tok", -1)
+    packed = call(
+        pack_kernel, shape((pairs, lat, wide)), (jnp.transpose(weather, (1, 2, 0)),), moved=weather.size * 10
+    )
     taps = shape((2, 4 * chans, 6 * chans))
     weights = call(
         weights_kernel,
@@ -184,18 +229,35 @@
         scratch=[pltpu.VMEM((patch_embed.shape[0], LANES), jnp.float32)],
         moved=conv_first.size * 20,
     )
-    packed = lax.dynamic_update_slice_in_dim(packed, before, 0, 0)
-    packed = lax.dynamic_update_slice_in_dim(packed, after, pairs + 1, 0)
     blocks, weights = band_blocks(packed, weights)
-    full_lat = len(blocks) * lat
-    held = pltpu.VMEM((pairs + 2, full_lat, wide), jnp.bfloat16)
+    lat = len(blocks) * lat
+    edge = shape((1, lat, wide))
+    field, low, high = call(
+        functools.partial(join_kernel, lax.axis_size("ch"), lax.axis_size("sub")),
+        (shape((pairs, lat, wide)), edge, edge),
+        blocks,
+        moved=packed.size * 4 * len(blocks),
+    )
+    before = turned(high, "tok", 1)
+    after = turned(low, "tok", -1)
+    work = 2 * lat * 4 * chans * 6 * chans * 5
+    held = shape((4, lat, wide))
+    hidden = pltpu.VMEM((pairs, lat, wide), jnp.bfloat16)
+    inner, upper_edge, lower_edge = call(
+        inner_kernel,
+        (shape((embed, (pairs - 4) * lat // 2)), held, held),
+        (field, *weights),
+        scratch=[hidden, hidden, pltpu.VMEM(((pairs - 4) * lat, wide), jnp.float32)],
+        flops=work * (pairs - 3),
+        moved=field.size * 2,
+    )
     return call(
-        functools.partial(encode_kernel, lax.axis_size("ch"), lax.axis_size("sub")),
-        shape((embed, pairs * full_lat // 2)),
-        (*blocks, *weights),
-        scratch=[held, held, held, pltpu.VMEM((pairs * full_lat, wide), jnp.float32)],
-        flops=2 * (pairs + 1) * full_lat * 4 * chans * 6 * chans * 5,
-        moved=packed.size * 2 * len(blocks),
+        outer_kernel,
+        shape((embed, pairs * lat // 2)),
+        (field, before, after, upper_edge, lower_edge, *weights, inner),
+        scratch=[pltpu.VMEM((4 * lat, wide), jnp.float32)],
+        flops=work * 4,
+        moved=field.size * 2,
     )
 
 

time: 76 us -> 74.4 us (0.979)
  waiting for transfers between devices: 49 us -> 46.7 us
    ppermute x17, waiting for transfers between devices: 49 us -> 46.7 us  [turned(): lax.ppermute(value, axis, [(i, (i + away) % count) for i in range(count)])]
    pallas_call x7 -> x9, Pallas kernels: 8.01 us -> 8.66 us  [call(): pl.pallas_call(kernel, out_shape=out_shape, in_specs=[pl.BlockSpec(memory...]
  transfers between devices with their start and end apart: 17 -> 17, of which waited for: 15 -> 13; matrix products, arithmetic and copies ran while one was open for 1% -> 1% of each run, Pallas kernels for 5% -> 8%
where the time goes in v7:
time: 74.4 us; the launch traced here: 74.1 us
  waiting for transfers between devices  46.7 us (63%)
  starting transfers between devices  13 us (17%)
  Pallas kernels  8.66 us (12%)
  local copies, waits for them, and re-layouts  3.89 us (5%)
  other arithmetic  1.65 us (2%)
    ppermute x17, waiting for transfers between devices, turned(): lax.ppermute(value, axis, [(i, (i + away) % count) for i in range(count)])  46.7 us
    ppermute x17, starting transfers between devices, turned(): lax.ppermute(value, axis, [(i, (i + away) % count) for i in range(count)])  13 us
    pallas_call x9, Pallas kernels, call(): pl.pallas_call(kernel, out_shape=out_shape, in_specs=[pl.BlockSpec(memory...  8.66 us
    unnamed x10, local copies, waits for them, and re-layouts  3.89 us
  transfers between devices with their start and end apart: 17, of which 13 were waited for; matrix products, arithmetic and copies ran while one was open for 1% of the time, Pallas kernels for 8%

profile of v7, /device:TPU:0, one launch (start us, length us, event | category | flops | bytes accessed | tf_op | source)
XLA Modules:
  0.0 74.1 jit_solution(5066983244882261049)
XLA Ops:
  0.0 1.0 %copy-done.1 = f32[64,32,32]{0,2,1:T(8,128)S(1)} copy-done((f32[64,32,32]{0,2,1:T(8,128)S(1)}, f32[64,32,32]{0,2,1:T(8,128)}, u32[]{:S(2)}) %copy-start.1) | copy-done | bytes 262168
  1.0 0.1 shard_map.55.refs_0_
  1.2 3.0 %collective-permute-start.1 = (bf16[16,32,128]{2,1,0:T(8,128)(2,1)S(1)}, bf16[16,32,128]{2,1,0:T(8,128)(2,1)S(1)}, u32[]{:S(2)}, u32[]{:S(2)}) collective-permute-start(bf16[16,32,128]{2,1,0:T(8,128)(2,1)S(1)} %shard_map.55.refs_0_), channel_id=1, source_target_pairs={{0,2},{2,0},{1,3},{3,1},{4,6},{6,4},{5,7},{7,5},{8,10},{10,8},{9,1... | collective-permute-start | bytes 393224 | tf_op jit(solution)/shard_map/ppermute | solution.py:203
  4.2 1.0 %copy-done.2 = f32[9,64,64]{2,1,0:T(8,128)S(1)} copy-done((f32[9,64,64]{2,1,0:T(8,128)S(1)}, f32[9,64,64]{2,1,0:T(8,128)}, u32[]{:S(2)}) %copy-start.2) | copy-done | bytes 147480
  5.1 1.0 %copy-done.3 = f32[9,64,64]{2,1,0:T(8,128)S(1)} copy-done((f32[9,64,64]{2,1,0:T(8,128)S(1)}, f32[9,64,64]{2,1,0:T(8,128)}, u32[]{:S(2)}) %copy-start.3) | copy-done | bytes 147480
  6.1 0.9 %copy-done.4 = bf16[256,384]{1,0:T(8,128)(2,1)S(1)} copy-done((bf16[256,384]{1,0:T(8,128)(2,1)S(1)}, bf16[256,384]{1,0:T(8,128)(2,1)}, u32[]{:S(2)}) %copy-start.4) | copy-done | bytes 196632
  7.0 0.6 shard_map.56
  7.6 0.0 collective-permute-done.1.refs_2_
  7.7 0.5 collective-permute-start.2
  8.2 1.0 %collective-permute-done.2.refs_3_ = bf16[16,32,128]{2,1,0:T(8,128)(2,1)S(1)} collective-permute-done((bf16[16,32,128]{2,1,0:T(8,128)(2,1)S(1)}, bf16[16,32,128]{2,1,0:T(8,128)(2,1)S(1)}, u32[]{:S(2)}, u32[]{:S(2)}) %collective-permute-start.2) | collective-permute-done | bytes 131104 | tf_op jit(solution)/shard_map/ppermute | solution.py:203
  9.2 0.1 shard_map.57
  9.2 1.7 %collective-permute-start.3 = (bf16[1,128,128]{2,1,0:T(8,128)(2,1)S(1)}, bf16[1,128,128]{2,1,0:T(8,128)(2,1)S(1)}, u32[]{:S(2)}, u32[]{:S(2)}) collective-permute-start(bf16[1,128,128]{2,1,0:T(8,128)(2,1)S(1)} %get-tuple-element.31), channel_id=1, source_target_pairs={{0,4},{4,8},{8,12},{12,0},{1,5},{5,9},{9,13},{13,1},{2,6},{6,10},{... | collective-permute-start | bytes 98312 | tf_op jit(solution)/shard_map/ppermute | solution.py:203
  10.9 2.2 %collective-permute-start.4 = (bf16[1,128,128]{2,1,0:T(8,128)(2,1)S(1)}, bf16[1,128,128]{2,1,0:T(8,128)(2,1)S(1)}, u32[]{:S(2)}, u32[]{:S(2)}) collective-permute-start(bf16[1,128,128]{2,1,0:T(8,128)(2,1)S(1)} %get-tuple-element.32), channel_id=1, source_target_pairs={{0,12},{4,0},{8,4},{12,8},{1,13},{5,1},{9,5},{13,9},{2,14},{6,2},{... | collective-permute-start | bytes 98312 | tf_op jit(solution)/shard_map/ppermute | solution.py:203
  13.1 2.7 %shard_map.58 = (bf16[384,768]{1,0:T(8,128)(2,1)S(1)}, bf16[4,128,128]{2,1,0:T(8,128)(2,1)S(1)}, bf16[4,128,128]{2,1,0:T(8,128)(2,1)S(1)}) custom-call(bf16[16,128,128]{2,1,0:T(8,128)(2,1)S(1)} %get-tuple-element.30.field_ref, bf16[2,256,384]{2,1,0:T(8,128)(2,1)S(1)} %get-tuple-element.33.taps_one_ref, ...), custom_call_target="tpu_custom_call" | custom-call | flops 1635778560 | bytes 524288 | tf_op jit(solution)/shard_map/pallas_call | solution.py:190
  15.9 1.3 %shard_map.59.tokens_ref = bf16[384,1024]{1,0:T(8,128)(2,1)S(1)} custom-call(bf16[16,128,128]{2,1,0:T(8,128)(2,1)S(1)} %get-tuple-element.30.field_ref, bf16[1,128,128]{2,1,0:T(8,128)(2,1)S(1)} %collective-permute-done.3.before_ref, bf16[1,128,128]{2,1,0:T(8,128)(2,1)S(1)} %collective-permute-done.4.after_ref, ...), custom_call_target="tpu_custom_call" | custom-call | flops 503316480 | bytes 524288 | tf_op jit(solution)/shard_map/pallas_call | solution.py:190
  17.2 1.0 %shard_map.63 = (bf16[96,1024]{1,0:T(8,128)(2,1)S(1)}, f32[288,1024]{1,0:T(8,128)S(1)}) custom-call(bf16[384,1024]{1,0:T(8,128)(2,1)S(1)} %shard_map.59.tokens_ref, bf16[1024,4096]{1,0:T(8,128)(2,1)S(1)} %copy-done), custom_call_target="tpu_custom_call" | custom-call | tf_op jit(solution)/shard_map/pallas_call | solution.py:190
  18.2 0.6 collective-permute-start.14
  18.8 1.0 %shard_map.62 = (bf16[96,1024]{1,0:T(8,128)(2,1)S(1)}, f32[288,1024]{1,0:T(8,128)S(1)}) custom-call(bf16[384,1024]{1,0:T(8,128)(2,1)S(1)} %shard_map.59.tokens_ref, bf16[1024,4096]{1,0:T(8,128)(2,1)S(1)} %copy-done), custom_call_target="tpu_custom_call" | custom-call | tf_op jit(solution)/shard_map/pallas_call | solution.py:190
  19.7 1.0 %shard_map.61 = (bf16[96,1024]{1,0:T(8,128)(2,1)S(1)}, f32[288,1024]{1,0:T(8,128)S(1)}) custom-call(bf16[384,1024]{1,0:T(8,128)(2,1)S(1)} %shard_map.59.tokens_ref, bf16[1024,4096]{1,0:T(8,128)(2,1)S(1)} %copy-done), custom_call_target="tpu_custom_call" | custom-call | tf_op jit(solution)/shard_map/pallas_call | solution.py:190
  20.7 1.0 %shard_map.60 = (bf16[96,1024]{1,0:T(8,128)(2,1)S(1)}, f32[288,1024]{1,0:T(8,128)S(1)}) custom-call(bf16[384,1024]{1,0:T(8,128)(2,1)S(1)} %shard_map.59.tokens_ref, bf16[1024,4096]{1,0:T(8,128)(2,1)S(1)} %copy-done), custom_call_target="tpu_custom_call" | custom-call | tf_op jit(solution)/shard_map/pallas_call | solution.py:190
  21.7 1.6 %collective-permute-start.11 = (bf16[96,1024]{1,0:T(8,128)(2,1)S(1)}, bf16[96,1024]{1,0:T(8,128)(2,1)S(1)}, u32[]{:S(2)}, u32[]{:S(2)}) collective-permute-start(bf16[96,1024]{1,0:T(8,128)(2,1)S(1)} %get-tuple-element.43), channel_id=1, source_target_pairs={{0,4},{4,8},{8,12},{12,0},{1,5},{5,9},{9,13},{13,1},{2,6},{6,10},{... | collective-permute-start | bytes 589832 | tf_op jit(solution)/shard_map/ppermute | solution.py:203
  23.3 2.0 %collective-permute-start.8 = (bf16[96,1024]{1,0:T(8,128)(2,1)S(1)}, bf16[96,1024]{1,0:T(8,128)(2,1)S(1)}, u32[]{:S(2)}, u32[]{:S(2)}) collective-permute-start(bf16[96,1024]{1,0:T(8,128)(2,1)S(1)} %get-tuple-element.41), channel_id=1, source_target_pairs={{0,4},{4,8},{8,12},{12,0},{1,5},{5,9},{9,13},{13,1},{2,6},{6,10},{... | collective-permute-start | bytes 589832 | tf_op jit(solution)/shard_map/ppermute | solution.py:203
  25.3 0.9 %collective-permute-start.5 = (bf16[96,1024]{1,0:T(8,128)(2,1)S(1)}, bf16[96,1024]{1,0:T(8,128)(2,1)S(1)}, u32[]{:S(2)}, u32[]{:S(2)}) collective-permute-start(bf16[96,1024]{1,0:T(8,128)(2,1)S(1)} %get-tuple-element.39), channel_id=1, source_target_pairs={{0,4},{4,8},{8,12},{12,0},{1,5},{5,9},{9,13},{13,1},{2,6},{6,10},{... | collective-permute-start | bytes 589832 | tf_op jit(solution)/shard_map/ppermute | solution.py:203
  26.2 1.6 %collective-permute-done.14 = bf16[96,1024]{1,0:T(8,128)(2,1)S(1)} collective-permute-done((bf16[96,1024]{1,0:T(8,128)(2,1)S(1)}, bf16[96,1024]{1,0:T(8,128)(2,1)S(1)}, u32[]{:S(2)}, u32[]{:S(2)}) %collective-permute-start.14) | collective-permute-done | bytes 196640 | tf_op jit(solution)/shard_map/ppermute | solution.py:203
  27.8 0.1 collective-permute-start.15
  27.9 4.1 %collective-permute-done.11 = bf16[96,1024]{1,0:T(8,128)(2,1)S(1)} collective-permute-done((bf16[96,1024]{1,0:T(8,128)(2,1)S(1)}, bf16[96,1024]{1,0:T(8,128)(2,1)S(1)}, u32[]{:S(2)}, u32[]{:S(2)}) %collective-permute-start.11) | collective-permute-done | bytes 196640 | tf_op jit(solution)/shard_map/ppermute | solution.py:203
  32.1 0.1 collective-permute-start.12
  32.1 4.1 %collective-permute-done.8 = bf16[96,1024]{1,0:T(8,128)(2,1)S(1)} collective-permute-done((bf16[96,1024]{1,0:T(8,128)(2,1)S(1)}, bf16[96,1024]{1,0:T(8,128)(2,1)S(1)}, u32[]{:S(2)}, u32[]{:S(2)}) %collective-permute-start.8) | collective-permute-done | bytes 196640 | tf_op jit(solution)/shard_map/ppermute | solution.py:203
  36.3 0.1 collective-permute-start.9
  36.3 4.1 %collective-permute-done.5 = bf16[96,1024]{1,0:T(8,128)(2,1)S(1)} collective-permute-done((bf16[96,1024]{1,0:T(8,128)(2,1)S(1)}, bf16[96,1024]{1,0:T(8,128)(2,1)S(1)}, u32[]{:S(2)}, u32[]{:S(2)}) %collective-permute-start.5) | collective-permute-done | bytes 196640 | tf_op jit(solution)/shard_map/ppermute | solution.py:203
  40.5 0.1 collective-permute-start.6
  40.6 4.1 %collective-permute-done.15 = bf16[96,1024]{1,0:T(8,128)(2,1)S(1)} collective-permute-done((bf16[96,1024]{1,0:T(8,128)(2,1)S(1)}, bf16[96,1024]{1,0:T(8,128)(2,1)S(1)}, u32[]{:S(2)}, u32[]{:S(2)}) %collective-permute-start.15) | collective-permute-done | bytes 196640 | tf_op jit(solution)/shard_map/ppermute | solution.py:203
  44.7 0.1 collective-permute-start.16
  44.8 4.1 %collective-permute-done.12 = bf16[96,1024]{1,0:T(8,128)(2,1)S(1)} collective-permute-done((bf16[96,1024]{1,0:T(8,128)(2,1)S(1)}, bf16[96,1024]{1,0:T(8,128)(2,1)S(1)}, u32[]{:S(2)}, u32[]{:S(2)}) %collective-permute-start.12) | collective-permute-done | bytes 196640 | tf_op jit(solution)/shard_map/ppermute | solution.py:203
  48.9 0.1 collective-permute-start.13
  49.0 4.1 %collective-permute-done.9 = bf16[96,1024]{1,0:T(8,128)(2,1)S(1)} collective-permute-done((bf16[96,1024]{1,0:T(8,128)(2,1)S(1)}, bf16[96,1024]{1,0:T(8,128)(2,1)S(1)}, u32[]{:S(2)}, u32[]{:S(2)}) %collective-permute-start.9) | collective-permute-done | bytes 196640 | tf_op jit(solution)/shard_map/ppermute | solution.py:203
  53.1 0.1 collective-permute-start.10
  53.2 4.1 %collective-permute-done.6 = bf16[96,1024]{1,0:T(8,128)(2,1)S(1)} collective-permute-done((bf16[96,1024]{1,0:T(8,128)(2,1)S(1)}, bf16[96,1024]{1,0:T(8,128)(2,1)S(1)}, u32[]{:S(2)}, u32[]{:S(2)}) %collective-permute-start.6) | collective-permute-done | bytes 196640 | tf_op jit(solution)/shard_map/ppermute | solution.py:203
  57.3 0.1 collective-permute-start.7
  57.4 4.1 %collective-permute-done.16 = bf16[96,1024]{1,0:T(8,128)(2,1)S(1)} collective-permute-done((bf16[96,1024]{1,0:T(8,128)(2,1)S(1)}, bf16[96,1024]{1,0:T(8,128)(2,1)S(1)}, u32[]{:S(2)}, u32[]{:S(2)}) %collective-permute-start.16) | collective-permute-done | bytes 196640 | tf_op jit(solution)/shard_map/ppermute | solution.py:203
  61.5 0.1 multiply_convert_fusion
  61.6 4.1 %collective-permute-done.13 = bf16[96,1024]{1,0:T(8,128)(2,1)S(1)} collective-permute-done((bf16[96,1024]{1,0:T(8,128)(2,1)S(1)}, bf16[96,1024]{1,0:T(8,128)(2,1)S(1)}, u32[]{:S(2)}, u32[]{:S(2)}) %collective-permute-start.13) | collective-permute-done | bytes 196640 | tf_op jit(solution)/shard_map/ppermute | solution.py:203
  65.7 0.1 multiply_convert_fusion.1
  65.8 4.1 %collective-permute-done.10 = bf16[96,1024]{1,0:T(8,128)(2,1)S(1)} collective-permute-done((bf16[96,1024]{1,0:T(8,128)(2,1)S(1)}, bf16[96,1024]{1,0:T(8,128)(2,1)S(1)}, u32[]{:S(2)}, u32[]{:S(2)}) %collective-permute-start.10) | collective-permute-done | bytes 196640 | tf_op jit(solution)/shard_map/ppermute | solution.py:203
  69.9 0.1 multiply_convert_fusion.2
  70.0 3.0 %collective-permute-done.7 = bf16[96,1024]{1,0:T(8,128)(2,1)S(1)} collective-permute-done((bf16[96,1024]{1,0:T(8,128)(2,1)S(1)}, bf16[96,1024]{1,0:T(8,128)(2,1)S(1)}, u32[]{:S(2)}, u32[]{:S(2)}) %collective-permute-start.7) | collective-permute-done | bytes 196640 | tf_op jit(solution)/shard_map/ppermute | solution.py:203
  73.1 0.1 multiply_convert_fusion.3
  73.2 0.9 %pad_maximum_fusion = bf16[96,4096]{1,0:T(8,128)(2,1)} fusion(bf16[96,1024]{1,0:T(8,128)(2,1)S(1)} %multiply_convert_fusion, bf16[96,1024]{1,0:T(8,128)(2,1)S(1)} %multiply_convert_fusion.1, bf16[96,1024]{1,0:T(8,128)(2,1)S(1)} %multiply_convert_fusion.2, bf16[96,1024]{1,0:T(8,128)(2,1)S(1)} %multiply_convert_fusion.3), kind=kLoop, calls=%fused_computation | loop fusion | flops 3145728 | bytes 1572864 | tf_op jit(solution)/shard_map/concatenate | solution.py:302
  (18 shorter events, 0.3 us)
Async XLA Ops:
  0.0 1.0 %copy-start.1 = (f32[64,32,32]{0,2,1:T(8,128)S(1)}, f32[64,32,32]{0,2,1:T(8,128)}, u32[]{:S(2)}) copy-start(f32[64,32,32]{0,2,1:T(8,128)} %param.5) | copy-start | bytes 786436
  1.2 6.5 %collective-permute-start.1 = (bf16[16,32,128]{2,1,0:T(8,128)(2,1)S(1)}, bf16[16,32,128]{2,1,0:T(8,128)(2,1)S(1)}, u32[]{:S(2)}, u32[]{:S(2)}) collective-permute-start(bf16[16,32,128]{2,1,0:T(8,128)(2,1)S(1)} %shard_map.55.refs_0_), channel_id=1, source_target_pairs={{0,2},{2,0},{1,3},{3,1},{4,6},{6,4},{5,7},{7,5},{8,10},{10,8},{9,1... | collective-permute-start | bytes 393224 | tf_op jit(solution)/shard_map/ppermute | solution.py:203
  4.2 4.0 %collective-permute-start = (bf16[16,32,128]{2,1,0:T(8,128)(2,1)S(1)}, bf16[16,32,128]{2,1,0:T(8,128)(2,1)S(1)}, u32[]{:S(2)}, u32[]{:S(2)}) collective-permute-start(bf16[16,32,128]{2,1,0:T(8,128)(2,1)S(1)} %shard_map.55.refs_0_), channel_id=1, source_target_pairs={{0,1},{1,0},{2,3},{3,2},{4,5},{5,4},{6,7},{7,6},{8,9},{9,8},{10,11... | collective-permute-start | bytes 393224 | tf_op jit(solution)/shard_map/ppermute | solution.py:203
  4.2 1.0 %copy-start.2 = (f32[9,64,64]{2,1,0:T(8,128)S(1)}, f32[9,64,64]{2,1,0:T(8,128)}, u32[]{:S(2)}) copy-start(f32[9,64,64]{2,1,0:T(8,128)} %first_ref.1) | copy-start | bytes 442372
  5.1 1.0 %copy-start.3 = (f32[9,64,64]{2,1,0:T(8,128)S(1)}, f32[9,64,64]{2,1,0:T(8,128)}, u32[]{:S(2)}) copy-start(f32[9,64,64]{2,1,0:T(8,128)} %second_ref.1) | copy-start | bytes 442372
  6.1 0.9 %copy-start.4 = (bf16[256,384]{1,0:T(8,128)(2,1)S(1)}, bf16[256,384]{1,0:T(8,128)(2,1)}, u32[]{:S(2)}) copy-start(bf16[256,384]{1,0:T(8,128)(2,1)} %embed_ref.1) | copy-start | bytes 589828
  7.7 1.5 %collective-permute-start.2 = (bf16[16,32,128]{2,1,0:T(8,128)(2,1)S(1)}, bf16[16,32,128]{2,1,0:T(8,128)(2,1)S(1)}, u32[]{:S(2)}, u32[]{:S(2)}) collective-permute-start(bf16[16,32,128]{2,1,0:T(8,128)(2,1)S(1)} %collective-permute-done.1.refs_2_), channel_id=1, source_target_pairs={{0,1},{1,0},{2,3},{3,2},{4,5},{5,4},{6,7},{7,6},{8,9},{9,8},{10,11... | collective-permute-start | bytes 393224 | tf_op jit(solution)/shard_map/ppermute | solution.py:203
  9.2 6.6 %collective-permute-start.3 = (bf16[1,128,128]{2,1,0:T(8,128)(2,1)S(1)}, bf16[1,128,128]{2,1,0:T(8,128)(2,1)S(1)}, u32[]{:S(2)}, u32[]{:S(2)}) collective-permute-start(bf16[1,128,128]{2,1,0:T(8,128)(2,1)S(1)} %get-tuple-element.31), channel_id=1, source_target_pairs={{0,4},{4,8},{8,12},{12,0},{1,5},{5,9},{9,13},{13,1},{2,6},{6,10},{... | collective-permute-start | bytes 98312 | tf_op jit(solution)/shard_map/ppermute | solution.py:203
  10.9 5.0 %collective-permute-start.4 = (bf16[1,128,128]{2,1,0:T(8,128)(2,1)S(1)}, bf16[1,128,128]{2,1,0:T(8,128)(2,1)S(1)}, u32[]{:S(2)}, u32[]{:S(2)}) collective-permute-start(bf16[1,128,128]{2,1,0:T(8,128)(2,1)S(1)} %get-tuple-element.32), channel_id=1, source_target_pairs={{0,12},{4,0},{8,4},{12,8},{1,13},{5,1},{9,5},{13,9},{2,14},{6,2},{... | collective-permute-start | bytes 98312 | tf_op jit(solution)/shard_map/ppermute | solution.py:203
  13.1 4.0 %copy-start = (bf16[1024,4096]{1,0:T(8,128)(2,1)S(1)}, bf16[1024,4096]{1,0:T(8,128)(2,1)}, u32[]{:S(2)}) copy-start(bf16[1024,4096]{1,0:T(8,128)(2,1)} %mixing_ref.7) | copy-start | bytes 25165828
  18.2 9.6 %collective-permute-start.14 = (bf16[96,1024]{1,0:T(8,128)(2,1)S(1)}, bf16[96,1024]{1,0:T(8,128)(2,1)S(1)}, u32[]{:S(2)}, u32[]{:S(2)}) collective-permute-start(bf16[96,1024]{1,0:T(8,128)(2,1)S(1)} %get-tuple-element.45), channel_id=1, source_target_pairs={{0,4},{4,8},{8,12},{12,0},{1,5},{5,9},{9,13},{13,1},{2,6},{6,10},{... | collective-permute-start | bytes 589832 | tf_op jit(solution)/shard_map/ppermute | solution.py:203
  21.7 10.3 %collective-permute-start.11 = (bf16[96,1024]{1,0:T(8,128)(2,1)S(1)}, bf16[96,1024]{1,0:T(8,128)(2,1)S(1)}, u32[]{:S(2)}, u32[]{:S(2)}) collective-permute-start(bf16[96,1024]{1,0:T(8,128)(2,1)S(1)} %get-tuple-element.43), channel_id=1, source_target_pairs={{0,4},{4,8},{8,12},{12,0},{1,5},{5,9},{9,13},{13,1},{2,6},{6,10},{... | collective-permute-start | bytes 589832 | tf_op jit(solution)/shard_map/ppermute | solution.py:203
  23.3 12.9 %collective-permute-start.8 = (bf16[96,1024]{1,0:T(8,128)(2,1)S(1)}, bf16[96,1024]{1,0:T(8,128)(2,1)S(1)}, u32[]{:S(2)}, u32[]{:S(2)}) collective-permute-start(bf16[96,1024]{1,0:T(8,128)(2,1)S(1)} %get-tuple-element.41), channel_id=1, source_target_pairs={{0,4},{4,8},{8,12},{12,0},{1,5},{5,9},{9,13},{13,1},{2,6},{6,10},{... | collective-permute-start | bytes 589832 | tf_op jit(solution)/shard_map/ppermute | solution.py:203
  25.3 15.2 %collective-permute-start.5 = (bf16[96,1024]{1,0:T(8,128)(2,1)S(1)}, bf16[96,1024]{1,0:T(8,128)(2,1)S(1)}, u32[]{:S(2)}, u32[]{:S(2)}) collective-permute-start(bf16[96,1024]{1,0:T(8,128)(2,1)S(1)} %get-tuple-element.39), channel_id=1, source_target_pairs={{0,4},{4,8},{8,12},{12,0},{1,5},{5,9},{9,13},{13,1},{2,6},{6,10},{... | collective-permute-start | bytes 589832 | tf_op jit(solution)/shard_map/ppermute | solution.py:203
  27.8 16.8 %collective-permute-start.15 = (bf16[96,1024]{1,0:T(8,128)(2,1)S(1)}, bf16[96,1024]{1,0:T(8,128)(2,1)S(1)}, u32[]{:S(2)}, u32[]{:S(2)}) collective-permute-start(bf16[96,1024]{1,0:T(8,128)(2,1)S(1)} %add_convert_fusion.1), channel_id=1, source_target_pairs={{0,4},{4,8},{8,12},{12,0},{1,5},{5,9},{9,13},{13,1},{2,6},{6,10},{... | collective-permute-start | bytes 589832 | tf_op jit(solution)/shard_map/ppermute | solution.py:203
  32.1 16.8 %collective-permute-start.12 = (bf16[96,1024]{1,0:T(8,128)(2,1)S(1)}, bf16[96,1024]{1,0:T(8,128)(2,1)S(1)}, u32[]{:S(2)}, u32[]{:S(2)}) collective-permute-start(bf16[96,1024]{1,0:T(8,128)(2,1)S(1)} %add_convert_fusion.3), channel_id=1, source_target_pairs={{0,4},{4,8},{8,12},{12,0},{1,5},{5,9},{9,13},{13,1},{2,6},{6,10},{... | collective-permute-start | bytes 589832 | tf_op jit(solution)/shard_map/ppermute | solution.py:203
  36.3 16.8 %collective-permute-start.9 = (bf16[96,1024]{1,0:T(8,128)(2,1)S(1)}, bf16[96,1024]{1,0:T(8,128)(2,1)S(1)}, u32[]{:S(2)}, u32[]{:S(2)}) collective-permute-start(bf16[96,1024]{1,0:T(8,128)(2,1)S(1)} %add_convert_fusion.5), channel_id=1, source_target_pairs={{0,4},{4,8},{8,12},{12,0},{1,5},{5,9},{9,13},{13,1},{2,6},{6,10},{... | collective-permute-start | bytes 589832 | tf_op jit(solution)/shard_map/ppermute | solution.py:203
  40.5 16.8 %collective-permute-start.6 = (bf16[96,1024]{1,0:T(8,128)(2,1)S(1)}, bf16[96,1024]{1,0:T(8,128)(2,1)S(1)}, u32[]{:S(2)}, u32[]{:S(2)}) collective-permute-start(bf16[96,1024]{1,0:T(8,128)(2,1)S(1)} %add_convert_fusion.7), channel_id=1, source_target_pairs={{0,4},{4,8},{8,12},{12,0},{1,5},{5,9},{9,13},{13,1},{2,6},{6,10},{... | collective-permute-start | bytes 589832 | tf_op jit(solution)/shard_map/ppermute | solution.py:203
  44.7 16.8 %collective-permute-start.16 = (bf16[96,1024]{1,0:T(8,128)(2,1)S(1)}, bf16[96,1024]{1,0:T(8,128)(2,1)S(1)}, u32[]{:S(2)}, u32[]{:S(2)}) collective-permute-start(bf16[96,1024]{1,0:T(8,128)(2,1)S(1)} %add_convert_fusion), channel_id=1, source_target_pairs={{0,4},{4,8},{8,12},{12,0},{1,5},{5,9},{9,13},{13,1},{2,6},{6,10},{... | collective-permute-start | bytes 589832 | tf_op jit(solution)/shard_map/ppermute | solution.py:203
  48.9 16.8 %collective-permute-start.13 = (bf16[96,1024]{1,0:T(8,128)(2,1)S(1)}, bf16[96,1024]{1,0:T(8,128)(2,1)S(1)}, u32[]{:S(2)}, u32[]{:S(2)}) collective-permute-start(bf16[96,1024]{1,0:T(8,128)(2,1)S(1)} %add_convert_fusion.2), channel_id=1, source_target_pairs={{0,4},{4,8},{8,12},{12,0},{1,5},{5,9},{9,13},{13,1},{2,6},{6,10},{... | collective-permute-start | bytes 589832 | tf_op jit(solution)/shard_map/ppermute | solution.py:203
  53.1 16.8 %collective-permute-start.10 = (bf16[96,1024]{1,0:T(8,128)(2,1)S(1)}, bf16[96,1024]{1,0:T(8,128)(2,1)S(1)}, u32[]{:S(2)}, u32[]{:S(2)}) collective-permute-start(bf16[96,1024]{1,0:T(8,128)(2,1)S(1)} %add_convert_fusion.4), channel_id=1, source_target_pairs={{0,4},{4,8},{8,12},{12,0},{1,5},{5,9},{9,13},{13,1},{2,6},{6,10},{... | collective-permute-start | bytes 589832 | tf_op jit(solution)/shard_map/ppermute | solution.py:203
  57.3 15.7 %collective-permute-start.7 = (bf16[96,1024]{1,0:T(8,128)(2,1)S(1)}, bf16[96,1024]{1,0:T(8,128)(2,1)S(1)}, u32[]{:S(2)}, u32[]{:S(2)}) collective-permute-start(bf16[96,1024]{1,0:T(8,128)(2,1)S(1)} %add_convert_fusion.6), channel_id=1, source_target_pairs={{0,4},{4,8},{8,12},{12,0},{1,5},{5,9},{9,13},{13,1},{2,6},{6,10},{... | collective-permute-start | bytes 589832 | tf_op jit(solution)/shard_map/ppermute | solution.py:203

commit v8 on v7

--- a/solution.py
+++ b/solution.py
@@ -59,7 +59,7 @@
     chans = embed_ref.shape[0] // 4
     embed = embed_ref.shape[1]
     count = lax.axis_size("tok")
-    turn = lax.axis_index("tok") * (embed // count)
+    turn = lax.rem(lax.axis_index("tok") + 1, count) * (embed // count)
     turned_embed = pltpu.roll(embed_ref[...].astype(jnp.float32), lax.rem(embed - turn, embed), axis=1)
     for first in range(0, embed, LANES):
         scratch[...] = turned_embed[:, first : first + LANES]
@@ -261,44 +261,50 @@
     )
 
 
-def partial_kernel(first, tokens_ref, mixing_ref, sent_ref, kept_ref):
-    width = sent_ref.shape[1]
+def sent_kernel(tokens_ref, mixing_ref, *sent_refs):
+    rows, width = sent_refs[0].shape
     step = STEP if width % STEP == 0 else width
-    tokens = tokens_ref[...]
+    tokens = tokens_ref[:rows]
+    for piece, sent_ref in enumerate(sent_refs):
+        for at in range(0, width, step):
+            product = dot(tokens, mixing_ref[:, pl.ds(piece * width + at, step)])
+            sent_ref[:, pl.ds(at, step)] = product.astype(sent_ref.dtype)
+
+
+def hop_kernel(first, arrived_ref, tokens_ref, mixing_ref, sent_ref, kept_ref):
+    rows, width = sent_ref.shape
+    step = STEP if width % STEP == 0 else width
+    tokens = tokens_ref[rows:]
     for at in range(0, width, step):
-        product = jnp.dot(tokens, mixing_ref[:, pl.ds(first + at, step)], preferred_element_type=jnp.float32)
-        kept_ref[:, pl.ds(at, step)] = product[: kept_ref.shape[0]]
-        sent_ref[:, pl.ds(at, step)] = product[kept_ref.shape[0] :].astype(sent_ref.dtype)
-
-
-def partial(tokens, token_mixing, first, width, rows):
-    return call(
-        functools.partial(partial_kernel, first),
-        (
-            jax.ShapeDtypeStruct((rows, width), jnp.bfloat16),
-            jax.ShapeDtypeStruct((tokens.shape[0] - rows, width), jnp.float32),
-        ),
-        (tokens, token_mixing),
-    )
+        product = dot(tokens, mixing_ref[:, pl.ds(first + at, step)])
+        arrived = arrived_ref[:, pl.ds(at, step)].astype(jnp.float32)
+        sent_ref[:, pl.ds(at, step)] = (arrived + product[:rows]).astype(sent_ref.dtype)
+        kept_ref[:, pl.ds(at, step)] = product[rows:]
 
 
 def lift(tokens, token_mixing, pieces):
     count = lax.axis_size("tok")
-    rows = tokens.shape[0] // count
+    embed = tokens.shape[0]
+    rows = embed // count
     width = token_mixing.shape[1] // pieces
-    travelling, kept = [], []
-    for piece in range(pieces):
-        sent, others = partial(tokens, token_mixing, piece * width, width, rows)
-        travelling.append(sent)
-        kept.append(others)
+    sent = jax.ShapeDtypeStruct((rows, width), jnp.bfloat16)
+    travelling = list(call(sent_kernel, [sent] * pieces, (tokens, token_mixing)))
+    kept = [None] * pieces
     for step in range(1, count):
         for piece in range(pieces):
-            arrived = turned(travelling[piece], "tok", 1).astype(jnp.float32)
-            at = (count - 1 - step) * rows
-            summed = arrived + kept[piece][at : at + rows]
-            if step == count - 1:
-                summed = gelu(summed)
-            travelling[piece] = summed.astype(jnp.bfloat16)
+            arrived = turned(travelling[piece], "tok", -1)
+            if step == 1:
+                travelling[piece], kept[piece] = call(
+                    functools.partial(hop_kernel, piece * width),
+                    [sent, jax.ShapeDtypeStruct((embed - 2 * rows, width), jnp.float32)],
+                    (arrived, tokens, token_mixing),
+                )
+            else:
+                at = (step - 2) * rows
+                summed = arrived.astype(jnp.float32) + kept[piece][at : at + rows]
+                if step == count - 1:
+                    summed = gelu(summed)
+                travelling[piece] = summed.astype(jnp.bfloat16)
     return jnp.concatenate(travelling, axis=1)
 
 

time: 74.4 us -> 73.1 us (0.983)
  waiting for transfers between devices: 46.7 us -> 15 us
  starting transfers between devices: 13 us -> 43 us
    ppermute x17, waiting for transfers between devices: 46.7 us -> 15 us  [turned(): lax.ppermute(value, axis, [(i, (i + away) % count) for i in range(count)])]
    ppermute x17, starting transfers between devices: 13 us -> 43 us  [turned(): lax.ppermute(value, axis, [(i, (i + away) % count) for i in range(count)])]
    pallas_call x9 -> x10, Pallas kernels: 8.66 us -> 9.32 us  [call(): pl.pallas_call(kernel, out_shape=out_shape, in_specs=[pl.BlockSpec(memory...]
  transfers between devices with their start and end apart: 17 -> 17, of which waited for: 13 -> 5; matrix products, arithmetic and copies ran while one was open for 1% -> 1% of each run, Pallas kernels for 8% -> 9%
where the time goes in v8:
time: 73.1 us; the launch traced here: 72.8 us
  starting transfers between devices  43 us (59%)
  waiting for transfers between devices  15 us (21%)
  Pallas kernels  9.32 us (13%)
  local copies, waits for them, and re-layouts  3.89 us (5%)
  other arithmetic  1.5 us (2%)
    ppermute x17, starting transfers between devices, turned(): lax.ppermute(value, axis, [(i, (i + away) % count) for i in range(count)])  43 us
    ppermute x17, waiting for transfers between devices, turned(): lax.ppermute(value, axis, [(i, (i + away) % count) for i in range(count)])  15 us
    pallas_call x10, Pallas kernels, call(): pl.pallas_call(kernel, out_shape=out_shape, in_specs=[pl.BlockSpec(memory...  9.32 us
    unnamed x10, local copies, waits for them, and re-layouts  3.89 us
  transfers between devices with their start and end apart: 17, of which 5 were waited for; matrix products, arithmetic and copies ran while one was open for 1% of the time, Pallas kernels for 9%

profile of v8, /device:TPU:0, one launch (start us, length us, event | category | flops | bytes accessed | tf_op | source)
XLA Modules:
  0.0 72.8 jit_solution(15162860426542264469)
XLA Ops:
  0.0 1.0 %copy-done.1 = f32[64,32,32]{0,2,1:T(8,128)S(1)} copy-done((f32[64,32,32]{0,2,1:T(8,128)S(1)}, f32[64,32,32]{0,2,1:T(8,128)}, u32[]{:S(2)}) %copy-start.1) | copy-done | bytes 262168
  1.0 0.1 shard_map.55.refs_0_
  1.2 3.0 %collective-permute-start.1 = (bf16[16,32,128]{2,1,0:T(8,128)(2,1)S(1)}, bf16[16,32,128]{2,1,0:T(8,128)(2,1)S(1)}, u32[]{:S(2)}, u32[]{:S(2)}) collective-permute-start(bf16[16,32,128]{2,1,0:T(8,128)(2,1)S(1)} %shard_map.55.refs_0_), channel_id=1, source_target_pairs={{0,2},{2,0},{1,3},{3,1},{4,6},{6,4},{5,7},{7,5},{8,10},{10,8},{9,1... | collective-permute-start | bytes 393224 | tf_op jit(solution)/shard_map/ppermute | solution.py:203
  4.2 1.0 %copy-done.2 = f32[9,64,64]{2,1,0:T(8,128)S(1)} copy-done((f32[9,64,64]{2,1,0:T(8,128)S(1)}, f32[9,64,64]{2,1,0:T(8,128)}, u32[]{:S(2)}) %copy-start.2) | copy-done | bytes 147480
  5.1 1.0 %copy-done.3 = f32[9,64,64]{2,1,0:T(8,128)S(1)} copy-done((f32[9,64,64]{2,1,0:T(8,128)S(1)}, f32[9,64,64]{2,1,0:T(8,128)}, u32[]{:S(2)}) %copy-start.3) | copy-done | bytes 147480
  6.1 0.9 %copy-done.4 = bf16[256,384]{1,0:T(8,128)(2,1)S(1)} copy-done((bf16[256,384]{1,0:T(8,128)(2,1)S(1)}, bf16[256,384]{1,0:T(8,128)(2,1)}, u32[]{:S(2)}) %copy-start.4) | copy-done | bytes 196632
  7.0 0.6 shard_map.56
  7.6 0.0 collective-permute-done.1.refs_2_
  7.7 0.5 collective-permute-start.2
  8.2 0.0 collective-permute-done.refs_1_
  8.2 1.0 %collective-permute-done.2.refs_3_ = bf16[16,32,128]{2,1,0:T(8,128)(2,1)S(1)} collective-permute-done((bf16[16,32,128]{2,1,0:T(8,128)(2,1)S(1)}, bf16[16,32,128]{2,1,0:T(8,128)(2,1)S(1)}, u32[]{:S(2)}, u32[]{:S(2)}) %collective-permute-start.2) | collective-permute-done | bytes 131104 | tf_op jit(solution)/shard_map/ppermute | solution.py:203
  9.2 0.1 shard_map.57
  9.2 1.7 %collective-permute-start.3 = (bf16[1,128,128]{2,1,0:T(8,128)(2,1)S(1)}, bf16[1,128,128]{2,1,0:T(8,128)(2,1)S(1)}, u32[]{:S(2)}, u32[]{:S(2)}) collective-permute-start(bf16[1,128,128]{2,1,0:T(8,128)(2,1)S(1)} %get-tuple-element.35), channel_id=1, source_target_pairs={{0,4},{4,8},{8,12},{12,0},{1,5},{5,9},{9,13},{13,1},{2,6},{6,10},{... | collective-permute-start | bytes 98312 | tf_op jit(solution)/shard_map/ppermute | solution.py:203
  10.9 2.2 %collective-permute-start.4 = (bf16[1,128,128]{2,1,0:T(8,128)(2,1)S(1)}, bf16[1,128,128]{2,1,0:T(8,128)(2,1)S(1)}, u32[]{:S(2)}, u32[]{:S(2)}) collective-permute-start(bf16[1,128,128]{2,1,0:T(8,128)(2,1)S(1)} %get-tuple-element.36), channel_id=1, source_target_pairs={{0,12},{4,0},{8,4},{12,8},{1,13},{5,1},{9,5},{13,9},{2,14},{6,2},{... | collective-permute-start | bytes 98312 | tf_op jit(solution)/shard_map/ppermute | solution.py:203
  13.1 2.7 %shard_map.58 = (bf16[384,768]{1,0:T(8,128)(2,1)S(1)}, bf16[4,128,128]{2,1,0:T(8,128)(2,1)S(1)}, bf16[4,128,128]{2,1,0:T(8,128)(2,1)S(1)}) custom-call(bf16[16,128,128]{2,1,0:T(8,128)(2,1)S(1)} %get-tuple-element.34.field_ref, bf16[2,256,384]{2,1,0:T(8,128)(2,1)S(1)} %get-tuple-element.37.taps_one_ref, ...), custom_call_target="tpu_custom_call" | custom-call | flops 1635778560 | bytes 524288 | tf_op jit(solution)/shard_map/pallas_call | solution.py:190
  15.9 0.0 collective-permute-done.4.after_ref
  15.9 1.3 %shard_map.59.tokens_ref = bf16[384,1024]{1,0:T(8,128)(2,1)S(1)} custom-call(bf16[16,128,128]{2,1,0:T(8,128)(2,1)S(1)} %get-tuple-element.34.field_ref, bf16[1,128,128]{2,1,0:T(8,128)(2,1)S(1)} %collective-permute-done.3.before_ref, bf16[1,128,128]{2,1,0:T(8,128)(2,1)S(1)} %collective-permute-done.4.after_ref, ...), custom_call_target="tpu_custom_call" | custom-call | flops 503316480 | bytes 524288 | tf_op jit(solution)/shard_map/pallas_call | solution.py:190
  17.2 1.5 %shard_map.60 = (bf16[96,1024]{1,0:T(8,128)(2,1)S(1)}, bf16[96,1024]{1,0:T(8,128)(2,1)S(1)}, bf16[96,1024]{1,0:T(8,128)(2,1)S(1)}, bf16[96,1024]{1,0:T(8,128)(2,1)S(1)}) custom-call(bf16[384,1024]{1,0:T(8,128)(2,1)S(1)} %shard_map.59.tokens_ref, bf16[1024,4096]{1,0:T(8,128)(2,1)S(1)} %copy-done), custom_call_target="tpu_custom_call" | custom-call | tf_op jit(solution)/shard_map/pallas_call | solution.py:190
  18.7 3.0 %collective-permute-start.5 = (bf16[96,1024]{1,0:T(8,128)(2,1)S(1)}, bf16[96,1024]{1,0:T(8,128)(2,1)S(1)}, u32[]{:S(2)}, u32[]{:S(2)}) collective-permute-start(bf16[96,1024]{1,0:T(8,128)(2,1)S(1)} %get-tuple-element.43), channel_id=1, source_target_pairs={{0,12},{4,0},{8,4},{12,8},{1,13},{5,1},{9,5},{13,9},{2,14},{6,2},{... | collective-permute-start | bytes 589832 | tf_op jit(solution)/shard_map/ppermute | solution.py:203
  21.6 0.1 collective-permute-start.8
  21.7 0.4 collective-permute-start.11
  22.2 1.5 %collective-permute-start.14 = (bf16[96,1024]{1,0:T(8,128)(2,1)S(1)}, bf16[96,1024]{1,0:T(8,128)(2,1)S(1)}, u32[]{:S(2)}, u32[]{:S(2)}) collective-permute-start(bf16[96,1024]{1,0:T(8,128)(2,1)S(1)} %get-tuple-element.52), channel_id=1, source_target_pairs={{0,12},{4,0},{8,4},{12,8},{1,13},{5,1},{9,5},{13,9},{2,14},{6,2},{... | collective-permute-start | bytes 589832 | tf_op jit(solution)/shard_map/ppermute | solution.py:203
  23.7 3.3 %collective-permute-done.5.arrived_ref = bf16[96,1024]{1,0:T(8,128)(2,1)S(1)} collective-permute-done((bf16[96,1024]{1,0:T(8,128)(2,1)S(1)}, bf16[96,1024]{1,0:T(8,128)(2,1)S(1)}, u32[]{:S(2)}, u32[]{:S(2)}) %collective-permute-start.5) | collective-permute-done | bytes 196640 | tf_op jit(solution)/shard_map/ppermute | solution.py:203
  27.0 0.8 %shard_map.61 = (bf16[96,1024]{1,0:T(8,128)(2,1)S(1)}, f32[192,1024]{1,0:T(8,128)S(1)}) custom-call(bf16[96,1024]{1,0:T(8,128)(2,1)S(1)} %collective-permute-done.5.arrived_ref, bf16[384,1024]{1,0:T(8,128)(2,1)S(1)} %shard_map.59.tokens_ref, bf16[1024,4096]{1,0:T(8,128)(2,1)S(1)} %copy-done), custom_call_target="tpu_custom_call" | custom-call | tf_op jit(solution)/shard_map/pallas_call | solution.py:190
  27.8 4.3 %collective-permute-start.6 = (bf16[96,1024]{1,0:T(8,128)(2,1)S(1)}, bf16[96,1024]{1,0:T(8,128)(2,1)S(1)}, u32[]{:S(2)}, u32[]{:S(2)}) collective-permute-start(bf16[96,1024]{1,0:T(8,128)(2,1)S(1)} %get-tuple-element.44), channel_id=1, source_target_pairs={{0,12},{4,0},{8,4},{12,8},{1,13},{5,1},{9,5},{13,9},{2,14},{6,2},{... | collective-permute-start | bytes 589832 | tf_op jit(solution)/shard_map/ppermute | solution.py:203
  32.1 0.0 collective-permute-done.8.arrived_ref
  32.1 0.8 %shard_map.62 = (bf16[96,1024]{1,0:T(8,128)(2,1)S(1)}, f32[192,1024]{1,0:T(8,128)S(1)}) custom-call(bf16[96,1024]{1,0:T(8,128)(2,1)S(1)} %collective-permute-done.8.arrived_ref, bf16[384,1024]{1,0:T(8,128)(2,1)S(1)} %shard_map.59.tokens_ref, bf16[1024,4096]{1,0:T(8,128)(2,1)S(1)} %copy-done), custom_call_target="tpu_custom_call" | custom-call | tf_op jit(solution)/shard_map/pallas_call | solution.py:190
  32.9 3.4 %collective-permute-start.9 = (bf16[96,1024]{1,0:T(8,128)(2,1)S(1)}, bf16[96,1024]{1,0:T(8,128)(2,1)S(1)}, u32[]{:S(2)}, u32[]{:S(2)}) collective-permute-start(bf16[96,1024]{1,0:T(8,128)(2,1)S(1)} %get-tuple-element.47), channel_id=1, source_target_pairs={{0,12},{4,0},{8,4},{12,8},{1,13},{5,1},{9,5},{13,9},{2,14},{6,2},{... | collective-permute-start | bytes 589832 | tf_op jit(solution)/shard_map/ppermute | solution.py:203
  36.3 0.8 %shard_map.63 = (bf16[96,1024]{1,0:T(8,128)(2,1)S(1)}, f32[192,1024]{1,0:T(8,128)S(1)}) custom-call(bf16[96,1024]{1,0:T(8,128)(2,1)S(1)} %collective-permute-done.11.arrived_ref, bf16[384,1024]{1,0:T(8,128)(2,1)S(1)} %shard_map.59.tokens_ref, bf16[1024,4096]{1,0:T(8,128)(2,1)S(1)} %copy-done), custom_call_target="tpu_custom_call" | custom-call | tf_op jit(solution)/shard_map/pallas_call | solution.py:190
  37.1 3.4 %collective-permute-start.12 = (bf16[96,1024]{1,0:T(8,128)(2,1)S(1)}, bf16[96,1024]{1,0:T(8,128)(2,1)S(1)}, u32[]{:S(2)}, u32[]{:S(2)}) collective-permute-start(bf16[96,1024]{1,0:T(8,128)(2,1)S(1)} %get-tuple-element.50), channel_id=1, source_target_pairs={{0,12},{4,0},{8,4},{12,8},{1,13},{5,1},{9,5},{13,9},{2,14},{6,2},{... | collective-permute-start | bytes 589832 | tf_op jit(solution)/shard_map/ppermute | solution.py:203
  40.5 0.0 collective-permute-done.14.arrived_ref
  40.5 0.8 %shard_map.64 = (bf16[96,1024]{1,0:T(8,128)(2,1)S(1)}, f32[192,1024]{1,0:T(8,128)S(1)}) custom-call(bf16[96,1024]{1,0:T(8,128)(2,1)S(1)} %collective-permute-done.14.arrived_ref, bf16[384,1024]{1,0:T(8,128)(2,1)S(1)} %shard_map.59.tokens_ref, bf16[1024,4096]{1,0:T(8,128)(2,1)S(1)} %copy-done), custom_call_target="tpu_custom_call" | custom-call | tf_op jit(solution)/shard_map/pallas_call | solution.py:190
  41.3 3.4 %collective-permute-start.15 = (bf16[96,1024]{1,0:T(8,128)(2,1)S(1)}, bf16[96,1024]{1,0:T(8,128)(2,1)S(1)}, u32[]{:S(2)}, u32[]{:S(2)}) collective-permute-start(bf16[96,1024]{1,0:T(8,128)(2,1)S(1)} %get-tuple-element.53), channel_id=1, source_target_pairs={{0,12},{4,0},{8,4},{12,8},{1,13},{5,1},{9,5},{13,9},{2,14},{6,2},{... | collective-permute-start | bytes 589832 | tf_op jit(solution)/shard_map/ppermute | solution.py:203
  44.7 0.0 collective-permute-done.6
  44.8 3.4 %collective-permute-start.7 = (bf16[96,1024]{1,0:T(8,128)(2,1)S(1)}, bf16[96,1024]{1,0:T(8,128)(2,1)S(1)}, u32[]{:S(2)}, u32[]{:S(2)}) collective-permute-start(bf16[96,1024]{1,0:T(8,128)(2,1)S(1)} %add_convert_fusion.3), channel_id=1, source_target_pairs={{0,12},{4,0},{8,4},{12,8},{1,13},{5,1},{9,5},{13,9},{2,14},{6,2},{... | collective-permute-start | bytes 589832 | tf_op jit(solution)/shard_map/ppermute | solution.py:203
  48.2 0.0 collective-permute-done.9
  48.3 4.2 %collective-permute-start.10 = (bf16[96,1024]{1,0:T(8,128)(2,1)S(1)}, bf16[96,1024]{1,0:T(8,128)(2,1)S(1)}, u32[]{:S(2)}, u32[]{:S(2)}) collective-permute-start(bf16[96,1024]{1,0:T(8,128)(2,1)S(1)} %add_convert_fusion.2), channel_id=1, source_target_pairs={{0,12},{4,0},{8,4},{12,8},{1,13},{5,1},{9,5},{13,9},{2,14},{6,2},{... | collective-permute-start | bytes 589832 | tf_op jit(solution)/shard_map/ppermute | solution.py:203
  52.4 0.0 collective-permute-done.12
  52.5 4.2 %collective-permute-start.13 = (bf16[96,1024]{1,0:T(8,128)(2,1)S(1)}, bf16[96,1024]{1,0:T(8,128)(2,1)S(1)}, u32[]{:S(2)}, u32[]{:S(2)}) collective-permute-start(bf16[96,1024]{1,0:T(8,128)(2,1)S(1)} %add_convert_fusion.1), channel_id=1, source_target_pairs={{0,12},{4,0},{8,4},{12,8},{1,13},{5,1},{9,5},{13,9},{2,14},{6,2},{... | collective-permute-start | bytes 589832 | tf_op jit(solution)/shard_map/ppermute | solution.py:203
  56.7 4.2 %collective-permute-start.16 = (bf16[96,1024]{1,0:T(8,128)(2,1)S(1)}, bf16[96,1024]{1,0:T(8,128)(2,1)S(1)}, u32[]{:S(2)}, u32[]{:S(2)}) collective-permute-start(bf16[96,1024]{1,0:T(8,128)(2,1)S(1)} %add_convert_fusion), channel_id=1, source_target_pairs={{0,12},{4,0},{8,4},{12,8},{1,13},{5,1},{9,5},{13,9},{2,14},{6,2},{... | collective-permute-start | bytes 589832 | tf_op jit(solution)/shard_map/ppermute | solution.py:203
  60.9 0.1 multiply_convert_fusion.3
  61.0 3.9 %collective-permute-done.10 = bf16[96,1024]{1,0:T(8,128)(2,1)S(1)} collective-permute-done((bf16[96,1024]{1,0:T(8,128)(2,1)S(1)}, bf16[96,1024]{1,0:T(8,128)(2,1)S(1)}, u32[]{:S(2)}, u32[]{:S(2)}) %collective-permute-start.10) | collective-permute-done | bytes 196640 | tf_op jit(solution)/shard_map/ppermute | solution.py:203
  64.9 0.1 multiply_convert_fusion.2
  65.0 4.1 %collective-permute-done.13 = bf16[96,1024]{1,0:T(8,128)(2,1)S(1)} collective-permute-done((bf16[96,1024]{1,0:T(8,128)(2,1)S(1)}, bf16[96,1024]{1,0:T(8,128)(2,1)S(1)}, u32[]{:S(2)}, u32[]{:S(2)}) %collective-permute-start.13) | collective-permute-done | bytes 196640 | tf_op jit(solution)/shard_map/ppermute | solution.py:203
  69.1 0.1 multiply_convert_fusion.1
  69.2 2.5 %collective-permute-done.16 = bf16[96,1024]{1,0:T(8,128)(2,1)S(1)} collective-permute-done((bf16[96,1024]{1,0:T(8,128)(2,1)S(1)}, bf16[96,1024]{1,0:T(8,128)(2,1)S(1)}, u32[]{:S(2)}, u32[]{:S(2)}) %collective-permute-start.16) | collective-permute-done | bytes 196640 | tf_op jit(solution)/shard_map/ppermute | solution.py:203
  71.8 0.1 multiply_convert_fusion
  71.9 0.9 %pad_maximum_fusion = bf16[96,4096]{1,0:T(8,128)(2,1)} fusion(bf16[96,1024]{1,0:T(8,128)(2,1)S(1)} %multiply_convert_fusion, bf16[96,1024]{1,0:T(8,128)(2,1)S(1)} %multiply_convert_fusion.1, bf16[96,1024]{1,0:T(8,128)(2,1)S(1)} %multiply_convert_fusion.2, bf16[96,1024]{1,0:T(8,128)(2,1)S(1)} %multiply_convert_fusion.3), kind=kLoop, calls=%fused_computation | loop fusion | flops 3145728 | bytes 1572864 | tf_op jit(solution)/shard_map/concatenate | solution.py:308
  (15 shorter events, 0.2 us)
Async XLA Ops:
  0.0 1.0 %copy-start.1 = (f32[64,32,32]{0,2,1:T(8,128)S(1)}, f32[64,32,32]{0,2,1:T(8,128)}, u32[]{:S(2)}) copy-start(f32[64,32,32]{0,2,1:T(8,128)} %param.5) | copy-start | bytes 786436
  1.2 6.5 %collective-permute-start.1 = (bf16[16,32,128]{2,1,0:T(8,128)(2,1)S(1)}, bf16[16,32,128]{2,1,0:T(8,128)(2,1)S(1)}, u32[]{:S(2)}, u32[]{:S(2)}) collective-permute-start(bf16[16,32,128]{2,1,0:T(8,128)(2,1)S(1)} %shard_map.55.refs_0_), channel_id=1, source_target_pairs={{0,2},{2,0},{1,3},{3,1},{4,6},{6,4},{5,7},{7,5},{8,10},{10,8},{9,1... | collective-permute-start | bytes 393224 | tf_op jit(solution)/shard_map/ppermute | solution.py:203
  4.2 4.0 %collective-permute-start = (bf16[16,32,128]{2,1,0:T(8,128)(2,1)S(1)}, bf16[16,32,128]{2,1,0:T(8,128)(2,1)S(1)}, u32[]{:S(2)}, u32[]{:S(2)}) collective-permute-start(bf16[16,32,128]{2,1,0:T(8,128)(2,1)S(1)} %shard_map.55.refs_0_), channel_id=1, source_target_pairs={{0,1},{1,0},{2,3},{3,2},{4,5},{5,4},{6,7},{7,6},{8,9},{9,8},{10,11... | collective-permute-start | bytes 393224 | tf_op jit(solution)/shard_map/ppermute | solution.py:203
  4.2 1.0 %copy-start.2 = (f32[9,64,64]{2,1,0:T(8,128)S(1)}, f32[9,64,64]{2,1,0:T(8,128)}, u32[]{:S(2)}) copy-start(f32[9,64,64]{2,1,0:T(8,128)} %first_ref.1) | copy-start | bytes 442372
  5.1 1.0 %copy-start.3 = (f32[9,64,64]{2,1,0:T(8,128)S(1)}, f32[9,64,64]{2,1,0:T(8,128)}, u32[]{:S(2)}) copy-start(f32[9,64,64]{2,1,0:T(8,128)} %second_ref.1) | copy-start | bytes 442372
  6.1 0.9 %copy-start.4 = (bf16[256,384]{1,0:T(8,128)(2,1)S(1)}, bf16[256,384]{1,0:T(8,128)(2,1)}, u32[]{:S(2)}) copy-start(bf16[256,384]{1,0:T(8,128)(2,1)} %embed_ref.1) | copy-start | bytes 589828
  7.7 1.5 %collective-permute-start.2 = (bf16[16,32,128]{2,1,0:T(8,128)(2,1)S(1)}, bf16[16,32,128]{2,1,0:T(8,128)(2,1)S(1)}, u32[]{:S(2)}, u32[]{:S(2)}) collective-permute-start(bf16[16,32,128]{2,1,0:T(8,128)(2,1)S(1)} %collective-permute-done.1.refs_2_), channel_id=1, source_target_pairs={{0,1},{1,0},{2,3},{3,2},{4,5},{5,4},{6,7},{7,6},{8,9},{9,8},{10,11... | collective-permute-start | bytes 393224 | tf_op jit(solution)/shard_map/ppermute | solution.py:203
  9.2 6.6 %collective-permute-start.3 = (bf16[1,128,128]{2,1,0:T(8,128)(2,1)S(1)}, bf16[1,128,128]{2,1,0:T(8,128)(2,1)S(1)}, u32[]{:S(2)}, u32[]{:S(2)}) collective-permute-start(bf16[1,128,128]{2,1,0:T(8,128)(2,1)S(1)} %get-tuple-element.35), channel_id=1, source_target_pairs={{0,4},{4,8},{8,12},{12,0},{1,5},{5,9},{9,13},{13,1},{2,6},{6,10},{... | collective-permute-start | bytes 98312 | tf_op jit(solution)/shard_map/ppermute | solution.py:203
  10.9 5.0 %collective-permute-start.4 = (bf16[1,128,128]{2,1,0:T(8,128)(2,1)S(1)}, bf16[1,128,128]{2,1,0:T(8,128)(2,1)S(1)}, u32[]{:S(2)}, u32[]{:S(2)}) collective-permute-start(bf16[1,128,128]{2,1,0:T(8,128)(2,1)S(1)} %get-tuple-element.36), channel_id=1, source_target_pairs={{0,12},{4,0},{8,4},{12,8},{1,13},{5,1},{9,5},{13,9},{2,14},{6,2},{... | collective-permute-start | bytes 98312 | tf_op jit(solution)/shard_map/ppermute | solution.py:203
  13.1 4.0 %copy-start = (bf16[1024,4096]{1,0:T(8,128)(2,1)S(1)}, bf16[1024,4096]{1,0:T(8,128)(2,1)}, u32[]{:S(2)}) copy-start(bf16[1024,4096]{1,0:T(8,128)(2,1)} %mixing_ref.9) | copy-start | bytes 25165828
  18.7 8.3 %collective-permute-start.5 = (bf16[96,1024]{1,0:T(8,128)(2,1)S(1)}, bf16[96,1024]{1,0:T(8,128)(2,1)S(1)}, u32[]{:S(2)}, u32[]{:S(2)}) collective-permute-start(bf16[96,1024]{1,0:T(8,128)(2,1)S(1)} %get-tuple-element.43), channel_id=1, source_target_pairs={{0,12},{4,0},{8,4},{12,8},{1,13},{5,1},{9,5},{13,9},{2,14},{6,2},{... | collective-permute-start | bytes 589832 | tf_op jit(solution)/shard_map/ppermute | solution.py:203
  21.6 10.5 %collective-permute-start.8 = (bf16[96,1024]{1,0:T(8,128)(2,1)S(1)}, bf16[96,1024]{1,0:T(8,128)(2,1)S(1)}, u32[]{:S(2)}, u32[]{:S(2)}) collective-permute-start(bf16[96,1024]{1,0:T(8,128)(2,1)S(1)} %get-tuple-element.46), channel_id=1, source_target_pairs={{0,12},{4,0},{8,4},{12,8},{1,13},{5,1},{9,5},{13,9},{2,14},{6,2},{... | collective-permute-start | bytes 589832 | tf_op jit(solution)/shard_map/ppermute | solution.py:203
  21.7 14.6 %collective-permute-start.11 = (bf16[96,1024]{1,0:T(8,128)(2,1)S(1)}, bf16[96,1024]{1,0:T(8,128)(2,1)S(1)}, u32[]{:S(2)}, u32[]{:S(2)}) collective-permute-start(bf16[96,1024]{1,0:T(8,128)(2,1)S(1)} %get-tuple-element.49), channel_id=1, source_target_pairs={{0,12},{4,0},{8,4},{12,8},{1,13},{5,1},{9,5},{13,9},{2,14},{6,2},{... | collective-permute-start | bytes 589832 | tf_op jit(solution)/shard_map/ppermute | solution.py:203
  22.2 18.4 %collective-permute-start.14 = (bf16[96,1024]{1,0:T(8,128)(2,1)S(1)}, bf16[96,1024]{1,0:T(8,128)(2,1)S(1)}, u32[]{:S(2)}, u32[]{:S(2)}) collective-permute-start(bf16[96,1024]{1,0:T(8,128)(2,1)S(1)} %get-tuple-element.52), channel_id=1, source_target_pairs={{0,12},{4,0},{8,4},{12,8},{1,13},{5,1},{9,5},{13,9},{2,14},{6,2},{... | collective-permute-start | bytes 589832 | tf_op jit(solution)/shard_map/ppermute | solution.py:203
  27.8 17.0 %collective-permute-start.6 = (bf16[96,1024]{1,0:T(8,128)(2,1)S(1)}, bf16[96,1024]{1,0:T(8,128)(2,1)S(1)}, u32[]{:S(2)}, u32[]{:S(2)}) collective-permute-start(bf16[96,1024]{1,0:T(8,128)(2,1)S(1)} %get-tuple-element.44), channel_id=1, source_target_pairs={{0,12},{4,0},{8,4},{12,8},{1,13},{5,1},{9,5},{13,9},{2,14},{6,2},{... | collective-permute-start | bytes 589832 | tf_op jit(solution)/shard_map/ppermute | solution.py:203
  32.9 15.3 %collective-permute-start.9 = (bf16[96,1024]{1,0:T(8,128)(2,1)S(1)}, bf16[96,1024]{1,0:T(8,128)(2,1)S(1)}, u32[]{:S(2)}, u32[]{:S(2)}) collective-permute-start(bf16[96,1024]{1,0:T(8,128)(2,1)S(1)} %get-tuple-element.47), channel_id=1, source_target_pairs={{0,12},{4,0},{8,4},{12,8},{1,13},{5,1},{9,5},{13,9},{2,14},{6,2},{... | collective-permute-start | bytes 589832 | tf_op jit(solution)/shard_map/ppermute | solution.py:203
  37.1 15.3 %collective-permute-start.12 = (bf16[96,1024]{1,0:T(8,128)(2,1)S(1)}, bf16[96,1024]{1,0:T(8,128)(2,1)S(1)}, u32[]{:S(2)}, u32[]{:S(2)}) collective-permute-start(bf16[96,1024]{1,0:T(8,128)(2,1)S(1)} %get-tuple-element.50), channel_id=1, source_target_pairs={{0,12},{4,0},{8,4},{12,8},{1,13},{5,1},{9,5},{13,9},{2,14},{6,2},{... | collective-permute-start | bytes 589832 | tf_op jit(solution)/shard_map/ppermute | solution.py:203
  41.3 15.3 %collective-permute-start.15 = (bf16[96,1024]{1,0:T(8,128)(2,1)S(1)}, bf16[96,1024]{1,0:T(8,128)(2,1)S(1)}, u32[]{:S(2)}, u32[]{:S(2)}) collective-permute-start(bf16[96,1024]{1,0:T(8,128)(2,1)S(1)} %get-tuple-element.53), channel_id=1, source_target_pairs={{0,12},{4,0},{8,4},{12,8},{1,13},{5,1},{9,5},{13,9},{2,14},{6,2},{... | collective-permute-start | bytes 589832 | tf_op jit(solution)/shard_map/ppermute | solution.py:203
  44.8 16.1 %collective-permute-start.7 = (bf16[96,1024]{1,0:T(8,128)(2,1)S(1)}, bf16[96,1024]{1,0:T(8,128)(2,1)S(1)}, u32[]{:S(2)}, u32[]{:S(2)}) collective-permute-start(bf16[96,1024]{1,0:T(8,128)(2,1)S(1)} %add_convert_fusion.3), channel_id=1, source_target_pairs={{0,12},{4,0},{8,4},{12,8},{1,13},{5,1},{9,5},{13,9},{2,14},{6,2},{... | collective-permute-start | bytes 589832 | tf_op jit(solution)/shard_map/ppermute | solution.py:203
  48.3 16.6 %collective-permute-start.10 = (bf16[96,1024]{1,0:T(8,128)(2,1)S(1)}, bf16[96,1024]{1,0:T(8,128)(2,1)S(1)}, u32[]{:S(2)}, u32[]{:S(2)}) collective-permute-start(bf16[96,1024]{1,0:T(8,128)(2,1)S(1)} %add_convert_fusion.2), channel_id=1, source_target_pairs={{0,12},{4,0},{8,4},{12,8},{1,13},{5,1},{9,5},{13,9},{2,14},{6,2},{... | collective-permute-start | bytes 589832 | tf_op jit(solution)/shard_map/ppermute | solution.py:203
  52.5 16.6 %collective-permute-start.13 = (bf16[96,1024]{1,0:T(8,128)(2,1)S(1)}, bf16[96,1024]{1,0:T(8,128)(2,1)S(1)}, u32[]{:S(2)}, u32[]{:S(2)}) collective-permute-start(bf16[96,1024]{1,0:T(8,128)(2,1)S(1)} %add_convert_fusion.1), channel_id=1, source_target_pairs={{0,12},{4,0},{8,4},{12,8},{1,13},{5,1},{9,5},{13,9},{2,14},{6,2},{... | collective-permute-start | bytes 589832 | tf_op jit(solution)/shard_map/ppermute | solution.py:203
  56.7 15.1 %collective-permute-start.16 = (bf16[96,1024]{1,0:T(8,128)(2,1)S(1)}, bf16[96,1024]{1,0:T(8,128)(2,1)S(1)}, u32[]{:S(2)}, u32[]{:S(2)}) collective-permute-start(bf16[96,1024]{1,0:T(8,128)(2,1)S(1)} %add_convert_fusion), channel_id=1, source_target_pairs={{0,12},{4,0},{8,4},{12,8},{1,13},{5,1},{9,5},{13,9},{2,14},{6,2},{... | collective-permute-start | bytes 589832 | tf_op jit(solution)/shard_map/ppermute | solution.py:203

commit v9 on v8

--- a/solution.py
+++ b/solution.py
@@ -7,7 +7,7 @@
 from jax.experimental.pallas import tpu as pltpu
 from jax.sharding import PartitionSpec as P
 
-PIECES = 4
+PIECES = 2
 STEP = 256
 LANES = 128
 VMEM_BYTES = 24 * 1024 * 1024

time: 73.1 us -> 73.1 us (level)
  waiting for transfers between devices: 15 us -> 30.6 us
  starting transfers between devices: 43 us -> 27.8 us
    ppermute x17 -> x11, waiting for transfers between devices: 15 us -> 30.6 us  [turned(): lax.ppermute(value, axis, [(i, (i + away) % count) for i in range(count)])]
    ppermute x17 -> x11, starting transfers between devices: 43 us -> 27.8 us  [turned(): lax.ppermute(value, axis, [(i, (i + away) % count) for i in range(count)])]
    pallas_call x10 -> x8, Pallas kernels: 9.32 us -> 8.98 us  [call(): pl.pallas_call(kernel, out_shape=out_shape, in_specs=[pl.BlockSpec(memory...]
  transfers between devices with their start and end apart: 17 -> 11, of which waited for: 5 -> 7; matrix products, arithmetic and copies ran while one was open for 1% -> 0% of each run, Pallas kernels for 9% -> 8%
where the time goes in v9:
time: 73.1 us; the launch traced here: 72.9 us
  waiting for transfers between devices  30.6 us (42%)
  starting transfers between devices  27.8 us (38%)
  Pallas kernels  8.98 us (12%)
  local copies, waits for them, and re-layouts  3.89 us (5%)
  other arithmetic  1.48 us (2%)
    ppermute x11, waiting for transfers between devices, turned(): lax.ppermute(value, axis, [(i, (i + away) % count) for i in range(count)])  30.6 us
    ppermute x11, starting transfers between devices, turned(): lax.ppermute(value, axis, [(i, (i + away) % count) for i in range(count)])  27.8 us
    pallas_call x8, Pallas kernels, call(): pl.pallas_call(kernel, out_shape=out_shape, in_specs=[pl.BlockSpec(memory...  8.98 us
    unnamed x10, local copies, waits for them, and re-layouts  3.89 us
  transfers between devices with their start and end apart: 11, of which 7 were waited for; matrix products, arithmetic and copies ran while one was open for 0% of the time, Pallas kernels for 8%

profile of v9, /device:TPU:0, one launch (start us, length us, event | category | flops | bytes accessed | tf_op | source)
XLA Modules:
  0.0 72.9 jit_solution(4728778923626848878)
XLA Ops:
  0.0 0.0 copy-start.1
  0.0 1.0 %copy-done.1 = f32[64,32,32]{0,2,1:T(8,128)S(1)} copy-done((f32[64,32,32]{0,2,1:T(8,128)S(1)}, f32[64,32,32]{0,2,1:T(8,128)}, u32[]{:S(2)}) %copy-start.1) | copy-done | bytes 262168
  1.0 0.1 shard_map.55.refs_0_
  1.2 3.0 %collective-permute-start.1 = (bf16[16,32,128]{2,1,0:T(8,128)(2,1)S(1)}, bf16[16,32,128]{2,1,0:T(8,128)(2,1)S(1)}, u32[]{:S(2)}, u32[]{:S(2)}) collective-permute-start(bf16[16,32,128]{2,1,0:T(8,128)(2,1)S(1)} %shard_map.55.refs_0_), channel_id=1, source_target_pairs={{0,2},{2,0},{1,3},{3,1},{4,6},{6,4},{5,7},{7,5},{8,10},{10,8},{9,1... | collective-permute-start | bytes 393224 | tf_op jit(solution)/shard_map/ppermute | solution.py:203
  4.2 0.0 collective-permute-start
  4.2 0.0 copy-start.2
  4.2 1.0 %copy-done.2 = f32[9,64,64]{2,1,0:T(8,128)S(1)} copy-done((f32[9,64,64]{2,1,0:T(8,128)S(1)}, f32[9,64,64]{2,1,0:T(8,128)}, u32[]{:S(2)}) %copy-start.2) | copy-done | bytes 147480
  5.1 0.0 copy-start.3
  5.1 1.0 %copy-done.3 = f32[9,64,64]{2,1,0:T(8,128)S(1)} copy-done((f32[9,64,64]{2,1,0:T(8,128)S(1)}, f32[9,64,64]{2,1,0:T(8,128)}, u32[]{:S(2)}) %copy-start.3) | copy-done | bytes 147480
  6.1 0.0 copy-start.4
  6.1 0.9 %copy-done.4 = bf16[256,384]{1,0:T(8,128)(2,1)S(1)} copy-done((bf16[256,384]{1,0:T(8,128)(2,1)S(1)}, bf16[256,384]{1,0:T(8,128)(2,1)}, u32[]{:S(2)}) %copy-start.4) | copy-done | bytes 196632
  7.0 0.6 shard_map.56
  7.6 0.0 collective-permute-done.1.refs_2_
  7.7 0.5 collective-permute-start.2
  8.2 0.0 collective-permute-done.refs_1_
  8.2 1.0 %collective-permute-done.2.refs_3_ = bf16[16,32,128]{2,1,0:T(8,128)(2,1)S(1)} collective-permute-done((bf16[16,32,128]{2,1,0:T(8,128)(2,1)S(1)}, bf16[16,32,128]{2,1,0:T(8,128)(2,1)S(1)}, u32[]{:S(2)}, u32[]{:S(2)}) %collective-permute-start.2) | collective-permute-done | bytes 131104 | tf_op jit(solution)/shard_map/ppermute | solution.py:203
  9.2 0.1 shard_map.57
  9.2 1.7 %collective-permute-start.3 = (bf16[1,128,128]{2,1,0:T(8,128)(2,1)S(1)}, bf16[1,128,128]{2,1,0:T(8,128)(2,1)S(1)}, u32[]{:S(2)}, u32[]{:S(2)}) collective-permute-start(bf16[1,128,128]{2,1,0:T(8,128)(2,1)S(1)} %get-tuple-element.29), channel_id=1, source_target_pairs={{0,4},{4,8},{8,12},{12,0},{1,5},{5,9},{9,13},{13,1},{2,6},{6,10},{... | collective-permute-start | bytes 98312 | tf_op jit(solution)/shard_map/ppermute | solution.py:203
  10.9 2.2 %collective-permute-start.4 = (bf16[1,128,128]{2,1,0:T(8,128)(2,1)S(1)}, bf16[1,128,128]{2,1,0:T(8,128)(2,1)S(1)}, u32[]{:S(2)}, u32[]{:S(2)}) collective-permute-start(bf16[1,128,128]{2,1,0:T(8,128)(2,1)S(1)} %get-tuple-element.30), channel_id=1, source_target_pairs={{0,12},{4,0},{8,4},{12,8},{1,13},{5,1},{9,5},{13,9},{2,14},{6,2},{... | collective-permute-start | bytes 98312 | tf_op jit(solution)/shard_map/ppermute | solution.py:203
  13.1 0.0 copy-start
  13.1 2.7 %shard_map.58 = (bf16[384,768]{1,0:T(8,128)(2,1)S(1)}, bf16[4,128,128]{2,1,0:T(8,128)(2,1)S(1)}, bf16[4,128,128]{2,1,0:T(8,128)(2,1)S(1)}) custom-call(bf16[16,128,128]{2,1,0:T(8,128)(2,1)S(1)} %get-tuple-element.28.field_ref, bf16[2,256,384]{2,1,0:T(8,128)(2,1)S(1)} %get-tuple-element.31.taps_one_ref, ...), custom_call_target="tpu_custom_call" | custom-call | flops 1635778560 | bytes 524288 | tf_op jit(solution)/shard_map/pallas_call | solution.py:190
  15.9 0.0 collective-permute-done.3.before_ref
  15.9 0.0 collective-permute-done.4.after_ref
  15.9 1.3 %shard_map.59.tokens_ref = bf16[384,1024]{1,0:T(8,128)(2,1)S(1)} custom-call(bf16[16,128,128]{2,1,0:T(8,128)(2,1)S(1)} %get-tuple-element.28.field_ref, bf16[1,128,128]{2,1,0:T(8,128)(2,1)S(1)} %collective-permute-done.3.before_ref, bf16[1,128,128]{2,1,0:T(8,128)(2,1)S(1)} %collective-permute-done.4.after_ref, ...), custom_call_target="tpu_custom_call" | custom-call | flops 503316480 | bytes 524288 | tf_op jit(solution)/shard_map/pallas_call | solution.py:190
  17.2 0.0 copy-done
  17.2 1.5 %shard_map.60 = (bf16[96,2048]{1,0:T(8,128)(2,1)S(1)}, bf16[96,2048]{1,0:T(8,128)(2,1)S(1)}) custom-call(bf16[384,1024]{1,0:T(8,128)(2,1)S(1)} %shard_map.59.tokens_ref, bf16[1024,4096]{1,0:T(8,128)(2,1)S(1)} %copy-done), custom_call_target="tpu_custom_call" | custom-call | tf_op jit(solution)/shard_map/pallas_call | solution.py:190
  18.7 3.0 %collective-permute-start.8 = (bf16[96,2048]{1,0:T(8,128)(2,1)S(1)}, bf16[96,2048]{1,0:T(8,128)(2,1)S(1)}, u32[]{:S(2)}, u32[]{:S(2)}) collective-permute-start(bf16[96,2048]{1,0:T(8,128)(2,1)S(1)} %get-tuple-element.40), channel_id=1, source_target_pairs={{0,12},{4,0},{8,4},{12,8},{1,13},{5,1},{9,5},{13,9},{2,14},{6,2},{... | collective-permute-start | bytes 1179656 | tf_op jit(solution)/shard_map/ppermute | solution.py:203
  21.6 0.1 collective-permute-start.5
  21.7 9.5 %collective-permute-done.8.arrived_ref = bf16[96,2048]{1,0:T(8,128)(2,1)S(1)} collective-permute-done((bf16[96,2048]{1,0:T(8,128)(2,1)S(1)}, bf16[96,2048]{1,0:T(8,128)(2,1)S(1)}, u32[]{:S(2)}, u32[]{:S(2)}) %collective-permute-start.8) | collective-permute-done | bytes 393248 | tf_op jit(solution)/shard_map/ppermute | solution.py:203
  31.2 1.4 %shard_map.62 = (bf16[96,2048]{1,0:T(8,128)(2,1)S(1)}, f32[192,2048]{1,0:T(8,128)S(1)}) custom-call(bf16[96,2048]{1,0:T(8,128)(2,1)S(1)} %collective-permute-done.8.arrived_ref, bf16[384,1024]{1,0:T(8,128)(2,1)S(1)} %shard_map.59.tokens_ref, bf16[1024,4096]{1,0:T(8,128)(2,1)S(1)} %copy-done), custom_call_target="tpu_custom_call" | custom-call | tf_op jit(solution)/shard_map/pallas_call | solution.py:190
  32.6 4.3 %collective-permute-start.9 = (bf16[96,2048]{1,0:T(8,128)(2,1)S(1)}, bf16[96,2048]{1,0:T(8,128)(2,1)S(1)}, u32[]{:S(2)}, u32[]{:S(2)}) collective-permute-start(bf16[96,2048]{1,0:T(8,128)(2,1)S(1)} %get-tuple-element.41), channel_id=1, source_target_pairs={{0,12},{4,0},{8,4},{12,8},{1,13},{5,1},{9,5},{13,9},{2,14},{6,2},{... | collective-permute-start | bytes 1179656 | tf_op jit(solution)/shard_map/ppermute | solution.py:203
  36.9 2.7 %collective-permute-done.5.arrived_ref = bf16[96,2048]{1,0:T(8,128)(2,1)S(1)} collective-permute-done((bf16[96,2048]{1,0:T(8,128)(2,1)S(1)}, bf16[96,2048]{1,0:T(8,128)(2,1)S(1)}, u32[]{:S(2)}, u32[]{:S(2)}) %collective-permute-start.5) | collective-permute-done | bytes 393248 | tf_op jit(solution)/shard_map/ppermute | solution.py:203
  39.6 1.4 %shard_map.61 = (bf16[96,2048]{1,0:T(8,128)(2,1)S(1)}, f32[192,2048]{1,0:T(8,128)S(1)}) custom-call(bf16[96,2048]{1,0:T(8,128)(2,1)S(1)} %collective-permute-done.5.arrived_ref, bf16[384,1024]{1,0:T(8,128)(2,1)S(1)} %shard_map.59.tokens_ref, bf16[1024,4096]{1,0:T(8,128)(2,1)S(1)} %copy-done), custom_call_target="tpu_custom_call" | custom-call | tf_op jit(solution)/shard_map/pallas_call | solution.py:190
  41.0 4.3 %collective-permute-start.6 = (bf16[96,2048]{1,0:T(8,128)(2,1)S(1)}, bf16[96,2048]{1,0:T(8,128)(2,1)S(1)}, u32[]{:S(2)}, u32[]{:S(2)}) collective-permute-start(bf16[96,2048]{1,0:T(8,128)(2,1)S(1)} %get-tuple-element.38), channel_id=1, source_target_pairs={{0,12},{4,0},{8,4},{12,8},{1,13},{5,1},{9,5},{13,9},{2,14},{6,2},{... | collective-permute-start | bytes 1179656 | tf_op jit(solution)/shard_map/ppermute | solution.py:203
  45.4 2.7 %collective-permute-done.9 = bf16[96,2048]{1,0:T(8,128)(2,1)S(1)} collective-permute-done((bf16[96,2048]{1,0:T(8,128)(2,1)S(1)}, bf16[96,2048]{1,0:T(8,128)(2,1)S(1)}, u32[]{:S(2)}, u32[]{:S(2)}) %collective-permute-start.9) | collective-permute-done | bytes 393248 | tf_op jit(solution)/shard_map/ppermute | solution.py:203
  48.1 0.1 add_convert_fusion
  48.1 4.3 %collective-permute-start.10 = (bf16[96,2048]{1,0:T(8,128)(2,1)S(1)}, bf16[96,2048]{1,0:T(8,128)(2,1)S(1)}, u32[]{:S(2)}, u32[]{:S(2)}) collective-permute-start(bf16[96,2048]{1,0:T(8,128)(2,1)S(1)} %add_convert_fusion), channel_id=1, source_target_pairs={{0,12},{4,0},{8,4},{12,8},{1,13},{5,1},{9,5},{13,9},{2,14},{6,2},{... | collective-permute-start | bytes 1179656 | tf_op jit(solution)/shard_map/ppermute | solution.py:203
  52.5 4.0 %collective-permute-done.6 = bf16[96,2048]{1,0:T(8,128)(2,1)S(1)} collective-permute-done((bf16[96,2048]{1,0:T(8,128)(2,1)S(1)}, bf16[96,2048]{1,0:T(8,128)(2,1)S(1)}, u32[]{:S(2)}, u32[]{:S(2)}) %collective-permute-start.6) | collective-permute-done | bytes 393248 | tf_op jit(solution)/shard_map/ppermute | solution.py:203
  56.5 0.1 add_convert_fusion.1
  56.6 4.3 %collective-permute-start.7 = (bf16[96,2048]{1,0:T(8,128)(2,1)S(1)}, bf16[96,2048]{1,0:T(8,128)(2,1)S(1)}, u32[]{:S(2)}, u32[]{:S(2)}) collective-permute-start(bf16[96,2048]{1,0:T(8,128)(2,1)S(1)} %add_convert_fusion.1), channel_id=1, source_target_pairs={{0,12},{4,0},{8,4},{12,8},{1,13},{5,1},{9,5},{13,9},{2,14},{6,2},{... | collective-permute-start | bytes 1179656 | tf_op jit(solution)/shard_map/ppermute | solution.py:203
  60.9 4.0 %collective-permute-done.10 = bf16[96,2048]{1,0:T(8,128)(2,1)S(1)} collective-permute-done((bf16[96,2048]{1,0:T(8,128)(2,1)S(1)}, bf16[96,2048]{1,0:T(8,128)(2,1)S(1)}, u32[]{:S(2)}, u32[]{:S(2)}) %collective-permute-start.10) | collective-permute-done | bytes 393248 | tf_op jit(solution)/shard_map/ppermute | solution.py:203
  64.9 0.2 multiply_convert_fusion
  65.1 6.6 %collective-permute-done.7 = bf16[96,2048]{1,0:T(8,128)(2,1)S(1)} collective-permute-done((bf16[96,2048]{1,0:T(8,128)(2,1)S(1)}, bf16[96,2048]{1,0:T(8,128)(2,1)S(1)}, u32[]{:S(2)}, u32[]{:S(2)}) %collective-permute-start.7) | collective-permute-done | bytes 393248 | tf_op jit(solution)/shard_map/ppermute | solution.py:203
  71.8 0.2 multiply_convert_fusion.1
  72.0 0.9 %pad_maximum_fusion = bf16[96,4096]{1,0:T(8,128)(2,1)} fusion(bf16[96,2048]{1,0:T(8,128)(2,1)S(1)} %multiply_convert_fusion, bf16[96,2048]{1,0:T(8,128)(2,1)S(1)} %multiply_convert_fusion.1), kind=kLoop, calls=%fused_computation | loop fusion | flops 1572864 | bytes 1572864 | tf_op jit(solution)/shard_map/concatenate | solution.py:308
Async XLA Ops:
  0.0 1.0 %copy-start.1 = (f32[64,32,32]{0,2,1:T(8,128)S(1)}, f32[64,32,32]{0,2,1:T(8,128)}, u32[]{:S(2)}) copy-start(f32[64,32,32]{0,2,1:T(8,128)} %param.5) | copy-start | bytes 786436
  1.2 6.5 %collective-permute-start.1 = (bf16[16,32,128]{2,1,0:T(8,128)(2,1)S(1)}, bf16[16,32,128]{2,1,0:T(8,128)(2,1)S(1)}, u32[]{:S(2)}, u32[]{:S(2)}) collective-permute-start(bf16[16,32,128]{2,1,0:T(8,128)(2,1)S(1)} %shard_map.55.refs_0_), channel_id=1, source_target_pairs={{0,2},{2,0},{1,3},{3,1},{4,6},{6,4},{5,7},{7,5},{8,10},{10,8},{9,1... | collective-permute-start | bytes 393224 | tf_op jit(solution)/shard_map/ppermute | solution.py:203
  4.2 4.0 %collective-permute-start = (bf16[16,32,128]{2,1,0:T(8,128)(2,1)S(1)}, bf16[16,32,128]{2,1,0:T(8,128)(2,1)S(1)}, u32[]{:S(2)}, u32[]{:S(2)}) collective-permute-start(bf16[16,32,128]{2,1,0:T(8,128)(2,1)S(1)} %shard_map.55.refs_0_), channel_id=1, source_target_pairs={{0,1},{1,0},{2,3},{3,2},{4,5},{5,4},{6,7},{7,6},{8,9},{9,8},{10,11... | collective-permute-start | bytes 393224 | tf_op jit(solution)/shard_map/ppermute | solution.py:203
  4.2 1.0 %copy-start.2 = (f32[9,64,64]{2,1,0:T(8,128)S(1)}, f32[9,64,64]{2,1,0:T(8,128)}, u32[]{:S(2)}) copy-start(f32[9,64,64]{2,1,0:T(8,128)} %first_ref.1) | copy-start | bytes 442372
  5.1 1.0 %copy-start.3 = (f32[9,64,64]{2,1,0:T(8,128)S(1)}, f32[9,64,64]{2,1,0:T(8,128)}, u32[]{:S(2)}) copy-start(f32[9,64,64]{2,1,0:T(8,128)} %second_ref.1) | copy-start | bytes 442372
  6.1 0.9 %copy-start.4 = (bf16[256,384]{1,0:T(8,128)(2,1)S(1)}, bf16[256,384]{1,0:T(8,128)(2,1)}, u32[]{:S(2)}) copy-start(bf16[256,384]{1,0:T(8,128)(2,1)} %embed_ref.1) | copy-start | bytes 589828
  7.7 1.5 %collective-permute-start.2 = (bf16[16,32,128]{2,1,0:T(8,128)(2,1)S(1)}, bf16[16,32,128]{2,1,0:T(8,128)(2,1)S(1)}, u32[]{:S(2)}, u32[]{:S(2)}) collective-permute-start(bf16[16,32,128]{2,1,0:T(8,128)(2,1)S(1)} %collective-permute-done.1.refs_2_), channel_id=1, source_target_pairs={{0,1},{1,0},{2,3},{3,2},{4,5},{5,4},{6,7},{7,6},{8,9},{9,8},{10,11... | collective-permute-start | bytes 393224 | tf_op jit(solution)/shard_map/ppermute | solution.py:203
  9.2 6.6 %collective-permute-start.3 = (bf16[1,128,128]{2,1,0:T(8,128)(2,1)S(1)}, bf16[1,128,128]{2,1,0:T(8,128)(2,1)S(1)}, u32[]{:S(2)}, u32[]{:S(2)}) collective-permute-start(bf16[1,128,128]{2,1,0:T(8,128)(2,1)S(1)} %get-tuple-element.29), channel_id=1, source_target_pairs={{0,4},{4,8},{8,12},{12,0},{1,5},{5,9},{9,13},{13,1},{2,6},{6,10},{... | collective-permute-start | bytes 98312 | tf_op jit(solution)/shard_map/ppermute | solution.py:203
  10.9 5.0 %collective-permute-start.4 = (bf16[1,128,128]{2,1,0:T(8,128)(2,1)S(1)}, bf16[1,128,128]{2,1,0:T(8,128)(2,1)S(1)}, u32[]{:S(2)}, u32[]{:S(2)}) collective-permute-start(bf16[1,128,128]{2,1,0:T(8,128)(2,1)S(1)} %get-tuple-element.30), channel_id=1, source_target_pairs={{0,12},{4,0},{8,4},{12,8},{1,13},{5,1},{9,5},{13,9},{2,14},{6,2},{... | collective-permute-start | bytes 98312 | tf_op jit(solution)/shard_map/ppermute | solution.py:203
  13.1 4.0 %copy-start = (bf16[1024,4096]{1,0:T(8,128)(2,1)S(1)}, bf16[1024,4096]{1,0:T(8,128)(2,1)}, u32[]{:S(2)}) copy-start(bf16[1024,4096]{1,0:T(8,128)(2,1)} %mixing_ref.5) | copy-start | bytes 25165828
  18.7 12.6 %collective-permute-start.8 = (bf16[96,2048]{1,0:T(8,128)(2,1)S(1)}, bf16[96,2048]{1,0:T(8,128)(2,1)S(1)}, u32[]{:S(2)}, u32[]{:S(2)}) collective-permute-start(bf16[96,2048]{1,0:T(8,128)(2,1)S(1)} %get-tuple-element.40), channel_id=1, source_target_pairs={{0,12},{4,0},{8,4},{12,8},{1,13},{5,1},{9,5},{13,9},{2,14},{6,2},{... | collective-permute-start | bytes 1179656 | tf_op jit(solution)/shard_map/ppermute | solution.py:203
  21.6 18.0 %collective-permute-start.5 = (bf16[96,2048]{1,0:T(8,128)(2,1)S(1)}, bf16[96,2048]{1,0:T(8,128)(2,1)S(1)}, u32[]{:S(2)}, u32[]{:S(2)}) collective-permute-start(bf16[96,2048]{1,0:T(8,128)(2,1)S(1)} %get-tuple-element.37), channel_id=1, source_target_pairs={{0,12},{4,0},{8,4},{12,8},{1,13},{5,1},{9,5},{13,9},{2,14},{6,2},{... | collective-permute-start | bytes 1179656 | tf_op jit(solution)/shard_map/ppermute | solution.py:203
  32.6 15.5 %collective-permute-start.9 = (bf16[96,2048]{1,0:T(8,128)(2,1)S(1)}, bf16[96,2048]{1,0:T(8,128)(2,1)S(1)}, u32[]{:S(2)}, u32[]{:S(2)}) collective-permute-start(bf16[96,2048]{1,0:T(8,128)(2,1)S(1)} %get-tuple-element.41), channel_id=1, source_target_pairs={{0,12},{4,0},{8,4},{12,8},{1,13},{5,1},{9,5},{13,9},{2,14},{6,2},{... | collective-permute-start | bytes 1179656 | tf_op jit(solution)/shard_map/ppermute | solution.py:203
  41.0 15.5 %collective-permute-start.6 = (bf16[96,2048]{1,0:T(8,128)(2,1)S(1)}, bf16[96,2048]{1,0:T(8,128)(2,1)S(1)}, u32[]{:S(2)}, u32[]{:S(2)}) collective-permute-start(bf16[96,2048]{1,0:T(8,128)(2,1)S(1)} %get-tuple-element.38), channel_id=1, source_target_pairs={{0,12},{4,0},{8,4},{12,8},{1,13},{5,1},{9,5},{13,9},{2,14},{6,2},{... | collective-permute-start | bytes 1179656 | tf_op jit(solution)/shard_map/ppermute | solution.py:203
  48.1 16.8 %collective-permute-start.10 = (bf16[96,2048]{1,0:T(8,128)(2,1)S(1)}, bf16[96,2048]{1,0:T(8,128)(2,1)S(1)}, u32[]{:S(2)}, u32[]{:S(2)}) collective-permute-start(bf16[96,2048]{1,0:T(8,128)(2,1)S(1)} %add_convert_fusion), channel_id=1, source_target_pairs={{0,12},{4,0},{8,4},{12,8},{1,13},{5,1},{9,5},{13,9},{2,14},{6,2},{... | collective-permute-start | bytes 1179656 | tf_op jit(solution)/shard_map/ppermute | solution.py:203
  56.6 15.2 %collective-permute-start.7 = (bf16[96,2048]{1,0:T(8,128)(2,1)S(1)}, bf16[96,2048]{1,0:T(8,128)(2,1)S(1)}, u32[]{:S(2)}, u32[]{:S(2)}) collective-permute-start(bf16[96,2048]{1,0:T(8,128)(2,1)S(1)} %add_convert_fusion.1), channel_id=1, source_target_pairs={{0,12},{4,0},{8,4},{12,8},{1,13},{5,1},{9,5},{13,9},{2,14},{6,2},{... | collective-permute-start | bytes 1179656 | tf_op jit(solution)/shard_map/ppermute | solution.py:203

commit v10 on v8

--- a/solution.py
+++ b/solution.py
@@ -54,8 +54,7 @@
 def weights_kernel(first_ref, second_ref, embed_ref, taps_one_ref, taps_two_ref, embed_out_ref, scratch):
     for source, target in ((first_ref, taps_one_ref), (second_ref, taps_two_ref)):
         upper, lower = split_two(spread_taps(source))
-        target[0] = upper
-        target[1] = lower
+        target[...] = jnp.concatenate([upper, lower, upper], axis=0)
     chans = embed_ref.shape[0] // 4
     embed = embed_ref.shape[1]
     count = lax.axis_size("tok")
@@ -89,14 +88,11 @@
 def add_lat_taps(products, lat):
     wide = products.shape[1] // 3
     count = products.shape[0]
-    row = lax.broadcasted_iota(jnp.int32, (count, wide), 0) % lat
-    below = pltpu.roll(products[:, :wide], 1, axis=0)
-    above = pltpu.roll(products[:, 2 * wide :], count - 1, axis=0)
-    return (
-        products[:, wide : 2 * wide]
-        + jnp.where(row == 0, 0.0, below)
-        + jnp.where(row == lat - 1, 0.0, above)
-    )
+    row = lax.broadcasted_iota(jnp.int32, (1, lat, wide), 1)
+    below = pltpu.roll(products[:, :wide], 1, axis=0).reshape(-1, lat, wide)
+    above = pltpu.roll(products[:, 2 * wide :], count - 1, axis=0).reshape(-1, lat, wide)
+    here = products[:, wide : 2 * wide].reshape(-1, lat, wide)
+    return here + jnp.where(row == 0, 0.0, below) + jnp.where(row == lat - 1, 0.0, above)
 
 
 def gelu(value):
@@ -109,15 +105,15 @@
 
 def first_conv(field_at, pairs, taps_ref, lat):
     rows = window(field_at, pairs)
-    products = dot(rows, taps_ref[0]) + dot(rows, taps_ref[1])
-    parts = split_two(gelu(add_lat_taps(products, lat)))
-    return [part.reshape(len(pairs), lat, part.shape[1]) for part in parts]
+    products = dot(jnp.concatenate([rows, rows], axis=-1), taps_ref[: 2 * rows.shape[1]])
+    return split_two(gelu(add_lat_taps(products, lat)))
 
 
 def second_conv(upper_at, lower_at, pairs, taps_ref, lat):
     upper, lower = window(upper_at, pairs), window(lower_at, pairs)
-    products = dot(upper, taps_ref[0]) + dot(upper, taps_ref[1]) + dot(lower, taps_ref[0])
-    return add_lat_taps(products, lat).astype(jnp.bfloat16).astype(jnp.float32)
+    products = dot(jnp.concatenate([upper, upper, lower], axis=-1), taps_ref[...])
+    rounded = add_lat_taps(products, lat).astype(jnp.bfloat16).astype(jnp.float32)
+    return rounded.reshape(-1, rounded.shape[2])
 
 
 def embed_patches(two_ref, embed_ref):
@@ -221,7 +217,7 @@
     packed = call(
         pack_kernel, shape((pairs, lat, wide)), (jnp.transpose(weather, (1, 2, 0)),), moved=weather.size * 10
     )
-    taps = shape((2, 4 * chans, 6 * chans))
+    taps = shape((12 * chans, 6 * chans))
     weights = call(
         weights_kernel,
         (taps, taps, shape((embed, 4 * chans))),
@@ -261,14 +257,13 @@
     )
 
 
-def sent_kernel(tokens_ref, mixing_ref, *sent_refs):
-    rows, width = sent_refs[0].shape
+def sent_kernel(first, tokens_ref, mixing_ref, sent_ref):
+    rows, width = sent_ref.shape
     step = STEP if width % STEP == 0 else width
     tokens = tokens_ref[:rows]
-    for piece, sent_ref in enumerate(sent_refs):
-        for at in range(0, width, step):
-            product = dot(tokens, mixing_ref[:, pl.ds(piece * width + at, step)])
-            sent_ref[:, pl.ds(at, step)] = product.astype(sent_ref.dtype)
+    for at in range(0, width, step):
+        product = dot(tokens, mixing_ref[:, pl.ds(first + at, step)])
+        sent_ref[:, pl.ds(at, step)] = product.astype(sent_ref.dtype)
 
 
 def hop_kernel(first, arrived_ref, tokens_ref, mixing_ref, sent_ref, kept_ref):
@@ -288,7 +283,9 @@
     rows = embed // count
     width = token_mixing.shape[1] // pieces
     sent = jax.ShapeDtypeStruct((rows, width), jnp.bfloat16)
-    travelling = list(call(sent_kernel, [sent] * pieces, (tokens, token_mixing)))
+    travelling = [
+        call(functools.partial(sent_kernel, piece * width), sent, (tokens, token_mixing)) for piece in range(pieces)
+    ]
     kept = [None] * pieces
     for step in range(1, count):
         for piece in range(pieces):

time: 73.1 us -> 72.1 us (0.986)
  waiting for transfers between devices: 15 us -> 13.4 us
    ppermute x17, waiting for transfers between devices: 15 us -> 13.4 us  [turned(): lax.ppermute(value, axis, [(i, (i + away) % count) for i in range(count)])]
    pallas_call x10 -> x13, Pallas kernels: 9.32 us -> 9.71 us  [call(): pl.pallas_call(kernel, out_shape=out_shape, in_specs=[pl.BlockSpec(memory...]
  transfers between devices with their start and end apart: 17 -> 17, of which waited for: 5 -> 5; matrix products, arithmetic and copies ran while one was open for 1% -> 1% of each run, Pallas kernels for 9% -> 11%
where the time goes in v10:
time: 72.1 us; the launch traced here: 71.8 us
  starting transfers between devices  43.2 us (60%)
  waiting for transfers between devices  13.4 us (19%)
  Pallas kernels  9.71 us (13%)
  local copies, waits for them, and re-layouts  3.89 us (5%)
  other arithmetic  1.5 us (2%)
    ppermute x17, starting transfers between devices, turned(): lax.ppermute(value, axis, [(i, (i + away) % count) for i in range(count)])  43.2 us
    ppermute x17, waiting for transfers between devices, turned(): lax.ppermute(value, axis, [(i, (i + away) % count) for i in range(count)])  13.4 us
    pallas_call x13, Pallas kernels, call(): pl.pallas_call(kernel, out_shape=out_shape, in_specs=[pl.BlockSpec(memory...  9.71 us
    unnamed x10, local copies, waits for them, and re-layouts  3.89 us
  transfers between devices with their start and end apart: 17, of which 5 were waited for; matrix products, arithmetic and copies ran while one was open for 1% of the time, Pallas kernels for 11%

profile of v10, /device:TPU:0, one launch (start us, length us, event | category | flops | bytes accessed | tf_op | source)
XLA Modules:
  0.0 71.8 jit_solution(12002647646769526554)
XLA Ops:
  0.0 1.0 %copy-done.1 = f32[64,32,32]{0,2,1:T(8,128)S(1)} copy-done((f32[64,32,32]{0,2,1:T(8,128)S(1)}, f32[64,32,32]{0,2,1:T(8,128)}, u32[]{:S(2)}) %copy-start.1) | copy-done | bytes 262168
  1.0 0.1 shard_map.55.refs_0_
  1.2 3.0 %collective-permute-start.1 = (bf16[16,32,128]{2,1,0:T(8,128)(2,1)S(1)}, bf16[16,32,128]{2,1,0:T(8,128)(2,1)S(1)}, u32[]{:S(2)}, u32[]{:S(2)}) collective-permute-start(bf16[16,32,128]{2,1,0:T(8,128)(2,1)S(1)} %shard_map.55.refs_0_), channel_id=1, source_target_pairs={{0,2},{2,0},{1,3},{3,1},{4,6},{6,4},{5,7},{7,5},{8,10},{10,8},{9,1... | collective-permute-start | bytes 393224 | tf_op jit(solution)/shard_map/ppermute | solution.py:199
  4.2 1.0 %copy-done.2 = f32[9,64,64]{2,1,0:T(8,128)S(1)} copy-done((f32[9,64,64]{2,1,0:T(8,128)S(1)}, f32[9,64,64]{2,1,0:T(8,128)}, u32[]{:S(2)}) %copy-start.2) | copy-done | bytes 147480
  5.1 1.0 %copy-done.3 = f32[9,64,64]{2,1,0:T(8,128)S(1)} copy-done((f32[9,64,64]{2,1,0:T(8,128)S(1)}, f32[9,64,64]{2,1,0:T(8,128)}, u32[]{:S(2)}) %copy-start.3) | copy-done | bytes 147480
  6.1 0.9 %copy-done.4 = bf16[256,384]{1,0:T(8,128)(2,1)S(1)} copy-done((bf16[256,384]{1,0:T(8,128)(2,1)S(1)}, bf16[256,384]{1,0:T(8,128)(2,1)}, u32[]{:S(2)}) %copy-start.4) | copy-done | bytes 196632
  7.0 0.6 shard_map.56
  7.6 0.0 collective-permute-done.1.refs_2_
  7.7 0.5 collective-permute-start.2
  8.2 0.0 collective-permute-done.refs_1_
  8.2 1.0 %collective-permute-done.2.refs_3_ = bf16[16,32,128]{2,1,0:T(8,128)(2,1)S(1)} collective-permute-done((bf16[16,32,128]{2,1,0:T(8,128)(2,1)S(1)}, bf16[16,32,128]{2,1,0:T(8,128)(2,1)S(1)}, u32[]{:S(2)}, u32[]{:S(2)}) %collective-permute-start.2) | collective-permute-done | bytes 131104 | tf_op jit(solution)/shard_map/ppermute | solution.py:199
  9.2 0.1 shard_map.57
  9.2 1.7 %collective-permute-start.3 = (bf16[1,128,128]{2,1,0:T(8,128)(2,1)S(1)}, bf16[1,128,128]{2,1,0:T(8,128)(2,1)S(1)}, u32[]{:S(2)}, u32[]{:S(2)}) collective-permute-start(bf16[1,128,128]{2,1,0:T(8,128)(2,1)S(1)} %get-tuple-element.31), channel_id=1, source_target_pairs={{0,4},{4,8},{8,12},{12,0},{1,5},{5,9},{9,13},{13,1},{2,6},{6,10},{... | collective-permute-start | bytes 98312 | tf_op jit(solution)/shard_map/ppermute | solution.py:199
  10.9 2.2 %collective-permute-start.4 = (bf16[1,128,128]{2,1,0:T(8,128)(2,1)S(1)}, bf16[1,128,128]{2,1,0:T(8,128)(2,1)S(1)}, u32[]{:S(2)}, u32[]{:S(2)}) collective-permute-start(bf16[1,128,128]{2,1,0:T(8,128)(2,1)S(1)} %get-tuple-element.32), channel_id=1, source_target_pairs={{0,12},{4,0},{8,4},{12,8},{1,13},{5,1},{9,5},{13,9},{2,14},{6,2},{... | collective-permute-start | bytes 98312 | tf_op jit(solution)/shard_map/ppermute | solution.py:199
  13.1 2.7 %shard_map.58 = (bf16[384,768]{1,0:T(8,128)(2,1)S(1)}, bf16[4,128,128]{2,1,0:T(8,128)(2,1)S(1)}, bf16[4,128,128]{2,1,0:T(8,128)(2,1)S(1)}) custom-call(bf16[16,128,128]{2,1,0:T(8,128)(2,1)S(1)} %get-tuple-element.30.field_ref, bf16[768,384]{1,0:T(8,128)(2,1)S(1)} %get-tuple-element.33.taps_one_ref, bf16[768,384]{1,0:T(8,128)(2,1)S(1)} %get-tuple-element.34.taps_two_ref, ...), custom_call_target="tpu_custom_call" | custom-call | flops 1635778560 | bytes 524288 | tf_op jit(solution)/shard_map/pallas_call | solution.py:186
  15.9 0.0 collective-permute-done.3.before_ref
  15.9 0.0 collective-permute-done.4.after_ref
  15.9 1.3 %shard_map.59.tokens_ref = bf16[384,1024]{1,0:T(8,128)(2,1)S(1)} custom-call(bf16[16,128,128]{2,1,0:T(8,128)(2,1)S(1)} %get-tuple-element.30.field_ref, bf16[1,128,128]{2,1,0:T(8,128)(2,1)S(1)} %collective-permute-done.3.before_ref, bf16[1,128,128]{2,1,0:T(8,128)(2,1)S(1)} %collective-permute-done.4.after_ref, ...), custom_call_target="tpu_custom_call" | custom-call | flops 503316480 | bytes 524288 | tf_op jit(solution)/shard_map/pallas_call | solution.py:186
  17.2 0.5 shard_map.66
  17.7 3.0 %collective-permute-start.14 = (bf16[96,1024]{1,0:T(8,128)(2,1)S(1)}, bf16[96,1024]{1,0:T(8,128)(2,1)S(1)}, u32[]{:S(2)}, u32[]{:S(2)}) collective-permute-start(bf16[96,1024]{1,0:T(8,128)(2,1)S(1)} %shard_map.66), channel_id=1, source_target_pairs={{0,12},{4,0},{8,4},{12,8},{1,13},{5,1},{9,5},{13,9},{2,14},{6,2},{... | collective-permute-start | bytes 589832 | tf_op jit(solution)/shard_map/ppermute | solution.py:199
  20.7 0.5 shard_map.64
  21.1 0.1 collective-permute-start.11
  21.2 0.5 shard_map.60
  21.7 0.5 collective-permute-start.5
  22.2 0.5 shard_map.62
  22.7 1.5 %collective-permute-start.8 = (bf16[96,1024]{1,0:T(8,128)(2,1)S(1)}, bf16[96,1024]{1,0:T(8,128)(2,1)S(1)}, u32[]{:S(2)}, u32[]{:S(2)}) collective-permute-start(bf16[96,1024]{1,0:T(8,128)(2,1)S(1)} %shard_map.62), channel_id=1, source_target_pairs={{0,12},{4,0},{8,4},{12,8},{1,13},{5,1},{9,5},{13,9},{2,14},{6,2},{... | collective-permute-start | bytes 589832 | tf_op jit(solution)/shard_map/ppermute | solution.py:199
  24.2 1.8 %collective-permute-done.14.arrived_ref = bf16[96,1024]{1,0:T(8,128)(2,1)S(1)} collective-permute-done((bf16[96,1024]{1,0:T(8,128)(2,1)S(1)}, bf16[96,1024]{1,0:T(8,128)(2,1)S(1)}, u32[]{:S(2)}, u32[]{:S(2)}) %collective-permute-start.14) | collective-permute-done | bytes 196640 | tf_op jit(solution)/shard_map/ppermute | solution.py:199
  26.0 0.8 %shard_map.67 = (bf16[96,1024]{1,0:T(8,128)(2,1)S(1)}, f32[192,1024]{1,0:T(8,128)S(1)}) custom-call(bf16[96,1024]{1,0:T(8,128)(2,1)S(1)} %collective-permute-done.14.arrived_ref, bf16[384,1024]{1,0:T(8,128)(2,1)S(1)} %shard_map.59.tokens_ref, bf16[1024,4096]{1,0:T(8,128)(2,1)S(1)} %copy-done), custom_call_target="tpu_custom_call" | custom-call | tf_op jit(solution)/shard_map/pallas_call | solution.py:186
  26.8 4.3 %collective-permute-start.15 = (bf16[96,1024]{1,0:T(8,128)(2,1)S(1)}, bf16[96,1024]{1,0:T(8,128)(2,1)S(1)}, u32[]{:S(2)}, u32[]{:S(2)}) collective-permute-start(bf16[96,1024]{1,0:T(8,128)(2,1)S(1)} %get-tuple-element.45), channel_id=1, source_target_pairs={{0,12},{4,0},{8,4},{12,8},{1,13},{5,1},{9,5},{13,9},{2,14},{6,2},{... | collective-permute-start | bytes 589832 | tf_op jit(solution)/shard_map/ppermute | solution.py:199
  31.1 0.0 collective-permute-done.11.arrived_ref
  31.1 0.8 %shard_map.65 = (bf16[96,1024]{1,0:T(8,128)(2,1)S(1)}, f32[192,1024]{1,0:T(8,128)S(1)}) custom-call(bf16[96,1024]{1,0:T(8,128)(2,1)S(1)} %collective-permute-done.11.arrived_ref, bf16[384,1024]{1,0:T(8,128)(2,1)S(1)} %shard_map.59.tokens_ref, bf16[1024,4096]{1,0:T(8,128)(2,1)S(1)} %copy-done), custom_call_target="tpu_custom_call" | custom-call | tf_op jit(solution)/shard_map/pallas_call | solution.py:186
  31.9 3.4 %collective-permute-start.12 = (bf16[96,1024]{1,0:T(8,128)(2,1)S(1)}, bf16[96,1024]{1,0:T(8,128)(2,1)S(1)}, u32[]{:S(2)}, u32[]{:S(2)}) collective-permute-start(bf16[96,1024]{1,0:T(8,128)(2,1)S(1)} %get-tuple-element.43), channel_id=1, source_target_pairs={{0,12},{4,0},{8,4},{12,8},{1,13},{5,1},{9,5},{13,9},{2,14},{6,2},{... | collective-permute-start | bytes 589832 | tf_op jit(solution)/shard_map/ppermute | solution.py:199
  35.3 0.8 %shard_map.61 = (bf16[96,1024]{1,0:T(8,128)(2,1)S(1)}, f32[192,1024]{1,0:T(8,128)S(1)}) custom-call(bf16[96,1024]{1,0:T(8,128)(2,1)S(1)} %collective-permute-done.5.arrived_ref, bf16[384,1024]{1,0:T(8,128)(2,1)S(1)} %shard_map.59.tokens_ref, bf16[1024,4096]{1,0:T(8,128)(2,1)S(1)} %copy-done), custom_call_target="tpu_custom_call" | custom-call | tf_op jit(solution)/shard_map/pallas_call | solution.py:186
  36.1 3.4 %collective-permute-start.6 = (bf16[96,1024]{1,0:T(8,128)(2,1)S(1)}, bf16[96,1024]{1,0:T(8,128)(2,1)S(1)}, u32[]{:S(2)}, u32[]{:S(2)}) collective-permute-start(bf16[96,1024]{1,0:T(8,128)(2,1)S(1)} %get-tuple-element.39), channel_id=1, source_target_pairs={{0,12},{4,0},{8,4},{12,8},{1,13},{5,1},{9,5},{13,9},{2,14},{6,2},{... | collective-permute-start | bytes 589832 | tf_op jit(solution)/shard_map/ppermute | solution.py:199
  39.5 0.8 %shard_map.63 = (bf16[96,1024]{1,0:T(8,128)(2,1)S(1)}, f32[192,1024]{1,0:T(8,128)S(1)}) custom-call(bf16[96,1024]{1,0:T(8,128)(2,1)S(1)} %collective-permute-done.8.arrived_ref, bf16[384,1024]{1,0:T(8,128)(2,1)S(1)} %shard_map.59.tokens_ref, bf16[1024,4096]{1,0:T(8,128)(2,1)S(1)} %copy-done), custom_call_target="tpu_custom_call" | custom-call | tf_op jit(solution)/shard_map/pallas_call | solution.py:186
  40.3 3.4 %collective-permute-start.9 = (bf16[96,1024]{1,0:T(8,128)(2,1)S(1)}, bf16[96,1024]{1,0:T(8,128)(2,1)S(1)}, u32[]{:S(2)}, u32[]{:S(2)}) collective-permute-start(bf16[96,1024]{1,0:T(8,128)(2,1)S(1)} %get-tuple-element.41), channel_id=1, source_target_pairs={{0,12},{4,0},{8,4},{12,8},{1,13},{5,1},{9,5},{13,9},{2,14},{6,2},{... | collective-permute-start | bytes 589832 | tf_op jit(solution)/shard_map/ppermute | solution.py:199
  43.8 3.4 %collective-permute-start.16 = (bf16[96,1024]{1,0:T(8,128)(2,1)S(1)}, bf16[96,1024]{1,0:T(8,128)(2,1)S(1)}, u32[]{:S(2)}, u32[]{:S(2)}) collective-permute-start(bf16[96,1024]{1,0:T(8,128)(2,1)S(1)} %add_convert_fusion), channel_id=1, source_target_pairs={{0,12},{4,0},{8,4},{12,8},{1,13},{5,1},{9,5},{13,9},{2,14},{6,2},{... | collective-permute-start | bytes 589832 | tf_op jit(solution)/shard_map/ppermute | solution.py:199
  47.3 4.2 %collective-permute-start.13 = (bf16[96,1024]{1,0:T(8,128)(2,1)S(1)}, bf16[96,1024]{1,0:T(8,128)(2,1)S(1)}, u32[]{:S(2)}, u32[]{:S(2)}) collective-permute-start(bf16[96,1024]{1,0:T(8,128)(2,1)S(1)} %add_convert_fusion.1), channel_id=1, source_target_pairs={{0,12},{4,0},{8,4},{12,8},{1,13},{5,1},{9,5},{13,9},{2,14},{6,2},{... | collective-permute-start | bytes 589832 | tf_op jit(solution)/shard_map/ppermute | solution.py:199
  51.5 4.2 %collective-permute-start.7 = (bf16[96,1024]{1,0:T(8,128)(2,1)S(1)}, bf16[96,1024]{1,0:T(8,128)(2,1)S(1)}, u32[]{:S(2)}, u32[]{:S(2)}) collective-permute-start(bf16[96,1024]{1,0:T(8,128)(2,1)S(1)} %add_convert_fusion.3), channel_id=1, source_target_pairs={{0,12},{4,0},{8,4},{12,8},{1,13},{5,1},{9,5},{13,9},{2,14},{6,2},{... | collective-permute-start | bytes 589832 | tf_op jit(solution)/shard_map/ppermute | solution.py:199
  55.7 4.2 %collective-permute-start.10 = (bf16[96,1024]{1,0:T(8,128)(2,1)S(1)}, bf16[96,1024]{1,0:T(8,128)(2,1)S(1)}, u32[]{:S(2)}, u32[]{:S(2)}) collective-permute-start(bf16[96,1024]{1,0:T(8,128)(2,1)S(1)} %add_convert_fusion.2), channel_id=1, source_target_pairs={{0,12},{4,0},{8,4},{12,8},{1,13},{5,1},{9,5},{13,9},{2,14},{6,2},{... | collective-permute-start | bytes 589832 | tf_op jit(solution)/shard_map/ppermute | solution.py:199
  59.9 0.1 multiply_convert_fusion
  60.0 3.9 %collective-permute-done.13 = bf16[96,1024]{1,0:T(8,128)(2,1)S(1)} collective-permute-done((bf16[96,1024]{1,0:T(8,128)(2,1)S(1)}, bf16[96,1024]{1,0:T(8,128)(2,1)S(1)}, u32[]{:S(2)}, u32[]{:S(2)}) %collective-permute-start.13) | collective-permute-done | bytes 196640 | tf_op jit(solution)/shard_map/ppermute | solution.py:199
  63.9 0.1 multiply_convert_fusion.1
  64.0 4.1 %collective-permute-done.7 = bf16[96,1024]{1,0:T(8,128)(2,1)S(1)} collective-permute-done((bf16[96,1024]{1,0:T(8,128)(2,1)S(1)}, bf16[96,1024]{1,0:T(8,128)(2,1)S(1)}, u32[]{:S(2)}, u32[]{:S(2)}) %collective-permute-start.7) | collective-permute-done | bytes 196640 | tf_op jit(solution)/shard_map/ppermute | solution.py:199
  68.1 0.1 multiply_convert_fusion.3
  68.2 2.5 %collective-permute-done.10 = bf16[96,1024]{1,0:T(8,128)(2,1)S(1)} collective-permute-done((bf16[96,1024]{1,0:T(8,128)(2,1)S(1)}, bf16[96,1024]{1,0:T(8,128)(2,1)S(1)}, u32[]{:S(2)}, u32[]{:S(2)}) %collective-permute-start.10) | collective-permute-done | bytes 196640 | tf_op jit(solution)/shard_map/ppermute | solution.py:199
  70.8 0.1 multiply_convert_fusion.2
  70.9 0.9 %pad_maximum_fusion = bf16[96,4096]{1,0:T(8,128)(2,1)} fusion(bf16[96,1024]{1,0:T(8,128)(2,1)S(1)} %multiply_convert_fusion, bf16[96,1024]{1,0:T(8,128)(2,1)S(1)} %multiply_convert_fusion.1, bf16[96,1024]{1,0:T(8,128)(2,1)S(1)} %multiply_convert_fusion.2, bf16[96,1024]{1,0:T(8,128)(2,1)S(1)} %multiply_convert_fusion.3), kind=kLoop, calls=%fused_computation | loop fusion | flops 3145728 | bytes 1572864 | tf_op jit(solution)/shard_map/concatenate | solution.py:305
  (18 shorter events, 0.2 us)
Async XLA Ops:
  0.0 1.0 %copy-start.1 = (f32[64,32,32]{0,2,1:T(8,128)S(1)}, f32[64,32,32]{0,2,1:T(8,128)}, u32[]{:S(2)}) copy-start(f32[64,32,32]{0,2,1:T(8,128)} %param.5) | copy-start | bytes 786436
  1.2 6.5 %collective-permute-start.1 = (bf16[16,32,128]{2,1,0:T(8,128)(2,1)S(1)}, bf16[16,32,128]{2,1,0:T(8,128)(2,1)S(1)}, u32[]{:S(2)}, u32[]{:S(2)}) collective-permute-start(bf16[16,32,128]{2,1,0:T(8,128)(2,1)S(1)} %shard_map.55.refs_0_), channel_id=1, source_target_pairs={{0,2},{2,0},{1,3},{3,1},{4,6},{6,4},{5,7},{7,5},{8,10},{10,8},{9,1... | collective-permute-start | bytes 393224 | tf_op jit(solution)/shard_map/ppermute | solution.py:199
  4.2 4.0 %collective-permute-start = (bf16[16,32,128]{2,1,0:T(8,128)(2,1)S(1)}, bf16[16,32,128]{2,1,0:T(8,128)(2,1)S(1)}, u32[]{:S(2)}, u32[]{:S(2)}) collective-permute-start(bf16[16,32,128]{2,1,0:T(8,128)(2,1)S(1)} %shard_map.55.refs_0_), channel_id=1, source_target_pairs={{0,1},{1,0},{2,3},{3,2},{4,5},{5,4},{6,7},{7,6},{8,9},{9,8},{10,11... | collective-permute-start | bytes 393224 | tf_op jit(solution)/shard_map/ppermute | solution.py:199
  4.2 1.0 %copy-start.2 = (f32[9,64,64]{2,1,0:T(8,128)S(1)}, f32[9,64,64]{2,1,0:T(8,128)}, u32[]{:S(2)}) copy-start(f32[9,64,64]{2,1,0:T(8,128)} %first_ref.1) | copy-start | bytes 442372
  5.1 1.0 %copy-start.3 = (f32[9,64,64]{2,1,0:T(8,128)S(1)}, f32[9,64,64]{2,1,0:T(8,128)}, u32[]{:S(2)}) copy-start(f32[9,64,64]{2,1,0:T(8,128)} %second_ref.1) | copy-start | bytes 442372
  6.1 0.9 %copy-start.4 = (bf16[256,384]{1,0:T(8,128)(2,1)S(1)}, bf16[256,384]{1,0:T(8,128)(2,1)}, u32[]{:S(2)}) copy-start(bf16[256,384]{1,0:T(8,128)(2,1)} %embed_ref.1) | copy-start | bytes 589828
  7.7 1.5 %collective-permute-start.2 = (bf16[16,32,128]{2,1,0:T(8,128)(2,1)S(1)}, bf16[16,32,128]{2,1,0:T(8,128)(2,1)S(1)}, u32[]{:S(2)}, u32[]{:S(2)}) collective-permute-start(bf16[16,32,128]{2,1,0:T(8,128)(2,1)S(1)} %collective-permute-done.1.refs_2_), channel_id=1, source_target_pairs={{0,1},{1,0},{2,3},{3,2},{4,5},{5,4},{6,7},{7,6},{8,9},{9,8},{10,11... | collective-permute-start | bytes 393224 | tf_op jit(solution)/shard_map/ppermute | solution.py:199
  9.2 6.6 %collective-permute-start.3 = (bf16[1,128,128]{2,1,0:T(8,128)(2,1)S(1)}, bf16[1,128,128]{2,1,0:T(8,128)(2,1)S(1)}, u32[]{:S(2)}, u32[]{:S(2)}) collective-permute-start(bf16[1,128,128]{2,1,0:T(8,128)(2,1)S(1)} %get-tuple-element.31), channel_id=1, source_target_pairs={{0,4},{4,8},{8,12},{12,0},{1,5},{5,9},{9,13},{13,1},{2,6},{6,10},{... | collective-permute-start | bytes 98312 | tf_op jit(solution)/shard_map/ppermute | solution.py:199
  10.9 4.9 %collective-permute-start.4 = (bf16[1,128,128]{2,1,0:T(8,128)(2,1)S(1)}, bf16[1,128,128]{2,1,0:T(8,128)(2,1)S(1)}, u32[]{:S(2)}, u32[]{:S(2)}) collective-permute-start(bf16[1,128,128]{2,1,0:T(8,128)(2,1)S(1)} %get-tuple-element.32), channel_id=1, source_target_pairs={{0,12},{4,0},{8,4},{12,8},{1,13},{5,1},{9,5},{13,9},{2,14},{6,2},{... | collective-permute-start | bytes 98312 | tf_op jit(solution)/shard_map/ppermute | solution.py:199
  13.1 4.0 %copy-start = (bf16[1024,4096]{1,0:T(8,128)(2,1)S(1)}, bf16[1024,4096]{1,0:T(8,128)(2,1)}, u32[]{:S(2)}) copy-start(bf16[1024,4096]{1,0:T(8,128)(2,1)} %mixing_ref.15) | copy-start | bytes 25165828
  17.7 8.4 %collective-permute-start.14 = (bf16[96,1024]{1,0:T(8,128)(2,1)S(1)}, bf16[96,1024]{1,0:T(8,128)(2,1)S(1)}, u32[]{:S(2)}, u32[]{:S(2)}) collective-permute-start(bf16[96,1024]{1,0:T(8,128)(2,1)S(1)} %shard_map.66), channel_id=1, source_target_pairs={{0,12},{4,0},{8,4},{12,8},{1,13},{5,1},{9,5},{13,9},{2,14},{6,2},{... | collective-permute-start | bytes 589832 | tf_op jit(solution)/shard_map/ppermute | solution.py:199
  21.1 10.0 %collective-permute-start.11 = (bf16[96,1024]{1,0:T(8,128)(2,1)S(1)}, bf16[96,1024]{1,0:T(8,128)(2,1)S(1)}, u32[]{:S(2)}, u32[]{:S(2)}) collective-permute-start(bf16[96,1024]{1,0:T(8,128)(2,1)S(1)} %shard_map.64), channel_id=1, source_target_pairs={{0,12},{4,0},{8,4},{12,8},{1,13},{5,1},{9,5},{13,9},{2,14},{6,2},{... | collective-permute-start | bytes 589832 | tf_op jit(solution)/shard_map/ppermute | solution.py:199
  21.7 13.6 %collective-permute-start.5 = (bf16[96,1024]{1,0:T(8,128)(2,1)S(1)}, bf16[96,1024]{1,0:T(8,128)(2,1)S(1)}, u32[]{:S(2)}, u32[]{:S(2)}) collective-permute-start(bf16[96,1024]{1,0:T(8,128)(2,1)S(1)} %shard_map.60), channel_id=1, source_target_pairs={{0,12},{4,0},{8,4},{12,8},{1,13},{5,1},{9,5},{13,9},{2,14},{6,2},{... | collective-permute-start | bytes 589832 | tf_op jit(solution)/shard_map/ppermute | solution.py:199
  22.7 16.9 %collective-permute-start.8 = (bf16[96,1024]{1,0:T(8,128)(2,1)S(1)}, bf16[96,1024]{1,0:T(8,128)(2,1)S(1)}, u32[]{:S(2)}, u32[]{:S(2)}) collective-permute-start(bf16[96,1024]{1,0:T(8,128)(2,1)S(1)} %shard_map.62), channel_id=1, source_target_pairs={{0,12},{4,0},{8,4},{12,8},{1,13},{5,1},{9,5},{13,9},{2,14},{6,2},{... | collective-permute-start | bytes 589832 | tf_op jit(solution)/shard_map/ppermute | solution.py:199
  26.8 17.0 %collective-permute-start.15 = (bf16[96,1024]{1,0:T(8,128)(2,1)S(1)}, bf16[96,1024]{1,0:T(8,128)(2,1)S(1)}, u32[]{:S(2)}, u32[]{:S(2)}) collective-permute-start(bf16[96,1024]{1,0:T(8,128)(2,1)S(1)} %get-tuple-element.45), channel_id=1, source_target_pairs={{0,12},{4,0},{8,4},{12,8},{1,13},{5,1},{9,5},{13,9},{2,14},{6,2},{... | collective-permute-start | bytes 589832 | tf_op jit(solution)/shard_map/ppermute | solution.py:199
  31.9 15.3 %collective-permute-start.12 = (bf16[96,1024]{1,0:T(8,128)(2,1)S(1)}, bf16[96,1024]{1,0:T(8,128)(2,1)S(1)}, u32[]{:S(2)}, u32[]{:S(2)}) collective-permute-start(bf16[96,1024]{1,0:T(8,128)(2,1)S(1)} %get-tuple-element.43), channel_id=1, source_target_pairs={{0,12},{4,0},{8,4},{12,8},{1,13},{5,1},{9,5},{13,9},{2,14},{6,2},{... | collective-permute-start | bytes 589832 | tf_op jit(solution)/shard_map/ppermute | solution.py:199
  36.1 15.3 %collective-permute-start.6 = (bf16[96,1024]{1,0:T(8,128)(2,1)S(1)}, bf16[96,1024]{1,0:T(8,128)(2,1)S(1)}, u32[]{:S(2)}, u32[]{:S(2)}) collective-permute-start(bf16[96,1024]{1,0:T(8,128)(2,1)S(1)} %get-tuple-element.39), channel_id=1, source_target_pairs={{0,12},{4,0},{8,4},{12,8},{1,13},{5,1},{9,5},{13,9},{2,14},{6,2},{... | collective-permute-start | bytes 589832 | tf_op jit(solution)/shard_map/ppermute | solution.py:199
  40.3 15.3 %collective-permute-start.9 = (bf16[96,1024]{1,0:T(8,128)(2,1)S(1)}, bf16[96,1024]{1,0:T(8,128)(2,1)S(1)}, u32[]{:S(2)}, u32[]{:S(2)}) collective-permute-start(bf16[96,1024]{1,0:T(8,128)(2,1)S(1)} %get-tuple-element.41), channel_id=1, source_target_pairs={{0,12},{4,0},{8,4},{12,8},{1,13},{5,1},{9,5},{13,9},{2,14},{6,2},{... | collective-permute-start | bytes 589832 | tf_op jit(solution)/shard_map/ppermute | solution.py:199
  43.8 16.1 %collective-permute-start.16 = (bf16[96,1024]{1,0:T(8,128)(2,1)S(1)}, bf16[96,1024]{1,0:T(8,128)(2,1)S(1)}, u32[]{:S(2)}, u32[]{:S(2)}) collective-permute-start(bf16[96,1024]{1,0:T(8,128)(2,1)S(1)} %add_convert_fusion), channel_id=1, source_target_pairs={{0,12},{4,0},{8,4},{12,8},{1,13},{5,1},{9,5},{13,9},{2,14},{6,2},{... | collective-permute-start | bytes 589832 | tf_op jit(solution)/shard_map/ppermute | solution.py:199
  47.3 16.6 %collective-permute-start.13 = (bf16[96,1024]{1,0:T(8,128)(2,1)S(1)}, bf16[96,1024]{1,0:T(8,128)(2,1)S(1)}, u32[]{:S(2)}, u32[]{:S(2)}) collective-permute-start(bf16[96,1024]{1,0:T(8,128)(2,1)S(1)} %add_convert_fusion.1), channel_id=1, source_target_pairs={{0,12},{4,0},{8,4},{12,8},{1,13},{5,1},{9,5},{13,9},{2,14},{6,2},{... | collective-permute-start | bytes 589832 | tf_op jit(solution)/shard_map/ppermute | solution.py:199
  51.5 16.6 %collective-permute-start.7 = (bf16[96,1024]{1,0:T(8,128)(2,1)S(1)}, bf16[96,1024]{1,0:T(8,128)(2,1)S(1)}, u32[]{:S(2)}, u32[]{:S(2)}) collective-permute-start(bf16[96,1024]{1,0:T(8,128)(2,1)S(1)} %add_convert_fusion.3), channel_id=1, source_target_pairs={{0,12},{4,0},{8,4},{12,8},{1,13},{5,1},{9,5},{13,9},{2,14},{6,2},{... | collective-permute-start | bytes 589832 | tf_op jit(solution)/shard_map/ppermute | solution.py:199
  55.7 15.1 %collective-permute-start.10 = (bf16[96,1024]{1,0:T(8,128)(2,1)S(1)}, bf16[96,1024]{1,0:T(8,128)(2,1)S(1)}, u32[]{:S(2)}, u32[]{:S(2)}) collective-permute-start(bf16[96,1024]{1,0:T(8,128)(2,1)S(1)} %add_convert_fusion.2), channel_id=1, source_target_pairs={{0,12},{4,0},{8,4},{12,8},{1,13},{5,1},{9,5},{13,9},{2,14},{6,2},{... | collective-permute-start | bytes 589832 | tf_op jit(solution)/shard_map/ppermute | solution.py:199

commit v11 on v10

--- a/solution.py
+++ b/solution.py
@@ -11,7 +11,7 @@
 STEP = 256
 LANES = 128
 VMEM_BYTES = 24 * 1024 * 1024
-ROWS_AT_ONCE = 1024
+ROWS_AT_ONCE = 512
 
 
 def pack_kernel(field_ref, packed_ref):
@@ -67,14 +67,6 @@
         embed_out_ref[pl.ds(first, LANES), :] = rows.astype(embed_out_ref.dtype)
 
 
-def pairs_at_once(pairs, lat):
-    best = 1
-    for size in range(1, pairs + 1):
-        if pairs % size == 0 and size * lat <= ROWS_AT_ONCE:
-            best = size
-    return best
-
-
 def window(pair_at, pairs):
     rows = []
     for pair in pairs:
@@ -103,17 +95,20 @@
     return jnp.dot(left, right, preferred_element_type=jnp.float32)
 
 
-def first_conv(field_at, pairs, taps_ref, lat):
-    rows = window(field_at, pairs)
-    products = dot(jnp.concatenate([rows, rows], axis=-1), taps_ref[: 2 * rows.shape[1]])
-    return split_two(gelu(add_lat_taps(products, lat)))
-
-
-def second_conv(upper_at, lower_at, pairs, taps_ref, lat):
-    upper, lower = window(upper_at, pairs), window(lower_at, pairs)
-    products = dot(jnp.concatenate([upper, upper, lower], axis=-1), taps_ref[...])
+def first_conv(rows, taps, lat):
+    return gelu(add_lat_taps(dot(jnp.concatenate([rows, rows], axis=-1), taps), lat))
+
+
+def second_conv(upper, lower, taps, lat):
+    products = dot(jnp.concatenate([upper, upper, lower], axis=-1), taps)
     rounded = add_lat_taps(products, lat).astype(jnp.bfloat16).astype(jnp.float32)
     return rounded.reshape(-1, rounded.shape[2])
+
+
+def reordered(taps_ref, parts, order):
+    chans = taps_ref.shape[0] // 12
+    rows = [taps_ref[pl.ds((4 * part + at) * chans, chans), :] for part in range(parts) for at in order]
+    return jnp.concatenate(rows, axis=0)
 
 
 def embed_patches(two_ref, embed_ref):
@@ -127,59 +122,67 @@
 
 
 def runs(first, last, lat):
-    size = pairs_at_once(last - first, lat)
-    return [list(range(at, at + size)) for at in range(first, last, size)]
+    count = -(-(last - first) * lat // max(ROWS_AT_ONCE, lat))
+    cuts = [first + (last - first) * at // count for at in range(count + 1)]
+    return [list(range(*cut)) for cut in zip(cuts[:-1], cuts[1:])]
+
+
+def turned_half(value):
+    turned_value = pltpu.roll(value.astype(jnp.float32), value.shape[1] // 2, axis=1)
+    return turned_value.astype(value.dtype)
 
 
 def inner_kernel(
     field_ref, taps_one_ref, taps_two_ref, embed_ref, tokens_ref, upper_edge_ref, lower_edge_ref, upper_ref, lower_ref, two_ref
 ):
     pairs, lat, wide = field_ref.shape
-    for run in runs(1, pairs - 1, lat):
-        upper, lower = first_conv(lambda pair: field_ref[pair], run, taps_one_ref, lat)
+    first_runs, second_runs = runs(0, pairs, lat), runs(1, pairs - 1, lat)
+
+    def field_at(pair):
+        return field_ref[min(max(pair, 0), pairs - 1)]
+
+    two_ref[pl.ds(0, lat), :] = jnp.zeros((lat, wide), jnp.float32)
+    two_ref[pl.ds((pairs - 1) * lat, lat), :] = jnp.zeros((lat, wide), jnp.float32)
+    for run in first_runs:
+        rows = window(field_at, run)
+        upper, lower = split_two(first_conv(rows, taps_one_ref[: 2 * rows.shape[1]], lat))
         upper_ref[pl.ds(run[0], len(run))] = upper
         lower_ref[pl.ds(run[0], len(run))] = lower
-    for inside, edge in ((upper_ref, upper_edge_ref), (lower_ref, lower_edge_ref)):
-        edge[pl.ds(0, 2)] = inside[pl.ds(1, 2)]
-        edge[pl.ds(2, 2)] = inside[pl.ds(pairs - 3, 2)]
-    for run in runs(2, pairs - 2, lat):
-        two = second_conv(lambda pair: upper_ref[pair], lambda pair: lower_ref[pair], run, taps_two_ref, lat)
-        two_ref[pl.ds((run[0] - 2) * lat, len(run) * lat), :] = two
+        while second_runs and (second_runs[0][-1] < run[-1]):
+            ready = second_runs.pop(0)
+            upper_rows = window(lambda pair: upper_ref[pair], ready)
+            lower_rows = window(lambda pair: lower_ref[pair], ready)
+            two = second_conv(upper_rows, lower_rows, taps_two_ref[...], lat)
+            two_ref[pl.ds(ready[0] * lat, len(ready) * lat), :] = two
+    lane = lax.broadcasted_iota(jnp.int32, (lat, wide), 1)
+    for hidden, edge in ((upper_ref, upper_edge_ref), (lower_ref, lower_edge_ref)):
+        edge[0] = jnp.where(lane < wide // 2, hidden[1], hidden[0])
+        edge[1] = turned_half(jnp.where(lane < wide // 2, hidden[pairs - 1], hidden[pairs - 2]))
     tokens_ref[...] = embed_patches(two_ref, embed_ref)
 
 
 def outer_kernel(
-    field_ref, before_ref, after_ref, upper_edge_ref, lower_edge_ref, taps_one_ref, taps_two_ref, embed_ref, inner_ref, tokens_ref, two_ref
+    field_ref, after_ref, before_ref, upper_edge_ref, lower_edge_ref, taps_one_ref, taps_two_ref, embed_ref, inner_ref, tokens_ref, two_ref
 ):
     pairs, lat, wide = field_ref.shape
-
-    def field_at(pair):
-        if pair < 0:
-            return before_ref[0]
-        if pair >= pairs:
-            return after_ref[0]
-        return field_ref[pair]
-
-    outermost = [-1, 0, pairs - 1, pairs]
-    next_inside = [1, 2, pairs - 3, pairs - 2]
-    upper, lower = first_conv(field_at, outermost, taps_one_ref, lat)
-
-    def hidden_at(found, edge_ref):
-        def at(pair):
-            if pair in outermost:
-                return found[outermost.index(pair)]
-            return edge_ref[next_inside.index(pair)]
-
-        return at
-
-    two_ref[...] = second_conv(
-        hidden_at(upper, upper_edge_ref), hidden_at(lower, lower_edge_ref), [0, 1, pairs - 2, pairs - 1], taps_two_ref, lat
-    )
+    left = jnp.concatenate([before_ref[0], field_ref[0]], axis=-1)
+    right = jnp.concatenate([field_ref[pairs - 1], after_ref[0]], axis=-1)
+    rows = jnp.concatenate([left, right], axis=0)
+    hidden = first_conv(rows, reordered(taps_one_ref, 2, (3, 0, 1, 2)), lat)
+    parts = []
+    for (at_left, at_right), edge in zip(
+        zip(split_two(hidden[0]), split_two(turned_half(hidden[1]))), (upper_edge_ref, lower_edge_ref)
+    ):
+        left = jnp.concatenate([at_left, edge[0]], axis=-1)
+        right = jnp.concatenate([edge[1], at_right], axis=-1)
+        parts.append(jnp.concatenate([left, right], axis=0))
+    two_ref[...] = second_conv(*parts, reordered(taps_two_ref, 3, (3, 0, 2, 1)), lat)
     outer = embed_patches(two_ref, embed_ref)
-    inner = inner_ref.shape[1]
-    tokens_ref[:, :lat] = outer[:, :lat]
-    tokens_ref[:, pl.ds(lat, inner)] = inner_ref[...]
-    tokens_ref[:, pl.ds(lat + inner, lat)] = outer[:, lat:]
+    column = lax.broadcasted_iota(jnp.int32, outer.shape, 1)
+    rest = inner_ref.shape[1] - lat
+    tokens_ref[...] = inner_ref[...]
+    tokens_ref[:, :lat] = jnp.where(column < lat // 2, outer, inner_ref[:, :lat])
+    tokens_ref[:, pl.ds(rest, lat)] = jnp.where(column < lat // 2, inner_ref[:, pl.ds(rest, lat)], outer)
 
 
 def call(kernel, out_shape, inputs, scratch=(), flops=0, moved=0):
@@ -234,25 +237,25 @@
         blocks,
         moved=packed.size * 4 * len(blocks),
     )
+    after = turned(low, "tok", -1)
     before = turned(high, "tok", 1)
-    after = turned(low, "tok", -1)
     work = 2 * lat * 4 * chans * 6 * chans * 5
-    held = shape((4, lat, wide))
+    held = shape((2, lat, wide))
     hidden = pltpu.VMEM((pairs, lat, wide), jnp.bfloat16)
     inner, upper_edge, lower_edge = call(
         inner_kernel,
-        (shape((embed, (pairs - 4) * lat // 2)), held, held),
+        (shape((embed, pairs * lat // 2)), held, held),
         (field, *weights),
-        scratch=[hidden, hidden, pltpu.VMEM(((pairs - 4) * lat, wide), jnp.float32)],
-        flops=work * (pairs - 3),
+        scratch=[hidden, hidden, pltpu.VMEM((pairs * lat, wide), jnp.float32)],
+        flops=work * (pairs - 1),
         moved=field.size * 2,
     )
     return call(
         outer_kernel,
         shape((embed, pairs * lat // 2)),
-        (field, before, after, upper_edge, lower_edge, *weights, inner),
-        scratch=[pltpu.VMEM((4 * lat, wide), jnp.float32)],
-        flops=work * 4,
+        (field, after, before, upper_edge, lower_edge, *weights, inner),
+        scratch=[pltpu.VMEM((2 * lat, wide), jnp.float32)],
+        flops=work * 2,
         moved=field.size * 2,
     )
 

time: 72.1 us -> 73.5 us (1.019)
  waiting for transfers between devices: 13.4 us -> 16.7 us
  starting transfers between devices: 43.2 us -> 41 us
    ppermute x17, waiting for transfers between devices: 13.4 us -> 16.7 us  [turned(): lax.ppermute(value, axis, [(i, (i + away) % count) for i in range(count)])]
    ppermute x17, starting transfers between devices: 43.2 us -> 41 us  [turned(): lax.ppermute(value, axis, [(i, (i + away) % count) for i in range(count)])]
  transfers between devices with their start and end apart: 17 -> 17, of which waited for: 5 -> 10; matrix products, arithmetic and copies ran while one was open for 1% -> 1% of each run, Pallas kernels for 11% -> 11%
where the time goes in v11:
time: 73.5 us; the launch traced here: 73.3 us
  starting transfers between devices  41 us (56%)
  waiting for transfers between devices  16.7 us (23%)
  Pallas kernels  10 us (14%)
  local copies, waits for them, and re-layouts  3.89 us (5%)
  other arithmetic  1.5 us (2%)
    ppermute x17, starting transfers between devices, turned(): lax.ppermute(value, axis, [(i, (i + away) % count) for i in range(count)])  41 us
    ppermute x17, waiting for transfers between devices, turned(): lax.ppermute(value, axis, [(i, (i + away) % count) for i in range(count)])  16.7 us
    pallas_call x13, Pallas kernels, call(): pl.pallas_call(kernel, out_shape=out_shape, in_specs=[pl.BlockSpec(memory...  10 us
    unnamed x10, local copies, waits for them, and re-layouts  3.89 us
  transfers between devices with their start and end apart: 17, of which 10 were waited for; matrix products, arithmetic and copies ran while one was open for 1% of the time, Pallas kernels for 11%

profile of v11, /device:TPU:0, one launch (start us, length us, event | category | flops | bytes accessed | tf_op | source)
XLA Modules:
  0.0 73.3 jit_solution(7276772162916573247)
XLA Ops:
  0.0 1.0 %copy-done.1 = f32[64,32,32]{0,2,1:T(8,128)S(1)} copy-done((f32[64,32,32]{0,2,1:T(8,128)S(1)}, f32[64,32,32]{0,2,1:T(8,128)}, u32[]{:S(2)}) %copy-start.1) | copy-done | bytes 262168
  1.0 0.1 shard_map.55.refs_0_
  1.2 3.0 %collective-permute-start.1 = (bf16[16,32,128]{2,1,0:T(8,128)(2,1)S(1)}, bf16[16,32,128]{2,1,0:T(8,128)(2,1)S(1)}, u32[]{:S(2)}, u32[]{:S(2)}) collective-permute-start(bf16[16,32,128]{2,1,0:T(8,128)(2,1)S(1)} %shard_map.55.refs_0_), channel_id=1, source_target_pairs={{0,2},{2,0},{1,3},{3,1},{4,6},{6,4},{5,7},{7,5},{8,10},{10,8},{9,1... | collective-permute-start | bytes 393224 | tf_op jit(solution)/shard_map/ppermute | solution.py:202
  4.2 1.0 %copy-done.2 = f32[9,64,64]{2,1,0:T(8,128)S(1)} copy-done((f32[9,64,64]{2,1,0:T(8,128)S(1)}, f32[9,64,64]{2,1,0:T(8,128)}, u32[]{:S(2)}) %copy-start.2) | copy-done | bytes 147480
  5.1 1.0 %copy-done.3 = f32[9,64,64]{2,1,0:T(8,128)S(1)} copy-done((f32[9,64,64]{2,1,0:T(8,128)S(1)}, f32[9,64,64]{2,1,0:T(8,128)}, u32[]{:S(2)}) %copy-start.3) | copy-done | bytes 147480
  6.1 0.9 %copy-done.4 = bf16[256,384]{1,0:T(8,128)(2,1)S(1)} copy-done((bf16[256,384]{1,0:T(8,128)(2,1)S(1)}, bf16[256,384]{1,0:T(8,128)(2,1)}, u32[]{:S(2)}) %copy-start.4) | copy-done | bytes 196632
  7.0 0.6 shard_map.56
  7.6 0.0 collective-permute-done.1.refs_2_
  7.7 0.5 collective-permute-start.2
  8.2 1.0 %collective-permute-done.2.refs_3_ = bf16[16,32,128]{2,1,0:T(8,128)(2,1)S(1)} collective-permute-done((bf16[16,32,128]{2,1,0:T(8,128)(2,1)S(1)}, bf16[16,32,128]{2,1,0:T(8,128)(2,1)S(1)}, u32[]{:S(2)}, u32[]{:S(2)}) %collective-permute-start.2) | collective-permute-done | bytes 131104 | tf_op jit(solution)/shard_map/ppermute | solution.py:202
  9.2 0.1 shard_map.57
  9.2 3.7 %collective-permute-start.3 = (bf16[1,128,128]{2,1,0:T(8,128)(2,1)S(1)}, bf16[1,128,128]{2,1,0:T(8,128)(2,1)S(1)}, u32[]{:S(2)}, u32[]{:S(2)}) collective-permute-start(bf16[1,128,128]{2,1,0:T(8,128)(2,1)S(1)} %get-tuple-element.31), channel_id=1, source_target_pairs={{0,12},{4,0},{8,4},{12,8},{1,13},{5,1},{9,5},{13,9},{2,14},{6,2},{... | collective-permute-start | bytes 98312 | tf_op jit(solution)/shard_map/ppermute | solution.py:202
  13.0 3.3 %shard_map.58 = (bf16[384,1024]{1,0:T(8,128)(2,1)S(1)}, bf16[2,128,128]{2,1,0:T(8,128)(2,1)S(1)}, bf16[2,128,128]{2,1,0:T(8,128)(2,1)S(1)}) custom-call(bf16[16,128,128]{2,1,0:T(8,128)(2,1)S(1)} %get-tuple-element.30.field_ref, bf16[768,384]{1,0:T(8,128)(2,1)S(1)} %get-tuple-element.33.taps_one_ref, bf16[768,384]{1,0:T(8,128)(2,1)S(1)} %get-tuple-element.34.taps_two_ref, ...), custom_call_target="tpu_custom_call" | custom-call | flops 1887436800 | bytes 524288 | tf_op jit(solution)/shard_map/pallas_call | solution.py:189
  16.3 2.4 %collective-permute-done.4.before_ref = bf16[1,128,128]{2,1,0:T(8,128)(2,1)S(1)} collective-permute-done((bf16[1,128,128]{2,1,0:T(8,128)(2,1)S(1)}, bf16[1,128,128]{2,1,0:T(8,128)(2,1)S(1)}, u32[]{:S(2)}, u32[]{:S(2)}) %collective-permute-start.4) | collective-permute-done | bytes 32800 | tf_op jit(solution)/shard_map/ppermute | solution.py:202
  18.7 1.0 %shard_map.59.tokens_ref = bf16[384,1024]{1,0:T(8,128)(2,1)S(1)} custom-call(bf16[16,128,128]{2,1,0:T(8,128)(2,1)S(1)} %get-tuple-element.30.field_ref, bf16[1,128,128]{2,1,0:T(8,128)(2,1)S(1)} %collective-permute-done.3.after_ref, bf16[1,128,128]{2,1,0:T(8,128)(2,1)S(1)} %collective-permute-done.4.before_ref, ...), custom_call_target="tpu_custom_call" | custom-call | flops 251658240 | bytes 524288 | tf_op jit(solution)/shard_map/pallas_call | solution.py:189
  19.7 0.5 shard_map.66
  20.2 1.5 %collective-permute-start.14 = (bf16[96,1024]{1,0:T(8,128)(2,1)S(1)}, bf16[96,1024]{1,0:T(8,128)(2,1)S(1)}, u32[]{:S(2)}, u32[]{:S(2)}) collective-permute-start(bf16[96,1024]{1,0:T(8,128)(2,1)S(1)} %shard_map.66), channel_id=1, source_target_pairs={{0,12},{4,0},{8,4},{12,8},{1,13},{5,1},{9,5},{13,9},{2,14},{6,2},{... | collective-permute-start | bytes 589832 | tf_op jit(solution)/shard_map/ppermute | solution.py:202
  21.7 0.5 shard_map.64
  22.2 0.1 collective-permute-start.11
  22.2 0.5 shard_map.60
  22.7 0.1 collective-permute-start.5
  22.8 0.5 shard_map.62
  23.2 3.5 %collective-permute-start.8 = (bf16[96,1024]{1,0:T(8,128)(2,1)S(1)}, bf16[96,1024]{1,0:T(8,128)(2,1)S(1)}, u32[]{:S(2)}, u32[]{:S(2)}) collective-permute-start(bf16[96,1024]{1,0:T(8,128)(2,1)S(1)} %shard_map.62), channel_id=1, source_target_pairs={{0,12},{4,0},{8,4},{12,8},{1,13},{5,1},{9,5},{13,9},{2,14},{6,2},{... | collective-permute-start | bytes 589832 | tf_op jit(solution)/shard_map/ppermute | solution.py:202
  26.8 0.9 %collective-permute-done.14.arrived_ref = bf16[96,1024]{1,0:T(8,128)(2,1)S(1)} collective-permute-done((bf16[96,1024]{1,0:T(8,128)(2,1)S(1)}, bf16[96,1024]{1,0:T(8,128)(2,1)S(1)}, u32[]{:S(2)}, u32[]{:S(2)}) %collective-permute-start.14) | collective-permute-done | bytes 196640 | tf_op jit(solution)/shard_map/ppermute | solution.py:202
  27.6 0.8 %shard_map.67 = (bf16[96,1024]{1,0:T(8,128)(2,1)S(1)}, f32[192,1024]{1,0:T(8,128)S(1)}) custom-call(bf16[96,1024]{1,0:T(8,128)(2,1)S(1)} %collective-permute-done.14.arrived_ref, bf16[384,1024]{1,0:T(8,128)(2,1)S(1)} %shard_map.59.tokens_ref, bf16[1024,4096]{1,0:T(8,128)(2,1)S(1)} %copy-done), custom_call_target="tpu_custom_call" | custom-call | tf_op jit(solution)/shard_map/pallas_call | solution.py:189
  28.4 3.7 %collective-permute-start.15 = (bf16[96,1024]{1,0:T(8,128)(2,1)S(1)}, bf16[96,1024]{1,0:T(8,128)(2,1)S(1)}, u32[]{:S(2)}, u32[]{:S(2)}) collective-permute-start(bf16[96,1024]{1,0:T(8,128)(2,1)S(1)} %get-tuple-element.45), channel_id=1, source_target_pairs={{0,12},{4,0},{8,4},{12,8},{1,13},{5,1},{9,5},{13,9},{2,14},{6,2},{... | collective-permute-start | bytes 589832 | tf_op jit(solution)/shard_map/ppermute | solution.py:202
  32.1 0.8 %shard_map.65 = (bf16[96,1024]{1,0:T(8,128)(2,1)S(1)}, f32[192,1024]{1,0:T(8,128)S(1)}) custom-call(bf16[96,1024]{1,0:T(8,128)(2,1)S(1)} %collective-permute-done.11.arrived_ref, bf16[384,1024]{1,0:T(8,128)(2,1)S(1)} %shard_map.59.tokens_ref, bf16[1024,4096]{1,0:T(8,128)(2,1)S(1)} %copy-done), custom_call_target="tpu_custom_call" | custom-call | tf_op jit(solution)/shard_map/pallas_call | solution.py:189
  32.9 3.4 %collective-permute-start.12 = (bf16[96,1024]{1,0:T(8,128)(2,1)S(1)}, bf16[96,1024]{1,0:T(8,128)(2,1)S(1)}, u32[]{:S(2)}, u32[]{:S(2)}) collective-permute-start(bf16[96,1024]{1,0:T(8,128)(2,1)S(1)} %get-tuple-element.43), channel_id=1, source_target_pairs={{0,12},{4,0},{8,4},{12,8},{1,13},{5,1},{9,5},{13,9},{2,14},{6,2},{... | collective-permute-start | bytes 589832 | tf_op jit(solution)/shard_map/ppermute | solution.py:202
  36.3 0.8 %shard_map.61 = (bf16[96,1024]{1,0:T(8,128)(2,1)S(1)}, f32[192,1024]{1,0:T(8,128)S(1)}) custom-call(bf16[96,1024]{1,0:T(8,128)(2,1)S(1)} %collective-permute-done.5.arrived_ref, bf16[384,1024]{1,0:T(8,128)(2,1)S(1)} %shard_map.59.tokens_ref, bf16[1024,4096]{1,0:T(8,128)(2,1)S(1)} %copy-done), custom_call_target="tpu_custom_call" | custom-call | tf_op jit(solution)/shard_map/pallas_call | solution.py:189
  37.1 3.4 %collective-permute-start.6 = (bf16[96,1024]{1,0:T(8,128)(2,1)S(1)}, bf16[96,1024]{1,0:T(8,128)(2,1)S(1)}, u32[]{:S(2)}, u32[]{:S(2)}) collective-permute-start(bf16[96,1024]{1,0:T(8,128)(2,1)S(1)} %get-tuple-element.39), channel_id=1, source_target_pairs={{0,12},{4,0},{8,4},{12,8},{1,13},{5,1},{9,5},{13,9},{2,14},{6,2},{... | collective-permute-start | bytes 589832 | tf_op jit(solution)/shard_map/ppermute | solution.py:202
  40.5 0.8 %shard_map.63 = (bf16[96,1024]{1,0:T(8,128)(2,1)S(1)}, f32[192,1024]{1,0:T(8,128)S(1)}) custom-call(bf16[96,1024]{1,0:T(8,128)(2,1)S(1)} %collective-permute-done.8.arrived_ref, bf16[384,1024]{1,0:T(8,128)(2,1)S(1)} %shard_map.59.tokens_ref, bf16[1024,4096]{1,0:T(8,128)(2,1)S(1)} %copy-done), custom_call_target="tpu_custom_call" | custom-call | tf_op jit(solution)/shard_map/pallas_call | solution.py:189
  41.3 3.4 %collective-permute-start.9 = (bf16[96,1024]{1,0:T(8,128)(2,1)S(1)}, bf16[96,1024]{1,0:T(8,128)(2,1)S(1)}, u32[]{:S(2)}, u32[]{:S(2)}) collective-permute-start(bf16[96,1024]{1,0:T(8,128)(2,1)S(1)} %get-tuple-element.41), channel_id=1, source_target_pairs={{0,12},{4,0},{8,4},{12,8},{1,13},{5,1},{9,5},{13,9},{2,14},{6,2},{... | collective-permute-start | bytes 589832 | tf_op jit(solution)/shard_map/ppermute | solution.py:202
  44.8 3.4 %collective-permute-start.16 = (bf16[96,1024]{1,0:T(8,128)(2,1)S(1)}, bf16[96,1024]{1,0:T(8,128)(2,1)S(1)}, u32[]{:S(2)}, u32[]{:S(2)}) collective-permute-start(bf16[96,1024]{1,0:T(8,128)(2,1)S(1)} %add_convert_fusion), channel_id=1, source_target_pairs={{0,12},{4,0},{8,4},{12,8},{1,13},{5,1},{9,5},{13,9},{2,14},{6,2},{... | collective-permute-start | bytes 589832 | tf_op jit(solution)/shard_map/ppermute | solution.py:202
  48.2 0.5 collective-permute-done.12
  48.7 3.7 %collective-permute-start.13 = (bf16[96,1024]{1,0:T(8,128)(2,1)S(1)}, bf16[96,1024]{1,0:T(8,128)(2,1)S(1)}, u32[]{:S(2)}, u32[]{:S(2)}) collective-permute-start(bf16[96,1024]{1,0:T(8,128)(2,1)S(1)} %add_convert_fusion.1), channel_id=1, source_target_pairs={{0,12},{4,0},{8,4},{12,8},{1,13},{5,1},{9,5},{13,9},{2,14},{6,2},{... | collective-permute-start | bytes 589832 | tf_op jit(solution)/shard_map/ppermute | solution.py:202
  52.5 0.5 collective-permute-done.6
  53.0 3.7 %collective-permute-start.7 = (bf16[96,1024]{1,0:T(8,128)(2,1)S(1)}, bf16[96,1024]{1,0:T(8,128)(2,1)S(1)}, u32[]{:S(2)}, u32[]{:S(2)}) collective-permute-start(bf16[96,1024]{1,0:T(8,128)(2,1)S(1)} %add_convert_fusion.3), channel_id=1, source_target_pairs={{0,12},{4,0},{8,4},{12,8},{1,13},{5,1},{9,5},{13,9},{2,14},{6,2},{... | collective-permute-start | bytes 589832 | tf_op jit(solution)/shard_map/ppermute | solution.py:202
  56.7 0.5 collective-permute-done.9
  57.2 3.7 %collective-permute-start.10 = (bf16[96,1024]{1,0:T(8,128)(2,1)S(1)}, bf16[96,1024]{1,0:T(8,128)(2,1)S(1)}, u32[]{:S(2)}, u32[]{:S(2)}) collective-permute-start(bf16[96,1024]{1,0:T(8,128)(2,1)S(1)} %add_convert_fusion.2), channel_id=1, source_target_pairs={{0,12},{4,0},{8,4},{12,8},{1,13},{5,1},{9,5},{13,9},{2,14},{6,2},{... | collective-permute-start | bytes 589832 | tf_op jit(solution)/shard_map/ppermute | solution.py:202
  60.9 0.5 collective-permute-done.16
  61.3 0.1 multiply_convert_fusion
  61.4 4.1 %collective-permute-done.13 = bf16[96,1024]{1,0:T(8,128)(2,1)S(1)} collective-permute-done((bf16[96,1024]{1,0:T(8,128)(2,1)S(1)}, bf16[96,1024]{1,0:T(8,128)(2,1)S(1)}, u32[]{:S(2)}, u32[]{:S(2)}) %collective-permute-start.13) | collective-permute-done | bytes 196640 | tf_op jit(solution)/shard_map/ppermute | solution.py:202
  65.5 0.1 multiply_convert_fusion.1
  65.7 4.1 %collective-permute-done.7 = bf16[96,1024]{1,0:T(8,128)(2,1)S(1)} collective-permute-done((bf16[96,1024]{1,0:T(8,128)(2,1)S(1)}, bf16[96,1024]{1,0:T(8,128)(2,1)S(1)}, u32[]{:S(2)}, u32[]{:S(2)}) %collective-permute-start.7) | collective-permute-done | bytes 196640 | tf_op jit(solution)/shard_map/ppermute | solution.py:202
  69.8 0.1 multiply_convert_fusion.3
  69.9 2.4 %collective-permute-done.10 = bf16[96,1024]{1,0:T(8,128)(2,1)S(1)} collective-permute-done((bf16[96,1024]{1,0:T(8,128)(2,1)S(1)}, bf16[96,1024]{1,0:T(8,128)(2,1)S(1)}, u32[]{:S(2)}, u32[]{:S(2)}) %collective-permute-start.10) | collective-permute-done | bytes 196640 | tf_op jit(solution)/shard_map/ppermute | solution.py:202
  72.3 0.1 multiply_convert_fusion.2
  72.4 0.9 %pad_maximum_fusion = bf16[96,4096]{1,0:T(8,128)(2,1)} fusion(bf16[96,1024]{1,0:T(8,128)(2,1)S(1)} %multiply_convert_fusion, bf16[96,1024]{1,0:T(8,128)(2,1)S(1)} %multiply_convert_fusion.1, bf16[96,1024]{1,0:T(8,128)(2,1)S(1)} %multiply_convert_fusion.2, bf16[96,1024]{1,0:T(8,128)(2,1)S(1)} %multiply_convert_fusion.3), kind=kLoop, calls=%fused_computation | loop fusion | flops 3145728 | bytes 1572864 | tf_op jit(solution)/shard_map/concatenate | solution.py:308
  (18 shorter events, 0.2 us)
Async XLA Ops:
  0.0 1.0 %copy-start.1 = (f32[64,32,32]{0,2,1:T(8,128)S(1)}, f32[64,32,32]{0,2,1:T(8,128)}, u32[]{:S(2)}) copy-start(f32[64,32,32]{0,2,1:T(8,128)} %param.5) | copy-start | bytes 786436
  1.2 6.5 %collective-permute-start.1 = (bf16[16,32,128]{2,1,0:T(8,128)(2,1)S(1)}, bf16[16,32,128]{2,1,0:T(8,128)(2,1)S(1)}, u32[]{:S(2)}, u32[]{:S(2)}) collective-permute-start(bf16[16,32,128]{2,1,0:T(8,128)(2,1)S(1)} %shard_map.55.refs_0_), channel_id=1, source_target_pairs={{0,2},{2,0},{1,3},{3,1},{4,6},{6,4},{5,7},{7,5},{8,10},{10,8},{9,1... | collective-permute-start | bytes 393224 | tf_op jit(solution)/shard_map/ppermute | solution.py:202
  4.2 4.0 %collective-permute-start = (bf16[16,32,128]{2,1,0:T(8,128)(2,1)S(1)}, bf16[16,32,128]{2,1,0:T(8,128)(2,1)S(1)}, u32[]{:S(2)}, u32[]{:S(2)}) collective-permute-start(bf16[16,32,128]{2,1,0:T(8,128)(2,1)S(1)} %shard_map.55.refs_0_), channel_id=1, source_target_pairs={{0,1},{1,0},{2,3},{3,2},{4,5},{5,4},{6,7},{7,6},{8,9},{9,8},{10,11... | collective-permute-start | bytes 393224 | tf_op jit(solution)/shard_map/ppermute | solution.py:202
  4.2 1.0 %copy-start.2 = (f32[9,64,64]{2,1,0:T(8,128)S(1)}, f32[9,64,64]{2,1,0:T(8,128)}, u32[]{:S(2)}) copy-start(f32[9,64,64]{2,1,0:T(8,128)} %first_ref.1) | copy-start | bytes 442372
  5.1 1.0 %copy-start.3 = (f32[9,64,64]{2,1,0:T(8,128)S(1)}, f32[9,64,64]{2,1,0:T(8,128)}, u32[]{:S(2)}) copy-start(f32[9,64,64]{2,1,0:T(8,128)} %second_ref.1) | copy-start | bytes 442372
  6.1 0.9 %copy-start.4 = (bf16[256,384]{1,0:T(8,128)(2,1)S(1)}, bf16[256,384]{1,0:T(8,128)(2,1)}, u32[]{:S(2)}) copy-start(bf16[256,384]{1,0:T(8,128)(2,1)} %embed_ref.1) | copy-start | bytes 589828
  7.7 1.5 %collective-permute-start.2 = (bf16[16,32,128]{2,1,0:T(8,128)(2,1)S(1)}, bf16[16,32,128]{2,1,0:T(8,128)(2,1)S(1)}, u32[]{:S(2)}, u32[]{:S(2)}) collective-permute-start(bf16[16,32,128]{2,1,0:T(8,128)(2,1)S(1)} %collective-permute-done.1.refs_2_), channel_id=1, source_target_pairs={{0,1},{1,0},{2,3},{3,2},{4,5},{5,4},{6,7},{7,6},{8,9},{9,8},{10,11... | collective-permute-start | bytes 393224 | tf_op jit(solution)/shard_map/ppermute | solution.py:202
  9.2 7.0 %collective-permute-start.3 = (bf16[1,128,128]{2,1,0:T(8,128)(2,1)S(1)}, bf16[1,128,128]{2,1,0:T(8,128)(2,1)S(1)}, u32[]{:S(2)}, u32[]{:S(2)}) collective-permute-start(bf16[1,128,128]{2,1,0:T(8,128)(2,1)S(1)} %get-tuple-element.31), channel_id=1, source_target_pairs={{0,12},{4,0},{8,4},{12,8},{1,13},{5,1},{9,5},{13,9},{2,14},{6,2},{... | collective-permute-start | bytes 98312 | tf_op jit(solution)/shard_map/ppermute | solution.py:202
  13.0 5.7 %collective-permute-start.4 = (bf16[1,128,128]{2,1,0:T(8,128)(2,1)S(1)}, bf16[1,128,128]{2,1,0:T(8,128)(2,1)S(1)}, u32[]{:S(2)}, u32[]{:S(2)}) collective-permute-start(bf16[1,128,128]{2,1,0:T(8,128)(2,1)S(1)} %get-tuple-element.32), channel_id=1, source_target_pairs={{0,4},{4,8},{8,12},{12,0},{1,5},{5,9},{9,13},{13,1},{2,6},{6,10},{... | collective-permute-start | bytes 98312 | tf_op jit(solution)/shard_map/ppermute | solution.py:202
  13.0 6.7 %copy-start = (bf16[1024,4096]{1,0:T(8,128)(2,1)S(1)}, bf16[1024,4096]{1,0:T(8,128)(2,1)}, u32[]{:S(2)}) copy-start(bf16[1024,4096]{1,0:T(8,128)(2,1)} %mixing_ref.15) | copy-start | bytes 25165828
  20.2 7.4 %collective-permute-start.14 = (bf16[96,1024]{1,0:T(8,128)(2,1)S(1)}, bf16[96,1024]{1,0:T(8,128)(2,1)S(1)}, u32[]{:S(2)}, u32[]{:S(2)}) collective-permute-start(bf16[96,1024]{1,0:T(8,128)(2,1)S(1)} %shard_map.66), channel_id=1, source_target_pairs={{0,12},{4,0},{8,4},{12,8},{1,13},{5,1},{9,5},{13,9},{2,14},{6,2},{... | collective-permute-start | bytes 589832 | tf_op jit(solution)/shard_map/ppermute | solution.py:202
  22.2 10.0 %collective-permute-start.11 = (bf16[96,1024]{1,0:T(8,128)(2,1)S(1)}, bf16[96,1024]{1,0:T(8,128)(2,1)S(1)}, u32[]{:S(2)}, u32[]{:S(2)}) collective-permute-start(bf16[96,1024]{1,0:T(8,128)(2,1)S(1)} %shard_map.64), channel_id=1, source_target_pairs={{0,12},{4,0},{8,4},{12,8},{1,13},{5,1},{9,5},{13,9},{2,14},{6,2},{... | collective-permute-start | bytes 589832 | tf_op jit(solution)/shard_map/ppermute | solution.py:202
  22.7 13.6 %collective-permute-start.5 = (bf16[96,1024]{1,0:T(8,128)(2,1)S(1)}, bf16[96,1024]{1,0:T(8,128)(2,1)S(1)}, u32[]{:S(2)}, u32[]{:S(2)}) collective-permute-start(bf16[96,1024]{1,0:T(8,128)(2,1)S(1)} %shard_map.60), channel_id=1, source_target_pairs={{0,12},{4,0},{8,4},{12,8},{1,13},{5,1},{9,5},{13,9},{2,14},{6,2},{... | collective-permute-start | bytes 589832 | tf_op jit(solution)/shard_map/ppermute | solution.py:202
  23.2 17.3 %collective-permute-start.8 = (bf16[96,1024]{1,0:T(8,128)(2,1)S(1)}, bf16[96,1024]{1,0:T(8,128)(2,1)S(1)}, u32[]{:S(2)}, u32[]{:S(2)}) collective-permute-start(bf16[96,1024]{1,0:T(8,128)(2,1)S(1)} %shard_map.62), channel_id=1, source_target_pairs={{0,12},{4,0},{8,4},{12,8},{1,13},{5,1},{9,5},{13,9},{2,14},{6,2},{... | collective-permute-start | bytes 589832 | tf_op jit(solution)/shard_map/ppermute | solution.py:202
  28.4 16.4 %collective-permute-start.15 = (bf16[96,1024]{1,0:T(8,128)(2,1)S(1)}, bf16[96,1024]{1,0:T(8,128)(2,1)S(1)}, u32[]{:S(2)}, u32[]{:S(2)}) collective-permute-start(bf16[96,1024]{1,0:T(8,128)(2,1)S(1)} %get-tuple-element.45), channel_id=1, source_target_pairs={{0,12},{4,0},{8,4},{12,8},{1,13},{5,1},{9,5},{13,9},{2,14},{6,2},{... | collective-permute-start | bytes 589832 | tf_op jit(solution)/shard_map/ppermute | solution.py:202
  32.9 15.8 %collective-permute-start.12 = (bf16[96,1024]{1,0:T(8,128)(2,1)S(1)}, bf16[96,1024]{1,0:T(8,128)(2,1)S(1)}, u32[]{:S(2)}, u32[]{:S(2)}) collective-permute-start(bf16[96,1024]{1,0:T(8,128)(2,1)S(1)} %get-tuple-element.43), channel_id=1, source_target_pairs={{0,12},{4,0},{8,4},{12,8},{1,13},{5,1},{9,5},{13,9},{2,14},{6,2},{... | collective-permute-start | bytes 589832 | tf_op jit(solution)/shard_map/ppermute | solution.py:202
  37.1 15.8 %collective-permute-start.6 = (bf16[96,1024]{1,0:T(8,128)(2,1)S(1)}, bf16[96,1024]{1,0:T(8,128)(2,1)S(1)}, u32[]{:S(2)}, u32[]{:S(2)}) collective-permute-start(bf16[96,1024]{1,0:T(8,128)(2,1)S(1)} %get-tuple-element.39), channel_id=1, source_target_pairs={{0,12},{4,0},{8,4},{12,8},{1,13},{5,1},{9,5},{13,9},{2,14},{6,2},{... | collective-permute-start | bytes 589832 | tf_op jit(solution)/shard_map/ppermute | solution.py:202
  41.3 15.8 %collective-permute-start.9 = (bf16[96,1024]{1,0:T(8,128)(2,1)S(1)}, bf16[96,1024]{1,0:T(8,128)(2,1)S(1)}, u32[]{:S(2)}, u32[]{:S(2)}) collective-permute-start(bf16[96,1024]{1,0:T(8,128)(2,1)S(1)} %get-tuple-element.41), channel_id=1, source_target_pairs={{0,12},{4,0},{8,4},{12,8},{1,13},{5,1},{9,5},{13,9},{2,14},{6,2},{... | collective-permute-start | bytes 589832 | tf_op jit(solution)/shard_map/ppermute | solution.py:202
  44.8 16.5 %collective-permute-start.16 = (bf16[96,1024]{1,0:T(8,128)(2,1)S(1)}, bf16[96,1024]{1,0:T(8,128)(2,1)S(1)}, u32[]{:S(2)}, u32[]{:S(2)}) collective-permute-start(bf16[96,1024]{1,0:T(8,128)(2,1)S(1)} %add_convert_fusion), channel_id=1, source_target_pairs={{0,12},{4,0},{8,4},{12,8},{1,13},{5,1},{9,5},{13,9},{2,14},{6,2},{... | collective-permute-start | bytes 589832 | tf_op jit(solution)/shard_map/ppermute | solution.py:202
  48.7 16.8 %collective-permute-start.13 = (bf16[96,1024]{1,0:T(8,128)(2,1)S(1)}, bf16[96,1024]{1,0:T(8,128)(2,1)S(1)}, u32[]{:S(2)}, u32[]{:S(2)}) collective-permute-start(bf16[96,1024]{1,0:T(8,128)(2,1)S(1)} %add_convert_fusion.1), channel_id=1, source_target_pairs={{0,12},{4,0},{8,4},{12,8},{1,13},{5,1},{9,5},{13,9},{2,14},{6,2},{... | collective-permute-start | bytes 589832 | tf_op jit(solution)/shard_map/ppermute | solution.py:202
  53.0 16.8 %collective-permute-start.7 = (bf16[96,1024]{1,0:T(8,128)(2,1)S(1)}, bf16[96,1024]{1,0:T(8,128)(2,1)S(1)}, u32[]{:S(2)}, u32[]{:S(2)}) collective-permute-start(bf16[96,1024]{1,0:T(8,128)(2,1)S(1)} %add_convert_fusion.3), channel_id=1, source_target_pairs={{0,12},{4,0},{8,4},{12,8},{1,13},{5,1},{9,5},{13,9},{2,14},{6,2},{... | collective-permute-start | bytes 589832 | tf_op jit(solution)/shard_map/ppermute | solution.py:202
  57.2 15.1 %collective-permute-start.10 = (bf16[96,1024]{1,0:T(8,128)(2,1)S(1)}, bf16[96,1024]{1,0:T(8,128)(2,1)S(1)}, u32[]{:S(2)}, u32[]{:S(2)}) collective-permute-start(bf16[96,1024]{1,0:T(8,128)(2,1)S(1)} %add_convert_fusion.2), channel_id=1, source_target_pairs={{0,12},{4,0},{8,4},{12,8},{1,13},{5,1},{9,5},{13,9},{2,14},{6,2},{... | collective-permute-start | bytes 589832 | tf_op jit(solution)/shard_map/ppermute | solution.py:202

commit v12 on v10

--- a/solution.py
+++ b/solution.py
@@ -54,7 +54,7 @@
 def weights_kernel(first_ref, second_ref, embed_ref, taps_one_ref, taps_two_ref, embed_out_ref, scratch):
     for source, target in ((first_ref, taps_one_ref), (second_ref, taps_two_ref)):
         upper, lower = split_two(spread_taps(source))
-        target[...] = jnp.concatenate([upper, lower, upper], axis=0)
+        target[...] = jnp.concatenate([upper, lower], axis=1)
     chans = embed_ref.shape[0] // 4
     embed = embed_ref.shape[1]
     count = lax.axis_size("tok")
@@ -103,15 +103,20 @@
     return jnp.dot(left, right, preferred_element_type=jnp.float32)
 
 
+def dot_both(rows, taps_ref):
+    both = dot(rows, taps_ref[...])
+    half = both.shape[1] // 2
+    return both[:, :half] + both[:, half:]
+
+
 def first_conv(field_at, pairs, taps_ref, lat):
-    rows = window(field_at, pairs)
-    products = dot(jnp.concatenate([rows, rows], axis=-1), taps_ref[: 2 * rows.shape[1]])
+    products = dot_both(window(field_at, pairs), taps_ref)
     return split_two(gelu(add_lat_taps(products, lat)))
 
 
 def second_conv(upper_at, lower_at, pairs, taps_ref, lat):
     upper, lower = window(upper_at, pairs), window(lower_at, pairs)
-    products = dot(jnp.concatenate([upper, upper, lower], axis=-1), taps_ref[...])
+    products = dot_both(upper, taps_ref) + dot(lower, taps_ref[:, : taps_ref.shape[1] // 2])
     rounded = add_lat_taps(products, lat).astype(jnp.bfloat16).astype(jnp.float32)
     return rounded.reshape(-1, rounded.shape[2])
 
@@ -217,7 +222,7 @@
     packed = call(
         pack_kernel, shape((pairs, lat, wide)), (jnp.transpose(weather, (1, 2, 0)),), moved=weather.size * 10
     )
-    taps = shape((12 * chans, 6 * chans))
+    taps = shape((4 * chans, 12 * chans))
     weights = call(
         weights_kernel,
         (taps, taps, shape((embed, 4 * chans))),

time: 72.1 us -> 71.6 us (level)
  transfers between devices with their start and end apart: 17 -> 17, of which waited for: 5 -> 5; matrix products, arithmetic and copies ran while one was open for 1% -> 1% of each run, Pallas kernels for 11% -> 10%
where the time goes in v12:
time: 71.6 us; the launch traced here: 71.4 us
  starting transfers between devices  43.2 us (60%)
  waiting for transfers between devices  13.4 us (19%)
  Pallas kernels  9.28 us (13%)
  local copies, waits for them, and re-layouts  3.89 us (5%)
  other arithmetic  1.5 us (2%)
    ppermute x17, starting transfers between devices, turned(): lax.ppermute(value, axis, [(i, (i + away) % count) for i in range(count)])  43.2 us
    ppermute x17, waiting for transfers between devices, turned(): lax.ppermute(value, axis, [(i, (i + away) % count) for i in range(count)])  13.4 us
    pallas_call x13, Pallas kernels, call(): pl.pallas_call(kernel, out_shape=out_shape, in_specs=[pl.BlockSpec(memory...  9.28 us
    unnamed x10, local copies, waits for them, and re-layouts  3.89 us
  transfers between devices with their start and end apart: 17, of which 5 were waited for; matrix products, arithmetic and copies ran while one was open for 1% of the time, Pallas kernels for 10%

profile of v12, /device:TPU:0, one launch (start us, length us, event | category | flops | bytes accessed | tf_op | source)
XLA Modules:
  0.0 71.4 jit_solution(9103118631475063621)
XLA Ops:
  0.0 1.0 %copy-done.1 = f32[64,32,32]{0,2,1:T(8,128)S(1)} copy-done((f32[64,32,32]{0,2,1:T(8,128)S(1)}, f32[64,32,32]{0,2,1:T(8,128)}, u32[]{:S(2)}) %copy-start.1) | copy-done | bytes 262168
  1.0 0.1 shard_map.55.refs_0_
  1.2 3.0 %collective-permute-start.1 = (bf16[16,32,128]{2,1,0:T(8,128)(2,1)S(1)}, bf16[16,32,128]{2,1,0:T(8,128)(2,1)S(1)}, u32[]{:S(2)}, u32[]{:S(2)}) collective-permute-start(bf16[16,32,128]{2,1,0:T(8,128)(2,1)S(1)} %shard_map.55.refs_0_), channel_id=1, source_target_pairs={{0,2},{2,0},{1,3},{3,1},{4,6},{6,4},{5,7},{7,5},{8,10},{10,8},{9,1... | collective-permute-start | bytes 393224 | tf_op jit(solution)/shard_map/ppermute | solution.py:204
  4.2 0.0 collective-permute-start
  4.2 1.0 %copy-done.2 = f32[9,64,64]{2,1,0:T(8,128)S(1)} copy-done((f32[9,64,64]{2,1,0:T(8,128)S(1)}, f32[9,64,64]{2,1,0:T(8,128)}, u32[]{:S(2)}) %copy-start.2) | copy-done | bytes 147480
  5.1 1.0 %copy-done.3 = f32[9,64,64]{2,1,0:T(8,128)S(1)} copy-done((f32[9,64,64]{2,1,0:T(8,128)S(1)}, f32[9,64,64]{2,1,0:T(8,128)}, u32[]{:S(2)}) %copy-start.3) | copy-done | bytes 147480
  6.1 0.9 %copy-done.4 = bf16[256,384]{1,0:T(8,128)(2,1)S(1)} copy-done((bf16[256,384]{1,0:T(8,128)(2,1)S(1)}, bf16[256,384]{1,0:T(8,128)(2,1)}, u32[]{:S(2)}) %copy-start.4) | copy-done | bytes 196632
  7.0 0.6 shard_map.56
  7.6 0.0 collective-permute-done.1.refs_2_
  7.7 0.5 collective-permute-start.2
  8.2 1.0 %collective-permute-done.2.refs_3_ = bf16[16,32,128]{2,1,0:T(8,128)(2,1)S(1)} collective-permute-done((bf16[16,32,128]{2,1,0:T(8,128)(2,1)S(1)}, bf16[16,32,128]{2,1,0:T(8,128)(2,1)S(1)}, u32[]{:S(2)}, u32[]{:S(2)}) %collective-permute-start.2) | collective-permute-done | bytes 131104 | tf_op jit(solution)/shard_map/ppermute | solution.py:204
  9.2 0.1 shard_map.57
  9.2 1.7 %collective-permute-start.3 = (bf16[1,128,128]{2,1,0:T(8,128)(2,1)S(1)}, bf16[1,128,128]{2,1,0:T(8,128)(2,1)S(1)}, u32[]{:S(2)}, u32[]{:S(2)}) collective-permute-start(bf16[1,128,128]{2,1,0:T(8,128)(2,1)S(1)} %get-tuple-element.31), channel_id=1, source_target_pairs={{0,4},{4,8},{8,12},{12,0},{1,5},{5,9},{9,13},{13,1},{2,6},{6,10},{... | collective-permute-start | bytes 98312 | tf_op jit(solution)/shard_map/ppermute | solution.py:204
  10.9 2.2 %collective-permute-start.4 = (bf16[1,128,128]{2,1,0:T(8,128)(2,1)S(1)}, bf16[1,128,128]{2,1,0:T(8,128)(2,1)S(1)}, u32[]{:S(2)}, u32[]{:S(2)}) collective-permute-start(bf16[1,128,128]{2,1,0:T(8,128)(2,1)S(1)} %get-tuple-element.32), channel_id=1, source_target_pairs={{0,12},{4,0},{8,4},{12,8},{1,13},{5,1},{9,5},{13,9},{2,14},{6,2},{... | collective-permute-start | bytes 98312 | tf_op jit(solution)/shard_map/ppermute | solution.py:204
  13.1 2.4 %shard_map.58 = (bf16[384,768]{1,0:T(8,128)(2,1)S(1)}, bf16[4,128,128]{2,1,0:T(8,128)(2,1)S(1)}, bf16[4,128,128]{2,1,0:T(8,128)(2,1)S(1)}) custom-call(bf16[16,128,128]{2,1,0:T(8,128)(2,1)S(1)} %get-tuple-element.30.field_ref, bf16[256,768]{1,0:T(8,128)(2,1)S(1)} %get-tuple-element.33.taps_one_ref, bf16[256,768]{1,0:T(8,128)(2,1)S(1)} %get-tuple-element.34.taps_two_ref, ...), custom_call_target="tpu_custom_call" | custom-call | flops 1635778560 | bytes 524288 | tf_op jit(solution)/shard_map/pallas_call | solution.py:191
  15.5 0.0 collective-permute-done.3.before_ref
  15.5 1.2 %shard_map.59.tokens_ref = bf16[384,1024]{1,0:T(8,128)(2,1)S(1)} custom-call(bf16[16,128,128]{2,1,0:T(8,128)(2,1)S(1)} %get-tuple-element.30.field_ref, bf16[1,128,128]{2,1,0:T(8,128)(2,1)S(1)} %collective-permute-done.3.before_ref, bf16[1,128,128]{2,1,0:T(8,128)(2,1)S(1)} %collective-permute-done.4.after_ref, ...), custom_call_target="tpu_custom_call" | custom-call | flops 503316480 | bytes 524288 | tf_op jit(solution)/shard_map/pallas_call | solution.py:191
  16.8 0.5 shard_map.60
  17.2 3.4 %collective-permute-start.5 = (bf16[96,1024]{1,0:T(8,128)(2,1)S(1)}, bf16[96,1024]{1,0:T(8,128)(2,1)S(1)}, u32[]{:S(2)}, u32[]{:S(2)}) collective-permute-start(bf16[96,1024]{1,0:T(8,128)(2,1)S(1)} %shard_map.60), channel_id=1, source_target_pairs={{0,12},{4,0},{8,4},{12,8},{1,13},{5,1},{9,5},{13,9},{2,14},{6,2},{... | collective-permute-start | bytes 589832 | tf_op jit(solution)/shard_map/ppermute | solution.py:204
  20.6 0.5 shard_map.62
  21.1 0.1 collective-permute-start.8
  21.2 0.5 shard_map.64
  21.6 0.5 collective-permute-start.11
  22.1 0.5 shard_map.66
  22.6 1.2 %collective-permute-start.14 = (bf16[96,1024]{1,0:T(8,128)(2,1)S(1)}, bf16[96,1024]{1,0:T(8,128)(2,1)S(1)}, u32[]{:S(2)}, u32[]{:S(2)}) collective-permute-start(bf16[96,1024]{1,0:T(8,128)(2,1)S(1)} %shard_map.66), channel_id=1, source_target_pairs={{0,12},{4,0},{8,4},{12,8},{1,13},{5,1},{9,5},{13,9},{2,14},{6,2},{... | collective-permute-start | bytes 589832 | tf_op jit(solution)/shard_map/ppermute | solution.py:204
  23.8 2.1 %collective-permute-done.5.arrived_ref = bf16[96,1024]{1,0:T(8,128)(2,1)S(1)} collective-permute-done((bf16[96,1024]{1,0:T(8,128)(2,1)S(1)}, bf16[96,1024]{1,0:T(8,128)(2,1)S(1)}, u32[]{:S(2)}, u32[]{:S(2)}) %collective-permute-start.5) | collective-permute-done | bytes 196640 | tf_op jit(solution)/shard_map/ppermute | solution.py:204
  25.9 0.8 %shard_map.61 = (bf16[96,1024]{1,0:T(8,128)(2,1)S(1)}, f32[192,1024]{1,0:T(8,128)S(1)}) custom-call(bf16[96,1024]{1,0:T(8,128)(2,1)S(1)} %collective-permute-done.5.arrived_ref, bf16[384,1024]{1,0:T(8,128)(2,1)S(1)} %shard_map.59.tokens_ref, bf16[1024,4096]{1,0:T(8,128)(2,1)S(1)} %copy-done), custom_call_target="tpu_custom_call" | custom-call | tf_op jit(solution)/shard_map/pallas_call | solution.py:191
  26.7 4.3 %collective-permute-start.6 = (bf16[96,1024]{1,0:T(8,128)(2,1)S(1)}, bf16[96,1024]{1,0:T(8,128)(2,1)S(1)}, u32[]{:S(2)}, u32[]{:S(2)}) collective-permute-start(bf16[96,1024]{1,0:T(8,128)(2,1)S(1)} %get-tuple-element.39), channel_id=1, source_target_pairs={{0,12},{4,0},{8,4},{12,8},{1,13},{5,1},{9,5},{13,9},{2,14},{6,2},{... | collective-permute-start | bytes 589832 | tf_op jit(solution)/shard_map/ppermute | solution.py:204
  31.1 0.8 %shard_map.63 = (bf16[96,1024]{1,0:T(8,128)(2,1)S(1)}, f32[192,1024]{1,0:T(8,128)S(1)}) custom-call(bf16[96,1024]{1,0:T(8,128)(2,1)S(1)} %collective-permute-done.8.arrived_ref, bf16[384,1024]{1,0:T(8,128)(2,1)S(1)} %shard_map.59.tokens_ref, bf16[1024,4096]{1,0:T(8,128)(2,1)S(1)} %copy-done), custom_call_target="tpu_custom_call" | custom-call | tf_op jit(solution)/shard_map/pallas_call | solution.py:191
  31.8 3.4 %collective-permute-start.9 = (bf16[96,1024]{1,0:T(8,128)(2,1)S(1)}, bf16[96,1024]{1,0:T(8,128)(2,1)S(1)}, u32[]{:S(2)}, u32[]{:S(2)}) collective-permute-start(bf16[96,1024]{1,0:T(8,128)(2,1)S(1)} %get-tuple-element.41), channel_id=1, source_target_pairs={{0,12},{4,0},{8,4},{12,8},{1,13},{5,1},{9,5},{13,9},{2,14},{6,2},{... | collective-permute-start | bytes 589832 | tf_op jit(solution)/shard_map/ppermute | solution.py:204
  35.3 0.0 collective-permute-done.11.arrived_ref
  35.3 0.8 %shard_map.65 = (bf16[96,1024]{1,0:T(8,128)(2,1)S(1)}, f32[192,1024]{1,0:T(8,128)S(1)}) custom-call(bf16[96,1024]{1,0:T(8,128)(2,1)S(1)} %collective-permute-done.11.arrived_ref, bf16[384,1024]{1,0:T(8,128)(2,1)S(1)} %shard_map.59.tokens_ref, bf16[1024,4096]{1,0:T(8,128)(2,1)S(1)} %copy-done), custom_call_target="tpu_custom_call" | custom-call | tf_op jit(solution)/shard_map/pallas_call | solution.py:191
  36.0 3.4 %collective-permute-start.12 = (bf16[96,1024]{1,0:T(8,128)(2,1)S(1)}, bf16[96,1024]{1,0:T(8,128)(2,1)S(1)}, u32[]{:S(2)}, u32[]{:S(2)}) collective-permute-start(bf16[96,1024]{1,0:T(8,128)(2,1)S(1)} %get-tuple-element.43), channel_id=1, source_target_pairs={{0,12},{4,0},{8,4},{12,8},{1,13},{5,1},{9,5},{13,9},{2,14},{6,2},{... | collective-permute-start | bytes 589832 | tf_op jit(solution)/shard_map/ppermute | solution.py:204
  39.5 0.8 %shard_map.67 = (bf16[96,1024]{1,0:T(8,128)(2,1)S(1)}, f32[192,1024]{1,0:T(8,128)S(1)}) custom-call(bf16[96,1024]{1,0:T(8,128)(2,1)S(1)} %collective-permute-done.14.arrived_ref, bf16[384,1024]{1,0:T(8,128)(2,1)S(1)} %shard_map.59.tokens_ref, bf16[1024,4096]{1,0:T(8,128)(2,1)S(1)} %copy-done), custom_call_target="tpu_custom_call" | custom-call | tf_op jit(solution)/shard_map/pallas_call | solution.py:191
  40.3 3.4 %collective-permute-start.15 = (bf16[96,1024]{1,0:T(8,128)(2,1)S(1)}, bf16[96,1024]{1,0:T(8,128)(2,1)S(1)}, u32[]{:S(2)}, u32[]{:S(2)}) collective-permute-start(bf16[96,1024]{1,0:T(8,128)(2,1)S(1)} %get-tuple-element.45), channel_id=1, source_target_pairs={{0,12},{4,0},{8,4},{12,8},{1,13},{5,1},{9,5},{13,9},{2,14},{6,2},{... | collective-permute-start | bytes 589832 | tf_op jit(solution)/shard_map/ppermute | solution.py:204
  43.7 3.4 %collective-permute-start.7 = (bf16[96,1024]{1,0:T(8,128)(2,1)S(1)}, bf16[96,1024]{1,0:T(8,128)(2,1)S(1)}, u32[]{:S(2)}, u32[]{:S(2)}) collective-permute-start(bf16[96,1024]{1,0:T(8,128)(2,1)S(1)} %add_convert_fusion.3), channel_id=1, source_target_pairs={{0,12},{4,0},{8,4},{12,8},{1,13},{5,1},{9,5},{13,9},{2,14},{6,2},{... | collective-permute-start | bytes 589832 | tf_op jit(solution)/shard_map/ppermute | solution.py:204
  47.2 0.0 collective-permute-done.9
  47.2 4.2 %collective-permute-start.10 = (bf16[96,1024]{1,0:T(8,128)(2,1)S(1)}, bf16[96,1024]{1,0:T(8,128)(2,1)S(1)}, u32[]{:S(2)}, u32[]{:S(2)}) collective-permute-start(bf16[96,1024]{1,0:T(8,128)(2,1)S(1)} %add_convert_fusion.2), channel_id=1, source_target_pairs={{0,12},{4,0},{8,4},{12,8},{1,13},{5,1},{9,5},{13,9},{2,14},{6,2},{... | collective-permute-start | bytes 589832 | tf_op jit(solution)/shard_map/ppermute | solution.py:204
  51.4 4.2 %collective-permute-start.13 = (bf16[96,1024]{1,0:T(8,128)(2,1)S(1)}, bf16[96,1024]{1,0:T(8,128)(2,1)S(1)}, u32[]{:S(2)}, u32[]{:S(2)}) collective-permute-start(bf16[96,1024]{1,0:T(8,128)(2,1)S(1)} %add_convert_fusion.1), channel_id=1, source_target_pairs={{0,12},{4,0},{8,4},{12,8},{1,13},{5,1},{9,5},{13,9},{2,14},{6,2},{... | collective-permute-start | bytes 589832 | tf_op jit(solution)/shard_map/ppermute | solution.py:204
  55.6 4.2 %collective-permute-start.16 = (bf16[96,1024]{1,0:T(8,128)(2,1)S(1)}, bf16[96,1024]{1,0:T(8,128)(2,1)S(1)}, u32[]{:S(2)}, u32[]{:S(2)}) collective-permute-start(bf16[96,1024]{1,0:T(8,128)(2,1)S(1)} %add_convert_fusion), channel_id=1, source_target_pairs={{0,12},{4,0},{8,4},{12,8},{1,13},{5,1},{9,5},{13,9},{2,14},{6,2},{... | collective-permute-start | bytes 589832 | tf_op jit(solution)/shard_map/ppermute | solution.py:204
  59.8 0.1 multiply_convert_fusion.3
  59.9 3.9 %collective-permute-done.10 = bf16[96,1024]{1,0:T(8,128)(2,1)S(1)} collective-permute-done((bf16[96,1024]{1,0:T(8,128)(2,1)S(1)}, bf16[96,1024]{1,0:T(8,128)(2,1)S(1)}, u32[]{:S(2)}, u32[]{:S(2)}) %collective-permute-start.10) | collective-permute-done | bytes 196640 | tf_op jit(solution)/shard_map/ppermute | solution.py:204
  63.9 0.1 multiply_convert_fusion.2
  64.0 4.1 %collective-permute-done.13 = bf16[96,1024]{1,0:T(8,128)(2,1)S(1)} collective-permute-done((bf16[96,1024]{1,0:T(8,128)(2,1)S(1)}, bf16[96,1024]{1,0:T(8,128)(2,1)S(1)}, u32[]{:S(2)}, u32[]{:S(2)}) %collective-permute-start.13) | collective-permute-done | bytes 196640 | tf_op jit(solution)/shard_map/ppermute | solution.py:204
  68.1 0.1 multiply_convert_fusion.1
  68.2 2.2 %collective-permute-done.16 = bf16[96,1024]{1,0:T(8,128)(2,1)S(1)} collective-permute-done((bf16[96,1024]{1,0:T(8,128)(2,1)S(1)}, bf16[96,1024]{1,0:T(8,128)(2,1)S(1)}, u32[]{:S(2)}, u32[]{:S(2)}) %collective-permute-start.16) | collective-permute-done | bytes 196640 | tf_op jit(solution)/shard_map/ppermute | solution.py:204
  70.3 0.1 multiply_convert_fusion
  70.5 0.9 %pad_maximum_fusion = bf16[96,4096]{1,0:T(8,128)(2,1)} fusion(bf16[96,1024]{1,0:T(8,128)(2,1)S(1)} %multiply_convert_fusion, bf16[96,1024]{1,0:T(8,128)(2,1)S(1)} %multiply_convert_fusion.1, bf16[96,1024]{1,0:T(8,128)(2,1)S(1)} %multiply_convert_fusion.2, bf16[96,1024]{1,0:T(8,128)(2,1)S(1)} %multiply_convert_fusion.3), kind=kLoop, calls=%fused_computation | loop fusion | flops 3145728 | bytes 1572864 | tf_op jit(solution)/shard_map/concatenate | solution.py:310
  (18 shorter events, 0.2 us)
Async XLA Ops:
  0.0 1.0 %copy-start.1 = (f32[64,32,32]{0,2,1:T(8,128)S(1)}, f32[64,32,32]{0,2,1:T(8,128)}, u32[]{:S(2)}) copy-start(f32[64,32,32]{0,2,1:T(8,128)} %param.5) | copy-start | bytes 786436
  1.2 6.5 %collective-permute-start.1 = (bf16[16,32,128]{2,1,0:T(8,128)(2,1)S(1)}, bf16[16,32,128]{2,1,0:T(8,128)(2,1)S(1)}, u32[]{:S(2)}, u32[]{:S(2)}) collective-permute-start(bf16[16,32,128]{2,1,0:T(8,128)(2,1)S(1)} %shard_map.55.refs_0_), channel_id=1, source_target_pairs={{0,2},{2,0},{1,3},{3,1},{4,6},{6,4},{5,7},{7,5},{8,10},{10,8},{9,1... | collective-permute-start | bytes 393224 | tf_op jit(solution)/shard_map/ppermute | solution.py:204
  4.2 4.0 %collective-permute-start = (bf16[16,32,128]{2,1,0:T(8,128)(2,1)S(1)}, bf16[16,32,128]{2,1,0:T(8,128)(2,1)S(1)}, u32[]{:S(2)}, u32[]{:S(2)}) collective-permute-start(bf16[16,32,128]{2,1,0:T(8,128)(2,1)S(1)} %shard_map.55.refs_0_), channel_id=1, source_target_pairs={{0,1},{1,0},{2,3},{3,2},{4,5},{5,4},{6,7},{7,6},{8,9},{9,8},{10,11... | collective-permute-start | bytes 393224 | tf_op jit(solution)/shard_map/ppermute | solution.py:204
  4.2 1.0 %copy-start.2 = (f32[9,64,64]{2,1,0:T(8,128)S(1)}, f32[9,64,64]{2,1,0:T(8,128)}, u32[]{:S(2)}) copy-start(f32[9,64,64]{2,1,0:T(8,128)} %first_ref.1) | copy-start | bytes 442372
  5.1 1.0 %copy-start.3 = (f32[9,64,64]{2,1,0:T(8,128)S(1)}, f32[9,64,64]{2,1,0:T(8,128)}, u32[]{:S(2)}) copy-start(f32[9,64,64]{2,1,0:T(8,128)} %second_ref.1) | copy-start | bytes 442372
  6.1 0.9 %copy-start.4 = (bf16[256,384]{1,0:T(8,128)(2,1)S(1)}, bf16[256,384]{1,0:T(8,128)(2,1)}, u32[]{:S(2)}) copy-start(bf16[256,384]{1,0:T(8,128)(2,1)} %embed_ref.1) | copy-start | bytes 589828
  7.7 1.5 %collective-permute-start.2 = (bf16[16,32,128]{2,1,0:T(8,128)(2,1)S(1)}, bf16[16,32,128]{2,1,0:T(8,128)(2,1)S(1)}, u32[]{:S(2)}, u32[]{:S(2)}) collective-permute-start(bf16[16,32,128]{2,1,0:T(8,128)(2,1)S(1)} %collective-permute-done.1.refs_2_), channel_id=1, source_target_pairs={{0,1},{1,0},{2,3},{3,2},{4,5},{5,4},{6,7},{7,6},{8,9},{9,8},{10,11... | collective-permute-start | bytes 393224 | tf_op jit(solution)/shard_map/ppermute | solution.py:204
  9.2 6.3 %collective-permute-start.3 = (bf16[1,128,128]{2,1,0:T(8,128)(2,1)S(1)}, bf16[1,128,128]{2,1,0:T(8,128)(2,1)S(1)}, u32[]{:S(2)}, u32[]{:S(2)}) collective-permute-start(bf16[1,128,128]{2,1,0:T(8,128)(2,1)S(1)} %get-tuple-element.31), channel_id=1, source_target_pairs={{0,4},{4,8},{8,12},{12,0},{1,5},{5,9},{9,13},{13,1},{2,6},{6,10},{... | collective-permute-start | bytes 98312 | tf_op jit(solution)/shard_map/ppermute | solution.py:204
  10.9 4.6 %collective-permute-start.4 = (bf16[1,128,128]{2,1,0:T(8,128)(2,1)S(1)}, bf16[1,128,128]{2,1,0:T(8,128)(2,1)S(1)}, u32[]{:S(2)}, u32[]{:S(2)}) collective-permute-start(bf16[1,128,128]{2,1,0:T(8,128)(2,1)S(1)} %get-tuple-element.32), channel_id=1, source_target_pairs={{0,12},{4,0},{8,4},{12,8},{1,13},{5,1},{9,5},{13,9},{2,14},{6,2},{... | collective-permute-start | bytes 98312 | tf_op jit(solution)/shard_map/ppermute | solution.py:204
  13.1 3.6 %copy-start = (bf16[1024,4096]{1,0:T(8,128)(2,1)S(1)}, bf16[1024,4096]{1,0:T(8,128)(2,1)}, u32[]{:S(2)}) copy-start(bf16[1024,4096]{1,0:T(8,128)(2,1)} %mixing_ref.15) | copy-start | bytes 25165828
  17.2 8.7 %collective-permute-start.5 = (bf16[96,1024]{1,0:T(8,128)(2,1)S(1)}, bf16[96,1024]{1,0:T(8,128)(2,1)S(1)}, u32[]{:S(2)}, u32[]{:S(2)}) collective-permute-start(bf16[96,1024]{1,0:T(8,128)(2,1)S(1)} %shard_map.60), channel_id=1, source_target_pairs={{0,12},{4,0},{8,4},{12,8},{1,13},{5,1},{9,5},{13,9},{2,14},{6,2},{... | collective-permute-start | bytes 589832 | tf_op jit(solution)/shard_map/ppermute | solution.py:204
  21.1 10.0 %collective-permute-start.8 = (bf16[96,1024]{1,0:T(8,128)(2,1)S(1)}, bf16[96,1024]{1,0:T(8,128)(2,1)S(1)}, u32[]{:S(2)}, u32[]{:S(2)}) collective-permute-start(bf16[96,1024]{1,0:T(8,128)(2,1)S(1)} %shard_map.62), channel_id=1, source_target_pairs={{0,12},{4,0},{8,4},{12,8},{1,13},{5,1},{9,5},{13,9},{2,14},{6,2},{... | collective-permute-start | bytes 589832 | tf_op jit(solution)/shard_map/ppermute | solution.py:204
  21.6 13.6 %collective-permute-start.11 = (bf16[96,1024]{1,0:T(8,128)(2,1)S(1)}, bf16[96,1024]{1,0:T(8,128)(2,1)S(1)}, u32[]{:S(2)}, u32[]{:S(2)}) collective-permute-start(bf16[96,1024]{1,0:T(8,128)(2,1)S(1)} %shard_map.64), channel_id=1, source_target_pairs={{0,12},{4,0},{8,4},{12,8},{1,13},{5,1},{9,5},{13,9},{2,14},{6,2},{... | collective-permute-start | bytes 589832 | tf_op jit(solution)/shard_map/ppermute | solution.py:204
  22.6 16.9 %collective-permute-start.14 = (bf16[96,1024]{1,0:T(8,128)(2,1)S(1)}, bf16[96,1024]{1,0:T(8,128)(2,1)S(1)}, u32[]{:S(2)}, u32[]{:S(2)}) collective-permute-start(bf16[96,1024]{1,0:T(8,128)(2,1)S(1)} %shard_map.66), channel_id=1, source_target_pairs={{0,12},{4,0},{8,4},{12,8},{1,13},{5,1},{9,5},{13,9},{2,14},{6,2},{... | collective-permute-start | bytes 589832 | tf_op jit(solution)/shard_map/ppermute | solution.py:204
  26.7 17.0 %collective-permute-start.6 = (bf16[96,1024]{1,0:T(8,128)(2,1)S(1)}, bf16[96,1024]{1,0:T(8,128)(2,1)S(1)}, u32[]{:S(2)}, u32[]{:S(2)}) collective-permute-start(bf16[96,1024]{1,0:T(8,128)(2,1)S(1)} %get-tuple-element.39), channel_id=1, source_target_pairs={{0,12},{4,0},{8,4},{12,8},{1,13},{5,1},{9,5},{13,9},{2,14},{6,2},{... | collective-permute-start | bytes 589832 | tf_op jit(solution)/shard_map/ppermute | solution.py:204
  31.8 15.3 %collective-permute-start.9 = (bf16[96,1024]{1,0:T(8,128)(2,1)S(1)}, bf16[96,1024]{1,0:T(8,128)(2,1)S(1)}, u32[]{:S(2)}, u32[]{:S(2)}) collective-permute-start(bf16[96,1024]{1,0:T(8,128)(2,1)S(1)} %get-tuple-element.41), channel_id=1, source_target_pairs={{0,12},{4,0},{8,4},{12,8},{1,13},{5,1},{9,5},{13,9},{2,14},{6,2},{... | collective-permute-start | bytes 589832 | tf_op jit(solution)/shard_map/ppermute | solution.py:204
  36.0 15.3 %collective-permute-start.12 = (bf16[96,1024]{1,0:T(8,128)(2,1)S(1)}, bf16[96,1024]{1,0:T(8,128)(2,1)S(1)}, u32[]{:S(2)}, u32[]{:S(2)}) collective-permute-start(bf16[96,1024]{1,0:T(8,128)(2,1)S(1)} %get-tuple-element.43), channel_id=1, source_target_pairs={{0,12},{4,0},{8,4},{12,8},{1,13},{5,1},{9,5},{13,9},{2,14},{6,2},{... | collective-permute-start | bytes 589832 | tf_op jit(solution)/shard_map/ppermute | solution.py:204
  40.3 15.3 %collective-permute-start.15 = (bf16[96,1024]{1,0:T(8,128)(2,1)S(1)}, bf16[96,1024]{1,0:T(8,128)(2,1)S(1)}, u32[]{:S(2)}, u32[]{:S(2)}) collective-permute-start(bf16[96,1024]{1,0:T(8,128)(2,1)S(1)} %get-tuple-element.45), channel_id=1, source_target_pairs={{0,12},{4,0},{8,4},{12,8},{1,13},{5,1},{9,5},{13,9},{2,14},{6,2},{... | collective-permute-start | bytes 589832 | tf_op jit(solution)/shard_map/ppermute | solution.py:204
  43.7 16.1 %collective-permute-start.7 = (bf16[96,1024]{1,0:T(8,128)(2,1)S(1)}, bf16[96,1024]{1,0:T(8,128)(2,1)S(1)}, u32[]{:S(2)}, u32[]{:S(2)}) collective-permute-start(bf16[96,1024]{1,0:T(8,128)(2,1)S(1)} %add_convert_fusion.3), channel_id=1, source_target_pairs={{0,12},{4,0},{8,4},{12,8},{1,13},{5,1},{9,5},{13,9},{2,14},{6,2},{... | collective-permute-start | bytes 589832 | tf_op jit(solution)/shard_map/ppermute | solution.py:204
  47.2 16.6 %collective-permute-start.10 = (bf16[96,1024]{1,0:T(8,128)(2,1)S(1)}, bf16[96,1024]{1,0:T(8,128)(2,1)S(1)}, u32[]{:S(2)}, u32[]{:S(2)}) collective-permute-start(bf16[96,1024]{1,0:T(8,128)(2,1)S(1)} %add_convert_fusion.2), channel_id=1, source_target_pairs={{0,12},{4,0},{8,4},{12,8},{1,13},{5,1},{9,5},{13,9},{2,14},{6,2},{... | collective-permute-start | bytes 589832 | tf_op jit(solution)/shard_map/ppermute | solution.py:204
  51.4 16.6 %collective-permute-start.13 = (bf16[96,1024]{1,0:T(8,128)(2,1)S(1)}, bf16[96,1024]{1,0:T(8,128)(2,1)S(1)}, u32[]{:S(2)}, u32[]{:S(2)}) collective-permute-start(bf16[96,1024]{1,0:T(8,128)(2,1)S(1)} %add_convert_fusion.1), channel_id=1, source_target_pairs={{0,12},{4,0},{8,4},{12,8},{1,13},{5,1},{9,5},{13,9},{2,14},{6,2},{... | collective-permute-start | bytes 589832 | tf_op jit(solution)/shard_map/ppermute | solution.py:204
  55.6 14.7 %collective-permute-start.16 = (bf16[96,1024]{1,0:T(8,128)(2,1)S(1)}, bf16[96,1024]{1,0:T(8,128)(2,1)S(1)}, u32[]{:S(2)}, u32[]{:S(2)}) collective-permute-start(bf16[96,1024]{1,0:T(8,128)(2,1)S(1)} %add_convert_fusion), channel_id=1, source_target_pairs={{0,12},{4,0},{8,4},{12,8},{1,13},{5,1},{9,5},{13,9},{2,14},{6,2},{... | collective-permute-start | bytes 589832 | tf_op jit(solution)/shard_map/ppermute | solution.py:204

commit v13 on v12

--- a/solution.py
+++ b/solution.py
@@ -262,19 +262,19 @@
     )
 
 
-def sent_kernel(first, tokens_ref, mixing_ref, sent_ref):
+def sent_kernel(first, block, tokens_ref, mixing_ref, sent_ref):
     rows, width = sent_ref.shape
     step = STEP if width % STEP == 0 else width
-    tokens = tokens_ref[:rows]
+    tokens = tokens_ref[pl.ds(block * rows, rows), :]
     for at in range(0, width, step):
         product = dot(tokens, mixing_ref[:, pl.ds(first + at, step)])
         sent_ref[:, pl.ds(at, step)] = product.astype(sent_ref.dtype)
 
 
-def hop_kernel(first, arrived_ref, tokens_ref, mixing_ref, sent_ref, kept_ref):
+def hop_kernel(first, blocks, arrived_ref, tokens_ref, mixing_ref, sent_ref, kept_ref):
     rows, width = sent_ref.shape
     step = STEP if width % STEP == 0 else width
-    tokens = tokens_ref[rows:]
+    tokens = jnp.concatenate([tokens_ref[pl.ds(block * rows, rows), :] for block in blocks], axis=0)
     for at in range(0, width, step):
         product = dot(tokens, mixing_ref[:, pl.ds(first + at, step)])
         arrived = arrived_ref[:, pl.ds(at, step)].astype(jnp.float32)
@@ -288,16 +288,19 @@
     rows = embed // count
     width = token_mixing.shape[1] // pieces
     sent = jax.ShapeDtypeStruct((rows, width), jnp.bfloat16)
+    ways = [1 if piece % 2 == 0 else -1 for piece in range(pieces)]
+    blocks = [list(range(count - 2, -1, -1)) if way == 1 else list(range(count - 1)) for way in ways]
     travelling = [
-        call(functools.partial(sent_kernel, piece * width), sent, (tokens, token_mixing)) for piece in range(pieces)
+        call(functools.partial(sent_kernel, piece * width, blocks[piece][0]), sent, (tokens, token_mixing))
+        for piece in range(pieces)
     ]
     kept = [None] * pieces
     for step in range(1, count):
         for piece in range(pieces):
-            arrived = turned(travelling[piece], "tok", -1)
+            arrived = turned(travelling[piece], "tok", ways[piece])
             if step == 1:
                 travelling[piece], kept[piece] = call(
-                    functools.partial(hop_kernel, piece * width),
+                    functools.partial(hop_kernel, piece * width, blocks[piece][1:] + [count - 1]),
                     [sent, jax.ShapeDtypeStruct((embed - 2 * rows, width), jnp.float32)],
                     (arrived, tokens, token_mixing),
                 )

time: 71.6 us -> 72.2 us (level)
  waiting for transfers between devices: 13.4 us -> 33.1 us
  starting transfers between devices: 43.2 us -> 24 us
    ppermute x17, waiting for transfers between devices: 13.4 us -> 33.1 us  [turned(): lax.ppermute(value, axis, [(i, (i + away) % count) for i in range(count)])]
    ppermute x17, starting transfers between devices: 43.2 us -> 24 us  [turned(): lax.ppermute(value, axis, [(i, (i + away) % count) for i in range(count)])]
  transfers between devices with their start and end apart: 17 -> 17, of which waited for: 5 -> 13; matrix products, arithmetic and copies ran while one was open for 1% -> 1% of each run, Pallas kernels for 10% -> 10%
where the time goes in v13:
time: 72.2 us; the launch traced here: 71.9 us
  waiting for transfers between devices  33.1 us (46%)
  starting transfers between devices  24 us (33%)
  Pallas kernels  9.27 us (13%)
  local copies, waits for them, and re-layouts  3.89 us (5%)
  other arithmetic  1.5 us (2%)
    ppermute x17, waiting for transfers between devices, turned(): lax.ppermute(value, axis, [(i, (i + away) % count) for i in range(count)])  33.1 us
    ppermute x17, starting transfers between devices, turned(): lax.ppermute(value, axis, [(i, (i + away) % count) for i in range(count)])  24 us
    pallas_call x13, Pallas kernels, call(): pl.pallas_call(kernel, out_shape=out_shape, in_specs=[pl.BlockSpec(memory...  9.27 us
    unnamed x10, local copies, waits for them, and re-layouts  3.89 us
  transfers between devices with their start and end apart: 17, of which 13 were waited for; matrix products, arithmetic and copies ran while one was open for 1% of the time, Pallas kernels for 10%

profile of v13, /device:TPU:0, one launch (start us, length us, event | category | flops | bytes accessed | tf_op | source)
XLA Modules:
  0.0 71.9 jit_solution(1780041447407782969)
XLA Ops:
  0.0 1.0 %copy-done.1 = f32[64,32,32]{0,2,1:T(8,128)S(1)} copy-done((f32[64,32,32]{0,2,1:T(8,128)S(1)}, f32[64,32,32]{0,2,1:T(8,128)}, u32[]{:S(2)}) %copy-start.1) | copy-done | bytes 262168
  1.0 0.1 shard_map.55.refs_0_
  1.2 3.0 %collective-permute-start.1 = (bf16[16,32,128]{2,1,0:T(8,128)(2,1)S(1)}, bf16[16,32,128]{2,1,0:T(8,128)(2,1)S(1)}, u32[]{:S(2)}, u32[]{:S(2)}) collective-permute-start(bf16[16,32,128]{2,1,0:T(8,128)(2,1)S(1)} %shard_map.55.refs_0_), channel_id=1, source_target_pairs={{0,2},{2,0},{1,3},{3,1},{4,6},{6,4},{5,7},{7,5},{8,10},{10,8},{9,1... | collective-permute-start | bytes 393224 | tf_op jit(solution)/shard_map/ppermute | solution.py:204
  4.2 1.0 %copy-done.2 = f32[9,64,64]{2,1,0:T(8,128)S(1)} copy-done((f32[9,64,64]{2,1,0:T(8,128)S(1)}, f32[9,64,64]{2,1,0:T(8,128)}, u32[]{:S(2)}) %copy-start.2) | copy-done | bytes 147480
  5.1 1.0 %copy-done.3 = f32[9,64,64]{2,1,0:T(8,128)S(1)} copy-done((f32[9,64,64]{2,1,0:T(8,128)S(1)}, f32[9,64,64]{2,1,0:T(8,128)}, u32[]{:S(2)}) %copy-start.3) | copy-done | bytes 147480
  6.1 0.9 %copy-done.4 = bf16[256,384]{1,0:T(8,128)(2,1)S(1)} copy-done((bf16[256,384]{1,0:T(8,128)(2,1)S(1)}, bf16[256,384]{1,0:T(8,128)(2,1)}, u32[]{:S(2)}) %copy-start.4) | copy-done | bytes 196632
  7.0 0.6 shard_map.56
  7.7 0.5 collective-permute-start.2
  8.2 1.0 %collective-permute-done.2.refs_3_ = bf16[16,32,128]{2,1,0:T(8,128)(2,1)S(1)} collective-permute-done((bf16[16,32,128]{2,1,0:T(8,128)(2,1)S(1)}, bf16[16,32,128]{2,1,0:T(8,128)(2,1)S(1)}, u32[]{:S(2)}, u32[]{:S(2)}) %collective-permute-start.2) | collective-permute-done | bytes 131104 | tf_op jit(solution)/shard_map/ppermute | solution.py:204
  9.2 1.7 %collective-permute-start.3 = (bf16[1,128,128]{2,1,0:T(8,128)(2,1)S(1)}, bf16[1,128,128]{2,1,0:T(8,128)(2,1)S(1)}, u32[]{:S(2)}, u32[]{:S(2)}) collective-permute-start(bf16[1,128,128]{2,1,0:T(8,128)(2,1)S(1)} %get-tuple-element.31), channel_id=1, source_target_pairs={{0,4},{4,8},{8,12},{12,0},{1,5},{5,9},{9,13},{13,1},{2,6},{6,10},{... | collective-permute-start | bytes 98312 | tf_op jit(solution)/shard_map/ppermute | solution.py:204
  10.9 2.2 %collective-permute-start.4 = (bf16[1,128,128]{2,1,0:T(8,128)(2,1)S(1)}, bf16[1,128,128]{2,1,0:T(8,128)(2,1)S(1)}, u32[]{:S(2)}, u32[]{:S(2)}) collective-permute-start(bf16[1,128,128]{2,1,0:T(8,128)(2,1)S(1)} %get-tuple-element.32), channel_id=1, source_target_pairs={{0,12},{4,0},{8,4},{12,8},{1,13},{5,1},{9,5},{13,9},{2,14},{6,2},{... | collective-permute-start | bytes 98312 | tf_op jit(solution)/shard_map/ppermute | solution.py:204
  13.1 2.4 %shard_map.58 = (bf16[384,768]{1,0:T(8,128)(2,1)S(1)}, bf16[4,128,128]{2,1,0:T(8,128)(2,1)S(1)}, bf16[4,128,128]{2,1,0:T(8,128)(2,1)S(1)}) custom-call(bf16[16,128,128]{2,1,0:T(8,128)(2,1)S(1)} %get-tuple-element.30.field_ref, bf16[256,768]{1,0:T(8,128)(2,1)S(1)} %get-tuple-element.33.taps_one_ref, bf16[256,768]{1,0:T(8,128)(2,1)S(1)} %get-tuple-element.34.taps_two_ref, ...), custom_call_target="tpu_custom_call" | custom-call | flops 1635778560 | bytes 524288 | tf_op jit(solution)/shard_map/pallas_call | solution.py:191
  15.5 1.2 %shard_map.59.tokens_ref = bf16[384,1024]{1,0:T(8,128)(2,1)S(1)} custom-call(bf16[16,128,128]{2,1,0:T(8,128)(2,1)S(1)} %get-tuple-element.30.field_ref, bf16[1,128,128]{2,1,0:T(8,128)(2,1)S(1)} %collective-permute-done.3.before_ref, bf16[1,128,128]{2,1,0:T(8,128)(2,1)S(1)} %collective-permute-done.4.after_ref, ...), custom_call_target="tpu_custom_call" | custom-call | flops 503316480 | bytes 524288 | tf_op jit(solution)/shard_map/pallas_call | solution.py:191
  16.8 0.5 shard_map.60
  17.2 0.9 %collective-permute-start.5 = (bf16[96,1024]{1,0:T(8,128)(2,1)S(1)}, bf16[96,1024]{1,0:T(8,128)(2,1)S(1)}, u32[]{:S(2)}, u32[]{:S(2)}) collective-permute-start(bf16[96,1024]{1,0:T(8,128)(2,1)S(1)} %shard_map.60), channel_id=1, source_target_pairs={{0,4},{4,8},{8,12},{12,0},{1,5},{5,9},{9,13},{13,1},{2,6},{6,10},{... | collective-permute-start | bytes 589832 | tf_op jit(solution)/shard_map/ppermute | solution.py:204
  18.2 0.5 shard_map.62
  18.6 3.0 %collective-permute-start.8 = (bf16[96,1024]{1,0:T(8,128)(2,1)S(1)}, bf16[96,1024]{1,0:T(8,128)(2,1)S(1)}, u32[]{:S(2)}, u32[]{:S(2)}) collective-permute-start(bf16[96,1024]{1,0:T(8,128)(2,1)S(1)} %shard_map.62), channel_id=1, source_target_pairs={{0,12},{4,0},{8,4},{12,8},{1,13},{5,1},{9,5},{13,9},{2,14},{6,2},{... | collective-permute-start | bytes 589832 | tf_op jit(solution)/shard_map/ppermute | solution.py:204
  21.6 0.5 shard_map.64
  22.2 0.5 shard_map.66
  22.6 3.9 %collective-permute-start.14 = (bf16[96,1024]{1,0:T(8,128)(2,1)S(1)}, bf16[96,1024]{1,0:T(8,128)(2,1)S(1)}, u32[]{:S(2)}, u32[]{:S(2)}) collective-permute-start(bf16[96,1024]{1,0:T(8,128)(2,1)S(1)} %shard_map.66), channel_id=1, source_target_pairs={{0,12},{4,0},{8,4},{12,8},{1,13},{5,1},{9,5},{13,9},{2,14},{6,2},{... | collective-permute-start | bytes 589832 | tf_op jit(solution)/shard_map/ppermute | solution.py:204
  26.5 0.4 collective-permute-done.5.arrived_ref
  26.9 0.8 %shard_map.61 = (bf16[96,1024]{1,0:T(8,128)(2,1)S(1)}, f32[192,1024]{1,0:T(8,128)S(1)}) custom-call(bf16[96,1024]{1,0:T(8,128)(2,1)S(1)} %collective-permute-done.5.arrived_ref, bf16[384,1024]{1,0:T(8,128)(2,1)S(1)} %shard_map.59.tokens_ref, bf16[1024,4096]{1,0:T(8,128)(2,1)S(1)} %copy-done), custom_call_target="tpu_custom_call" | custom-call | tf_op jit(solution)/shard_map/pallas_call | solution.py:191
  27.6 1.2 %collective-permute-start.6 = (bf16[96,1024]{1,0:T(8,128)(2,1)S(1)}, bf16[96,1024]{1,0:T(8,128)(2,1)S(1)}, u32[]{:S(2)}, u32[]{:S(2)}) collective-permute-start(bf16[96,1024]{1,0:T(8,128)(2,1)S(1)} %get-tuple-element.39), channel_id=1, source_target_pairs={{0,4},{4,8},{8,12},{12,0},{1,5},{5,9},{9,13},{13,1},{2,6},{6,10},{... | collective-permute-start | bytes 589832 | tf_op jit(solution)/shard_map/ppermute | solution.py:204
  28.8 4.7 %collective-permute-done.8.arrived_ref = bf16[96,1024]{1,0:T(8,128)(2,1)S(1)} collective-permute-done((bf16[96,1024]{1,0:T(8,128)(2,1)S(1)}, bf16[96,1024]{1,0:T(8,128)(2,1)S(1)}, u32[]{:S(2)}, u32[]{:S(2)}) %collective-permute-start.8) | collective-permute-done | bytes 196640 | tf_op jit(solution)/shard_map/ppermute | solution.py:204
  33.5 0.8 %shard_map.63 = (bf16[96,1024]{1,0:T(8,128)(2,1)S(1)}, f32[192,1024]{1,0:T(8,128)S(1)}) custom-call(bf16[96,1024]{1,0:T(8,128)(2,1)S(1)} %collective-permute-done.8.arrived_ref, bf16[384,1024]{1,0:T(8,128)(2,1)S(1)} %shard_map.59.tokens_ref, bf16[1024,4096]{1,0:T(8,128)(2,1)S(1)} %copy-done), custom_call_target="tpu_custom_call" | custom-call | tf_op jit(solution)/shard_map/pallas_call | solution.py:191
  34.4 1.0 %collective-permute-done.11.arrived_ref = bf16[96,1024]{1,0:T(8,128)(2,1)S(1)} collective-permute-done((bf16[96,1024]{1,0:T(8,128)(2,1)S(1)}, bf16[96,1024]{1,0:T(8,128)(2,1)S(1)}, u32[]{:S(2)}, u32[]{:S(2)}) %collective-permute-start.11) | collective-permute-done | bytes 196640 | tf_op jit(solution)/shard_map/ppermute | solution.py:204
  35.3 0.8 %shard_map.65 = (bf16[96,1024]{1,0:T(8,128)(2,1)S(1)}, f32[192,1024]{1,0:T(8,128)S(1)}) custom-call(bf16[96,1024]{1,0:T(8,128)(2,1)S(1)} %collective-permute-done.11.arrived_ref, bf16[384,1024]{1,0:T(8,128)(2,1)S(1)} %shard_map.59.tokens_ref, bf16[1024,4096]{1,0:T(8,128)(2,1)S(1)} %copy-done), custom_call_target="tpu_custom_call" | custom-call | tf_op jit(solution)/shard_map/pallas_call | solution.py:191
  36.1 1.1 %collective-permute-start.12 = (bf16[96,1024]{1,0:T(8,128)(2,1)S(1)}, bf16[96,1024]{1,0:T(8,128)(2,1)S(1)}, u32[]{:S(2)}, u32[]{:S(2)}) collective-permute-start(bf16[96,1024]{1,0:T(8,128)(2,1)S(1)} %get-tuple-element.43), channel_id=1, source_target_pairs={{0,4},{4,8},{8,12},{12,0},{1,5},{5,9},{9,13},{13,1},{2,6},{6,10},{... | collective-permute-start | bytes 589832 | tf_op jit(solution)/shard_map/ppermute | solution.py:204
  37.2 2.7 %collective-permute-done.14.arrived_ref = bf16[96,1024]{1,0:T(8,128)(2,1)S(1)} collective-permute-done((bf16[96,1024]{1,0:T(8,128)(2,1)S(1)}, bf16[96,1024]{1,0:T(8,128)(2,1)S(1)}, u32[]{:S(2)}, u32[]{:S(2)}) %collective-permute-start.14) | collective-permute-done | bytes 196640 | tf_op jit(solution)/shard_map/ppermute | solution.py:204
  39.9 0.8 %shard_map.67 = (bf16[96,1024]{1,0:T(8,128)(2,1)S(1)}, f32[192,1024]{1,0:T(8,128)S(1)}) custom-call(bf16[96,1024]{1,0:T(8,128)(2,1)S(1)} %collective-permute-done.14.arrived_ref, bf16[384,1024]{1,0:T(8,128)(2,1)S(1)} %shard_map.59.tokens_ref, bf16[1024,4096]{1,0:T(8,128)(2,1)S(1)} %copy-done), custom_call_target="tpu_custom_call" | custom-call | tf_op jit(solution)/shard_map/pallas_call | solution.py:191
  40.6 1.9 %collective-permute-start.15 = (bf16[96,1024]{1,0:T(8,128)(2,1)S(1)}, bf16[96,1024]{1,0:T(8,128)(2,1)S(1)}, u32[]{:S(2)}, u32[]{:S(2)}) collective-permute-start(bf16[96,1024]{1,0:T(8,128)(2,1)S(1)} %get-tuple-element.45), channel_id=1, source_target_pairs={{0,12},{4,0},{8,4},{12,8},{1,13},{5,1},{9,5},{13,9},{2,14},{6,2},{... | collective-permute-start | bytes 589832 | tf_op jit(solution)/shard_map/ppermute | solution.py:204
  42.5 1.3 %collective-permute-done.6 = bf16[96,1024]{1,0:T(8,128)(2,1)S(1)} collective-permute-done((bf16[96,1024]{1,0:T(8,128)(2,1)S(1)}, bf16[96,1024]{1,0:T(8,128)(2,1)S(1)}, u32[]{:S(2)}, u32[]{:S(2)}) %collective-permute-start.6) | collective-permute-done | bytes 196640 | tf_op jit(solution)/shard_map/ppermute | solution.py:204
  43.8 1.0 %collective-permute-start.7 = (bf16[96,1024]{1,0:T(8,128)(2,1)S(1)}, bf16[96,1024]{1,0:T(8,128)(2,1)S(1)}, u32[]{:S(2)}, u32[]{:S(2)}) collective-permute-start(bf16[96,1024]{1,0:T(8,128)(2,1)S(1)} %add_convert_fusion.3), channel_id=1, source_target_pairs={{0,4},{4,8},{8,12},{12,0},{1,5},{5,9},{9,13},{13,1},{2,6},{6,10},{... | collective-permute-start | bytes 589832 | tf_op jit(solution)/shard_map/ppermute | solution.py:204
  44.8 3.3 %collective-permute-done.9 = bf16[96,1024]{1,0:T(8,128)(2,1)S(1)} collective-permute-done((bf16[96,1024]{1,0:T(8,128)(2,1)S(1)}, bf16[96,1024]{1,0:T(8,128)(2,1)S(1)}, u32[]{:S(2)}, u32[]{:S(2)}) %collective-permute-start.9) | collective-permute-done | bytes 196640 | tf_op jit(solution)/shard_map/ppermute | solution.py:204
  48.1 1.3 %collective-permute-start.10 = (bf16[96,1024]{1,0:T(8,128)(2,1)S(1)}, bf16[96,1024]{1,0:T(8,128)(2,1)S(1)}, u32[]{:S(2)}, u32[]{:S(2)}) collective-permute-start(bf16[96,1024]{1,0:T(8,128)(2,1)S(1)} %add_convert_fusion.2), channel_id=1, source_target_pairs={{0,12},{4,0},{8,4},{12,8},{1,13},{5,1},{9,5},{13,9},{2,14},{6,2},{... | collective-permute-start | bytes 589832 | tf_op jit(solution)/shard_map/ppermute | solution.py:204
  49.5 2.8 %collective-permute-done.12 = bf16[96,1024]{1,0:T(8,128)(2,1)S(1)} collective-permute-done((bf16[96,1024]{1,0:T(8,128)(2,1)S(1)}, bf16[96,1024]{1,0:T(8,128)(2,1)S(1)}, u32[]{:S(2)}, u32[]{:S(2)}) %collective-permute-start.12) | collective-permute-done | bytes 196640 | tf_op jit(solution)/shard_map/ppermute | solution.py:204
  52.3 0.9 %collective-permute-start.13 = (bf16[96,1024]{1,0:T(8,128)(2,1)S(1)}, bf16[96,1024]{1,0:T(8,128)(2,1)S(1)}, u32[]{:S(2)}, u32[]{:S(2)}) collective-permute-start(bf16[96,1024]{1,0:T(8,128)(2,1)S(1)} %add_convert_fusion.1), channel_id=1, source_target_pairs={{0,4},{4,8},{8,12},{12,0},{1,5},{5,9},{9,13},{13,1},{2,6},{6,10},{... | collective-permute-start | bytes 589832 | tf_op jit(solution)/shard_map/ppermute | solution.py:204
  53.2 3.3 %collective-permute-done.15 = bf16[96,1024]{1,0:T(8,128)(2,1)S(1)} collective-permute-done((bf16[96,1024]{1,0:T(8,128)(2,1)S(1)}, bf16[96,1024]{1,0:T(8,128)(2,1)S(1)}, u32[]{:S(2)}, u32[]{:S(2)}) %collective-permute-start.15) | collective-permute-done | bytes 196640 | tf_op jit(solution)/shard_map/ppermute | solution.py:204
  56.6 1.3 %collective-permute-start.16 = (bf16[96,1024]{1,0:T(8,128)(2,1)S(1)}, bf16[96,1024]{1,0:T(8,128)(2,1)S(1)}, u32[]{:S(2)}, u32[]{:S(2)}) collective-permute-start(bf16[96,1024]{1,0:T(8,128)(2,1)S(1)} %add_convert_fusion), channel_id=1, source_target_pairs={{0,12},{4,0},{8,4},{12,8},{1,13},{5,1},{9,5},{13,9},{2,14},{6,2},{... | collective-permute-start | bytes 589832 | tf_op jit(solution)/shard_map/ppermute | solution.py:204
  57.9 2.8 %collective-permute-done.7 = bf16[96,1024]{1,0:T(8,128)(2,1)S(1)} collective-permute-done((bf16[96,1024]{1,0:T(8,128)(2,1)S(1)}, bf16[96,1024]{1,0:T(8,128)(2,1)S(1)}, u32[]{:S(2)}, u32[]{:S(2)}) %collective-permute-start.7) | collective-permute-done | bytes 196640 | tf_op jit(solution)/shard_map/ppermute | solution.py:204
  60.7 0.1 multiply_convert_fusion.3
  60.8 4.1 %collective-permute-done.10 = bf16[96,1024]{1,0:T(8,128)(2,1)S(1)} collective-permute-done((bf16[96,1024]{1,0:T(8,128)(2,1)S(1)}, bf16[96,1024]{1,0:T(8,128)(2,1)S(1)}, u32[]{:S(2)}, u32[]{:S(2)}) %collective-permute-start.10) | collective-permute-done | bytes 196640 | tf_op jit(solution)/shard_map/ppermute | solution.py:204
  64.9 0.1 multiply_convert_fusion.2
  65.0 4.2 %collective-permute-done.13 = bf16[96,1024]{1,0:T(8,128)(2,1)S(1)} collective-permute-done((bf16[96,1024]{1,0:T(8,128)(2,1)S(1)}, bf16[96,1024]{1,0:T(8,128)(2,1)S(1)}, u32[]{:S(2)}, u32[]{:S(2)}) %collective-permute-start.13) | collective-permute-done | bytes 196640 | tf_op jit(solution)/shard_map/ppermute | solution.py:204
  69.2 0.1 multiply_convert_fusion.1
  69.3 1.6 %collective-permute-done.16 = bf16[96,1024]{1,0:T(8,128)(2,1)S(1)} collective-permute-done((bf16[96,1024]{1,0:T(8,128)(2,1)S(1)}, bf16[96,1024]{1,0:T(8,128)(2,1)S(1)}, u32[]{:S(2)}, u32[]{:S(2)}) %collective-permute-start.16) | collective-permute-done | bytes 196640 | tf_op jit(solution)/shard_map/ppermute | solution.py:204
  70.9 0.1 multiply_convert_fusion
  71.0 0.9 %pad_maximum_fusion = bf16[96,4096]{1,0:T(8,128)(2,1)} fusion(bf16[96,1024]{1,0:T(8,128)(2,1)S(1)} %multiply_convert_fusion, bf16[96,1024]{1,0:T(8,128)(2,1)S(1)} %multiply_convert_fusion.1, bf16[96,1024]{1,0:T(8,128)(2,1)S(1)} %multiply_convert_fusion.2, bf16[96,1024]{1,0:T(8,128)(2,1)S(1)} %multiply_convert_fusion.3), kind=kLoop, calls=%fused_computation | loop fusion | flops 3145728 | bytes 1572864 | tf_op jit(solution)/shard_map/concatenate | solution.py:313
  (18 shorter events, 0.4 us)
Async XLA Ops:
  0.0 1.0 %copy-start.1 = (f32[64,32,32]{0,2,1:T(8,128)S(1)}, f32[64,32,32]{0,2,1:T(8,128)}, u32[]{:S(2)}) copy-start(f32[64,32,32]{0,2,1:T(8,128)} %param.5) | copy-start | bytes 786436
  1.2 6.5 %collective-permute-start.1 = (bf16[16,32,128]{2,1,0:T(8,128)(2,1)S(1)}, bf16[16,32,128]{2,1,0:T(8,128)(2,1)S(1)}, u32[]{:S(2)}, u32[]{:S(2)}) collective-permute-start(bf16[16,32,128]{2,1,0:T(8,128)(2,1)S(1)} %shard_map.55.refs_0_), channel_id=1, source_target_pairs={{0,2},{2,0},{1,3},{3,1},{4,6},{6,4},{5,7},{7,5},{8,10},{10,8},{9,1... | collective-permute-start | bytes 393224 | tf_op jit(solution)/shard_map/ppermute | solution.py:204
  4.2 4.0 %collective-permute-start = (bf16[16,32,128]{2,1,0:T(8,128)(2,1)S(1)}, bf16[16,32,128]{2,1,0:T(8,128)(2,1)S(1)}, u32[]{:S(2)}, u32[]{:S(2)}) collective-permute-start(bf16[16,32,128]{2,1,0:T(8,128)(2,1)S(1)} %shard_map.55.refs_0_), channel_id=1, source_target_pairs={{0,1},{1,0},{2,3},{3,2},{4,5},{5,4},{6,7},{7,6},{8,9},{9,8},{10,11... | collective-permute-start | bytes 393224 | tf_op jit(solution)/shard_map/ppermute | solution.py:204
  4.2 1.0 %copy-start.2 = (f32[9,64,64]{2,1,0:T(8,128)S(1)}, f32[9,64,64]{2,1,0:T(8,128)}, u32[]{:S(2)}) copy-start(f32[9,64,64]{2,1,0:T(8,128)} %first_ref.1) | copy-start | bytes 442372
  5.1 1.0 %copy-start.3 = (f32[9,64,64]{2,1,0:T(8,128)S(1)}, f32[9,64,64]{2,1,0:T(8,128)}, u32[]{:S(2)}) copy-start(f32[9,64,64]{2,1,0:T(8,128)} %second_ref.1) | copy-start | bytes 442372
  6.1 0.9 %copy-start.4 = (bf16[256,384]{1,0:T(8,128)(2,1)S(1)}, bf16[256,384]{1,0:T(8,128)(2,1)}, u32[]{:S(2)}) copy-start(bf16[256,384]{1,0:T(8,128)(2,1)} %embed_ref.1) | copy-start | bytes 589828
  7.7 1.5 %collective-permute-start.2 = (bf16[16,32,128]{2,1,0:T(8,128)(2,1)S(1)}, bf16[16,32,128]{2,1,0:T(8,128)(2,1)S(1)}, u32[]{:S(2)}, u32[]{:S(2)}) collective-permute-start(bf16[16,32,128]{2,1,0:T(8,128)(2,1)S(1)} %collective-permute-done.1.refs_2_), channel_id=1, source_target_pairs={{0,1},{1,0},{2,3},{3,2},{4,5},{5,4},{6,7},{7,6},{8,9},{9,8},{10,11... | collective-permute-start | bytes 393224 | tf_op jit(solution)/shard_map/ppermute | solution.py:204
  9.2 6.3 %collective-permute-start.3 = (bf16[1,128,128]{2,1,0:T(8,128)(2,1)S(1)}, bf16[1,128,128]{2,1,0:T(8,128)(2,1)S(1)}, u32[]{:S(2)}, u32[]{:S(2)}) collective-permute-start(bf16[1,128,128]{2,1,0:T(8,128)(2,1)S(1)} %get-tuple-element.31), channel_id=1, source_target_pairs={{0,4},{4,8},{8,12},{12,0},{1,5},{5,9},{9,13},{13,1},{2,6},{6,10},{... | collective-permute-start | bytes 98312 | tf_op jit(solution)/shard_map/ppermute | solution.py:204
  10.9 4.6 %collective-permute-start.4 = (bf16[1,128,128]{2,1,0:T(8,128)(2,1)S(1)}, bf16[1,128,128]{2,1,0:T(8,128)(2,1)S(1)}, u32[]{:S(2)}, u32[]{:S(2)}) collective-permute-start(bf16[1,128,128]{2,1,0:T(8,128)(2,1)S(1)} %get-tuple-element.32), channel_id=1, source_target_pairs={{0,12},{4,0},{8,4},{12,8},{1,13},{5,1},{9,5},{13,9},{2,14},{6,2},{... | collective-permute-start | bytes 98312 | tf_op jit(solution)/shard_map/ppermute | solution.py:204
  13.1 3.6 %copy-start = (bf16[1024,4096]{1,0:T(8,128)(2,1)S(1)}, bf16[1024,4096]{1,0:T(8,128)(2,1)}, u32[]{:S(2)}) copy-start(bf16[1024,4096]{1,0:T(8,128)(2,1)} %mixing_ref.15) | copy-start | bytes 25165828
  17.2 9.6 %collective-permute-start.5 = (bf16[96,1024]{1,0:T(8,128)(2,1)S(1)}, bf16[96,1024]{1,0:T(8,128)(2,1)S(1)}, u32[]{:S(2)}, u32[]{:S(2)}) collective-permute-start(bf16[96,1024]{1,0:T(8,128)(2,1)S(1)} %shard_map.60), channel_id=1, source_target_pairs={{0,4},{4,8},{8,12},{12,0},{1,5},{5,9},{9,13},{13,1},{2,6},{6,10},{... | collective-permute-start | bytes 589832 | tf_op jit(solution)/shard_map/ppermute | solution.py:204
  18.6 14.9 %collective-permute-start.8 = (bf16[96,1024]{1,0:T(8,128)(2,1)S(1)}, bf16[96,1024]{1,0:T(8,128)(2,1)S(1)}, u32[]{:S(2)}, u32[]{:S(2)}) collective-permute-start(bf16[96,1024]{1,0:T(8,128)(2,1)S(1)} %shard_map.62), channel_id=1, source_target_pairs={{0,12},{4,0},{8,4},{12,8},{1,13},{5,1},{9,5},{13,9},{2,14},{6,2},{... | collective-permute-start | bytes 589832 | tf_op jit(solution)/shard_map/ppermute | solution.py:204
  22.1 13.2 %collective-permute-start.11 = (bf16[96,1024]{1,0:T(8,128)(2,1)S(1)}, bf16[96,1024]{1,0:T(8,128)(2,1)S(1)}, u32[]{:S(2)}, u32[]{:S(2)}) collective-permute-start(bf16[96,1024]{1,0:T(8,128)(2,1)S(1)} %shard_map.64), channel_id=1, source_target_pairs={{0,4},{4,8},{8,12},{12,0},{1,5},{5,9},{9,13},{13,1},{2,6},{6,10},{... | collective-permute-start | bytes 589832 | tf_op jit(solution)/shard_map/ppermute | solution.py:204
  22.6 17.2 %collective-permute-start.14 = (bf16[96,1024]{1,0:T(8,128)(2,1)S(1)}, bf16[96,1024]{1,0:T(8,128)(2,1)S(1)}, u32[]{:S(2)}, u32[]{:S(2)}) collective-permute-start(bf16[96,1024]{1,0:T(8,128)(2,1)S(1)} %shard_map.66), channel_id=1, source_target_pairs={{0,12},{4,0},{8,4},{12,8},{1,13},{5,1},{9,5},{13,9},{2,14},{6,2},{... | collective-permute-start | bytes 589832 | tf_op jit(solution)/shard_map/ppermute | solution.py:204
  27.6 16.2 %collective-permute-start.6 = (bf16[96,1024]{1,0:T(8,128)(2,1)S(1)}, bf16[96,1024]{1,0:T(8,128)(2,1)S(1)}, u32[]{:S(2)}, u32[]{:S(2)}) collective-permute-start(bf16[96,1024]{1,0:T(8,128)(2,1)S(1)} %get-tuple-element.39), channel_id=1, source_target_pairs={{0,4},{4,8},{8,12},{12,0},{1,5},{5,9},{9,13},{13,1},{2,6},{6,10},{... | collective-permute-start | bytes 589832 | tf_op jit(solution)/shard_map/ppermute | solution.py:204
  34.3 13.8 %collective-permute-start.9 = (bf16[96,1024]{1,0:T(8,128)(2,1)S(1)}, bf16[96,1024]{1,0:T(8,128)(2,1)S(1)}, u32[]{:S(2)}, u32[]{:S(2)}) collective-permute-start(bf16[96,1024]{1,0:T(8,128)(2,1)S(1)} %get-tuple-element.41), channel_id=1, source_target_pairs={{0,12},{4,0},{8,4},{12,8},{1,13},{5,1},{9,5},{13,9},{2,14},{6,2},{... | collective-permute-start | bytes 589832 | tf_op jit(solution)/shard_map/ppermute | solution.py:204
  36.1 16.2 %collective-permute-start.12 = (bf16[96,1024]{1,0:T(8,128)(2,1)S(1)}, bf16[96,1024]{1,0:T(8,128)(2,1)S(1)}, u32[]{:S(2)}, u32[]{:S(2)}) collective-permute-start(bf16[96,1024]{1,0:T(8,128)(2,1)S(1)} %get-tuple-element.43), channel_id=1, source_target_pairs={{0,4},{4,8},{8,12},{12,0},{1,5},{5,9},{9,13},{13,1},{2,6},{6,10},{... | collective-permute-start | bytes 589832 | tf_op jit(solution)/shard_map/ppermute | solution.py:204
  40.6 15.9 %collective-permute-start.15 = (bf16[96,1024]{1,0:T(8,128)(2,1)S(1)}, bf16[96,1024]{1,0:T(8,128)(2,1)S(1)}, u32[]{:S(2)}, u32[]{:S(2)}) collective-permute-start(bf16[96,1024]{1,0:T(8,128)(2,1)S(1)} %get-tuple-element.45), channel_id=1, source_target_pairs={{0,12},{4,0},{8,4},{12,8},{1,13},{5,1},{9,5},{13,9},{2,14},{6,2},{... | collective-permute-start | bytes 589832 | tf_op jit(solution)/shard_map/ppermute | solution.py:204
  43.8 16.9 %collective-permute-start.7 = (bf16[96,1024]{1,0:T(8,128)(2,1)S(1)}, bf16[96,1024]{1,0:T(8,128)(2,1)S(1)}, u32[]{:S(2)}, u32[]{:S(2)}) collective-permute-start(bf16[96,1024]{1,0:T(8,128)(2,1)S(1)} %add_convert_fusion.3), channel_id=1, source_target_pairs={{0,4},{4,8},{8,12},{12,0},{1,5},{5,9},{9,13},{13,1},{2,6},{6,10},{... | collective-permute-start | bytes 589832 | tf_op jit(solution)/shard_map/ppermute | solution.py:204
  48.1 16.8 %collective-permute-start.10 = (bf16[96,1024]{1,0:T(8,128)(2,1)S(1)}, bf16[96,1024]{1,0:T(8,128)(2,1)S(1)}, u32[]{:S(2)}, u32[]{:S(2)}) collective-permute-start(bf16[96,1024]{1,0:T(8,128)(2,1)S(1)} %add_convert_fusion.2), channel_id=1, source_target_pairs={{0,12},{4,0},{8,4},{12,8},{1,13},{5,1},{9,5},{13,9},{2,14},{6,2},{... | collective-permute-start | bytes 589832 | tf_op jit(solution)/shard_map/ppermute | solution.py:204
  52.3 16.9 %collective-permute-start.13 = (bf16[96,1024]{1,0:T(8,128)(2,1)S(1)}, bf16[96,1024]{1,0:T(8,128)(2,1)S(1)}, u32[]{:S(2)}, u32[]{:S(2)}) collective-permute-start(bf16[96,1024]{1,0:T(8,128)(2,1)S(1)} %add_convert_fusion.1), channel_id=1, source_target_pairs={{0,4},{4,8},{8,12},{12,0},{1,5},{5,9},{9,13},{13,1},{2,6},{6,10},{... | collective-permute-start | bytes 589832 | tf_op jit(solution)/shard_map/ppermute | solution.py:204
  56.6 14.3 %collective-permute-start.16 = (bf16[96,1024]{1,0:T(8,128)(2,1)S(1)}, bf16[96,1024]{1,0:T(8,128)(2,1)S(1)}, u32[]{:S(2)}, u32[]{:S(2)}) collective-permute-start(bf16[96,1024]{1,0:T(8,128)(2,1)S(1)} %add_convert_fusion), channel_id=1, source_target_pairs={{0,12},{4,0},{8,4},{12,8},{1,13},{5,1},{9,5},{13,9},{2,14},{6,2},{... | collective-permute-start | bytes 589832 | tf_op jit(solution)/shard_map/ppermute | solution.py:204

commit v14 on v13

--- a/solution.py
+++ b/solution.py
@@ -10,6 +10,7 @@
 PIECES = 4
 STEP = 256
 LANES = 128
+WRITES = 4
 VMEM_BYTES = 24 * 1024 * 1024
 ROWS_AT_ONCE = 1024
 
@@ -282,6 +283,41 @@
         kept_ref[:, pl.ds(at, step)] = product[rows:]
 
 
+def last_kernel(first, arrived_ref, kept_ref, *refs):
+    result_ref, held_ref, written = refs[-3:]
+    rows, width = arrived_ref.shape
+    part = width // written.shape[0]
+    copies = []
+    for at in range(written.shape[0]):
+        here = pl.ds(at * part, part)
+        own = kept_ref[kept_ref.shape[0] - rows :, at * part : (at + 1) * part]
+        held_ref[:, here] = gelu(arrived_ref[:, here].astype(jnp.float32) + own).astype(held_ref.dtype)
+        target = result_ref.at[:, pl.ds(first + at * part, part)]
+        copies.append(pltpu.make_async_copy(held_ref.at[:, here], target, written.at[at]))
+        copies[-1].start()
+    for copy in copies:
+        copy.wait()
+
+
+def finish(first, arrived, kept, result, columns):
+    rows, width = arrived.shape
+    near, far = pl.BlockSpec(memory_space=pltpu.VMEM), pl.BlockSpec(memory_space=pl.ANY)
+    earlier = [] if result is None else [result]
+    return pl.pallas_call(
+        functools.partial(last_kernel, first),
+        out_shape=jax.ShapeDtypeStruct((rows, columns), jnp.bfloat16),
+        in_specs=[near, near] + [far] * len(earlier),
+        out_specs=far,
+        input_output_aliases={2: 0} if earlier else {},
+        scratch_shapes=[
+            pltpu.VMEM((rows, width), jnp.bfloat16),
+            pltpu.SemaphoreType.DMA((WRITES if width % (WRITES * LANES) == 0 else 1,)),
+        ],
+        compiler_params=pltpu.CompilerParams(vmem_limit_bytes=VMEM_BYTES),
+        cost_estimate=pl.CostEstimate(flops=0, bytes_accessed=0, transcendentals=0),
+    )(arrived, kept, *earlier)
+
+
 def lift(tokens, token_mixing, pieces):
     count = lax.axis_size("tok")
     embed = tokens.shape[0]
@@ -295,6 +331,7 @@
         for piece in range(pieces)
     ]
     kept = [None] * pieces
+    result = None
     for step in range(1, count):
         for piece in range(pieces):
             arrived = turned(travelling[piece], "tok", ways[piece])
@@ -304,13 +341,13 @@
                     [sent, jax.ShapeDtypeStruct((embed - 2 * rows, width), jnp.float32)],
                     (arrived, tokens, token_mixing),
                 )
-            else:
+            elif step < count - 1:
                 at = (step - 2) * rows
                 summed = arrived.astype(jnp.float32) + kept[piece][at : at + rows]
-                if step == count - 1:
-                    summed = gelu(summed)
                 travelling[piece] = summed.astype(jnp.bfloat16)
-    return jnp.concatenate(travelling, axis=1)
+            else:
+                result = finish(piece * width, arrived, kept[piece], result, pieces * width)
+    return result
 
 
 def local(weather, conv_first, conv_second, patch_embed, token_mixing):

time: 72.2 us -> 72 us (level)
  Pallas kernels: 9.27 us -> 12.3 us
  waiting for transfers between devices: 33.1 us -> 31.1 us
  other arithmetic: 1.5 us -> 0.16 us
    pallas_call x0 -> x4, Pallas kernels: none -> 3.03 us  [finish(): pl.pallas_call(functools.partial(last_kernel, first), out_shape=jax.Shape...]
    ppermute x17, waiting for transfers between devices: 33.1 us -> 31.1 us  [turned(): lax.ppermute(value, axis, [(i, (i + away) % count) for i in range(count)])]
    concatenate x1 -> x0, other arithmetic: 0.94 us -> none  [lift(): return jnp.concatenate(travelling, axis=1)]
  transfers between devices with their start and end apart: 17 -> 17, of which waited for: 13 -> 13; matrix products, arithmetic and copies ran while one was open for 1% -> 0% of each run, Pallas kernels for 10% -> 14%
where the time goes in v14:
time: 72 us; the launch traced here: 71.8 us
  waiting for transfers between devices  31.1 us (43%)
  starting transfers between devices  24 us (33%)
  Pallas kernels  12.3 us (17%)
  local copies, waits for them, and re-layouts  4.04 us (6%)
    ppermute x17, waiting for transfers between devices, turned(): lax.ppermute(value, axis, [(i, (i + away) % count) for i in range(count)])  31.1 us
    ppermute x17, starting transfers between devices, turned(): lax.ppermute(value, axis, [(i, (i + away) % count) for i in range(count)])  24 us
    pallas_call x13, Pallas kernels, call(): pl.pallas_call(kernel, out_shape=out_shape, in_specs=[pl.BlockSpec(memory...  9.28 us
    unnamed x10, local copies, waits for them, and re-layouts  4.04 us
    pallas_call x4, Pallas kernels, finish(): pl.pallas_call(functools.partial(last_kernel, first), out_shape=jax.Shape...  3.03 us
  transfers between devices with their start and end apart: 17, of which 13 were waited for; matrix products, arithmetic and copies ran while one was open for 0% of the time, Pallas kernels for 14%

profile of v14, /device:TPU:0, one launch (start us, length us, event | category | flops | bytes accessed | tf_op | source)
XLA Modules:
  0.0 71.8 jit_solution(13294486564296829551)
XLA Ops:
  0.0 1.2 %copy-done.1 = f32[64,32,32]{0,2,1:T(8,128)S(1)} copy-done((f32[64,32,32]{0,2,1:T(8,128)S(1)}, f32[64,32,32]{0,2,1:T(8,128)}, u32[]{:S(2)}) %copy-start.1) | copy-done | bytes 262168
  1.2 0.1 shard_map.55.refs_0_
  1.3 3.0 %collective-permute-start.1 = (bf16[16,32,128]{2,1,0:T(8,128)(2,1)S(1)}, bf16[16,32,128]{2,1,0:T(8,128)(2,1)S(1)}, u32[]{:S(2)}, u32[]{:S(2)}) collective-permute-start(bf16[16,32,128]{2,1,0:T(8,128)(2,1)S(1)} %shard_map.55.refs_0_), channel_id=1, source_target_pairs={{0,2},{2,0},{1,3},{3,1},{4,6},{6,4},{5,7},{7,5},{8,10},{10,8},{9,1... | collective-permute-start | bytes 393224 | tf_op jit(solution)/shard_map/ppermute | solution.py:205
  4.3 1.0 %copy-done.2 = f32[9,64,64]{2,1,0:T(8,128)S(1)} copy-done((f32[9,64,64]{2,1,0:T(8,128)S(1)}, f32[9,64,64]{2,1,0:T(8,128)}, u32[]{:S(2)}) %copy-start.2) | copy-done | bytes 147480
  5.3 1.0 %copy-done.3 = f32[9,64,64]{2,1,0:T(8,128)S(1)} copy-done((f32[9,64,64]{2,1,0:T(8,128)S(1)}, f32[9,64,64]{2,1,0:T(8,128)}, u32[]{:S(2)}) %copy-start.3) | copy-done | bytes 147480
  6.2 0.9 %copy-done.4 = bf16[256,384]{1,0:T(8,128)(2,1)S(1)} copy-done((bf16[256,384]{1,0:T(8,128)(2,1)S(1)}, bf16[256,384]{1,0:T(8,128)(2,1)}, u32[]{:S(2)}) %copy-start.4) | copy-done | bytes 196632
  7.2 0.6 shard_map.56
  7.8 0.5 collective-permute-start.2
  8.3 1.0 %collective-permute-done.2.refs_3_ = bf16[16,32,128]{2,1,0:T(8,128)(2,1)S(1)} collective-permute-done((bf16[16,32,128]{2,1,0:T(8,128)(2,1)S(1)}, bf16[16,32,128]{2,1,0:T(8,128)(2,1)S(1)}, u32[]{:S(2)}, u32[]{:S(2)}) %collective-permute-start.2) | collective-permute-done | bytes 131104 | tf_op jit(solution)/shard_map/ppermute | solution.py:205
  9.3 0.1 shard_map.57
  9.4 1.7 %collective-permute-start.3 = (bf16[1,128,128]{2,1,0:T(8,128)(2,1)S(1)}, bf16[1,128,128]{2,1,0:T(8,128)(2,1)S(1)}, u32[]{:S(2)}, u32[]{:S(2)}) collective-permute-start(bf16[1,128,128]{2,1,0:T(8,128)(2,1)S(1)} %get-tuple-element.31), channel_id=1, source_target_pairs={{0,4},{4,8},{8,12},{12,0},{1,5},{5,9},{9,13},{13,1},{2,6},{6,10},{... | collective-permute-start | bytes 98312 | tf_op jit(solution)/shard_map/ppermute | solution.py:205
  11.1 2.2 %collective-permute-start.4 = (bf16[1,128,128]{2,1,0:T(8,128)(2,1)S(1)}, bf16[1,128,128]{2,1,0:T(8,128)(2,1)S(1)}, u32[]{:S(2)}, u32[]{:S(2)}) collective-permute-start(bf16[1,128,128]{2,1,0:T(8,128)(2,1)S(1)} %get-tuple-element.32), channel_id=1, source_target_pairs={{0,12},{4,0},{8,4},{12,8},{1,13},{5,1},{9,5},{13,9},{2,14},{6,2},{... | collective-permute-start | bytes 98312 | tf_op jit(solution)/shard_map/ppermute | solution.py:205
  13.3 2.4 %shard_map.58 = (bf16[384,768]{1,0:T(8,128)(2,1)S(1)}, bf16[4,128,128]{2,1,0:T(8,128)(2,1)S(1)}, bf16[4,128,128]{2,1,0:T(8,128)(2,1)S(1)}) custom-call(bf16[16,128,128]{2,1,0:T(8,128)(2,1)S(1)} %get-tuple-element.30.field_ref, bf16[256,768]{1,0:T(8,128)(2,1)S(1)} %get-tuple-element.33.taps_one_ref, bf16[256,768]{1,0:T(8,128)(2,1)S(1)} %get-tuple-element.34.taps_two_ref, ...), custom_call_target="tpu_custom_call" | custom-call | flops 1635778560 | bytes 524288 | tf_op jit(solution)/shard_map/pallas_call | solution.py:192
  15.7 1.2 %shard_map.59.tokens_ref = bf16[384,1024]{1,0:T(8,128)(2,1)S(1)} custom-call(bf16[16,128,128]{2,1,0:T(8,128)(2,1)S(1)} %get-tuple-element.30.field_ref, bf16[1,128,128]{2,1,0:T(8,128)(2,1)S(1)} %collective-permute-done.3.before_ref, bf16[1,128,128]{2,1,0:T(8,128)(2,1)S(1)} %collective-permute-done.4.after_ref, ...), custom_call_target="tpu_custom_call" | custom-call | flops 503316480 | bytes 524288 | tf_op jit(solution)/shard_map/pallas_call | solution.py:192
  16.9 0.5 shard_map.66
  17.4 0.9 %collective-permute-start.14 = (bf16[96,1024]{1,0:T(8,128)(2,1)S(1)}, bf16[96,1024]{1,0:T(8,128)(2,1)S(1)}, u32[]{:S(2)}, u32[]{:S(2)}) collective-permute-start(bf16[96,1024]{1,0:T(8,128)(2,1)S(1)} %shard_map.66), channel_id=1, source_target_pairs={{0,4},{4,8},{8,12},{12,0},{1,5},{5,9},{9,13},{13,1},{2,6},{6,10},{... | collective-permute-start | bytes 589832 | tf_op jit(solution)/shard_map/ppermute | solution.py:205
  18.3 0.5 shard_map.64
  18.8 3.0 %collective-permute-start.11 = (bf16[96,1024]{1,0:T(8,128)(2,1)S(1)}, bf16[96,1024]{1,0:T(8,128)(2,1)S(1)}, u32[]{:S(2)}, u32[]{:S(2)}) collective-permute-start(bf16[96,1024]{1,0:T(8,128)(2,1)S(1)} %shard_map.64), channel_id=1, source_target_pairs={{0,12},{4,0},{8,4},{12,8},{1,13},{5,1},{9,5},{13,9},{2,14},{6,2},{... | collective-permute-start | bytes 589832 | tf_op jit(solution)/shard_map/ppermute | solution.py:205
  21.8 0.5 shard_map.62
  22.3 0.5 shard_map.60
  22.8 3.9 %collective-permute-start.5 = (bf16[96,1024]{1,0:T(8,128)(2,1)S(1)}, bf16[96,1024]{1,0:T(8,128)(2,1)S(1)}, u32[]{:S(2)}, u32[]{:S(2)}) collective-permute-start(bf16[96,1024]{1,0:T(8,128)(2,1)S(1)} %shard_map.60), channel_id=1, source_target_pairs={{0,12},{4,0},{8,4},{12,8},{1,13},{5,1},{9,5},{13,9},{2,14},{6,2},{... | collective-permute-start | bytes 589832 | tf_op jit(solution)/shard_map/ppermute | solution.py:205
  26.6 0.4 collective-permute-done.14.arrived_ref
  27.0 0.8 %shard_map.67 = (bf16[96,1024]{1,0:T(8,128)(2,1)S(1)}, f32[192,1024]{1,0:T(8,128)S(1)}) custom-call(bf16[96,1024]{1,0:T(8,128)(2,1)S(1)} %collective-permute-done.14.arrived_ref, bf16[384,1024]{1,0:T(8,128)(2,1)S(1)} %shard_map.59.tokens_ref, bf16[1024,4096]{1,0:T(8,128)(2,1)S(1)} %copy-done), custom_call_target="tpu_custom_call" | custom-call | tf_op jit(solution)/shard_map/pallas_call | solution.py:192
  27.8 1.2 %collective-permute-start.15 = (bf16[96,1024]{1,0:T(8,128)(2,1)S(1)}, bf16[96,1024]{1,0:T(8,128)(2,1)S(1)}, u32[]{:S(2)}, u32[]{:S(2)}) collective-permute-start(bf16[96,1024]{1,0:T(8,128)(2,1)S(1)} %get-tuple-element.45), channel_id=1, source_target_pairs={{0,4},{4,8},{8,12},{12,0},{1,5},{5,9},{9,13},{13,1},{2,6},{6,10},{... | collective-permute-start | bytes 589832 | tf_op jit(solution)/shard_map/ppermute | solution.py:205
  29.0 4.7 %collective-permute-done.11.arrived_ref = bf16[96,1024]{1,0:T(8,128)(2,1)S(1)} collective-permute-done((bf16[96,1024]{1,0:T(8,128)(2,1)S(1)}, bf16[96,1024]{1,0:T(8,128)(2,1)S(1)}, u32[]{:S(2)}, u32[]{:S(2)}) %collective-permute-start.11) | collective-permute-done | bytes 196640 | tf_op jit(solution)/shard_map/ppermute | solution.py:205
  33.7 0.8 %shard_map.65 = (bf16[96,1024]{1,0:T(8,128)(2,1)S(1)}, f32[192,1024]{1,0:T(8,128)S(1)}) custom-call(bf16[96,1024]{1,0:T(8,128)(2,1)S(1)} %collective-permute-done.11.arrived_ref, bf16[384,1024]{1,0:T(8,128)(2,1)S(1)} %shard_map.59.tokens_ref, bf16[1024,4096]{1,0:T(8,128)(2,1)S(1)} %copy-done), custom_call_target="tpu_custom_call" | custom-call | tf_op jit(solution)/shard_map/pallas_call | solution.py:192
  34.5 1.0 %collective-permute-done.8.arrived_ref = bf16[96,1024]{1,0:T(8,128)(2,1)S(1)} collective-permute-done((bf16[96,1024]{1,0:T(8,128)(2,1)S(1)}, bf16[96,1024]{1,0:T(8,128)(2,1)S(1)}, u32[]{:S(2)}, u32[]{:S(2)}) %collective-permute-start.8) | collective-permute-done | bytes 196640 | tf_op jit(solution)/shard_map/ppermute | solution.py:205
  35.5 0.8 %shard_map.63 = (bf16[96,1024]{1,0:T(8,128)(2,1)S(1)}, f32[192,1024]{1,0:T(8,128)S(1)}) custom-call(bf16[96,1024]{1,0:T(8,128)(2,1)S(1)} %collective-permute-done.8.arrived_ref, bf16[384,1024]{1,0:T(8,128)(2,1)S(1)} %shard_map.59.tokens_ref, bf16[1024,4096]{1,0:T(8,128)(2,1)S(1)} %copy-done), custom_call_target="tpu_custom_call" | custom-call | tf_op jit(solution)/shard_map/pallas_call | solution.py:192
  36.3 1.1 %collective-permute-start.9 = (bf16[96,1024]{1,0:T(8,128)(2,1)S(1)}, bf16[96,1024]{1,0:T(8,128)(2,1)S(1)}, u32[]{:S(2)}, u32[]{:S(2)}) collective-permute-start(bf16[96,1024]{1,0:T(8,128)(2,1)S(1)} %get-tuple-element.41), channel_id=1, source_target_pairs={{0,4},{4,8},{8,12},{12,0},{1,5},{5,9},{9,13},{13,1},{2,6},{6,10},{... | collective-permute-start | bytes 589832 | tf_op jit(solution)/shard_map/ppermute | solution.py:205
  37.4 2.7 %collective-permute-done.5.arrived_ref = bf16[96,1024]{1,0:T(8,128)(2,1)S(1)} collective-permute-done((bf16[96,1024]{1,0:T(8,128)(2,1)S(1)}, bf16[96,1024]{1,0:T(8,128)(2,1)S(1)}, u32[]{:S(2)}, u32[]{:S(2)}) %collective-permute-start.5) | collective-permute-done | bytes 196640 | tf_op jit(solution)/shard_map/ppermute | solution.py:205
  40.0 0.8 %shard_map.61 = (bf16[96,1024]{1,0:T(8,128)(2,1)S(1)}, f32[192,1024]{1,0:T(8,128)S(1)}) custom-call(bf16[96,1024]{1,0:T(8,128)(2,1)S(1)} %collective-permute-done.5.arrived_ref, bf16[384,1024]{1,0:T(8,128)(2,1)S(1)} %shard_map.59.tokens_ref, bf16[1024,4096]{1,0:T(8,128)(2,1)S(1)} %copy-done), custom_call_target="tpu_custom_call" | custom-call | tf_op jit(solution)/shard_map/pallas_call | solution.py:192
  40.8 1.9 %collective-permute-start.6 = (bf16[96,1024]{1,0:T(8,128)(2,1)S(1)}, bf16[96,1024]{1,0:T(8,128)(2,1)S(1)}, u32[]{:S(2)}, u32[]{:S(2)}) collective-permute-start(bf16[96,1024]{1,0:T(8,128)(2,1)S(1)} %get-tuple-element.39), channel_id=1, source_target_pairs={{0,12},{4,0},{8,4},{12,8},{1,13},{5,1},{9,5},{13,9},{2,14},{6,2},{... | collective-permute-start | bytes 589832 | tf_op jit(solution)/shard_map/ppermute | solution.py:205
  42.7 1.3 %collective-permute-done.15 = bf16[96,1024]{1,0:T(8,128)(2,1)S(1)} collective-permute-done((bf16[96,1024]{1,0:T(8,128)(2,1)S(1)}, bf16[96,1024]{1,0:T(8,128)(2,1)S(1)}, u32[]{:S(2)}, u32[]{:S(2)}) %collective-permute-start.15) | collective-permute-done | bytes 196640 | tf_op jit(solution)/shard_map/ppermute | solution.py:205
  44.0 1.0 %collective-permute-start.16 = (bf16[96,1024]{1,0:T(8,128)(2,1)S(1)}, bf16[96,1024]{1,0:T(8,128)(2,1)S(1)}, u32[]{:S(2)}, u32[]{:S(2)}) collective-permute-start(bf16[96,1024]{1,0:T(8,128)(2,1)S(1)} %add_convert_fusion), channel_id=1, source_target_pairs={{0,4},{4,8},{8,12},{12,0},{1,5},{5,9},{9,13},{13,1},{2,6},{6,10},{... | collective-permute-start | bytes 589832 | tf_op jit(solution)/shard_map/ppermute | solution.py:205
  45.0 3.3 %collective-permute-done.12 = bf16[96,1024]{1,0:T(8,128)(2,1)S(1)} collective-permute-done((bf16[96,1024]{1,0:T(8,128)(2,1)S(1)}, bf16[96,1024]{1,0:T(8,128)(2,1)S(1)}, u32[]{:S(2)}, u32[]{:S(2)}) %collective-permute-start.12) | collective-permute-done | bytes 196640 | tf_op jit(solution)/shard_map/ppermute | solution.py:205
  48.3 1.3 %collective-permute-start.13 = (bf16[96,1024]{1,0:T(8,128)(2,1)S(1)}, bf16[96,1024]{1,0:T(8,128)(2,1)S(1)}, u32[]{:S(2)}, u32[]{:S(2)}) collective-permute-start(bf16[96,1024]{1,0:T(8,128)(2,1)S(1)} %add_convert_fusion.1), channel_id=1, source_target_pairs={{0,12},{4,0},{8,4},{12,8},{1,13},{5,1},{9,5},{13,9},{2,14},{6,2},{... | collective-permute-start | bytes 589832 | tf_op jit(solution)/shard_map/ppermute | solution.py:205
  49.6 2.8 %collective-permute-done.9 = bf16[96,1024]{1,0:T(8,128)(2,1)S(1)} collective-permute-done((bf16[96,1024]{1,0:T(8,128)(2,1)S(1)}, bf16[96,1024]{1,0:T(8,128)(2,1)S(1)}, u32[]{:S(2)}, u32[]{:S(2)}) %collective-permute-start.9) | collective-permute-done | bytes 196640 | tf_op jit(solution)/shard_map/ppermute | solution.py:205
  52.5 0.9 %collective-permute-start.10 = (bf16[96,1024]{1,0:T(8,128)(2,1)S(1)}, bf16[96,1024]{1,0:T(8,128)(2,1)S(1)}, u32[]{:S(2)}, u32[]{:S(2)}) collective-permute-start(bf16[96,1024]{1,0:T(8,128)(2,1)S(1)} %add_convert_fusion.2), channel_id=1, source_target_pairs={{0,4},{4,8},{8,12},{12,0},{1,5},{5,9},{9,13},{13,1},{2,6},{6,10},{... | collective-permute-start | bytes 589832 | tf_op jit(solution)/shard_map/ppermute | solution.py:205
  53.4 3.3 %collective-permute-done.6 = bf16[96,1024]{1,0:T(8,128)(2,1)S(1)} collective-permute-done((bf16[96,1024]{1,0:T(8,128)(2,1)S(1)}, bf16[96,1024]{1,0:T(8,128)(2,1)S(1)}, u32[]{:S(2)}, u32[]{:S(2)}) %collective-permute-start.6) | collective-permute-done | bytes 196640 | tf_op jit(solution)/shard_map/ppermute | solution.py:205
  56.7 1.3 %collective-permute-start.7 = (bf16[96,1024]{1,0:T(8,128)(2,1)S(1)}, bf16[96,1024]{1,0:T(8,128)(2,1)S(1)}, u32[]{:S(2)}, u32[]{:S(2)}) collective-permute-start(bf16[96,1024]{1,0:T(8,128)(2,1)S(1)} %add_convert_fusion.3), channel_id=1, source_target_pairs={{0,12},{4,0},{8,4},{12,8},{1,13},{5,1},{9,5},{13,9},{2,14},{6,2},{... | collective-permute-start | bytes 589832 | tf_op jit(solution)/shard_map/ppermute | solution.py:205
  58.1 2.8 %collective-permute-done.16.arrived_ref = bf16[96,1024]{1,0:T(8,128)(2,1)S(1)} collective-permute-done((bf16[96,1024]{1,0:T(8,128)(2,1)S(1)}, bf16[96,1024]{1,0:T(8,128)(2,1)S(1)}, u32[]{:S(2)}, u32[]{:S(2)}) %collective-permute-start.16) | collective-permute-done | bytes 196640 | tf_op jit(solution)/shard_map/ppermute | solution.py:205
  60.9 0.8 %shard_map.68.refs_0_ = bf16[96,4096]{1,0:T(8,128)(2,1)} custom-call(bf16[96,1024]{1,0:T(8,128)(2,1)S(1)} %collective-permute-done.16.arrived_ref, f32[192,1024]{1,0:T(8,128)S(1)} %get-tuple-element.46.kept_ref), custom_call_target="tpu_custom_call" | custom-call | tf_op jit(solution)/shard_map/pallas_call | solution.py:306
  61.7 3.4 %collective-permute-done.13.arrived_ref = bf16[96,1024]{1,0:T(8,128)(2,1)S(1)} collective-permute-done((bf16[96,1024]{1,0:T(8,128)(2,1)S(1)}, bf16[96,1024]{1,0:T(8,128)(2,1)S(1)}, u32[]{:S(2)}, u32[]{:S(2)}) %collective-permute-start.13) | collective-permute-done | bytes 196640 | tf_op jit(solution)/shard_map/ppermute | solution.py:205
  65.1 0.8 %shard_map.69.refs_0_ = bf16[96,4096]{1,0:T(8,128)(2,1)} custom-call(bf16[96,1024]{1,0:T(8,128)(2,1)S(1)} %collective-permute-done.13.arrived_ref, f32[192,1024]{1,0:T(8,128)S(1)} %get-tuple-element.44.kept_ref, bf16[96,4096]{1,0:T(8,128)(2,1)} %shard_map.68.refs_0_), custom_call_target="tpu_custom_call", output_to_operand_aliasing={{}: (2, {})} | custom-call | tf_op jit(solution)/shard_map/pallas_call | solution.py:306
  65.9 3.5 %collective-permute-done.10.arrived_ref = bf16[96,1024]{1,0:T(8,128)(2,1)S(1)} collective-permute-done((bf16[96,1024]{1,0:T(8,128)(2,1)S(1)}, bf16[96,1024]{1,0:T(8,128)(2,1)S(1)}, u32[]{:S(2)}, u32[]{:S(2)}) %collective-permute-start.10) | collective-permute-done | bytes 196640 | tf_op jit(solution)/shard_map/ppermute | solution.py:205
  69.4 0.8 %shard_map.70.refs_0_ = bf16[96,4096]{1,0:T(8,128)(2,1)} custom-call(bf16[96,1024]{1,0:T(8,128)(2,1)S(1)} %collective-permute-done.10.arrived_ref, f32[192,1024]{1,0:T(8,128)S(1)} %get-tuple-element.42.kept_ref, bf16[96,4096]{1,0:T(8,128)(2,1)} %shard_map.69.refs_0_), custom_call_target="tpu_custom_call", output_to_operand_aliasing={{}: (2, {})} | custom-call | tf_op jit(solution)/shard_map/pallas_call | solution.py:306
  70.1 0.9 %collective-permute-done.7.arrived_ref = bf16[96,1024]{1,0:T(8,128)(2,1)S(1)} collective-permute-done((bf16[96,1024]{1,0:T(8,128)(2,1)S(1)}, bf16[96,1024]{1,0:T(8,128)(2,1)S(1)}, u32[]{:S(2)}, u32[]{:S(2)}) %collective-permute-start.7) | collective-permute-done | bytes 196640 | tf_op jit(solution)/shard_map/ppermute | solution.py:205
  71.0 0.8 %shard_map.71 = bf16[96,4096]{1,0:T(8,128)(2,1)} custom-call(bf16[96,1024]{1,0:T(8,128)(2,1)S(1)} %collective-permute-done.7.arrived_ref, f32[192,1024]{1,0:T(8,128)S(1)} %get-tuple-element.40.kept_ref, bf16[96,4096]{1,0:T(8,128)(2,1)} %shard_map.70.refs_0_), custom_call_target="tpu_custom_call", output_to_operand_aliasing={{}: (2, {})} | custom-call | tf_op jit(solution)/shard_map/pallas_call | solution.py:306
  (17 shorter events, 0.3 us)
Async XLA Ops:
  0.0 16.9 %copy-start = (bf16[1024,4096]{1,0:T(8,128)(2,1)S(1)}, bf16[1024,4096]{1,0:T(8,128)(2,1)}, u32[]{:S(2)}) copy-start(bf16[1024,4096]{1,0:T(8,128)(2,1)} %mixing_ref.15) | copy-start | bytes 25165828
  0.0 1.2 %copy-start.1 = (f32[64,32,32]{0,2,1:T(8,128)S(1)}, f32[64,32,32]{0,2,1:T(8,128)}, u32[]{:S(2)}) copy-start(f32[64,32,32]{0,2,1:T(8,128)} %param.5) | copy-start | bytes 786436
  1.3 6.5 %collective-permute-start.1 = (bf16[16,32,128]{2,1,0:T(8,128)(2,1)S(1)}, bf16[16,32,128]{2,1,0:T(8,128)(2,1)S(1)}, u32[]{:S(2)}, u32[]{:S(2)}) collective-permute-start(bf16[16,32,128]{2,1,0:T(8,128)(2,1)S(1)} %shard_map.55.refs_0_), channel_id=1, source_target_pairs={{0,2},{2,0},{1,3},{3,1},{4,6},{6,4},{5,7},{7,5},{8,10},{10,8},{9,1... | collective-permute-start | bytes 393224 | tf_op jit(solution)/shard_map/ppermute | solution.py:205
  4.3 4.0 %collective-permute-start = (bf16[16,32,128]{2,1,0:T(8,128)(2,1)S(1)}, bf16[16,32,128]{2,1,0:T(8,128)(2,1)S(1)}, u32[]{:S(2)}, u32[]{:S(2)}) collective-permute-start(bf16[16,32,128]{2,1,0:T(8,128)(2,1)S(1)} %shard_map.55.refs_0_), channel_id=1, source_target_pairs={{0,1},{1,0},{2,3},{3,2},{4,5},{5,4},{6,7},{7,6},{8,9},{9,8},{10,11... | collective-permute-start | bytes 393224 | tf_op jit(solution)/shard_map/ppermute | solution.py:205
  4.3 1.0 %copy-start.2 = (f32[9,64,64]{2,1,0:T(8,128)S(1)}, f32[9,64,64]{2,1,0:T(8,128)}, u32[]{:S(2)}) copy-start(f32[9,64,64]{2,1,0:T(8,128)} %first_ref.1) | copy-start | bytes 442372
  5.3 1.0 %copy-start.3 = (f32[9,64,64]{2,1,0:T(8,128)S(1)}, f32[9,64,64]{2,1,0:T(8,128)}, u32[]{:S(2)}) copy-start(f32[9,64,64]{2,1,0:T(8,128)} %second_ref.1) | copy-start | bytes 442372
  6.2 0.9 %copy-start.4 = (bf16[256,384]{1,0:T(8,128)(2,1)S(1)}, bf16[256,384]{1,0:T(8,128)(2,1)}, u32[]{:S(2)}) copy-start(bf16[256,384]{1,0:T(8,128)(2,1)} %embed_ref.1) | copy-start | bytes 589828
  7.8 1.5 %collective-permute-start.2 = (bf16[16,32,128]{2,1,0:T(8,128)(2,1)S(1)}, bf16[16,32,128]{2,1,0:T(8,128)(2,1)S(1)}, u32[]{:S(2)}, u32[]{:S(2)}) collective-permute-start(bf16[16,32,128]{2,1,0:T(8,128)(2,1)S(1)} %collective-permute-done.1.refs_2_), channel_id=1, source_target_pairs={{0,1},{1,0},{2,3},{3,2},{4,5},{5,4},{6,7},{7,6},{8,9},{9,8},{10,11... | collective-permute-start | bytes 393224 | tf_op jit(solution)/shard_map/ppermute | solution.py:205
  9.4 6.3 %collective-permute-start.3 = (bf16[1,128,128]{2,1,0:T(8,128)(2,1)S(1)}, bf16[1,128,128]{2,1,0:T(8,128)(2,1)S(1)}, u32[]{:S(2)}, u32[]{:S(2)}) collective-permute-start(bf16[1,128,128]{2,1,0:T(8,128)(2,1)S(1)} %get-tuple-element.31), channel_id=1, source_target_pairs={{0,4},{4,8},{8,12},{12,0},{1,5},{5,9},{9,13},{13,1},{2,6},{6,10},{... | collective-permute-start | bytes 98312 | tf_op jit(solution)/shard_map/ppermute | solution.py:205
  11.1 4.6 %collective-permute-start.4 = (bf16[1,128,128]{2,1,0:T(8,128)(2,1)S(1)}, bf16[1,128,128]{2,1,0:T(8,128)(2,1)S(1)}, u32[]{:S(2)}, u32[]{:S(2)}) collective-permute-start(bf16[1,128,128]{2,1,0:T(8,128)(2,1)S(1)} %get-tuple-element.32), channel_id=1, source_target_pairs={{0,12},{4,0},{8,4},{12,8},{1,13},{5,1},{9,5},{13,9},{2,14},{6,2},{... | collective-permute-start | bytes 98312 | tf_op jit(solution)/shard_map/ppermute | solution.py:205
  17.4 9.6 %collective-permute-start.14 = (bf16[96,1024]{1,0:T(8,128)(2,1)S(1)}, bf16[96,1024]{1,0:T(8,128)(2,1)S(1)}, u32[]{:S(2)}, u32[]{:S(2)}) collective-permute-start(bf16[96,1024]{1,0:T(8,128)(2,1)S(1)} %shard_map.66), channel_id=1, source_target_pairs={{0,4},{4,8},{8,12},{12,0},{1,5},{5,9},{9,13},{13,1},{2,6},{6,10},{... | collective-permute-start | bytes 589832 | tf_op jit(solution)/shard_map/ppermute | solution.py:205
  18.8 14.9 %collective-permute-start.11 = (bf16[96,1024]{1,0:T(8,128)(2,1)S(1)}, bf16[96,1024]{1,0:T(8,128)(2,1)S(1)}, u32[]{:S(2)}, u32[]{:S(2)}) collective-permute-start(bf16[96,1024]{1,0:T(8,128)(2,1)S(1)} %shard_map.64), channel_id=1, source_target_pairs={{0,12},{4,0},{8,4},{12,8},{1,13},{5,1},{9,5},{13,9},{2,14},{6,2},{... | collective-permute-start | bytes 589832 | tf_op jit(solution)/shard_map/ppermute | solution.py:205
  22.2 13.2 %collective-permute-start.8 = (bf16[96,1024]{1,0:T(8,128)(2,1)S(1)}, bf16[96,1024]{1,0:T(8,128)(2,1)S(1)}, u32[]{:S(2)}, u32[]{:S(2)}) collective-permute-start(bf16[96,1024]{1,0:T(8,128)(2,1)S(1)} %shard_map.62), channel_id=1, source_target_pairs={{0,4},{4,8},{8,12},{12,0},{1,5},{5,9},{9,13},{13,1},{2,6},{6,10},{... | collective-permute-start | bytes 589832 | tf_op jit(solution)/shard_map/ppermute | solution.py:205
  22.8 17.2 %collective-permute-start.5 = (bf16[96,1024]{1,0:T(8,128)(2,1)S(1)}, bf16[96,1024]{1,0:T(8,128)(2,1)S(1)}, u32[]{:S(2)}, u32[]{:S(2)}) collective-permute-start(bf16[96,1024]{1,0:T(8,128)(2,1)S(1)} %shard_map.60), channel_id=1, source_target_pairs={{0,12},{4,0},{8,4},{12,8},{1,13},{5,1},{9,5},{13,9},{2,14},{6,2},{... | collective-permute-start | bytes 589832 | tf_op jit(solution)/shard_map/ppermute | solution.py:205
  27.8 16.2 %collective-permute-start.15 = (bf16[96,1024]{1,0:T(8,128)(2,1)S(1)}, bf16[96,1024]{1,0:T(8,128)(2,1)S(1)}, u32[]{:S(2)}, u32[]{:S(2)}) collective-permute-start(bf16[96,1024]{1,0:T(8,128)(2,1)S(1)} %get-tuple-element.45), channel_id=1, source_target_pairs={{0,4},{4,8},{8,12},{12,0},{1,5},{5,9},{9,13},{13,1},{2,6},{6,10},{... | collective-permute-start | bytes 589832 | tf_op jit(solution)/shard_map/ppermute | solution.py:205
  34.4 13.8 %collective-permute-start.12 = (bf16[96,1024]{1,0:T(8,128)(2,1)S(1)}, bf16[96,1024]{1,0:T(8,128)(2,1)S(1)}, u32[]{:S(2)}, u32[]{:S(2)}) collective-permute-start(bf16[96,1024]{1,0:T(8,128)(2,1)S(1)} %get-tuple-element.43), channel_id=1, source_target_pairs={{0,12},{4,0},{8,4},{12,8},{1,13},{5,1},{9,5},{13,9},{2,14},{6,2},{... | collective-permute-start | bytes 589832 | tf_op jit(solution)/shard_map/ppermute | solution.py:205
  36.3 16.2 %collective-permute-start.9 = (bf16[96,1024]{1,0:T(8,128)(2,1)S(1)}, bf16[96,1024]{1,0:T(8,128)(2,1)S(1)}, u32[]{:S(2)}, u32[]{:S(2)}) collective-permute-start(bf16[96,1024]{1,0:T(8,128)(2,1)S(1)} %get-tuple-element.41), channel_id=1, source_target_pairs={{0,4},{4,8},{8,12},{12,0},{1,5},{5,9},{9,13},{13,1},{2,6},{6,10},{... | collective-permute-start | bytes 589832 | tf_op jit(solution)/shard_map/ppermute | solution.py:205
  40.8 15.9 %collective-permute-start.6 = (bf16[96,1024]{1,0:T(8,128)(2,1)S(1)}, bf16[96,1024]{1,0:T(8,128)(2,1)S(1)}, u32[]{:S(2)}, u32[]{:S(2)}) collective-permute-start(bf16[96,1024]{1,0:T(8,128)(2,1)S(1)} %get-tuple-element.39), channel_id=1, source_target_pairs={{0,12},{4,0},{8,4},{12,8},{1,13},{5,1},{9,5},{13,9},{2,14},{6,2},{... | collective-permute-start | bytes 589832 | tf_op jit(solution)/shard_map/ppermute | solution.py:205
  44.0 16.9 %collective-permute-start.16 = (bf16[96,1024]{1,0:T(8,128)(2,1)S(1)}, bf16[96,1024]{1,0:T(8,128)(2,1)S(1)}, u32[]{:S(2)}, u32[]{:S(2)}) collective-permute-start(bf16[96,1024]{1,0:T(8,128)(2,1)S(1)} %add_convert_fusion), channel_id=1, source_target_pairs={{0,4},{4,8},{8,12},{12,0},{1,5},{5,9},{9,13},{13,1},{2,6},{6,10},{... | collective-permute-start | bytes 589832 | tf_op jit(solution)/shard_map/ppermute | solution.py:205
  48.3 16.8 %collective-permute-start.13 = (bf16[96,1024]{1,0:T(8,128)(2,1)S(1)}, bf16[96,1024]{1,0:T(8,128)(2,1)S(1)}, u32[]{:S(2)}, u32[]{:S(2)}) collective-permute-start(bf16[96,1024]{1,0:T(8,128)(2,1)S(1)} %add_convert_fusion.1), channel_id=1, source_target_pairs={{0,12},{4,0},{8,4},{12,8},{1,13},{5,1},{9,5},{13,9},{2,14},{6,2},{... | collective-permute-start | bytes 589832 | tf_op jit(solution)/shard_map/ppermute | solution.py:205
  52.5 16.9 %collective-permute-start.10 = (bf16[96,1024]{1,0:T(8,128)(2,1)S(1)}, bf16[96,1024]{1,0:T(8,128)(2,1)S(1)}, u32[]{:S(2)}, u32[]{:S(2)}) collective-permute-start(bf16[96,1024]{1,0:T(8,128)(2,1)S(1)} %add_convert_fusion.2), channel_id=1, source_target_pairs={{0,4},{4,8},{8,12},{12,0},{1,5},{5,9},{9,13},{13,1},{2,6},{6,10},{... | collective-permute-start | bytes 589832 | tf_op jit(solution)/shard_map/ppermute | solution.py:205
  56.7 14.3 %collective-permute-start.7 = (bf16[96,1024]{1,0:T(8,128)(2,1)S(1)}, bf16[96,1024]{1,0:T(8,128)(2,1)S(1)}, u32[]{:S(2)}, u32[]{:S(2)}) collective-permute-start(bf16[96,1024]{1,0:T(8,128)(2,1)S(1)} %add_convert_fusion.3), channel_id=1, source_target_pairs={{0,12},{4,0},{8,4},{12,8},{1,13},{5,1},{9,5},{13,9},{2,14},{6,2},{... | collective-permute-start | bytes 589832 | tf_op jit(solution)/shard_map/ppermute | solution.py:205

commit v15 on v14

--- a/solution.py
+++ b/solution.py
@@ -15,25 +15,27 @@
 ROWS_AT_ONCE = 1024
 
 
-def pack_kernel(field_ref, packed_ref):
+def pack_kernel(field_ref, packed_ref, low_ref, high_ref):
     lon, lat, chans = field_ref.shape
     pairs = field_ref[...].reshape(lon // 2, 2, lat, chans)
-    packed_ref[...] = jnp.concatenate([pairs[:, 0], pairs[:, 1]], axis=-1).astype(packed_ref.dtype)
+    joined = jnp.concatenate([pairs[:, 0], pairs[:, 1]], axis=-1).astype(packed_ref.dtype)
+    packed_ref[...] = joined
+    low_ref[...] = joined[:1]
+    high_ref[...] = joined[-1:]
+
+
+def place(away, count_ch, count_sub, width):
+    away_ch, away_sub = away // count_sub, away % count_sub
+    at_ch = lax.rem(lax.axis_index("ch") + count_ch - away_ch, count_ch)
+    at_sub = lax.rem(lax.axis_index("sub") + count_sub - away_sub, count_sub)
+    return pl.ds(pl.multiple_of((at_ch * count_sub + at_sub) * width, width), width)
 
 
 def join_kernel(count_ch, count_sub, *refs):
-    blocks, (field_ref, low_ref, high_ref) = refs[:-3], refs[-3:]
-    pairs, lat, wide = field_ref.shape
-    width = lat // (count_ch * count_sub)
-    for away_ch in range(count_ch):
-        for away_sub in range(count_sub):
-            at_ch = lax.rem(lax.axis_index("ch") + count_ch - away_ch, count_ch)
-            at_sub = lax.rem(lax.axis_index("sub") + count_sub - away_sub, count_sub)
-            here = pl.ds(pl.multiple_of((at_ch * count_sub + at_sub) * width, width), width)
-            block = blocks[away_ch * count_sub + away_sub][...]
-            field_ref[:, here, :] = block
-            low_ref[:, here, :] = block[:1]
-            high_ref[:, here, :] = block[pairs - 1 :]
+    blocks, field_ref = refs[:-1], refs[-1]
+    width = field_ref.shape[1] // len(blocks)
+    for away, block in enumerate(blocks):
+        field_ref[:, place(away, count_ch, count_sub, width), :] = block[...]
 
 
 def split_two(value):
@@ -154,16 +156,19 @@
     tokens_ref[...] = embed_patches(two_ref, embed_ref)
 
 
-def outer_kernel(
-    field_ref, before_ref, after_ref, upper_edge_ref, lower_edge_ref, taps_one_ref, taps_two_ref, embed_ref, inner_ref, tokens_ref, two_ref
-):
+def outer_kernel(count_ch, count_sub, field_ref, *refs):
+    count = count_ch * count_sub
+    sides, refs = refs[:count], refs[count:]
+    upper_edge_ref, lower_edge_ref, taps_one_ref, taps_two_ref, embed_ref, inner_ref, tokens_ref, two_ref, sides_ref = refs
     pairs, lat, wide = field_ref.shape
+    for away, block in enumerate(sides):
+        sides_ref[:, place(away, count_ch, count_sub, lat // count), :] = block[...]
 
     def field_at(pair):
         if pair < 0:
-            return before_ref[0]
+            return sides_ref[0]
         if pair >= pairs:
-            return after_ref[0]
+            return sides_ref[1]
         return field_ref[pair]
 
     outermost = [-1, 0, pairs - 1, pairs]
@@ -205,14 +210,24 @@
     return lax.ppermute(value, axis, [(i, (i + away) % count) for i in range(count)])
 
 
-def band_blocks(block, beside):
+def band_blocks(block):
     rows = [block] + [turned(block, "ch", away) for away in range(1, lax.axis_size("ch"))]
-    rows[1:], beside = lax.optimization_barrier((rows[1:], beside))
     blocks = []
     for row in rows:
         blocks.append(row)
         blocks.extend(turned(row, "sub", away) for away in range(1, lax.axis_size("sub")))
-    return blocks, beside
+    return blocks
+
+
+def direct_blocks(block):
+    sizes = lax.axis_size("ch"), lax.axis_size("sub")
+    devices = [(at_ch, at_sub) for at_ch in range(sizes[0]) for at_sub in range(sizes[1])]
+    blocks = [block]
+    for away in devices[1:]:
+        targets = [tuple((at + step) % size for at, step, size in zip(device, away, sizes)) for device in devices]
+        route = [(number, devices.index(target)) for number, target in enumerate(targets)]
+        blocks.append(lax.ppermute(block, ("ch", "sub"), route))
+    return blocks
 
 
 def encode(weather, conv_first, conv_second, patch_embed):
@@ -220,9 +235,16 @@
     pairs, wide = lon // 2, 2 * chans
     embed = patch_embed.shape[1]
     shape = functools.partial(jax.ShapeDtypeStruct, dtype=jnp.bfloat16)
-    packed = call(
-        pack_kernel, shape((pairs, lat, wide)), (jnp.transpose(weather, (1, 2, 0)),), moved=weather.size * 10
-    )
+    edge = shape((1, lat, wide))
+    packed, low, high = call(
+        pack_kernel,
+        (shape((pairs, lat, wide)), edge, edge),
+        (jnp.transpose(weather, (1, 2, 0)),),
+        moved=weather.size * 10,
+    )
+    before = turned(high, "tok", 1)
+    after = turned(low, "tok", -1)
+    blocks = band_blocks(packed)
     taps = shape((4 * chans, 12 * chans))
     weights = call(
         weights_kernel,
@@ -231,17 +253,15 @@
         scratch=[pltpu.VMEM((patch_embed.shape[0], LANES), jnp.float32)],
         moved=conv_first.size * 20,
     )
-    blocks, weights = band_blocks(packed, weights)
+    sides = direct_blocks(jnp.concatenate([before, after], axis=0))
+    counts = lax.axis_size("ch"), lax.axis_size("sub")
     lat = len(blocks) * lat
-    edge = shape((1, lat, wide))
-    field, low, high = call(
-        functools.partial(join_kernel, lax.axis_size("ch"), lax.axis_size("sub")),
-        (shape((pairs, lat, wide)), edge, edge),
+    field = call(
+        functools.partial(join_kernel, *counts),
+        shape((pairs, lat, wide)),
         blocks,
         moved=packed.size * 4 * len(blocks),
     )
-    before = turned(high, "tok", 1)
-    after = turned(low, "tok", -1)
     work = 2 * lat * 4 * chans * 6 * chans * 5
     held = shape((4, lat, wide))
     hidden = pltpu.VMEM((pairs, lat, wide), jnp.bfloat16)
@@ -254,10 +274,10 @@
         moved=field.size * 2,
     )
     return call(
-        outer_kernel,
+        functools.partial(outer_kernel, *counts),
         shape((embed, pairs * lat // 2)),
-        (field, before, after, upper_edge, lower_edge, *weights, inner),
-        scratch=[pltpu.VMEM((4 * lat, wide), jnp.float32)],
+        (field, *sides, upper_edge, lower_edge, *weights, inner),
+        scratch=[pltpu.VMEM((4 * lat, wide), jnp.float32), pltpu.VMEM((2, lat, wide), jnp.bfloat16)],
         flops=work * 4,
         moved=field.size * 2,
     )

time: 72 us -> 73.3 us (1.018)
  waiting for transfers between devices: 31.1 us -> 32.1 us
    ppermute x0 -> x3, starting transfers between devices: none -> 1.93 us  [direct_blocks(): blocks.append(lax.ppermute(block, ('ch', 'sub'), route))]
    ppermute x17, starting transfers between devices: 24 us -> 22.3 us  [turned(): lax.ppermute(value, axis, [(i, (i + away) % count) for i in range(count)])]
    ppermute x17, waiting for transfers between devices: 31.1 us -> 32 us  [turned(): lax.ppermute(value, axis, [(i, (i + away) % count) for i in range(count)])]
    unnamed x10 -> x11, local copies, waits for them, and re-layouts: 4.04 us -> 4.04 us
  transfers between devices with their start and end apart: 17 -> 20, of which waited for: 13 -> 12; matrix products, arithmetic and copies ran while one was open for 0% -> 0% of each run, Pallas kernels for 14% -> 13%
where the time goes in v15:
time: 73.3 us; the launch traced here: 73.1 us
  waiting for transfers between devices  32.1 us (44%)
  starting transfers between devices  24.3 us (33%)
  Pallas kernels  12.3 us (17%)
  local copies, waits for them, and re-layouts  4.05 us (6%)
    ppermute x17, waiting for transfers between devices, turned(): lax.ppermute(value, axis, [(i, (i + away) % count) for i in range(count)])  32 us
    ppermute x17, starting transfers between devices, turned(): lax.ppermute(value, axis, [(i, (i + away) % count) for i in range(count)])  22.3 us
    pallas_call x13, Pallas kernels, call(): pl.pallas_call(kernel, out_shape=out_shape, in_specs=[pl.BlockSpec(memory...  9.27 us
    unnamed x11, local copies, waits for them, and re-layouts  4.04 us
    pallas_call x4, Pallas kernels, finish(): pl.pallas_call(functools.partial(last_kernel, first), out_shape=jax.Shape...  3.03 us
    ppermute x3, starting transfers between devices, direct_blocks(): blocks.append(lax.ppermute(block, ('ch', 'sub'), route))  1.93 us
  transfers between devices with their start and end apart: 20, of which 12 were waited for; matrix products, arithmetic and copies ran while one was open for 0% of the time, Pallas kernels for 13%

profile of v15, /device:TPU:0, one launch (start us, length us, event | category | flops | bytes accessed | tf_op | source)
XLA Modules:
  0.0 73.1 jit_solution(16888538817093409805)
XLA Ops:
  0.0 1.2 %copy-done.1 = f32[64,32,32]{0,2,1:T(8,128)S(1)} copy-done((f32[64,32,32]{0,2,1:T(8,128)S(1)}, f32[64,32,32]{0,2,1:T(8,128)}, u32[]{:S(2)}) %copy-start.1) | copy-done | bytes 262168
  1.2 0.1 shard_map.55
  1.3 3.0 %collective-permute-start.1 = (bf16[16,32,128]{2,1,0:T(8,128)(2,1)S(1)}, bf16[16,32,128]{2,1,0:T(8,128)(2,1)S(1)}, u32[]{:S(2)}, u32[]{:S(2)}) collective-permute-start(bf16[16,32,128]{2,1,0:T(8,128)(2,1)S(1)} %get-tuple-element.22.refs_0_), channel_id=1, source_target_pairs={{0,2},{2,0},{1,3},{3,1},{4,6},{6,4},{5,7},{7,5},{8,10},{10,8},{9,1... | collective-permute-start | bytes 393224 | tf_op jit(solution)/shard_map/ppermute | solution.py:210
  4.3 1.6 %collective-permute-start.3 = (bf16[1,32,128]{2,1,0:T(8,128)(2,1)S(1)}, bf16[1,32,128]{2,1,0:T(8,128)(2,1)S(1)}, u32[]{:S(2)}, u32[]{:S(2)}) collective-permute-start(bf16[1,32,128]{2,1,0:T(8,128)(2,1)S(1)} %get-tuple-element.23), channel_id=1, source_target_pairs={{0,4},{4,8},{8,12},{12,0},{1,5},{5,9},{9,13},{13,1},{2,6},{6,10},{... | collective-permute-start | bytes 24584 | tf_op jit(solution)/shard_map/ppermute | solution.py:210
  5.9 2.2 %collective-permute-start.4 = (bf16[1,32,128]{2,1,0:T(8,128)(2,1)S(1)}, bf16[1,32,128]{2,1,0:T(8,128)(2,1)S(1)}, u32[]{:S(2)}, u32[]{:S(2)}) collective-permute-start(bf16[1,32,128]{2,1,0:T(8,128)(2,1)S(1)} %get-tuple-element.24), channel_id=1, source_target_pairs={{0,12},{4,0},{8,4},{12,8},{1,13},{5,1},{9,5},{13,9},{2,14},{6,2},{... | collective-permute-start | bytes 24584 | tf_op jit(solution)/shard_map/ppermute | solution.py:210
  8.1 1.0 %copy-done.2 = f32[9,64,64]{2,1,0:T(8,128)S(1)} copy-done((f32[9,64,64]{2,1,0:T(8,128)S(1)}, f32[9,64,64]{2,1,0:T(8,128)}, u32[]{:S(2)}) %copy-start.2) | copy-done | bytes 147480
  9.1 1.0 %copy-done.3 = f32[9,64,64]{2,1,0:T(8,128)S(1)} copy-done((f32[9,64,64]{2,1,0:T(8,128)S(1)}, f32[9,64,64]{2,1,0:T(8,128)}, u32[]{:S(2)}) %copy-start.3) | copy-done | bytes 147480
  10.1 0.9 %copy-done.4 = bf16[256,384]{1,0:T(8,128)(2,1)S(1)} copy-done((bf16[256,384]{1,0:T(8,128)(2,1)S(1)}, bf16[256,384]{1,0:T(8,128)(2,1)}, u32[]{:S(2)}) %copy-start.4) | copy-done | bytes 196632
  11.0 0.6 shard_map.57
  11.6 0.3 collective-permute-start.2
  11.9 0.3 collective-permute-start.5
  12.3 0.3 collective-permute-start.6
  12.6 1.3 %collective-permute-start.7 = (bf16[2,32,128]{2,1,0:T(8,128)(2,1)S(1)}, bf16[2,32,128]{2,1,0:T(8,128)(2,1)S(1)}, u32[]{:S(2)}, u32[]{:S(2)}) collective-permute-start(bf16[2,32,128]{2,1,0:T(8,128)(2,1)S(1)} %constant_dynamic-update-slice_fusion.refs_0_), channel_id=1, source_target_pairs={{0,3},{1,2},{2,1},{3,0},{4,7},{5,6},{6,5},{7,4},{8,11},{9,10},{10,... | collective-permute-start | bytes 49160 | tf_op jit(solution)/shard_map/ppermute | solution.py:229
  13.9 2.4 %shard_map.58 = (bf16[384,768]{1,0:T(8,128)(2,1)S(1)}, bf16[4,128,128]{2,1,0:T(8,128)(2,1)S(1)}, bf16[4,128,128]{2,1,0:T(8,128)(2,1)S(1)}) custom-call(bf16[16,128,128]{2,1,0:T(8,128)(2,1)S(1)} %shard_map.56.field_ref, bf16[256,768]{1,0:T(8,128)(2,1)S(1)} %get-tuple-element.25.taps_one_ref.refs_6_, ...), custom_call_target="tpu_custom_call" | custom-call | flops 1635778560 | bytes 524288 | tf_op jit(solution)/shard_map/pallas_call | solution.py:197
  16.3 1.2 %shard_map.59.tokens_ref = bf16[384,1024]{1,0:T(8,128)(2,1)S(1)} custom-call(bf16[16,128,128]{2,1,0:T(8,128)(2,1)S(1)} %shard_map.56.field_ref, bf16[2,32,128]{2,1,0:T(8,128)(2,1)S(1)} %constant_dynamic-update-slice_fusion.refs_0_, bf16[2,32,128]{2,1,0:T(8,128)(2,1)S(1)} %collective-permute-done.5.refs_1_, ...), custom_call_target="tpu_custom_call" | custom-call | flops 503316480 | bytes 524288 | tf_op jit(solution)/shard_map/pallas_call | solution.py:197
  17.5 0.5 shard_map.66
  18.0 0.1 collective-permute-start.17
  18.1 0.5 shard_map.64
  18.6 3.9 %collective-permute-start.14 = (bf16[96,1024]{1,0:T(8,128)(2,1)S(1)}, bf16[96,1024]{1,0:T(8,128)(2,1)S(1)}, u32[]{:S(2)}, u32[]{:S(2)}) collective-permute-start(bf16[96,1024]{1,0:T(8,128)(2,1)S(1)} %shard_map.64), channel_id=1, source_target_pairs={{0,12},{4,0},{8,4},{12,8},{1,13},{5,1},{9,5},{13,9},{2,14},{6,2},{... | collective-permute-start | bytes 589832 | tf_op jit(solution)/shard_map/ppermute | solution.py:210
  22.4 0.5 shard_map.62
  22.9 0.1 collective-permute-start.11
  22.9 0.5 shard_map.60
  23.4 3.9 %collective-permute-start.8 = (bf16[96,1024]{1,0:T(8,128)(2,1)S(1)}, bf16[96,1024]{1,0:T(8,128)(2,1)S(1)}, u32[]{:S(2)}, u32[]{:S(2)}) collective-permute-start(bf16[96,1024]{1,0:T(8,128)(2,1)S(1)} %shard_map.60), channel_id=1, source_target_pairs={{0,12},{4,0},{8,4},{12,8},{1,13},{5,1},{9,5},{13,9},{2,14},{6,2},{... | collective-permute-start | bytes 589832 | tf_op jit(solution)/shard_map/ppermute | solution.py:210
  27.3 0.3 collective-permute-done.17.arrived_ref
  27.6 0.8 %shard_map.67 = (bf16[96,1024]{1,0:T(8,128)(2,1)S(1)}, f32[192,1024]{1,0:T(8,128)S(1)}) custom-call(bf16[96,1024]{1,0:T(8,128)(2,1)S(1)} %collective-permute-done.17.arrived_ref, bf16[384,1024]{1,0:T(8,128)(2,1)S(1)} %shard_map.59.tokens_ref, bf16[1024,4096]{1,0:T(8,128)(2,1)S(1)} %copy-done), custom_call_target="tpu_custom_call" | custom-call | tf_op jit(solution)/shard_map/pallas_call | solution.py:197
  28.4 0.1 collective-permute-start.18
  28.4 2.1 %collective-permute-done.14.arrived_ref = bf16[96,1024]{1,0:T(8,128)(2,1)S(1)} collective-permute-done((bf16[96,1024]{1,0:T(8,128)(2,1)S(1)}, bf16[96,1024]{1,0:T(8,128)(2,1)S(1)}, u32[]{:S(2)}, u32[]{:S(2)}) %collective-permute-start.14) | collective-permute-done | bytes 196640 | tf_op jit(solution)/shard_map/ppermute | solution.py:210
  30.5 0.8 %shard_map.65 = (bf16[96,1024]{1,0:T(8,128)(2,1)S(1)}, f32[192,1024]{1,0:T(8,128)S(1)}) custom-call(bf16[96,1024]{1,0:T(8,128)(2,1)S(1)} %collective-permute-done.14.arrived_ref, bf16[384,1024]{1,0:T(8,128)(2,1)S(1)} %shard_map.59.tokens_ref, bf16[1024,4096]{1,0:T(8,128)(2,1)S(1)} %copy-done), custom_call_target="tpu_custom_call" | custom-call | tf_op jit(solution)/shard_map/pallas_call | solution.py:197
  31.3 1.8 %collective-permute-start.15 = (bf16[96,1024]{1,0:T(8,128)(2,1)S(1)}, bf16[96,1024]{1,0:T(8,128)(2,1)S(1)}, u32[]{:S(2)}, u32[]{:S(2)}) collective-permute-start(bf16[96,1024]{1,0:T(8,128)(2,1)S(1)} %get-tuple-element.35), channel_id=1, source_target_pairs={{0,12},{4,0},{8,4},{12,8},{1,13},{5,1},{9,5},{13,9},{2,14},{6,2},{... | collective-permute-start | bytes 589832 | tf_op jit(solution)/shard_map/ppermute | solution.py:210
  33.1 3.0 %collective-permute-done.11.arrived_ref = bf16[96,1024]{1,0:T(8,128)(2,1)S(1)} collective-permute-done((bf16[96,1024]{1,0:T(8,128)(2,1)S(1)}, bf16[96,1024]{1,0:T(8,128)(2,1)S(1)}, u32[]{:S(2)}, u32[]{:S(2)}) %collective-permute-start.11) | collective-permute-done | bytes 196640 | tf_op jit(solution)/shard_map/ppermute | solution.py:210
  36.1 0.8 %shard_map.63 = (bf16[96,1024]{1,0:T(8,128)(2,1)S(1)}, f32[192,1024]{1,0:T(8,128)S(1)}) custom-call(bf16[96,1024]{1,0:T(8,128)(2,1)S(1)} %collective-permute-done.11.arrived_ref, bf16[384,1024]{1,0:T(8,128)(2,1)S(1)} %shard_map.59.tokens_ref, bf16[1024,4096]{1,0:T(8,128)(2,1)S(1)} %copy-done), custom_call_target="tpu_custom_call" | custom-call | tf_op jit(solution)/shard_map/pallas_call | solution.py:197
  36.9 2.0 %collective-permute-done.8.arrived_ref = bf16[96,1024]{1,0:T(8,128)(2,1)S(1)} collective-permute-done((bf16[96,1024]{1,0:T(8,128)(2,1)S(1)}, bf16[96,1024]{1,0:T(8,128)(2,1)S(1)}, u32[]{:S(2)}, u32[]{:S(2)}) %collective-permute-start.8) | collective-permute-done | bytes 196640 | tf_op jit(solution)/shard_map/ppermute | solution.py:210
  38.9 0.8 %shard_map.61 = (bf16[96,1024]{1,0:T(8,128)(2,1)S(1)}, f32[192,1024]{1,0:T(8,128)S(1)}) custom-call(bf16[96,1024]{1,0:T(8,128)(2,1)S(1)} %collective-permute-done.8.arrived_ref, bf16[384,1024]{1,0:T(8,128)(2,1)S(1)} %shard_map.59.tokens_ref, bf16[1024,4096]{1,0:T(8,128)(2,1)S(1)} %copy-done), custom_call_target="tpu_custom_call" | custom-call | tf_op jit(solution)/shard_map/pallas_call | solution.py:197
  39.7 1.8 %collective-permute-start.9 = (bf16[96,1024]{1,0:T(8,128)(2,1)S(1)}, bf16[96,1024]{1,0:T(8,128)(2,1)S(1)}, u32[]{:S(2)}, u32[]{:S(2)}) collective-permute-start(bf16[96,1024]{1,0:T(8,128)(2,1)S(1)} %get-tuple-element.31), channel_id=1, source_target_pairs={{0,12},{4,0},{8,4},{12,8},{1,13},{5,1},{9,5},{13,9},{2,14},{6,2},{... | collective-permute-start | bytes 589832 | tf_op jit(solution)/shard_map/ppermute | solution.py:210
  41.6 3.0 %collective-permute-done.18 = bf16[96,1024]{1,0:T(8,128)(2,1)S(1)} collective-permute-done((bf16[96,1024]{1,0:T(8,128)(2,1)S(1)}, bf16[96,1024]{1,0:T(8,128)(2,1)S(1)}, u32[]{:S(2)}, u32[]{:S(2)}) %collective-permute-start.18) | collective-permute-done | bytes 196640 | tf_op jit(solution)/shard_map/ppermute | solution.py:210
  44.7 2.7 %collective-permute-done.15 = bf16[96,1024]{1,0:T(8,128)(2,1)S(1)} collective-permute-done((bf16[96,1024]{1,0:T(8,128)(2,1)S(1)}, bf16[96,1024]{1,0:T(8,128)(2,1)S(1)}, u32[]{:S(2)}, u32[]{:S(2)}) %collective-permute-start.15) | collective-permute-done | bytes 196640 | tf_op jit(solution)/shard_map/ppermute | solution.py:210
  47.4 1.7 %collective-permute-start.16 = (bf16[96,1024]{1,0:T(8,128)(2,1)S(1)}, bf16[96,1024]{1,0:T(8,128)(2,1)S(1)}, u32[]{:S(2)}, u32[]{:S(2)}) collective-permute-start(bf16[96,1024]{1,0:T(8,128)(2,1)S(1)} %add_convert_fusion.1), channel_id=1, source_target_pairs={{0,12},{4,0},{8,4},{12,8},{1,13},{5,1},{9,5},{13,9},{2,14},{6,2},{... | collective-permute-start | bytes 589832 | tf_op jit(solution)/shard_map/ppermute | solution.py:210
  49.1 3.9 %collective-permute-done.12 = bf16[96,1024]{1,0:T(8,128)(2,1)S(1)} collective-permute-done((bf16[96,1024]{1,0:T(8,128)(2,1)S(1)}, bf16[96,1024]{1,0:T(8,128)(2,1)S(1)}, u32[]{:S(2)}, u32[]{:S(2)}) %collective-permute-start.12) | collective-permute-done | bytes 196640 | tf_op jit(solution)/shard_map/ppermute | solution.py:210
  53.1 2.7 %collective-permute-done.9 = bf16[96,1024]{1,0:T(8,128)(2,1)S(1)} collective-permute-done((bf16[96,1024]{1,0:T(8,128)(2,1)S(1)}, bf16[96,1024]{1,0:T(8,128)(2,1)S(1)}, u32[]{:S(2)}, u32[]{:S(2)}) %collective-permute-start.9) | collective-permute-done | bytes 196640 | tf_op jit(solution)/shard_map/ppermute | solution.py:210
  55.8 1.8 %collective-permute-start.10 = (bf16[96,1024]{1,0:T(8,128)(2,1)S(1)}, bf16[96,1024]{1,0:T(8,128)(2,1)S(1)}, u32[]{:S(2)}, u32[]{:S(2)}) collective-permute-start(bf16[96,1024]{1,0:T(8,128)(2,1)S(1)} %add_convert_fusion.3), channel_id=1, source_target_pairs={{0,12},{4,0},{8,4},{12,8},{1,13},{5,1},{9,5},{13,9},{2,14},{6,2},{... | collective-permute-start | bytes 589832 | tf_op jit(solution)/shard_map/ppermute | solution.py:210
  57.6 3.9 %collective-permute-done.19.arrived_ref = bf16[96,1024]{1,0:T(8,128)(2,1)S(1)} collective-permute-done((bf16[96,1024]{1,0:T(8,128)(2,1)S(1)}, bf16[96,1024]{1,0:T(8,128)(2,1)S(1)}, u32[]{:S(2)}, u32[]{:S(2)}) %collective-permute-start.19) | collective-permute-done | bytes 196640 | tf_op jit(solution)/shard_map/ppermute | solution.py:210
  61.5 0.8 %shard_map.68.refs_0_ = bf16[96,4096]{1,0:T(8,128)(2,1)} custom-call(bf16[96,1024]{1,0:T(8,128)(2,1)S(1)} %collective-permute-done.19.arrived_ref, f32[192,1024]{1,0:T(8,128)S(1)} %get-tuple-element.38.kept_ref), custom_call_target="tpu_custom_call" | custom-call | tf_op jit(solution)/shard_map/pallas_call | solution.py:326
  62.3 2.0 %collective-permute-done.16.arrived_ref = bf16[96,1024]{1,0:T(8,128)(2,1)S(1)} collective-permute-done((bf16[96,1024]{1,0:T(8,128)(2,1)S(1)}, bf16[96,1024]{1,0:T(8,128)(2,1)S(1)}, u32[]{:S(2)}, u32[]{:S(2)}) %collective-permute-start.16) | collective-permute-done | bytes 196640 | tf_op jit(solution)/shard_map/ppermute | solution.py:210
  64.2 0.8 %shard_map.69.refs_0_ = bf16[96,4096]{1,0:T(8,128)(2,1)} custom-call(bf16[96,1024]{1,0:T(8,128)(2,1)S(1)} %collective-permute-done.16.arrived_ref, f32[192,1024]{1,0:T(8,128)S(1)} %get-tuple-element.36.kept_ref, bf16[96,4096]{1,0:T(8,128)(2,1)} %shard_map.68.refs_0_), custom_call_target="tpu_custom_call", output_to_operand_aliasing={{}: (2, {})} | custom-call | tf_op jit(solution)/shard_map/pallas_call | solution.py:326
  65.0 5.0 %collective-permute-done.13.arrived_ref = bf16[96,1024]{1,0:T(8,128)(2,1)S(1)} collective-permute-done((bf16[96,1024]{1,0:T(8,128)(2,1)S(1)}, bf16[96,1024]{1,0:T(8,128)(2,1)S(1)}, u32[]{:S(2)}, u32[]{:S(2)}) %collective-permute-start.13) | collective-permute-done | bytes 196640 | tf_op jit(solution)/shard_map/ppermute | solution.py:210
  70.0 0.8 %shard_map.70.refs_0_ = bf16[96,4096]{1,0:T(8,128)(2,1)} custom-call(bf16[96,1024]{1,0:T(8,128)(2,1)S(1)} %collective-permute-done.13.arrived_ref, f32[192,1024]{1,0:T(8,128)S(1)} %get-tuple-element.34.kept_ref, bf16[96,4096]{1,0:T(8,128)(2,1)} %shard_map.69.refs_0_), custom_call_target="tpu_custom_call", output_to_operand_aliasing={{}: (2, {})} | custom-call | tf_op jit(solution)/shard_map/pallas_call | solution.py:326
  70.7 1.6 %collective-permute-done.10.arrived_ref = bf16[96,1024]{1,0:T(8,128)(2,1)S(1)} collective-permute-done((bf16[96,1024]{1,0:T(8,128)(2,1)S(1)}, bf16[96,1024]{1,0:T(8,128)(2,1)S(1)}, u32[]{:S(2)}, u32[]{:S(2)}) %collective-permute-start.10) | collective-permute-done | bytes 196640 | tf_op jit(solution)/shard_map/ppermute | solution.py:210
  72.3 0.8 %shard_map.71 = bf16[96,4096]{1,0:T(8,128)(2,1)} custom-call(bf16[96,1024]{1,0:T(8,128)(2,1)S(1)} %collective-permute-done.10.arrived_ref, f32[192,1024]{1,0:T(8,128)S(1)} %get-tuple-element.32.kept_ref, bf16[96,4096]{1,0:T(8,128)(2,1)} %shard_map.70.refs_0_), custom_call_target="tpu_custom_call", output_to_operand_aliasing={{}: (2, {})} | custom-call | tf_op jit(solution)/shard_map/pallas_call | solution.py:326
  (25 shorter events, 0.4 us)
Async XLA Ops:
  0.0 17.5 %copy-start = (bf16[1024,4096]{1,0:T(8,128)(2,1)S(1)}, bf16[1024,4096]{1,0:T(8,128)(2,1)}, u32[]{:S(2)}) copy-start(bf16[1024,4096]{1,0:T(8,128)(2,1)} %mixing_ref.15) | copy-start | bytes 25165828
  0.0 1.2 %copy-start.1 = (f32[64,32,32]{0,2,1:T(8,128)S(1)}, f32[64,32,32]{0,2,1:T(8,128)}, u32[]{:S(2)}) copy-start(f32[64,32,32]{0,2,1:T(8,128)} %param.5) | copy-start | bytes 786436
  1.3 10.3 %collective-permute-start.1 = (bf16[16,32,128]{2,1,0:T(8,128)(2,1)S(1)}, bf16[16,32,128]{2,1,0:T(8,128)(2,1)S(1)}, u32[]{:S(2)}, u32[]{:S(2)}) collective-permute-start(bf16[16,32,128]{2,1,0:T(8,128)(2,1)S(1)} %get-tuple-element.22.refs_0_), channel_id=1, source_target_pairs={{0,2},{2,0},{1,3},{3,1},{4,6},{6,4},{5,7},{7,5},{8,10},{10,8},{9,1... | collective-permute-start | bytes 393224 | tf_op jit(solution)/shard_map/ppermute | solution.py:210
  4.3 7.6 %collective-permute-start.3 = (bf16[1,32,128]{2,1,0:T(8,128)(2,1)S(1)}, bf16[1,32,128]{2,1,0:T(8,128)(2,1)S(1)}, u32[]{:S(2)}, u32[]{:S(2)}) collective-permute-start(bf16[1,32,128]{2,1,0:T(8,128)(2,1)S(1)} %get-tuple-element.23), channel_id=1, source_target_pairs={{0,4},{4,8},{8,12},{12,0},{1,5},{5,9},{9,13},{13,1},{2,6},{6,10},{... | collective-permute-start | bytes 24584 | tf_op jit(solution)/shard_map/ppermute | solution.py:210
  5.9 8.0 %collective-permute-start = (bf16[16,32,128]{2,1,0:T(8,128)(2,1)S(1)}, bf16[16,32,128]{2,1,0:T(8,128)(2,1)S(1)}, u32[]{:S(2)}, u32[]{:S(2)}) collective-permute-start(bf16[16,32,128]{2,1,0:T(8,128)(2,1)S(1)} %get-tuple-element.22.refs_0_), channel_id=1, source_target_pairs={{0,1},{1,0},{2,3},{3,2},{4,5},{5,4},{6,7},{7,6},{8,9},{9,8},{10,11... | collective-permute-start | bytes 393224 | tf_op jit(solution)/shard_map/ppermute | solution.py:210
  5.9 6.0 %collective-permute-start.4 = (bf16[1,32,128]{2,1,0:T(8,128)(2,1)S(1)}, bf16[1,32,128]{2,1,0:T(8,128)(2,1)S(1)}, u32[]{:S(2)}, u32[]{:S(2)}) collective-permute-start(bf16[1,32,128]{2,1,0:T(8,128)(2,1)S(1)} %get-tuple-element.24), channel_id=1, source_target_pairs={{0,12},{4,0},{8,4},{12,8},{1,13},{5,1},{9,5},{13,9},{2,14},{6,2},{... | collective-permute-start | bytes 24584 | tf_op jit(solution)/shard_map/ppermute | solution.py:210
  8.1 1.0 %copy-start.2 = (f32[9,64,64]{2,1,0:T(8,128)S(1)}, f32[9,64,64]{2,1,0:T(8,128)}, u32[]{:S(2)}) copy-start(f32[9,64,64]{2,1,0:T(8,128)} %first_ref.1) | copy-start | bytes 442372
  9.1 1.0 %copy-start.3 = (f32[9,64,64]{2,1,0:T(8,128)S(1)}, f32[9,64,64]{2,1,0:T(8,128)}, u32[]{:S(2)}) copy-start(f32[9,64,64]{2,1,0:T(8,128)} %second_ref.1) | copy-start | bytes 442372
  10.1 0.9 %copy-start.4 = (bf16[256,384]{1,0:T(8,128)(2,1)S(1)}, bf16[256,384]{1,0:T(8,128)(2,1)}, u32[]{:S(2)}) copy-start(bf16[256,384]{1,0:T(8,128)(2,1)} %embed_ref.1) | copy-start | bytes 589828
  11.6 2.2 %collective-permute-start.2 = (bf16[16,32,128]{2,1,0:T(8,128)(2,1)S(1)}, bf16[16,32,128]{2,1,0:T(8,128)(2,1)S(1)}, u32[]{:S(2)}, u32[]{:S(2)}) collective-permute-start(bf16[16,32,128]{2,1,0:T(8,128)(2,1)S(1)} %collective-permute-done.1.refs_2_), channel_id=1, source_target_pairs={{0,1},{1,0},{2,3},{3,2},{4,5},{5,4},{6,7},{7,6},{8,9},{9,8},{10,11... | collective-permute-start | bytes 393224 | tf_op jit(solution)/shard_map/ppermute | solution.py:210
  11.9 4.4 %collective-permute-start.5 = (bf16[2,32,128]{2,1,0:T(8,128)(2,1)S(1)}, bf16[2,32,128]{2,1,0:T(8,128)(2,1)S(1)}, u32[]{:S(2)}, u32[]{:S(2)}) collective-permute-start(bf16[2,32,128]{2,1,0:T(8,128)(2,1)S(1)} %constant_dynamic-update-slice_fusion.refs_0_), channel_id=1, source_target_pairs={{0,1},{1,0},{2,3},{3,2},{4,5},{5,4},{6,7},{7,6},{8,9},{9,8},{10,11... | collective-permute-start | bytes 49160 | tf_op jit(solution)/shard_map/ppermute | solution.py:229
  12.3 4.0 %collective-permute-start.6 = (bf16[2,32,128]{2,1,0:T(8,128)(2,1)S(1)}, bf16[2,32,128]{2,1,0:T(8,128)(2,1)S(1)}, u32[]{:S(2)}, u32[]{:S(2)}) collective-permute-start(bf16[2,32,128]{2,1,0:T(8,128)(2,1)S(1)} %constant_dynamic-update-slice_fusion.refs_0_), channel_id=1, source_target_pairs={{0,2},{1,3},{2,0},{3,1},{4,6},{5,7},{6,4},{7,5},{8,10},{9,11},{10,... | collective-permute-start | bytes 49160 | tf_op jit(solution)/shard_map/ppermute | solution.py:229
  12.6 3.7 %collective-permute-start.7 = (bf16[2,32,128]{2,1,0:T(8,128)(2,1)S(1)}, bf16[2,32,128]{2,1,0:T(8,128)(2,1)S(1)}, u32[]{:S(2)}, u32[]{:S(2)}) collective-permute-start(bf16[2,32,128]{2,1,0:T(8,128)(2,1)S(1)} %constant_dynamic-update-slice_fusion.refs_0_), channel_id=1, source_target_pairs={{0,3},{1,2},{2,1},{3,0},{4,7},{5,6},{6,5},{7,4},{8,11},{9,10},{10,... | collective-permute-start | bytes 49160 | tf_op jit(solution)/shard_map/ppermute | solution.py:229
  18.0 9.6 %collective-permute-start.17 = (bf16[96,1024]{1,0:T(8,128)(2,1)S(1)}, bf16[96,1024]{1,0:T(8,128)(2,1)S(1)}, u32[]{:S(2)}, u32[]{:S(2)}) collective-permute-start(bf16[96,1024]{1,0:T(8,128)(2,1)S(1)} %shard_map.66), channel_id=1, source_target_pairs={{0,4},{4,8},{8,12},{12,0},{1,5},{5,9},{9,13},{13,1},{2,6},{6,10},{... | collective-permute-start | bytes 589832 | tf_op jit(solution)/shard_map/ppermute | solution.py:210
  18.6 12.0 %collective-permute-start.14 = (bf16[96,1024]{1,0:T(8,128)(2,1)S(1)}, bf16[96,1024]{1,0:T(8,128)(2,1)S(1)}, u32[]{:S(2)}, u32[]{:S(2)}) collective-permute-start(bf16[96,1024]{1,0:T(8,128)(2,1)S(1)} %shard_map.64), channel_id=1, source_target_pairs={{0,12},{4,0},{8,4},{12,8},{1,13},{5,1},{9,5},{13,9},{2,14},{6,2},{... | collective-permute-start | bytes 589832 | tf_op jit(solution)/shard_map/ppermute | solution.py:210
  22.9 13.2 %collective-permute-start.11 = (bf16[96,1024]{1,0:T(8,128)(2,1)S(1)}, bf16[96,1024]{1,0:T(8,128)(2,1)S(1)}, u32[]{:S(2)}, u32[]{:S(2)}) collective-permute-start(bf16[96,1024]{1,0:T(8,128)(2,1)S(1)} %shard_map.62), channel_id=1, source_target_pairs={{0,4},{4,8},{8,12},{12,0},{1,5},{5,9},{9,13},{13,1},{2,6},{6,10},{... | collective-permute-start | bytes 589832 | tf_op jit(solution)/shard_map/ppermute | solution.py:210
  23.4 15.5 %collective-permute-start.8 = (bf16[96,1024]{1,0:T(8,128)(2,1)S(1)}, bf16[96,1024]{1,0:T(8,128)(2,1)S(1)}, u32[]{:S(2)}, u32[]{:S(2)}) collective-permute-start(bf16[96,1024]{1,0:T(8,128)(2,1)S(1)} %shard_map.60), channel_id=1, source_target_pairs={{0,12},{4,0},{8,4},{12,8},{1,13},{5,1},{9,5},{13,9},{2,14},{6,2},{... | collective-permute-start | bytes 589832 | tf_op jit(solution)/shard_map/ppermute | solution.py:210
  28.4 16.2 %collective-permute-start.18 = (bf16[96,1024]{1,0:T(8,128)(2,1)S(1)}, bf16[96,1024]{1,0:T(8,128)(2,1)S(1)}, u32[]{:S(2)}, u32[]{:S(2)}) collective-permute-start(bf16[96,1024]{1,0:T(8,128)(2,1)S(1)} %get-tuple-element.37), channel_id=1, source_target_pairs={{0,4},{4,8},{8,12},{12,0},{1,5},{5,9},{9,13},{13,1},{2,6},{6,10},{... | collective-permute-start | bytes 589832 | tf_op jit(solution)/shard_map/ppermute | solution.py:210
  31.3 16.1 %collective-permute-start.15 = (bf16[96,1024]{1,0:T(8,128)(2,1)S(1)}, bf16[96,1024]{1,0:T(8,128)(2,1)S(1)}, u32[]{:S(2)}, u32[]{:S(2)}) collective-permute-start(bf16[96,1024]{1,0:T(8,128)(2,1)S(1)} %get-tuple-element.35), channel_id=1, source_target_pairs={{0,12},{4,0},{8,4},{12,8},{1,13},{5,1},{9,5},{13,9},{2,14},{6,2},{... | collective-permute-start | bytes 589832 | tf_op jit(solution)/shard_map/ppermute | solution.py:210
  36.9 16.2 %collective-permute-start.12 = (bf16[96,1024]{1,0:T(8,128)(2,1)S(1)}, bf16[96,1024]{1,0:T(8,128)(2,1)S(1)}, u32[]{:S(2)}, u32[]{:S(2)}) collective-permute-start(bf16[96,1024]{1,0:T(8,128)(2,1)S(1)} %get-tuple-element.33), channel_id=1, source_target_pairs={{0,4},{4,8},{8,12},{12,0},{1,5},{5,9},{9,13},{13,1},{2,6},{6,10},{... | collective-permute-start | bytes 589832 | tf_op jit(solution)/shard_map/ppermute | solution.py:210
  39.7 16.1 %collective-permute-start.9 = (bf16[96,1024]{1,0:T(8,128)(2,1)S(1)}, bf16[96,1024]{1,0:T(8,128)(2,1)S(1)}, u32[]{:S(2)}, u32[]{:S(2)}) collective-permute-start(bf16[96,1024]{1,0:T(8,128)(2,1)S(1)} %get-tuple-element.31), channel_id=1, source_target_pairs={{0,12},{4,0},{8,4},{12,8},{1,13},{5,1},{9,5},{13,9},{2,14},{6,2},{... | collective-permute-start | bytes 589832 | tf_op jit(solution)/shard_map/ppermute | solution.py:210
  44.6 16.9 %collective-permute-start.19 = (bf16[96,1024]{1,0:T(8,128)(2,1)S(1)}, bf16[96,1024]{1,0:T(8,128)(2,1)S(1)}, u32[]{:S(2)}, u32[]{:S(2)}) collective-permute-start(bf16[96,1024]{1,0:T(8,128)(2,1)S(1)} %add_convert_fusion), channel_id=1, source_target_pairs={{0,4},{4,8},{8,12},{12,0},{1,5},{5,9},{9,13},{13,1},{2,6},{6,10},{... | collective-permute-start | bytes 589832 | tf_op jit(solution)/shard_map/ppermute | solution.py:210
  47.4 16.8 %collective-permute-start.16 = (bf16[96,1024]{1,0:T(8,128)(2,1)S(1)}, bf16[96,1024]{1,0:T(8,128)(2,1)S(1)}, u32[]{:S(2)}, u32[]{:S(2)}) collective-permute-start(bf16[96,1024]{1,0:T(8,128)(2,1)S(1)} %add_convert_fusion.1), channel_id=1, source_target_pairs={{0,12},{4,0},{8,4},{12,8},{1,13},{5,1},{9,5},{13,9},{2,14},{6,2},{... | collective-permute-start | bytes 589832 | tf_op jit(solution)/shard_map/ppermute | solution.py:210
  53.1 16.9 %collective-permute-start.13 = (bf16[96,1024]{1,0:T(8,128)(2,1)S(1)}, bf16[96,1024]{1,0:T(8,128)(2,1)S(1)}, u32[]{:S(2)}, u32[]{:S(2)}) collective-permute-start(bf16[96,1024]{1,0:T(8,128)(2,1)S(1)} %add_convert_fusion.2), channel_id=1, source_target_pairs={{0,4},{4,8},{8,12},{12,0},{1,5},{5,9},{9,13},{13,1},{2,6},{6,10},{... | collective-permute-start | bytes 589832 | tf_op jit(solution)/shard_map/ppermute | solution.py:210
  55.8 16.5 %collective-permute-start.10 = (bf16[96,1024]{1,0:T(8,128)(2,1)S(1)}, bf16[96,1024]{1,0:T(8,128)(2,1)S(1)}, u32[]{:S(2)}, u32[]{:S(2)}) collective-permute-start(bf16[96,1024]{1,0:T(8,128)(2,1)S(1)} %add_convert_fusion.3), channel_id=1, source_target_pairs={{0,12},{4,0},{8,4},{12,8},{1,13},{5,1},{9,5},{13,9},{2,14},{6,2},{... | collective-permute-start | bytes 589832 | tf_op jit(solution)/shard_map/ppermute | solution.py:210

commit v16 on v15

--- a/solution.py
+++ b/solution.py
@@ -10,6 +10,7 @@
 PIECES = 4
 STEP = 256
 LANES = 128
+PACK_COST = 20 * 10**9
 WRITES = 4
 VMEM_BYTES = 24 * 1024 * 1024
 ROWS_AT_ONCE = 1024
@@ -241,6 +242,7 @@
         (shape((pairs, lat, wide)), edge, edge),
         (jnp.transpose(weather, (1, 2, 0)),),
         moved=weather.size * 10,
+        flops=PACK_COST,
     )
     before = turned(high, "tok", 1)
     after = turned(low, "tok", -1)

time: 73.3 us -> 71.8 us (0.980)
  starting transfers between devices: 24.3 us -> 35.8 us
  waiting for transfers between devices: 32.1 us -> 22 us
  local copies, waits for them, and re-layouts: 4.05 us -> 1.22 us
    ppermute x17, starting transfers between devices: 22.3 us -> 33.8 us  [turned(): lax.ppermute(value, axis, [(i, (i + away) % count) for i in range(count)])]
    ppermute x17, waiting for transfers between devices: 32 us -> 22 us  [turned(): lax.ppermute(value, axis, [(i, (i + away) % count) for i in range(count)])]
    unnamed x11 -> x13, local copies, waits for them, and re-layouts: 4.04 us -> 1.21 us
  transfers between devices with their start and end apart: 20 -> 20, of which waited for: 12 -> 13; matrix products, arithmetic and copies ran while one was open for 0% -> 0% of each run, Pallas kernels for 13% -> 14%
where the time goes in v16:
time: 71.8 us; the launch traced here: 71.7 us
  starting transfers between devices  35.8 us (50%)
  waiting for transfers between devices  22 us (31%)
  Pallas kernels  12.3 us (17%)
  local copies, waits for them, and re-layouts  1.22 us (2%)
    ppermute x17, starting transfers between devices, turned(): lax.ppermute(value, axis, [(i, (i + away) % count) for i in range(count)])  33.8 us
    ppermute x17, waiting for transfers between devices, turned(): lax.ppermute(value, axis, [(i, (i + away) % count) for i in range(count)])  22 us
    pallas_call x13, Pallas kernels, call(): pl.pallas_call(kernel, out_shape=out_shape, in_specs=[pl.BlockSpec(memory...  9.27 us
    pallas_call x4, Pallas kernels, finish(): pl.pallas_call(functools.partial(last_kernel, first), out_shape=jax.Shape...  3.03 us
    ppermute x3, starting transfers between devices, direct_blocks(): blocks.append(lax.ppermute(block, ('ch', 'sub'), route))  1.93 us
  transfers between devices with their start and end apart: 20, of which 13 were waited for; matrix products, arithmetic and copies ran while one was open for 0% of the time, Pallas kernels for 14%

profile of v16, /device:TPU:0, one launch (start us, length us, event | category | flops | bytes accessed | tf_op | source)
XLA Modules:
  0.0 71.7 jit_solution(6680076162266190733)
XLA Ops:
  0.0 1.2 %copy-done.3 = f32[64,32,32]{0,2,1:T(8,128)S(1)} copy-done((f32[64,32,32]{0,2,1:T(8,128)S(1)}, f32[64,32,32]{0,2,1:T(8,128)}, u32[]{:S(2)}) %copy-start.3) | copy-done | bytes 262168
  1.2 0.1 shard_map.55
  1.3 3.0 %collective-permute-start.1 = (bf16[16,32,128]{2,1,0:T(8,128)(2,1)S(1)}, bf16[16,32,128]{2,1,0:T(8,128)(2,1)S(1)}, u32[]{:S(2)}, u32[]{:S(2)}) collective-permute-start(bf16[16,32,128]{2,1,0:T(8,128)(2,1)S(1)} %get-tuple-element.22.refs_0_), channel_id=1, source_target_pairs={{0,2},{2,0},{1,3},{3,1},{4,6},{6,4},{5,7},{7,5},{8,10},{10,8},{9,1... | collective-permute-start | bytes 393224 | tf_op jit(solution)/shard_map/ppermute | solution.py:211
  4.3 1.6 %collective-permute-start.3 = (bf16[1,32,128]{2,1,0:T(8,128)(2,1)S(1)}, bf16[1,32,128]{2,1,0:T(8,128)(2,1)S(1)}, u32[]{:S(2)}, u32[]{:S(2)}) collective-permute-start(bf16[1,32,128]{2,1,0:T(8,128)(2,1)S(1)} %get-tuple-element.23), channel_id=1, source_target_pairs={{0,4},{4,8},{8,12},{12,0},{1,5},{5,9},{9,13},{13,1},{2,6},{6,10},{... | collective-permute-start | bytes 24584 | tf_op jit(solution)/shard_map/ppermute | solution.py:211
  5.9 2.2 %collective-permute-start.4 = (bf16[1,32,128]{2,1,0:T(8,128)(2,1)S(1)}, bf16[1,32,128]{2,1,0:T(8,128)(2,1)S(1)}, u32[]{:S(2)}, u32[]{:S(2)}) collective-permute-start(bf16[1,32,128]{2,1,0:T(8,128)(2,1)S(1)} %get-tuple-element.24), channel_id=1, source_target_pairs={{0,12},{4,0},{8,4},{12,8},{1,13},{5,1},{9,5},{13,9},{2,14},{6,2},{... | collective-permute-start | bytes 24584 | tf_op jit(solution)/shard_map/ppermute | solution.py:211
  8.2 0.6 shard_map.57
  8.8 0.3 collective-permute-start.2
  9.1 0.7 collective-permute-done.3
  9.8 0.1 collective-permute-start.5
  9.9 0.4 collective-permute-start.6
  10.2 1.5 %collective-permute-start.7 = (bf16[2,32,128]{2,1,0:T(8,128)(2,1)S(1)}, bf16[2,32,128]{2,1,0:T(8,128)(2,1)S(1)}, u32[]{:S(2)}, u32[]{:S(2)}) collective-permute-start(bf16[2,32,128]{2,1,0:T(8,128)(2,1)S(1)} %constant_dynamic-update-slice_fusion.refs_0_), channel_id=1, source_target_pairs={{0,3},{1,2},{2,1},{3,0},{4,7},{5,6},{6,5},{7,4},{8,11},{9,10},{10,... | collective-permute-start | bytes 49160 | tf_op jit(solution)/shard_map/ppermute | solution.py:230
  11.8 2.4 %shard_map.58 = (bf16[384,768]{1,0:T(8,128)(2,1)S(1)}, bf16[4,128,128]{2,1,0:T(8,128)(2,1)S(1)}, bf16[4,128,128]{2,1,0:T(8,128)(2,1)S(1)}) custom-call(bf16[16,128,128]{2,1,0:T(8,128)(2,1)S(1)} %shard_map.56.field_ref, bf16[256,768]{1,0:T(8,128)(2,1)S(1)} %get-tuple-element.25.taps_one_ref.refs_6_, ...), custom_call_target="tpu_custom_call" | custom-call | flops 1635778560 | bytes 524288 | tf_op jit(solution)/shard_map/pallas_call | solution.py:198
  14.2 1.2 %shard_map.59.tokens_ref = bf16[384,1024]{1,0:T(8,128)(2,1)S(1)} custom-call(bf16[16,128,128]{2,1,0:T(8,128)(2,1)S(1)} %shard_map.56.field_ref, bf16[2,32,128]{2,1,0:T(8,128)(2,1)S(1)} %constant_dynamic-update-slice_fusion.refs_0_, bf16[2,32,128]{2,1,0:T(8,128)(2,1)S(1)} %collective-permute-done.5.refs_1_, ...), custom_call_target="tpu_custom_call" | custom-call | flops 503316480 | bytes 524288 | tf_op jit(solution)/shard_map/pallas_call | solution.py:198
  15.4 0.5 shard_map.66
  15.9 1.3 %collective-permute-start.17 = (bf16[96,1024]{1,0:T(8,128)(2,1)S(1)}, bf16[96,1024]{1,0:T(8,128)(2,1)S(1)}, u32[]{:S(2)}, u32[]{:S(2)}) collective-permute-start(bf16[96,1024]{1,0:T(8,128)(2,1)S(1)} %shard_map.66), channel_id=1, source_target_pairs={{0,4},{4,8},{8,12},{12,0},{1,5},{5,9},{9,13},{13,1},{2,6},{6,10},{... | collective-permute-start | bytes 589832 | tf_op jit(solution)/shard_map/ppermute | solution.py:211
  17.2 0.5 shard_map.64
  17.7 2.6 %collective-permute-start.14 = (bf16[96,1024]{1,0:T(8,128)(2,1)S(1)}, bf16[96,1024]{1,0:T(8,128)(2,1)S(1)}, u32[]{:S(2)}, u32[]{:S(2)}) collective-permute-start(bf16[96,1024]{1,0:T(8,128)(2,1)S(1)} %shard_map.64), channel_id=1, source_target_pairs={{0,12},{4,0},{8,4},{12,8},{1,13},{5,1},{9,5},{13,9},{2,14},{6,2},{... | collective-permute-start | bytes 589832 | tf_op jit(solution)/shard_map/ppermute | solution.py:211
  20.3 0.5 shard_map.62
  20.8 0.5 shard_map.60
  21.3 3.9 %collective-permute-start.8 = (bf16[96,1024]{1,0:T(8,128)(2,1)S(1)}, bf16[96,1024]{1,0:T(8,128)(2,1)S(1)}, u32[]{:S(2)}, u32[]{:S(2)}) collective-permute-start(bf16[96,1024]{1,0:T(8,128)(2,1)S(1)} %shard_map.60), channel_id=1, source_target_pairs={{0,12},{4,0},{8,4},{12,8},{1,13},{5,1},{9,5},{13,9},{2,14},{6,2},{... | collective-permute-start | bytes 589832 | tf_op jit(solution)/shard_map/ppermute | solution.py:211
  25.2 0.3 collective-permute-done.17.arrived_ref
  25.5 0.8 %shard_map.67 = (bf16[96,1024]{1,0:T(8,128)(2,1)S(1)}, f32[192,1024]{1,0:T(8,128)S(1)}) custom-call(bf16[96,1024]{1,0:T(8,128)(2,1)S(1)} %collective-permute-done.17.arrived_ref, bf16[384,1024]{1,0:T(8,128)(2,1)S(1)} %shard_map.59.tokens_ref, bf16[1024,4096]{1,0:T(8,128)(2,1)S(1)} %bitcast.2), custom_call_target="tpu_custom_call" | custom-call | tf_op jit(solution)/shard_map/pallas_call | solution.py:198
  26.3 2.4 %collective-permute-start.18 = (bf16[96,1024]{1,0:T(8,128)(2,1)S(1)}, bf16[96,1024]{1,0:T(8,128)(2,1)S(1)}, u32[]{:S(2)}, u32[]{:S(2)}) collective-permute-start(bf16[96,1024]{1,0:T(8,128)(2,1)S(1)} %get-tuple-element.37), channel_id=1, source_target_pairs={{0,4},{4,8},{8,12},{12,0},{1,5},{5,9},{9,13},{13,1},{2,6},{6,10},{... | collective-permute-start | bytes 589832 | tf_op jit(solution)/shard_map/ppermute | solution.py:211
  28.7 1.1 %collective-permute-done.14.arrived_ref = bf16[96,1024]{1,0:T(8,128)(2,1)S(1)} collective-permute-done((bf16[96,1024]{1,0:T(8,128)(2,1)S(1)}, bf16[96,1024]{1,0:T(8,128)(2,1)S(1)}, u32[]{:S(2)}, u32[]{:S(2)}) %collective-permute-start.14) | collective-permute-done | bytes 196640 | tf_op jit(solution)/shard_map/ppermute | solution.py:211
  29.8 0.8 %shard_map.65 = (bf16[96,1024]{1,0:T(8,128)(2,1)S(1)}, f32[192,1024]{1,0:T(8,128)S(1)}) custom-call(bf16[96,1024]{1,0:T(8,128)(2,1)S(1)} %collective-permute-done.14.arrived_ref, bf16[384,1024]{1,0:T(8,128)(2,1)S(1)} %shard_map.59.tokens_ref, bf16[1024,4096]{1,0:T(8,128)(2,1)S(1)} %bitcast.2), custom_call_target="tpu_custom_call" | custom-call | tf_op jit(solution)/shard_map/pallas_call | solution.py:198
  30.6 2.8 %collective-permute-start.15 = (bf16[96,1024]{1,0:T(8,128)(2,1)S(1)}, bf16[96,1024]{1,0:T(8,128)(2,1)S(1)}, u32[]{:S(2)}, u32[]{:S(2)}) collective-permute-start(bf16[96,1024]{1,0:T(8,128)(2,1)S(1)} %get-tuple-element.35), channel_id=1, source_target_pairs={{0,12},{4,0},{8,4},{12,8},{1,13},{5,1},{9,5},{13,9},{2,14},{6,2},{... | collective-permute-start | bytes 589832 | tf_op jit(solution)/shard_map/ppermute | solution.py:211
  33.3 0.7 collective-permute-done.11.arrived_ref
  34.0 0.8 %shard_map.63 = (bf16[96,1024]{1,0:T(8,128)(2,1)S(1)}, f32[192,1024]{1,0:T(8,128)S(1)}) custom-call(bf16[96,1024]{1,0:T(8,128)(2,1)S(1)} %collective-permute-done.11.arrived_ref, bf16[384,1024]{1,0:T(8,128)(2,1)S(1)} %shard_map.59.tokens_ref, bf16[1024,4096]{1,0:T(8,128)(2,1)S(1)} %bitcast.2), custom_call_target="tpu_custom_call" | custom-call | tf_op jit(solution)/shard_map/pallas_call | solution.py:198
  34.8 2.3 %collective-permute-start.12 = (bf16[96,1024]{1,0:T(8,128)(2,1)S(1)}, bf16[96,1024]{1,0:T(8,128)(2,1)S(1)}, u32[]{:S(2)}, u32[]{:S(2)}) collective-permute-start(bf16[96,1024]{1,0:T(8,128)(2,1)S(1)} %get-tuple-element.33), channel_id=1, source_target_pairs={{0,4},{4,8},{8,12},{12,0},{1,5},{5,9},{9,13},{13,1},{2,6},{6,10},{... | collective-permute-start | bytes 589832 | tf_op jit(solution)/shard_map/ppermute | solution.py:211
  37.1 1.1 %collective-permute-done.8.arrived_ref = bf16[96,1024]{1,0:T(8,128)(2,1)S(1)} collective-permute-done((bf16[96,1024]{1,0:T(8,128)(2,1)S(1)}, bf16[96,1024]{1,0:T(8,128)(2,1)S(1)}, u32[]{:S(2)}, u32[]{:S(2)}) %collective-permute-start.8) | collective-permute-done | bytes 196640 | tf_op jit(solution)/shard_map/ppermute | solution.py:211
  38.2 0.8 %shard_map.61 = (bf16[96,1024]{1,0:T(8,128)(2,1)S(1)}, f32[192,1024]{1,0:T(8,128)S(1)}) custom-call(bf16[96,1024]{1,0:T(8,128)(2,1)S(1)} %collective-permute-done.8.arrived_ref, bf16[384,1024]{1,0:T(8,128)(2,1)S(1)} %shard_map.59.tokens_ref, bf16[1024,4096]{1,0:T(8,128)(2,1)S(1)} %bitcast.2), custom_call_target="tpu_custom_call" | custom-call | tf_op jit(solution)/shard_map/pallas_call | solution.py:198
  39.0 2.8 %collective-permute-start.9 = (bf16[96,1024]{1,0:T(8,128)(2,1)S(1)}, bf16[96,1024]{1,0:T(8,128)(2,1)S(1)}, u32[]{:S(2)}, u32[]{:S(2)}) collective-permute-start(bf16[96,1024]{1,0:T(8,128)(2,1)S(1)} %get-tuple-element.31), channel_id=1, source_target_pairs={{0,12},{4,0},{8,4},{12,8},{1,13},{5,1},{9,5},{13,9},{2,14},{6,2},{... | collective-permute-start | bytes 589832 | tf_op jit(solution)/shard_map/ppermute | solution.py:211
  41.7 0.7 collective-permute-done.18
  42.5 2.2 %collective-permute-start.19 = (bf16[96,1024]{1,0:T(8,128)(2,1)S(1)}, bf16[96,1024]{1,0:T(8,128)(2,1)S(1)}, u32[]{:S(2)}, u32[]{:S(2)}) collective-permute-start(bf16[96,1024]{1,0:T(8,128)(2,1)S(1)} %add_convert_fusion), channel_id=1, source_target_pairs={{0,4},{4,8},{8,12},{12,0},{1,5},{5,9},{9,13},{13,1},{2,6},{6,10},{... | collective-permute-start | bytes 589832 | tf_op jit(solution)/shard_map/ppermute | solution.py:211
  44.7 1.9 %collective-permute-done.15 = bf16[96,1024]{1,0:T(8,128)(2,1)S(1)} collective-permute-done((bf16[96,1024]{1,0:T(8,128)(2,1)S(1)}, bf16[96,1024]{1,0:T(8,128)(2,1)S(1)}, u32[]{:S(2)}, u32[]{:S(2)}) %collective-permute-start.15) | collective-permute-done | bytes 196640 | tf_op jit(solution)/shard_map/ppermute | solution.py:211
  46.6 2.1 %collective-permute-start.16 = (bf16[96,1024]{1,0:T(8,128)(2,1)S(1)}, bf16[96,1024]{1,0:T(8,128)(2,1)S(1)}, u32[]{:S(2)}, u32[]{:S(2)}) collective-permute-start(bf16[96,1024]{1,0:T(8,128)(2,1)S(1)} %add_convert_fusion.1), channel_id=1, source_target_pairs={{0,12},{4,0},{8,4},{12,8},{1,13},{5,1},{9,5},{13,9},{2,14},{6,2},{... | collective-permute-start | bytes 589832 | tf_op jit(solution)/shard_map/ppermute | solution.py:211
  48.7 2.2 %collective-permute-done.12 = bf16[96,1024]{1,0:T(8,128)(2,1)S(1)} collective-permute-done((bf16[96,1024]{1,0:T(8,128)(2,1)S(1)}, bf16[96,1024]{1,0:T(8,128)(2,1)S(1)}, u32[]{:S(2)}, u32[]{:S(2)}) %collective-permute-start.12) | collective-permute-done | bytes 196640 | tf_op jit(solution)/shard_map/ppermute | solution.py:211
  51.0 2.1 %collective-permute-start.13 = (bf16[96,1024]{1,0:T(8,128)(2,1)S(1)}, bf16[96,1024]{1,0:T(8,128)(2,1)S(1)}, u32[]{:S(2)}, u32[]{:S(2)}) collective-permute-start(bf16[96,1024]{1,0:T(8,128)(2,1)S(1)} %add_convert_fusion.2), channel_id=1, source_target_pairs={{0,4},{4,8},{8,12},{12,0},{1,5},{5,9},{9,13},{13,1},{2,6},{6,10},{... | collective-permute-start | bytes 589832 | tf_op jit(solution)/shard_map/ppermute | solution.py:211
  53.1 1.9 %collective-permute-done.9 = bf16[96,1024]{1,0:T(8,128)(2,1)S(1)} collective-permute-done((bf16[96,1024]{1,0:T(8,128)(2,1)S(1)}, bf16[96,1024]{1,0:T(8,128)(2,1)S(1)}, u32[]{:S(2)}, u32[]{:S(2)}) %collective-permute-start.9) | collective-permute-done | bytes 196640 | tf_op jit(solution)/shard_map/ppermute | solution.py:211
  55.0 2.1 %collective-permute-start.10 = (bf16[96,1024]{1,0:T(8,128)(2,1)S(1)}, bf16[96,1024]{1,0:T(8,128)(2,1)S(1)}, u32[]{:S(2)}, u32[]{:S(2)}) collective-permute-start(bf16[96,1024]{1,0:T(8,128)(2,1)S(1)} %add_convert_fusion.3), channel_id=1, source_target_pairs={{0,12},{4,0},{8,4},{12,8},{1,13},{5,1},{9,5},{13,9},{2,14},{6,2},{... | collective-permute-start | bytes 589832 | tf_op jit(solution)/shard_map/ppermute | solution.py:211
  57.1 2.2 %collective-permute-done.19.arrived_ref = bf16[96,1024]{1,0:T(8,128)(2,1)S(1)} collective-permute-done((bf16[96,1024]{1,0:T(8,128)(2,1)S(1)}, bf16[96,1024]{1,0:T(8,128)(2,1)S(1)}, u32[]{:S(2)}, u32[]{:S(2)}) %collective-permute-start.19) | collective-permute-done | bytes 196640 | tf_op jit(solution)/shard_map/ppermute | solution.py:211
  59.4 0.8 %shard_map.68.refs_0_ = bf16[96,4096]{1,0:T(8,128)(2,1)} custom-call(bf16[96,1024]{1,0:T(8,128)(2,1)S(1)} %collective-permute-done.19.arrived_ref, f32[192,1024]{1,0:T(8,128)S(1)} %get-tuple-element.38.kept_ref), custom_call_target="tpu_custom_call" | custom-call | tf_op jit(solution)/shard_map/pallas_call | solution.py:328
  60.2 3.2 %collective-permute-done.16.arrived_ref = bf16[96,1024]{1,0:T(8,128)(2,1)S(1)} collective-permute-done((bf16[96,1024]{1,0:T(8,128)(2,1)S(1)}, bf16[96,1024]{1,0:T(8,128)(2,1)S(1)}, u32[]{:S(2)}, u32[]{:S(2)}) %collective-permute-start.16) | collective-permute-done | bytes 196640 | tf_op jit(solution)/shard_map/ppermute | solution.py:211
  63.3 0.8 %shard_map.69.refs_0_ = bf16[96,4096]{1,0:T(8,128)(2,1)} custom-call(bf16[96,1024]{1,0:T(8,128)(2,1)S(1)} %collective-permute-done.16.arrived_ref, f32[192,1024]{1,0:T(8,128)S(1)} %get-tuple-element.36.kept_ref, bf16[96,4096]{1,0:T(8,128)(2,1)} %shard_map.68.refs_0_), custom_call_target="tpu_custom_call", output_to_operand_aliasing={{}: (2, {})} | custom-call | tf_op jit(solution)/shard_map/pallas_call | solution.py:328
  64.1 3.8 %collective-permute-done.13.arrived_ref = bf16[96,1024]{1,0:T(8,128)(2,1)S(1)} collective-permute-done((bf16[96,1024]{1,0:T(8,128)(2,1)S(1)}, bf16[96,1024]{1,0:T(8,128)(2,1)S(1)}, u32[]{:S(2)}, u32[]{:S(2)}) %collective-permute-start.13) | collective-permute-done | bytes 196640 | tf_op jit(solution)/shard_map/ppermute | solution.py:211
  67.9 0.8 %shard_map.70.refs_0_ = bf16[96,4096]{1,0:T(8,128)(2,1)} custom-call(bf16[96,1024]{1,0:T(8,128)(2,1)S(1)} %collective-permute-done.13.arrived_ref, f32[192,1024]{1,0:T(8,128)S(1)} %get-tuple-element.34.kept_ref, bf16[96,4096]{1,0:T(8,128)(2,1)} %shard_map.69.refs_0_), custom_call_target="tpu_custom_call", output_to_operand_aliasing={{}: (2, {})} | custom-call | tf_op jit(solution)/shard_map/pallas_call | solution.py:328
  68.6 2.3 %collective-permute-done.10.arrived_ref = bf16[96,1024]{1,0:T(8,128)(2,1)S(1)} collective-permute-done((bf16[96,1024]{1,0:T(8,128)(2,1)S(1)}, bf16[96,1024]{1,0:T(8,128)(2,1)S(1)}, u32[]{:S(2)}, u32[]{:S(2)}) %collective-permute-start.10) | collective-permute-done | bytes 196640 | tf_op jit(solution)/shard_map/ppermute | solution.py:211
  70.9 0.8 %shard_map.71 = bf16[96,4096]{1,0:T(8,128)(2,1)} custom-call(bf16[96,1024]{1,0:T(8,128)(2,1)S(1)} %collective-permute-done.10.arrived_ref, f32[192,1024]{1,0:T(8,128)S(1)} %get-tuple-element.32.kept_ref, bf16[96,4096]{1,0:T(8,128)(2,1)} %shard_map.70.refs_0_), custom_call_target="tpu_custom_call", output_to_operand_aliasing={{}: (2, {})} | custom-call | tf_op jit(solution)/shard_map/pallas_call | solution.py:328
  (28 shorter events, 0.3 us)
Async XLA Ops:
  0.0 15.4 %slice-start = ((s8[8388608]{0:T(1024)(128)(4,1)}), s8[4194304]{0:T(1024)(128)(4,1)S(1)}, s32[]{:S(2)}) async-start(s8[8388608]{0:T(1024)(128)(4,1)} %bitcast.1), calls=%async_computation | async-start | bytes 8388608
  0.0 1.2 %copy-start.3 = (f32[64,32,32]{0,2,1:T(8,128)S(1)}, f32[64,32,32]{0,2,1:T(8,128)}, u32[]{:S(2)}) copy-start(f32[64,32,32]{0,2,1:T(8,128)} %param.5) | copy-start | bytes 786436
  1.2 7.0 %copy-start = (f32[9,64,64]{2,1,0:T(8,128)S(1)}, f32[9,64,64]{2,1,0:T(8,128)}, u32[]{:S(2)}) copy-start(f32[9,64,64]{2,1,0:T(8,128)} %first_ref.1) | copy-start | bytes 442372
  1.2 7.0 %copy-start.1 = (f32[9,64,64]{2,1,0:T(8,128)S(1)}, f32[9,64,64]{2,1,0:T(8,128)}, u32[]{:S(2)}) copy-start(f32[9,64,64]{2,1,0:T(8,128)} %second_ref.1) | copy-start | bytes 442372
  1.2 7.0 %copy-start.2 = (bf16[256,384]{1,0:T(8,128)(2,1)S(1)}, bf16[256,384]{1,0:T(8,128)(2,1)}, u32[]{:S(2)}) copy-start(bf16[256,384]{1,0:T(8,128)(2,1)} %embed_ref.1) | copy-start | bytes 589828
  1.2 14.2 %slice-start.1 = ((s8[8388608]{0:T(1024)(128)(4,1)}), s8[4194304]{0:T(1024)(128)(4,1)S(1)}, s32[]{:S(2)}) async-start(s8[8388608]{0:T(1024)(128)(4,1)} %bitcast.1), calls=%async_computation.1 | async-start | bytes 8388608
  1.3 7.4 %collective-permute-start.1 = (bf16[16,32,128]{2,1,0:T(8,128)(2,1)S(1)}, bf16[16,32,128]{2,1,0:T(8,128)(2,1)S(1)}, u32[]{:S(2)}, u32[]{:S(2)}) collective-permute-start(bf16[16,32,128]{2,1,0:T(8,128)(2,1)S(1)} %get-tuple-element.22.refs_0_), channel_id=1, source_target_pairs={{0,2},{2,0},{1,3},{3,1},{4,6},{6,4},{5,7},{7,5},{8,10},{10,8},{9,1... | collective-permute-start | bytes 393224 | tf_op jit(solution)/shard_map/ppermute | solution.py:211
  4.3 5.4 %collective-permute-start.3 = (bf16[1,32,128]{2,1,0:T(8,128)(2,1)S(1)}, bf16[1,32,128]{2,1,0:T(8,128)(2,1)S(1)}, u32[]{:S(2)}, u32[]{:S(2)}) collective-permute-start(bf16[1,32,128]{2,1,0:T(8,128)(2,1)S(1)} %get-tuple-element.23), channel_id=1, source_target_pairs={{0,4},{4,8},{8,12},{12,0},{1,5},{5,9},{9,13},{13,1},{2,6},{6,10},{... | collective-permute-start | bytes 24584 | tf_op jit(solution)/shard_map/ppermute | solution.py:211
  5.9 5.8 %collective-permute-start = (bf16[16,32,128]{2,1,0:T(8,128)(2,1)S(1)}, bf16[16,32,128]{2,1,0:T(8,128)(2,1)S(1)}, u32[]{:S(2)}, u32[]{:S(2)}) collective-permute-start(bf16[16,32,128]{2,1,0:T(8,128)(2,1)S(1)} %get-tuple-element.22.refs_0_), channel_id=1, source_target_pairs={{0,1},{1,0},{2,3},{3,2},{4,5},{5,4},{6,7},{7,6},{8,9},{9,8},{10,11... | collective-permute-start | bytes 393224 | tf_op jit(solution)/shard_map/ppermute | solution.py:211
  5.9 3.9 %collective-permute-start.4 = (bf16[1,32,128]{2,1,0:T(8,128)(2,1)S(1)}, bf16[1,32,128]{2,1,0:T(8,128)(2,1)S(1)}, u32[]{:S(2)}, u32[]{:S(2)}) collective-permute-start(bf16[1,32,128]{2,1,0:T(8,128)(2,1)S(1)} %get-tuple-element.24), channel_id=1, source_target_pairs={{0,12},{4,0},{8,4},{12,8},{1,13},{5,1},{9,5},{13,9},{2,14},{6,2},{... | collective-permute-start | bytes 24584 | tf_op jit(solution)/shard_map/ppermute | solution.py:211
  8.8 3.0 %collective-permute-start.2 = (bf16[16,32,128]{2,1,0:T(8,128)(2,1)S(1)}, bf16[16,32,128]{2,1,0:T(8,128)(2,1)S(1)}, u32[]{:S(2)}, u32[]{:S(2)}) collective-permute-start(bf16[16,32,128]{2,1,0:T(8,128)(2,1)S(1)} %collective-permute-done.1.refs_2_), channel_id=1, source_target_pairs={{0,1},{1,0},{2,3},{3,2},{4,5},{5,4},{6,7},{7,6},{8,9},{9,8},{10,11... | collective-permute-start | bytes 393224 | tf_op jit(solution)/shard_map/ppermute | solution.py:211
  9.8 4.4 %collective-permute-start.5 = (bf16[2,32,128]{2,1,0:T(8,128)(2,1)S(1)}, bf16[2,32,128]{2,1,0:T(8,128)(2,1)S(1)}, u32[]{:S(2)}, u32[]{:S(2)}) collective-permute-start(bf16[2,32,128]{2,1,0:T(8,128)(2,1)S(1)} %constant_dynamic-update-slice_fusion.refs_0_), channel_id=1, source_target_pairs={{0,1},{1,0},{2,3},{3,2},{4,5},{5,4},{6,7},{7,6},{8,9},{9,8},{10,11... | collective-permute-start | bytes 49160 | tf_op jit(solution)/shard_map/ppermute | solution.py:230
  9.9 4.3 %collective-permute-start.6 = (bf16[2,32,128]{2,1,0:T(8,128)(2,1)S(1)}, bf16[2,32,128]{2,1,0:T(8,128)(2,1)S(1)}, u32[]{:S(2)}, u32[]{:S(2)}) collective-permute-start(bf16[2,32,128]{2,1,0:T(8,128)(2,1)S(1)} %constant_dynamic-update-slice_fusion.refs_0_), channel_id=1, source_target_pairs={{0,2},{1,3},{2,0},{3,1},{4,6},{5,7},{6,4},{7,5},{8,10},{9,11},{10,... | collective-permute-start | bytes 49160 | tf_op jit(solution)/shard_map/ppermute | solution.py:230
  10.2 4.0 %collective-permute-start.7 = (bf16[2,32,128]{2,1,0:T(8,128)(2,1)S(1)}, bf16[2,32,128]{2,1,0:T(8,128)(2,1)S(1)}, u32[]{:S(2)}, u32[]{:S(2)}) collective-permute-start(bf16[2,32,128]{2,1,0:T(8,128)(2,1)S(1)} %constant_dynamic-update-slice_fusion.refs_0_), channel_id=1, source_target_pairs={{0,3},{1,2},{2,1},{3,0},{4,7},{5,6},{6,5},{7,4},{8,11},{9,10},{10,... | collective-permute-start | bytes 49160 | tf_op jit(solution)/shard_map/ppermute | solution.py:230
  15.9 9.6 %collective-permute-start.17 = (bf16[96,1024]{1,0:T(8,128)(2,1)S(1)}, bf16[96,1024]{1,0:T(8,128)(2,1)S(1)}, u32[]{:S(2)}, u32[]{:S(2)}) collective-permute-start(bf16[96,1024]{1,0:T(8,128)(2,1)S(1)} %shard_map.66), channel_id=1, source_target_pairs={{0,4},{4,8},{8,12},{12,0},{1,5},{5,9},{9,13},{13,1},{2,6},{6,10},{... | collective-permute-start | bytes 589832 | tf_op jit(solution)/shard_map/ppermute | solution.py:211
  17.7 12.1 %collective-permute-start.14 = (bf16[96,1024]{1,0:T(8,128)(2,1)S(1)}, bf16[96,1024]{1,0:T(8,128)(2,1)S(1)}, u32[]{:S(2)}, u32[]{:S(2)}) collective-permute-start(bf16[96,1024]{1,0:T(8,128)(2,1)S(1)} %shard_map.64), channel_id=1, source_target_pairs={{0,12},{4,0},{8,4},{12,8},{1,13},{5,1},{9,5},{13,9},{2,14},{6,2},{... | collective-permute-start | bytes 589832 | tf_op jit(solution)/shard_map/ppermute | solution.py:211
  20.8 13.2 %collective-permute-start.11 = (bf16[96,1024]{1,0:T(8,128)(2,1)S(1)}, bf16[96,1024]{1,0:T(8,128)(2,1)S(1)}, u32[]{:S(2)}, u32[]{:S(2)}) collective-permute-start(bf16[96,1024]{1,0:T(8,128)(2,1)S(1)} %shard_map.62), channel_id=1, source_target_pairs={{0,4},{4,8},{8,12},{12,0},{1,5},{5,9},{9,13},{13,1},{2,6},{6,10},{... | collective-permute-start | bytes 589832 | tf_op jit(solution)/shard_map/ppermute | solution.py:211
  21.3 16.9 %collective-permute-start.8 = (bf16[96,1024]{1,0:T(8,128)(2,1)S(1)}, bf16[96,1024]{1,0:T(8,128)(2,1)S(1)}, u32[]{:S(2)}, u32[]{:S(2)}) collective-permute-start(bf16[96,1024]{1,0:T(8,128)(2,1)S(1)} %shard_map.60), channel_id=1, source_target_pairs={{0,12},{4,0},{8,4},{12,8},{1,13},{5,1},{9,5},{13,9},{2,14},{6,2},{... | collective-permute-start | bytes 589832 | tf_op jit(solution)/shard_map/ppermute | solution.py:211
  26.3 16.2 %collective-permute-start.18 = (bf16[96,1024]{1,0:T(8,128)(2,1)S(1)}, bf16[96,1024]{1,0:T(8,128)(2,1)S(1)}, u32[]{:S(2)}, u32[]{:S(2)}) collective-permute-start(bf16[96,1024]{1,0:T(8,128)(2,1)S(1)} %get-tuple-element.37), channel_id=1, source_target_pairs={{0,4},{4,8},{8,12},{12,0},{1,5},{5,9},{9,13},{13,1},{2,6},{6,10},{... | collective-permute-start | bytes 589832 | tf_op jit(solution)/shard_map/ppermute | solution.py:211
  30.6 16.0 %collective-permute-start.15 = (bf16[96,1024]{1,0:T(8,128)(2,1)S(1)}, bf16[96,1024]{1,0:T(8,128)(2,1)S(1)}, u32[]{:S(2)}, u32[]{:S(2)}) collective-permute-start(bf16[96,1024]{1,0:T(8,128)(2,1)S(1)} %get-tuple-element.35), channel_id=1, source_target_pairs={{0,12},{4,0},{8,4},{12,8},{1,13},{5,1},{9,5},{13,9},{2,14},{6,2},{... | collective-permute-start | bytes 589832 | tf_op jit(solution)/shard_map/ppermute | solution.py:211
  34.8 16.2 %collective-permute-start.12 = (bf16[96,1024]{1,0:T(8,128)(2,1)S(1)}, bf16[96,1024]{1,0:T(8,128)(2,1)S(1)}, u32[]{:S(2)}, u32[]{:S(2)}) collective-permute-start(bf16[96,1024]{1,0:T(8,128)(2,1)S(1)} %get-tuple-element.33), channel_id=1, source_target_pairs={{0,4},{4,8},{8,12},{12,0},{1,5},{5,9},{9,13},{13,1},{2,6},{6,10},{... | collective-permute-start | bytes 589832 | tf_op jit(solution)/shard_map/ppermute | solution.py:211
  39.0 16.0 %collective-permute-start.9 = (bf16[96,1024]{1,0:T(8,128)(2,1)S(1)}, bf16[96,1024]{1,0:T(8,128)(2,1)S(1)}, u32[]{:S(2)}, u32[]{:S(2)}) collective-permute-start(bf16[96,1024]{1,0:T(8,128)(2,1)S(1)} %get-tuple-element.31), channel_id=1, source_target_pairs={{0,12},{4,0},{8,4},{12,8},{1,13},{5,1},{9,5},{13,9},{2,14},{6,2},{... | collective-permute-start | bytes 589832 | tf_op jit(solution)/shard_map/ppermute | solution.py:211
  42.5 16.9 %collective-permute-start.19 = (bf16[96,1024]{1,0:T(8,128)(2,1)S(1)}, bf16[96,1024]{1,0:T(8,128)(2,1)S(1)}, u32[]{:S(2)}, u32[]{:S(2)}) collective-permute-start(bf16[96,1024]{1,0:T(8,128)(2,1)S(1)} %add_convert_fusion), channel_id=1, source_target_pairs={{0,4},{4,8},{8,12},{12,0},{1,5},{5,9},{9,13},{13,1},{2,6},{6,10},{... | collective-permute-start | bytes 589832 | tf_op jit(solution)/shard_map/ppermute | solution.py:211
  46.6 16.7 %collective-permute-start.16 = (bf16[96,1024]{1,0:T(8,128)(2,1)S(1)}, bf16[96,1024]{1,0:T(8,128)(2,1)S(1)}, u32[]{:S(2)}, u32[]{:S(2)}) collective-permute-start(bf16[96,1024]{1,0:T(8,128)(2,1)S(1)} %add_convert_fusion.1), channel_id=1, source_target_pairs={{0,12},{4,0},{8,4},{12,8},{1,13},{5,1},{9,5},{13,9},{2,14},{6,2},{... | collective-permute-start | bytes 589832 | tf_op jit(solution)/shard_map/ppermute | solution.py:211
  51.0 16.9 %collective-permute-start.13 = (bf16[96,1024]{1,0:T(8,128)(2,1)S(1)}, bf16[96,1024]{1,0:T(8,128)(2,1)S(1)}, u32[]{:S(2)}, u32[]{:S(2)}) collective-permute-start(bf16[96,1024]{1,0:T(8,128)(2,1)S(1)} %add_convert_fusion.2), channel_id=1, source_target_pairs={{0,4},{4,8},{8,12},{12,0},{1,5},{5,9},{9,13},{13,1},{2,6},{6,10},{... | collective-permute-start | bytes 589832 | tf_op jit(solution)/shard_map/ppermute | solution.py:211
  55.0 15.9 %collective-permute-start.10 = (bf16[96,1024]{1,0:T(8,128)(2,1)S(1)}, bf16[96,1024]{1,0:T(8,128)(2,1)S(1)}, u32[]{:S(2)}, u32[]{:S(2)}) collective-permute-start(bf16[96,1024]{1,0:T(8,128)(2,1)S(1)} %add_convert_fusion.3), channel_id=1, source_target_pairs={{0,12},{4,0},{8,4},{12,8},{1,13},{5,1},{9,5},{13,9},{2,14},{6,2},{... | collective-permute-start | bytes 589832 | tf_op jit(solution)/shard_map/ppermute | solution.py:211

commit v17 on v16

--- a/solution.py
+++ b/solution.py
@@ -346,7 +346,7 @@
     rows = embed // count
     width = token_mixing.shape[1] // pieces
     sent = jax.ShapeDtypeStruct((rows, width), jnp.bfloat16)
-    ways = [1 if piece % 2 == 0 else -1 for piece in range(pieces)]
+    ways = [1] * pieces
     blocks = [list(range(count - 2, -1, -1)) if way == 1 else list(range(count - 1)) for way in ways]
     travelling = [
         call(functools.partial(sent_kernel, piece * width, blocks[piece][0]), sent, (tokens, token_mixing))

time: 71.8 us -> 72.3 us (level)
  waiting for transfers between devices: 22 us -> 43.5 us
  starting transfers between devices: 35.8 us -> 14.7 us
    ppermute x17, waiting for transfers between devices: 22 us -> 43.5 us  [turned(): lax.ppermute(value, axis, [(i, (i + away) % count) for i in range(count)])]
    ppermute x17, starting transfers between devices: 33.8 us -> 12.8 us  [turned(): lax.ppermute(value, axis, [(i, (i + away) % count) for i in range(count)])]
where the time goes in v17:
time: 72.3 us; the launch traced here: 72.2 us
  waiting for transfers between devices  43.5 us (60%)
  starting transfers between devices  14.7 us (20%)
  Pallas kernels  12.3 us (17%)
  local copies, waits for them, and re-layouts  1.22 us (2%)
    ppermute x17, waiting for transfers between devices, turned(): lax.ppermute(value, axis, [(i, (i + away) % count) for i in range(count)])  43.5 us
    ppermute x17, starting transfers between devices, turned(): lax.ppermute(value, axis, [(i, (i + away) % count) for i in range(count)])  12.8 us
    pallas_call x13, Pallas kernels, call(): pl.pallas_call(kernel, out_shape=out_shape, in_specs=[pl.BlockSpec(memory...  9.28 us
    pallas_call x4, Pallas kernels, finish(): pl.pallas_call(functools.partial(last_kernel, first), out_shape=jax.Shape...  3.03 us
    ppermute x3, starting transfers between devices, direct_blocks(): blocks.append(lax.ppermute(block, ('ch', 'sub'), route))  1.93 us
  transfers between devices with their start and end apart: 20, of which 13 were waited for; matrix products, arithmetic and copies ran while one was open for 0% of the time, Pallas kernels for 14%

profile of v17, /device:TPU:0, one launch (start us, length us, event | category | flops | bytes accessed | tf_op | source)
XLA Modules:
  0.0 72.2 jit_solution(10564700142964195724)
XLA Ops:
  0.0 1.2 %copy-done.3 = f32[64,32,32]{0,2,1:T(8,128)S(1)} copy-done((f32[64,32,32]{0,2,1:T(8,128)S(1)}, f32[64,32,32]{0,2,1:T(8,128)}, u32[]{:S(2)}) %copy-start.3) | copy-done | bytes 262168
  1.2 0.1 shard_map.55
  1.3 3.0 %collective-permute-start.1 = (bf16[16,32,128]{2,1,0:T(8,128)(2,1)S(1)}, bf16[16,32,128]{2,1,0:T(8,128)(2,1)S(1)}, u32[]{:S(2)}, u32[]{:S(2)}) collective-permute-start(bf16[16,32,128]{2,1,0:T(8,128)(2,1)S(1)} %get-tuple-element.22.refs_0_), channel_id=1, source_target_pairs={{0,2},{2,0},{1,3},{3,1},{4,6},{6,4},{5,7},{7,5},{8,10},{10,8},{9,1... | collective-permute-start | bytes 393224 | tf_op jit(solution)/shard_map/ppermute | solution.py:211
  4.3 1.6 %collective-permute-start.3 = (bf16[1,32,128]{2,1,0:T(8,128)(2,1)S(1)}, bf16[1,32,128]{2,1,0:T(8,128)(2,1)S(1)}, u32[]{:S(2)}, u32[]{:S(2)}) collective-permute-start(bf16[1,32,128]{2,1,0:T(8,128)(2,1)S(1)} %get-tuple-element.23), channel_id=1, source_target_pairs={{0,4},{4,8},{8,12},{12,0},{1,5},{5,9},{9,13},{13,1},{2,6},{6,10},{... | collective-permute-start | bytes 24584 | tf_op jit(solution)/shard_map/ppermute | solution.py:211
  5.9 2.2 %collective-permute-start.4 = (bf16[1,32,128]{2,1,0:T(8,128)(2,1)S(1)}, bf16[1,32,128]{2,1,0:T(8,128)(2,1)S(1)}, u32[]{:S(2)}, u32[]{:S(2)}) collective-permute-start(bf16[1,32,128]{2,1,0:T(8,128)(2,1)S(1)} %get-tuple-element.24), channel_id=1, source_target_pairs={{0,12},{4,0},{8,4},{12,8},{1,13},{5,1},{9,5},{13,9},{2,14},{6,2},{... | collective-permute-start | bytes 24584 | tf_op jit(solution)/shard_map/ppermute | solution.py:211
  8.2 0.6 shard_map.57
  8.8 0.3 collective-permute-start.2
  9.1 0.7 collective-permute-done.3
  9.8 0.1 collective-permute-start.5
  9.9 0.4 collective-permute-start.6
  10.2 1.5 %collective-permute-start.7 = (bf16[2,32,128]{2,1,0:T(8,128)(2,1)S(1)}, bf16[2,32,128]{2,1,0:T(8,128)(2,1)S(1)}, u32[]{:S(2)}, u32[]{:S(2)}) collective-permute-start(bf16[2,32,128]{2,1,0:T(8,128)(2,1)S(1)} %constant_dynamic-update-slice_fusion.refs_0_), channel_id=1, source_target_pairs={{0,3},{1,2},{2,1},{3,0},{4,7},{5,6},{6,5},{7,4},{8,11},{9,10},{10,... | collective-permute-start | bytes 49160 | tf_op jit(solution)/shard_map/ppermute | solution.py:230
  11.8 2.4 %shard_map.58 = (bf16[384,768]{1,0:T(8,128)(2,1)S(1)}, bf16[4,128,128]{2,1,0:T(8,128)(2,1)S(1)}, bf16[4,128,128]{2,1,0:T(8,128)(2,1)S(1)}) custom-call(bf16[16,128,128]{2,1,0:T(8,128)(2,1)S(1)} %shard_map.56.field_ref, bf16[256,768]{1,0:T(8,128)(2,1)S(1)} %get-tuple-element.25.taps_one_ref.refs_6_, ...), custom_call_target="tpu_custom_call" | custom-call | flops 1635778560 | bytes 524288 | tf_op jit(solution)/shard_map/pallas_call | solution.py:198
  14.2 1.2 %shard_map.59.tokens_ref = bf16[384,1024]{1,0:T(8,128)(2,1)S(1)} custom-call(bf16[16,128,128]{2,1,0:T(8,128)(2,1)S(1)} %shard_map.56.field_ref, bf16[2,32,128]{2,1,0:T(8,128)(2,1)S(1)} %constant_dynamic-update-slice_fusion.refs_0_, bf16[2,32,128]{2,1,0:T(8,128)(2,1)S(1)} %collective-permute-done.5.refs_1_, ...), custom_call_target="tpu_custom_call" | custom-call | flops 503316480 | bytes 524288 | tf_op jit(solution)/shard_map/pallas_call | solution.py:198
  15.4 0.5 shard_map.66
  15.9 1.3 %collective-permute-start.17 = (bf16[96,1024]{1,0:T(8,128)(2,1)S(1)}, bf16[96,1024]{1,0:T(8,128)(2,1)S(1)}, u32[]{:S(2)}, u32[]{:S(2)}) collective-permute-start(bf16[96,1024]{1,0:T(8,128)(2,1)S(1)} %shard_map.66), channel_id=1, source_target_pairs={{0,4},{4,8},{8,12},{12,0},{1,5},{5,9},{9,13},{13,1},{2,6},{6,10},{... | collective-permute-start | bytes 589832 | tf_op jit(solution)/shard_map/ppermute | solution.py:211
  17.2 0.5 shard_map.64
  17.7 1.6 %collective-permute-start.14 = (bf16[96,1024]{1,0:T(8,128)(2,1)S(1)}, bf16[96,1024]{1,0:T(8,128)(2,1)S(1)}, u32[]{:S(2)}, u32[]{:S(2)}) collective-permute-start(bf16[96,1024]{1,0:T(8,128)(2,1)S(1)} %shard_map.64), channel_id=1, source_target_pairs={{0,4},{4,8},{8,12},{12,0},{1,5},{5,9},{9,13},{13,1},{2,6},{6,10},{... | collective-permute-start | bytes 589832 | tf_op jit(solution)/shard_map/ppermute | solution.py:211
  19.3 0.5 shard_map.62
  19.8 2.1 %collective-permute-start.11 = (bf16[96,1024]{1,0:T(8,128)(2,1)S(1)}, bf16[96,1024]{1,0:T(8,128)(2,1)S(1)}, u32[]{:S(2)}, u32[]{:S(2)}) collective-permute-start(bf16[96,1024]{1,0:T(8,128)(2,1)S(1)} %shard_map.62), channel_id=1, source_target_pairs={{0,4},{4,8},{8,12},{12,0},{1,5},{5,9},{9,13},{13,1},{2,6},{6,10},{... | collective-permute-start | bytes 589832 | tf_op jit(solution)/shard_map/ppermute | solution.py:211
  21.9 0.5 shard_map.60
  22.3 0.1 collective-permute-start.8
  22.5 3.0 %collective-permute-done.17.arrived_ref = bf16[96,1024]{1,0:T(8,128)(2,1)S(1)} collective-permute-done((bf16[96,1024]{1,0:T(8,128)(2,1)S(1)}, bf16[96,1024]{1,0:T(8,128)(2,1)S(1)}, u32[]{:S(2)}, u32[]{:S(2)}) %collective-permute-start.17) | collective-permute-done | bytes 196640 | tf_op jit(solution)/shard_map/ppermute | solution.py:211
  25.5 0.8 %shard_map.67 = (bf16[96,1024]{1,0:T(8,128)(2,1)S(1)}, f32[192,1024]{1,0:T(8,128)S(1)}) custom-call(bf16[96,1024]{1,0:T(8,128)(2,1)S(1)} %collective-permute-done.17.arrived_ref, bf16[384,1024]{1,0:T(8,128)(2,1)S(1)} %shard_map.59.tokens_ref, bf16[1024,4096]{1,0:T(8,128)(2,1)S(1)} %bitcast.2), custom_call_target="tpu_custom_call" | custom-call | tf_op jit(solution)/shard_map/pallas_call | solution.py:198
  26.2 0.1 collective-permute-start.18
  26.3 3.4 %collective-permute-done.14.arrived_ref = bf16[96,1024]{1,0:T(8,128)(2,1)S(1)} collective-permute-done((bf16[96,1024]{1,0:T(8,128)(2,1)S(1)}, bf16[96,1024]{1,0:T(8,128)(2,1)S(1)}, u32[]{:S(2)}, u32[]{:S(2)}) %collective-permute-start.14) | collective-permute-done | bytes 196640 | tf_op jit(solution)/shard_map/ppermute | solution.py:211
  29.7 0.8 %shard_map.65 = (bf16[96,1024]{1,0:T(8,128)(2,1)S(1)}, f32[192,1024]{1,0:T(8,128)S(1)}) custom-call(bf16[96,1024]{1,0:T(8,128)(2,1)S(1)} %collective-permute-done.14.arrived_ref, bf16[384,1024]{1,0:T(8,128)(2,1)S(1)} %shard_map.59.tokens_ref, bf16[1024,4096]{1,0:T(8,128)(2,1)S(1)} %bitcast.2), custom_call_target="tpu_custom_call" | custom-call | tf_op jit(solution)/shard_map/pallas_call | solution.py:198
  30.5 0.1 collective-permute-start.15
  30.5 3.4 %collective-permute-done.11.arrived_ref = bf16[96,1024]{1,0:T(8,128)(2,1)S(1)} collective-permute-done((bf16[96,1024]{1,0:T(8,128)(2,1)S(1)}, bf16[96,1024]{1,0:T(8,128)(2,1)S(1)}, u32[]{:S(2)}, u32[]{:S(2)}) %collective-permute-start.11) | collective-permute-done | bytes 196640 | tf_op jit(solution)/shard_map/ppermute | solution.py:211
  33.9 0.8 %shard_map.63 = (bf16[96,1024]{1,0:T(8,128)(2,1)S(1)}, f32[192,1024]{1,0:T(8,128)S(1)}) custom-call(bf16[96,1024]{1,0:T(8,128)(2,1)S(1)} %collective-permute-done.11.arrived_ref, bf16[384,1024]{1,0:T(8,128)(2,1)S(1)} %shard_map.59.tokens_ref, bf16[1024,4096]{1,0:T(8,128)(2,1)S(1)} %bitcast.2), custom_call_target="tpu_custom_call" | custom-call | tf_op jit(solution)/shard_map/pallas_call | solution.py:198
  34.7 0.1 collective-permute-start.12
  34.7 3.4 %collective-permute-done.8.arrived_ref = bf16[96,1024]{1,0:T(8,128)(2,1)S(1)} collective-permute-done((bf16[96,1024]{1,0:T(8,128)(2,1)S(1)}, bf16[96,1024]{1,0:T(8,128)(2,1)S(1)}, u32[]{:S(2)}, u32[]{:S(2)}) %collective-permute-start.8) | collective-permute-done | bytes 196640 | tf_op jit(solution)/shard_map/ppermute | solution.py:211
  38.1 0.8 %shard_map.61 = (bf16[96,1024]{1,0:T(8,128)(2,1)S(1)}, f32[192,1024]{1,0:T(8,128)S(1)}) custom-call(bf16[96,1024]{1,0:T(8,128)(2,1)S(1)} %collective-permute-done.8.arrived_ref, bf16[384,1024]{1,0:T(8,128)(2,1)S(1)} %shard_map.59.tokens_ref, bf16[1024,4096]{1,0:T(8,128)(2,1)S(1)} %bitcast.2), custom_call_target="tpu_custom_call" | custom-call | tf_op jit(solution)/shard_map/pallas_call | solution.py:198
  38.9 0.1 collective-permute-start.9
  38.9 3.4 %collective-permute-done.18 = bf16[96,1024]{1,0:T(8,128)(2,1)S(1)} collective-permute-done((bf16[96,1024]{1,0:T(8,128)(2,1)S(1)}, bf16[96,1024]{1,0:T(8,128)(2,1)S(1)}, u32[]{:S(2)}, u32[]{:S(2)}) %collective-permute-start.18) | collective-permute-done | bytes 196640 | tf_op jit(solution)/shard_map/ppermute | solution.py:211
  42.4 0.1 collective-permute-start.19
  42.4 4.1 %collective-permute-done.15 = bf16[96,1024]{1,0:T(8,128)(2,1)S(1)} collective-permute-done((bf16[96,1024]{1,0:T(8,128)(2,1)S(1)}, bf16[96,1024]{1,0:T(8,128)(2,1)S(1)}, u32[]{:S(2)}, u32[]{:S(2)}) %collective-permute-start.15) | collective-permute-done | bytes 196640 | tf_op jit(solution)/shard_map/ppermute | solution.py:211
  46.6 0.1 collective-permute-start.16
  46.6 4.1 %collective-permute-done.12 = bf16[96,1024]{1,0:T(8,128)(2,1)S(1)} collective-permute-done((bf16[96,1024]{1,0:T(8,128)(2,1)S(1)}, bf16[96,1024]{1,0:T(8,128)(2,1)S(1)}, u32[]{:S(2)}, u32[]{:S(2)}) %collective-permute-start.12) | collective-permute-done | bytes 196640 | tf_op jit(solution)/shard_map/ppermute | solution.py:211
  50.8 0.1 collective-permute-start.13
  50.9 4.1 %collective-permute-done.9 = bf16[96,1024]{1,0:T(8,128)(2,1)S(1)} collective-permute-done((bf16[96,1024]{1,0:T(8,128)(2,1)S(1)}, bf16[96,1024]{1,0:T(8,128)(2,1)S(1)}, u32[]{:S(2)}, u32[]{:S(2)}) %collective-permute-start.9) | collective-permute-done | bytes 196640 | tf_op jit(solution)/shard_map/ppermute | solution.py:211
  55.1 4.1 %collective-permute-done.19.arrived_ref = bf16[96,1024]{1,0:T(8,128)(2,1)S(1)} collective-permute-done((bf16[96,1024]{1,0:T(8,128)(2,1)S(1)}, bf16[96,1024]{1,0:T(8,128)(2,1)S(1)}, u32[]{:S(2)}, u32[]{:S(2)}) %collective-permute-start.19) | collective-permute-done | bytes 196640 | tf_op jit(solution)/shard_map/ppermute | solution.py:211
  59.2 0.8 %shard_map.68.refs_0_ = bf16[96,4096]{1,0:T(8,128)(2,1)} custom-call(bf16[96,1024]{1,0:T(8,128)(2,1)S(1)} %collective-permute-done.19.arrived_ref, f32[192,1024]{1,0:T(8,128)S(1)} %get-tuple-element.38.kept_ref), custom_call_target="tpu_custom_call" | custom-call | tf_op jit(solution)/shard_map/pallas_call | solution.py:328
  59.9 3.4 %collective-permute-done.16.arrived_ref = bf16[96,1024]{1,0:T(8,128)(2,1)S(1)} collective-permute-done((bf16[96,1024]{1,0:T(8,128)(2,1)S(1)}, bf16[96,1024]{1,0:T(8,128)(2,1)S(1)}, u32[]{:S(2)}, u32[]{:S(2)}) %collective-permute-start.16) | collective-permute-done | bytes 196640 | tf_op jit(solution)/shard_map/ppermute | solution.py:211
  63.4 0.8 %shard_map.69.refs_0_ = bf16[96,4096]{1,0:T(8,128)(2,1)} custom-call(bf16[96,1024]{1,0:T(8,128)(2,1)S(1)} %collective-permute-done.16.arrived_ref, f32[192,1024]{1,0:T(8,128)S(1)} %get-tuple-element.36.kept_ref, bf16[96,4096]{1,0:T(8,128)(2,1)} %shard_map.68.refs_0_), custom_call_target="tpu_custom_call", output_to_operand_aliasing={{}: (2, {})} | custom-call | tf_op jit(solution)/shard_map/pallas_call | solution.py:328
  64.1 3.4 %collective-permute-done.13.arrived_ref = bf16[96,1024]{1,0:T(8,128)(2,1)S(1)} collective-permute-done((bf16[96,1024]{1,0:T(8,128)(2,1)S(1)}, bf16[96,1024]{1,0:T(8,128)(2,1)S(1)}, u32[]{:S(2)}, u32[]{:S(2)}) %collective-permute-start.13) | collective-permute-done | bytes 196640 | tf_op jit(solution)/shard_map/ppermute | solution.py:211
  67.6 0.8 %shard_map.70.refs_0_ = bf16[96,4096]{1,0:T(8,128)(2,1)} custom-call(bf16[96,1024]{1,0:T(8,128)(2,1)S(1)} %collective-permute-done.13.arrived_ref, f32[192,1024]{1,0:T(8,128)S(1)} %get-tuple-element.34.kept_ref, bf16[96,4096]{1,0:T(8,128)(2,1)} %shard_map.69.refs_0_), custom_call_target="tpu_custom_call", output_to_operand_aliasing={{}: (2, {})} | custom-call | tf_op jit(solution)/shard_map/pallas_call | solution.py:328
  68.4 3.0 %collective-permute-done.10.arrived_ref = bf16[96,1024]{1,0:T(8,128)(2,1)S(1)} collective-permute-done((bf16[96,1024]{1,0:T(8,128)(2,1)S(1)}, bf16[96,1024]{1,0:T(8,128)(2,1)S(1)}, u32[]{:S(2)}, u32[]{:S(2)}) %collective-permute-start.10) | collective-permute-done | bytes 196640 | tf_op jit(solution)/shard_map/ppermute | solution.py:211
  71.4 0.8 %shard_map.71 = bf16[96,4096]{1,0:T(8,128)(2,1)} custom-call(bf16[96,1024]{1,0:T(8,128)(2,1)S(1)} %collective-permute-done.10.arrived_ref, f32[192,1024]{1,0:T(8,128)S(1)} %get-tuple-element.32.kept_ref, bf16[96,4096]{1,0:T(8,128)(2,1)} %shard_map.70.refs_0_), custom_call_target="tpu_custom_call", output_to_operand_aliasing={{}: (2, {})} | custom-call | tf_op jit(solution)/shard_map/pallas_call | solution.py:328
  (28 shorter events, 0.3 us)
Async XLA Ops:
  0.0 15.4 %slice-start = ((s8[8388608]{0:T(1024)(128)(4,1)}), s8[4194304]{0:T(1024)(128)(4,1)S(1)}, s32[]{:S(2)}) async-start(s8[8388608]{0:T(1024)(128)(4,1)} %bitcast.1), calls=%async_computation | async-start | bytes 8388608
  0.0 1.2 %copy-start.3 = (f32[64,32,32]{0,2,1:T(8,128)S(1)}, f32[64,32,32]{0,2,1:T(8,128)}, u32[]{:S(2)}) copy-start(f32[64,32,32]{0,2,1:T(8,128)} %param.5) | copy-start | bytes 786436
  1.2 7.0 %copy-start = (f32[9,64,64]{2,1,0:T(8,128)S(1)}, f32[9,64,64]{2,1,0:T(8,128)}, u32[]{:S(2)}) copy-start(f32[9,64,64]{2,1,0:T(8,128)} %first_ref.1) | copy-start | bytes 442372
  1.2 7.0 %copy-start.1 = (f32[9,64,64]{2,1,0:T(8,128)S(1)}, f32[9,64,64]{2,1,0:T(8,128)}, u32[]{:S(2)}) copy-start(f32[9,64,64]{2,1,0:T(8,128)} %second_ref.1) | copy-start | bytes 442372
  1.2 7.0 %copy-start.2 = (bf16[256,384]{1,0:T(8,128)(2,1)S(1)}, bf16[256,384]{1,0:T(8,128)(2,1)}, u32[]{:S(2)}) copy-start(bf16[256,384]{1,0:T(8,128)(2,1)} %embed_ref.1) | copy-start | bytes 589828
  1.2 14.2 %slice-start.1 = ((s8[8388608]{0:T(1024)(128)(4,1)}), s8[4194304]{0:T(1024)(128)(4,1)S(1)}, s32[]{:S(2)}) async-start(s8[8388608]{0:T(1024)(128)(4,1)} %bitcast.1), calls=%async_computation.1 | async-start | bytes 8388608
  1.3 7.4 %collective-permute-start.1 = (bf16[16,32,128]{2,1,0:T(8,128)(2,1)S(1)}, bf16[16,32,128]{2,1,0:T(8,128)(2,1)S(1)}, u32[]{:S(2)}, u32[]{:S(2)}) collective-permute-start(bf16[16,32,128]{2,1,0:T(8,128)(2,1)S(1)} %get-tuple-element.22.refs_0_), channel_id=1, source_target_pairs={{0,2},{2,0},{1,3},{3,1},{4,6},{6,4},{5,7},{7,5},{8,10},{10,8},{9,1... | collective-permute-start | bytes 393224 | tf_op jit(solution)/shard_map/ppermute | solution.py:211
  4.3 5.4 %collective-permute-start.3 = (bf16[1,32,128]{2,1,0:T(8,128)(2,1)S(1)}, bf16[1,32,128]{2,1,0:T(8,128)(2,1)S(1)}, u32[]{:S(2)}, u32[]{:S(2)}) collective-permute-start(bf16[1,32,128]{2,1,0:T(8,128)(2,1)S(1)} %get-tuple-element.23), channel_id=1, source_target_pairs={{0,4},{4,8},{8,12},{12,0},{1,5},{5,9},{9,13},{13,1},{2,6},{6,10},{... | collective-permute-start | bytes 24584 | tf_op jit(solution)/shard_map/ppermute | solution.py:211
  5.9 5.8 %collective-permute-start = (bf16[16,32,128]{2,1,0:T(8,128)(2,1)S(1)}, bf16[16,32,128]{2,1,0:T(8,128)(2,1)S(1)}, u32[]{:S(2)}, u32[]{:S(2)}) collective-permute-start(bf16[16,32,128]{2,1,0:T(8,128)(2,1)S(1)} %get-tuple-element.22.refs_0_), channel_id=1, source_target_pairs={{0,1},{1,0},{2,3},{3,2},{4,5},{5,4},{6,7},{7,6},{8,9},{9,8},{10,11... | collective-permute-start | bytes 393224 | tf_op jit(solution)/shard_map/ppermute | solution.py:211
  5.9 3.9 %collective-permute-start.4 = (bf16[1,32,128]{2,1,0:T(8,128)(2,1)S(1)}, bf16[1,32,128]{2,1,0:T(8,128)(2,1)S(1)}, u32[]{:S(2)}, u32[]{:S(2)}) collective-permute-start(bf16[1,32,128]{2,1,0:T(8,128)(2,1)S(1)} %get-tuple-element.24), channel_id=1, source_target_pairs={{0,12},{4,0},{8,4},{12,8},{1,13},{5,1},{9,5},{13,9},{2,14},{6,2},{... | collective-permute-start | bytes 24584 | tf_op jit(solution)/shard_map/ppermute | solution.py:211
  8.8 3.0 %collective-permute-start.2 = (bf16[16,32,128]{2,1,0:T(8,128)(2,1)S(1)}, bf16[16,32,128]{2,1,0:T(8,128)(2,1)S(1)}, u32[]{:S(2)}, u32[]{:S(2)}) collective-permute-start(bf16[16,32,128]{2,1,0:T(8,128)(2,1)S(1)} %collective-permute-done.1.refs_2_), channel_id=1, source_target_pairs={{0,1},{1,0},{2,3},{3,2},{4,5},{5,4},{6,7},{7,6},{8,9},{9,8},{10,11... | collective-permute-start | bytes 393224 | tf_op jit(solution)/shard_map/ppermute | solution.py:211
  9.8 4.4 %collective-permute-start.5 = (bf16[2,32,128]{2,1,0:T(8,128)(2,1)S(1)}, bf16[2,32,128]{2,1,0:T(8,128)(2,1)S(1)}, u32[]{:S(2)}, u32[]{:S(2)}) collective-permute-start(bf16[2,32,128]{2,1,0:T(8,128)(2,1)S(1)} %constant_dynamic-update-slice_fusion.refs_0_), channel_id=1, source_target_pairs={{0,1},{1,0},{2,3},{3,2},{4,5},{5,4},{6,7},{7,6},{8,9},{9,8},{10,11... | collective-permute-start | bytes 49160 | tf_op jit(solution)/shard_map/ppermute | solution.py:230
  9.9 4.3 %collective-permute-start.6 = (bf16[2,32,128]{2,1,0:T(8,128)(2,1)S(1)}, bf16[2,32,128]{2,1,0:T(8,128)(2,1)S(1)}, u32[]{:S(2)}, u32[]{:S(2)}) collective-permute-start(bf16[2,32,128]{2,1,0:T(8,128)(2,1)S(1)} %constant_dynamic-update-slice_fusion.refs_0_), channel_id=1, source_target_pairs={{0,2},{1,3},{2,0},{3,1},{4,6},{5,7},{6,4},{7,5},{8,10},{9,11},{10,... | collective-permute-start | bytes 49160 | tf_op jit(solution)/shard_map/ppermute | solution.py:230
  10.2 4.0 %collective-permute-start.7 = (bf16[2,32,128]{2,1,0:T(8,128)(2,1)S(1)}, bf16[2,32,128]{2,1,0:T(8,128)(2,1)S(1)}, u32[]{:S(2)}, u32[]{:S(2)}) collective-permute-start(bf16[2,32,128]{2,1,0:T(8,128)(2,1)S(1)} %constant_dynamic-update-slice_fusion.refs_0_), channel_id=1, source_target_pairs={{0,3},{1,2},{2,1},{3,0},{4,7},{5,6},{6,5},{7,4},{8,11},{9,10},{10,... | collective-permute-start | bytes 49160 | tf_op jit(solution)/shard_map/ppermute | solution.py:230
  15.9 9.5 %collective-permute-start.17 = (bf16[96,1024]{1,0:T(8,128)(2,1)S(1)}, bf16[96,1024]{1,0:T(8,128)(2,1)S(1)}, u32[]{:S(2)}, u32[]{:S(2)}) collective-permute-start(bf16[96,1024]{1,0:T(8,128)(2,1)S(1)} %shard_map.66), channel_id=1, source_target_pairs={{0,4},{4,8},{8,12},{12,0},{1,5},{5,9},{9,13},{13,1},{2,6},{6,10},{... | collective-permute-start | bytes 589832 | tf_op jit(solution)/shard_map/ppermute | solution.py:211
  17.7 12.0 %collective-permute-start.14 = (bf16[96,1024]{1,0:T(8,128)(2,1)S(1)}, bf16[96,1024]{1,0:T(8,128)(2,1)S(1)}, u32[]{:S(2)}, u32[]{:S(2)}) collective-permute-start(bf16[96,1024]{1,0:T(8,128)(2,1)S(1)} %shard_map.64), channel_id=1, source_target_pairs={{0,4},{4,8},{8,12},{12,0},{1,5},{5,9},{9,13},{13,1},{2,6},{6,10},{... | collective-permute-start | bytes 589832 | tf_op jit(solution)/shard_map/ppermute | solution.py:211
  19.8 14.1 %collective-permute-start.11 = (bf16[96,1024]{1,0:T(8,128)(2,1)S(1)}, bf16[96,1024]{1,0:T(8,128)(2,1)S(1)}, u32[]{:S(2)}, u32[]{:S(2)}) collective-permute-start(bf16[96,1024]{1,0:T(8,128)(2,1)S(1)} %shard_map.62), channel_id=1, source_target_pairs={{0,4},{4,8},{8,12},{12,0},{1,5},{5,9},{9,13},{13,1},{2,6},{6,10},{... | collective-permute-start | bytes 589832 | tf_op jit(solution)/shard_map/ppermute | solution.py:211
  22.3 15.8 %collective-permute-start.8 = (bf16[96,1024]{1,0:T(8,128)(2,1)S(1)}, bf16[96,1024]{1,0:T(8,128)(2,1)S(1)}, u32[]{:S(2)}, u32[]{:S(2)}) collective-permute-start(bf16[96,1024]{1,0:T(8,128)(2,1)S(1)} %shard_map.60), channel_id=1, source_target_pairs={{0,4},{4,8},{8,12},{12,0},{1,5},{5,9},{9,13},{13,1},{2,6},{6,10},{... | collective-permute-start | bytes 589832 | tf_op jit(solution)/shard_map/ppermute | solution.py:211
  26.2 16.1 %collective-permute-start.18 = (bf16[96,1024]{1,0:T(8,128)(2,1)S(1)}, bf16[96,1024]{1,0:T(8,128)(2,1)S(1)}, u32[]{:S(2)}, u32[]{:S(2)}) collective-permute-start(bf16[96,1024]{1,0:T(8,128)(2,1)S(1)} %get-tuple-element.37), channel_id=1, source_target_pairs={{0,4},{4,8},{8,12},{12,0},{1,5},{5,9},{9,13},{13,1},{2,6},{6,10},{... | collective-permute-start | bytes 589832 | tf_op jit(solution)/shard_map/ppermute | solution.py:211
  30.5 16.1 %collective-permute-start.15 = (bf16[96,1024]{1,0:T(8,128)(2,1)S(1)}, bf16[96,1024]{1,0:T(8,128)(2,1)S(1)}, u32[]{:S(2)}, u32[]{:S(2)}) collective-permute-start(bf16[96,1024]{1,0:T(8,128)(2,1)S(1)} %get-tuple-element.35), channel_id=1, source_target_pairs={{0,4},{4,8},{8,12},{12,0},{1,5},{5,9},{9,13},{13,1},{2,6},{6,10},{... | collective-permute-start | bytes 589832 | tf_op jit(solution)/shard_map/ppermute | solution.py:211
  34.7 16.1 %collective-permute-start.12 = (bf16[96,1024]{1,0:T(8,128)(2,1)S(1)}, bf16[96,1024]{1,0:T(8,128)(2,1)S(1)}, u32[]{:S(2)}, u32[]{:S(2)}) collective-permute-start(bf16[96,1024]{1,0:T(8,128)(2,1)S(1)} %get-tuple-element.33), channel_id=1, source_target_pairs={{0,4},{4,8},{8,12},{12,0},{1,5},{5,9},{9,13},{13,1},{2,6},{6,10},{... | collective-permute-start | bytes 589832 | tf_op jit(solution)/shard_map/ppermute | solution.py:211
  38.9 16.1 %collective-permute-start.9 = (bf16[96,1024]{1,0:T(8,128)(2,1)S(1)}, bf16[96,1024]{1,0:T(8,128)(2,1)S(1)}, u32[]{:S(2)}, u32[]{:S(2)}) collective-permute-start(bf16[96,1024]{1,0:T(8,128)(2,1)S(1)} %get-tuple-element.31), channel_id=1, source_target_pairs={{0,4},{4,8},{8,12},{12,0},{1,5},{5,9},{9,13},{13,1},{2,6},{6,10},{... | collective-permute-start | bytes 589832 | tf_op jit(solution)/shard_map/ppermute | solution.py:211
  42.4 16.8 %collective-permute-start.19 = (bf16[96,1024]{1,0:T(8,128)(2,1)S(1)}, bf16[96,1024]{1,0:T(8,128)(2,1)S(1)}, u32[]{:S(2)}, u32[]{:S(2)}) collective-permute-start(bf16[96,1024]{1,0:T(8,128)(2,1)S(1)} %add_convert_fusion), channel_id=1, source_target_pairs={{0,4},{4,8},{8,12},{12,0},{1,5},{5,9},{9,13},{13,1},{2,6},{6,10},{... | collective-permute-start | bytes 589832 | tf_op jit(solution)/shard_map/ppermute | solution.py:211
  46.6 16.8 %collective-permute-start.16 = (bf16[96,1024]{1,0:T(8,128)(2,1)S(1)}, bf16[96,1024]{1,0:T(8,128)(2,1)S(1)}, u32[]{:S(2)}, u32[]{:S(2)}) collective-permute-start(bf16[96,1024]{1,0:T(8,128)(2,1)S(1)} %add_convert_fusion.1), channel_id=1, source_target_pairs={{0,4},{4,8},{8,12},{12,0},{1,5},{5,9},{9,13},{13,1},{2,6},{6,10},{... | collective-permute-start | bytes 589832 | tf_op jit(solution)/shard_map/ppermute | solution.py:211
  50.8 16.8 %collective-permute-start.13 = (bf16[96,1024]{1,0:T(8,128)(2,1)S(1)}, bf16[96,1024]{1,0:T(8,128)(2,1)S(1)}, u32[]{:S(2)}, u32[]{:S(2)}) collective-permute-start(bf16[96,1024]{1,0:T(8,128)(2,1)S(1)} %add_convert_fusion.2), channel_id=1, source_target_pairs={{0,4},{4,8},{8,12},{12,0},{1,5},{5,9},{9,13},{13,1},{2,6},{6,10},{... | collective-permute-start | bytes 589832 | tf_op jit(solution)/shard_map/ppermute | solution.py:211
  55.0 16.4 %collective-permute-start.10 = (bf16[96,1024]{1,0:T(8,128)(2,1)S(1)}, bf16[96,1024]{1,0:T(8,128)(2,1)S(1)}, u32[]{:S(2)}, u32[]{:S(2)}) collective-permute-start(bf16[96,1024]{1,0:T(8,128)(2,1)S(1)} %add_convert_fusion.3), channel_id=1, source_target_pairs={{0,4},{4,8},{8,12},{12,0},{1,5},{5,9},{9,13},{13,1},{2,6},{6,10},{... | collective-permute-start | bytes 589832 | tf_op jit(solution)/shard_map/ppermute | solution.py:211

commit v18 on v17

--- a/solution.py
+++ b/solution.py
@@ -346,7 +346,7 @@
     rows = embed // count
     width = token_mixing.shape[1] // pieces
     sent = jax.ShapeDtypeStruct((rows, width), jnp.bfloat16)
-    ways = [1] * pieces
+    ways = [-1] * pieces
     blocks = [list(range(count - 2, -1, -1)) if way == 1 else list(range(count - 1)) for way in ways]
     travelling = [
         call(functools.partial(sent_kernel, piece * width, blocks[piece][0]), sent, (tokens, token_mixing))

time: 72.3 us -> 71.6 us (level)
  waiting for transfers between devices: 43.5 us -> 12.8 us
  starting transfers between devices: 14.7 us -> 44.8 us
    ppermute x17, waiting for transfers between devices: 43.5 us -> 12.7 us  [turned(): lax.ppermute(value, axis, [(i, (i + away) % count) for i in range(count)])]
    ppermute x17, starting transfers between devices: 12.8 us -> 42.8 us  [turned(): lax.ppermute(value, axis, [(i, (i + away) % count) for i in range(count)])]
  transfers between devices with their start and end apart: 20 -> 20, of which waited for: 13 -> 5; matrix products, arithmetic and copies ran while one was open for 0% -> 0% of each run, Pallas kernels for 14% -> 14%
where the time goes in v18:
time: 71.6 us; the launch traced here: 71.4 us
  starting transfers between devices  44.8 us (63%)
  waiting for transfers between devices  12.8 us (18%)
  Pallas kernels  12.3 us (17%)
  local copies, waits for them, and re-layouts  1.22 us (2%)
    ppermute x17, starting transfers between devices, turned(): lax.ppermute(value, axis, [(i, (i + away) % count) for i in range(count)])  42.8 us
    ppermute x17, waiting for transfers between devices, turned(): lax.ppermute(value, axis, [(i, (i + away) % count) for i in range(count)])  12.7 us
    pallas_call x13, Pallas kernels, call(): pl.pallas_call(kernel, out_shape=out_shape, in_specs=[pl.BlockSpec(memory...  9.28 us
    pallas_call x4, Pallas kernels, finish(): pl.pallas_call(functools.partial(last_kernel, first), out_shape=jax.Shape...  3.03 us
    ppermute x3, starting transfers between devices, direct_blocks(): blocks.append(lax.ppermute(block, ('ch', 'sub'), route))  1.93 us
  transfers between devices with their start and end apart: 20, of which 5 were waited for; matrix products, arithmetic and copies ran while one was open for 0% of the time, Pallas kernels for 14%

profile of v18, /device:TPU:0, one launch (start us, length us, event | category | flops | bytes accessed | tf_op | source)
XLA Modules:
  0.0 71.4 jit_solution(6077524539435034515)
XLA Ops:
  0.0 1.2 %copy-done.3 = f32[64,32,32]{0,2,1:T(8,128)S(1)} copy-done((f32[64,32,32]{0,2,1:T(8,128)S(1)}, f32[64,32,32]{0,2,1:T(8,128)}, u32[]{:S(2)}) %copy-start.3) | copy-done | bytes 262168
  1.2 0.1 shard_map.55
  1.3 3.0 %collective-permute-start.1 = (bf16[16,32,128]{2,1,0:T(8,128)(2,1)S(1)}, bf16[16,32,128]{2,1,0:T(8,128)(2,1)S(1)}, u32[]{:S(2)}, u32[]{:S(2)}) collective-permute-start(bf16[16,32,128]{2,1,0:T(8,128)(2,1)S(1)} %get-tuple-element.22.refs_0_), channel_id=1, source_target_pairs={{0,2},{2,0},{1,3},{3,1},{4,6},{6,4},{5,7},{7,5},{8,10},{10,8},{9,1... | collective-permute-start | bytes 393224 | tf_op jit(solution)/shard_map/ppermute | solution.py:211
  4.3 1.6 %collective-permute-start.3 = (bf16[1,32,128]{2,1,0:T(8,128)(2,1)S(1)}, bf16[1,32,128]{2,1,0:T(8,128)(2,1)S(1)}, u32[]{:S(2)}, u32[]{:S(2)}) collective-permute-start(bf16[1,32,128]{2,1,0:T(8,128)(2,1)S(1)} %get-tuple-element.23), channel_id=1, source_target_pairs={{0,4},{4,8},{8,12},{12,0},{1,5},{5,9},{9,13},{13,1},{2,6},{6,10},{... | collective-permute-start | bytes 24584 | tf_op jit(solution)/shard_map/ppermute | solution.py:211
  5.9 2.2 %collective-permute-start.4 = (bf16[1,32,128]{2,1,0:T(8,128)(2,1)S(1)}, bf16[1,32,128]{2,1,0:T(8,128)(2,1)S(1)}, u32[]{:S(2)}, u32[]{:S(2)}) collective-permute-start(bf16[1,32,128]{2,1,0:T(8,128)(2,1)S(1)} %get-tuple-element.24), channel_id=1, source_target_pairs={{0,12},{4,0},{8,4},{12,8},{1,13},{5,1},{9,5},{13,9},{2,14},{6,2},{... | collective-permute-start | bytes 24584 | tf_op jit(solution)/shard_map/ppermute | solution.py:211
  8.2 0.6 shard_map.57
  8.8 0.3 collective-permute-start.2
  9.1 0.7 collective-permute-done.3
  9.8 0.0 collective-permute-done.4
  9.8 0.1 collective-permute-start.5
  9.9 0.4 collective-permute-start.6
  10.2 1.5 %collective-permute-start.7 = (bf16[2,32,128]{2,1,0:T(8,128)(2,1)S(1)}, bf16[2,32,128]{2,1,0:T(8,128)(2,1)S(1)}, u32[]{:S(2)}, u32[]{:S(2)}) collective-permute-start(bf16[2,32,128]{2,1,0:T(8,128)(2,1)S(1)} %constant_dynamic-update-slice_fusion.refs_0_), channel_id=1, source_target_pairs={{0,3},{1,2},{2,1},{3,0},{4,7},{5,6},{6,5},{7,4},{8,11},{9,10},{10,... | collective-permute-start | bytes 49160 | tf_op jit(solution)/shard_map/ppermute | solution.py:230
  11.8 2.4 %shard_map.58 = (bf16[384,768]{1,0:T(8,128)(2,1)S(1)}, bf16[4,128,128]{2,1,0:T(8,128)(2,1)S(1)}, bf16[4,128,128]{2,1,0:T(8,128)(2,1)S(1)}) custom-call(bf16[16,128,128]{2,1,0:T(8,128)(2,1)S(1)} %shard_map.56.field_ref, bf16[256,768]{1,0:T(8,128)(2,1)S(1)} %get-tuple-element.25.taps_one_ref.refs_6_, ...), custom_call_target="tpu_custom_call" | custom-call | flops 1635778560 | bytes 524288 | tf_op jit(solution)/shard_map/pallas_call | solution.py:198
  14.2 0.0 collective-permute-done.5.refs_1_
  14.2 0.0 collective-permute-done.7.refs_3_
  14.2 1.2 %shard_map.59.tokens_ref = bf16[384,1024]{1,0:T(8,128)(2,1)S(1)} custom-call(bf16[16,128,128]{2,1,0:T(8,128)(2,1)S(1)} %shard_map.56.field_ref, bf16[2,32,128]{2,1,0:T(8,128)(2,1)S(1)} %constant_dynamic-update-slice_fusion.refs_0_, bf16[2,32,128]{2,1,0:T(8,128)(2,1)S(1)} %collective-permute-done.5.refs_1_, ...), custom_call_target="tpu_custom_call" | custom-call | flops 503316480 | bytes 524288 | tf_op jit(solution)/shard_map/pallas_call | solution.py:198
  15.4 0.5 shard_map.66
  15.9 3.8 %collective-permute-start.17 = (bf16[96,1024]{1,0:T(8,128)(2,1)S(1)}, bf16[96,1024]{1,0:T(8,128)(2,1)S(1)}, u32[]{:S(2)}, u32[]{:S(2)}) collective-permute-start(bf16[96,1024]{1,0:T(8,128)(2,1)S(1)} %shard_map.66), channel_id=1, source_target_pairs={{0,12},{4,0},{8,4},{12,8},{1,13},{5,1},{9,5},{13,9},{2,14},{6,2},{... | collective-permute-start | bytes 589832 | tf_op jit(solution)/shard_map/ppermute | solution.py:211
  19.7 0.5 shard_map.64
  20.2 0.1 collective-permute-start.14
  20.2 0.5 shard_map.62
  20.7 0.5 collective-permute-start.11
  21.2 0.5 shard_map.60
  21.7 0.8 %collective-permute-start.8 = (bf16[96,1024]{1,0:T(8,128)(2,1)S(1)}, bf16[96,1024]{1,0:T(8,128)(2,1)S(1)}, u32[]{:S(2)}, u32[]{:S(2)}) collective-permute-start(bf16[96,1024]{1,0:T(8,128)(2,1)S(1)} %shard_map.60), channel_id=1, source_target_pairs={{0,12},{4,0},{8,4},{12,8},{1,13},{5,1},{9,5},{13,9},{2,14},{6,2},{... | collective-permute-start | bytes 589832 | tf_op jit(solution)/shard_map/ppermute | solution.py:211
  22.5 2.5 %collective-permute-done.17.arrived_ref = bf16[96,1024]{1,0:T(8,128)(2,1)S(1)} collective-permute-done((bf16[96,1024]{1,0:T(8,128)(2,1)S(1)}, bf16[96,1024]{1,0:T(8,128)(2,1)S(1)}, u32[]{:S(2)}, u32[]{:S(2)}) %collective-permute-start.17) | collective-permute-done | bytes 196640 | tf_op jit(solution)/shard_map/ppermute | solution.py:211
  24.9 0.8 %shard_map.67 = (bf16[96,1024]{1,0:T(8,128)(2,1)S(1)}, f32[192,1024]{1,0:T(8,128)S(1)}) custom-call(bf16[96,1024]{1,0:T(8,128)(2,1)S(1)} %collective-permute-done.17.arrived_ref, bf16[384,1024]{1,0:T(8,128)(2,1)S(1)} %shard_map.59.tokens_ref, bf16[1024,4096]{1,0:T(8,128)(2,1)S(1)} %bitcast.2), custom_call_target="tpu_custom_call" | custom-call | tf_op jit(solution)/shard_map/pallas_call | solution.py:198
  25.7 4.3 %collective-permute-start.18 = (bf16[96,1024]{1,0:T(8,128)(2,1)S(1)}, bf16[96,1024]{1,0:T(8,128)(2,1)S(1)}, u32[]{:S(2)}, u32[]{:S(2)}) collective-permute-start(bf16[96,1024]{1,0:T(8,128)(2,1)S(1)} %get-tuple-element.37), channel_id=1, source_target_pairs={{0,12},{4,0},{8,4},{12,8},{1,13},{5,1},{9,5},{13,9},{2,14},{6,2},{... | collective-permute-start | bytes 589832 | tf_op jit(solution)/shard_map/ppermute | solution.py:211
  30.1 0.0 collective-permute-done.14.arrived_ref
  30.1 0.8 %shard_map.65 = (bf16[96,1024]{1,0:T(8,128)(2,1)S(1)}, f32[192,1024]{1,0:T(8,128)S(1)}) custom-call(bf16[96,1024]{1,0:T(8,128)(2,1)S(1)} %collective-permute-done.14.arrived_ref, bf16[384,1024]{1,0:T(8,128)(2,1)S(1)} %shard_map.59.tokens_ref, bf16[1024,4096]{1,0:T(8,128)(2,1)S(1)} %bitcast.2), custom_call_target="tpu_custom_call" | custom-call | tf_op jit(solution)/shard_map/pallas_call | solution.py:198
  30.8 3.4 %collective-permute-start.15 = (bf16[96,1024]{1,0:T(8,128)(2,1)S(1)}, bf16[96,1024]{1,0:T(8,128)(2,1)S(1)}, u32[]{:S(2)}, u32[]{:S(2)}) collective-permute-start(bf16[96,1024]{1,0:T(8,128)(2,1)S(1)} %get-tuple-element.35), channel_id=1, source_target_pairs={{0,12},{4,0},{8,4},{12,8},{1,13},{5,1},{9,5},{13,9},{2,14},{6,2},{... | collective-permute-start | bytes 589832 | tf_op jit(solution)/shard_map/ppermute | solution.py:211
  34.3 0.0 collective-permute-done.11.arrived_ref
  34.3 0.8 %shard_map.63 = (bf16[96,1024]{1,0:T(8,128)(2,1)S(1)}, f32[192,1024]{1,0:T(8,128)S(1)}) custom-call(bf16[96,1024]{1,0:T(8,128)(2,1)S(1)} %collective-permute-done.11.arrived_ref, bf16[384,1024]{1,0:T(8,128)(2,1)S(1)} %shard_map.59.tokens_ref, bf16[1024,4096]{1,0:T(8,128)(2,1)S(1)} %bitcast.2), custom_call_target="tpu_custom_call" | custom-call | tf_op jit(solution)/shard_map/pallas_call | solution.py:198
  35.0 3.4 %collective-permute-start.12 = (bf16[96,1024]{1,0:T(8,128)(2,1)S(1)}, bf16[96,1024]{1,0:T(8,128)(2,1)S(1)}, u32[]{:S(2)}, u32[]{:S(2)}) collective-permute-start(bf16[96,1024]{1,0:T(8,128)(2,1)S(1)} %get-tuple-element.33), channel_id=1, source_target_pairs={{0,12},{4,0},{8,4},{12,8},{1,13},{5,1},{9,5},{13,9},{2,14},{6,2},{... | collective-permute-start | bytes 589832 | tf_op jit(solution)/shard_map/ppermute | solution.py:211
  38.5 0.0 collective-permute-done.8.arrived_ref
  38.5 0.8 %shard_map.61 = (bf16[96,1024]{1,0:T(8,128)(2,1)S(1)}, f32[192,1024]{1,0:T(8,128)S(1)}) custom-call(bf16[96,1024]{1,0:T(8,128)(2,1)S(1)} %collective-permute-done.8.arrived_ref, bf16[384,1024]{1,0:T(8,128)(2,1)S(1)} %shard_map.59.tokens_ref, bf16[1024,4096]{1,0:T(8,128)(2,1)S(1)} %bitcast.2), custom_call_target="tpu_custom_call" | custom-call | tf_op jit(solution)/shard_map/pallas_call | solution.py:198
  39.3 3.4 %collective-permute-start.9 = (bf16[96,1024]{1,0:T(8,128)(2,1)S(1)}, bf16[96,1024]{1,0:T(8,128)(2,1)S(1)}, u32[]{:S(2)}, u32[]{:S(2)}) collective-permute-start(bf16[96,1024]{1,0:T(8,128)(2,1)S(1)} %get-tuple-element.31), channel_id=1, source_target_pairs={{0,12},{4,0},{8,4},{12,8},{1,13},{5,1},{9,5},{13,9},{2,14},{6,2},{... | collective-permute-start | bytes 589832 | tf_op jit(solution)/shard_map/ppermute | solution.py:211
  42.7 0.0 collective-permute-done.18
  42.7 3.4 %collective-permute-start.19 = (bf16[96,1024]{1,0:T(8,128)(2,1)S(1)}, bf16[96,1024]{1,0:T(8,128)(2,1)S(1)}, u32[]{:S(2)}, u32[]{:S(2)}) collective-permute-start(bf16[96,1024]{1,0:T(8,128)(2,1)S(1)} %add_convert_fusion), channel_id=1, source_target_pairs={{0,12},{4,0},{8,4},{12,8},{1,13},{5,1},{9,5},{13,9},{2,14},{6,2},{... | collective-permute-start | bytes 589832 | tf_op jit(solution)/shard_map/ppermute | solution.py:211
  46.2 4.2 %collective-permute-start.16 = (bf16[96,1024]{1,0:T(8,128)(2,1)S(1)}, bf16[96,1024]{1,0:T(8,128)(2,1)S(1)}, u32[]{:S(2)}, u32[]{:S(2)}) collective-permute-start(bf16[96,1024]{1,0:T(8,128)(2,1)S(1)} %add_convert_fusion.1), channel_id=1, source_target_pairs={{0,12},{4,0},{8,4},{12,8},{1,13},{5,1},{9,5},{13,9},{2,14},{6,2},{... | collective-permute-start | bytes 589832 | tf_op jit(solution)/shard_map/ppermute | solution.py:211
  50.4 4.2 %collective-permute-start.13 = (bf16[96,1024]{1,0:T(8,128)(2,1)S(1)}, bf16[96,1024]{1,0:T(8,128)(2,1)S(1)}, u32[]{:S(2)}, u32[]{:S(2)}) collective-permute-start(bf16[96,1024]{1,0:T(8,128)(2,1)S(1)} %add_convert_fusion.2), channel_id=1, source_target_pairs={{0,12},{4,0},{8,4},{12,8},{1,13},{5,1},{9,5},{13,9},{2,14},{6,2},{... | collective-permute-start | bytes 589832 | tf_op jit(solution)/shard_map/ppermute | solution.py:211
  54.6 4.2 %collective-permute-start.10 = (bf16[96,1024]{1,0:T(8,128)(2,1)S(1)}, bf16[96,1024]{1,0:T(8,128)(2,1)S(1)}, u32[]{:S(2)}, u32[]{:S(2)}) collective-permute-start(bf16[96,1024]{1,0:T(8,128)(2,1)S(1)} %add_convert_fusion.3), channel_id=1, source_target_pairs={{0,12},{4,0},{8,4},{12,8},{1,13},{5,1},{9,5},{13,9},{2,14},{6,2},{... | collective-permute-start | bytes 589832 | tf_op jit(solution)/shard_map/ppermute | solution.py:211
  58.8 0.8 %shard_map.68.refs_0_ = bf16[96,4096]{1,0:T(8,128)(2,1)} custom-call(bf16[96,1024]{1,0:T(8,128)(2,1)S(1)} %collective-permute-done.19.arrived_ref, f32[192,1024]{1,0:T(8,128)S(1)} %get-tuple-element.38.kept_ref), custom_call_target="tpu_custom_call" | custom-call | tf_op jit(solution)/shard_map/pallas_call | solution.py:328
  59.6 3.3 %collective-permute-done.16.arrived_ref = bf16[96,1024]{1,0:T(8,128)(2,1)S(1)} collective-permute-done((bf16[96,1024]{1,0:T(8,128)(2,1)S(1)}, bf16[96,1024]{1,0:T(8,128)(2,1)S(1)}, u32[]{:S(2)}, u32[]{:S(2)}) %collective-permute-start.16) | collective-permute-done | bytes 196640 | tf_op jit(solution)/shard_map/ppermute | solution.py:211
  62.9 0.8 %shard_map.69.refs_0_ = bf16[96,4096]{1,0:T(8,128)(2,1)} custom-call(bf16[96,1024]{1,0:T(8,128)(2,1)S(1)} %collective-permute-done.16.arrived_ref, f32[192,1024]{1,0:T(8,128)S(1)} %get-tuple-element.36.kept_ref, bf16[96,4096]{1,0:T(8,128)(2,1)} %shard_map.68.refs_0_), custom_call_target="tpu_custom_call", output_to_operand_aliasing={{}: (2, {})} | custom-call | tf_op jit(solution)/shard_map/pallas_call | solution.py:328
  63.6 3.4 %collective-permute-done.13.arrived_ref = bf16[96,1024]{1,0:T(8,128)(2,1)S(1)} collective-permute-done((bf16[96,1024]{1,0:T(8,128)(2,1)S(1)}, bf16[96,1024]{1,0:T(8,128)(2,1)S(1)}, u32[]{:S(2)}, u32[]{:S(2)}) %collective-permute-start.13) | collective-permute-done | bytes 196640 | tf_op jit(solution)/shard_map/ppermute | solution.py:211
  67.1 0.8 %shard_map.70.refs_0_ = bf16[96,4096]{1,0:T(8,128)(2,1)} custom-call(bf16[96,1024]{1,0:T(8,128)(2,1)S(1)} %collective-permute-done.13.arrived_ref, f32[192,1024]{1,0:T(8,128)S(1)} %get-tuple-element.34.kept_ref, bf16[96,4096]{1,0:T(8,128)(2,1)} %shard_map.69.refs_0_), custom_call_target="tpu_custom_call", output_to_operand_aliasing={{}: (2, {})} | custom-call | tf_op jit(solution)/shard_map/pallas_call | solution.py:328
  67.8 2.8 %collective-permute-done.10.arrived_ref = bf16[96,1024]{1,0:T(8,128)(2,1)S(1)} collective-permute-done((bf16[96,1024]{1,0:T(8,128)(2,1)S(1)}, bf16[96,1024]{1,0:T(8,128)(2,1)S(1)}, u32[]{:S(2)}, u32[]{:S(2)}) %collective-permute-start.10) | collective-permute-done | bytes 196640 | tf_op jit(solution)/shard_map/ppermute | solution.py:211
  70.7 0.8 %shard_map.71 = bf16[96,4096]{1,0:T(8,128)(2,1)} custom-call(bf16[96,1024]{1,0:T(8,128)(2,1)S(1)} %collective-permute-done.10.arrived_ref, f32[192,1024]{1,0:T(8,128)S(1)} %get-tuple-element.32.kept_ref, bf16[96,4096]{1,0:T(8,128)(2,1)} %shard_map.70.refs_0_), custom_call_target="tpu_custom_call", output_to_operand_aliasing={{}: (2, {})} | custom-call | tf_op jit(solution)/shard_map/pallas_call | solution.py:328
  (28 shorter events, 0.3 us)
Async XLA Ops:
  0.0 15.4 %slice-start = ((s8[8388608]{0:T(1024)(128)(4,1)}), s8[4194304]{0:T(1024)(128)(4,1)S(1)}, s32[]{:S(2)}) async-start(s8[8388608]{0:T(1024)(128)(4,1)} %bitcast.1), calls=%async_computation | async-start | bytes 8388608
  0.0 1.2 %copy-start.3 = (f32[64,32,32]{0,2,1:T(8,128)S(1)}, f32[64,32,32]{0,2,1:T(8,128)}, u32[]{:S(2)}) copy-start(f32[64,32,32]{0,2,1:T(8,128)} %param.5) | copy-start | bytes 786436
  1.2 7.0 %copy-start = (f32[9,64,64]{2,1,0:T(8,128)S(1)}, f32[9,64,64]{2,1,0:T(8,128)}, u32[]{:S(2)}) copy-start(f32[9,64,64]{2,1,0:T(8,128)} %first_ref.1) | copy-start | bytes 442372
  1.2 7.0 %copy-start.1 = (f32[9,64,64]{2,1,0:T(8,128)S(1)}, f32[9,64,64]{2,1,0:T(8,128)}, u32[]{:S(2)}) copy-start(f32[9,64,64]{2,1,0:T(8,128)} %second_ref.1) | copy-start | bytes 442372
  1.2 7.0 %copy-start.2 = (bf16[256,384]{1,0:T(8,128)(2,1)S(1)}, bf16[256,384]{1,0:T(8,128)(2,1)}, u32[]{:S(2)}) copy-start(bf16[256,384]{1,0:T(8,128)(2,1)} %embed_ref.1) | copy-start | bytes 589828
  1.2 14.2 %slice-start.1 = ((s8[8388608]{0:T(1024)(128)(4,1)}), s8[4194304]{0:T(1024)(128)(4,1)S(1)}, s32[]{:S(2)}) async-start(s8[8388608]{0:T(1024)(128)(4,1)} %bitcast.1), calls=%async_computation.1 | async-start | bytes 8388608
  1.3 7.4 %collective-permute-start.1 = (bf16[16,32,128]{2,1,0:T(8,128)(2,1)S(1)}, bf16[16,32,128]{2,1,0:T(8,128)(2,1)S(1)}, u32[]{:S(2)}, u32[]{:S(2)}) collective-permute-start(bf16[16,32,128]{2,1,0:T(8,128)(2,1)S(1)} %get-tuple-element.22.refs_0_), channel_id=1, source_target_pairs={{0,2},{2,0},{1,3},{3,1},{4,6},{6,4},{5,7},{7,5},{8,10},{10,8},{9,1... | collective-permute-start | bytes 393224 | tf_op jit(solution)/shard_map/ppermute | solution.py:211
  4.3 5.4 %collective-permute-start.3 = (bf16[1,32,128]{2,1,0:T(8,128)(2,1)S(1)}, bf16[1,32,128]{2,1,0:T(8,128)(2,1)S(1)}, u32[]{:S(2)}, u32[]{:S(2)}) collective-permute-start(bf16[1,32,128]{2,1,0:T(8,128)(2,1)S(1)} %get-tuple-element.23), channel_id=1, source_target_pairs={{0,4},{4,8},{8,12},{12,0},{1,5},{5,9},{9,13},{13,1},{2,6},{6,10},{... | collective-permute-start | bytes 24584 | tf_op jit(solution)/shard_map/ppermute | solution.py:211
  5.9 5.8 %collective-permute-start = (bf16[16,32,128]{2,1,0:T(8,128)(2,1)S(1)}, bf16[16,32,128]{2,1,0:T(8,128)(2,1)S(1)}, u32[]{:S(2)}, u32[]{:S(2)}) collective-permute-start(bf16[16,32,128]{2,1,0:T(8,128)(2,1)S(1)} %get-tuple-element.22.refs_0_), channel_id=1, source_target_pairs={{0,1},{1,0},{2,3},{3,2},{4,5},{5,4},{6,7},{7,6},{8,9},{9,8},{10,11... | collective-permute-start | bytes 393224 | tf_op jit(solution)/shard_map/ppermute | solution.py:211
  5.9 3.9 %collective-permute-start.4 = (bf16[1,32,128]{2,1,0:T(8,128)(2,1)S(1)}, bf16[1,32,128]{2,1,0:T(8,128)(2,1)S(1)}, u32[]{:S(2)}, u32[]{:S(2)}) collective-permute-start(bf16[1,32,128]{2,1,0:T(8,128)(2,1)S(1)} %get-tuple-element.24), channel_id=1, source_target_pairs={{0,12},{4,0},{8,4},{12,8},{1,13},{5,1},{9,5},{13,9},{2,14},{6,2},{... | collective-permute-start | bytes 24584 | tf_op jit(solution)/shard_map/ppermute | solution.py:211
  8.8 3.0 %collective-permute-start.2 = (bf16[16,32,128]{2,1,0:T(8,128)(2,1)S(1)}, bf16[16,32,128]{2,1,0:T(8,128)(2,1)S(1)}, u32[]{:S(2)}, u32[]{:S(2)}) collective-permute-start(bf16[16,32,128]{2,1,0:T(8,128)(2,1)S(1)} %collective-permute-done.1.refs_2_), channel_id=1, source_target_pairs={{0,1},{1,0},{2,3},{3,2},{4,5},{5,4},{6,7},{7,6},{8,9},{9,8},{10,11... | collective-permute-start | bytes 393224 | tf_op jit(solution)/shard_map/ppermute | solution.py:211
  9.8 4.4 %collective-permute-start.5 = (bf16[2,32,128]{2,1,0:T(8,128)(2,1)S(1)}, bf16[2,32,128]{2,1,0:T(8,128)(2,1)S(1)}, u32[]{:S(2)}, u32[]{:S(2)}) collective-permute-start(bf16[2,32,128]{2,1,0:T(8,128)(2,1)S(1)} %constant_dynamic-update-slice_fusion.refs_0_), channel_id=1, source_target_pairs={{0,1},{1,0},{2,3},{3,2},{4,5},{5,4},{6,7},{7,6},{8,9},{9,8},{10,11... | collective-permute-start | bytes 49160 | tf_op jit(solution)/shard_map/ppermute | solution.py:230
  9.9 4.3 %collective-permute-start.6 = (bf16[2,32,128]{2,1,0:T(8,128)(2,1)S(1)}, bf16[2,32,128]{2,1,0:T(8,128)(2,1)S(1)}, u32[]{:S(2)}, u32[]{:S(2)}) collective-permute-start(bf16[2,32,128]{2,1,0:T(8,128)(2,1)S(1)} %constant_dynamic-update-slice_fusion.refs_0_), channel_id=1, source_target_pairs={{0,2},{1,3},{2,0},{3,1},{4,6},{5,7},{6,4},{7,5},{8,10},{9,11},{10,... | collective-permute-start | bytes 49160 | tf_op jit(solution)/shard_map/ppermute | solution.py:230
  10.2 4.0 %collective-permute-start.7 = (bf16[2,32,128]{2,1,0:T(8,128)(2,1)S(1)}, bf16[2,32,128]{2,1,0:T(8,128)(2,1)S(1)}, u32[]{:S(2)}, u32[]{:S(2)}) collective-permute-start(bf16[2,32,128]{2,1,0:T(8,128)(2,1)S(1)} %constant_dynamic-update-slice_fusion.refs_0_), channel_id=1, source_target_pairs={{0,3},{1,2},{2,1},{3,0},{4,7},{5,6},{6,5},{7,4},{8,11},{9,10},{10,... | collective-permute-start | bytes 49160 | tf_op jit(solution)/shard_map/ppermute | solution.py:230
  15.9 9.0 %collective-permute-start.17 = (bf16[96,1024]{1,0:T(8,128)(2,1)S(1)}, bf16[96,1024]{1,0:T(8,128)(2,1)S(1)}, u32[]{:S(2)}, u32[]{:S(2)}) collective-permute-start(bf16[96,1024]{1,0:T(8,128)(2,1)S(1)} %shard_map.66), channel_id=1, source_target_pairs={{0,12},{4,0},{8,4},{12,8},{1,13},{5,1},{9,5},{13,9},{2,14},{6,2},{... | collective-permute-start | bytes 589832 | tf_op jit(solution)/shard_map/ppermute | solution.py:211
  20.2 9.9 %collective-permute-start.14 = (bf16[96,1024]{1,0:T(8,128)(2,1)S(1)}, bf16[96,1024]{1,0:T(8,128)(2,1)S(1)}, u32[]{:S(2)}, u32[]{:S(2)}) collective-permute-start(bf16[96,1024]{1,0:T(8,128)(2,1)S(1)} %shard_map.64), channel_id=1, source_target_pairs={{0,12},{4,0},{8,4},{12,8},{1,13},{5,1},{9,5},{13,9},{2,14},{6,2},{... | collective-permute-start | bytes 589832 | tf_op jit(solution)/shard_map/ppermute | solution.py:211
  20.7 13.6 %collective-permute-start.11 = (bf16[96,1024]{1,0:T(8,128)(2,1)S(1)}, bf16[96,1024]{1,0:T(8,128)(2,1)S(1)}, u32[]{:S(2)}, u32[]{:S(2)}) collective-permute-start(bf16[96,1024]{1,0:T(8,128)(2,1)S(1)} %shard_map.62), channel_id=1, source_target_pairs={{0,12},{4,0},{8,4},{12,8},{1,13},{5,1},{9,5},{13,9},{2,14},{6,2},{... | collective-permute-start | bytes 589832 | tf_op jit(solution)/shard_map/ppermute | solution.py:211
  21.7 16.8 %collective-permute-start.8 = (bf16[96,1024]{1,0:T(8,128)(2,1)S(1)}, bf16[96,1024]{1,0:T(8,128)(2,1)S(1)}, u32[]{:S(2)}, u32[]{:S(2)}) collective-permute-start(bf16[96,1024]{1,0:T(8,128)(2,1)S(1)} %shard_map.60), channel_id=1, source_target_pairs={{0,12},{4,0},{8,4},{12,8},{1,13},{5,1},{9,5},{13,9},{2,14},{6,2},{... | collective-permute-start | bytes 589832 | tf_op jit(solution)/shard_map/ppermute | solution.py:211
  25.7 17.0 %collective-permute-start.18 = (bf16[96,1024]{1,0:T(8,128)(2,1)S(1)}, bf16[96,1024]{1,0:T(8,128)(2,1)S(1)}, u32[]{:S(2)}, u32[]{:S(2)}) collective-permute-start(bf16[96,1024]{1,0:T(8,128)(2,1)S(1)} %get-tuple-element.37), channel_id=1, source_target_pairs={{0,12},{4,0},{8,4},{12,8},{1,13},{5,1},{9,5},{13,9},{2,14},{6,2},{... | collective-permute-start | bytes 589832 | tf_op jit(solution)/shard_map/ppermute | solution.py:211
  30.8 15.3 %collective-permute-start.15 = (bf16[96,1024]{1,0:T(8,128)(2,1)S(1)}, bf16[96,1024]{1,0:T(8,128)(2,1)S(1)}, u32[]{:S(2)}, u32[]{:S(2)}) collective-permute-start(bf16[96,1024]{1,0:T(8,128)(2,1)S(1)} %get-tuple-element.35), channel_id=1, source_target_pairs={{0,12},{4,0},{8,4},{12,8},{1,13},{5,1},{9,5},{13,9},{2,14},{6,2},{... | collective-permute-start | bytes 589832 | tf_op jit(solution)/shard_map/ppermute | solution.py:211
  35.0 15.3 %collective-permute-start.12 = (bf16[96,1024]{1,0:T(8,128)(2,1)S(1)}, bf16[96,1024]{1,0:T(8,128)(2,1)S(1)}, u32[]{:S(2)}, u32[]{:S(2)}) collective-permute-start(bf16[96,1024]{1,0:T(8,128)(2,1)S(1)} %get-tuple-element.33), channel_id=1, source_target_pairs={{0,12},{4,0},{8,4},{12,8},{1,13},{5,1},{9,5},{13,9},{2,14},{6,2},{... | collective-permute-start | bytes 589832 | tf_op jit(solution)/shard_map/ppermute | solution.py:211
  39.3 15.3 %collective-permute-start.9 = (bf16[96,1024]{1,0:T(8,128)(2,1)S(1)}, bf16[96,1024]{1,0:T(8,128)(2,1)S(1)}, u32[]{:S(2)}, u32[]{:S(2)}) collective-permute-start(bf16[96,1024]{1,0:T(8,128)(2,1)S(1)} %get-tuple-element.31), channel_id=1, source_target_pairs={{0,12},{4,0},{8,4},{12,8},{1,13},{5,1},{9,5},{13,9},{2,14},{6,2},{... | collective-permute-start | bytes 589832 | tf_op jit(solution)/shard_map/ppermute | solution.py:211
  42.7 16.1 %collective-permute-start.19 = (bf16[96,1024]{1,0:T(8,128)(2,1)S(1)}, bf16[96,1024]{1,0:T(8,128)(2,1)S(1)}, u32[]{:S(2)}, u32[]{:S(2)}) collective-permute-start(bf16[96,1024]{1,0:T(8,128)(2,1)S(1)} %add_convert_fusion), channel_id=1, source_target_pairs={{0,12},{4,0},{8,4},{12,8},{1,13},{5,1},{9,5},{13,9},{2,14},{6,2},{... | collective-permute-start | bytes 589832 | tf_op jit(solution)/shard_map/ppermute | solution.py:211
  46.2 16.6 %collective-permute-start.16 = (bf16[96,1024]{1,0:T(8,128)(2,1)S(1)}, bf16[96,1024]{1,0:T(8,128)(2,1)S(1)}, u32[]{:S(2)}, u32[]{:S(2)}) collective-permute-start(bf16[96,1024]{1,0:T(8,128)(2,1)S(1)} %add_convert_fusion.1), channel_id=1, source_target_pairs={{0,12},{4,0},{8,4},{12,8},{1,13},{5,1},{9,5},{13,9},{2,14},{6,2},{... | collective-permute-start | bytes 589832 | tf_op jit(solution)/shard_map/ppermute | solution.py:211
  50.4 16.6 %collective-permute-start.13 = (bf16[96,1024]{1,0:T(8,128)(2,1)S(1)}, bf16[96,1024]{1,0:T(8,128)(2,1)S(1)}, u32[]{:S(2)}, u32[]{:S(2)}) collective-permute-start(bf16[96,1024]{1,0:T(8,128)(2,1)S(1)} %add_convert_fusion.2), channel_id=1, source_target_pairs={{0,12},{4,0},{8,4},{12,8},{1,13},{5,1},{9,5},{13,9},{2,14},{6,2},{... | collective-permute-start | bytes 589832 | tf_op jit(solution)/shard_map/ppermute | solution.py:211
  54.6 16.0 %collective-permute-start.10 = (bf16[96,1024]{1,0:T(8,128)(2,1)S(1)}, bf16[96,1024]{1,0:T(8,128)(2,1)S(1)}, u32[]{:S(2)}, u32[]{:S(2)}) collective-permute-start(bf16[96,1024]{1,0:T(8,128)(2,1)S(1)} %add_convert_fusion.3), channel_id=1, source_target_pairs={{0,12},{4,0},{8,4},{12,8},{1,13},{5,1},{9,5},{13,9},{2,14},{6,2},{... | collective-permute-start | bytes 589832 | tf_op jit(solution)/shard_map/ppermute | solution.py:211

commit v19 on v18

--- a/solution.py
+++ b/solution.py
@@ -7,7 +7,7 @@
 from jax.experimental.pallas import tpu as pltpu
 from jax.sharding import PartitionSpec as P
 
-PIECES = 4
+PIECES = (2, 3, 3)
 STEP = 256
 LANES = 128
 PACK_COST = 20 * 10**9
@@ -340,27 +340,26 @@
     )(arrived, kept, *earlier)
 
 
-def lift(tokens, token_mixing, pieces):
+def lift(tokens, token_mixing, shares):
     count = lax.axis_size("tok")
-    embed = tokens.shape[0]
+    embed, columns = tokens.shape[0], token_mixing.shape[1]
     rows = embed // count
-    width = token_mixing.shape[1] // pieces
-    sent = jax.ShapeDtypeStruct((rows, width), jnp.bfloat16)
-    ways = [-1] * pieces
-    blocks = [list(range(count - 2, -1, -1)) if way == 1 else list(range(count - 1)) for way in ways]
+    cuts = [columns * sum(shares[:at]) // sum(shares) for at in range(len(shares) + 1)]
+    widths = [last - first for first, last in zip(cuts[:-1], cuts[1:])]
+    pieces = len(widths)
+    sent = [jax.ShapeDtypeStruct((rows, width), jnp.bfloat16) for width in widths]
     travelling = [
-        call(functools.partial(sent_kernel, piece * width, blocks[piece][0]), sent, (tokens, token_mixing))
-        for piece in range(pieces)
+        call(functools.partial(sent_kernel, cuts[piece], 0), sent[piece], (tokens, token_mixing)) for piece in range(pieces)
     ]
     kept = [None] * pieces
     result = None
     for step in range(1, count):
         for piece in range(pieces):
-            arrived = turned(travelling[piece], "tok", ways[piece])
+            arrived = turned(travelling[piece], "tok", -1)
             if step == 1:
                 travelling[piece], kept[piece] = call(
-                    functools.partial(hop_kernel, piece * width, blocks[piece][1:] + [count - 1]),
-                    [sent, jax.ShapeDtypeStruct((embed - 2 * rows, width), jnp.float32)],
+                    functools.partial(hop_kernel, cuts[piece], list(range(1, count))),
+                    [sent[piece], jax.ShapeDtypeStruct((embed - 2 * rows, widths[piece]), jnp.float32)],
                     (arrived, tokens, token_mixing),
                 )
             elif step < count - 1:
@@ -368,7 +367,7 @@
                 summed = arrived.astype(jnp.float32) + kept[piece][at : at + rows]
                 travelling[piece] = summed.astype(jnp.bfloat16)
             else:
-                result = finish(piece * width, arrived, kept[piece], result, pieces * width)
+                result = finish(cuts[piece], arrived, kept[piece], result, columns)
     return result
 
 

time: 71.6 us -> 77.7 us (1.085)
  waiting for transfers between devices: 12.8 us -> 38.6 us
  starting transfers between devices: 44.8 us -> 26.2 us
  Pallas kernels: 12.3 us -> 11.4 us
    ppermute x17 -> x14, waiting for transfers between devices: 12.7 us -> 38.5 us  [turned(): lax.ppermute(value, axis, [(i, (i + away) % count) for i in range(count)])]
    ppermute x17 -> x14, starting transfers between devices: 42.8 us -> 24.3 us  [turned(): lax.ppermute(value, axis, [(i, (i + away) % count) for i in range(count)])]
    pallas_call x4 -> x3, Pallas kernels: 3.03 us -> 2.41 us  [finish(): pl.pallas_call(functools.partial(last_kernel, first), out_shape=jax.Shape...]
    pallas_call x13 -> x11, Pallas kernels: 9.28 us -> 8.97 us  [call(): pl.pallas_call(kernel, out_shape=out_shape, in_specs=[pl.BlockSpec(memory...]
  transfers between devices with their start and end apart: 20 -> 17, of which waited for: 5 -> 5; matrix products, arithmetic and copies ran while one was open for 0% -> 0% of each run, Pallas kernels for 14% -> 11%
where the time goes in v19:
time: 77.7 us; the launch traced here: 77.6 us
  waiting for transfers between devices  38.6 us (50%)
  starting transfers between devices  26.2 us (34%)
  Pallas kernels  11.4 us (15%)
  local copies, waits for them, and re-layouts  1.07 us (1%)
    ppermute x14, waiting for transfers between devices, turned(): lax.ppermute(value, axis, [(i, (i + away) % count) for i in range(count)])  38.5 us
    ppermute x14, starting transfers between devices, turned(): lax.ppermute(value, axis, [(i, (i + away) % count) for i in range(count)])  24.3 us
    pallas_call x11, Pallas kernels, call(): pl.pallas_call(kernel, out_shape=out_shape, in_specs=[pl.BlockSpec(memory...  8.97 us
    pallas_call x3, Pallas kernels, finish(): pl.pallas_call(functools.partial(last_kernel, first), out_shape=jax.Shape...  2.41 us
    ppermute x3, starting transfers between devices, direct_blocks(): blocks.append(lax.ppermute(block, ('ch', 'sub'), route))  1.93 us
  transfers between devices with their start and end apart: 17, of which 5 were waited for; matrix products, arithmetic and copies ran while one was open for 0% of the time, Pallas kernels for 11%

profile of v19, /device:TPU:0, one launch (start us, length us, event | category | flops | bytes accessed | tf_op | source)
XLA Modules:
  0.0 77.6 jit_solution(7081528144210741753)
XLA Ops:
  0.0 1.0 %copy-done.4 = f32[64,32,32]{0,2,1:T(8,128)S(1)} copy-done((f32[64,32,32]{0,2,1:T(8,128)S(1)}, f32[64,32,32]{0,2,1:T(8,128)}, u32[]{:S(2)}) %copy-start.4) | copy-done | bytes 262168
  1.0 0.1 shard_map.55
  1.2 3.0 %collective-permute-start.1 = (bf16[16,32,128]{2,1,0:T(8,128)(2,1)S(1)}, bf16[16,32,128]{2,1,0:T(8,128)(2,1)S(1)}, u32[]{:S(2)}, u32[]{:S(2)}) collective-permute-start(bf16[16,32,128]{2,1,0:T(8,128)(2,1)S(1)} %get-tuple-element.20.refs_0_), channel_id=1, source_target_pairs={{0,2},{2,0},{1,3},{3,1},{4,6},{6,4},{5,7},{7,5},{8,10},{10,8},{9,1... | collective-permute-start | bytes 393224 | tf_op jit(solution)/shard_map/ppermute | solution.py:211
  4.2 1.6 %collective-permute-start.3 = (bf16[1,32,128]{2,1,0:T(8,128)(2,1)S(1)}, bf16[1,32,128]{2,1,0:T(8,128)(2,1)S(1)}, u32[]{:S(2)}, u32[]{:S(2)}) collective-permute-start(bf16[1,32,128]{2,1,0:T(8,128)(2,1)S(1)} %get-tuple-element.21), channel_id=1, source_target_pairs={{0,4},{4,8},{8,12},{12,0},{1,5},{5,9},{9,13},{13,1},{2,6},{6,10},{... | collective-permute-start | bytes 24584 | tf_op jit(solution)/shard_map/ppermute | solution.py:211
  5.7 0.0 collective-permute-start
  5.7 2.2 %collective-permute-start.4 = (bf16[1,32,128]{2,1,0:T(8,128)(2,1)S(1)}, bf16[1,32,128]{2,1,0:T(8,128)(2,1)S(1)}, u32[]{:S(2)}, u32[]{:S(2)}) collective-permute-start(bf16[1,32,128]{2,1,0:T(8,128)(2,1)S(1)} %get-tuple-element.22), channel_id=1, source_target_pairs={{0,12},{4,0},{8,4},{12,8},{1,13},{5,1},{9,5},{13,9},{2,14},{6,2},{... | collective-permute-start | bytes 24584 | tf_op jit(solution)/shard_map/ppermute | solution.py:211
  8.0 0.6 shard_map.57
  8.6 0.0 collective-permute-done.1.refs_2_
  8.6 0.3 collective-permute-start.2
  8.9 0.7 collective-permute-done.3
  9.6 0.0 collective-permute-done.4
  9.6 0.1 collective-permute-start.5
  9.7 0.4 collective-permute-start.6
  10.1 1.5 %collective-permute-start.7 = (bf16[2,32,128]{2,1,0:T(8,128)(2,1)S(1)}, bf16[2,32,128]{2,1,0:T(8,128)(2,1)S(1)}, u32[]{:S(2)}, u32[]{:S(2)}) collective-permute-start(bf16[2,32,128]{2,1,0:T(8,128)(2,1)S(1)} %constant_dynamic-update-slice_fusion.refs_0_), channel_id=1, source_target_pairs={{0,3},{1,2},{2,1},{3,0},{4,7},{5,6},{6,5},{7,4},{8,11},{9,10},{10,... | collective-permute-start | bytes 49160 | tf_op jit(solution)/shard_map/ppermute | solution.py:230
  11.6 0.0 collective-permute-done.refs_1_
  11.6 0.0 collective-permute-done.2.refs_3_
  11.6 0.0 copy-start
  11.6 2.4 %shard_map.58 = (bf16[384,768]{1,0:T(8,128)(2,1)S(1)}, bf16[4,128,128]{2,1,0:T(8,128)(2,1)S(1)}, bf16[4,128,128]{2,1,0:T(8,128)(2,1)S(1)}) custom-call(bf16[16,128,128]{2,1,0:T(8,128)(2,1)S(1)} %shard_map.56.field_ref, bf16[256,768]{1,0:T(8,128)(2,1)S(1)} %get-tuple-element.23.taps_one_ref.refs_6_, ...), custom_call_target="tpu_custom_call" | custom-call | flops 1635778560 | bytes 524288 | tf_op jit(solution)/shard_map/pallas_call | solution.py:198
  14.0 0.0 collective-permute-done.5.refs_1_
  14.0 0.0 collective-permute-done.6.refs_2_
  14.0 0.0 collective-permute-done.7.refs_3_
  14.1 1.2 %shard_map.59.tokens_ref = bf16[384,1024]{1,0:T(8,128)(2,1)S(1)} custom-call(bf16[16,128,128]{2,1,0:T(8,128)(2,1)S(1)} %shard_map.56.field_ref, bf16[2,32,128]{2,1,0:T(8,128)(2,1)S(1)} %constant_dynamic-update-slice_fusion.refs_0_, bf16[2,32,128]{2,1,0:T(8,128)(2,1)S(1)} %collective-permute-done.5.refs_1_, ...), custom_call_target="tpu_custom_call" | custom-call | flops 503316480 | bytes 524288 | tf_op jit(solution)/shard_map/pallas_call | solution.py:198
  15.3 0.6 shard_map.62
  15.9 3.8 %collective-permute-start.11 = (bf16[96,1536]{1,0:T(8,128)(2,1)S(1)}, bf16[96,1536]{1,0:T(8,128)(2,1)S(1)}, u32[]{:S(2)}, u32[]{:S(2)}) collective-permute-start(bf16[96,1536]{1,0:T(8,128)(2,1)S(1)} %shard_map.62), channel_id=1, source_target_pairs={{0,12},{4,0},{8,4},{12,8},{1,13},{5,1},{9,5},{13,9},{2,14},{6,2},{... | collective-permute-start | bytes 884744 | tf_op jit(solution)/shard_map/ppermute | solution.py:211
  19.7 0.6 shard_map.60
  20.3 0.1 collective-permute-start.8
  20.4 6.7 %collective-permute-done.11.arrived_ref = bf16[96,1536]{1,0:T(8,128)(2,1)S(1)} collective-permute-done((bf16[96,1536]{1,0:T(8,128)(2,1)S(1)}, bf16[96,1536]{1,0:T(8,128)(2,1)S(1)}, u32[]{:S(2)}, u32[]{:S(2)}) %collective-permute-start.11) | collective-permute-done | bytes 294944 | tf_op jit(solution)/shard_map/ppermute | solution.py:211
  27.1 1.1 %shard_map.63 = (bf16[96,1536]{1,0:T(8,128)(2,1)S(1)}, f32[192,1536]{1,0:T(8,128)S(1)}) custom-call(bf16[96,1536]{1,0:T(8,128)(2,1)S(1)} %collective-permute-done.11.arrived_ref, bf16[384,1024]{1,0:T(8,128)(2,1)S(1)} %shard_map.59.tokens_ref, bf16[1024,4096]{1,0:T(8,128)(2,1)S(1)} %copy-done), custom_call_target="tpu_custom_call" | custom-call | tf_op jit(solution)/shard_map/pallas_call | solution.py:198
  28.1 4.3 %collective-permute-start.12 = (bf16[96,1536]{1,0:T(8,128)(2,1)S(1)}, bf16[96,1536]{1,0:T(8,128)(2,1)S(1)}, u32[]{:S(2)}, u32[]{:S(2)}) collective-permute-start(bf16[96,1536]{1,0:T(8,128)(2,1)S(1)} %get-tuple-element.31), channel_id=1, source_target_pairs={{0,12},{4,0},{8,4},{12,8},{1,13},{5,1},{9,5},{13,9},{2,14},{6,2},{... | collective-permute-start | bytes 884744 | tf_op jit(solution)/shard_map/ppermute | solution.py:211
  32.5 0.5 shard_map.64
  32.9 0.1 collective-permute-start.14
  33.0 10.3 %collective-permute-done.14.arrived_ref = bf16[96,1024]{1,0:T(8,128)(2,1)S(1)} collective-permute-done((bf16[96,1024]{1,0:T(8,128)(2,1)S(1)}, bf16[96,1024]{1,0:T(8,128)(2,1)S(1)}, u32[]{:S(2)}, u32[]{:S(2)}) %collective-permute-start.14) | collective-permute-done | bytes 196640 | tf_op jit(solution)/shard_map/ppermute | solution.py:211
  43.3 0.8 shard_map.65
  44.0 4.4 %collective-permute-start.15 = (bf16[96,1024]{1,0:T(8,128)(2,1)S(1)}, bf16[96,1024]{1,0:T(8,128)(2,1)S(1)}, u32[]{:S(2)}, u32[]{:S(2)}) collective-permute-start(bf16[96,1024]{1,0:T(8,128)(2,1)S(1)} %get-tuple-element.33), channel_id=1, source_target_pairs={{0,12},{4,0},{8,4},{12,8},{1,13},{5,1},{9,5},{13,9},{2,14},{6,2},{... | collective-permute-start | bytes 589832 | tf_op jit(solution)/shard_map/ppermute | solution.py:211
  48.4 1.1 %shard_map.61 = (bf16[96,1536]{1,0:T(8,128)(2,1)S(1)}, f32[192,1536]{1,0:T(8,128)S(1)}) custom-call(bf16[96,1536]{1,0:T(8,128)(2,1)S(1)} %collective-permute-done.8.arrived_ref, bf16[384,1024]{1,0:T(8,128)(2,1)S(1)} %shard_map.59.tokens_ref, bf16[1024,4096]{1,0:T(8,128)(2,1)S(1)} %copy-done), custom_call_target="tpu_custom_call" | custom-call | tf_op jit(solution)/shard_map/pallas_call | solution.py:198
  49.5 0.1 collective-permute-start.9
  49.6 0.0 collective-permute-done.12
  49.6 0.1 add_convert_fusion
  49.6 0.1 collective-permute-start.13
  49.7 10.4 %collective-permute-done.9 = bf16[96,1536]{1,0:T(8,128)(2,1)S(1)} collective-permute-done((bf16[96,1536]{1,0:T(8,128)(2,1)S(1)}, bf16[96,1536]{1,0:T(8,128)(2,1)S(1)}, u32[]{:S(2)}, u32[]{:S(2)}) %collective-permute-start.9) | collective-permute-done | bytes 294944 | tf_op jit(solution)/shard_map/ppermute | solution.py:211
  60.1 0.1 add_convert_fusion.1
  60.1 4.3 %collective-permute-start.10 = (bf16[96,1536]{1,0:T(8,128)(2,1)S(1)}, bf16[96,1536]{1,0:T(8,128)(2,1)S(1)}, u32[]{:S(2)}, u32[]{:S(2)}) collective-permute-start(bf16[96,1536]{1,0:T(8,128)(2,1)S(1)} %add_convert_fusion.1), channel_id=1, source_target_pairs={{0,12},{4,0},{8,4},{12,8},{1,13},{5,1},{9,5},{13,9},{2,14},{6,2},{... | collective-permute-start | bytes 884744 | tf_op jit(solution)/shard_map/ppermute | solution.py:211
  64.5 0.1 collective-permute-start.16
  64.6 10.5 %collective-permute-done.16.arrived_ref = bf16[96,1024]{1,0:T(8,128)(2,1)S(1)} collective-permute-done((bf16[96,1024]{1,0:T(8,128)(2,1)S(1)}, bf16[96,1024]{1,0:T(8,128)(2,1)S(1)}, u32[]{:S(2)}, u32[]{:S(2)}) %collective-permute-start.16) | collective-permute-done | bytes 196640 | tf_op jit(solution)/shard_map/ppermute | solution.py:211
  75.1 0.8 shard_map.66.refs_0_
  75.9 0.8 %shard_map.67.refs_0_ = bf16[96,4096]{1,0:T(8,128)(2,1)} custom-call(bf16[96,1536]{1,0:T(8,128)(2,1)S(1)} %collective-permute-done.13.arrived_ref, f32[192,1536]{1,0:T(8,128)S(1)} %get-tuple-element.32.kept_ref, bf16[96,4096]{1,0:T(8,128)(2,1)} %shard_map.66.refs_0_), custom_call_target="tpu_custom_call", output_to_operand_aliasing={{}: (2, {})} | custom-call | tf_op jit(solution)/shard_map/pallas_call | solution.py:328
  76.7 0.0 collective-permute-done.10.arrived_ref
  76.7 0.8 %shard_map.68 = bf16[96,4096]{1,0:T(8,128)(2,1)} custom-call(bf16[96,1536]{1,0:T(8,128)(2,1)S(1)} %collective-permute-done.10.arrived_ref, f32[192,1536]{1,0:T(8,128)S(1)} %get-tuple-element.30.kept_ref, bf16[96,4096]{1,0:T(8,128)(2,1)} %shard_map.67.refs_0_), custom_call_target="tpu_custom_call", output_to_operand_aliasing={{}: (2, {})} | custom-call | tf_op jit(solution)/shard_map/pallas_call | solution.py:328
  (15 shorter events, 0.1 us)
Async XLA Ops:
  0.0 1.0 %copy-start.4 = (f32[64,32,32]{0,2,1:T(8,128)S(1)}, f32[64,32,32]{0,2,1:T(8,128)}, u32[]{:S(2)}) copy-start(f32[64,32,32]{0,2,1:T(8,128)} %param.5) | copy-start | bytes 786436
  1.0 6.9 %copy-start.1 = (f32[9,64,64]{2,1,0:T(8,128)S(1)}, f32[9,64,64]{2,1,0:T(8,128)}, u32[]{:S(2)}) copy-start(f32[9,64,64]{2,1,0:T(8,128)} %first_ref.1) | copy-start | bytes 442372
  1.0 6.9 %copy-start.2 = (f32[9,64,64]{2,1,0:T(8,128)S(1)}, f32[9,64,64]{2,1,0:T(8,128)}, u32[]{:S(2)}) copy-start(f32[9,64,64]{2,1,0:T(8,128)} %second_ref.1) | copy-start | bytes 442372
  1.0 7.0 %copy-start.3 = (bf16[256,384]{1,0:T(8,128)(2,1)S(1)}, bf16[256,384]{1,0:T(8,128)(2,1)}, u32[]{:S(2)}) copy-start(bf16[256,384]{1,0:T(8,128)(2,1)} %embed_ref.1) | copy-start | bytes 589828
  1.2 7.4 %collective-permute-start.1 = (bf16[16,32,128]{2,1,0:T(8,128)(2,1)S(1)}, bf16[16,32,128]{2,1,0:T(8,128)(2,1)S(1)}, u32[]{:S(2)}, u32[]{:S(2)}) collective-permute-start(bf16[16,32,128]{2,1,0:T(8,128)(2,1)S(1)} %get-tuple-element.20.refs_0_), channel_id=1, source_target_pairs={{0,2},{2,0},{1,3},{3,1},{4,6},{6,4},{5,7},{7,5},{8,10},{10,8},{9,1... | collective-permute-start | bytes 393224 | tf_op jit(solution)/shard_map/ppermute | solution.py:211
  4.2 5.4 %collective-permute-start.3 = (bf16[1,32,128]{2,1,0:T(8,128)(2,1)S(1)}, bf16[1,32,128]{2,1,0:T(8,128)(2,1)S(1)}, u32[]{:S(2)}, u32[]{:S(2)}) collective-permute-start(bf16[1,32,128]{2,1,0:T(8,128)(2,1)S(1)} %get-tuple-element.21), channel_id=1, source_target_pairs={{0,4},{4,8},{8,12},{12,0},{1,5},{5,9},{9,13},{13,1},{2,6},{6,10},{... | collective-permute-start | bytes 24584 | tf_op jit(solution)/shard_map/ppermute | solution.py:211
  5.7 5.8 %collective-permute-start = (bf16[16,32,128]{2,1,0:T(8,128)(2,1)S(1)}, bf16[16,32,128]{2,1,0:T(8,128)(2,1)S(1)}, u32[]{:S(2)}, u32[]{:S(2)}) collective-permute-start(bf16[16,32,128]{2,1,0:T(8,128)(2,1)S(1)} %get-tuple-element.20.refs_0_), channel_id=1, source_target_pairs={{0,1},{1,0},{2,3},{3,2},{4,5},{5,4},{6,7},{7,6},{8,9},{9,8},{10,11... | collective-permute-start | bytes 393224 | tf_op jit(solution)/shard_map/ppermute | solution.py:211
  5.7 3.9 %collective-permute-start.4 = (bf16[1,32,128]{2,1,0:T(8,128)(2,1)S(1)}, bf16[1,32,128]{2,1,0:T(8,128)(2,1)S(1)}, u32[]{:S(2)}, u32[]{:S(2)}) collective-permute-start(bf16[1,32,128]{2,1,0:T(8,128)(2,1)S(1)} %get-tuple-element.22), channel_id=1, source_target_pairs={{0,12},{4,0},{8,4},{12,8},{1,13},{5,1},{9,5},{13,9},{2,14},{6,2},{... | collective-permute-start | bytes 24584 | tf_op jit(solution)/shard_map/ppermute | solution.py:211
  8.6 3.0 %collective-permute-start.2 = (bf16[16,32,128]{2,1,0:T(8,128)(2,1)S(1)}, bf16[16,32,128]{2,1,0:T(8,128)(2,1)S(1)}, u32[]{:S(2)}, u32[]{:S(2)}) collective-permute-start(bf16[16,32,128]{2,1,0:T(8,128)(2,1)S(1)} %collective-permute-done.1.refs_2_), channel_id=1, source_target_pairs={{0,1},{1,0},{2,3},{3,2},{4,5},{5,4},{6,7},{7,6},{8,9},{9,8},{10,11... | collective-permute-start | bytes 393224 | tf_op jit(solution)/shard_map/ppermute | solution.py:211
  9.6 4.4 %collective-permute-start.5 = (bf16[2,32,128]{2,1,0:T(8,128)(2,1)S(1)}, bf16[2,32,128]{2,1,0:T(8,128)(2,1)S(1)}, u32[]{:S(2)}, u32[]{:S(2)}) collective-permute-start(bf16[2,32,128]{2,1,0:T(8,128)(2,1)S(1)} %constant_dynamic-update-slice_fusion.refs_0_), channel_id=1, source_target_pairs={{0,1},{1,0},{2,3},{3,2},{4,5},{5,4},{6,7},{7,6},{8,9},{9,8},{10,11... | collective-permute-start | bytes 49160 | tf_op jit(solution)/shard_map/ppermute | solution.py:230
  9.7 4.3 %collective-permute-start.6 = (bf16[2,32,128]{2,1,0:T(8,128)(2,1)S(1)}, bf16[2,32,128]{2,1,0:T(8,128)(2,1)S(1)}, u32[]{:S(2)}, u32[]{:S(2)}) collective-permute-start(bf16[2,32,128]{2,1,0:T(8,128)(2,1)S(1)} %constant_dynamic-update-slice_fusion.refs_0_), channel_id=1, source_target_pairs={{0,2},{1,3},{2,0},{3,1},{4,6},{5,7},{6,4},{7,5},{8,10},{9,11},{10,... | collective-permute-start | bytes 49160 | tf_op jit(solution)/shard_map/ppermute | solution.py:230
  10.1 4.0 %collective-permute-start.7 = (bf16[2,32,128]{2,1,0:T(8,128)(2,1)S(1)}, bf16[2,32,128]{2,1,0:T(8,128)(2,1)S(1)}, u32[]{:S(2)}, u32[]{:S(2)}) collective-permute-start(bf16[2,32,128]{2,1,0:T(8,128)(2,1)S(1)} %constant_dynamic-update-slice_fusion.refs_0_), channel_id=1, source_target_pairs={{0,3},{1,2},{2,1},{3,0},{4,7},{5,6},{6,5},{7,4},{8,11},{9,10},{10,... | collective-permute-start | bytes 49160 | tf_op jit(solution)/shard_map/ppermute | solution.py:230
  11.6 3.6 %copy-start = (bf16[1024,4096]{1,0:T(8,128)(2,1)S(1)}, bf16[1024,4096]{1,0:T(8,128)(2,1)}, u32[]{:S(2)}) copy-start(bf16[1024,4096]{1,0:T(8,128)(2,1)} %mixing_ref.11) | copy-start | bytes 25165828
  15.9 11.2 %collective-permute-start.11 = (bf16[96,1536]{1,0:T(8,128)(2,1)S(1)}, bf16[96,1536]{1,0:T(8,128)(2,1)S(1)}, u32[]{:S(2)}, u32[]{:S(2)}) collective-permute-start(bf16[96,1536]{1,0:T(8,128)(2,1)S(1)} %shard_map.62), channel_id=1, source_target_pairs={{0,12},{4,0},{8,4},{12,8},{1,13},{5,1},{9,5},{13,9},{2,14},{6,2},{... | collective-permute-start | bytes 884744 | tf_op jit(solution)/shard_map/ppermute | solution.py:211
  20.3 28.1 %collective-permute-start.8 = (bf16[96,1536]{1,0:T(8,128)(2,1)S(1)}, bf16[96,1536]{1,0:T(8,128)(2,1)S(1)}, u32[]{:S(2)}, u32[]{:S(2)}) collective-permute-start(bf16[96,1536]{1,0:T(8,128)(2,1)S(1)} %shard_map.60), channel_id=1, source_target_pairs={{0,12},{4,0},{8,4},{12,8},{1,13},{5,1},{9,5},{13,9},{2,14},{6,2},{... | collective-permute-start | bytes 884744 | tf_op jit(solution)/shard_map/ppermute | solution.py:211
  28.1 21.4 %collective-permute-start.12 = (bf16[96,1536]{1,0:T(8,128)(2,1)S(1)}, bf16[96,1536]{1,0:T(8,128)(2,1)S(1)}, u32[]{:S(2)}, u32[]{:S(2)}) collective-permute-start(bf16[96,1536]{1,0:T(8,128)(2,1)S(1)} %get-tuple-element.31), channel_id=1, source_target_pairs={{0,12},{4,0},{8,4},{12,8},{1,13},{5,1},{9,5},{13,9},{2,14},{6,2},{... | collective-permute-start | bytes 884744 | tf_op jit(solution)/shard_map/ppermute | solution.py:211
  32.9 10.3 %collective-permute-start.14 = (bf16[96,1024]{1,0:T(8,128)(2,1)S(1)}, bf16[96,1024]{1,0:T(8,128)(2,1)S(1)}, u32[]{:S(2)}, u32[]{:S(2)}) collective-permute-start(bf16[96,1024]{1,0:T(8,128)(2,1)S(1)} %shard_map.64), channel_id=1, source_target_pairs={{0,12},{4,0},{8,4},{12,8},{1,13},{5,1},{9,5},{13,9},{2,14},{6,2},{... | collective-permute-start | bytes 589832 | tf_op jit(solution)/shard_map/ppermute | solution.py:211
  44.0 20.4 %collective-permute-start.15 = (bf16[96,1024]{1,0:T(8,128)(2,1)S(1)}, bf16[96,1024]{1,0:T(8,128)(2,1)S(1)}, u32[]{:S(2)}, u32[]{:S(2)}) collective-permute-start(bf16[96,1024]{1,0:T(8,128)(2,1)S(1)} %get-tuple-element.33), channel_id=1, source_target_pairs={{0,12},{4,0},{8,4},{12,8},{1,13},{5,1},{9,5},{13,9},{2,14},{6,2},{... | collective-permute-start | bytes 589832 | tf_op jit(solution)/shard_map/ppermute | solution.py:211
  49.5 10.6 %collective-permute-start.9 = (bf16[96,1536]{1,0:T(8,128)(2,1)S(1)}, bf16[96,1536]{1,0:T(8,128)(2,1)S(1)}, u32[]{:S(2)}, u32[]{:S(2)}) collective-permute-start(bf16[96,1536]{1,0:T(8,128)(2,1)S(1)} %get-tuple-element.29), channel_id=1, source_target_pairs={{0,12},{4,0},{8,4},{12,8},{1,13},{5,1},{9,5},{13,9},{2,14},{6,2},{... | collective-permute-start | bytes 884744 | tf_op jit(solution)/shard_map/ppermute | solution.py:211
  49.6 26.2 %collective-permute-start.13 = (bf16[96,1536]{1,0:T(8,128)(2,1)S(1)}, bf16[96,1536]{1,0:T(8,128)(2,1)S(1)}, u32[]{:S(2)}, u32[]{:S(2)}) collective-permute-start(bf16[96,1536]{1,0:T(8,128)(2,1)S(1)} %add_convert_fusion), channel_id=1, source_target_pairs={{0,12},{4,0},{8,4},{12,8},{1,13},{5,1},{9,5},{13,9},{2,14},{6,2},{... | collective-permute-start | bytes 884744 | tf_op jit(solution)/shard_map/ppermute | solution.py:211
  60.1 16.6 %collective-permute-start.10 = (bf16[96,1536]{1,0:T(8,128)(2,1)S(1)}, bf16[96,1536]{1,0:T(8,128)(2,1)S(1)}, u32[]{:S(2)}, u32[]{:S(2)}) collective-permute-start(bf16[96,1536]{1,0:T(8,128)(2,1)S(1)} %add_convert_fusion.1), channel_id=1, source_target_pairs={{0,12},{4,0},{8,4},{12,8},{1,13},{5,1},{9,5},{13,9},{2,14},{6,2},{... | collective-permute-start | bytes 884744 | tf_op jit(solution)/shard_map/ppermute | solution.py:211
  64.5 10.6 %collective-permute-start.16 = (bf16[96,1024]{1,0:T(8,128)(2,1)S(1)}, bf16[96,1024]{1,0:T(8,128)(2,1)S(1)}, u32[]{:S(2)}, u32[]{:S(2)}) collective-permute-start(bf16[96,1024]{1,0:T(8,128)(2,1)S(1)} %add_convert_fusion.2), channel_id=1, source_target_pairs={{0,12},{4,0},{8,4},{12,8},{1,13},{5,1},{9,5},{13,9},{2,14},{6,2},{... | collective-permute-start | bytes 589832 | tf_op jit(solution)/shard_map/ppermute | solution.py:211

commit v20 on v19

--- a/solution.py
+++ b/solution.py
@@ -7,7 +7,7 @@
 from jax.experimental.pallas import tpu as pltpu
 from jax.sharding import PartitionSpec as P
 
-PIECES = (2, 3, 3)
+PIECES = (1, 1)
 STEP = 256
 LANES = 128
 PACK_COST = 20 * 10**9

time: 77.7 us -> 71.6 us (0.921)
  waiting for transfers between devices: 38.6 us -> 29.4 us
  starting transfers between devices: 26.2 us -> 30.2 us
  Pallas kernels: 11.4 us -> 10.4 us
    ppermute x14 -> x11, waiting for transfers between devices: 38.5 us -> 29.4 us  [turned(): lax.ppermute(value, axis, [(i, (i + away) % count) for i in range(count)])]
    ppermute x14 -> x11, starting transfers between devices: 24.3 us -> 28.3 us  [turned(): lax.ppermute(value, axis, [(i, (i + away) % count) for i in range(count)])]
    pallas_call x3 -> x2, Pallas kernels: 2.41 us -> 1.74 us  [finish(): pl.pallas_call(functools.partial(last_kernel, first), out_shape=jax.Shape...]
    pallas_call x11 -> x9, Pallas kernels: 8.97 us -> 8.68 us  [call(): pl.pallas_call(kernel, out_shape=out_shape, in_specs=[pl.BlockSpec(memory...]
  transfers between devices with their start and end apart: 17 -> 14, of which waited for: 5 -> 7; matrix products, arithmetic and copies ran while one was open for 0% -> 0% of each run, Pallas kernels for 11% -> 10%
where the time goes in v20:
time: 71.6 us; the launch traced here: 71.4 us
  starting transfers between devices  30.2 us (42%)
  waiting for transfers between devices  29.4 us (41%)
  Pallas kernels  10.4 us (15%)
  local copies, waits for them, and re-layouts  1.07 us (1%)
    ppermute x11, waiting for transfers between devices, turned(): lax.ppermute(value, axis, [(i, (i + away) % count) for i in range(count)])  29.4 us
    ppermute x11, starting transfers between devices, turned(): lax.ppermute(value, axis, [(i, (i + away) % count) for i in range(count)])  28.3 us
    pallas_call x9, Pallas kernels, call(): pl.pallas_call(kernel, out_shape=out_shape, in_specs=[pl.BlockSpec(memory...  8.68 us
    ppermute x3, starting transfers between devices, direct_blocks(): blocks.append(lax.ppermute(block, ('ch', 'sub'), route))  1.92 us
    pallas_call x2, Pallas kernels, finish(): pl.pallas_call(functools.partial(last_kernel, first), out_shape=jax.Shape...  1.74 us
  transfers between devices with their start and end apart: 14, of which 7 were waited for; matrix products, arithmetic and copies ran while one was open for 0% of the time, Pallas kernels for 10%

profile of v20, /device:TPU:0, one launch (start us, length us, event | category | flops | bytes accessed | tf_op | source)
XLA Modules:
  0.0 71.4 jit_solution(3583682238975613136)
XLA Ops:
  0.0 0.0 copy-start.4
  0.0 1.0 %copy-done.4 = f32[64,32,32]{0,2,1:T(8,128)S(1)} copy-done((f32[64,32,32]{0,2,1:T(8,128)S(1)}, f32[64,32,32]{0,2,1:T(8,128)}, u32[]{:S(2)}) %copy-start.4) | copy-done | bytes 262168
  1.0 0.0 copy-start.1
  1.0 0.1 shard_map.55
  1.2 3.0 %collective-permute-start.1 = (bf16[16,32,128]{2,1,0:T(8,128)(2,1)S(1)}, bf16[16,32,128]{2,1,0:T(8,128)(2,1)S(1)}, u32[]{:S(2)}, u32[]{:S(2)}) collective-permute-start(bf16[16,32,128]{2,1,0:T(8,128)(2,1)S(1)} %get-tuple-element.18.refs_0_), channel_id=1, source_target_pairs={{0,2},{2,0},{1,3},{3,1},{4,6},{6,4},{5,7},{7,5},{8,10},{10,8},{9,1... | collective-permute-start | bytes 393224 | tf_op jit(solution)/shard_map/ppermute | solution.py:211
  4.2 1.6 %collective-permute-start.3 = (bf16[1,32,128]{2,1,0:T(8,128)(2,1)S(1)}, bf16[1,32,128]{2,1,0:T(8,128)(2,1)S(1)}, u32[]{:S(2)}, u32[]{:S(2)}) collective-permute-start(bf16[1,32,128]{2,1,0:T(8,128)(2,1)S(1)} %get-tuple-element.19), channel_id=1, source_target_pairs={{0,4},{4,8},{8,12},{12,0},{1,5},{5,9},{9,13},{13,1},{2,6},{6,10},{... | collective-permute-start | bytes 24584 | tf_op jit(solution)/shard_map/ppermute | solution.py:211
  5.7 0.0 collective-permute-start
  5.7 2.2 %collective-permute-start.4 = (bf16[1,32,128]{2,1,0:T(8,128)(2,1)S(1)}, bf16[1,32,128]{2,1,0:T(8,128)(2,1)S(1)}, u32[]{:S(2)}, u32[]{:S(2)}) collective-permute-start(bf16[1,32,128]{2,1,0:T(8,128)(2,1)S(1)} %get-tuple-element.20), channel_id=1, source_target_pairs={{0,12},{4,0},{8,4},{12,8},{1,13},{5,1},{9,5},{13,9},{2,14},{6,2},{... | collective-permute-start | bytes 24584 | tf_op jit(solution)/shard_map/ppermute | solution.py:211
  8.0 0.0 copy-done.1
  8.0 0.0 copy-done.2
  8.0 0.0 copy-done.3
  8.0 0.6 shard_map.57
  8.6 0.0 collective-permute-done.1.refs_2_
  8.6 0.3 collective-permute-start.2
  8.9 0.7 collective-permute-done.3
  9.6 0.0 collective-permute-done.4
  9.6 0.1 collective-permute-start.7
  9.7 1.2 %collective-permute-start.6 = (bf16[2,32,128]{2,1,0:T(8,128)(2,1)S(1)}, bf16[2,32,128]{2,1,0:T(8,128)(2,1)S(1)}, u32[]{:S(2)}, u32[]{:S(2)}) collective-permute-start(bf16[2,32,128]{2,1,0:T(8,128)(2,1)S(1)} %constant_dynamic-update-slice_fusion.refs_0_), channel_id=1, source_target_pairs={{0,2},{1,3},{2,0},{3,1},{4,6},{5,7},{6,4},{7,5},{8,10},{9,11},{10,... | collective-permute-start | bytes 49160 | tf_op jit(solution)/shard_map/ppermute | solution.py:230
  10.9 0.6 collective-permute-start.5
  11.6 0.0 collective-permute-done.refs_1_
  11.6 0.0 collective-permute-done.2.refs_3_
  11.6 0.0 copy-start
  11.6 2.4 %shard_map.58 = (bf16[384,768]{1,0:T(8,128)(2,1)S(1)}, bf16[4,128,128]{2,1,0:T(8,128)(2,1)S(1)}, bf16[4,128,128]{2,1,0:T(8,128)(2,1)S(1)}) custom-call(bf16[16,128,128]{2,1,0:T(8,128)(2,1)S(1)} %shard_map.56.field_ref, bf16[256,768]{1,0:T(8,128)(2,1)S(1)} %get-tuple-element.21.taps_one_ref.refs_6_, ...), custom_call_target="tpu_custom_call" | custom-call | flops 1635778560 | bytes 524288 | tf_op jit(solution)/shard_map/pallas_call | solution.py:198
  14.0 0.0 collective-permute-done.7.refs_3_
  14.0 0.0 collective-permute-done.6.refs_2_
  14.0 0.0 collective-permute-done.5.refs_1_
  14.0 1.2 %shard_map.59.tokens_ref = bf16[384,1024]{1,0:T(8,128)(2,1)S(1)} custom-call(bf16[16,128,128]{2,1,0:T(8,128)(2,1)S(1)} %shard_map.56.field_ref, bf16[2,32,128]{2,1,0:T(8,128)(2,1)S(1)} %constant_dynamic-update-slice_fusion.refs_0_, bf16[2,32,128]{2,1,0:T(8,128)(2,1)S(1)} %collective-permute-done.5.refs_1_, ...), custom_call_target="tpu_custom_call" | custom-call | flops 503316480 | bytes 524288 | tf_op jit(solution)/shard_map/pallas_call | solution.py:198
  15.3 0.0 copy-done
  15.3 0.8 %shard_map.62 = bf16[96,2048]{1,0:T(8,128)(2,1)S(1)} custom-call(bf16[384,1024]{1,0:T(8,128)(2,1)S(1)} %shard_map.59.tokens_ref, bf16[1024,4096]{1,0:T(8,128)(2,1)S(1)} %copy-done), custom_call_target="tpu_custom_call" | custom-call | tf_op jit(solution)/shard_map/pallas_call | solution.py:198
  16.1 3.8 %collective-permute-start.11 = (bf16[96,2048]{1,0:T(8,128)(2,1)S(1)}, bf16[96,2048]{1,0:T(8,128)(2,1)S(1)}, u32[]{:S(2)}, u32[]{:S(2)}) collective-permute-start(bf16[96,2048]{1,0:T(8,128)(2,1)S(1)} %shard_map.62), channel_id=1, source_target_pairs={{0,12},{4,0},{8,4},{12,8},{1,13},{5,1},{9,5},{13,9},{2,14},{6,2},{... | collective-permute-start | bytes 1179656 | tf_op jit(solution)/shard_map/ppermute | solution.py:211
  19.9 0.8 %shard_map.60 = bf16[96,2048]{1,0:T(8,128)(2,1)S(1)} custom-call(bf16[384,1024]{1,0:T(8,128)(2,1)S(1)} %shard_map.59.tokens_ref, bf16[1024,4096]{1,0:T(8,128)(2,1)S(1)} %copy-done), custom_call_target="tpu_custom_call" | custom-call | tf_op jit(solution)/shard_map/pallas_call | solution.py:198
  20.7 0.1 collective-permute-start.8
  20.7 8.6 %collective-permute-done.11.arrived_ref = bf16[96,2048]{1,0:T(8,128)(2,1)S(1)} collective-permute-done((bf16[96,2048]{1,0:T(8,128)(2,1)S(1)}, bf16[96,2048]{1,0:T(8,128)(2,1)S(1)}, u32[]{:S(2)}, u32[]{:S(2)}) %collective-permute-start.11) | collective-permute-done | bytes 393248 | tf_op jit(solution)/shard_map/ppermute | solution.py:211
  29.4 1.4 %shard_map.63 = (bf16[96,2048]{1,0:T(8,128)(2,1)S(1)}, f32[192,2048]{1,0:T(8,128)S(1)}) custom-call(bf16[96,2048]{1,0:T(8,128)(2,1)S(1)} %collective-permute-done.11.arrived_ref, bf16[384,1024]{1,0:T(8,128)(2,1)S(1)} %shard_map.59.tokens_ref, bf16[1024,4096]{1,0:T(8,128)(2,1)S(1)} %copy-done), custom_call_target="tpu_custom_call" | custom-call | tf_op jit(solution)/shard_map/pallas_call | solution.py:198
  30.8 4.3 %collective-permute-start.12 = (bf16[96,2048]{1,0:T(8,128)(2,1)S(1)}, bf16[96,2048]{1,0:T(8,128)(2,1)S(1)}, u32[]{:S(2)}, u32[]{:S(2)}) collective-permute-start(bf16[96,2048]{1,0:T(8,128)(2,1)S(1)} %get-tuple-element.29), channel_id=1, source_target_pairs={{0,12},{4,0},{8,4},{12,8},{1,13},{5,1},{9,5},{13,9},{2,14},{6,2},{... | collective-permute-start | bytes 1179656 | tf_op jit(solution)/shard_map/ppermute | solution.py:211
  35.1 2.7 %collective-permute-done.8.arrived_ref = bf16[96,2048]{1,0:T(8,128)(2,1)S(1)} collective-permute-done((bf16[96,2048]{1,0:T(8,128)(2,1)S(1)}, bf16[96,2048]{1,0:T(8,128)(2,1)S(1)}, u32[]{:S(2)}, u32[]{:S(2)}) %collective-permute-start.8) | collective-permute-done | bytes 393248 | tf_op jit(solution)/shard_map/ppermute | solution.py:211
  37.8 1.4 %shard_map.61 = (bf16[96,2048]{1,0:T(8,128)(2,1)S(1)}, f32[192,2048]{1,0:T(8,128)S(1)}) custom-call(bf16[96,2048]{1,0:T(8,128)(2,1)S(1)} %collective-permute-done.8.arrived_ref, bf16[384,1024]{1,0:T(8,128)(2,1)S(1)} %shard_map.59.tokens_ref, bf16[1024,4096]{1,0:T(8,128)(2,1)S(1)} %copy-done), custom_call_target="tpu_custom_call" | custom-call | tf_op jit(solution)/shard_map/pallas_call | solution.py:198
  39.2 4.3 %collective-permute-start.9 = (bf16[96,2048]{1,0:T(8,128)(2,1)S(1)}, bf16[96,2048]{1,0:T(8,128)(2,1)S(1)}, u32[]{:S(2)}, u32[]{:S(2)}) collective-permute-start(bf16[96,2048]{1,0:T(8,128)(2,1)S(1)} %get-tuple-element.27), channel_id=1, source_target_pairs={{0,12},{4,0},{8,4},{12,8},{1,13},{5,1},{9,5},{13,9},{2,14},{6,2},{... | collective-permute-start | bytes 1179656 | tf_op jit(solution)/shard_map/ppermute | solution.py:211
  43.5 2.7 %collective-permute-done.12 = bf16[96,2048]{1,0:T(8,128)(2,1)S(1)} collective-permute-done((bf16[96,2048]{1,0:T(8,128)(2,1)S(1)}, bf16[96,2048]{1,0:T(8,128)(2,1)S(1)}, u32[]{:S(2)}, u32[]{:S(2)}) %collective-permute-start.12) | collective-permute-done | bytes 393248 | tf_op jit(solution)/shard_map/ppermute | solution.py:211
  46.2 0.1 add_convert_fusion
  46.3 4.3 %collective-permute-start.13 = (bf16[96,2048]{1,0:T(8,128)(2,1)S(1)}, bf16[96,2048]{1,0:T(8,128)(2,1)S(1)}, u32[]{:S(2)}, u32[]{:S(2)}) collective-permute-start(bf16[96,2048]{1,0:T(8,128)(2,1)S(1)} %add_convert_fusion), channel_id=1, source_target_pairs={{0,12},{4,0},{8,4},{12,8},{1,13},{5,1},{9,5},{13,9},{2,14},{6,2},{... | collective-permute-start | bytes 1179656 | tf_op jit(solution)/shard_map/ppermute | solution.py:211
  50.6 4.0 %collective-permute-done.9 = bf16[96,2048]{1,0:T(8,128)(2,1)S(1)} collective-permute-done((bf16[96,2048]{1,0:T(8,128)(2,1)S(1)}, bf16[96,2048]{1,0:T(8,128)(2,1)S(1)}, u32[]{:S(2)}, u32[]{:S(2)}) %collective-permute-start.9) | collective-permute-done | bytes 393248 | tf_op jit(solution)/shard_map/ppermute | solution.py:211
  54.6 0.1 add_convert_fusion.1
  54.7 4.3 %collective-permute-start.10 = (bf16[96,2048]{1,0:T(8,128)(2,1)S(1)}, bf16[96,2048]{1,0:T(8,128)(2,1)S(1)}, u32[]{:S(2)}, u32[]{:S(2)}) collective-permute-start(bf16[96,2048]{1,0:T(8,128)(2,1)S(1)} %add_convert_fusion.1), channel_id=1, source_target_pairs={{0,12},{4,0},{8,4},{12,8},{1,13},{5,1},{9,5},{13,9},{2,14},{6,2},{... | collective-permute-start | bytes 1179656 | tf_op jit(solution)/shard_map/ppermute | solution.py:211
  59.1 4.0 %collective-permute-done.13.arrived_ref = bf16[96,2048]{1,0:T(8,128)(2,1)S(1)} collective-permute-done((bf16[96,2048]{1,0:T(8,128)(2,1)S(1)}, bf16[96,2048]{1,0:T(8,128)(2,1)S(1)}, u32[]{:S(2)}, u32[]{:S(2)}) %collective-permute-start.13) | collective-permute-done | bytes 393248 | tf_op jit(solution)/shard_map/ppermute | solution.py:211
  63.1 0.9 %shard_map.64.refs_0_ = bf16[96,4096]{1,0:T(8,128)(2,1)} custom-call(bf16[96,2048]{1,0:T(8,128)(2,1)S(1)} %collective-permute-done.13.arrived_ref, f32[192,2048]{1,0:T(8,128)S(1)} %get-tuple-element.30.kept_ref), custom_call_target="tpu_custom_call" | custom-call | tf_op jit(solution)/shard_map/pallas_call | solution.py:328
  64.0 6.6 %collective-permute-done.10.arrived_ref = bf16[96,2048]{1,0:T(8,128)(2,1)S(1)} collective-permute-done((bf16[96,2048]{1,0:T(8,128)(2,1)S(1)}, bf16[96,2048]{1,0:T(8,128)(2,1)S(1)}, u32[]{:S(2)}, u32[]{:S(2)}) %collective-permute-start.10) | collective-permute-done | bytes 393248 | tf_op jit(solution)/shard_map/ppermute | solution.py:211
  70.6 0.9 %shard_map.65 = bf16[96,4096]{1,0:T(8,128)(2,1)} custom-call(bf16[96,2048]{1,0:T(8,128)(2,1)S(1)} %collective-permute-done.10.arrived_ref, f32[192,2048]{1,0:T(8,128)S(1)} %get-tuple-element.28.kept_ref, bf16[96,4096]{1,0:T(8,128)(2,1)} %shard_map.64.refs_0_), custom_call_target="tpu_custom_call", output_to_operand_aliasing={{}: (2, {})} | custom-call | tf_op jit(solution)/shard_map/pallas_call | solution.py:328
  (5 shorter events, 0.1 us)
Async XLA Ops:
  0.0 1.0 %copy-start.4 = (f32[64,32,32]{0,2,1:T(8,128)S(1)}, f32[64,32,32]{0,2,1:T(8,128)}, u32[]{:S(2)}) copy-start(f32[64,32,32]{0,2,1:T(8,128)} %param.5) | copy-start | bytes 786436
  1.0 6.9 %copy-start.1 = (f32[9,64,64]{2,1,0:T(8,128)S(1)}, f32[9,64,64]{2,1,0:T(8,128)}, u32[]{:S(2)}) copy-start(f32[9,64,64]{2,1,0:T(8,128)} %first_ref.1) | copy-start | bytes 442372
  1.0 6.9 %copy-start.2 = (f32[9,64,64]{2,1,0:T(8,128)S(1)}, f32[9,64,64]{2,1,0:T(8,128)}, u32[]{:S(2)}) copy-start(f32[9,64,64]{2,1,0:T(8,128)} %second_ref.1) | copy-start | bytes 442372
  1.0 7.0 %copy-start.3 = (bf16[256,384]{1,0:T(8,128)(2,1)S(1)}, bf16[256,384]{1,0:T(8,128)(2,1)}, u32[]{:S(2)}) copy-start(bf16[256,384]{1,0:T(8,128)(2,1)} %embed_ref.1) | copy-start | bytes 589828
  1.2 7.4 %collective-permute-start.1 = (bf16[16,32,128]{2,1,0:T(8,128)(2,1)S(1)}, bf16[16,32,128]{2,1,0:T(8,128)(2,1)S(1)}, u32[]{:S(2)}, u32[]{:S(2)}) collective-permute-start(bf16[16,32,128]{2,1,0:T(8,128)(2,1)S(1)} %get-tuple-element.18.refs_0_), channel_id=1, source_target_pairs={{0,2},{2,0},{1,3},{3,1},{4,6},{6,4},{5,7},{7,5},{8,10},{10,8},{9,1... | collective-permute-start | bytes 393224 | tf_op jit(solution)/shard_map/ppermute | solution.py:211
  4.2 5.4 %collective-permute-start.3 = (bf16[1,32,128]{2,1,0:T(8,128)(2,1)S(1)}, bf16[1,32,128]{2,1,0:T(8,128)(2,1)S(1)}, u32[]{:S(2)}, u32[]{:S(2)}) collective-permute-start(bf16[1,32,128]{2,1,0:T(8,128)(2,1)S(1)} %get-tuple-element.19), channel_id=1, source_target_pairs={{0,4},{4,8},{8,12},{12,0},{1,5},{5,9},{9,13},{13,1},{2,6},{6,10},{... | collective-permute-start | bytes 24584 | tf_op jit(solution)/shard_map/ppermute | solution.py:211
  5.7 5.8 %collective-permute-start = (bf16[16,32,128]{2,1,0:T(8,128)(2,1)S(1)}, bf16[16,32,128]{2,1,0:T(8,128)(2,1)S(1)}, u32[]{:S(2)}, u32[]{:S(2)}) collective-permute-start(bf16[16,32,128]{2,1,0:T(8,128)(2,1)S(1)} %get-tuple-element.18.refs_0_), channel_id=1, source_target_pairs={{0,1},{1,0},{2,3},{3,2},{4,5},{5,4},{6,7},{7,6},{8,9},{9,8},{10,11... | collective-permute-start | bytes 393224 | tf_op jit(solution)/shard_map/ppermute | solution.py:211
  5.7 3.9 %collective-permute-start.4 = (bf16[1,32,128]{2,1,0:T(8,128)(2,1)S(1)}, bf16[1,32,128]{2,1,0:T(8,128)(2,1)S(1)}, u32[]{:S(2)}, u32[]{:S(2)}) collective-permute-start(bf16[1,32,128]{2,1,0:T(8,128)(2,1)S(1)} %get-tuple-element.20), channel_id=1, source_target_pairs={{0,12},{4,0},{8,4},{12,8},{1,13},{5,1},{9,5},{13,9},{2,14},{6,2},{... | collective-permute-start | bytes 24584 | tf_op jit(solution)/shard_map/ppermute | solution.py:211
  8.6 3.0 %collective-permute-start.2 = (bf16[16,32,128]{2,1,0:T(8,128)(2,1)S(1)}, bf16[16,32,128]{2,1,0:T(8,128)(2,1)S(1)}, u32[]{:S(2)}, u32[]{:S(2)}) collective-permute-start(bf16[16,32,128]{2,1,0:T(8,128)(2,1)S(1)} %collective-permute-done.1.refs_2_), channel_id=1, source_target_pairs={{0,1},{1,0},{2,3},{3,2},{4,5},{5,4},{6,7},{7,6},{8,9},{9,8},{10,11... | collective-permute-start | bytes 393224 | tf_op jit(solution)/shard_map/ppermute | solution.py:211
  9.6 4.4 %collective-permute-start.7 = (bf16[2,32,128]{2,1,0:T(8,128)(2,1)S(1)}, bf16[2,32,128]{2,1,0:T(8,128)(2,1)S(1)}, u32[]{:S(2)}, u32[]{:S(2)}) collective-permute-start(bf16[2,32,128]{2,1,0:T(8,128)(2,1)S(1)} %constant_dynamic-update-slice_fusion.refs_0_), channel_id=1, source_target_pairs={{0,3},{1,2},{2,1},{3,0},{4,7},{5,6},{6,5},{7,4},{8,11},{9,10},{10,... | collective-permute-start | bytes 49160 | tf_op jit(solution)/shard_map/ppermute | solution.py:230
  9.7 4.3 %collective-permute-start.6 = (bf16[2,32,128]{2,1,0:T(8,128)(2,1)S(1)}, bf16[2,32,128]{2,1,0:T(8,128)(2,1)S(1)}, u32[]{:S(2)}, u32[]{:S(2)}) collective-permute-start(bf16[2,32,128]{2,1,0:T(8,128)(2,1)S(1)} %constant_dynamic-update-slice_fusion.refs_0_), channel_id=1, source_target_pairs={{0,2},{1,3},{2,0},{3,1},{4,6},{5,7},{6,4},{7,5},{8,10},{9,11},{10,... | collective-permute-start | bytes 49160 | tf_op jit(solution)/shard_map/ppermute | solution.py:230
  10.9 3.1 %collective-permute-start.5 = (bf16[2,32,128]{2,1,0:T(8,128)(2,1)S(1)}, bf16[2,32,128]{2,1,0:T(8,128)(2,1)S(1)}, u32[]{:S(2)}, u32[]{:S(2)}) collective-permute-start(bf16[2,32,128]{2,1,0:T(8,128)(2,1)S(1)} %constant_dynamic-update-slice_fusion.refs_0_), channel_id=1, source_target_pairs={{0,1},{1,0},{2,3},{3,2},{4,5},{5,4},{6,7},{7,6},{8,9},{9,8},{10,11... | collective-permute-start | bytes 49160 | tf_op jit(solution)/shard_map/ppermute | solution.py:230
  11.6 3.6 %copy-start = (bf16[1024,4096]{1,0:T(8,128)(2,1)S(1)}, bf16[1024,4096]{1,0:T(8,128)(2,1)}, u32[]{:S(2)}) copy-start(bf16[1024,4096]{1,0:T(8,128)(2,1)} %mixing_ref.7) | copy-start | bytes 25165828
  16.1 13.3 %collective-permute-start.11 = (bf16[96,2048]{1,0:T(8,128)(2,1)S(1)}, bf16[96,2048]{1,0:T(8,128)(2,1)S(1)}, u32[]{:S(2)}, u32[]{:S(2)}) collective-permute-start(bf16[96,2048]{1,0:T(8,128)(2,1)S(1)} %shard_map.62), channel_id=1, source_target_pairs={{0,12},{4,0},{8,4},{12,8},{1,13},{5,1},{9,5},{13,9},{2,14},{6,2},{... | collective-permute-start | bytes 1179656 | tf_op jit(solution)/shard_map/ppermute | solution.py:211
  20.7 17.1 %collective-permute-start.8 = (bf16[96,2048]{1,0:T(8,128)(2,1)S(1)}, bf16[96,2048]{1,0:T(8,128)(2,1)S(1)}, u32[]{:S(2)}, u32[]{:S(2)}) collective-permute-start(bf16[96,2048]{1,0:T(8,128)(2,1)S(1)} %shard_map.60), channel_id=1, source_target_pairs={{0,12},{4,0},{8,4},{12,8},{1,13},{5,1},{9,5},{13,9},{2,14},{6,2},{... | collective-permute-start | bytes 1179656 | tf_op jit(solution)/shard_map/ppermute | solution.py:211
  30.8 15.5 %collective-permute-start.12 = (bf16[96,2048]{1,0:T(8,128)(2,1)S(1)}, bf16[96,2048]{1,0:T(8,128)(2,1)S(1)}, u32[]{:S(2)}, u32[]{:S(2)}) collective-permute-start(bf16[96,2048]{1,0:T(8,128)(2,1)S(1)} %get-tuple-element.29), channel_id=1, source_target_pairs={{0,12},{4,0},{8,4},{12,8},{1,13},{5,1},{9,5},{13,9},{2,14},{6,2},{... | collective-permute-start | bytes 1179656 | tf_op jit(solution)/shard_map/ppermute | solution.py:211
  39.2 15.5 %collective-permute-start.9 = (bf16[96,2048]{1,0:T(8,128)(2,1)S(1)}, bf16[96,2048]{1,0:T(8,128)(2,1)S(1)}, u32[]{:S(2)}, u32[]{:S(2)}) collective-permute-start(bf16[96,2048]{1,0:T(8,128)(2,1)S(1)} %get-tuple-element.27), channel_id=1, source_target_pairs={{0,12},{4,0},{8,4},{12,8},{1,13},{5,1},{9,5},{13,9},{2,14},{6,2},{... | collective-permute-start | bytes 1179656 | tf_op jit(solution)/shard_map/ppermute | solution.py:211
  46.3 16.8 %collective-permute-start.13 = (bf16[96,2048]{1,0:T(8,128)(2,1)S(1)}, bf16[96,2048]{1,0:T(8,128)(2,1)S(1)}, u32[]{:S(2)}, u32[]{:S(2)}) collective-permute-start(bf16[96,2048]{1,0:T(8,128)(2,1)S(1)} %add_convert_fusion), channel_id=1, source_target_pairs={{0,12},{4,0},{8,4},{12,8},{1,13},{5,1},{9,5},{13,9},{2,14},{6,2},{... | collective-permute-start | bytes 1179656 | tf_op jit(solution)/shard_map/ppermute | solution.py:211
  54.7 15.8 %collective-permute-start.10 = (bf16[96,2048]{1,0:T(8,128)(2,1)S(1)}, bf16[96,2048]{1,0:T(8,128)(2,1)S(1)}, u32[]{:S(2)}, u32[]{:S(2)}) collective-permute-start(bf16[96,2048]{1,0:T(8,128)(2,1)S(1)} %add_convert_fusion.1), channel_id=1, source_target_pairs={{0,12},{4,0},{8,4},{12,8},{1,13},{5,1},{9,5},{13,9},{2,14},{6,2},{... | collective-permute-start | bytes 1179656 | tf_op jit(solution)/shard_map/ppermute | solution.py:211

commit v21 on v18

--- a/solution.py
+++ b/solution.py
@@ -13,7 +13,7 @@
 PACK_COST = 20 * 10**9
 WRITES = 4
 VMEM_BYTES = 24 * 1024 * 1024
-ROWS_AT_ONCE = 1024
+ROWS_AT_ONCE = 2048
 
 
 def pack_kernel(field_ref, packed_ref, low_ref, high_ref):

time: 71.6 us -> 71.9 us (level)
  no operation moved by 1% of the time
where the time goes in v21:
time: 71.9 us; the launch traced here: 71.7 us
  starting transfers between devices  44.8 us (62%)
  waiting for transfers between devices  12.8 us (18%)
  Pallas kernels  12.6 us (18%)
  local copies, waits for them, and re-layouts  1.22 us (2%)
    ppermute x17, starting transfers between devices, turned(): lax.ppermute(value, axis, [(i, (i + away) % count) for i in range(count)])  42.9 us
    ppermute x17, waiting for transfers between devices, turned(): lax.ppermute(value, axis, [(i, (i + away) % count) for i in range(count)])  12.8 us
    pallas_call x13, Pallas kernels, call(): pl.pallas_call(kernel, out_shape=out_shape, in_specs=[pl.BlockSpec(memory...  9.59 us
    pallas_call x4, Pallas kernels, finish(): pl.pallas_call(functools.partial(last_kernel, first), out_shape=jax.Shape...  3.03 us
    ppermute x3, starting transfers between devices, direct_blocks(): blocks.append(lax.ppermute(block, ('ch', 'sub'), route))  1.93 us
  transfers between devices with their start and end apart: 20, of which 5 were waited for; matrix products, arithmetic and copies ran while one was open for 0% of the time, Pallas kernels for 14%

profile of v21, /device:TPU:0, one launch (start us, length us, event | category | flops | bytes accessed | tf_op | source)
XLA Modules:
  0.0 71.7 jit_solution(1634113073880269976)
XLA Ops:
  0.0 1.2 %copy-done.3 = f32[64,32,32]{0,2,1:T(8,128)S(1)} copy-done((f32[64,32,32]{0,2,1:T(8,128)S(1)}, f32[64,32,32]{0,2,1:T(8,128)}, u32[]{:S(2)}) %copy-start.3) | copy-done | bytes 262168
  1.2 0.1 shard_map.55
  1.3 3.0 %collective-permute-start.1 = (bf16[16,32,128]{2,1,0:T(8,128)(2,1)S(1)}, bf16[16,32,128]{2,1,0:T(8,128)(2,1)S(1)}, u32[]{:S(2)}, u32[]{:S(2)}) collective-permute-start(bf16[16,32,128]{2,1,0:T(8,128)(2,1)S(1)} %get-tuple-element.22.refs_0_), channel_id=1, source_target_pairs={{0,2},{2,0},{1,3},{3,1},{4,6},{6,4},{5,7},{7,5},{8,10},{10,8},{9,1... | collective-permute-start | bytes 393224 | tf_op jit(solution)/shard_map/ppermute | solution.py:211
  4.3 1.6 %collective-permute-start.3 = (bf16[1,32,128]{2,1,0:T(8,128)(2,1)S(1)}, bf16[1,32,128]{2,1,0:T(8,128)(2,1)S(1)}, u32[]{:S(2)}, u32[]{:S(2)}) collective-permute-start(bf16[1,32,128]{2,1,0:T(8,128)(2,1)S(1)} %get-tuple-element.23), channel_id=1, source_target_pairs={{0,4},{4,8},{8,12},{12,0},{1,5},{5,9},{9,13},{13,1},{2,6},{6,10},{... | collective-permute-start | bytes 24584 | tf_op jit(solution)/shard_map/ppermute | solution.py:211
  5.9 0.0 collective-permute-start
  5.9 2.2 %collective-permute-start.4 = (bf16[1,32,128]{2,1,0:T(8,128)(2,1)S(1)}, bf16[1,32,128]{2,1,0:T(8,128)(2,1)S(1)}, u32[]{:S(2)}, u32[]{:S(2)}) collective-permute-start(bf16[1,32,128]{2,1,0:T(8,128)(2,1)S(1)} %get-tuple-element.24), channel_id=1, source_target_pairs={{0,12},{4,0},{8,4},{12,8},{1,13},{5,1},{9,5},{13,9},{2,14},{6,2},{... | collective-permute-start | bytes 24584 | tf_op jit(solution)/shard_map/ppermute | solution.py:211
  8.2 0.6 shard_map.57
  8.8 0.0 collective-permute-done.1.refs_2_
  8.8 0.3 collective-permute-start.2
  9.1 0.7 collective-permute-done.3
  9.8 0.1 collective-permute-start.5
  9.9 0.4 collective-permute-start.6
  10.2 1.5 %collective-permute-start.7 = (bf16[2,32,128]{2,1,0:T(8,128)(2,1)S(1)}, bf16[2,32,128]{2,1,0:T(8,128)(2,1)S(1)}, u32[]{:S(2)}, u32[]{:S(2)}) collective-permute-start(bf16[2,32,128]{2,1,0:T(8,128)(2,1)S(1)} %constant_dynamic-update-slice_fusion.refs_0_), channel_id=1, source_target_pairs={{0,3},{1,2},{2,1},{3,0},{4,7},{5,6},{6,5},{7,4},{8,11},{9,10},{10,... | collective-permute-start | bytes 49160 | tf_op jit(solution)/shard_map/ppermute | solution.py:230
  11.7 0.0 collective-permute-done.refs_1_
  11.8 2.7 %shard_map.58 = (bf16[384,768]{1,0:T(8,128)(2,1)S(1)}, bf16[4,128,128]{2,1,0:T(8,128)(2,1)S(1)}, bf16[4,128,128]{2,1,0:T(8,128)(2,1)S(1)}) custom-call(bf16[16,128,128]{2,1,0:T(8,128)(2,1)S(1)} %shard_map.56.field_ref, bf16[256,768]{1,0:T(8,128)(2,1)S(1)} %get-tuple-element.25.taps_one_ref.refs_6_, ...), custom_call_target="tpu_custom_call" | custom-call | flops 1635778560 | bytes 524288 | tf_op jit(solution)/shard_map/pallas_call | solution.py:198
  14.5 0.0 collective-permute-done.5.refs_1_
  14.5 0.0 collective-permute-done.7.refs_3_
  14.5 1.2 %shard_map.59.tokens_ref = bf16[384,1024]{1,0:T(8,128)(2,1)S(1)} custom-call(bf16[16,128,128]{2,1,0:T(8,128)(2,1)S(1)} %shard_map.56.field_ref, bf16[2,32,128]{2,1,0:T(8,128)(2,1)S(1)} %constant_dynamic-update-slice_fusion.refs_0_, bf16[2,32,128]{2,1,0:T(8,128)(2,1)S(1)} %collective-permute-done.5.refs_1_, ...), custom_call_target="tpu_custom_call" | custom-call | flops 503316480 | bytes 524288 | tf_op jit(solution)/shard_map/pallas_call | solution.py:198
  15.8 0.5 shard_map.66
  16.2 3.8 %collective-permute-start.17 = (bf16[96,1024]{1,0:T(8,128)(2,1)S(1)}, bf16[96,1024]{1,0:T(8,128)(2,1)S(1)}, u32[]{:S(2)}, u32[]{:S(2)}) collective-permute-start(bf16[96,1024]{1,0:T(8,128)(2,1)S(1)} %shard_map.66), channel_id=1, source_target_pairs={{0,12},{4,0},{8,4},{12,8},{1,13},{5,1},{9,5},{13,9},{2,14},{6,2},{... | collective-permute-start | bytes 589832 | tf_op jit(solution)/shard_map/ppermute | solution.py:211
  20.0 0.5 shard_map.64
  20.5 0.1 collective-permute-start.14
  20.6 0.5 shard_map.62
  21.0 0.5 collective-permute-start.11
  21.5 0.5 shard_map.60
  22.0 0.8 %collective-permute-start.8 = (bf16[96,1024]{1,0:T(8,128)(2,1)S(1)}, bf16[96,1024]{1,0:T(8,128)(2,1)S(1)}, u32[]{:S(2)}, u32[]{:S(2)}) collective-permute-start(bf16[96,1024]{1,0:T(8,128)(2,1)S(1)} %shard_map.60), channel_id=1, source_target_pairs={{0,12},{4,0},{8,4},{12,8},{1,13},{5,1},{9,5},{13,9},{2,14},{6,2},{... | collective-permute-start | bytes 589832 | tf_op jit(solution)/shard_map/ppermute | solution.py:211
  22.8 2.5 %collective-permute-done.17.arrived_ref = bf16[96,1024]{1,0:T(8,128)(2,1)S(1)} collective-permute-done((bf16[96,1024]{1,0:T(8,128)(2,1)S(1)}, bf16[96,1024]{1,0:T(8,128)(2,1)S(1)}, u32[]{:S(2)}, u32[]{:S(2)}) %collective-permute-start.17) | collective-permute-done | bytes 196640 | tf_op jit(solution)/shard_map/ppermute | solution.py:211
  25.3 0.8 %shard_map.67 = (bf16[96,1024]{1,0:T(8,128)(2,1)S(1)}, f32[192,1024]{1,0:T(8,128)S(1)}) custom-call(bf16[96,1024]{1,0:T(8,128)(2,1)S(1)} %collective-permute-done.17.arrived_ref, bf16[384,1024]{1,0:T(8,128)(2,1)S(1)} %shard_map.59.tokens_ref, bf16[1024,4096]{1,0:T(8,128)(2,1)S(1)} %bitcast.2), custom_call_target="tpu_custom_call" | custom-call | tf_op jit(solution)/shard_map/pallas_call | solution.py:198
  26.1 4.3 %collective-permute-start.18 = (bf16[96,1024]{1,0:T(8,128)(2,1)S(1)}, bf16[96,1024]{1,0:T(8,128)(2,1)S(1)}, u32[]{:S(2)}, u32[]{:S(2)}) collective-permute-start(bf16[96,1024]{1,0:T(8,128)(2,1)S(1)} %get-tuple-element.37), channel_id=1, source_target_pairs={{0,12},{4,0},{8,4},{12,8},{1,13},{5,1},{9,5},{13,9},{2,14},{6,2},{... | collective-permute-start | bytes 589832 | tf_op jit(solution)/shard_map/ppermute | solution.py:211
  30.4 0.8 %shard_map.65 = (bf16[96,1024]{1,0:T(8,128)(2,1)S(1)}, f32[192,1024]{1,0:T(8,128)S(1)}) custom-call(bf16[96,1024]{1,0:T(8,128)(2,1)S(1)} %collective-permute-done.14.arrived_ref, bf16[384,1024]{1,0:T(8,128)(2,1)S(1)} %shard_map.59.tokens_ref, bf16[1024,4096]{1,0:T(8,128)(2,1)S(1)} %bitcast.2), custom_call_target="tpu_custom_call" | custom-call | tf_op jit(solution)/shard_map/pallas_call | solution.py:198
  31.2 3.4 %collective-permute-start.15 = (bf16[96,1024]{1,0:T(8,128)(2,1)S(1)}, bf16[96,1024]{1,0:T(8,128)(2,1)S(1)}, u32[]{:S(2)}, u32[]{:S(2)}) collective-permute-start(bf16[96,1024]{1,0:T(8,128)(2,1)S(1)} %get-tuple-element.35), channel_id=1, source_target_pairs={{0,12},{4,0},{8,4},{12,8},{1,13},{5,1},{9,5},{13,9},{2,14},{6,2},{... | collective-permute-start | bytes 589832 | tf_op jit(solution)/shard_map/ppermute | solution.py:211
  34.6 0.8 %shard_map.63 = (bf16[96,1024]{1,0:T(8,128)(2,1)S(1)}, f32[192,1024]{1,0:T(8,128)S(1)}) custom-call(bf16[96,1024]{1,0:T(8,128)(2,1)S(1)} %collective-permute-done.11.arrived_ref, bf16[384,1024]{1,0:T(8,128)(2,1)S(1)} %shard_map.59.tokens_ref, bf16[1024,4096]{1,0:T(8,128)(2,1)S(1)} %bitcast.2), custom_call_target="tpu_custom_call" | custom-call | tf_op jit(solution)/shard_map/pallas_call | solution.py:198
  35.4 3.4 %collective-permute-start.12 = (bf16[96,1024]{1,0:T(8,128)(2,1)S(1)}, bf16[96,1024]{1,0:T(8,128)(2,1)S(1)}, u32[]{:S(2)}, u32[]{:S(2)}) collective-permute-start(bf16[96,1024]{1,0:T(8,128)(2,1)S(1)} %get-tuple-element.33), channel_id=1, source_target_pairs={{0,12},{4,0},{8,4},{12,8},{1,13},{5,1},{9,5},{13,9},{2,14},{6,2},{... | collective-permute-start | bytes 589832 | tf_op jit(solution)/shard_map/ppermute | solution.py:211
  38.8 0.8 %shard_map.61 = (bf16[96,1024]{1,0:T(8,128)(2,1)S(1)}, f32[192,1024]{1,0:T(8,128)S(1)}) custom-call(bf16[96,1024]{1,0:T(8,128)(2,1)S(1)} %collective-permute-done.8.arrived_ref, bf16[384,1024]{1,0:T(8,128)(2,1)S(1)} %shard_map.59.tokens_ref, bf16[1024,4096]{1,0:T(8,128)(2,1)S(1)} %bitcast.2), custom_call_target="tpu_custom_call" | custom-call | tf_op jit(solution)/shard_map/pallas_call | solution.py:198
  39.6 3.4 %collective-permute-start.9 = (bf16[96,1024]{1,0:T(8,128)(2,1)S(1)}, bf16[96,1024]{1,0:T(8,128)(2,1)S(1)}, u32[]{:S(2)}, u32[]{:S(2)}) collective-permute-start(bf16[96,1024]{1,0:T(8,128)(2,1)S(1)} %get-tuple-element.31), channel_id=1, source_target_pairs={{0,12},{4,0},{8,4},{12,8},{1,13},{5,1},{9,5},{13,9},{2,14},{6,2},{... | collective-permute-start | bytes 589832 | tf_op jit(solution)/shard_map/ppermute | solution.py:211
  43.1 3.4 %collective-permute-start.19 = (bf16[96,1024]{1,0:T(8,128)(2,1)S(1)}, bf16[96,1024]{1,0:T(8,128)(2,1)S(1)}, u32[]{:S(2)}, u32[]{:S(2)}) collective-permute-start(bf16[96,1024]{1,0:T(8,128)(2,1)S(1)} %add_convert_fusion), channel_id=1, source_target_pairs={{0,12},{4,0},{8,4},{12,8},{1,13},{5,1},{9,5},{13,9},{2,14},{6,2},{... | collective-permute-start | bytes 589832 | tf_op jit(solution)/shard_map/ppermute | solution.py:211
  46.5 0.0 collective-permute-done.15
  46.6 4.2 %collective-permute-start.16 = (bf16[96,1024]{1,0:T(8,128)(2,1)S(1)}, bf16[96,1024]{1,0:T(8,128)(2,1)S(1)}, u32[]{:S(2)}, u32[]{:S(2)}) collective-permute-start(bf16[96,1024]{1,0:T(8,128)(2,1)S(1)} %add_convert_fusion.1), channel_id=1, source_target_pairs={{0,12},{4,0},{8,4},{12,8},{1,13},{5,1},{9,5},{13,9},{2,14},{6,2},{... | collective-permute-start | bytes 589832 | tf_op jit(solution)/shard_map/ppermute | solution.py:211
  50.7 0.0 collective-permute-done.12
  50.8 4.2 %collective-permute-start.13 = (bf16[96,1024]{1,0:T(8,128)(2,1)S(1)}, bf16[96,1024]{1,0:T(8,128)(2,1)S(1)}, u32[]{:S(2)}, u32[]{:S(2)}) collective-permute-start(bf16[96,1024]{1,0:T(8,128)(2,1)S(1)} %add_convert_fusion.2), channel_id=1, source_target_pairs={{0,12},{4,0},{8,4},{12,8},{1,13},{5,1},{9,5},{13,9},{2,14},{6,2},{... | collective-permute-start | bytes 589832 | tf_op jit(solution)/shard_map/ppermute | solution.py:211
  55.0 4.2 %collective-permute-start.10 = (bf16[96,1024]{1,0:T(8,128)(2,1)S(1)}, bf16[96,1024]{1,0:T(8,128)(2,1)S(1)}, u32[]{:S(2)}, u32[]{:S(2)}) collective-permute-start(bf16[96,1024]{1,0:T(8,128)(2,1)S(1)} %add_convert_fusion.3), channel_id=1, source_target_pairs={{0,12},{4,0},{8,4},{12,8},{1,13},{5,1},{9,5},{13,9},{2,14},{6,2},{... | collective-permute-start | bytes 589832 | tf_op jit(solution)/shard_map/ppermute | solution.py:211
  59.2 0.8 %shard_map.68.refs_0_ = bf16[96,4096]{1,0:T(8,128)(2,1)} custom-call(bf16[96,1024]{1,0:T(8,128)(2,1)S(1)} %collective-permute-done.19.arrived_ref, f32[192,1024]{1,0:T(8,128)S(1)} %get-tuple-element.38.kept_ref), custom_call_target="tpu_custom_call" | custom-call | tf_op jit(solution)/shard_map/pallas_call | solution.py:328
  59.9 3.3 %collective-permute-done.16.arrived_ref = bf16[96,1024]{1,0:T(8,128)(2,1)S(1)} collective-permute-done((bf16[96,1024]{1,0:T(8,128)(2,1)S(1)}, bf16[96,1024]{1,0:T(8,128)(2,1)S(1)}, u32[]{:S(2)}, u32[]{:S(2)}) %collective-permute-start.16) | collective-permute-done | bytes 196640 | tf_op jit(solution)/shard_map/ppermute | solution.py:211
  63.2 0.8 %shard_map.69.refs_0_ = bf16[96,4096]{1,0:T(8,128)(2,1)} custom-call(bf16[96,1024]{1,0:T(8,128)(2,1)S(1)} %collective-permute-done.16.arrived_ref, f32[192,1024]{1,0:T(8,128)S(1)} %get-tuple-element.36.kept_ref, bf16[96,4096]{1,0:T(8,128)(2,1)} %shard_map.68.refs_0_), custom_call_target="tpu_custom_call", output_to_operand_aliasing={{}: (2, {})} | custom-call | tf_op jit(solution)/shard_map/pallas_call | solution.py:328
  64.0 3.4 %collective-permute-done.13.arrived_ref = bf16[96,1024]{1,0:T(8,128)(2,1)S(1)} collective-permute-done((bf16[96,1024]{1,0:T(8,128)(2,1)S(1)}, bf16[96,1024]{1,0:T(8,128)(2,1)S(1)}, u32[]{:S(2)}, u32[]{:S(2)}) %collective-permute-start.13) | collective-permute-done | bytes 196640 | tf_op jit(solution)/shard_map/ppermute | solution.py:211
  67.4 0.8 %shard_map.70.refs_0_ = bf16[96,4096]{1,0:T(8,128)(2,1)} custom-call(bf16[96,1024]{1,0:T(8,128)(2,1)S(1)} %collective-permute-done.13.arrived_ref, f32[192,1024]{1,0:T(8,128)S(1)} %get-tuple-element.34.kept_ref, bf16[96,4096]{1,0:T(8,128)(2,1)} %shard_map.69.refs_0_), custom_call_target="tpu_custom_call", output_to_operand_aliasing={{}: (2, {})} | custom-call | tf_op jit(solution)/shard_map/pallas_call | solution.py:328
  68.2 2.8 %collective-permute-done.10.arrived_ref = bf16[96,1024]{1,0:T(8,128)(2,1)S(1)} collective-permute-done((bf16[96,1024]{1,0:T(8,128)(2,1)S(1)}, bf16[96,1024]{1,0:T(8,128)(2,1)S(1)}, u32[]{:S(2)}, u32[]{:S(2)}) %collective-permute-start.10) | collective-permute-done | bytes 196640 | tf_op jit(solution)/shard_map/ppermute | solution.py:211
  71.0 0.8 %shard_map.71 = bf16[96,4096]{1,0:T(8,128)(2,1)} custom-call(bf16[96,1024]{1,0:T(8,128)(2,1)S(1)} %collective-permute-done.10.arrived_ref, f32[192,1024]{1,0:T(8,128)S(1)} %get-tuple-element.32.kept_ref, bf16[96,4096]{1,0:T(8,128)(2,1)} %shard_map.70.refs_0_), custom_call_target="tpu_custom_call", output_to_operand_aliasing={{}: (2, {})} | custom-call | tf_op jit(solution)/shard_map/pallas_call | solution.py:328
  (28 shorter events, 0.3 us)
Async XLA Ops:
  0.0 15.7 %slice-start = ((s8[8388608]{0:T(1024)(128)(4,1)}), s8[4194304]{0:T(1024)(128)(4,1)S(1)}, s32[]{:S(2)}) async-start(s8[8388608]{0:T(1024)(128)(4,1)} %bitcast.1), calls=%async_computation | async-start | bytes 8388608
  0.0 1.2 %copy-start.3 = (f32[64,32,32]{0,2,1:T(8,128)S(1)}, f32[64,32,32]{0,2,1:T(8,128)}, u32[]{:S(2)}) copy-start(f32[64,32,32]{0,2,1:T(8,128)} %param.5) | copy-start | bytes 786436
  1.2 7.0 %copy-start = (f32[9,64,64]{2,1,0:T(8,128)S(1)}, f32[9,64,64]{2,1,0:T(8,128)}, u32[]{:S(2)}) copy-start(f32[9,64,64]{2,1,0:T(8,128)} %first_ref.1) | copy-start | bytes 442372
  1.2 7.0 %copy-start.1 = (f32[9,64,64]{2,1,0:T(8,128)S(1)}, f32[9,64,64]{2,1,0:T(8,128)}, u32[]{:S(2)}) copy-start(f32[9,64,64]{2,1,0:T(8,128)} %second_ref.1) | copy-start | bytes 442372
  1.2 7.0 %copy-start.2 = (bf16[256,384]{1,0:T(8,128)(2,1)S(1)}, bf16[256,384]{1,0:T(8,128)(2,1)}, u32[]{:S(2)}) copy-start(bf16[256,384]{1,0:T(8,128)(2,1)} %embed_ref.1) | copy-start | bytes 589828
  1.2 14.5 %slice-start.1 = ((s8[8388608]{0:T(1024)(128)(4,1)}), s8[4194304]{0:T(1024)(128)(4,1)S(1)}, s32[]{:S(2)}) async-start(s8[8388608]{0:T(1024)(128)(4,1)} %bitcast.1), calls=%async_computation.1 | async-start | bytes 8388608
  1.3 7.4 %collective-permute-start.1 = (bf16[16,32,128]{2,1,0:T(8,128)(2,1)S(1)}, bf16[16,32,128]{2,1,0:T(8,128)(2,1)S(1)}, u32[]{:S(2)}, u32[]{:S(2)}) collective-permute-start(bf16[16,32,128]{2,1,0:T(8,128)(2,1)S(1)} %get-tuple-element.22.refs_0_), channel_id=1, source_target_pairs={{0,2},{2,0},{1,3},{3,1},{4,6},{6,4},{5,7},{7,5},{8,10},{10,8},{9,1... | collective-permute-start | bytes 393224 | tf_op jit(solution)/shard_map/ppermute | solution.py:211
  4.3 5.4 %collective-permute-start.3 = (bf16[1,32,128]{2,1,0:T(8,128)(2,1)S(1)}, bf16[1,32,128]{2,1,0:T(8,128)(2,1)S(1)}, u32[]{:S(2)}, u32[]{:S(2)}) collective-permute-start(bf16[1,32,128]{2,1,0:T(8,128)(2,1)S(1)} %get-tuple-element.23), channel_id=1, source_target_pairs={{0,4},{4,8},{8,12},{12,0},{1,5},{5,9},{9,13},{13,1},{2,6},{6,10},{... | collective-permute-start | bytes 24584 | tf_op jit(solution)/shard_map/ppermute | solution.py:211
  5.9 5.8 %collective-permute-start = (bf16[16,32,128]{2,1,0:T(8,128)(2,1)S(1)}, bf16[16,32,128]{2,1,0:T(8,128)(2,1)S(1)}, u32[]{:S(2)}, u32[]{:S(2)}) collective-permute-start(bf16[16,32,128]{2,1,0:T(8,128)(2,1)S(1)} %get-tuple-element.22.refs_0_), channel_id=1, source_target_pairs={{0,1},{1,0},{2,3},{3,2},{4,5},{5,4},{6,7},{7,6},{8,9},{9,8},{10,11... | collective-permute-start | bytes 393224 | tf_op jit(solution)/shard_map/ppermute | solution.py:211
  5.9 3.9 %collective-permute-start.4 = (bf16[1,32,128]{2,1,0:T(8,128)(2,1)S(1)}, bf16[1,32,128]{2,1,0:T(8,128)(2,1)S(1)}, u32[]{:S(2)}, u32[]{:S(2)}) collective-permute-start(bf16[1,32,128]{2,1,0:T(8,128)(2,1)S(1)} %get-tuple-element.24), channel_id=1, source_target_pairs={{0,12},{4,0},{8,4},{12,8},{1,13},{5,1},{9,5},{13,9},{2,14},{6,2},{... | collective-permute-start | bytes 24584 | tf_op jit(solution)/shard_map/ppermute | solution.py:211
  8.8 3.0 %collective-permute-start.2 = (bf16[16,32,128]{2,1,0:T(8,128)(2,1)S(1)}, bf16[16,32,128]{2,1,0:T(8,128)(2,1)S(1)}, u32[]{:S(2)}, u32[]{:S(2)}) collective-permute-start(bf16[16,32,128]{2,1,0:T(8,128)(2,1)S(1)} %collective-permute-done.1.refs_2_), channel_id=1, source_target_pairs={{0,1},{1,0},{2,3},{3,2},{4,5},{5,4},{6,7},{7,6},{8,9},{9,8},{10,11... | collective-permute-start | bytes 393224 | tf_op jit(solution)/shard_map/ppermute | solution.py:211
  9.8 4.7 %collective-permute-start.5 = (bf16[2,32,128]{2,1,0:T(8,128)(2,1)S(1)}, bf16[2,32,128]{2,1,0:T(8,128)(2,1)S(1)}, u32[]{:S(2)}, u32[]{:S(2)}) collective-permute-start(bf16[2,32,128]{2,1,0:T(8,128)(2,1)S(1)} %constant_dynamic-update-slice_fusion.refs_0_), channel_id=1, source_target_pairs={{0,1},{1,0},{2,3},{3,2},{4,5},{5,4},{6,7},{7,6},{8,9},{9,8},{10,11... | collective-permute-start | bytes 49160 | tf_op jit(solution)/shard_map/ppermute | solution.py:230
  9.9 4.6 %collective-permute-start.6 = (bf16[2,32,128]{2,1,0:T(8,128)(2,1)S(1)}, bf16[2,32,128]{2,1,0:T(8,128)(2,1)S(1)}, u32[]{:S(2)}, u32[]{:S(2)}) collective-permute-start(bf16[2,32,128]{2,1,0:T(8,128)(2,1)S(1)} %constant_dynamic-update-slice_fusion.refs_0_), channel_id=1, source_target_pairs={{0,2},{1,3},{2,0},{3,1},{4,6},{5,7},{6,4},{7,5},{8,10},{9,11},{10,... | collective-permute-start | bytes 49160 | tf_op jit(solution)/shard_map/ppermute | solution.py:230
  10.2 4.3 %collective-permute-start.7 = (bf16[2,32,128]{2,1,0:T(8,128)(2,1)S(1)}, bf16[2,32,128]{2,1,0:T(8,128)(2,1)S(1)}, u32[]{:S(2)}, u32[]{:S(2)}) collective-permute-start(bf16[2,32,128]{2,1,0:T(8,128)(2,1)S(1)} %constant_dynamic-update-slice_fusion.refs_0_), channel_id=1, source_target_pairs={{0,3},{1,2},{2,1},{3,0},{4,7},{5,6},{6,5},{7,4},{8,11},{9,10},{10,... | collective-permute-start | bytes 49160 | tf_op jit(solution)/shard_map/ppermute | solution.py:230
  16.2 9.1 %collective-permute-start.17 = (bf16[96,1024]{1,0:T(8,128)(2,1)S(1)}, bf16[96,1024]{1,0:T(8,128)(2,1)S(1)}, u32[]{:S(2)}, u32[]{:S(2)}) collective-permute-start(bf16[96,1024]{1,0:T(8,128)(2,1)S(1)} %shard_map.66), channel_id=1, source_target_pairs={{0,12},{4,0},{8,4},{12,8},{1,13},{5,1},{9,5},{13,9},{2,14},{6,2},{... | collective-permute-start | bytes 589832 | tf_op jit(solution)/shard_map/ppermute | solution.py:211
  20.5 9.9 %collective-permute-start.14 = (bf16[96,1024]{1,0:T(8,128)(2,1)S(1)}, bf16[96,1024]{1,0:T(8,128)(2,1)S(1)}, u32[]{:S(2)}, u32[]{:S(2)}) collective-permute-start(bf16[96,1024]{1,0:T(8,128)(2,1)S(1)} %shard_map.64), channel_id=1, source_target_pairs={{0,12},{4,0},{8,4},{12,8},{1,13},{5,1},{9,5},{13,9},{2,14},{6,2},{... | collective-permute-start | bytes 589832 | tf_op jit(solution)/shard_map/ppermute | solution.py:211
  21.0 13.6 %collective-permute-start.11 = (bf16[96,1024]{1,0:T(8,128)(2,1)S(1)}, bf16[96,1024]{1,0:T(8,128)(2,1)S(1)}, u32[]{:S(2)}, u32[]{:S(2)}) collective-permute-start(bf16[96,1024]{1,0:T(8,128)(2,1)S(1)} %shard_map.62), channel_id=1, source_target_pairs={{0,12},{4,0},{8,4},{12,8},{1,13},{5,1},{9,5},{13,9},{2,14},{6,2},{... | collective-permute-start | bytes 589832 | tf_op jit(solution)/shard_map/ppermute | solution.py:211
  22.0 16.8 %collective-permute-start.8 = (bf16[96,1024]{1,0:T(8,128)(2,1)S(1)}, bf16[96,1024]{1,0:T(8,128)(2,1)S(1)}, u32[]{:S(2)}, u32[]{:S(2)}) collective-permute-start(bf16[96,1024]{1,0:T(8,128)(2,1)S(1)} %shard_map.60), channel_id=1, source_target_pairs={{0,12},{4,0},{8,4},{12,8},{1,13},{5,1},{9,5},{13,9},{2,14},{6,2},{... | collective-permute-start | bytes 589832 | tf_op jit(solution)/shard_map/ppermute | solution.py:211
  26.1 17.0 %collective-permute-start.18 = (bf16[96,1024]{1,0:T(8,128)(2,1)S(1)}, bf16[96,1024]{1,0:T(8,128)(2,1)S(1)}, u32[]{:S(2)}, u32[]{:S(2)}) collective-permute-start(bf16[96,1024]{1,0:T(8,128)(2,1)S(1)} %get-tuple-element.37), channel_id=1, source_target_pairs={{0,12},{4,0},{8,4},{12,8},{1,13},{5,1},{9,5},{13,9},{2,14},{6,2},{... | collective-permute-start | bytes 589832 | tf_op jit(solution)/shard_map/ppermute | solution.py:211
  31.2 15.3 %collective-permute-start.15 = (bf16[96,1024]{1,0:T(8,128)(2,1)S(1)}, bf16[96,1024]{1,0:T(8,128)(2,1)S(1)}, u32[]{:S(2)}, u32[]{:S(2)}) collective-permute-start(bf16[96,1024]{1,0:T(8,128)(2,1)S(1)} %get-tuple-element.35), channel_id=1, source_target_pairs={{0,12},{4,0},{8,4},{12,8},{1,13},{5,1},{9,5},{13,9},{2,14},{6,2},{... | collective-permute-start | bytes 589832 | tf_op jit(solution)/shard_map/ppermute | solution.py:211
  35.4 15.3 %collective-permute-start.12 = (bf16[96,1024]{1,0:T(8,128)(2,1)S(1)}, bf16[96,1024]{1,0:T(8,128)(2,1)S(1)}, u32[]{:S(2)}, u32[]{:S(2)}) collective-permute-start(bf16[96,1024]{1,0:T(8,128)(2,1)S(1)} %get-tuple-element.33), channel_id=1, source_target_pairs={{0,12},{4,0},{8,4},{12,8},{1,13},{5,1},{9,5},{13,9},{2,14},{6,2},{... | collective-permute-start | bytes 589832 | tf_op jit(solution)/shard_map/ppermute | solution.py:211
  39.6 15.3 %collective-permute-start.9 = (bf16[96,1024]{1,0:T(8,128)(2,1)S(1)}, bf16[96,1024]{1,0:T(8,128)(2,1)S(1)}, u32[]{:S(2)}, u32[]{:S(2)}) collective-permute-start(bf16[96,1024]{1,0:T(8,128)(2,1)S(1)} %get-tuple-element.31), channel_id=1, source_target_pairs={{0,12},{4,0},{8,4},{12,8},{1,13},{5,1},{9,5},{13,9},{2,14},{6,2},{... | collective-permute-start | bytes 589832 | tf_op jit(solution)/shard_map/ppermute | solution.py:211
  43.1 16.1 %collective-permute-start.19 = (bf16[96,1024]{1,0:T(8,128)(2,1)S(1)}, bf16[96,1024]{1,0:T(8,128)(2,1)S(1)}, u32[]{:S(2)}, u32[]{:S(2)}) collective-permute-start(bf16[96,1024]{1,0:T(8,128)(2,1)S(1)} %add_convert_fusion), channel_id=1, source_target_pairs={{0,12},{4,0},{8,4},{12,8},{1,13},{5,1},{9,5},{13,9},{2,14},{6,2},{... | collective-permute-start | bytes 589832 | tf_op jit(solution)/shard_map/ppermute | solution.py:211
  46.6 16.6 %collective-permute-start.16 = (bf16[96,1024]{1,0:T(8,128)(2,1)S(1)}, bf16[96,1024]{1,0:T(8,128)(2,1)S(1)}, u32[]{:S(2)}, u32[]{:S(2)}) collective-permute-start(bf16[96,1024]{1,0:T(8,128)(2,1)S(1)} %add_convert_fusion.1), channel_id=1, source_target_pairs={{0,12},{4,0},{8,4},{12,8},{1,13},{5,1},{9,5},{13,9},{2,14},{6,2},{... | collective-permute-start | bytes 589832 | tf_op jit(solution)/shard_map/ppermute | solution.py:211
  50.8 16.6 %collective-permute-start.13 = (bf16[96,1024]{1,0:T(8,128)(2,1)S(1)}, bf16[96,1024]{1,0:T(8,128)(2,1)S(1)}, u32[]{:S(2)}, u32[]{:S(2)}) collective-permute-start(bf16[96,1024]{1,0:T(8,128)(2,1)S(1)} %add_convert_fusion.2), channel_id=1, source_target_pairs={{0,12},{4,0},{8,4},{12,8},{1,13},{5,1},{9,5},{13,9},{2,14},{6,2},{... | collective-permute-start | bytes 589832 | tf_op jit(solution)/shard_map/ppermute | solution.py:211
  55.0 16.0 %collective-permute-start.10 = (bf16[96,1024]{1,0:T(8,128)(2,1)S(1)}, bf16[96,1024]{1,0:T(8,128)(2,1)S(1)}, u32[]{:S(2)}, u32[]{:S(2)}) collective-permute-start(bf16[96,1024]{1,0:T(8,128)(2,1)S(1)} %add_convert_fusion.3), channel_id=1, source_target_pairs={{0,12},{4,0},{8,4},{12,8},{1,13},{5,1},{9,5},{13,9},{2,14},{6,2},{... | collective-permute-start | bytes 589832 | tf_op jit(solution)/shard_map/ppermute | solution.py:211

commit v22 on v21

--- a/solution.py
+++ b/solution.py
@@ -13,7 +13,7 @@
 PACK_COST = 20 * 10**9
 WRITES = 4
 VMEM_BYTES = 24 * 1024 * 1024
-ROWS_AT_ONCE = 2048
+ROWS_AT_ONCE = 640
 
 
 def pack_kernel(field_ref, packed_ref, low_ref, high_ref):
@@ -71,14 +71,6 @@
         embed_out_ref[pl.ds(first, LANES), :] = rows.astype(embed_out_ref.dtype)
 
 
-def pairs_at_once(pairs, lat):
-    best = 1
-    for size in range(1, pairs + 1):
-        if pairs % size == 0 and size * lat <= ROWS_AT_ONCE:
-            best = size
-    return best
-
-
 def window(pair_at, pairs):
     rows = []
     for pair in pairs:
@@ -136,8 +128,9 @@
 
 
 def runs(first, last, lat):
-    size = pairs_at_once(last - first, lat)
-    return [list(range(at, at + size)) for at in range(first, last, size)]
+    count = -(-(last - first) * lat // max(ROWS_AT_ONCE, lat))
+    cuts = [first + (last - first) * at // count for at in range(count + 1)]
+    return [list(range(*cut)) for cut in zip(cuts[:-1], cuts[1:])]
 
 
 def inner_kernel(

time: 71.9 us -> 71.5 us (level)
  no operation moved by 1% of the time
where the time goes in v22:
time: 71.5 us; the launch traced here: 71.4 us
  starting transfers between devices  44.8 us (63%)
  waiting for transfers between devices  12.8 us (18%)
  Pallas kernels  12.3 us (17%)
  local copies, waits for them, and re-layouts  1.22 us (2%)
    ppermute x17, starting transfers between devices, turned(): lax.ppermute(value, axis, [(i, (i + away) % count) for i in range(count)])  42.8 us
    ppermute x17, waiting for transfers between devices, turned(): lax.ppermute(value, axis, [(i, (i + away) % count) for i in range(count)])  12.8 us
    pallas_call x13, Pallas kernels, call(): pl.pallas_call(kernel, out_shape=out_shape, in_specs=[pl.BlockSpec(memory...  9.24 us
    pallas_call x4, Pallas kernels, finish(): pl.pallas_call(functools.partial(last_kernel, first), out_shape=jax.Shape...  3.03 us
    ppermute x3, starting transfers between devices, direct_blocks(): blocks.append(lax.ppermute(block, ('ch', 'sub'), route))  1.93 us
  transfers between devices with their start and end apart: 20, of which 5 were waited for; matrix products, arithmetic and copies ran while one was open for 0% of the time, Pallas kernels for 14%

profile of v22, /device:TPU:0, one launch (start us, length us, event | category | flops | bytes accessed | tf_op | source)
XLA Modules:
  0.0 71.4 jit_solution(6399310624790503435)
XLA Ops:
  0.0 1.2 %copy-done.3 = f32[64,32,32]{0,2,1:T(8,128)S(1)} copy-done((f32[64,32,32]{0,2,1:T(8,128)S(1)}, f32[64,32,32]{0,2,1:T(8,128)}, u32[]{:S(2)}) %copy-start.3) | copy-done | bytes 262168
  1.2 0.1 shard_map.55
  1.3 3.0 %collective-permute-start.1 = (bf16[16,32,128]{2,1,0:T(8,128)(2,1)S(1)}, bf16[16,32,128]{2,1,0:T(8,128)(2,1)S(1)}, u32[]{:S(2)}, u32[]{:S(2)}) collective-permute-start(bf16[16,32,128]{2,1,0:T(8,128)(2,1)S(1)} %get-tuple-element.22.refs_0_), channel_id=1, source_target_pairs={{0,2},{2,0},{1,3},{3,1},{4,6},{6,4},{5,7},{7,5},{8,10},{10,8},{9,1... | collective-permute-start | bytes 393224 | tf_op jit(solution)/shard_map/ppermute | solution.py:204
  4.3 1.6 %collective-permute-start.3 = (bf16[1,32,128]{2,1,0:T(8,128)(2,1)S(1)}, bf16[1,32,128]{2,1,0:T(8,128)(2,1)S(1)}, u32[]{:S(2)}, u32[]{:S(2)}) collective-permute-start(bf16[1,32,128]{2,1,0:T(8,128)(2,1)S(1)} %get-tuple-element.23), channel_id=1, source_target_pairs={{0,4},{4,8},{8,12},{12,0},{1,5},{5,9},{9,13},{13,1},{2,6},{6,10},{... | collective-permute-start | bytes 24584 | tf_op jit(solution)/shard_map/ppermute | solution.py:204
  5.9 0.0 collective-permute-start
  5.9 2.2 %collective-permute-start.4 = (bf16[1,32,128]{2,1,0:T(8,128)(2,1)S(1)}, bf16[1,32,128]{2,1,0:T(8,128)(2,1)S(1)}, u32[]{:S(2)}, u32[]{:S(2)}) collective-permute-start(bf16[1,32,128]{2,1,0:T(8,128)(2,1)S(1)} %get-tuple-element.24), channel_id=1, source_target_pairs={{0,12},{4,0},{8,4},{12,8},{1,13},{5,1},{9,5},{13,9},{2,14},{6,2},{... | collective-permute-start | bytes 24584 | tf_op jit(solution)/shard_map/ppermute | solution.py:204
  8.2 0.6 shard_map.57
  8.8 0.0 collective-permute-done.1.refs_2_
  8.8 0.3 collective-permute-start.2
  9.1 0.7 collective-permute-done.3
  9.8 0.0 collective-permute-done.4
  9.8 0.1 collective-permute-start.5
  9.9 0.4 collective-permute-start.6
  10.2 1.5 %collective-permute-start.7 = (bf16[2,32,128]{2,1,0:T(8,128)(2,1)S(1)}, bf16[2,32,128]{2,1,0:T(8,128)(2,1)S(1)}, u32[]{:S(2)}, u32[]{:S(2)}) collective-permute-start(bf16[2,32,128]{2,1,0:T(8,128)(2,1)S(1)} %constant_dynamic-update-slice_fusion.refs_0_), channel_id=1, source_target_pairs={{0,3},{1,2},{2,1},{3,0},{4,7},{5,6},{6,5},{7,4},{8,11},{9,10},{10,... | collective-permute-start | bytes 49160 | tf_op jit(solution)/shard_map/ppermute | solution.py:223
  11.7 0.0 collective-permute-done.2.refs_3_
  11.8 2.4 %shard_map.58 = (bf16[384,768]{1,0:T(8,128)(2,1)S(1)}, bf16[4,128,128]{2,1,0:T(8,128)(2,1)S(1)}, bf16[4,128,128]{2,1,0:T(8,128)(2,1)S(1)}) custom-call(bf16[16,128,128]{2,1,0:T(8,128)(2,1)S(1)} %shard_map.56.field_ref, bf16[256,768]{1,0:T(8,128)(2,1)S(1)} %get-tuple-element.25.taps_one_ref.refs_6_, ...), custom_call_target="tpu_custom_call" | custom-call | flops 1635778560 | bytes 524288 | tf_op jit(solution)/shard_map/pallas_call | solution.py:191
  14.1 0.0 collective-permute-done.5.refs_1_
  14.2 1.2 %shard_map.59.tokens_ref = bf16[384,1024]{1,0:T(8,128)(2,1)S(1)} custom-call(bf16[16,128,128]{2,1,0:T(8,128)(2,1)S(1)} %shard_map.56.field_ref, bf16[2,32,128]{2,1,0:T(8,128)(2,1)S(1)} %constant_dynamic-update-slice_fusion.refs_0_, bf16[2,32,128]{2,1,0:T(8,128)(2,1)S(1)} %collective-permute-done.5.refs_1_, ...), custom_call_target="tpu_custom_call" | custom-call | flops 503316480 | bytes 524288 | tf_op jit(solution)/shard_map/pallas_call | solution.py:191
  15.4 0.5 shard_map.66
  15.9 3.8 %collective-permute-start.17 = (bf16[96,1024]{1,0:T(8,128)(2,1)S(1)}, bf16[96,1024]{1,0:T(8,128)(2,1)S(1)}, u32[]{:S(2)}, u32[]{:S(2)}) collective-permute-start(bf16[96,1024]{1,0:T(8,128)(2,1)S(1)} %shard_map.66), channel_id=1, source_target_pairs={{0,12},{4,0},{8,4},{12,8},{1,13},{5,1},{9,5},{13,9},{2,14},{6,2},{... | collective-permute-start | bytes 589832 | tf_op jit(solution)/shard_map/ppermute | solution.py:204
  19.7 0.5 shard_map.64
  20.1 0.1 collective-permute-start.14
  20.2 0.5 shard_map.62
  20.7 0.5 collective-permute-start.11
  21.2 0.5 shard_map.60
  21.6 0.8 %collective-permute-start.8 = (bf16[96,1024]{1,0:T(8,128)(2,1)S(1)}, bf16[96,1024]{1,0:T(8,128)(2,1)S(1)}, u32[]{:S(2)}, u32[]{:S(2)}) collective-permute-start(bf16[96,1024]{1,0:T(8,128)(2,1)S(1)} %shard_map.60), channel_id=1, source_target_pairs={{0,12},{4,0},{8,4},{12,8},{1,13},{5,1},{9,5},{13,9},{2,14},{6,2},{... | collective-permute-start | bytes 589832 | tf_op jit(solution)/shard_map/ppermute | solution.py:204
  22.5 2.5 %collective-permute-done.17.arrived_ref = bf16[96,1024]{1,0:T(8,128)(2,1)S(1)} collective-permute-done((bf16[96,1024]{1,0:T(8,128)(2,1)S(1)}, bf16[96,1024]{1,0:T(8,128)(2,1)S(1)}, u32[]{:S(2)}, u32[]{:S(2)}) %collective-permute-start.17) | collective-permute-done | bytes 196640 | tf_op jit(solution)/shard_map/ppermute | solution.py:204
  24.9 0.8 %shard_map.67 = (bf16[96,1024]{1,0:T(8,128)(2,1)S(1)}, f32[192,1024]{1,0:T(8,128)S(1)}) custom-call(bf16[96,1024]{1,0:T(8,128)(2,1)S(1)} %collective-permute-done.17.arrived_ref, bf16[384,1024]{1,0:T(8,128)(2,1)S(1)} %shard_map.59.tokens_ref, bf16[1024,4096]{1,0:T(8,128)(2,1)S(1)} %bitcast.2), custom_call_target="tpu_custom_call" | custom-call | tf_op jit(solution)/shard_map/pallas_call | solution.py:191
  25.7 4.3 %collective-permute-start.18 = (bf16[96,1024]{1,0:T(8,128)(2,1)S(1)}, bf16[96,1024]{1,0:T(8,128)(2,1)S(1)}, u32[]{:S(2)}, u32[]{:S(2)}) collective-permute-start(bf16[96,1024]{1,0:T(8,128)(2,1)S(1)} %get-tuple-element.37), channel_id=1, source_target_pairs={{0,12},{4,0},{8,4},{12,8},{1,13},{5,1},{9,5},{13,9},{2,14},{6,2},{... | collective-permute-start | bytes 589832 | tf_op jit(solution)/shard_map/ppermute | solution.py:204
  30.0 0.0 collective-permute-done.14.arrived_ref
  30.0 0.8 %shard_map.65 = (bf16[96,1024]{1,0:T(8,128)(2,1)S(1)}, f32[192,1024]{1,0:T(8,128)S(1)}) custom-call(bf16[96,1024]{1,0:T(8,128)(2,1)S(1)} %collective-permute-done.14.arrived_ref, bf16[384,1024]{1,0:T(8,128)(2,1)S(1)} %shard_map.59.tokens_ref, bf16[1024,4096]{1,0:T(8,128)(2,1)S(1)} %bitcast.2), custom_call_target="tpu_custom_call" | custom-call | tf_op jit(solution)/shard_map/pallas_call | solution.py:191
  30.8 3.4 %collective-permute-start.15 = (bf16[96,1024]{1,0:T(8,128)(2,1)S(1)}, bf16[96,1024]{1,0:T(8,128)(2,1)S(1)}, u32[]{:S(2)}, u32[]{:S(2)}) collective-permute-start(bf16[96,1024]{1,0:T(8,128)(2,1)S(1)} %get-tuple-element.35), channel_id=1, source_target_pairs={{0,12},{4,0},{8,4},{12,8},{1,13},{5,1},{9,5},{13,9},{2,14},{6,2},{... | collective-permute-start | bytes 589832 | tf_op jit(solution)/shard_map/ppermute | solution.py:204
  34.2 0.0 collective-permute-done.11.arrived_ref
  34.2 0.8 %shard_map.63 = (bf16[96,1024]{1,0:T(8,128)(2,1)S(1)}, f32[192,1024]{1,0:T(8,128)S(1)}) custom-call(bf16[96,1024]{1,0:T(8,128)(2,1)S(1)} %collective-permute-done.11.arrived_ref, bf16[384,1024]{1,0:T(8,128)(2,1)S(1)} %shard_map.59.tokens_ref, bf16[1024,4096]{1,0:T(8,128)(2,1)S(1)} %bitcast.2), custom_call_target="tpu_custom_call" | custom-call | tf_op jit(solution)/shard_map/pallas_call | solution.py:191
  35.0 3.4 %collective-permute-start.12 = (bf16[96,1024]{1,0:T(8,128)(2,1)S(1)}, bf16[96,1024]{1,0:T(8,128)(2,1)S(1)}, u32[]{:S(2)}, u32[]{:S(2)}) collective-permute-start(bf16[96,1024]{1,0:T(8,128)(2,1)S(1)} %get-tuple-element.33), channel_id=1, source_target_pairs={{0,12},{4,0},{8,4},{12,8},{1,13},{5,1},{9,5},{13,9},{2,14},{6,2},{... | collective-permute-start | bytes 589832 | tf_op jit(solution)/shard_map/ppermute | solution.py:204
  38.5 0.8 %shard_map.61 = (bf16[96,1024]{1,0:T(8,128)(2,1)S(1)}, f32[192,1024]{1,0:T(8,128)S(1)}) custom-call(bf16[96,1024]{1,0:T(8,128)(2,1)S(1)} %collective-permute-done.8.arrived_ref, bf16[384,1024]{1,0:T(8,128)(2,1)S(1)} %shard_map.59.tokens_ref, bf16[1024,4096]{1,0:T(8,128)(2,1)S(1)} %bitcast.2), custom_call_target="tpu_custom_call" | custom-call | tf_op jit(solution)/shard_map/pallas_call | solution.py:191
  39.2 3.4 %collective-permute-start.9 = (bf16[96,1024]{1,0:T(8,128)(2,1)S(1)}, bf16[96,1024]{1,0:T(8,128)(2,1)S(1)}, u32[]{:S(2)}, u32[]{:S(2)}) collective-permute-start(bf16[96,1024]{1,0:T(8,128)(2,1)S(1)} %get-tuple-element.31), channel_id=1, source_target_pairs={{0,12},{4,0},{8,4},{12,8},{1,13},{5,1},{9,5},{13,9},{2,14},{6,2},{... | collective-permute-start | bytes 589832 | tf_op jit(solution)/shard_map/ppermute | solution.py:204
  42.7 3.4 %collective-permute-start.19 = (bf16[96,1024]{1,0:T(8,128)(2,1)S(1)}, bf16[96,1024]{1,0:T(8,128)(2,1)S(1)}, u32[]{:S(2)}, u32[]{:S(2)}) collective-permute-start(bf16[96,1024]{1,0:T(8,128)(2,1)S(1)} %add_convert_fusion), channel_id=1, source_target_pairs={{0,12},{4,0},{8,4},{12,8},{1,13},{5,1},{9,5},{13,9},{2,14},{6,2},{... | collective-permute-start | bytes 589832 | tf_op jit(solution)/shard_map/ppermute | solution.py:204
  46.2 4.2 %collective-permute-start.16 = (bf16[96,1024]{1,0:T(8,128)(2,1)S(1)}, bf16[96,1024]{1,0:T(8,128)(2,1)S(1)}, u32[]{:S(2)}, u32[]{:S(2)}) collective-permute-start(bf16[96,1024]{1,0:T(8,128)(2,1)S(1)} %add_convert_fusion.1), channel_id=1, source_target_pairs={{0,12},{4,0},{8,4},{12,8},{1,13},{5,1},{9,5},{13,9},{2,14},{6,2},{... | collective-permute-start | bytes 589832 | tf_op jit(solution)/shard_map/ppermute | solution.py:204
  50.4 4.2 %collective-permute-start.13 = (bf16[96,1024]{1,0:T(8,128)(2,1)S(1)}, bf16[96,1024]{1,0:T(8,128)(2,1)S(1)}, u32[]{:S(2)}, u32[]{:S(2)}) collective-permute-start(bf16[96,1024]{1,0:T(8,128)(2,1)S(1)} %add_convert_fusion.2), channel_id=1, source_target_pairs={{0,12},{4,0},{8,4},{12,8},{1,13},{5,1},{9,5},{13,9},{2,14},{6,2},{... | collective-permute-start | bytes 589832 | tf_op jit(solution)/shard_map/ppermute | solution.py:204
  54.6 4.2 %collective-permute-start.10 = (bf16[96,1024]{1,0:T(8,128)(2,1)S(1)}, bf16[96,1024]{1,0:T(8,128)(2,1)S(1)}, u32[]{:S(2)}, u32[]{:S(2)}) collective-permute-start(bf16[96,1024]{1,0:T(8,128)(2,1)S(1)} %add_convert_fusion.3), channel_id=1, source_target_pairs={{0,12},{4,0},{8,4},{12,8},{1,13},{5,1},{9,5},{13,9},{2,14},{6,2},{... | collective-permute-start | bytes 589832 | tf_op jit(solution)/shard_map/ppermute | solution.py:204
  58.8 0.8 %shard_map.68.refs_0_ = bf16[96,4096]{1,0:T(8,128)(2,1)} custom-call(bf16[96,1024]{1,0:T(8,128)(2,1)S(1)} %collective-permute-done.19.arrived_ref, f32[192,1024]{1,0:T(8,128)S(1)} %get-tuple-element.38.kept_ref), custom_call_target="tpu_custom_call" | custom-call | tf_op jit(solution)/shard_map/pallas_call | solution.py:321
  59.6 3.3 %collective-permute-done.16.arrived_ref = bf16[96,1024]{1,0:T(8,128)(2,1)S(1)} collective-permute-done((bf16[96,1024]{1,0:T(8,128)(2,1)S(1)}, bf16[96,1024]{1,0:T(8,128)(2,1)S(1)}, u32[]{:S(2)}, u32[]{:S(2)}) %collective-permute-start.16) | collective-permute-done | bytes 196640 | tf_op jit(solution)/shard_map/ppermute | solution.py:204
  62.8 0.8 %shard_map.69.refs_0_ = bf16[96,4096]{1,0:T(8,128)(2,1)} custom-call(bf16[96,1024]{1,0:T(8,128)(2,1)S(1)} %collective-permute-done.16.arrived_ref, f32[192,1024]{1,0:T(8,128)S(1)} %get-tuple-element.36.kept_ref, bf16[96,4096]{1,0:T(8,128)(2,1)} %shard_map.68.refs_0_), custom_call_target="tpu_custom_call", output_to_operand_aliasing={{}: (2, {})} | custom-call | tf_op jit(solution)/shard_map/pallas_call | solution.py:321
  63.6 3.4 %collective-permute-done.13.arrived_ref = bf16[96,1024]{1,0:T(8,128)(2,1)S(1)} collective-permute-done((bf16[96,1024]{1,0:T(8,128)(2,1)S(1)}, bf16[96,1024]{1,0:T(8,128)(2,1)S(1)}, u32[]{:S(2)}, u32[]{:S(2)}) %collective-permute-start.13) | collective-permute-done | bytes 196640 | tf_op jit(solution)/shard_map/ppermute | solution.py:204
  67.0 0.8 %shard_map.70.refs_0_ = bf16[96,4096]{1,0:T(8,128)(2,1)} custom-call(bf16[96,1024]{1,0:T(8,128)(2,1)S(1)} %collective-permute-done.13.arrived_ref, f32[192,1024]{1,0:T(8,128)S(1)} %get-tuple-element.34.kept_ref, bf16[96,4096]{1,0:T(8,128)(2,1)} %shard_map.69.refs_0_), custom_call_target="tpu_custom_call", output_to_operand_aliasing={{}: (2, {})} | custom-call | tf_op jit(solution)/shard_map/pallas_call | solution.py:321
  67.8 2.8 %collective-permute-done.10.arrived_ref = bf16[96,1024]{1,0:T(8,128)(2,1)S(1)} collective-permute-done((bf16[96,1024]{1,0:T(8,128)(2,1)S(1)}, bf16[96,1024]{1,0:T(8,128)(2,1)S(1)}, u32[]{:S(2)}, u32[]{:S(2)}) %collective-permute-start.10) | collective-permute-done | bytes 196640 | tf_op jit(solution)/shard_map/ppermute | solution.py:204
  70.6 0.8 %shard_map.71 = bf16[96,4096]{1,0:T(8,128)(2,1)} custom-call(bf16[96,1024]{1,0:T(8,128)(2,1)S(1)} %collective-permute-done.10.arrived_ref, f32[192,1024]{1,0:T(8,128)S(1)} %get-tuple-element.32.kept_ref, bf16[96,4096]{1,0:T(8,128)(2,1)} %shard_map.70.refs_0_), custom_call_target="tpu_custom_call", output_to_operand_aliasing={{}: (2, {})} | custom-call | tf_op jit(solution)/shard_map/pallas_call | solution.py:321
  (28 shorter events, 0.3 us)
Async XLA Ops:
  0.0 15.4 %slice-start = ((s8[8388608]{0:T(1024)(128)(4,1)}), s8[4194304]{0:T(1024)(128)(4,1)S(1)}, s32[]{:S(2)}) async-start(s8[8388608]{0:T(1024)(128)(4,1)} %bitcast.1), calls=%async_computation | async-start | bytes 8388608
  0.0 1.2 %copy-start.3 = (f32[64,32,32]{0,2,1:T(8,128)S(1)}, f32[64,32,32]{0,2,1:T(8,128)}, u32[]{:S(2)}) copy-start(f32[64,32,32]{0,2,1:T(8,128)} %param.5) | copy-start | bytes 786436
  1.2 7.0 %copy-start = (f32[9,64,64]{2,1,0:T(8,128)S(1)}, f32[9,64,64]{2,1,0:T(8,128)}, u32[]{:S(2)}) copy-start(f32[9,64,64]{2,1,0:T(8,128)} %first_ref.1) | copy-start | bytes 442372
  1.2 7.0 %copy-start.1 = (f32[9,64,64]{2,1,0:T(8,128)S(1)}, f32[9,64,64]{2,1,0:T(8,128)}, u32[]{:S(2)}) copy-start(f32[9,64,64]{2,1,0:T(8,128)} %second_ref.1) | copy-start | bytes 442372
  1.2 7.0 %copy-start.2 = (bf16[256,384]{1,0:T(8,128)(2,1)S(1)}, bf16[256,384]{1,0:T(8,128)(2,1)}, u32[]{:S(2)}) copy-start(bf16[256,384]{1,0:T(8,128)(2,1)} %embed_ref.1) | copy-start | bytes 589828
  1.2 14.2 %slice-start.1 = ((s8[8388608]{0:T(1024)(128)(4,1)}), s8[4194304]{0:T(1024)(128)(4,1)S(1)}, s32[]{:S(2)}) async-start(s8[8388608]{0:T(1024)(128)(4,1)} %bitcast.1), calls=%async_computation.1 | async-start | bytes 8388608
  1.3 7.4 %collective-permute-start.1 = (bf16[16,32,128]{2,1,0:T(8,128)(2,1)S(1)}, bf16[16,32,128]{2,1,0:T(8,128)(2,1)S(1)}, u32[]{:S(2)}, u32[]{:S(2)}) collective-permute-start(bf16[16,32,128]{2,1,0:T(8,128)(2,1)S(1)} %get-tuple-element.22.refs_0_), channel_id=1, source_target_pairs={{0,2},{2,0},{1,3},{3,1},{4,6},{6,4},{5,7},{7,5},{8,10},{10,8},{9,1... | collective-permute-start | bytes 393224 | tf_op jit(solution)/shard_map/ppermute | solution.py:204
  4.3 5.4 %collective-permute-start.3 = (bf16[1,32,128]{2,1,0:T(8,128)(2,1)S(1)}, bf16[1,32,128]{2,1,0:T(8,128)(2,1)S(1)}, u32[]{:S(2)}, u32[]{:S(2)}) collective-permute-start(bf16[1,32,128]{2,1,0:T(8,128)(2,1)S(1)} %get-tuple-element.23), channel_id=1, source_target_pairs={{0,4},{4,8},{8,12},{12,0},{1,5},{5,9},{9,13},{13,1},{2,6},{6,10},{... | collective-permute-start | bytes 24584 | tf_op jit(solution)/shard_map/ppermute | solution.py:204
  5.9 5.8 %collective-permute-start = (bf16[16,32,128]{2,1,0:T(8,128)(2,1)S(1)}, bf16[16,32,128]{2,1,0:T(8,128)(2,1)S(1)}, u32[]{:S(2)}, u32[]{:S(2)}) collective-permute-start(bf16[16,32,128]{2,1,0:T(8,128)(2,1)S(1)} %get-tuple-element.22.refs_0_), channel_id=1, source_target_pairs={{0,1},{1,0},{2,3},{3,2},{4,5},{5,4},{6,7},{7,6},{8,9},{9,8},{10,11... | collective-permute-start | bytes 393224 | tf_op jit(solution)/shard_map/ppermute | solution.py:204
  5.9 3.9 %collective-permute-start.4 = (bf16[1,32,128]{2,1,0:T(8,128)(2,1)S(1)}, bf16[1,32,128]{2,1,0:T(8,128)(2,1)S(1)}, u32[]{:S(2)}, u32[]{:S(2)}) collective-permute-start(bf16[1,32,128]{2,1,0:T(8,128)(2,1)S(1)} %get-tuple-element.24), channel_id=1, source_target_pairs={{0,12},{4,0},{8,4},{12,8},{1,13},{5,1},{9,5},{13,9},{2,14},{6,2},{... | collective-permute-start | bytes 24584 | tf_op jit(solution)/shard_map/ppermute | solution.py:204
  8.8 3.0 %collective-permute-start.2 = (bf16[16,32,128]{2,1,0:T(8,128)(2,1)S(1)}, bf16[16,32,128]{2,1,0:T(8,128)(2,1)S(1)}, u32[]{:S(2)}, u32[]{:S(2)}) collective-permute-start(bf16[16,32,128]{2,1,0:T(8,128)(2,1)S(1)} %collective-permute-done.1.refs_2_), channel_id=1, source_target_pairs={{0,1},{1,0},{2,3},{3,2},{4,5},{5,4},{6,7},{7,6},{8,9},{9,8},{10,11... | collective-permute-start | bytes 393224 | tf_op jit(solution)/shard_map/ppermute | solution.py:204
  9.8 4.4 %collective-permute-start.5 = (bf16[2,32,128]{2,1,0:T(8,128)(2,1)S(1)}, bf16[2,32,128]{2,1,0:T(8,128)(2,1)S(1)}, u32[]{:S(2)}, u32[]{:S(2)}) collective-permute-start(bf16[2,32,128]{2,1,0:T(8,128)(2,1)S(1)} %constant_dynamic-update-slice_fusion.refs_0_), channel_id=1, source_target_pairs={{0,1},{1,0},{2,3},{3,2},{4,5},{5,4},{6,7},{7,6},{8,9},{9,8},{10,11... | collective-permute-start | bytes 49160 | tf_op jit(solution)/shard_map/ppermute | solution.py:223
  9.9 4.3 %collective-permute-start.6 = (bf16[2,32,128]{2,1,0:T(8,128)(2,1)S(1)}, bf16[2,32,128]{2,1,0:T(8,128)(2,1)S(1)}, u32[]{:S(2)}, u32[]{:S(2)}) collective-permute-start(bf16[2,32,128]{2,1,0:T(8,128)(2,1)S(1)} %constant_dynamic-update-slice_fusion.refs_0_), channel_id=1, source_target_pairs={{0,2},{1,3},{2,0},{3,1},{4,6},{5,7},{6,4},{7,5},{8,10},{9,11},{10,... | collective-permute-start | bytes 49160 | tf_op jit(solution)/shard_map/ppermute | solution.py:223
  10.2 3.9 %collective-permute-start.7 = (bf16[2,32,128]{2,1,0:T(8,128)(2,1)S(1)}, bf16[2,32,128]{2,1,0:T(8,128)(2,1)S(1)}, u32[]{:S(2)}, u32[]{:S(2)}) collective-permute-start(bf16[2,32,128]{2,1,0:T(8,128)(2,1)S(1)} %constant_dynamic-update-slice_fusion.refs_0_), channel_id=1, source_target_pairs={{0,3},{1,2},{2,1},{3,0},{4,7},{5,6},{6,5},{7,4},{8,11},{9,10},{10,... | collective-permute-start | bytes 49160 | tf_op jit(solution)/shard_map/ppermute | solution.py:223
  15.9 9.0 %collective-permute-start.17 = (bf16[96,1024]{1,0:T(8,128)(2,1)S(1)}, bf16[96,1024]{1,0:T(8,128)(2,1)S(1)}, u32[]{:S(2)}, u32[]{:S(2)}) collective-permute-start(bf16[96,1024]{1,0:T(8,128)(2,1)S(1)} %shard_map.66), channel_id=1, source_target_pairs={{0,12},{4,0},{8,4},{12,8},{1,13},{5,1},{9,5},{13,9},{2,14},{6,2},{... | collective-permute-start | bytes 589832 | tf_op jit(solution)/shard_map/ppermute | solution.py:204
  20.1 9.9 %collective-permute-start.14 = (bf16[96,1024]{1,0:T(8,128)(2,1)S(1)}, bf16[96,1024]{1,0:T(8,128)(2,1)S(1)}, u32[]{:S(2)}, u32[]{:S(2)}) collective-permute-start(bf16[96,1024]{1,0:T(8,128)(2,1)S(1)} %shard_map.64), channel_id=1, source_target_pairs={{0,12},{4,0},{8,4},{12,8},{1,13},{5,1},{9,5},{13,9},{2,14},{6,2},{... | collective-permute-start | bytes 589832 | tf_op jit(solution)/shard_map/ppermute | solution.py:204
  20.7 13.6 %collective-permute-start.11 = (bf16[96,1024]{1,0:T(8,128)(2,1)S(1)}, bf16[96,1024]{1,0:T(8,128)(2,1)S(1)}, u32[]{:S(2)}, u32[]{:S(2)}) collective-permute-start(bf16[96,1024]{1,0:T(8,128)(2,1)S(1)} %shard_map.62), channel_id=1, source_target_pairs={{0,12},{4,0},{8,4},{12,8},{1,13},{5,1},{9,5},{13,9},{2,14},{6,2},{... | collective-permute-start | bytes 589832 | tf_op jit(solution)/shard_map/ppermute | solution.py:204
  21.6 16.8 %collective-permute-start.8 = (bf16[96,1024]{1,0:T(8,128)(2,1)S(1)}, bf16[96,1024]{1,0:T(8,128)(2,1)S(1)}, u32[]{:S(2)}, u32[]{:S(2)}) collective-permute-start(bf16[96,1024]{1,0:T(8,128)(2,1)S(1)} %shard_map.60), channel_id=1, source_target_pairs={{0,12},{4,0},{8,4},{12,8},{1,13},{5,1},{9,5},{13,9},{2,14},{6,2},{... | collective-permute-start | bytes 589832 | tf_op jit(solution)/shard_map/ppermute | solution.py:204
  25.7 17.0 %collective-permute-start.18 = (bf16[96,1024]{1,0:T(8,128)(2,1)S(1)}, bf16[96,1024]{1,0:T(8,128)(2,1)S(1)}, u32[]{:S(2)}, u32[]{:S(2)}) collective-permute-start(bf16[96,1024]{1,0:T(8,128)(2,1)S(1)} %get-tuple-element.37), channel_id=1, source_target_pairs={{0,12},{4,0},{8,4},{12,8},{1,13},{5,1},{9,5},{13,9},{2,14},{6,2},{... | collective-permute-start | bytes 589832 | tf_op jit(solution)/shard_map/ppermute | solution.py:204
  30.8 15.3 %collective-permute-start.15 = (bf16[96,1024]{1,0:T(8,128)(2,1)S(1)}, bf16[96,1024]{1,0:T(8,128)(2,1)S(1)}, u32[]{:S(2)}, u32[]{:S(2)}) collective-permute-start(bf16[96,1024]{1,0:T(8,128)(2,1)S(1)} %get-tuple-element.35), channel_id=1, source_target_pairs={{0,12},{4,0},{8,4},{12,8},{1,13},{5,1},{9,5},{13,9},{2,14},{6,2},{... | collective-permute-start | bytes 589832 | tf_op jit(solution)/shard_map/ppermute | solution.py:204
  35.0 15.3 %collective-permute-start.12 = (bf16[96,1024]{1,0:T(8,128)(2,1)S(1)}, bf16[96,1024]{1,0:T(8,128)(2,1)S(1)}, u32[]{:S(2)}, u32[]{:S(2)}) collective-permute-start(bf16[96,1024]{1,0:T(8,128)(2,1)S(1)} %get-tuple-element.33), channel_id=1, source_target_pairs={{0,12},{4,0},{8,4},{12,8},{1,13},{5,1},{9,5},{13,9},{2,14},{6,2},{... | collective-permute-start | bytes 589832 | tf_op jit(solution)/shard_map/ppermute | solution.py:204
  39.2 15.3 %collective-permute-start.9 = (bf16[96,1024]{1,0:T(8,128)(2,1)S(1)}, bf16[96,1024]{1,0:T(8,128)(2,1)S(1)}, u32[]{:S(2)}, u32[]{:S(2)}) collective-permute-start(bf16[96,1024]{1,0:T(8,128)(2,1)S(1)} %get-tuple-element.31), channel_id=1, source_target_pairs={{0,12},{4,0},{8,4},{12,8},{1,13},{5,1},{9,5},{13,9},{2,14},{6,2},{... | collective-permute-start | bytes 589832 | tf_op jit(solution)/shard_map/ppermute | solution.py:204
  42.7 16.1 %collective-permute-start.19 = (bf16[96,1024]{1,0:T(8,128)(2,1)S(1)}, bf16[96,1024]{1,0:T(8,128)(2,1)S(1)}, u32[]{:S(2)}, u32[]{:S(2)}) collective-permute-start(bf16[96,1024]{1,0:T(8,128)(2,1)S(1)} %add_convert_fusion), channel_id=1, source_target_pairs={{0,12},{4,0},{8,4},{12,8},{1,13},{5,1},{9,5},{13,9},{2,14},{6,2},{... | collective-permute-start | bytes 589832 | tf_op jit(solution)/shard_map/ppermute | solution.py:204
  46.2 16.6 %collective-permute-start.16 = (bf16[96,1024]{1,0:T(8,128)(2,1)S(1)}, bf16[96,1024]{1,0:T(8,128)(2,1)S(1)}, u32[]{:S(2)}, u32[]{:S(2)}) collective-permute-start(bf16[96,1024]{1,0:T(8,128)(2,1)S(1)} %add_convert_fusion.1), channel_id=1, source_target_pairs={{0,12},{4,0},{8,4},{12,8},{1,13},{5,1},{9,5},{13,9},{2,14},{6,2},{... | collective-permute-start | bytes 589832 | tf_op jit(solution)/shard_map/ppermute | solution.py:204
  50.4 16.6 %collective-permute-start.13 = (bf16[96,1024]{1,0:T(8,128)(2,1)S(1)}, bf16[96,1024]{1,0:T(8,128)(2,1)S(1)}, u32[]{:S(2)}, u32[]{:S(2)}) collective-permute-start(bf16[96,1024]{1,0:T(8,128)(2,1)S(1)} %add_convert_fusion.2), channel_id=1, source_target_pairs={{0,12},{4,0},{8,4},{12,8},{1,13},{5,1},{9,5},{13,9},{2,14},{6,2},{... | collective-permute-start | bytes 589832 | tf_op jit(solution)/shard_map/ppermute | solution.py:204
  54.6 16.0 %collective-permute-start.10 = (bf16[96,1024]{1,0:T(8,128)(2,1)S(1)}, bf16[96,1024]{1,0:T(8,128)(2,1)S(1)}, u32[]{:S(2)}, u32[]{:S(2)}) collective-permute-start(bf16[96,1024]{1,0:T(8,128)(2,1)S(1)} %add_convert_fusion.3), channel_id=1, source_target_pairs={{0,12},{4,0},{8,4},{12,8},{1,13},{5,1},{9,5},{13,9},{2,14},{6,2},{... | collective-permute-start | bytes 589832 | tf_op jit(solution)/shard_map/ppermute | solution.py:204

commit v23 on v22

--- a/solution.py
+++ b/solution.py
@@ -165,21 +165,22 @@
             return sides_ref[1]
         return field_ref[pair]
 
-    outermost = [-1, 0, pairs - 1, pairs]
+    outermost = [[-1, 0], [pairs - 1, pairs]]
     next_inside = [1, 2, pairs - 3, pairs - 2]
-    upper, lower = first_conv(field_at, outermost, taps_one_ref, lat)
-
-    def hidden_at(found, edge_ref):
+    found = [first_conv(field_at, side, taps_one_ref, lat) for side in outermost]
+
+    def hidden_at(side, part, edge_ref):
         def at(pair):
-            if pair in outermost:
-                return found[outermost.index(pair)]
+            if pair in outermost[side]:
+                return found[side][part][outermost[side].index(pair)]
             return edge_ref[next_inside.index(pair)]
 
         return at
 
-    two_ref[...] = second_conv(
-        hidden_at(upper, upper_edge_ref), hidden_at(lower, lower_edge_ref), [0, 1, pairs - 2, pairs - 1], taps_two_ref, lat
-    )
+    for side, ends in enumerate(([0, 1], [pairs - 2, pairs - 1])):
+        upper_at, lower_at = hidden_at(side, 0, upper_edge_ref), hidden_at(side, 1, lower_edge_ref)
+        two = second_conv(upper_at, lower_at, ends, taps_two_ref, lat)
+        two_ref[pl.ds(side * 2 * lat, 2 * lat), :] = two
     outer = embed_patches(two_ref, embed_ref)
     inner = inner_ref.shape[1]
     tokens_ref[:, :lat] = outer[:, :lat]

time: 71.5 us -> 71.4 us (level)
  no operation moved by 1% of the time
where the time goes in v23:
time: 71.4 us; the launch traced here: 71.3 us
  starting transfers between devices  44.8 us (63%)
  waiting for transfers between devices  12.8 us (18%)
  Pallas kernels  12.2 us (17%)
  local copies, waits for them, and re-layouts  1.22 us (2%)
    ppermute x17, starting transfers between devices, turned(): lax.ppermute(value, axis, [(i, (i + away) % count) for i in range(count)])  42.8 us
    ppermute x17, waiting for transfers between devices, turned(): lax.ppermute(value, axis, [(i, (i + away) % count) for i in range(count)])  12.8 us
    pallas_call x13, Pallas kernels, call(): pl.pallas_call(kernel, out_shape=out_shape, in_specs=[pl.BlockSpec(memory...  9.13 us
    pallas_call x4, Pallas kernels, finish(): pl.pallas_call(functools.partial(last_kernel, first), out_shape=jax.Shape...  3.03 us
    ppermute x3, starting transfers between devices, direct_blocks(): blocks.append(lax.ppermute(block, ('ch', 'sub'), route))  1.93 us
  transfers between devices with their start and end apart: 20, of which 5 were waited for; matrix products, arithmetic and copies ran while one was open for 0% of the time, Pallas kernels for 14%

profile of v23, /device:TPU:0, one launch (start us, length us, event | category | flops | bytes accessed | tf_op | source)
XLA Modules:
  0.0 71.3 jit_solution(8894501719946257848)
XLA Ops:
  0.0 1.2 %copy-done.3 = f32[64,32,32]{0,2,1:T(8,128)S(1)} copy-done((f32[64,32,32]{0,2,1:T(8,128)S(1)}, f32[64,32,32]{0,2,1:T(8,128)}, u32[]{:S(2)}) %copy-start.3) | copy-done | bytes 262168
  1.2 0.1 shard_map.55
  1.3 3.0 %collective-permute-start.1 = (bf16[16,32,128]{2,1,0:T(8,128)(2,1)S(1)}, bf16[16,32,128]{2,1,0:T(8,128)(2,1)S(1)}, u32[]{:S(2)}, u32[]{:S(2)}) collective-permute-start(bf16[16,32,128]{2,1,0:T(8,128)(2,1)S(1)} %get-tuple-element.22.refs_0_), channel_id=1, source_target_pairs={{0,2},{2,0},{1,3},{3,1},{4,6},{6,4},{5,7},{7,5},{8,10},{10,8},{9,1... | collective-permute-start | bytes 393224 | tf_op jit(solution)/shard_map/ppermute | solution.py:205
  4.3 1.6 %collective-permute-start.3 = (bf16[1,32,128]{2,1,0:T(8,128)(2,1)S(1)}, bf16[1,32,128]{2,1,0:T(8,128)(2,1)S(1)}, u32[]{:S(2)}, u32[]{:S(2)}) collective-permute-start(bf16[1,32,128]{2,1,0:T(8,128)(2,1)S(1)} %get-tuple-element.23), channel_id=1, source_target_pairs={{0,4},{4,8},{8,12},{12,0},{1,5},{5,9},{9,13},{13,1},{2,6},{6,10},{... | collective-permute-start | bytes 24584 | tf_op jit(solution)/shard_map/ppermute | solution.py:205
  5.9 0.0 collective-permute-start
  5.9 2.2 %collective-permute-start.4 = (bf16[1,32,128]{2,1,0:T(8,128)(2,1)S(1)}, bf16[1,32,128]{2,1,0:T(8,128)(2,1)S(1)}, u32[]{:S(2)}, u32[]{:S(2)}) collective-permute-start(bf16[1,32,128]{2,1,0:T(8,128)(2,1)S(1)} %get-tuple-element.24), channel_id=1, source_target_pairs={{0,12},{4,0},{8,4},{12,8},{1,13},{5,1},{9,5},{13,9},{2,14},{6,2},{... | collective-permute-start | bytes 24584 | tf_op jit(solution)/shard_map/ppermute | solution.py:205
  8.2 0.6 shard_map.57
  8.8 0.0 collective-permute-done.1.refs_2_
  8.8 0.3 collective-permute-start.2
  9.1 0.7 collective-permute-done.3
  9.8 0.0 collective-permute-done.4
  9.8 0.1 collective-permute-start.5
  9.9 0.4 collective-permute-start.6
  10.2 1.5 %collective-permute-start.7 = (bf16[2,32,128]{2,1,0:T(8,128)(2,1)S(1)}, bf16[2,32,128]{2,1,0:T(8,128)(2,1)S(1)}, u32[]{:S(2)}, u32[]{:S(2)}) collective-permute-start(bf16[2,32,128]{2,1,0:T(8,128)(2,1)S(1)} %constant_dynamic-update-slice_fusion.refs_0_), channel_id=1, source_target_pairs={{0,3},{1,2},{2,1},{3,0},{4,7},{5,6},{6,5},{7,4},{8,11},{9,10},{10,... | collective-permute-start | bytes 49160 | tf_op jit(solution)/shard_map/ppermute | solution.py:224
  11.8 2.4 %shard_map.58 = (bf16[384,768]{1,0:T(8,128)(2,1)S(1)}, bf16[4,128,128]{2,1,0:T(8,128)(2,1)S(1)}, bf16[4,128,128]{2,1,0:T(8,128)(2,1)S(1)}) custom-call(bf16[16,128,128]{2,1,0:T(8,128)(2,1)S(1)} %shard_map.56.field_ref, bf16[256,768]{1,0:T(8,128)(2,1)S(1)} %get-tuple-element.25.taps_one_ref.refs_6_, ...), custom_call_target="tpu_custom_call" | custom-call | flops 1635778560 | bytes 524288 | tf_op jit(solution)/shard_map/pallas_call | solution.py:192
  14.1 0.0 collective-permute-done.5.refs_1_
  14.2 0.0 collective-permute-done.7.refs_3_
  14.2 1.1 %shard_map.59.tokens_ref = bf16[384,1024]{1,0:T(8,128)(2,1)S(1)} custom-call(bf16[16,128,128]{2,1,0:T(8,128)(2,1)S(1)} %shard_map.56.field_ref, bf16[2,32,128]{2,1,0:T(8,128)(2,1)S(1)} %constant_dynamic-update-slice_fusion.refs_0_, bf16[2,32,128]{2,1,0:T(8,128)(2,1)S(1)} %collective-permute-done.5.refs_1_, ...), custom_call_target="tpu_custom_call" | custom-call | flops 503316480 | bytes 524288 | tf_op jit(solution)/shard_map/pallas_call | solution.py:192
  15.3 0.5 shard_map.66
  15.8 3.8 %collective-permute-start.17 = (bf16[96,1024]{1,0:T(8,128)(2,1)S(1)}, bf16[96,1024]{1,0:T(8,128)(2,1)S(1)}, u32[]{:S(2)}, u32[]{:S(2)}) collective-permute-start(bf16[96,1024]{1,0:T(8,128)(2,1)S(1)} %shard_map.66), channel_id=1, source_target_pairs={{0,12},{4,0},{8,4},{12,8},{1,13},{5,1},{9,5},{13,9},{2,14},{6,2},{... | collective-permute-start | bytes 589832 | tf_op jit(solution)/shard_map/ppermute | solution.py:205
  19.6 0.5 shard_map.64
  20.0 0.1 collective-permute-start.14
  20.1 0.5 shard_map.62
  20.6 0.5 collective-permute-start.11
  21.1 0.5 shard_map.60
  21.5 0.8 %collective-permute-start.8 = (bf16[96,1024]{1,0:T(8,128)(2,1)S(1)}, bf16[96,1024]{1,0:T(8,128)(2,1)S(1)}, u32[]{:S(2)}, u32[]{:S(2)}) collective-permute-start(bf16[96,1024]{1,0:T(8,128)(2,1)S(1)} %shard_map.60), channel_id=1, source_target_pairs={{0,12},{4,0},{8,4},{12,8},{1,13},{5,1},{9,5},{13,9},{2,14},{6,2},{... | collective-permute-start | bytes 589832 | tf_op jit(solution)/shard_map/ppermute | solution.py:205
  22.3 2.5 %collective-permute-done.17.arrived_ref = bf16[96,1024]{1,0:T(8,128)(2,1)S(1)} collective-permute-done((bf16[96,1024]{1,0:T(8,128)(2,1)S(1)}, bf16[96,1024]{1,0:T(8,128)(2,1)S(1)}, u32[]{:S(2)}, u32[]{:S(2)}) %collective-permute-start.17) | collective-permute-done | bytes 196640 | tf_op jit(solution)/shard_map/ppermute | solution.py:205
  24.8 0.8 %shard_map.67 = (bf16[96,1024]{1,0:T(8,128)(2,1)S(1)}, f32[192,1024]{1,0:T(8,128)S(1)}) custom-call(bf16[96,1024]{1,0:T(8,128)(2,1)S(1)} %collective-permute-done.17.arrived_ref, bf16[384,1024]{1,0:T(8,128)(2,1)S(1)} %shard_map.59.tokens_ref, bf16[1024,4096]{1,0:T(8,128)(2,1)S(1)} %bitcast.2), custom_call_target="tpu_custom_call" | custom-call | tf_op jit(solution)/shard_map/pallas_call | solution.py:192
  25.6 4.3 %collective-permute-start.18 = (bf16[96,1024]{1,0:T(8,128)(2,1)S(1)}, bf16[96,1024]{1,0:T(8,128)(2,1)S(1)}, u32[]{:S(2)}, u32[]{:S(2)}) collective-permute-start(bf16[96,1024]{1,0:T(8,128)(2,1)S(1)} %get-tuple-element.37), channel_id=1, source_target_pairs={{0,12},{4,0},{8,4},{12,8},{1,13},{5,1},{9,5},{13,9},{2,14},{6,2},{... | collective-permute-start | bytes 589832 | tf_op jit(solution)/shard_map/ppermute | solution.py:205
  29.9 0.8 %shard_map.65 = (bf16[96,1024]{1,0:T(8,128)(2,1)S(1)}, f32[192,1024]{1,0:T(8,128)S(1)}) custom-call(bf16[96,1024]{1,0:T(8,128)(2,1)S(1)} %collective-permute-done.14.arrived_ref, bf16[384,1024]{1,0:T(8,128)(2,1)S(1)} %shard_map.59.tokens_ref, bf16[1024,4096]{1,0:T(8,128)(2,1)S(1)} %bitcast.2), custom_call_target="tpu_custom_call" | custom-call | tf_op jit(solution)/shard_map/pallas_call | solution.py:192
  30.7 3.4 %collective-permute-start.15 = (bf16[96,1024]{1,0:T(8,128)(2,1)S(1)}, bf16[96,1024]{1,0:T(8,128)(2,1)S(1)}, u32[]{:S(2)}, u32[]{:S(2)}) collective-permute-start(bf16[96,1024]{1,0:T(8,128)(2,1)S(1)} %get-tuple-element.35), channel_id=1, source_target_pairs={{0,12},{4,0},{8,4},{12,8},{1,13},{5,1},{9,5},{13,9},{2,14},{6,2},{... | collective-permute-start | bytes 589832 | tf_op jit(solution)/shard_map/ppermute | solution.py:205
  34.1 0.8 %shard_map.63 = (bf16[96,1024]{1,0:T(8,128)(2,1)S(1)}, f32[192,1024]{1,0:T(8,128)S(1)}) custom-call(bf16[96,1024]{1,0:T(8,128)(2,1)S(1)} %collective-permute-done.11.arrived_ref, bf16[384,1024]{1,0:T(8,128)(2,1)S(1)} %shard_map.59.tokens_ref, bf16[1024,4096]{1,0:T(8,128)(2,1)S(1)} %bitcast.2), custom_call_target="tpu_custom_call" | custom-call | tf_op jit(solution)/shard_map/pallas_call | solution.py:192
  34.9 3.4 %collective-permute-start.12 = (bf16[96,1024]{1,0:T(8,128)(2,1)S(1)}, bf16[96,1024]{1,0:T(8,128)(2,1)S(1)}, u32[]{:S(2)}, u32[]{:S(2)}) collective-permute-start(bf16[96,1024]{1,0:T(8,128)(2,1)S(1)} %get-tuple-element.33), channel_id=1, source_target_pairs={{0,12},{4,0},{8,4},{12,8},{1,13},{5,1},{9,5},{13,9},{2,14},{6,2},{... | collective-permute-start | bytes 589832 | tf_op jit(solution)/shard_map/ppermute | solution.py:205
  38.3 0.8 %shard_map.61 = (bf16[96,1024]{1,0:T(8,128)(2,1)S(1)}, f32[192,1024]{1,0:T(8,128)S(1)}) custom-call(bf16[96,1024]{1,0:T(8,128)(2,1)S(1)} %collective-permute-done.8.arrived_ref, bf16[384,1024]{1,0:T(8,128)(2,1)S(1)} %shard_map.59.tokens_ref, bf16[1024,4096]{1,0:T(8,128)(2,1)S(1)} %bitcast.2), custom_call_target="tpu_custom_call" | custom-call | tf_op jit(solution)/shard_map/pallas_call | solution.py:192
  39.1 3.4 %collective-permute-start.9 = (bf16[96,1024]{1,0:T(8,128)(2,1)S(1)}, bf16[96,1024]{1,0:T(8,128)(2,1)S(1)}, u32[]{:S(2)}, u32[]{:S(2)}) collective-permute-start(bf16[96,1024]{1,0:T(8,128)(2,1)S(1)} %get-tuple-element.31), channel_id=1, source_target_pairs={{0,12},{4,0},{8,4},{12,8},{1,13},{5,1},{9,5},{13,9},{2,14},{6,2},{... | collective-permute-start | bytes 589832 | tf_op jit(solution)/shard_map/ppermute | solution.py:205
  42.6 3.4 %collective-permute-start.19 = (bf16[96,1024]{1,0:T(8,128)(2,1)S(1)}, bf16[96,1024]{1,0:T(8,128)(2,1)S(1)}, u32[]{:S(2)}, u32[]{:S(2)}) collective-permute-start(bf16[96,1024]{1,0:T(8,128)(2,1)S(1)} %add_convert_fusion), channel_id=1, source_target_pairs={{0,12},{4,0},{8,4},{12,8},{1,13},{5,1},{9,5},{13,9},{2,14},{6,2},{... | collective-permute-start | bytes 589832 | tf_op jit(solution)/shard_map/ppermute | solution.py:205
  46.0 0.0 collective-permute-done.15
  46.1 4.2 %collective-permute-start.16 = (bf16[96,1024]{1,0:T(8,128)(2,1)S(1)}, bf16[96,1024]{1,0:T(8,128)(2,1)S(1)}, u32[]{:S(2)}, u32[]{:S(2)}) collective-permute-start(bf16[96,1024]{1,0:T(8,128)(2,1)S(1)} %add_convert_fusion.1), channel_id=1, source_target_pairs={{0,12},{4,0},{8,4},{12,8},{1,13},{5,1},{9,5},{13,9},{2,14},{6,2},{... | collective-permute-start | bytes 589832 | tf_op jit(solution)/shard_map/ppermute | solution.py:205
  50.3 0.0 collective-permute-done.12
  50.3 4.2 %collective-permute-start.13 = (bf16[96,1024]{1,0:T(8,128)(2,1)S(1)}, bf16[96,1024]{1,0:T(8,128)(2,1)S(1)}, u32[]{:S(2)}, u32[]{:S(2)}) collective-permute-start(bf16[96,1024]{1,0:T(8,128)(2,1)S(1)} %add_convert_fusion.2), channel_id=1, source_target_pairs={{0,12},{4,0},{8,4},{12,8},{1,13},{5,1},{9,5},{13,9},{2,14},{6,2},{... | collective-permute-start | bytes 589832 | tf_op jit(solution)/shard_map/ppermute | solution.py:205
  54.5 4.2 %collective-permute-start.10 = (bf16[96,1024]{1,0:T(8,128)(2,1)S(1)}, bf16[96,1024]{1,0:T(8,128)(2,1)S(1)}, u32[]{:S(2)}, u32[]{:S(2)}) collective-permute-start(bf16[96,1024]{1,0:T(8,128)(2,1)S(1)} %add_convert_fusion.3), channel_id=1, source_target_pairs={{0,12},{4,0},{8,4},{12,8},{1,13},{5,1},{9,5},{13,9},{2,14},{6,2},{... | collective-permute-start | bytes 589832 | tf_op jit(solution)/shard_map/ppermute | solution.py:205
  58.7 0.8 %shard_map.68.refs_0_ = bf16[96,4096]{1,0:T(8,128)(2,1)} custom-call(bf16[96,1024]{1,0:T(8,128)(2,1)S(1)} %collective-permute-done.19.arrived_ref, f32[192,1024]{1,0:T(8,128)S(1)} %get-tuple-element.38.kept_ref), custom_call_target="tpu_custom_call" | custom-call | tf_op jit(solution)/shard_map/pallas_call | solution.py:322
  59.4 3.3 %collective-permute-done.16.arrived_ref = bf16[96,1024]{1,0:T(8,128)(2,1)S(1)} collective-permute-done((bf16[96,1024]{1,0:T(8,128)(2,1)S(1)}, bf16[96,1024]{1,0:T(8,128)(2,1)S(1)}, u32[]{:S(2)}, u32[]{:S(2)}) %collective-permute-start.16) | collective-permute-done | bytes 196640 | tf_op jit(solution)/shard_map/ppermute | solution.py:205
  62.7 0.8 %shard_map.69.refs_0_ = bf16[96,4096]{1,0:T(8,128)(2,1)} custom-call(bf16[96,1024]{1,0:T(8,128)(2,1)S(1)} %collective-permute-done.16.arrived_ref, f32[192,1024]{1,0:T(8,128)S(1)} %get-tuple-element.36.kept_ref, bf16[96,4096]{1,0:T(8,128)(2,1)} %shard_map.68.refs_0_), custom_call_target="tpu_custom_call", output_to_operand_aliasing={{}: (2, {})} | custom-call | tf_op jit(solution)/shard_map/pallas_call | solution.py:322
  63.5 3.4 %collective-permute-done.13.arrived_ref = bf16[96,1024]{1,0:T(8,128)(2,1)S(1)} collective-permute-done((bf16[96,1024]{1,0:T(8,128)(2,1)S(1)}, bf16[96,1024]{1,0:T(8,128)(2,1)S(1)}, u32[]{:S(2)}, u32[]{:S(2)}) %collective-permute-start.13) | collective-permute-done | bytes 196640 | tf_op jit(solution)/shard_map/ppermute | solution.py:205
  66.9 0.8 %shard_map.70.refs_0_ = bf16[96,4096]{1,0:T(8,128)(2,1)} custom-call(bf16[96,1024]{1,0:T(8,128)(2,1)S(1)} %collective-permute-done.13.arrived_ref, f32[192,1024]{1,0:T(8,128)S(1)} %get-tuple-element.34.kept_ref, bf16[96,4096]{1,0:T(8,128)(2,1)} %shard_map.69.refs_0_), custom_call_target="tpu_custom_call", output_to_operand_aliasing={{}: (2, {})} | custom-call | tf_op jit(solution)/shard_map/pallas_call | solution.py:322
  67.7 2.8 %collective-permute-done.10.arrived_ref = bf16[96,1024]{1,0:T(8,128)(2,1)S(1)} collective-permute-done((bf16[96,1024]{1,0:T(8,128)(2,1)S(1)}, bf16[96,1024]{1,0:T(8,128)(2,1)S(1)}, u32[]{:S(2)}, u32[]{:S(2)}) %collective-permute-start.10) | collective-permute-done | bytes 196640 | tf_op jit(solution)/shard_map/ppermute | solution.py:205
  70.5 0.8 %shard_map.71 = bf16[96,4096]{1,0:T(8,128)(2,1)} custom-call(bf16[96,1024]{1,0:T(8,128)(2,1)S(1)} %collective-permute-done.10.arrived_ref, f32[192,1024]{1,0:T(8,128)S(1)} %get-tuple-element.32.kept_ref, bf16[96,4096]{1,0:T(8,128)(2,1)} %shard_map.70.refs_0_), custom_call_target="tpu_custom_call", output_to_operand_aliasing={{}: (2, {})} | custom-call | tf_op jit(solution)/shard_map/pallas_call | solution.py:322
  (28 shorter events, 0.3 us)
Async XLA Ops:
  0.0 15.3 %slice-start = ((s8[8388608]{0:T(1024)(128)(4,1)}), s8[4194304]{0:T(1024)(128)(4,1)S(1)}, s32[]{:S(2)}) async-start(s8[8388608]{0:T(1024)(128)(4,1)} %bitcast.1), calls=%async_computation | async-start | bytes 8388608
  0.0 1.2 %copy-start.3 = (f32[64,32,32]{0,2,1:T(8,128)S(1)}, f32[64,32,32]{0,2,1:T(8,128)}, u32[]{:S(2)}) copy-start(f32[64,32,32]{0,2,1:T(8,128)} %param.5) | copy-start | bytes 786436
  1.2 7.0 %copy-start = (f32[9,64,64]{2,1,0:T(8,128)S(1)}, f32[9,64,64]{2,1,0:T(8,128)}, u32[]{:S(2)}) copy-start(f32[9,64,64]{2,1,0:T(8,128)} %first_ref.1) | copy-start | bytes 442372
  1.2 7.0 %copy-start.1 = (f32[9,64,64]{2,1,0:T(8,128)S(1)}, f32[9,64,64]{2,1,0:T(8,128)}, u32[]{:S(2)}) copy-start(f32[9,64,64]{2,1,0:T(8,128)} %second_ref.1) | copy-start | bytes 442372
  1.2 7.0 %copy-start.2 = (bf16[256,384]{1,0:T(8,128)(2,1)S(1)}, bf16[256,384]{1,0:T(8,128)(2,1)}, u32[]{:S(2)}) copy-start(bf16[256,384]{1,0:T(8,128)(2,1)} %embed_ref.1) | copy-start | bytes 589828
  1.2 14.1 %slice-start.1 = ((s8[8388608]{0:T(1024)(128)(4,1)}), s8[4194304]{0:T(1024)(128)(4,1)S(1)}, s32[]{:S(2)}) async-start(s8[8388608]{0:T(1024)(128)(4,1)} %bitcast.1), calls=%async_computation.1 | async-start | bytes 8388608
  1.3 7.4 %collective-permute-start.1 = (bf16[16,32,128]{2,1,0:T(8,128)(2,1)S(1)}, bf16[16,32,128]{2,1,0:T(8,128)(2,1)S(1)}, u32[]{:S(2)}, u32[]{:S(2)}) collective-permute-start(bf16[16,32,128]{2,1,0:T(8,128)(2,1)S(1)} %get-tuple-element.22.refs_0_), channel_id=1, source_target_pairs={{0,2},{2,0},{1,3},{3,1},{4,6},{6,4},{5,7},{7,5},{8,10},{10,8},{9,1... | collective-permute-start | bytes 393224 | tf_op jit(solution)/shard_map/ppermute | solution.py:205
  4.3 5.4 %collective-permute-start.3 = (bf16[1,32,128]{2,1,0:T(8,128)(2,1)S(1)}, bf16[1,32,128]{2,1,0:T(8,128)(2,1)S(1)}, u32[]{:S(2)}, u32[]{:S(2)}) collective-permute-start(bf16[1,32,128]{2,1,0:T(8,128)(2,1)S(1)} %get-tuple-element.23), channel_id=1, source_target_pairs={{0,4},{4,8},{8,12},{12,0},{1,5},{5,9},{9,13},{13,1},{2,6},{6,10},{... | collective-permute-start | bytes 24584 | tf_op jit(solution)/shard_map/ppermute | solution.py:205
  5.9 5.8 %collective-permute-start = (bf16[16,32,128]{2,1,0:T(8,128)(2,1)S(1)}, bf16[16,32,128]{2,1,0:T(8,128)(2,1)S(1)}, u32[]{:S(2)}, u32[]{:S(2)}) collective-permute-start(bf16[16,32,128]{2,1,0:T(8,128)(2,1)S(1)} %get-tuple-element.22.refs_0_), channel_id=1, source_target_pairs={{0,1},{1,0},{2,3},{3,2},{4,5},{5,4},{6,7},{7,6},{8,9},{9,8},{10,11... | collective-permute-start | bytes 393224 | tf_op jit(solution)/shard_map/ppermute | solution.py:205
  5.9 3.9 %collective-permute-start.4 = (bf16[1,32,128]{2,1,0:T(8,128)(2,1)S(1)}, bf16[1,32,128]{2,1,0:T(8,128)(2,1)S(1)}, u32[]{:S(2)}, u32[]{:S(2)}) collective-permute-start(bf16[1,32,128]{2,1,0:T(8,128)(2,1)S(1)} %get-tuple-element.24), channel_id=1, source_target_pairs={{0,12},{4,0},{8,4},{12,8},{1,13},{5,1},{9,5},{13,9},{2,14},{6,2},{... | collective-permute-start | bytes 24584 | tf_op jit(solution)/shard_map/ppermute | solution.py:205
  8.8 3.0 %collective-permute-start.2 = (bf16[16,32,128]{2,1,0:T(8,128)(2,1)S(1)}, bf16[16,32,128]{2,1,0:T(8,128)(2,1)S(1)}, u32[]{:S(2)}, u32[]{:S(2)}) collective-permute-start(bf16[16,32,128]{2,1,0:T(8,128)(2,1)S(1)} %collective-permute-done.1.refs_2_), channel_id=1, source_target_pairs={{0,1},{1,0},{2,3},{3,2},{4,5},{5,4},{6,7},{7,6},{8,9},{9,8},{10,11... | collective-permute-start | bytes 393224 | tf_op jit(solution)/shard_map/ppermute | solution.py:205
  9.8 4.4 %collective-permute-start.5 = (bf16[2,32,128]{2,1,0:T(8,128)(2,1)S(1)}, bf16[2,32,128]{2,1,0:T(8,128)(2,1)S(1)}, u32[]{:S(2)}, u32[]{:S(2)}) collective-permute-start(bf16[2,32,128]{2,1,0:T(8,128)(2,1)S(1)} %constant_dynamic-update-slice_fusion.refs_0_), channel_id=1, source_target_pairs={{0,1},{1,0},{2,3},{3,2},{4,5},{5,4},{6,7},{7,6},{8,9},{9,8},{10,11... | collective-permute-start | bytes 49160 | tf_op jit(solution)/shard_map/ppermute | solution.py:224
  9.9 4.3 %collective-permute-start.6 = (bf16[2,32,128]{2,1,0:T(8,128)(2,1)S(1)}, bf16[2,32,128]{2,1,0:T(8,128)(2,1)S(1)}, u32[]{:S(2)}, u32[]{:S(2)}) collective-permute-start(bf16[2,32,128]{2,1,0:T(8,128)(2,1)S(1)} %constant_dynamic-update-slice_fusion.refs_0_), channel_id=1, source_target_pairs={{0,2},{1,3},{2,0},{3,1},{4,6},{5,7},{6,4},{7,5},{8,10},{9,11},{10,... | collective-permute-start | bytes 49160 | tf_op jit(solution)/shard_map/ppermute | solution.py:224
  10.2 3.9 %collective-permute-start.7 = (bf16[2,32,128]{2,1,0:T(8,128)(2,1)S(1)}, bf16[2,32,128]{2,1,0:T(8,128)(2,1)S(1)}, u32[]{:S(2)}, u32[]{:S(2)}) collective-permute-start(bf16[2,32,128]{2,1,0:T(8,128)(2,1)S(1)} %constant_dynamic-update-slice_fusion.refs_0_), channel_id=1, source_target_pairs={{0,3},{1,2},{2,1},{3,0},{4,7},{5,6},{6,5},{7,4},{8,11},{9,10},{10,... | collective-permute-start | bytes 49160 | tf_op jit(solution)/shard_map/ppermute | solution.py:224
  15.8 9.0 %collective-permute-start.17 = (bf16[96,1024]{1,0:T(8,128)(2,1)S(1)}, bf16[96,1024]{1,0:T(8,128)(2,1)S(1)}, u32[]{:S(2)}, u32[]{:S(2)}) collective-permute-start(bf16[96,1024]{1,0:T(8,128)(2,1)S(1)} %shard_map.66), channel_id=1, source_target_pairs={{0,12},{4,0},{8,4},{12,8},{1,13},{5,1},{9,5},{13,9},{2,14},{6,2},{... | collective-permute-start | bytes 589832 | tf_op jit(solution)/shard_map/ppermute | solution.py:205
  20.0 9.9 %collective-permute-start.14 = (bf16[96,1024]{1,0:T(8,128)(2,1)S(1)}, bf16[96,1024]{1,0:T(8,128)(2,1)S(1)}, u32[]{:S(2)}, u32[]{:S(2)}) collective-permute-start(bf16[96,1024]{1,0:T(8,128)(2,1)S(1)} %shard_map.64), channel_id=1, source_target_pairs={{0,12},{4,0},{8,4},{12,8},{1,13},{5,1},{9,5},{13,9},{2,14},{6,2},{... | collective-permute-start | bytes 589832 | tf_op jit(solution)/shard_map/ppermute | solution.py:205
  20.6 13.6 %collective-permute-start.11 = (bf16[96,1024]{1,0:T(8,128)(2,1)S(1)}, bf16[96,1024]{1,0:T(8,128)(2,1)S(1)}, u32[]{:S(2)}, u32[]{:S(2)}) collective-permute-start(bf16[96,1024]{1,0:T(8,128)(2,1)S(1)} %shard_map.62), channel_id=1, source_target_pairs={{0,12},{4,0},{8,4},{12,8},{1,13},{5,1},{9,5},{13,9},{2,14},{6,2},{... | collective-permute-start | bytes 589832 | tf_op jit(solution)/shard_map/ppermute | solution.py:205
  21.5 16.8 %collective-permute-start.8 = (bf16[96,1024]{1,0:T(8,128)(2,1)S(1)}, bf16[96,1024]{1,0:T(8,128)(2,1)S(1)}, u32[]{:S(2)}, u32[]{:S(2)}) collective-permute-start(bf16[96,1024]{1,0:T(8,128)(2,1)S(1)} %shard_map.60), channel_id=1, source_target_pairs={{0,12},{4,0},{8,4},{12,8},{1,13},{5,1},{9,5},{13,9},{2,14},{6,2},{... | collective-permute-start | bytes 589832 | tf_op jit(solution)/shard_map/ppermute | solution.py:205
  25.6 17.0 %collective-permute-start.18 = (bf16[96,1024]{1,0:T(8,128)(2,1)S(1)}, bf16[96,1024]{1,0:T(8,128)(2,1)S(1)}, u32[]{:S(2)}, u32[]{:S(2)}) collective-permute-start(bf16[96,1024]{1,0:T(8,128)(2,1)S(1)} %get-tuple-element.37), channel_id=1, source_target_pairs={{0,12},{4,0},{8,4},{12,8},{1,13},{5,1},{9,5},{13,9},{2,14},{6,2},{... | collective-permute-start | bytes 589832 | tf_op jit(solution)/shard_map/ppermute | solution.py:205
  30.7 15.3 %collective-permute-start.15 = (bf16[96,1024]{1,0:T(8,128)(2,1)S(1)}, bf16[96,1024]{1,0:T(8,128)(2,1)S(1)}, u32[]{:S(2)}, u32[]{:S(2)}) collective-permute-start(bf16[96,1024]{1,0:T(8,128)(2,1)S(1)} %get-tuple-element.35), channel_id=1, source_target_pairs={{0,12},{4,0},{8,4},{12,8},{1,13},{5,1},{9,5},{13,9},{2,14},{6,2},{... | collective-permute-start | bytes 589832 | tf_op jit(solution)/shard_map/ppermute | solution.py:205
  34.9 15.3 %collective-permute-start.12 = (bf16[96,1024]{1,0:T(8,128)(2,1)S(1)}, bf16[96,1024]{1,0:T(8,128)(2,1)S(1)}, u32[]{:S(2)}, u32[]{:S(2)}) collective-permute-start(bf16[96,1024]{1,0:T(8,128)(2,1)S(1)} %get-tuple-element.33), channel_id=1, source_target_pairs={{0,12},{4,0},{8,4},{12,8},{1,13},{5,1},{9,5},{13,9},{2,14},{6,2},{... | collective-permute-start | bytes 589832 | tf_op jit(solution)/shard_map/ppermute | solution.py:205
  39.1 15.3 %collective-permute-start.9 = (bf16[96,1024]{1,0:T(8,128)(2,1)S(1)}, bf16[96,1024]{1,0:T(8,128)(2,1)S(1)}, u32[]{:S(2)}, u32[]{:S(2)}) collective-permute-start(bf16[96,1024]{1,0:T(8,128)(2,1)S(1)} %get-tuple-element.31), channel_id=1, source_target_pairs={{0,12},{4,0},{8,4},{12,8},{1,13},{5,1},{9,5},{13,9},{2,14},{6,2},{... | collective-permute-start | bytes 589832 | tf_op jit(solution)/shard_map/ppermute | solution.py:205
  42.6 16.1 %collective-permute-start.19 = (bf16[96,1024]{1,0:T(8,128)(2,1)S(1)}, bf16[96,1024]{1,0:T(8,128)(2,1)S(1)}, u32[]{:S(2)}, u32[]{:S(2)}) collective-permute-start(bf16[96,1024]{1,0:T(8,128)(2,1)S(1)} %add_convert_fusion), channel_id=1, source_target_pairs={{0,12},{4,0},{8,4},{12,8},{1,13},{5,1},{9,5},{13,9},{2,14},{6,2},{... | collective-permute-start | bytes 589832 | tf_op jit(solution)/shard_map/ppermute | solution.py:205
  46.1 16.6 %collective-permute-start.16 = (bf16[96,1024]{1,0:T(8,128)(2,1)S(1)}, bf16[96,1024]{1,0:T(8,128)(2,1)S(1)}, u32[]{:S(2)}, u32[]{:S(2)}) collective-permute-start(bf16[96,1024]{1,0:T(8,128)(2,1)S(1)} %add_convert_fusion.1), channel_id=1, source_target_pairs={{0,12},{4,0},{8,4},{12,8},{1,13},{5,1},{9,5},{13,9},{2,14},{6,2},{... | collective-permute-start | bytes 589832 | tf_op jit(solution)/shard_map/ppermute | solution.py:205
  50.3 16.6 %collective-permute-start.13 = (bf16[96,1024]{1,0:T(8,128)(2,1)S(1)}, bf16[96,1024]{1,0:T(8,128)(2,1)S(1)}, u32[]{:S(2)}, u32[]{:S(2)}) collective-permute-start(bf16[96,1024]{1,0:T(8,128)(2,1)S(1)} %add_convert_fusion.2), channel_id=1, source_target_pairs={{0,12},{4,0},{8,4},{12,8},{1,13},{5,1},{9,5},{13,9},{2,14},{6,2},{... | collective-permute-start | bytes 589832 | tf_op jit(solution)/shard_map/ppermute | solution.py:205
  54.5 16.0 %collective-permute-start.10 = (bf16[96,1024]{1,0:T(8,128)(2,1)S(1)}, bf16[96,1024]{1,0:T(8,128)(2,1)S(1)}, u32[]{:S(2)}, u32[]{:S(2)}) collective-permute-start(bf16[96,1024]{1,0:T(8,128)(2,1)S(1)} %add_convert_fusion.3), channel_id=1, source_target_pairs={{0,12},{4,0},{8,4},{12,8},{1,13},{5,1},{9,5},{13,9},{2,14},{6,2},{... | collective-permute-start | bytes 589832 | tf_op jit(solution)/shard_map/ppermute | solution.py:205

commit v24 on v23

--- a/solution.py
+++ b/solution.py
@@ -153,7 +153,8 @@
 def outer_kernel(count_ch, count_sub, field_ref, *refs):
     count = count_ch * count_sub
     sides, refs = refs[:count], refs[count:]
-    upper_edge_ref, lower_edge_ref, taps_one_ref, taps_two_ref, embed_ref, inner_ref, tokens_ref, two_ref, sides_ref = refs
+    upper_edge_ref, lower_edge_ref, taps_one_ref, taps_two_ref, embed_ref, inner_ref, mixing_ref = refs[:7]
+    tokens_ref, sent_ref, two_ref, sides_ref, product_ref = refs[7:]
     pairs, lat, wide = field_ref.shape
     for away, block in enumerate(sides):
         sides_ref[:, place(away, count_ch, count_sub, lat // count), :] = block[...]
@@ -168,6 +169,11 @@
     outermost = [[-1, 0], [pairs - 1, pairs]]
     next_inside = [1, 2, pairs - 3, pairs - 2]
     found = [first_conv(field_at, side, taps_one_ref, lat) for side in outermost]
+    inner = inner_ref.shape[1]
+    rows, width = sent_ref.shape
+    step = STEP if width % STEP == 0 else width
+    for at in range(0, width, step):
+        product_ref[:, pl.ds(at, step)] = dot(inner_ref[:rows], mixing_ref[pl.ds(lat, inner), pl.ds(at, step)])
 
     def hidden_at(side, part, edge_ref):
         def at(pair):
@@ -182,7 +188,11 @@
         two = second_conv(upper_at, lower_at, ends, taps_two_ref, lat)
         two_ref[pl.ds(side * 2 * lat, 2 * lat), :] = two
     outer = embed_patches(two_ref, embed_ref)
-    inner = inner_ref.shape[1]
+    for at in range(0, width, step):
+        here = pl.ds(at, step)
+        product = dot(outer[:rows, :lat], mixing_ref[pl.ds(0, lat), here])
+        product = product + dot(outer[:rows, lat:], mixing_ref[pl.ds(lat + inner, lat), here])
+        sent_ref[:, here] = (product_ref[:, here] + product).astype(sent_ref.dtype)
     tokens_ref[:, :lat] = outer[:, :lat]
     tokens_ref[:, pl.ds(lat, inner)] = inner_ref[...]
     tokens_ref[:, pl.ds(lat + inner, lat)] = outer[:, lat:]
@@ -225,7 +235,7 @@
     return blocks
 
 
-def encode(weather, conv_first, conv_second, patch_embed):
+def encode(weather, conv_first, conv_second, patch_embed, token_mixing):
     chans, lon, lat = weather.shape
     pairs, wide = lon // 2, 2 * chans
     embed = patch_embed.shape[1]
@@ -269,11 +279,16 @@
         flops=work * (pairs - 3),
         moved=field.size * 2,
     )
+    sent = (embed // lax.axis_size("tok"), token_mixing.shape[1] // PIECES)
     return call(
         functools.partial(outer_kernel, *counts),
-        shape((embed, pairs * lat // 2)),
-        (field, *sides, upper_edge, lower_edge, *weights, inner),
-        scratch=[pltpu.VMEM((4 * lat, wide), jnp.float32), pltpu.VMEM((2, lat, wide), jnp.bfloat16)],
+        (shape((embed, pairs * lat // 2)), shape(sent)),
+        (field, *sides, upper_edge, lower_edge, *weights, inner, token_mixing),
+        scratch=[
+            pltpu.VMEM((4 * lat, wide), jnp.float32),
+            pltpu.VMEM((2, lat, wide), jnp.bfloat16),
+            pltpu.VMEM(sent, jnp.float32),
+        ],
         flops=work * 4,
         moved=field.size * 2,
     )
@@ -334,7 +349,7 @@
     )(arrived, kept, *earlier)
 
 
-def lift(tokens, token_mixing, pieces):
+def lift(tokens, first_sent, token_mixing, pieces):
     count = lax.axis_size("tok")
     embed = tokens.shape[0]
     rows = embed // count
@@ -342,9 +357,9 @@
     sent = jax.ShapeDtypeStruct((rows, width), jnp.bfloat16)
     ways = [-1] * pieces
     blocks = [list(range(count - 2, -1, -1)) if way == 1 else list(range(count - 1)) for way in ways]
-    travelling = [
+    travelling = [first_sent] + [
         call(functools.partial(sent_kernel, piece * width, blocks[piece][0]), sent, (tokens, token_mixing))
-        for piece in range(pieces)
+        for piece in range(1, pieces)
     ]
     kept = [None] * pieces
     result = None
@@ -367,8 +382,8 @@
 
 
 def local(weather, conv_first, conv_second, patch_embed, token_mixing):
-    tokens = encode(weather, conv_first, conv_second, patch_embed)
-    return lift(tokens, token_mixing, PIECES)
+    tokens, first_sent = encode(weather, conv_first, conv_second, patch_embed, token_mixing)
+    return lift(tokens, first_sent, token_mixing, PIECES)
 
 
 def solution(mesh):

time: 71.4 us -> 71.3 us (level)
    pallas_call x13 -> x12, Pallas kernels: 9.13 us -> 8.99 us  [call(): pl.pallas_call(kernel, out_shape=out_shape, in_specs=[pl.BlockSpec(memory...]
where the time goes in v24:
time: 71.3 us; the launch traced here: 71.1 us
  starting transfers between devices  44.8 us (63%)
  waiting for transfers between devices  12.8 us (18%)
  Pallas kernels  12 us (17%)
  local copies, waits for them, and re-layouts  1.22 us (2%)
    ppermute x17, starting transfers between devices, turned(): lax.ppermute(value, axis, [(i, (i + away) % count) for i in range(count)])  42.8 us
    ppermute x17, waiting for transfers between devices, turned(): lax.ppermute(value, axis, [(i, (i + away) % count) for i in range(count)])  12.8 us
    pallas_call x12, Pallas kernels, call(): pl.pallas_call(kernel, out_shape=out_shape, in_specs=[pl.BlockSpec(memory...  8.99 us
    pallas_call x4, Pallas kernels, finish(): pl.pallas_call(functools.partial(last_kernel, first), out_shape=jax.Shape...  3.03 us
    ppermute x3, starting transfers between devices, direct_blocks(): blocks.append(lax.ppermute(block, ('ch', 'sub'), route))  1.93 us
  transfers between devices with their start and end apart: 20, of which 5 were waited for; matrix products, arithmetic and copies ran while one was open for 0% of the time, Pallas kernels for 14%

profile of v24, /device:TPU:0, one launch (start us, length us, event | category | flops | bytes accessed | tf_op | source)
XLA Modules:
  0.0 71.1 jit_solution(9347455349554723152)
XLA Ops:
  0.0 1.2 %copy-done.3 = f32[64,32,32]{0,2,1:T(8,128)S(1)} copy-done((f32[64,32,32]{0,2,1:T(8,128)S(1)}, f32[64,32,32]{0,2,1:T(8,128)}, u32[]{:S(2)}) %copy-start.3) | copy-done | bytes 262168
  1.2 0.1 shard_map.55
  1.3 3.0 %collective-permute-start.1 = (bf16[16,32,128]{2,1,0:T(8,128)(2,1)S(1)}, bf16[16,32,128]{2,1,0:T(8,128)(2,1)S(1)}, u32[]{:S(2)}, u32[]{:S(2)}) collective-permute-start(bf16[16,32,128]{2,1,0:T(8,128)(2,1)S(1)} %get-tuple-element.24.refs_0_), channel_id=1, source_target_pairs={{0,2},{2,0},{1,3},{3,1},{4,6},{6,4},{5,7},{7,5},{8,10},{10,8},{9,1... | collective-permute-start | bytes 393224 | tf_op jit(solution)/shard_map/ppermute | solution.py:215
  4.3 1.6 %collective-permute-start.3 = (bf16[1,32,128]{2,1,0:T(8,128)(2,1)S(1)}, bf16[1,32,128]{2,1,0:T(8,128)(2,1)S(1)}, u32[]{:S(2)}, u32[]{:S(2)}) collective-permute-start(bf16[1,32,128]{2,1,0:T(8,128)(2,1)S(1)} %get-tuple-element.25), channel_id=1, source_target_pairs={{0,4},{4,8},{8,12},{12,0},{1,5},{5,9},{9,13},{13,1},{2,6},{6,10},{... | collective-permute-start | bytes 24584 | tf_op jit(solution)/shard_map/ppermute | solution.py:215
  5.9 0.0 collective-permute-start
  5.9 2.2 %collective-permute-start.4 = (bf16[1,32,128]{2,1,0:T(8,128)(2,1)S(1)}, bf16[1,32,128]{2,1,0:T(8,128)(2,1)S(1)}, u32[]{:S(2)}, u32[]{:S(2)}) collective-permute-start(bf16[1,32,128]{2,1,0:T(8,128)(2,1)S(1)} %get-tuple-element.26), channel_id=1, source_target_pairs={{0,12},{4,0},{8,4},{12,8},{1,13},{5,1},{9,5},{13,9},{2,14},{6,2},{... | collective-permute-start | bytes 24584 | tf_op jit(solution)/shard_map/ppermute | solution.py:215
  8.2 0.6 shard_map.57
  8.8 0.0 collective-permute-done.1.refs_2_
  8.8 0.3 collective-permute-start.2
  9.1 0.7 %collective-permute-done.3 = bf16[1,32,128]{2,1,0:T(8,128)(2,1)S(1)} collective-permute-done((bf16[1,32,128]{2,1,0:T(8,128)(2,1)S(1)}, bf16[1,32,128]{2,1,0:T(8,128)(2,1)S(1)}, u32[]{:S(2)}, u32[]{:S(2)}) %collective-permute-start.3) | collective-permute-done | bytes 8224 | tf_op jit(solution)/shard_map/ppermute | solution.py:215
  9.8 0.1 collective-permute-start.5
  9.9 0.4 collective-permute-start.6
  10.2 1.5 %collective-permute-start.7 = (bf16[2,32,128]{2,1,0:T(8,128)(2,1)S(1)}, bf16[2,32,128]{2,1,0:T(8,128)(2,1)S(1)}, u32[]{:S(2)}, u32[]{:S(2)}) collective-permute-start(bf16[2,32,128]{2,1,0:T(8,128)(2,1)S(1)} %constant_dynamic-update-slice_fusion.refs_0_), channel_id=1, source_target_pairs={{0,3},{1,2},{2,1},{3,0},{4,7},{5,6},{6,5},{7,4},{8,11},{9,10},{10,... | collective-permute-start | bytes 49160 | tf_op jit(solution)/shard_map/ppermute | solution.py:234
  11.7 0.0 collective-permute-done.refs_1_
  11.8 2.4 %shard_map.58 = (bf16[384,768]{1,0:T(8,128)(2,1)S(1)}, bf16[4,128,128]{2,1,0:T(8,128)(2,1)S(1)}, bf16[4,128,128]{2,1,0:T(8,128)(2,1)S(1)}) custom-call(bf16[16,128,128]{2,1,0:T(8,128)(2,1)S(1)} %shard_map.56.field_ref, bf16[256,768]{1,0:T(8,128)(2,1)S(1)} %get-tuple-element.27.taps_one_ref.refs_6_, ...), custom_call_target="tpu_custom_call" | custom-call | flops 1635778560 | bytes 524288 | tf_op jit(solution)/shard_map/pallas_call | solution.py:202
  14.2 0.0 collective-permute-done.6.refs_2_
  14.2 0.0 collective-permute-done.7.refs_3_
  14.2 1.4 %shard_map.59 = (bf16[384,1024]{1,0:T(8,128)(2,1)S(1)}, bf16[96,1024]{1,0:T(8,128)(2,1)S(1)}) custom-call(bf16[16,128,128]{2,1,0:T(8,128)(2,1)S(1)} %shard_map.56.field_ref, bf16[2,32,128]{2,1,0:T(8,128)(2,1)S(1)} %constant_dynamic-update-slice_fusion.refs_0_, bf16[2,32,128]{2,1,0:T(8,128)(2,1)S(1)} %collective-permute-done.5.refs_1_, ...), custom_call_target="tpu_custom_call" | custom-call | flops 503316480 | bytes 524288 | tf_op jit(solution)/shard_map/pallas_call | solution.py:202
  15.6 3.8 %collective-permute-start.17 = (bf16[96,1024]{1,0:T(8,128)(2,1)S(1)}, bf16[96,1024]{1,0:T(8,128)(2,1)S(1)}, u32[]{:S(2)}, u32[]{:S(2)}) collective-permute-start(bf16[96,1024]{1,0:T(8,128)(2,1)S(1)} %get-tuple-element.40), channel_id=1, source_target_pairs={{0,12},{4,0},{8,4},{12,8},{1,13},{5,1},{9,5},{13,9},{2,14},{6,2},{... | collective-permute-start | bytes 589832 | tf_op jit(solution)/shard_map/ppermute | solution.py:215
  19.4 0.5 shard_map.64
  19.9 0.1 collective-permute-start.14
  20.0 0.5 shard_map.62
  20.4 0.5 collective-permute-start.11
  20.9 0.5 shard_map.60
  21.4 0.8 %collective-permute-start.8 = (bf16[96,1024]{1,0:T(8,128)(2,1)S(1)}, bf16[96,1024]{1,0:T(8,128)(2,1)S(1)}, u32[]{:S(2)}, u32[]{:S(2)}) collective-permute-start(bf16[96,1024]{1,0:T(8,128)(2,1)S(1)} %shard_map.60), channel_id=1, source_target_pairs={{0,12},{4,0},{8,4},{12,8},{1,13},{5,1},{9,5},{13,9},{2,14},{6,2},{... | collective-permute-start | bytes 589832 | tf_op jit(solution)/shard_map/ppermute | solution.py:215
  22.2 2.5 %collective-permute-done.17.arrived_ref = bf16[96,1024]{1,0:T(8,128)(2,1)S(1)} collective-permute-done((bf16[96,1024]{1,0:T(8,128)(2,1)S(1)}, bf16[96,1024]{1,0:T(8,128)(2,1)S(1)}, u32[]{:S(2)}, u32[]{:S(2)}) %collective-permute-start.17) | collective-permute-done | bytes 196640 | tf_op jit(solution)/shard_map/ppermute | solution.py:215
  24.7 0.8 %shard_map.66 = (bf16[96,1024]{1,0:T(8,128)(2,1)S(1)}, f32[192,1024]{1,0:T(8,128)S(1)}) custom-call(bf16[96,1024]{1,0:T(8,128)(2,1)S(1)} %collective-permute-done.17.arrived_ref, bf16[384,1024]{1,0:T(8,128)(2,1)S(1)} %get-tuple-element.33.tokens_ref, bf16[1024,4096]{1,0:T(8,128)(2,1)S(1)} %bitcast.2), custom_call_target="tpu_custom_call" | custom-call | tf_op jit(solution)/shard_map/pallas_call | solution.py:202
  25.5 4.3 %collective-permute-start.18 = (bf16[96,1024]{1,0:T(8,128)(2,1)S(1)}, bf16[96,1024]{1,0:T(8,128)(2,1)S(1)}, u32[]{:S(2)}, u32[]{:S(2)}) collective-permute-start(bf16[96,1024]{1,0:T(8,128)(2,1)S(1)} %get-tuple-element.41), channel_id=1, source_target_pairs={{0,12},{4,0},{8,4},{12,8},{1,13},{5,1},{9,5},{13,9},{2,14},{6,2},{... | collective-permute-start | bytes 589832 | tf_op jit(solution)/shard_map/ppermute | solution.py:215
  29.8 0.0 collective-permute-done.14.arrived_ref
  29.8 0.8 %shard_map.65 = (bf16[96,1024]{1,0:T(8,128)(2,1)S(1)}, f32[192,1024]{1,0:T(8,128)S(1)}) custom-call(bf16[96,1024]{1,0:T(8,128)(2,1)S(1)} %collective-permute-done.14.arrived_ref, bf16[384,1024]{1,0:T(8,128)(2,1)S(1)} %get-tuple-element.33.tokens_ref, bf16[1024,4096]{1,0:T(8,128)(2,1)S(1)} %bitcast.2), custom_call_target="tpu_custom_call" | custom-call | tf_op jit(solution)/shard_map/pallas_call | solution.py:202
  30.6 3.4 %collective-permute-start.15 = (bf16[96,1024]{1,0:T(8,128)(2,1)S(1)}, bf16[96,1024]{1,0:T(8,128)(2,1)S(1)}, u32[]{:S(2)}, u32[]{:S(2)}) collective-permute-start(bf16[96,1024]{1,0:T(8,128)(2,1)S(1)} %get-tuple-element.38), channel_id=1, source_target_pairs={{0,12},{4,0},{8,4},{12,8},{1,13},{5,1},{9,5},{13,9},{2,14},{6,2},{... | collective-permute-start | bytes 589832 | tf_op jit(solution)/shard_map/ppermute | solution.py:215
  34.0 0.0 collective-permute-done.11.arrived_ref
  34.0 0.8 %shard_map.63 = (bf16[96,1024]{1,0:T(8,128)(2,1)S(1)}, f32[192,1024]{1,0:T(8,128)S(1)}) custom-call(bf16[96,1024]{1,0:T(8,128)(2,1)S(1)} %collective-permute-done.11.arrived_ref, bf16[384,1024]{1,0:T(8,128)(2,1)S(1)} %get-tuple-element.33.tokens_ref, bf16[1024,4096]{1,0:T(8,128)(2,1)S(1)} %bitcast.2), custom_call_target="tpu_custom_call" | custom-call | tf_op jit(solution)/shard_map/pallas_call | solution.py:202
  34.8 3.4 %collective-permute-start.12 = (bf16[96,1024]{1,0:T(8,128)(2,1)S(1)}, bf16[96,1024]{1,0:T(8,128)(2,1)S(1)}, u32[]{:S(2)}, u32[]{:S(2)}) collective-permute-start(bf16[96,1024]{1,0:T(8,128)(2,1)S(1)} %get-tuple-element.36), channel_id=1, source_target_pairs={{0,12},{4,0},{8,4},{12,8},{1,13},{5,1},{9,5},{13,9},{2,14},{6,2},{... | collective-permute-start | bytes 589832 | tf_op jit(solution)/shard_map/ppermute | solution.py:215
  38.2 0.8 %shard_map.61 = (bf16[96,1024]{1,0:T(8,128)(2,1)S(1)}, f32[192,1024]{1,0:T(8,128)S(1)}) custom-call(bf16[96,1024]{1,0:T(8,128)(2,1)S(1)} %collective-permute-done.8.arrived_ref, bf16[384,1024]{1,0:T(8,128)(2,1)S(1)} %get-tuple-element.33.tokens_ref, bf16[1024,4096]{1,0:T(8,128)(2,1)S(1)} %bitcast.2), custom_call_target="tpu_custom_call" | custom-call | tf_op jit(solution)/shard_map/pallas_call | solution.py:202
  39.0 3.4 %collective-permute-start.9 = (bf16[96,1024]{1,0:T(8,128)(2,1)S(1)}, bf16[96,1024]{1,0:T(8,128)(2,1)S(1)}, u32[]{:S(2)}, u32[]{:S(2)}) collective-permute-start(bf16[96,1024]{1,0:T(8,128)(2,1)S(1)} %get-tuple-element.34), channel_id=1, source_target_pairs={{0,12},{4,0},{8,4},{12,8},{1,13},{5,1},{9,5},{13,9},{2,14},{6,2},{... | collective-permute-start | bytes 589832 | tf_op jit(solution)/shard_map/ppermute | solution.py:215
  42.4 0.0 collective-permute-done.18
  42.5 3.4 %collective-permute-start.19 = (bf16[96,1024]{1,0:T(8,128)(2,1)S(1)}, bf16[96,1024]{1,0:T(8,128)(2,1)S(1)}, u32[]{:S(2)}, u32[]{:S(2)}) collective-permute-start(bf16[96,1024]{1,0:T(8,128)(2,1)S(1)} %add_convert_fusion), channel_id=1, source_target_pairs={{0,12},{4,0},{8,4},{12,8},{1,13},{5,1},{9,5},{13,9},{2,14},{6,2},{... | collective-permute-start | bytes 589832 | tf_op jit(solution)/shard_map/ppermute | solution.py:215
  46.0 4.2 %collective-permute-start.16 = (bf16[96,1024]{1,0:T(8,128)(2,1)S(1)}, bf16[96,1024]{1,0:T(8,128)(2,1)S(1)}, u32[]{:S(2)}, u32[]{:S(2)}) collective-permute-start(bf16[96,1024]{1,0:T(8,128)(2,1)S(1)} %add_convert_fusion.1), channel_id=1, source_target_pairs={{0,12},{4,0},{8,4},{12,8},{1,13},{5,1},{9,5},{13,9},{2,14},{6,2},{... | collective-permute-start | bytes 589832 | tf_op jit(solution)/shard_map/ppermute | solution.py:215
  50.2 4.2 %collective-permute-start.13 = (bf16[96,1024]{1,0:T(8,128)(2,1)S(1)}, bf16[96,1024]{1,0:T(8,128)(2,1)S(1)}, u32[]{:S(2)}, u32[]{:S(2)}) collective-permute-start(bf16[96,1024]{1,0:T(8,128)(2,1)S(1)} %add_convert_fusion.2), channel_id=1, source_target_pairs={{0,12},{4,0},{8,4},{12,8},{1,13},{5,1},{9,5},{13,9},{2,14},{6,2},{... | collective-permute-start | bytes 589832 | tf_op jit(solution)/shard_map/ppermute | solution.py:215
  54.4 4.2 %collective-permute-start.10 = (bf16[96,1024]{1,0:T(8,128)(2,1)S(1)}, bf16[96,1024]{1,0:T(8,128)(2,1)S(1)}, u32[]{:S(2)}, u32[]{:S(2)}) collective-permute-start(bf16[96,1024]{1,0:T(8,128)(2,1)S(1)} %add_convert_fusion.3), channel_id=1, source_target_pairs={{0,12},{4,0},{8,4},{12,8},{1,13},{5,1},{9,5},{13,9},{2,14},{6,2},{... | collective-permute-start | bytes 589832 | tf_op jit(solution)/shard_map/ppermute | solution.py:215
  58.6 0.8 %shard_map.67.refs_0_ = bf16[96,4096]{1,0:T(8,128)(2,1)} custom-call(bf16[96,1024]{1,0:T(8,128)(2,1)S(1)} %collective-permute-done.19.arrived_ref, f32[192,1024]{1,0:T(8,128)S(1)} %get-tuple-element.42.kept_ref), custom_call_target="tpu_custom_call" | custom-call | tf_op jit(solution)/shard_map/pallas_call | solution.py:337
  59.3 3.3 %collective-permute-done.16.arrived_ref = bf16[96,1024]{1,0:T(8,128)(2,1)S(1)} collective-permute-done((bf16[96,1024]{1,0:T(8,128)(2,1)S(1)}, bf16[96,1024]{1,0:T(8,128)(2,1)S(1)}, u32[]{:S(2)}, u32[]{:S(2)}) %collective-permute-start.16) | collective-permute-done | bytes 196640 | tf_op jit(solution)/shard_map/ppermute | solution.py:215
  62.6 0.8 %shard_map.68.refs_0_ = bf16[96,4096]{1,0:T(8,128)(2,1)} custom-call(bf16[96,1024]{1,0:T(8,128)(2,1)S(1)} %collective-permute-done.16.arrived_ref, f32[192,1024]{1,0:T(8,128)S(1)} %get-tuple-element.39.kept_ref, bf16[96,4096]{1,0:T(8,128)(2,1)} %shard_map.67.refs_0_), custom_call_target="tpu_custom_call", output_to_operand_aliasing={{}: (2, {})} | custom-call | tf_op jit(solution)/shard_map/pallas_call | solution.py:337
  63.4 3.4 %collective-permute-done.13.arrived_ref = bf16[96,1024]{1,0:T(8,128)(2,1)S(1)} collective-permute-done((bf16[96,1024]{1,0:T(8,128)(2,1)S(1)}, bf16[96,1024]{1,0:T(8,128)(2,1)S(1)}, u32[]{:S(2)}, u32[]{:S(2)}) %collective-permute-start.13) | collective-permute-done | bytes 196640 | tf_op jit(solution)/shard_map/ppermute | solution.py:215
  66.8 0.8 %shard_map.69.refs_0_ = bf16[96,4096]{1,0:T(8,128)(2,1)} custom-call(bf16[96,1024]{1,0:T(8,128)(2,1)S(1)} %collective-permute-done.13.arrived_ref, f32[192,1024]{1,0:T(8,128)S(1)} %get-tuple-element.37.kept_ref, bf16[96,4096]{1,0:T(8,128)(2,1)} %shard_map.68.refs_0_), custom_call_target="tpu_custom_call", output_to_operand_aliasing={{}: (2, {})} | custom-call | tf_op jit(solution)/shard_map/pallas_call | solution.py:337
  67.6 2.8 %collective-permute-done.10.arrived_ref = bf16[96,1024]{1,0:T(8,128)(2,1)S(1)} collective-permute-done((bf16[96,1024]{1,0:T(8,128)(2,1)S(1)}, bf16[96,1024]{1,0:T(8,128)(2,1)S(1)}, u32[]{:S(2)}, u32[]{:S(2)}) %collective-permute-start.10) | collective-permute-done | bytes 196640 | tf_op jit(solution)/shard_map/ppermute | solution.py:215
  70.4 0.8 %shard_map.70 = bf16[96,4096]{1,0:T(8,128)(2,1)} custom-call(bf16[96,1024]{1,0:T(8,128)(2,1)S(1)} %collective-permute-done.10.arrived_ref, f32[192,1024]{1,0:T(8,128)S(1)} %get-tuple-element.35.kept_ref, bf16[96,4096]{1,0:T(8,128)(2,1)} %shard_map.69.refs_0_), custom_call_target="tpu_custom_call", output_to_operand_aliasing={{}: (2, {})} | custom-call | tf_op jit(solution)/shard_map/pallas_call | solution.py:337
  (27 shorter events, 0.3 us)
Async XLA Ops:
  0.0 14.2 %slice-start = ((s8[8388608]{0:T(1024)(128)(4,1)}), s8[4194304]{0:T(1024)(128)(4,1)S(1)}, s32[]{:S(2)}) async-start(s8[8388608]{0:T(1024)(128)(4,1)} %bitcast.1), calls=%async_computation | async-start | bytes 8388608
  0.0 1.2 %copy-start.3 = (f32[64,32,32]{0,2,1:T(8,128)S(1)}, f32[64,32,32]{0,2,1:T(8,128)}, u32[]{:S(2)}) copy-start(f32[64,32,32]{0,2,1:T(8,128)} %param.5) | copy-start | bytes 786436
  1.2 7.0 %copy-start = (f32[9,64,64]{2,1,0:T(8,128)S(1)}, f32[9,64,64]{2,1,0:T(8,128)}, u32[]{:S(2)}) copy-start(f32[9,64,64]{2,1,0:T(8,128)} %first_ref.1) | copy-start | bytes 442372
  1.2 7.0 %copy-start.1 = (f32[9,64,64]{2,1,0:T(8,128)S(1)}, f32[9,64,64]{2,1,0:T(8,128)}, u32[]{:S(2)}) copy-start(f32[9,64,64]{2,1,0:T(8,128)} %second_ref.1) | copy-start | bytes 442372
  1.2 7.0 %copy-start.2 = (bf16[256,384]{1,0:T(8,128)(2,1)S(1)}, bf16[256,384]{1,0:T(8,128)(2,1)}, u32[]{:S(2)}) copy-start(bf16[256,384]{1,0:T(8,128)(2,1)} %embed_ref.1) | copy-start | bytes 589828
  1.2 13.0 %slice-start.1 = ((s8[8388608]{0:T(1024)(128)(4,1)}), s8[4194304]{0:T(1024)(128)(4,1)S(1)}, s32[]{:S(2)}) async-start(s8[8388608]{0:T(1024)(128)(4,1)} %bitcast.1), calls=%async_computation.1 | async-start | bytes 8388608
  1.3 7.4 %collective-permute-start.1 = (bf16[16,32,128]{2,1,0:T(8,128)(2,1)S(1)}, bf16[16,32,128]{2,1,0:T(8,128)(2,1)S(1)}, u32[]{:S(2)}, u32[]{:S(2)}) collective-permute-start(bf16[16,32,128]{2,1,0:T(8,128)(2,1)S(1)} %get-tuple-element.24.refs_0_), channel_id=1, source_target_pairs={{0,2},{2,0},{1,3},{3,1},{4,6},{6,4},{5,7},{7,5},{8,10},{10,8},{9,1... | collective-permute-start | bytes 393224 | tf_op jit(solution)/shard_map/ppermute | solution.py:215
  4.3 5.4 %collective-permute-start.3 = (bf16[1,32,128]{2,1,0:T(8,128)(2,1)S(1)}, bf16[1,32,128]{2,1,0:T(8,128)(2,1)S(1)}, u32[]{:S(2)}, u32[]{:S(2)}) collective-permute-start(bf16[1,32,128]{2,1,0:T(8,128)(2,1)S(1)} %get-tuple-element.25), channel_id=1, source_target_pairs={{0,4},{4,8},{8,12},{12,0},{1,5},{5,9},{9,13},{13,1},{2,6},{6,10},{... | collective-permute-start | bytes 24584 | tf_op jit(solution)/shard_map/ppermute | solution.py:215
  5.9 5.8 %collective-permute-start = (bf16[16,32,128]{2,1,0:T(8,128)(2,1)S(1)}, bf16[16,32,128]{2,1,0:T(8,128)(2,1)S(1)}, u32[]{:S(2)}, u32[]{:S(2)}) collective-permute-start(bf16[16,32,128]{2,1,0:T(8,128)(2,1)S(1)} %get-tuple-element.24.refs_0_), channel_id=1, source_target_pairs={{0,1},{1,0},{2,3},{3,2},{4,5},{5,4},{6,7},{7,6},{8,9},{9,8},{10,11... | collective-permute-start | bytes 393224 | tf_op jit(solution)/shard_map/ppermute | solution.py:215
  5.9 3.9 %collective-permute-start.4 = (bf16[1,32,128]{2,1,0:T(8,128)(2,1)S(1)}, bf16[1,32,128]{2,1,0:T(8,128)(2,1)S(1)}, u32[]{:S(2)}, u32[]{:S(2)}) collective-permute-start(bf16[1,32,128]{2,1,0:T(8,128)(2,1)S(1)} %get-tuple-element.26), channel_id=1, source_target_pairs={{0,12},{4,0},{8,4},{12,8},{1,13},{5,1},{9,5},{13,9},{2,14},{6,2},{... | collective-permute-start | bytes 24584 | tf_op jit(solution)/shard_map/ppermute | solution.py:215
  8.8 3.0 %collective-permute-start.2 = (bf16[16,32,128]{2,1,0:T(8,128)(2,1)S(1)}, bf16[16,32,128]{2,1,0:T(8,128)(2,1)S(1)}, u32[]{:S(2)}, u32[]{:S(2)}) collective-permute-start(bf16[16,32,128]{2,1,0:T(8,128)(2,1)S(1)} %collective-permute-done.1.refs_2_), channel_id=1, source_target_pairs={{0,1},{1,0},{2,3},{3,2},{4,5},{5,4},{6,7},{7,6},{8,9},{9,8},{10,11... | collective-permute-start | bytes 393224 | tf_op jit(solution)/shard_map/ppermute | solution.py:215
  9.8 4.4 %collective-permute-start.5 = (bf16[2,32,128]{2,1,0:T(8,128)(2,1)S(1)}, bf16[2,32,128]{2,1,0:T(8,128)(2,1)S(1)}, u32[]{:S(2)}, u32[]{:S(2)}) collective-permute-start(bf16[2,32,128]{2,1,0:T(8,128)(2,1)S(1)} %constant_dynamic-update-slice_fusion.refs_0_), channel_id=1, source_target_pairs={{0,1},{1,0},{2,3},{3,2},{4,5},{5,4},{6,7},{7,6},{8,9},{9,8},{10,11... | collective-permute-start | bytes 49160 | tf_op jit(solution)/shard_map/ppermute | solution.py:234
  9.9 4.3 %collective-permute-start.6 = (bf16[2,32,128]{2,1,0:T(8,128)(2,1)S(1)}, bf16[2,32,128]{2,1,0:T(8,128)(2,1)S(1)}, u32[]{:S(2)}, u32[]{:S(2)}) collective-permute-start(bf16[2,32,128]{2,1,0:T(8,128)(2,1)S(1)} %constant_dynamic-update-slice_fusion.refs_0_), channel_id=1, source_target_pairs={{0,2},{1,3},{2,0},{3,1},{4,6},{5,7},{6,4},{7,5},{8,10},{9,11},{10,... | collective-permute-start | bytes 49160 | tf_op jit(solution)/shard_map/ppermute | solution.py:234
  10.2 3.9 %collective-permute-start.7 = (bf16[2,32,128]{2,1,0:T(8,128)(2,1)S(1)}, bf16[2,32,128]{2,1,0:T(8,128)(2,1)S(1)}, u32[]{:S(2)}, u32[]{:S(2)}) collective-permute-start(bf16[2,32,128]{2,1,0:T(8,128)(2,1)S(1)} %constant_dynamic-update-slice_fusion.refs_0_), channel_id=1, source_target_pairs={{0,3},{1,2},{2,1},{3,0},{4,7},{5,6},{6,5},{7,4},{8,11},{9,10},{10,... | collective-permute-start | bytes 49160 | tf_op jit(solution)/shard_map/ppermute | solution.py:234
  15.6 9.0 %collective-permute-start.17 = (bf16[96,1024]{1,0:T(8,128)(2,1)S(1)}, bf16[96,1024]{1,0:T(8,128)(2,1)S(1)}, u32[]{:S(2)}, u32[]{:S(2)}) collective-permute-start(bf16[96,1024]{1,0:T(8,128)(2,1)S(1)} %get-tuple-element.40), channel_id=1, source_target_pairs={{0,12},{4,0},{8,4},{12,8},{1,13},{5,1},{9,5},{13,9},{2,14},{6,2},{... | collective-permute-start | bytes 589832 | tf_op jit(solution)/shard_map/ppermute | solution.py:215
  19.9 9.9 %collective-permute-start.14 = (bf16[96,1024]{1,0:T(8,128)(2,1)S(1)}, bf16[96,1024]{1,0:T(8,128)(2,1)S(1)}, u32[]{:S(2)}, u32[]{:S(2)}) collective-permute-start(bf16[96,1024]{1,0:T(8,128)(2,1)S(1)} %shard_map.64), channel_id=1, source_target_pairs={{0,12},{4,0},{8,4},{12,8},{1,13},{5,1},{9,5},{13,9},{2,14},{6,2},{... | collective-permute-start | bytes 589832 | tf_op jit(solution)/shard_map/ppermute | solution.py:215
  20.4 13.6 %collective-permute-start.11 = (bf16[96,1024]{1,0:T(8,128)(2,1)S(1)}, bf16[96,1024]{1,0:T(8,128)(2,1)S(1)}, u32[]{:S(2)}, u32[]{:S(2)}) collective-permute-start(bf16[96,1024]{1,0:T(8,128)(2,1)S(1)} %shard_map.62), channel_id=1, source_target_pairs={{0,12},{4,0},{8,4},{12,8},{1,13},{5,1},{9,5},{13,9},{2,14},{6,2},{... | collective-permute-start | bytes 589832 | tf_op jit(solution)/shard_map/ppermute | solution.py:215
  21.4 16.8 %collective-permute-start.8 = (bf16[96,1024]{1,0:T(8,128)(2,1)S(1)}, bf16[96,1024]{1,0:T(8,128)(2,1)S(1)}, u32[]{:S(2)}, u32[]{:S(2)}) collective-permute-start(bf16[96,1024]{1,0:T(8,128)(2,1)S(1)} %shard_map.60), channel_id=1, source_target_pairs={{0,12},{4,0},{8,4},{12,8},{1,13},{5,1},{9,5},{13,9},{2,14},{6,2},{... | collective-permute-start | bytes 589832 | tf_op jit(solution)/shard_map/ppermute | solution.py:215
  25.5 17.0 %collective-permute-start.18 = (bf16[96,1024]{1,0:T(8,128)(2,1)S(1)}, bf16[96,1024]{1,0:T(8,128)(2,1)S(1)}, u32[]{:S(2)}, u32[]{:S(2)}) collective-permute-start(bf16[96,1024]{1,0:T(8,128)(2,1)S(1)} %get-tuple-element.41), channel_id=1, source_target_pairs={{0,12},{4,0},{8,4},{12,8},{1,13},{5,1},{9,5},{13,9},{2,14},{6,2},{... | collective-permute-start | bytes 589832 | tf_op jit(solution)/shard_map/ppermute | solution.py:215
  30.6 15.3 %collective-permute-start.15 = (bf16[96,1024]{1,0:T(8,128)(2,1)S(1)}, bf16[96,1024]{1,0:T(8,128)(2,1)S(1)}, u32[]{:S(2)}, u32[]{:S(2)}) collective-permute-start(bf16[96,1024]{1,0:T(8,128)(2,1)S(1)} %get-tuple-element.38), channel_id=1, source_target_pairs={{0,12},{4,0},{8,4},{12,8},{1,13},{5,1},{9,5},{13,9},{2,14},{6,2},{... | collective-permute-start | bytes 589832 | tf_op jit(solution)/shard_map/ppermute | solution.py:215
  34.8 15.3 %collective-permute-start.12 = (bf16[96,1024]{1,0:T(8,128)(2,1)S(1)}, bf16[96,1024]{1,0:T(8,128)(2,1)S(1)}, u32[]{:S(2)}, u32[]{:S(2)}) collective-permute-start(bf16[96,1024]{1,0:T(8,128)(2,1)S(1)} %get-tuple-element.36), channel_id=1, source_target_pairs={{0,12},{4,0},{8,4},{12,8},{1,13},{5,1},{9,5},{13,9},{2,14},{6,2},{... | collective-permute-start | bytes 589832 | tf_op jit(solution)/shard_map/ppermute | solution.py:215
  39.0 15.3 %collective-permute-start.9 = (bf16[96,1024]{1,0:T(8,128)(2,1)S(1)}, bf16[96,1024]{1,0:T(8,128)(2,1)S(1)}, u32[]{:S(2)}, u32[]{:S(2)}) collective-permute-start(bf16[96,1024]{1,0:T(8,128)(2,1)S(1)} %get-tuple-element.34), channel_id=1, source_target_pairs={{0,12},{4,0},{8,4},{12,8},{1,13},{5,1},{9,5},{13,9},{2,14},{6,2},{... | collective-permute-start | bytes 589832 | tf_op jit(solution)/shard_map/ppermute | solution.py:215
  42.5 16.1 %collective-permute-start.19 = (bf16[96,1024]{1,0:T(8,128)(2,1)S(1)}, bf16[96,1024]{1,0:T(8,128)(2,1)S(1)}, u32[]{:S(2)}, u32[]{:S(2)}) collective-permute-start(bf16[96,1024]{1,0:T(8,128)(2,1)S(1)} %add_convert_fusion), channel_id=1, source_target_pairs={{0,12},{4,0},{8,4},{12,8},{1,13},{5,1},{9,5},{13,9},{2,14},{6,2},{... | collective-permute-start | bytes 589832 | tf_op jit(solution)/shard_map/ppermute | solution.py:215
  46.0 16.6 %collective-permute-start.16 = (bf16[96,1024]{1,0:T(8,128)(2,1)S(1)}, bf16[96,1024]{1,0:T(8,128)(2,1)S(1)}, u32[]{:S(2)}, u32[]{:S(2)}) collective-permute-start(bf16[96,1024]{1,0:T(8,128)(2,1)S(1)} %add_convert_fusion.1), channel_id=1, source_target_pairs={{0,12},{4,0},{8,4},{12,8},{1,13},{5,1},{9,5},{13,9},{2,14},{6,2},{... | collective-permute-start | bytes 589832 | tf_op jit(solution)/shard_map/ppermute | solution.py:215
  50.2 16.6 %collective-permute-start.13 = (bf16[96,1024]{1,0:T(8,128)(2,1)S(1)}, bf16[96,1024]{1,0:T(8,128)(2,1)S(1)}, u32[]{:S(2)}, u32[]{:S(2)}) collective-permute-start(bf16[96,1024]{1,0:T(8,128)(2,1)S(1)} %add_convert_fusion.2), channel_id=1, source_target_pairs={{0,12},{4,0},{8,4},{12,8},{1,13},{5,1},{9,5},{13,9},{2,14},{6,2},{... | collective-permute-start | bytes 589832 | tf_op jit(solution)/shard_map/ppermute | solution.py:215
  54.4 16.0 %collective-permute-start.10 = (bf16[96,1024]{1,0:T(8,128)(2,1)S(1)}, bf16[96,1024]{1,0:T(8,128)(2,1)S(1)}, u32[]{:S(2)}, u32[]{:S(2)}) collective-permute-start(bf16[96,1024]{1,0:T(8,128)(2,1)S(1)} %add_convert_fusion.3), channel_id=1, source_target_pairs={{0,12},{4,0},{8,4},{12,8},{1,13},{5,1},{9,5},{13,9},{2,14},{6,2},{... | collective-permute-start | bytes 589832 | tf_op jit(solution)/shard_map/ppermute | solution.py:215

commit v25 on v24

--- a/solution.py
+++ b/solution.py
@@ -355,7 +355,7 @@
     rows = embed // count
     width = token_mixing.shape[1] // pieces
     sent = jax.ShapeDtypeStruct((rows, width), jnp.bfloat16)
-    ways = [-1] * pieces
+    ways = [-1 if piece % 2 == 0 else 1 for piece in range(pieces)]
     blocks = [list(range(count - 2, -1, -1)) if way == 1 else list(range(count - 1)) for way in ways]
     travelling = [first_sent] + [
         call(functools.partial(sent_kernel, piece * width, blocks[piece][0]), sent, (tokens, token_mixing))

time: 71.3 us -> 72.2 us (1.013)
  waiting for transfers between devices: 12.8 us -> 17.5 us
  starting transfers between devices: 44.8 us -> 41 us
    ppermute x17, waiting for transfers between devices: 12.8 us -> 17.5 us  [turned(): lax.ppermute(value, axis, [(i, (i + away) % count) for i in range(count)])]
    ppermute x17, starting transfers between devices: 42.8 us -> 39 us  [turned(): lax.ppermute(value, axis, [(i, (i + away) % count) for i in range(count)])]
  transfers between devices with their start and end apart: 20 -> 20, of which waited for: 5 -> 10; matrix products, arithmetic and copies ran while one was open for 0% -> 0% of each run, Pallas kernels for 14% -> 14%
where the time goes in v25:
time: 72.2 us; the launch traced here: 72.1 us
  starting transfers between devices  41 us (57%)
  waiting for transfers between devices  17.5 us (24%)
  Pallas kernels  12 us (17%)
  local copies, waits for them, and re-layouts  1.22 us (2%)
    ppermute x17, starting transfers between devices, turned(): lax.ppermute(value, axis, [(i, (i + away) % count) for i in range(count)])  39 us
    ppermute x17, waiting for transfers between devices, turned(): lax.ppermute(value, axis, [(i, (i + away) % count) for i in range(count)])  17.5 us
    pallas_call x12, Pallas kernels, call(): pl.pallas_call(kernel, out_shape=out_shape, in_specs=[pl.BlockSpec(memory...  9 us
    pallas_call x4, Pallas kernels, finish(): pl.pallas_call(functools.partial(last_kernel, first), out_shape=jax.Shape...  3.03 us
    ppermute x3, starting transfers between devices, direct_blocks(): blocks.append(lax.ppermute(block, ('ch', 'sub'), route))  1.93 us
  transfers between devices with their start and end apart: 20, of which 10 were waited for; matrix products, arithmetic and copies ran while one was open for 0% of the time, Pallas kernels for 14%

profile of v25, /device:TPU:0, one launch (start us, length us, event | category | flops | bytes accessed | tf_op | source)
XLA Modules:
  0.0 72.1 jit_solution(5446241842960452914)
XLA Ops:
  0.0 1.2 %copy-done.3 = f32[64,32,32]{0,2,1:T(8,128)S(1)} copy-done((f32[64,32,32]{0,2,1:T(8,128)S(1)}, f32[64,32,32]{0,2,1:T(8,128)}, u32[]{:S(2)}) %copy-start.3) | copy-done | bytes 262168
  1.2 0.1 shard_map.55
  1.3 3.0 %collective-permute-start.1 = (bf16[16,32,128]{2,1,0:T(8,128)(2,1)S(1)}, bf16[16,32,128]{2,1,0:T(8,128)(2,1)S(1)}, u32[]{:S(2)}, u32[]{:S(2)}) collective-permute-start(bf16[16,32,128]{2,1,0:T(8,128)(2,1)S(1)} %get-tuple-element.24.refs_0_), channel_id=1, source_target_pairs={{0,2},{2,0},{1,3},{3,1},{4,6},{6,4},{5,7},{7,5},{8,10},{10,8},{9,1... | collective-permute-start | bytes 393224 | tf_op jit(solution)/shard_map/ppermute | solution.py:215
  4.3 1.6 %collective-permute-start.3 = (bf16[1,32,128]{2,1,0:T(8,128)(2,1)S(1)}, bf16[1,32,128]{2,1,0:T(8,128)(2,1)S(1)}, u32[]{:S(2)}, u32[]{:S(2)}) collective-permute-start(bf16[1,32,128]{2,1,0:T(8,128)(2,1)S(1)} %get-tuple-element.25), channel_id=1, source_target_pairs={{0,4},{4,8},{8,12},{12,0},{1,5},{5,9},{9,13},{13,1},{2,6},{6,10},{... | collective-permute-start | bytes 24584 | tf_op jit(solution)/shard_map/ppermute | solution.py:215
  5.9 0.0 collective-permute-start
  5.9 2.2 %collective-permute-start.4 = (bf16[1,32,128]{2,1,0:T(8,128)(2,1)S(1)}, bf16[1,32,128]{2,1,0:T(8,128)(2,1)S(1)}, u32[]{:S(2)}, u32[]{:S(2)}) collective-permute-start(bf16[1,32,128]{2,1,0:T(8,128)(2,1)S(1)} %get-tuple-element.26), channel_id=1, source_target_pairs={{0,12},{4,0},{8,4},{12,8},{1,13},{5,1},{9,5},{13,9},{2,14},{6,2},{... | collective-permute-start | bytes 24584 | tf_op jit(solution)/shard_map/ppermute | solution.py:215
  8.2 0.6 shard_map.57
  8.8 0.0 collective-permute-done.1.refs_2_
  8.8 0.3 collective-permute-start.2
  9.1 0.7 collective-permute-done.3
  9.8 0.1 collective-permute-start.5
  9.9 0.4 collective-permute-start.6
  10.2 1.5 %collective-permute-start.7 = (bf16[2,32,128]{2,1,0:T(8,128)(2,1)S(1)}, bf16[2,32,128]{2,1,0:T(8,128)(2,1)S(1)}, u32[]{:S(2)}, u32[]{:S(2)}) collective-permute-start(bf16[2,32,128]{2,1,0:T(8,128)(2,1)S(1)} %constant_dynamic-update-slice_fusion.refs_0_), channel_id=1, source_target_pairs={{0,3},{1,2},{2,1},{3,0},{4,7},{5,6},{6,5},{7,4},{8,11},{9,10},{10,... | collective-permute-start | bytes 49160 | tf_op jit(solution)/shard_map/ppermute | solution.py:234
  11.7 0.0 collective-permute-done.refs_1_
  11.8 2.4 %shard_map.58 = (bf16[384,768]{1,0:T(8,128)(2,1)S(1)}, bf16[4,128,128]{2,1,0:T(8,128)(2,1)S(1)}, bf16[4,128,128]{2,1,0:T(8,128)(2,1)S(1)}) custom-call(bf16[16,128,128]{2,1,0:T(8,128)(2,1)S(1)} %shard_map.56.field_ref, bf16[256,768]{1,0:T(8,128)(2,1)S(1)} %get-tuple-element.27.taps_one_ref.refs_6_, ...), custom_call_target="tpu_custom_call" | custom-call | flops 1635778560 | bytes 524288 | tf_op jit(solution)/shard_map/pallas_call | solution.py:202
  14.2 1.4 %shard_map.59 = (bf16[384,1024]{1,0:T(8,128)(2,1)S(1)}, bf16[96,1024]{1,0:T(8,128)(2,1)S(1)}) custom-call(bf16[16,128,128]{2,1,0:T(8,128)(2,1)S(1)} %shard_map.56.field_ref, bf16[2,32,128]{2,1,0:T(8,128)(2,1)S(1)} %constant_dynamic-update-slice_fusion.refs_0_, bf16[2,32,128]{2,1,0:T(8,128)(2,1)S(1)} %collective-permute-done.5.refs_1_, ...), custom_call_target="tpu_custom_call" | custom-call | flops 503316480 | bytes 524288 | tf_op jit(solution)/shard_map/pallas_call | solution.py:202
  15.6 3.8 %collective-permute-start.17 = (bf16[96,1024]{1,0:T(8,128)(2,1)S(1)}, bf16[96,1024]{1,0:T(8,128)(2,1)S(1)}, u32[]{:S(2)}, u32[]{:S(2)}) collective-permute-start(bf16[96,1024]{1,0:T(8,128)(2,1)S(1)} %get-tuple-element.40), channel_id=1, source_target_pairs={{0,12},{4,0},{8,4},{12,8},{1,13},{5,1},{9,5},{13,9},{2,14},{6,2},{... | collective-permute-start | bytes 589832 | tf_op jit(solution)/shard_map/ppermute | solution.py:215
  19.4 0.5 shard_map.64
  19.9 0.1 collective-permute-start.14
  20.0 0.5 shard_map.62
  20.4 3.9 %collective-permute-start.11 = (bf16[96,1024]{1,0:T(8,128)(2,1)S(1)}, bf16[96,1024]{1,0:T(8,128)(2,1)S(1)}, u32[]{:S(2)}, u32[]{:S(2)}) collective-permute-start(bf16[96,1024]{1,0:T(8,128)(2,1)S(1)} %shard_map.62), channel_id=1, source_target_pairs={{0,12},{4,0},{8,4},{12,8},{1,13},{5,1},{9,5},{13,9},{2,14},{6,2},{... | collective-permute-start | bytes 589832 | tf_op jit(solution)/shard_map/ppermute | solution.py:215
  24.3 0.5 shard_map.60
  24.8 0.1 collective-permute-start.8
  24.8 0.8 %shard_map.66 = (bf16[96,1024]{1,0:T(8,128)(2,1)S(1)}, f32[192,1024]{1,0:T(8,128)S(1)}) custom-call(bf16[96,1024]{1,0:T(8,128)(2,1)S(1)} %collective-permute-done.17.arrived_ref, bf16[384,1024]{1,0:T(8,128)(2,1)S(1)} %get-tuple-element.33.tokens_ref, bf16[1024,4096]{1,0:T(8,128)(2,1)S(1)} %bitcast.2), custom_call_target="tpu_custom_call" | custom-call | tf_op jit(solution)/shard_map/pallas_call | solution.py:202
  25.6 4.2 %collective-permute-start.18 = (bf16[96,1024]{1,0:T(8,128)(2,1)S(1)}, bf16[96,1024]{1,0:T(8,128)(2,1)S(1)}, u32[]{:S(2)}, u32[]{:S(2)}) collective-permute-start(bf16[96,1024]{1,0:T(8,128)(2,1)S(1)} %get-tuple-element.41), channel_id=1, source_target_pairs={{0,12},{4,0},{8,4},{12,8},{1,13},{5,1},{9,5},{13,9},{2,14},{6,2},{... | collective-permute-start | bytes 589832 | tf_op jit(solution)/shard_map/ppermute | solution.py:215
  29.8 0.8 %shard_map.65 = (bf16[96,1024]{1,0:T(8,128)(2,1)S(1)}, f32[192,1024]{1,0:T(8,128)S(1)}) custom-call(bf16[96,1024]{1,0:T(8,128)(2,1)S(1)} %collective-permute-done.14.arrived_ref, bf16[384,1024]{1,0:T(8,128)(2,1)S(1)} %get-tuple-element.33.tokens_ref, bf16[1024,4096]{1,0:T(8,128)(2,1)S(1)} %bitcast.2), custom_call_target="tpu_custom_call" | custom-call | tf_op jit(solution)/shard_map/pallas_call | solution.py:202
  30.6 1.6 %collective-permute-start.15 = (bf16[96,1024]{1,0:T(8,128)(2,1)S(1)}, bf16[96,1024]{1,0:T(8,128)(2,1)S(1)}, u32[]{:S(2)}, u32[]{:S(2)}) collective-permute-start(bf16[96,1024]{1,0:T(8,128)(2,1)S(1)} %get-tuple-element.38), channel_id=1, source_target_pairs={{0,4},{4,8},{8,12},{12,0},{1,5},{5,9},{9,13},{13,1},{2,6},{6,10},{... | collective-permute-start | bytes 589832 | tf_op jit(solution)/shard_map/ppermute | solution.py:215
  32.2 0.9 %collective-permute-done.11.arrived_ref = bf16[96,1024]{1,0:T(8,128)(2,1)S(1)} collective-permute-done((bf16[96,1024]{1,0:T(8,128)(2,1)S(1)}, bf16[96,1024]{1,0:T(8,128)(2,1)S(1)}, u32[]{:S(2)}, u32[]{:S(2)}) %collective-permute-start.11) | collective-permute-done | bytes 196640 | tf_op jit(solution)/shard_map/ppermute | solution.py:215
  33.2 0.8 %shard_map.63 = (bf16[96,1024]{1,0:T(8,128)(2,1)S(1)}, f32[192,1024]{1,0:T(8,128)S(1)}) custom-call(bf16[96,1024]{1,0:T(8,128)(2,1)S(1)} %collective-permute-done.11.arrived_ref, bf16[384,1024]{1,0:T(8,128)(2,1)S(1)} %get-tuple-element.33.tokens_ref, bf16[1024,4096]{1,0:T(8,128)(2,1)S(1)} %bitcast.2), custom_call_target="tpu_custom_call" | custom-call | tf_op jit(solution)/shard_map/pallas_call | solution.py:202
  34.0 4.3 %collective-permute-start.12 = (bf16[96,1024]{1,0:T(8,128)(2,1)S(1)}, bf16[96,1024]{1,0:T(8,128)(2,1)S(1)}, u32[]{:S(2)}, u32[]{:S(2)}) collective-permute-start(bf16[96,1024]{1,0:T(8,128)(2,1)S(1)} %get-tuple-element.36), channel_id=1, source_target_pairs={{0,12},{4,0},{8,4},{12,8},{1,13},{5,1},{9,5},{13,9},{2,14},{6,2},{... | collective-permute-start | bytes 589832 | tf_op jit(solution)/shard_map/ppermute | solution.py:215
  38.3 0.8 %shard_map.61 = (bf16[96,1024]{1,0:T(8,128)(2,1)S(1)}, f32[192,1024]{1,0:T(8,128)S(1)}) custom-call(bf16[96,1024]{1,0:T(8,128)(2,1)S(1)} %collective-permute-done.8.arrived_ref, bf16[384,1024]{1,0:T(8,128)(2,1)S(1)} %get-tuple-element.33.tokens_ref, bf16[1024,4096]{1,0:T(8,128)(2,1)S(1)} %bitcast.2), custom_call_target="tpu_custom_call" | custom-call | tf_op jit(solution)/shard_map/pallas_call | solution.py:202
  39.1 1.6 %collective-permute-start.9 = (bf16[96,1024]{1,0:T(8,128)(2,1)S(1)}, bf16[96,1024]{1,0:T(8,128)(2,1)S(1)}, u32[]{:S(2)}, u32[]{:S(2)}) collective-permute-start(bf16[96,1024]{1,0:T(8,128)(2,1)S(1)} %get-tuple-element.34), channel_id=1, source_target_pairs={{0,4},{4,8},{8,12},{12,0},{1,5},{5,9},{9,13},{13,1},{2,6},{6,10},{... | collective-permute-start | bytes 589832 | tf_op jit(solution)/shard_map/ppermute | solution.py:215
  40.7 0.9 %collective-permute-done.18 = bf16[96,1024]{1,0:T(8,128)(2,1)S(1)} collective-permute-done((bf16[96,1024]{1,0:T(8,128)(2,1)S(1)}, bf16[96,1024]{1,0:T(8,128)(2,1)S(1)}, u32[]{:S(2)}, u32[]{:S(2)}) %collective-permute-start.18) | collective-permute-done | bytes 196640 | tf_op jit(solution)/shard_map/ppermute | solution.py:215
  41.7 4.3 %collective-permute-start.19 = (bf16[96,1024]{1,0:T(8,128)(2,1)S(1)}, bf16[96,1024]{1,0:T(8,128)(2,1)S(1)}, u32[]{:S(2)}, u32[]{:S(2)}) collective-permute-start(bf16[96,1024]{1,0:T(8,128)(2,1)S(1)} %add_convert_fusion), channel_id=1, source_target_pairs={{0,12},{4,0},{8,4},{12,8},{1,13},{5,1},{9,5},{13,9},{2,14},{6,2},{... | collective-permute-start | bytes 589832 | tf_op jit(solution)/shard_map/ppermute | solution.py:215
  46.0 0.5 collective-permute-done.15
  46.6 1.8 %collective-permute-start.16 = (bf16[96,1024]{1,0:T(8,128)(2,1)S(1)}, bf16[96,1024]{1,0:T(8,128)(2,1)S(1)}, u32[]{:S(2)}, u32[]{:S(2)}) collective-permute-start(bf16[96,1024]{1,0:T(8,128)(2,1)S(1)} %add_convert_fusion.1), channel_id=1, source_target_pairs={{0,4},{4,8},{8,12},{12,0},{1,5},{5,9},{9,13},{13,1},{2,6},{6,10},{... | collective-permute-start | bytes 589832 | tf_op jit(solution)/shard_map/ppermute | solution.py:215
  48.5 1.7 %collective-permute-done.12 = bf16[96,1024]{1,0:T(8,128)(2,1)S(1)} collective-permute-done((bf16[96,1024]{1,0:T(8,128)(2,1)S(1)}, bf16[96,1024]{1,0:T(8,128)(2,1)S(1)}, u32[]{:S(2)}, u32[]{:S(2)}) %collective-permute-start.12) | collective-permute-done | bytes 196640 | tf_op jit(solution)/shard_map/ppermute | solution.py:215
  50.2 4.3 %collective-permute-start.13 = (bf16[96,1024]{1,0:T(8,128)(2,1)S(1)}, bf16[96,1024]{1,0:T(8,128)(2,1)S(1)}, u32[]{:S(2)}, u32[]{:S(2)}) collective-permute-start(bf16[96,1024]{1,0:T(8,128)(2,1)S(1)} %add_convert_fusion.2), channel_id=1, source_target_pairs={{0,12},{4,0},{8,4},{12,8},{1,13},{5,1},{9,5},{13,9},{2,14},{6,2},{... | collective-permute-start | bytes 589832 | tf_op jit(solution)/shard_map/ppermute | solution.py:215
  54.5 0.5 collective-permute-done.9
  55.1 1.8 %collective-permute-start.10 = (bf16[96,1024]{1,0:T(8,128)(2,1)S(1)}, bf16[96,1024]{1,0:T(8,128)(2,1)S(1)}, u32[]{:S(2)}, u32[]{:S(2)}) collective-permute-start(bf16[96,1024]{1,0:T(8,128)(2,1)S(1)} %add_convert_fusion.3), channel_id=1, source_target_pairs={{0,4},{4,8},{8,12},{12,0},{1,5},{5,9},{9,13},{13,1},{2,6},{6,10},{... | collective-permute-start | bytes 589832 | tf_op jit(solution)/shard_map/ppermute | solution.py:215
  56.9 1.7 %collective-permute-done.19.arrived_ref = bf16[96,1024]{1,0:T(8,128)(2,1)S(1)} collective-permute-done((bf16[96,1024]{1,0:T(8,128)(2,1)S(1)}, bf16[96,1024]{1,0:T(8,128)(2,1)S(1)}, u32[]{:S(2)}, u32[]{:S(2)}) %collective-permute-start.19) | collective-permute-done | bytes 196640 | tf_op jit(solution)/shard_map/ppermute | solution.py:215
  58.6 0.8 %shard_map.67.refs_0_ = bf16[96,4096]{1,0:T(8,128)(2,1)} custom-call(bf16[96,1024]{1,0:T(8,128)(2,1)S(1)} %collective-permute-done.19.arrived_ref, f32[192,1024]{1,0:T(8,128)S(1)} %get-tuple-element.42.kept_ref), custom_call_target="tpu_custom_call" | custom-call | tf_op jit(solution)/shard_map/pallas_call | solution.py:337
  59.4 4.2 %collective-permute-done.16.arrived_ref = bf16[96,1024]{1,0:T(8,128)(2,1)S(1)} collective-permute-done((bf16[96,1024]{1,0:T(8,128)(2,1)S(1)}, bf16[96,1024]{1,0:T(8,128)(2,1)S(1)}, u32[]{:S(2)}, u32[]{:S(2)}) %collective-permute-start.16) | collective-permute-done | bytes 196640 | tf_op jit(solution)/shard_map/ppermute | solution.py:215
  63.5 0.8 %shard_map.68.refs_0_ = bf16[96,4096]{1,0:T(8,128)(2,1)} custom-call(bf16[96,1024]{1,0:T(8,128)(2,1)S(1)} %collective-permute-done.16.arrived_ref, f32[192,1024]{1,0:T(8,128)S(1)} %get-tuple-element.39.kept_ref, bf16[96,4096]{1,0:T(8,128)(2,1)} %shard_map.67.refs_0_), custom_call_target="tpu_custom_call", output_to_operand_aliasing={{}: (2, {})} | custom-call | tf_op jit(solution)/shard_map/pallas_call | solution.py:337
  64.3 2.8 %collective-permute-done.13.arrived_ref = bf16[96,1024]{1,0:T(8,128)(2,1)S(1)} collective-permute-done((bf16[96,1024]{1,0:T(8,128)(2,1)S(1)}, bf16[96,1024]{1,0:T(8,128)(2,1)S(1)}, u32[]{:S(2)}, u32[]{:S(2)}) %collective-permute-start.13) | collective-permute-done | bytes 196640 | tf_op jit(solution)/shard_map/ppermute | solution.py:215
  67.1 0.8 %shard_map.69.refs_0_ = bf16[96,4096]{1,0:T(8,128)(2,1)} custom-call(bf16[96,1024]{1,0:T(8,128)(2,1)S(1)} %collective-permute-done.13.arrived_ref, f32[192,1024]{1,0:T(8,128)S(1)} %get-tuple-element.37.kept_ref, bf16[96,4096]{1,0:T(8,128)(2,1)} %shard_map.68.refs_0_), custom_call_target="tpu_custom_call", output_to_operand_aliasing={{}: (2, {})} | custom-call | tf_op jit(solution)/shard_map/pallas_call | solution.py:337
  67.8 3.5 %collective-permute-done.10.arrived_ref = bf16[96,1024]{1,0:T(8,128)(2,1)S(1)} collective-permute-done((bf16[96,1024]{1,0:T(8,128)(2,1)S(1)}, bf16[96,1024]{1,0:T(8,128)(2,1)S(1)}, u32[]{:S(2)}, u32[]{:S(2)}) %collective-permute-start.10) | collective-permute-done | bytes 196640 | tf_op jit(solution)/shard_map/ppermute | solution.py:215
  71.3 0.8 %shard_map.70 = bf16[96,4096]{1,0:T(8,128)(2,1)} custom-call(bf16[96,1024]{1,0:T(8,128)(2,1)S(1)} %collective-permute-done.10.arrived_ref, f32[192,1024]{1,0:T(8,128)S(1)} %get-tuple-element.35.kept_ref, bf16[96,4096]{1,0:T(8,128)(2,1)} %shard_map.69.refs_0_), custom_call_target="tpu_custom_call", output_to_operand_aliasing={{}: (2, {})} | custom-call | tf_op jit(solution)/shard_map/pallas_call | solution.py:337
  (27 shorter events, 0.3 us)
Async XLA Ops:
  0.0 14.2 %slice-start = ((s8[8388608]{0:T(1024)(128)(4,1)}), s8[4194304]{0:T(1024)(128)(4,1)S(1)}, s32[]{:S(2)}) async-start(s8[8388608]{0:T(1024)(128)(4,1)} %bitcast.1), calls=%async_computation | async-start | bytes 8388608
  0.0 1.2 %copy-start.3 = (f32[64,32,32]{0,2,1:T(8,128)S(1)}, f32[64,32,32]{0,2,1:T(8,128)}, u32[]{:S(2)}) copy-start(f32[64,32,32]{0,2,1:T(8,128)} %param.5) | copy-start | bytes 786436
  1.2 7.0 %copy-start = (f32[9,64,64]{2,1,0:T(8,128)S(1)}, f32[9,64,64]{2,1,0:T(8,128)}, u32[]{:S(2)}) copy-start(f32[9,64,64]{2,1,0:T(8,128)} %first_ref.1) | copy-start | bytes 442372
  1.2 7.0 %copy-start.1 = (f32[9,64,64]{2,1,0:T(8,128)S(1)}, f32[9,64,64]{2,1,0:T(8,128)}, u32[]{:S(2)}) copy-start(f32[9,64,64]{2,1,0:T(8,128)} %second_ref.1) | copy-start | bytes 442372
  1.2 7.0 %copy-start.2 = (bf16[256,384]{1,0:T(8,128)(2,1)S(1)}, bf16[256,384]{1,0:T(8,128)(2,1)}, u32[]{:S(2)}) copy-start(bf16[256,384]{1,0:T(8,128)(2,1)} %embed_ref.1) | copy-start | bytes 589828
  1.2 13.0 %slice-start.1 = ((s8[8388608]{0:T(1024)(128)(4,1)}), s8[4194304]{0:T(1024)(128)(4,1)S(1)}, s32[]{:S(2)}) async-start(s8[8388608]{0:T(1024)(128)(4,1)} %bitcast.1), calls=%async_computation.1 | async-start | bytes 8388608
  1.3 7.4 %collective-permute-start.1 = (bf16[16,32,128]{2,1,0:T(8,128)(2,1)S(1)}, bf16[16,32,128]{2,1,0:T(8,128)(2,1)S(1)}, u32[]{:S(2)}, u32[]{:S(2)}) collective-permute-start(bf16[16,32,128]{2,1,0:T(8,128)(2,1)S(1)} %get-tuple-element.24.refs_0_), channel_id=1, source_target_pairs={{0,2},{2,0},{1,3},{3,1},{4,6},{6,4},{5,7},{7,5},{8,10},{10,8},{9,1... | collective-permute-start | bytes 393224 | tf_op jit(solution)/shard_map/ppermute | solution.py:215
  4.3 5.4 %collective-permute-start.3 = (bf16[1,32,128]{2,1,0:T(8,128)(2,1)S(1)}, bf16[1,32,128]{2,1,0:T(8,128)(2,1)S(1)}, u32[]{:S(2)}, u32[]{:S(2)}) collective-permute-start(bf16[1,32,128]{2,1,0:T(8,128)(2,1)S(1)} %get-tuple-element.25), channel_id=1, source_target_pairs={{0,4},{4,8},{8,12},{12,0},{1,5},{5,9},{9,13},{13,1},{2,6},{6,10},{... | collective-permute-start | bytes 24584 | tf_op jit(solution)/shard_map/ppermute | solution.py:215
  5.9 5.8 %collective-permute-start = (bf16[16,32,128]{2,1,0:T(8,128)(2,1)S(1)}, bf16[16,32,128]{2,1,0:T(8,128)(2,1)S(1)}, u32[]{:S(2)}, u32[]{:S(2)}) collective-permute-start(bf16[16,32,128]{2,1,0:T(8,128)(2,1)S(1)} %get-tuple-element.24.refs_0_), channel_id=1, source_target_pairs={{0,1},{1,0},{2,3},{3,2},{4,5},{5,4},{6,7},{7,6},{8,9},{9,8},{10,11... | collective-permute-start | bytes 393224 | tf_op jit(solution)/shard_map/ppermute | solution.py:215
  5.9 3.9 %collective-permute-start.4 = (bf16[1,32,128]{2,1,0:T(8,128)(2,1)S(1)}, bf16[1,32,128]{2,1,0:T(8,128)(2,1)S(1)}, u32[]{:S(2)}, u32[]{:S(2)}) collective-permute-start(bf16[1,32,128]{2,1,0:T(8,128)(2,1)S(1)} %get-tuple-element.26), channel_id=1, source_target_pairs={{0,12},{4,0},{8,4},{12,8},{1,13},{5,1},{9,5},{13,9},{2,14},{6,2},{... | collective-permute-start | bytes 24584 | tf_op jit(solution)/shard_map/ppermute | solution.py:215
  8.8 3.0 %collective-permute-start.2 = (bf16[16,32,128]{2,1,0:T(8,128)(2,1)S(1)}, bf16[16,32,128]{2,1,0:T(8,128)(2,1)S(1)}, u32[]{:S(2)}, u32[]{:S(2)}) collective-permute-start(bf16[16,32,128]{2,1,0:T(8,128)(2,1)S(1)} %collective-permute-done.1.refs_2_), channel_id=1, source_target_pairs={{0,1},{1,0},{2,3},{3,2},{4,5},{5,4},{6,7},{7,6},{8,9},{9,8},{10,11... | collective-permute-start | bytes 393224 | tf_op jit(solution)/shard_map/ppermute | solution.py:215
  9.8 4.4 %collective-permute-start.5 = (bf16[2,32,128]{2,1,0:T(8,128)(2,1)S(1)}, bf16[2,32,128]{2,1,0:T(8,128)(2,1)S(1)}, u32[]{:S(2)}, u32[]{:S(2)}) collective-permute-start(bf16[2,32,128]{2,1,0:T(8,128)(2,1)S(1)} %constant_dynamic-update-slice_fusion.refs_0_), channel_id=1, source_target_pairs={{0,1},{1,0},{2,3},{3,2},{4,5},{5,4},{6,7},{7,6},{8,9},{9,8},{10,11... | collective-permute-start | bytes 49160 | tf_op jit(solution)/shard_map/ppermute | solution.py:234
  9.9 4.3 %collective-permute-start.6 = (bf16[2,32,128]{2,1,0:T(8,128)(2,1)S(1)}, bf16[2,32,128]{2,1,0:T(8,128)(2,1)S(1)}, u32[]{:S(2)}, u32[]{:S(2)}) collective-permute-start(bf16[2,32,128]{2,1,0:T(8,128)(2,1)S(1)} %constant_dynamic-update-slice_fusion.refs_0_), channel_id=1, source_target_pairs={{0,2},{1,3},{2,0},{3,1},{4,6},{5,7},{6,4},{7,5},{8,10},{9,11},{10,... | collective-permute-start | bytes 49160 | tf_op jit(solution)/shard_map/ppermute | solution.py:234
  10.2 3.9 %collective-permute-start.7 = (bf16[2,32,128]{2,1,0:T(8,128)(2,1)S(1)}, bf16[2,32,128]{2,1,0:T(8,128)(2,1)S(1)}, u32[]{:S(2)}, u32[]{:S(2)}) collective-permute-start(bf16[2,32,128]{2,1,0:T(8,128)(2,1)S(1)} %constant_dynamic-update-slice_fusion.refs_0_), channel_id=1, source_target_pairs={{0,3},{1,2},{2,1},{3,0},{4,7},{5,6},{6,5},{7,4},{8,11},{9,10},{10,... | collective-permute-start | bytes 49160 | tf_op jit(solution)/shard_map/ppermute | solution.py:234
  15.6 9.2 %collective-permute-start.17 = (bf16[96,1024]{1,0:T(8,128)(2,1)S(1)}, bf16[96,1024]{1,0:T(8,128)(2,1)S(1)}, u32[]{:S(2)}, u32[]{:S(2)}) collective-permute-start(bf16[96,1024]{1,0:T(8,128)(2,1)S(1)} %get-tuple-element.40), channel_id=1, source_target_pairs={{0,12},{4,0},{8,4},{12,8},{1,13},{5,1},{9,5},{13,9},{2,14},{6,2},{... | collective-permute-start | bytes 589832 | tf_op jit(solution)/shard_map/ppermute | solution.py:215
  19.9 9.9 %collective-permute-start.14 = (bf16[96,1024]{1,0:T(8,128)(2,1)S(1)}, bf16[96,1024]{1,0:T(8,128)(2,1)S(1)}, u32[]{:S(2)}, u32[]{:S(2)}) collective-permute-start(bf16[96,1024]{1,0:T(8,128)(2,1)S(1)} %shard_map.64), channel_id=1, source_target_pairs={{0,4},{4,8},{8,12},{12,0},{1,5},{5,9},{9,13},{13,1},{2,6},{6,10},{... | collective-permute-start | bytes 589832 | tf_op jit(solution)/shard_map/ppermute | solution.py:215
  20.4 12.8 %collective-permute-start.11 = (bf16[96,1024]{1,0:T(8,128)(2,1)S(1)}, bf16[96,1024]{1,0:T(8,128)(2,1)S(1)}, u32[]{:S(2)}, u32[]{:S(2)}) collective-permute-start(bf16[96,1024]{1,0:T(8,128)(2,1)S(1)} %shard_map.62), channel_id=1, source_target_pairs={{0,12},{4,0},{8,4},{12,8},{1,13},{5,1},{9,5},{13,9},{2,14},{6,2},{... | collective-permute-start | bytes 589832 | tf_op jit(solution)/shard_map/ppermute | solution.py:215
  24.8 13.5 %collective-permute-start.8 = (bf16[96,1024]{1,0:T(8,128)(2,1)S(1)}, bf16[96,1024]{1,0:T(8,128)(2,1)S(1)}, u32[]{:S(2)}, u32[]{:S(2)}) collective-permute-start(bf16[96,1024]{1,0:T(8,128)(2,1)S(1)} %shard_map.60), channel_id=1, source_target_pairs={{0,4},{4,8},{8,12},{12,0},{1,5},{5,9},{9,13},{13,1},{2,6},{6,10},{... | collective-permute-start | bytes 589832 | tf_op jit(solution)/shard_map/ppermute | solution.py:215
  25.6 16.0 %collective-permute-start.18 = (bf16[96,1024]{1,0:T(8,128)(2,1)S(1)}, bf16[96,1024]{1,0:T(8,128)(2,1)S(1)}, u32[]{:S(2)}, u32[]{:S(2)}) collective-permute-start(bf16[96,1024]{1,0:T(8,128)(2,1)S(1)} %get-tuple-element.41), channel_id=1, source_target_pairs={{0,12},{4,0},{8,4},{12,8},{1,13},{5,1},{9,5},{13,9},{2,14},{6,2},{... | collective-permute-start | bytes 589832 | tf_op jit(solution)/shard_map/ppermute | solution.py:215
  30.6 16.0 %collective-permute-start.15 = (bf16[96,1024]{1,0:T(8,128)(2,1)S(1)}, bf16[96,1024]{1,0:T(8,128)(2,1)S(1)}, u32[]{:S(2)}, u32[]{:S(2)}) collective-permute-start(bf16[96,1024]{1,0:T(8,128)(2,1)S(1)} %get-tuple-element.38), channel_id=1, source_target_pairs={{0,4},{4,8},{8,12},{12,0},{1,5},{5,9},{9,13},{13,1},{2,6},{6,10},{... | collective-permute-start | bytes 589832 | tf_op jit(solution)/shard_map/ppermute | solution.py:215
  34.0 16.2 %collective-permute-start.12 = (bf16[96,1024]{1,0:T(8,128)(2,1)S(1)}, bf16[96,1024]{1,0:T(8,128)(2,1)S(1)}, u32[]{:S(2)}, u32[]{:S(2)}) collective-permute-start(bf16[96,1024]{1,0:T(8,128)(2,1)S(1)} %get-tuple-element.36), channel_id=1, source_target_pairs={{0,12},{4,0},{8,4},{12,8},{1,13},{5,1},{9,5},{13,9},{2,14},{6,2},{... | collective-permute-start | bytes 589832 | tf_op jit(solution)/shard_map/ppermute | solution.py:215
  39.1 16.0 %collective-permute-start.9 = (bf16[96,1024]{1,0:T(8,128)(2,1)S(1)}, bf16[96,1024]{1,0:T(8,128)(2,1)S(1)}, u32[]{:S(2)}, u32[]{:S(2)}) collective-permute-start(bf16[96,1024]{1,0:T(8,128)(2,1)S(1)} %get-tuple-element.34), channel_id=1, source_target_pairs={{0,4},{4,8},{8,12},{12,0},{1,5},{5,9},{9,13},{13,1},{2,6},{6,10},{... | collective-permute-start | bytes 589832 | tf_op jit(solution)/shard_map/ppermute | solution.py:215
  41.7 16.9 %collective-permute-start.19 = (bf16[96,1024]{1,0:T(8,128)(2,1)S(1)}, bf16[96,1024]{1,0:T(8,128)(2,1)S(1)}, u32[]{:S(2)}, u32[]{:S(2)}) collective-permute-start(bf16[96,1024]{1,0:T(8,128)(2,1)S(1)} %add_convert_fusion), channel_id=1, source_target_pairs={{0,12},{4,0},{8,4},{12,8},{1,13},{5,1},{9,5},{13,9},{2,14},{6,2},{... | collective-permute-start | bytes 589832 | tf_op jit(solution)/shard_map/ppermute | solution.py:215
  46.6 16.9 %collective-permute-start.16 = (bf16[96,1024]{1,0:T(8,128)(2,1)S(1)}, bf16[96,1024]{1,0:T(8,128)(2,1)S(1)}, u32[]{:S(2)}, u32[]{:S(2)}) collective-permute-start(bf16[96,1024]{1,0:T(8,128)(2,1)S(1)} %add_convert_fusion.1), channel_id=1, source_target_pairs={{0,4},{4,8},{8,12},{12,0},{1,5},{5,9},{9,13},{13,1},{2,6},{6,10},{... | collective-permute-start | bytes 589832 | tf_op jit(solution)/shard_map/ppermute | solution.py:215
  50.2 16.9 %collective-permute-start.13 = (bf16[96,1024]{1,0:T(8,128)(2,1)S(1)}, bf16[96,1024]{1,0:T(8,128)(2,1)S(1)}, u32[]{:S(2)}, u32[]{:S(2)}) collective-permute-start(bf16[96,1024]{1,0:T(8,128)(2,1)S(1)} %add_convert_fusion.2), channel_id=1, source_target_pairs={{0,12},{4,0},{8,4},{12,8},{1,13},{5,1},{9,5},{13,9},{2,14},{6,2},{... | collective-permute-start | bytes 589832 | tf_op jit(solution)/shard_map/ppermute | solution.py:215
  55.1 16.2 %collective-permute-start.10 = (bf16[96,1024]{1,0:T(8,128)(2,1)S(1)}, bf16[96,1024]{1,0:T(8,128)(2,1)S(1)}, u32[]{:S(2)}, u32[]{:S(2)}) collective-permute-start(bf16[96,1024]{1,0:T(8,128)(2,1)S(1)} %add_convert_fusion.3), channel_id=1, source_target_pairs={{0,4},{4,8},{8,12},{12,0},{1,5},{5,9},{9,13},{13,1},{2,6},{6,10},{... | collective-permute-start | bytes 589832 | tf_op jit(solution)/shard_map/ppermute | solution.py:215

commit v26 on v24

--- a/solution.py
+++ b/solution.py
@@ -7,7 +7,7 @@
 from jax.experimental.pallas import tpu as pltpu
 from jax.sharding import PartitionSpec as P
 
-PIECES = 4
+PIECES = 2
 STEP = 256
 LANES = 128
 PACK_COST = 20 * 10**9

time: 71.3 us -> 71.3 us (level)
  waiting for transfers between devices: 12.8 us -> 29.4 us
  starting transfers between devices: 44.8 us -> 30.2 us
  Pallas kernels: 12 us -> 10.2 us
    ppermute x17 -> x11, waiting for transfers between devices: 12.8 us -> 29.4 us  [turned(): lax.ppermute(value, axis, [(i, (i + away) % count) for i in range(count)])]
    ppermute x17 -> x11, starting transfers between devices: 42.8 us -> 28.3 us  [turned(): lax.ppermute(value, axis, [(i, (i + away) % count) for i in range(count)])]
    pallas_call x4 -> x2, Pallas kernels: 3.03 us -> 1.74 us  [finish(): pl.pallas_call(functools.partial(last_kernel, first), out_shape=jax.Shape...]
    pallas_call x12 -> x8, Pallas kernels: 8.99 us -> 8.41 us  [call(): pl.pallas_call(kernel, out_shape=out_shape, in_specs=[pl.BlockSpec(memory...]
  transfers between devices with their start and end apart: 20 -> 14, of which waited for: 5 -> 7; matrix products, arithmetic and copies ran while one was open for 0% -> 0% of each run, Pallas kernels for 14% -> 10%
where the time goes in v26:
time: 71.3 us; the launch traced here: 71.2 us
  starting transfers between devices  30.2 us (42%)
  waiting for transfers between devices  29.4 us (41%)
  Pallas kernels  10.2 us (14%)
  local copies, waits for them, and re-layouts  1.06 us (1%)
    ppermute x11, waiting for transfers between devices, turned(): lax.ppermute(value, axis, [(i, (i + away) % count) for i in range(count)])  29.4 us
    ppermute x11, starting transfers between devices, turned(): lax.ppermute(value, axis, [(i, (i + away) % count) for i in range(count)])  28.3 us
    pallas_call x8, Pallas kernels, call(): pl.pallas_call(kernel, out_shape=out_shape, in_specs=[pl.BlockSpec(memory...  8.41 us
    ppermute x3, starting transfers between devices, direct_blocks(): blocks.append(lax.ppermute(block, ('ch', 'sub'), route))  1.92 us
    pallas_call x2, Pallas kernels, finish(): pl.pallas_call(functools.partial(last_kernel, first), out_shape=jax.Shape...  1.74 us
  transfers between devices with their start and end apart: 14, of which 7 were waited for; matrix products, arithmetic and copies ran while one was open for 0% of the time, Pallas kernels for 10%

profile of v26, /device:TPU:0, one launch (start us, length us, event | category | flops | bytes accessed | tf_op | source)
XLA Modules:
  0.0 71.2 jit_solution(12253243104119328024)
XLA Ops:
  0.0 0.0 copy-start.4
  0.0 1.0 %copy-done.4 = f32[64,32,32]{0,2,1:T(8,128)S(1)} copy-done((f32[64,32,32]{0,2,1:T(8,128)S(1)}, f32[64,32,32]{0,2,1:T(8,128)}, u32[]{:S(2)}) %copy-start.4) | copy-done | bytes 262168
  1.0 0.0 copy-start.1
  1.0 0.0 copy-start.2
  1.0 0.0 copy-start
  1.1 0.1 shard_map.55
  1.2 3.0 %collective-permute-start.1 = (bf16[16,32,128]{2,1,0:T(8,128)(2,1)S(1)}, bf16[16,32,128]{2,1,0:T(8,128)(2,1)S(1)}, u32[]{:S(2)}, u32[]{:S(2)}) collective-permute-start(bf16[16,32,128]{2,1,0:T(8,128)(2,1)S(1)} %get-tuple-element.20.refs_0_), channel_id=1, source_target_pairs={{0,2},{2,0},{1,3},{3,1},{4,6},{6,4},{5,7},{7,5},{8,10},{10,8},{9,1... | collective-permute-start | bytes 393224 | tf_op jit(solution)/shard_map/ppermute | solution.py:215
  4.2 1.6 %collective-permute-start.3 = (bf16[1,32,128]{2,1,0:T(8,128)(2,1)S(1)}, bf16[1,32,128]{2,1,0:T(8,128)(2,1)S(1)}, u32[]{:S(2)}, u32[]{:S(2)}) collective-permute-start(bf16[1,32,128]{2,1,0:T(8,128)(2,1)S(1)} %get-tuple-element.21), channel_id=1, source_target_pairs={{0,4},{4,8},{8,12},{12,0},{1,5},{5,9},{9,13},{13,1},{2,6},{6,10},{... | collective-permute-start | bytes 24584 | tf_op jit(solution)/shard_map/ppermute | solution.py:215
  5.7 0.0 collective-permute-start
  5.7 2.2 %collective-permute-start.4 = (bf16[1,32,128]{2,1,0:T(8,128)(2,1)S(1)}, bf16[1,32,128]{2,1,0:T(8,128)(2,1)S(1)}, u32[]{:S(2)}, u32[]{:S(2)}) collective-permute-start(bf16[1,32,128]{2,1,0:T(8,128)(2,1)S(1)} %get-tuple-element.22), channel_id=1, source_target_pairs={{0,12},{4,0},{8,4},{12,8},{1,13},{5,1},{9,5},{13,9},{2,14},{6,2},{... | collective-permute-start | bytes 24584 | tf_op jit(solution)/shard_map/ppermute | solution.py:215
  8.0 0.0 copy-done.1
  8.0 0.0 copy-done.2
  8.0 0.0 copy-done.3
  8.0 0.6 shard_map.57
  8.6 0.0 collective-permute-done.1.refs_2_
  8.6 0.3 collective-permute-start.2
  8.9 0.7 %collective-permute-done.3 = bf16[1,32,128]{2,1,0:T(8,128)(2,1)S(1)} collective-permute-done((bf16[1,32,128]{2,1,0:T(8,128)(2,1)S(1)}, bf16[1,32,128]{2,1,0:T(8,128)(2,1)S(1)}, u32[]{:S(2)}, u32[]{:S(2)}) %collective-permute-start.3) | collective-permute-done | bytes 8224 | tf_op jit(solution)/shard_map/ppermute | solution.py:215
  9.6 0.0 collective-permute-done.4
  9.6 0.1 collective-permute-start.7
  9.7 1.2 %collective-permute-start.6 = (bf16[2,32,128]{2,1,0:T(8,128)(2,1)S(1)}, bf16[2,32,128]{2,1,0:T(8,128)(2,1)S(1)}, u32[]{:S(2)}, u32[]{:S(2)}) collective-permute-start(bf16[2,32,128]{2,1,0:T(8,128)(2,1)S(1)} %constant_dynamic-update-slice_fusion.refs_0_), channel_id=1, source_target_pairs={{0,2},{1,3},{2,0},{3,1},{4,6},{5,7},{6,4},{7,5},{8,10},{9,11},{10,... | collective-permute-start | bytes 49160 | tf_op jit(solution)/shard_map/ppermute | solution.py:234
  10.9 0.6 collective-permute-start.5
  11.6 0.0 collective-permute-done.refs_1_
  11.6 0.0 collective-permute-done.2.refs_3_
  11.6 2.3 %shard_map.58 = (bf16[384,768]{1,0:T(8,128)(2,1)S(1)}, bf16[4,128,128]{2,1,0:T(8,128)(2,1)S(1)}, bf16[4,128,128]{2,1,0:T(8,128)(2,1)S(1)}) custom-call(bf16[16,128,128]{2,1,0:T(8,128)(2,1)S(1)} %shard_map.56.field_ref, bf16[256,768]{1,0:T(8,128)(2,1)S(1)} %get-tuple-element.23.taps_one_ref.refs_6_, ...), custom_call_target="tpu_custom_call" | custom-call | flops 1635778560 | bytes 524288 | tf_op jit(solution)/shard_map/pallas_call | solution.py:202
  14.0 0.0 collective-permute-done.7.refs_3_
  14.0 0.0 collective-permute-done.6.refs_2_
  14.0 0.0 collective-permute-done.5.refs_1_
  14.0 0.0 copy-done
  14.0 1.8 %shard_map.59 = (bf16[384,1024]{1,0:T(8,128)(2,1)S(1)}, bf16[96,2048]{1,0:T(8,128)(2,1)S(1)}) custom-call(bf16[16,128,128]{2,1,0:T(8,128)(2,1)S(1)} %shard_map.56.field_ref, bf16[2,32,128]{2,1,0:T(8,128)(2,1)S(1)} %constant_dynamic-update-slice_fusion.refs_0_, bf16[2,32,128]{2,1,0:T(8,128)(2,1)S(1)} %collective-permute-done.5.refs_1_, ...), custom_call_target="tpu_custom_call" | custom-call | flops 503316480 | bytes 524288 | tf_op jit(solution)/shard_map/pallas_call | solution.py:202
  15.8 3.8 %collective-permute-start.11 = (bf16[96,2048]{1,0:T(8,128)(2,1)S(1)}, bf16[96,2048]{1,0:T(8,128)(2,1)S(1)}, u32[]{:S(2)}, u32[]{:S(2)}) collective-permute-start(bf16[96,2048]{1,0:T(8,128)(2,1)S(1)} %get-tuple-element.32), channel_id=1, source_target_pairs={{0,12},{4,0},{8,4},{12,8},{1,13},{5,1},{9,5},{13,9},{2,14},{6,2},{... | collective-permute-start | bytes 1179656 | tf_op jit(solution)/shard_map/ppermute | solution.py:215
  19.6 0.8 %shard_map.60 = bf16[96,2048]{1,0:T(8,128)(2,1)S(1)} custom-call(bf16[384,1024]{1,0:T(8,128)(2,1)S(1)} %get-tuple-element.29.tokens_ref, bf16[1024,4096]{1,0:T(8,128)(2,1)S(1)} %copy-done), custom_call_target="tpu_custom_call" | custom-call | tf_op jit(solution)/shard_map/pallas_call | solution.py:202
  20.4 0.1 collective-permute-start.8
  20.5 8.6 %collective-permute-done.11.arrived_ref = bf16[96,2048]{1,0:T(8,128)(2,1)S(1)} collective-permute-done((bf16[96,2048]{1,0:T(8,128)(2,1)S(1)}, bf16[96,2048]{1,0:T(8,128)(2,1)S(1)}, u32[]{:S(2)}, u32[]{:S(2)}) %collective-permute-start.11) | collective-permute-done | bytes 393248 | tf_op jit(solution)/shard_map/ppermute | solution.py:215
  29.1 1.4 %shard_map.62 = (bf16[96,2048]{1,0:T(8,128)(2,1)S(1)}, f32[192,2048]{1,0:T(8,128)S(1)}) custom-call(bf16[96,2048]{1,0:T(8,128)(2,1)S(1)} %collective-permute-done.11.arrived_ref, bf16[384,1024]{1,0:T(8,128)(2,1)S(1)} %get-tuple-element.29.tokens_ref, bf16[1024,4096]{1,0:T(8,128)(2,1)S(1)} %copy-done), custom_call_target="tpu_custom_call" | custom-call | tf_op jit(solution)/shard_map/pallas_call | solution.py:202
  30.5 4.3 %collective-permute-start.12 = (bf16[96,2048]{1,0:T(8,128)(2,1)S(1)}, bf16[96,2048]{1,0:T(8,128)(2,1)S(1)}, u32[]{:S(2)}, u32[]{:S(2)}) collective-permute-start(bf16[96,2048]{1,0:T(8,128)(2,1)S(1)} %get-tuple-element.33), channel_id=1, source_target_pairs={{0,12},{4,0},{8,4},{12,8},{1,13},{5,1},{9,5},{13,9},{2,14},{6,2},{... | collective-permute-start | bytes 1179656 | tf_op jit(solution)/shard_map/ppermute | solution.py:215
  34.8 2.7 %collective-permute-done.8.arrived_ref = bf16[96,2048]{1,0:T(8,128)(2,1)S(1)} collective-permute-done((bf16[96,2048]{1,0:T(8,128)(2,1)S(1)}, bf16[96,2048]{1,0:T(8,128)(2,1)S(1)}, u32[]{:S(2)}, u32[]{:S(2)}) %collective-permute-start.8) | collective-permute-done | bytes 393248 | tf_op jit(solution)/shard_map/ppermute | solution.py:215
  37.5 1.4 %shard_map.61 = (bf16[96,2048]{1,0:T(8,128)(2,1)S(1)}, f32[192,2048]{1,0:T(8,128)S(1)}) custom-call(bf16[96,2048]{1,0:T(8,128)(2,1)S(1)} %collective-permute-done.8.arrived_ref, bf16[384,1024]{1,0:T(8,128)(2,1)S(1)} %get-tuple-element.29.tokens_ref, bf16[1024,4096]{1,0:T(8,128)(2,1)S(1)} %copy-done), custom_call_target="tpu_custom_call" | custom-call | tf_op jit(solution)/shard_map/pallas_call | solution.py:202
  38.9 4.3 %collective-permute-start.9 = (bf16[96,2048]{1,0:T(8,128)(2,1)S(1)}, bf16[96,2048]{1,0:T(8,128)(2,1)S(1)}, u32[]{:S(2)}, u32[]{:S(2)}) collective-permute-start(bf16[96,2048]{1,0:T(8,128)(2,1)S(1)} %get-tuple-element.30), channel_id=1, source_target_pairs={{0,12},{4,0},{8,4},{12,8},{1,13},{5,1},{9,5},{13,9},{2,14},{6,2},{... | collective-permute-start | bytes 1179656 | tf_op jit(solution)/shard_map/ppermute | solution.py:215
  43.2 2.7 %collective-permute-done.12 = bf16[96,2048]{1,0:T(8,128)(2,1)S(1)} collective-permute-done((bf16[96,2048]{1,0:T(8,128)(2,1)S(1)}, bf16[96,2048]{1,0:T(8,128)(2,1)S(1)}, u32[]{:S(2)}, u32[]{:S(2)}) %collective-permute-start.12) | collective-permute-done | bytes 393248 | tf_op jit(solution)/shard_map/ppermute | solution.py:215
  46.0 0.1 add_convert_fusion
  46.0 4.3 %collective-permute-start.13 = (bf16[96,2048]{1,0:T(8,128)(2,1)S(1)}, bf16[96,2048]{1,0:T(8,128)(2,1)S(1)}, u32[]{:S(2)}, u32[]{:S(2)}) collective-permute-start(bf16[96,2048]{1,0:T(8,128)(2,1)S(1)} %add_convert_fusion), channel_id=1, source_target_pairs={{0,12},{4,0},{8,4},{12,8},{1,13},{5,1},{9,5},{13,9},{2,14},{6,2},{... | collective-permute-start | bytes 1179656 | tf_op jit(solution)/shard_map/ppermute | solution.py:215
  50.4 4.0 %collective-permute-done.9 = bf16[96,2048]{1,0:T(8,128)(2,1)S(1)} collective-permute-done((bf16[96,2048]{1,0:T(8,128)(2,1)S(1)}, bf16[96,2048]{1,0:T(8,128)(2,1)S(1)}, u32[]{:S(2)}, u32[]{:S(2)}) %collective-permute-start.9) | collective-permute-done | bytes 393248 | tf_op jit(solution)/shard_map/ppermute | solution.py:215
  54.4 0.1 add_convert_fusion.1
  54.5 4.3 %collective-permute-start.10 = (bf16[96,2048]{1,0:T(8,128)(2,1)S(1)}, bf16[96,2048]{1,0:T(8,128)(2,1)S(1)}, u32[]{:S(2)}, u32[]{:S(2)}) collective-permute-start(bf16[96,2048]{1,0:T(8,128)(2,1)S(1)} %add_convert_fusion.1), channel_id=1, source_target_pairs={{0,12},{4,0},{8,4},{12,8},{1,13},{5,1},{9,5},{13,9},{2,14},{6,2},{... | collective-permute-start | bytes 1179656 | tf_op jit(solution)/shard_map/ppermute | solution.py:215
  58.8 4.0 %collective-permute-done.13.arrived_ref = bf16[96,2048]{1,0:T(8,128)(2,1)S(1)} collective-permute-done((bf16[96,2048]{1,0:T(8,128)(2,1)S(1)}, bf16[96,2048]{1,0:T(8,128)(2,1)S(1)}, u32[]{:S(2)}, u32[]{:S(2)}) %collective-permute-start.13) | collective-permute-done | bytes 393248 | tf_op jit(solution)/shard_map/ppermute | solution.py:215
  62.8 0.9 %shard_map.63.refs_0_ = bf16[96,4096]{1,0:T(8,128)(2,1)} custom-call(bf16[96,2048]{1,0:T(8,128)(2,1)S(1)} %collective-permute-done.13.arrived_ref, f32[192,2048]{1,0:T(8,128)S(1)} %get-tuple-element.34.kept_ref), custom_call_target="tpu_custom_call" | custom-call | tf_op jit(solution)/shard_map/pallas_call | solution.py:337
  63.7 6.6 %collective-permute-done.10.arrived_ref = bf16[96,2048]{1,0:T(8,128)(2,1)S(1)} collective-permute-done((bf16[96,2048]{1,0:T(8,128)(2,1)S(1)}, bf16[96,2048]{1,0:T(8,128)(2,1)S(1)}, u32[]{:S(2)}, u32[]{:S(2)}) %collective-permute-start.10) | collective-permute-done | bytes 393248 | tf_op jit(solution)/shard_map/ppermute | solution.py:215
  70.3 0.9 %shard_map.64 = bf16[96,4096]{1,0:T(8,128)(2,1)} custom-call(bf16[96,2048]{1,0:T(8,128)(2,1)S(1)} %collective-permute-done.10.arrived_ref, f32[192,2048]{1,0:T(8,128)S(1)} %get-tuple-element.31.kept_ref, bf16[96,4096]{1,0:T(8,128)(2,1)} %shard_map.63.refs_0_), custom_call_target="tpu_custom_call", output_to_operand_aliasing={{}: (2, {})} | custom-call | tf_op jit(solution)/shard_map/pallas_call | solution.py:337
  (4 shorter events, 0.1 us)
Async XLA Ops:
  0.0 1.0 %copy-start.4 = (f32[64,32,32]{0,2,1:T(8,128)S(1)}, f32[64,32,32]{0,2,1:T(8,128)}, u32[]{:S(2)}) copy-start(f32[64,32,32]{0,2,1:T(8,128)} %param.5) | copy-start | bytes 786436
  1.0 7.0 %copy-start.1 = (f32[9,64,64]{2,1,0:T(8,128)S(1)}, f32[9,64,64]{2,1,0:T(8,128)}, u32[]{:S(2)}) copy-start(f32[9,64,64]{2,1,0:T(8,128)} %first_ref.1) | copy-start | bytes 442372
  1.0 7.0 %copy-start.2 = (f32[9,64,64]{2,1,0:T(8,128)S(1)}, f32[9,64,64]{2,1,0:T(8,128)}, u32[]{:S(2)}) copy-start(f32[9,64,64]{2,1,0:T(8,128)} %second_ref.1) | copy-start | bytes 442372
  1.0 7.0 %copy-start.3 = (bf16[256,384]{1,0:T(8,128)(2,1)S(1)}, bf16[256,384]{1,0:T(8,128)(2,1)}, u32[]{:S(2)}) copy-start(bf16[256,384]{1,0:T(8,128)(2,1)} %embed_ref.1) | copy-start | bytes 589828
  1.0 13.0 %copy-start = (bf16[1024,4096]{1,0:T(8,128)(2,1)S(1)}, bf16[1024,4096]{1,0:T(8,128)(2,1)}, u32[]{:S(2)}) copy-start(bf16[1024,4096]{1,0:T(8,128)(2,1)} %mixing_ref.5) | copy-start | bytes 25165828
  1.2 7.4 %collective-permute-start.1 = (bf16[16,32,128]{2,1,0:T(8,128)(2,1)S(1)}, bf16[16,32,128]{2,1,0:T(8,128)(2,1)S(1)}, u32[]{:S(2)}, u32[]{:S(2)}) collective-permute-start(bf16[16,32,128]{2,1,0:T(8,128)(2,1)S(1)} %get-tuple-element.20.refs_0_), channel_id=1, source_target_pairs={{0,2},{2,0},{1,3},{3,1},{4,6},{6,4},{5,7},{7,5},{8,10},{10,8},{9,1... | collective-permute-start | bytes 393224 | tf_op jit(solution)/shard_map/ppermute | solution.py:215
  4.2 5.4 %collective-permute-start.3 = (bf16[1,32,128]{2,1,0:T(8,128)(2,1)S(1)}, bf16[1,32,128]{2,1,0:T(8,128)(2,1)S(1)}, u32[]{:S(2)}, u32[]{:S(2)}) collective-permute-start(bf16[1,32,128]{2,1,0:T(8,128)(2,1)S(1)} %get-tuple-element.21), channel_id=1, source_target_pairs={{0,4},{4,8},{8,12},{12,0},{1,5},{5,9},{9,13},{13,1},{2,6},{6,10},{... | collective-permute-start | bytes 24584 | tf_op jit(solution)/shard_map/ppermute | solution.py:215
  5.7 5.8 %collective-permute-start = (bf16[16,32,128]{2,1,0:T(8,128)(2,1)S(1)}, bf16[16,32,128]{2,1,0:T(8,128)(2,1)S(1)}, u32[]{:S(2)}, u32[]{:S(2)}) collective-permute-start(bf16[16,32,128]{2,1,0:T(8,128)(2,1)S(1)} %get-tuple-element.20.refs_0_), channel_id=1, source_target_pairs={{0,1},{1,0},{2,3},{3,2},{4,5},{5,4},{6,7},{7,6},{8,9},{9,8},{10,11... | collective-permute-start | bytes 393224 | tf_op jit(solution)/shard_map/ppermute | solution.py:215
  5.7 3.9 %collective-permute-start.4 = (bf16[1,32,128]{2,1,0:T(8,128)(2,1)S(1)}, bf16[1,32,128]{2,1,0:T(8,128)(2,1)S(1)}, u32[]{:S(2)}, u32[]{:S(2)}) collective-permute-start(bf16[1,32,128]{2,1,0:T(8,128)(2,1)S(1)} %get-tuple-element.22), channel_id=1, source_target_pairs={{0,12},{4,0},{8,4},{12,8},{1,13},{5,1},{9,5},{13,9},{2,14},{6,2},{... | collective-permute-start | bytes 24584 | tf_op jit(solution)/shard_map/ppermute | solution.py:215
  8.6 3.0 %collective-permute-start.2 = (bf16[16,32,128]{2,1,0:T(8,128)(2,1)S(1)}, bf16[16,32,128]{2,1,0:T(8,128)(2,1)S(1)}, u32[]{:S(2)}, u32[]{:S(2)}) collective-permute-start(bf16[16,32,128]{2,1,0:T(8,128)(2,1)S(1)} %collective-permute-done.1.refs_2_), channel_id=1, source_target_pairs={{0,1},{1,0},{2,3},{3,2},{4,5},{5,4},{6,7},{7,6},{8,9},{9,8},{10,11... | collective-permute-start | bytes 393224 | tf_op jit(solution)/shard_map/ppermute | solution.py:215
  9.6 4.3 %collective-permute-start.7 = (bf16[2,32,128]{2,1,0:T(8,128)(2,1)S(1)}, bf16[2,32,128]{2,1,0:T(8,128)(2,1)S(1)}, u32[]{:S(2)}, u32[]{:S(2)}) collective-permute-start(bf16[2,32,128]{2,1,0:T(8,128)(2,1)S(1)} %constant_dynamic-update-slice_fusion.refs_0_), channel_id=1, source_target_pairs={{0,3},{1,2},{2,1},{3,0},{4,7},{5,6},{6,5},{7,4},{8,11},{9,10},{10,... | collective-permute-start | bytes 49160 | tf_op jit(solution)/shard_map/ppermute | solution.py:234
  9.7 4.3 %collective-permute-start.6 = (bf16[2,32,128]{2,1,0:T(8,128)(2,1)S(1)}, bf16[2,32,128]{2,1,0:T(8,128)(2,1)S(1)}, u32[]{:S(2)}, u32[]{:S(2)}) collective-permute-start(bf16[2,32,128]{2,1,0:T(8,128)(2,1)S(1)} %constant_dynamic-update-slice_fusion.refs_0_), channel_id=1, source_target_pairs={{0,2},{1,3},{2,0},{3,1},{4,6},{5,7},{6,4},{7,5},{8,10},{9,11},{10,... | collective-permute-start | bytes 49160 | tf_op jit(solution)/shard_map/ppermute | solution.py:234
  10.9 3.1 %collective-permute-start.5 = (bf16[2,32,128]{2,1,0:T(8,128)(2,1)S(1)}, bf16[2,32,128]{2,1,0:T(8,128)(2,1)S(1)}, u32[]{:S(2)}, u32[]{:S(2)}) collective-permute-start(bf16[2,32,128]{2,1,0:T(8,128)(2,1)S(1)} %constant_dynamic-update-slice_fusion.refs_0_), channel_id=1, source_target_pairs={{0,1},{1,0},{2,3},{3,2},{4,5},{5,4},{6,7},{7,6},{8,9},{9,8},{10,11... | collective-permute-start | bytes 49160 | tf_op jit(solution)/shard_map/ppermute | solution.py:234
  15.8 13.3 %collective-permute-start.11 = (bf16[96,2048]{1,0:T(8,128)(2,1)S(1)}, bf16[96,2048]{1,0:T(8,128)(2,1)S(1)}, u32[]{:S(2)}, u32[]{:S(2)}) collective-permute-start(bf16[96,2048]{1,0:T(8,128)(2,1)S(1)} %get-tuple-element.32), channel_id=1, source_target_pairs={{0,12},{4,0},{8,4},{12,8},{1,13},{5,1},{9,5},{13,9},{2,14},{6,2},{... | collective-permute-start | bytes 1179656 | tf_op jit(solution)/shard_map/ppermute | solution.py:215
  20.4 17.1 %collective-permute-start.8 = (bf16[96,2048]{1,0:T(8,128)(2,1)S(1)}, bf16[96,2048]{1,0:T(8,128)(2,1)S(1)}, u32[]{:S(2)}, u32[]{:S(2)}) collective-permute-start(bf16[96,2048]{1,0:T(8,128)(2,1)S(1)} %shard_map.60), channel_id=1, source_target_pairs={{0,12},{4,0},{8,4},{12,8},{1,13},{5,1},{9,5},{13,9},{2,14},{6,2},{... | collective-permute-start | bytes 1179656 | tf_op jit(solution)/shard_map/ppermute | solution.py:215
  30.5 15.5 %collective-permute-start.12 = (bf16[96,2048]{1,0:T(8,128)(2,1)S(1)}, bf16[96,2048]{1,0:T(8,128)(2,1)S(1)}, u32[]{:S(2)}, u32[]{:S(2)}) collective-permute-start(bf16[96,2048]{1,0:T(8,128)(2,1)S(1)} %get-tuple-element.33), channel_id=1, source_target_pairs={{0,12},{4,0},{8,4},{12,8},{1,13},{5,1},{9,5},{13,9},{2,14},{6,2},{... | collective-permute-start | bytes 1179656 | tf_op jit(solution)/shard_map/ppermute | solution.py:215
  38.9 15.5 %collective-permute-start.9 = (bf16[96,2048]{1,0:T(8,128)(2,1)S(1)}, bf16[96,2048]{1,0:T(8,128)(2,1)S(1)}, u32[]{:S(2)}, u32[]{:S(2)}) collective-permute-start(bf16[96,2048]{1,0:T(8,128)(2,1)S(1)} %get-tuple-element.30), channel_id=1, source_target_pairs={{0,12},{4,0},{8,4},{12,8},{1,13},{5,1},{9,5},{13,9},{2,14},{6,2},{... | collective-permute-start | bytes 1179656 | tf_op jit(solution)/shard_map/ppermute | solution.py:215
  46.0 16.8 %collective-permute-start.13 = (bf16[96,2048]{1,0:T(8,128)(2,1)S(1)}, bf16[96,2048]{1,0:T(8,128)(2,1)S(1)}, u32[]{:S(2)}, u32[]{:S(2)}) collective-permute-start(bf16[96,2048]{1,0:T(8,128)(2,1)S(1)} %add_convert_fusion), channel_id=1, source_target_pairs={{0,12},{4,0},{8,4},{12,8},{1,13},{5,1},{9,5},{13,9},{2,14},{6,2},{... | collective-permute-start | bytes 1179656 | tf_op jit(solution)/shard_map/ppermute | solution.py:215
  54.5 15.8 %collective-permute-start.10 = (bf16[96,2048]{1,0:T(8,128)(2,1)S(1)}, bf16[96,2048]{1,0:T(8,128)(2,1)S(1)}, u32[]{:S(2)}, u32[]{:S(2)}) collective-permute-start(bf16[96,2048]{1,0:T(8,128)(2,1)S(1)} %add_convert_fusion.1), channel_id=1, source_target_pairs={{0,12},{4,0},{8,4},{12,8},{1,13},{5,1},{9,5},{13,9},{2,14},{6,2},{... | collective-permute-start | bytes 1179656 | tf_op jit(solution)/shard_map/ppermute | solution.py:215

commit v27 on v24

--- a/solution.py
+++ b/solution.py
@@ -13,7 +13,7 @@
 PACK_COST = 20 * 10**9
 WRITES = 4
 VMEM_BYTES = 24 * 1024 * 1024
-ROWS_AT_ONCE = 640
+ROWS_AT_ONCE = 512
 
 
 def pack_kernel(field_ref, packed_ref, low_ref, high_ref):

time: 71.3 us -> 71.2 us (level)
  no operation moved by 1% of the time
where the time goes in v27:
time: 71.2 us; the launch traced here: 71.1 us
  starting transfers between devices  44.8 us (63%)
  waiting for transfers between devices  12.8 us (18%)
  Pallas kernels  12 us (17%)
  local copies, waits for them, and re-layouts  1.22 us (2%)
    ppermute x17, starting transfers between devices, turned(): lax.ppermute(value, axis, [(i, (i + away) % count) for i in range(count)])  42.8 us
    ppermute x17, waiting for transfers between devices, turned(): lax.ppermute(value, axis, [(i, (i + away) % count) for i in range(count)])  12.8 us
    pallas_call x12, Pallas kernels, call(): pl.pallas_call(kernel, out_shape=out_shape, in_specs=[pl.BlockSpec(memory...  8.93 us
    pallas_call x4, Pallas kernels, finish(): pl.pallas_call(functools.partial(last_kernel, first), out_shape=jax.Shape...  3.03 us
    ppermute x3, starting transfers between devices, direct_blocks(): blocks.append(lax.ppermute(block, ('ch', 'sub'), route))  1.93 us
  transfers between devices with their start and end apart: 20, of which 5 were waited for; matrix products, arithmetic and copies ran while one was open for 0% of the time, Pallas kernels for 14%

profile of v27, /device:TPU:0, one launch (start us, length us, event | category | flops | bytes accessed | tf_op | source)
XLA Modules:
  0.0 71.1 jit_solution(13269105292632466664)
XLA Ops:
  0.0 1.2 %copy-done.3 = f32[64,32,32]{0,2,1:T(8,128)S(1)} copy-done((f32[64,32,32]{0,2,1:T(8,128)S(1)}, f32[64,32,32]{0,2,1:T(8,128)}, u32[]{:S(2)}) %copy-start.3) | copy-done | bytes 262168
  1.2 0.1 shard_map.55
  1.3 3.0 %collective-permute-start.1 = (bf16[16,32,128]{2,1,0:T(8,128)(2,1)S(1)}, bf16[16,32,128]{2,1,0:T(8,128)(2,1)S(1)}, u32[]{:S(2)}, u32[]{:S(2)}) collective-permute-start(bf16[16,32,128]{2,1,0:T(8,128)(2,1)S(1)} %get-tuple-element.24.refs_0_), channel_id=1, source_target_pairs={{0,2},{2,0},{1,3},{3,1},{4,6},{6,4},{5,7},{7,5},{8,10},{10,8},{9,1... | collective-permute-start | bytes 393224 | tf_op jit(solution)/shard_map/ppermute | solution.py:215
  4.3 1.6 %collective-permute-start.3 = (bf16[1,32,128]{2,1,0:T(8,128)(2,1)S(1)}, bf16[1,32,128]{2,1,0:T(8,128)(2,1)S(1)}, u32[]{:S(2)}, u32[]{:S(2)}) collective-permute-start(bf16[1,32,128]{2,1,0:T(8,128)(2,1)S(1)} %get-tuple-element.25), channel_id=1, source_target_pairs={{0,4},{4,8},{8,12},{12,0},{1,5},{5,9},{9,13},{13,1},{2,6},{6,10},{... | collective-permute-start | bytes 24584 | tf_op jit(solution)/shard_map/ppermute | solution.py:215
  5.9 0.0 collective-permute-start
  5.9 2.2 %collective-permute-start.4 = (bf16[1,32,128]{2,1,0:T(8,128)(2,1)S(1)}, bf16[1,32,128]{2,1,0:T(8,128)(2,1)S(1)}, u32[]{:S(2)}, u32[]{:S(2)}) collective-permute-start(bf16[1,32,128]{2,1,0:T(8,128)(2,1)S(1)} %get-tuple-element.26), channel_id=1, source_target_pairs={{0,12},{4,0},{8,4},{12,8},{1,13},{5,1},{9,5},{13,9},{2,14},{6,2},{... | collective-permute-start | bytes 24584 | tf_op jit(solution)/shard_map/ppermute | solution.py:215
  8.2 0.6 shard_map.57
  8.8 0.3 collective-permute-start.2
  9.1 0.7 %collective-permute-done.3 = bf16[1,32,128]{2,1,0:T(8,128)(2,1)S(1)} collective-permute-done((bf16[1,32,128]{2,1,0:T(8,128)(2,1)S(1)}, bf16[1,32,128]{2,1,0:T(8,128)(2,1)S(1)}, u32[]{:S(2)}, u32[]{:S(2)}) %collective-permute-start.3) | collective-permute-done | bytes 8224 | tf_op jit(solution)/shard_map/ppermute | solution.py:215
  9.8 0.0 collective-permute-done.4
  9.8 0.1 collective-permute-start.5
  9.9 0.4 collective-permute-start.6
  10.2 1.5 %collective-permute-start.7 = (bf16[2,32,128]{2,1,0:T(8,128)(2,1)S(1)}, bf16[2,32,128]{2,1,0:T(8,128)(2,1)S(1)}, u32[]{:S(2)}, u32[]{:S(2)}) collective-permute-start(bf16[2,32,128]{2,1,0:T(8,128)(2,1)S(1)} %constant_dynamic-update-slice_fusion.refs_0_), channel_id=1, source_target_pairs={{0,3},{1,2},{2,1},{3,0},{4,7},{5,6},{6,5},{7,4},{8,11},{9,10},{10,... | collective-permute-start | bytes 49160 | tf_op jit(solution)/shard_map/ppermute | solution.py:234
  11.8 2.3 %shard_map.58 = (bf16[384,768]{1,0:T(8,128)(2,1)S(1)}, bf16[4,128,128]{2,1,0:T(8,128)(2,1)S(1)}, bf16[4,128,128]{2,1,0:T(8,128)(2,1)S(1)}) custom-call(bf16[16,128,128]{2,1,0:T(8,128)(2,1)S(1)} %shard_map.56.field_ref, bf16[256,768]{1,0:T(8,128)(2,1)S(1)} %get-tuple-element.27.taps_one_ref.refs_6_, ...), custom_call_target="tpu_custom_call" | custom-call | flops 1635778560 | bytes 524288 | tf_op jit(solution)/shard_map/pallas_call | solution.py:202
  14.1 0.0 collective-permute-done.5.refs_1_
  14.1 0.0 collective-permute-done.6.refs_2_
  14.1 1.4 %shard_map.59 = (bf16[384,1024]{1,0:T(8,128)(2,1)S(1)}, bf16[96,1024]{1,0:T(8,128)(2,1)S(1)}) custom-call(bf16[16,128,128]{2,1,0:T(8,128)(2,1)S(1)} %shard_map.56.field_ref, bf16[2,32,128]{2,1,0:T(8,128)(2,1)S(1)} %constant_dynamic-update-slice_fusion.refs_0_, bf16[2,32,128]{2,1,0:T(8,128)(2,1)S(1)} %collective-permute-done.5.refs_1_, ...), custom_call_target="tpu_custom_call" | custom-call | flops 503316480 | bytes 524288 | tf_op jit(solution)/shard_map/pallas_call | solution.py:202
  15.6 3.8 %collective-permute-start.17 = (bf16[96,1024]{1,0:T(8,128)(2,1)S(1)}, bf16[96,1024]{1,0:T(8,128)(2,1)S(1)}, u32[]{:S(2)}, u32[]{:S(2)}) collective-permute-start(bf16[96,1024]{1,0:T(8,128)(2,1)S(1)} %get-tuple-element.40), channel_id=1, source_target_pairs={{0,12},{4,0},{8,4},{12,8},{1,13},{5,1},{9,5},{13,9},{2,14},{6,2},{... | collective-permute-start | bytes 589832 | tf_op jit(solution)/shard_map/ppermute | solution.py:215
  19.4 0.5 shard_map.64
  19.8 0.1 collective-permute-start.14
  19.9 0.5 shard_map.62
  20.4 0.5 collective-permute-start.11
  20.9 0.5 shard_map.60
  21.3 0.8 %collective-permute-start.8 = (bf16[96,1024]{1,0:T(8,128)(2,1)S(1)}, bf16[96,1024]{1,0:T(8,128)(2,1)S(1)}, u32[]{:S(2)}, u32[]{:S(2)}) collective-permute-start(bf16[96,1024]{1,0:T(8,128)(2,1)S(1)} %shard_map.60), channel_id=1, source_target_pairs={{0,12},{4,0},{8,4},{12,8},{1,13},{5,1},{9,5},{13,9},{2,14},{6,2},{... | collective-permute-start | bytes 589832 | tf_op jit(solution)/shard_map/ppermute | solution.py:215
  22.1 2.5 %collective-permute-done.17.arrived_ref = bf16[96,1024]{1,0:T(8,128)(2,1)S(1)} collective-permute-done((bf16[96,1024]{1,0:T(8,128)(2,1)S(1)}, bf16[96,1024]{1,0:T(8,128)(2,1)S(1)}, u32[]{:S(2)}, u32[]{:S(2)}) %collective-permute-start.17) | collective-permute-done | bytes 196640 | tf_op jit(solution)/shard_map/ppermute | solution.py:215
  24.6 0.8 %shard_map.66 = (bf16[96,1024]{1,0:T(8,128)(2,1)S(1)}, f32[192,1024]{1,0:T(8,128)S(1)}) custom-call(bf16[96,1024]{1,0:T(8,128)(2,1)S(1)} %collective-permute-done.17.arrived_ref, bf16[384,1024]{1,0:T(8,128)(2,1)S(1)} %get-tuple-element.33.tokens_ref, bf16[1024,4096]{1,0:T(8,128)(2,1)S(1)} %bitcast.2), custom_call_target="tpu_custom_call" | custom-call | tf_op jit(solution)/shard_map/pallas_call | solution.py:202
  25.4 4.3 %collective-permute-start.18 = (bf16[96,1024]{1,0:T(8,128)(2,1)S(1)}, bf16[96,1024]{1,0:T(8,128)(2,1)S(1)}, u32[]{:S(2)}, u32[]{:S(2)}) collective-permute-start(bf16[96,1024]{1,0:T(8,128)(2,1)S(1)} %get-tuple-element.41), channel_id=1, source_target_pairs={{0,12},{4,0},{8,4},{12,8},{1,13},{5,1},{9,5},{13,9},{2,14},{6,2},{... | collective-permute-start | bytes 589832 | tf_op jit(solution)/shard_map/ppermute | solution.py:215
  29.7 0.8 %shard_map.65 = (bf16[96,1024]{1,0:T(8,128)(2,1)S(1)}, f32[192,1024]{1,0:T(8,128)S(1)}) custom-call(bf16[96,1024]{1,0:T(8,128)(2,1)S(1)} %collective-permute-done.14.arrived_ref, bf16[384,1024]{1,0:T(8,128)(2,1)S(1)} %get-tuple-element.33.tokens_ref, bf16[1024,4096]{1,0:T(8,128)(2,1)S(1)} %bitcast.2), custom_call_target="tpu_custom_call" | custom-call | tf_op jit(solution)/shard_map/pallas_call | solution.py:202
  30.5 3.4 %collective-permute-start.15 = (bf16[96,1024]{1,0:T(8,128)(2,1)S(1)}, bf16[96,1024]{1,0:T(8,128)(2,1)S(1)}, u32[]{:S(2)}, u32[]{:S(2)}) collective-permute-start(bf16[96,1024]{1,0:T(8,128)(2,1)S(1)} %get-tuple-element.38), channel_id=1, source_target_pairs={{0,12},{4,0},{8,4},{12,8},{1,13},{5,1},{9,5},{13,9},{2,14},{6,2},{... | collective-permute-start | bytes 589832 | tf_op jit(solution)/shard_map/ppermute | solution.py:215
  33.9 0.8 %shard_map.63 = (bf16[96,1024]{1,0:T(8,128)(2,1)S(1)}, f32[192,1024]{1,0:T(8,128)S(1)}) custom-call(bf16[96,1024]{1,0:T(8,128)(2,1)S(1)} %collective-permute-done.11.arrived_ref, bf16[384,1024]{1,0:T(8,128)(2,1)S(1)} %get-tuple-element.33.tokens_ref, bf16[1024,4096]{1,0:T(8,128)(2,1)S(1)} %bitcast.2), custom_call_target="tpu_custom_call" | custom-call | tf_op jit(solution)/shard_map/pallas_call | solution.py:202
  34.7 3.4 %collective-permute-start.12 = (bf16[96,1024]{1,0:T(8,128)(2,1)S(1)}, bf16[96,1024]{1,0:T(8,128)(2,1)S(1)}, u32[]{:S(2)}, u32[]{:S(2)}) collective-permute-start(bf16[96,1024]{1,0:T(8,128)(2,1)S(1)} %get-tuple-element.36), channel_id=1, source_target_pairs={{0,12},{4,0},{8,4},{12,8},{1,13},{5,1},{9,5},{13,9},{2,14},{6,2},{... | collective-permute-start | bytes 589832 | tf_op jit(solution)/shard_map/ppermute | solution.py:215
  38.1 0.8 %shard_map.61 = (bf16[96,1024]{1,0:T(8,128)(2,1)S(1)}, f32[192,1024]{1,0:T(8,128)S(1)}) custom-call(bf16[96,1024]{1,0:T(8,128)(2,1)S(1)} %collective-permute-done.8.arrived_ref, bf16[384,1024]{1,0:T(8,128)(2,1)S(1)} %get-tuple-element.33.tokens_ref, bf16[1024,4096]{1,0:T(8,128)(2,1)S(1)} %bitcast.2), custom_call_target="tpu_custom_call" | custom-call | tf_op jit(solution)/shard_map/pallas_call | solution.py:202
  38.9 3.4 %collective-permute-start.9 = (bf16[96,1024]{1,0:T(8,128)(2,1)S(1)}, bf16[96,1024]{1,0:T(8,128)(2,1)S(1)}, u32[]{:S(2)}, u32[]{:S(2)}) collective-permute-start(bf16[96,1024]{1,0:T(8,128)(2,1)S(1)} %get-tuple-element.34), channel_id=1, source_target_pairs={{0,12},{4,0},{8,4},{12,8},{1,13},{5,1},{9,5},{13,9},{2,14},{6,2},{... | collective-permute-start | bytes 589832 | tf_op jit(solution)/shard_map/ppermute | solution.py:215
  42.4 3.4 %collective-permute-start.19 = (bf16[96,1024]{1,0:T(8,128)(2,1)S(1)}, bf16[96,1024]{1,0:T(8,128)(2,1)S(1)}, u32[]{:S(2)}, u32[]{:S(2)}) collective-permute-start(bf16[96,1024]{1,0:T(8,128)(2,1)S(1)} %add_convert_fusion), channel_id=1, source_target_pairs={{0,12},{4,0},{8,4},{12,8},{1,13},{5,1},{9,5},{13,9},{2,14},{6,2},{... | collective-permute-start | bytes 589832 | tf_op jit(solution)/shard_map/ppermute | solution.py:215
  45.8 0.0 collective-permute-done.15
  45.9 4.2 %collective-permute-start.16 = (bf16[96,1024]{1,0:T(8,128)(2,1)S(1)}, bf16[96,1024]{1,0:T(8,128)(2,1)S(1)}, u32[]{:S(2)}, u32[]{:S(2)}) collective-permute-start(bf16[96,1024]{1,0:T(8,128)(2,1)S(1)} %add_convert_fusion.1), channel_id=1, source_target_pairs={{0,12},{4,0},{8,4},{12,8},{1,13},{5,1},{9,5},{13,9},{2,14},{6,2},{... | collective-permute-start | bytes 589832 | tf_op jit(solution)/shard_map/ppermute | solution.py:215
  50.1 0.0 collective-permute-done.12
  50.1 4.2 %collective-permute-start.13 = (bf16[96,1024]{1,0:T(8,128)(2,1)S(1)}, bf16[96,1024]{1,0:T(8,128)(2,1)S(1)}, u32[]{:S(2)}, u32[]{:S(2)}) collective-permute-start(bf16[96,1024]{1,0:T(8,128)(2,1)S(1)} %add_convert_fusion.2), channel_id=1, source_target_pairs={{0,12},{4,0},{8,4},{12,8},{1,13},{5,1},{9,5},{13,9},{2,14},{6,2},{... | collective-permute-start | bytes 589832 | tf_op jit(solution)/shard_map/ppermute | solution.py:215
  54.3 0.0 collective-permute-done.9
  54.3 4.2 %collective-permute-start.10 = (bf16[96,1024]{1,0:T(8,128)(2,1)S(1)}, bf16[96,1024]{1,0:T(8,128)(2,1)S(1)}, u32[]{:S(2)}, u32[]{:S(2)}) collective-permute-start(bf16[96,1024]{1,0:T(8,128)(2,1)S(1)} %add_convert_fusion.3), channel_id=1, source_target_pairs={{0,12},{4,0},{8,4},{12,8},{1,13},{5,1},{9,5},{13,9},{2,14},{6,2},{... | collective-permute-start | bytes 589832 | tf_op jit(solution)/shard_map/ppermute | solution.py:215
  58.5 0.0 collective-permute-done.19.arrived_ref
  58.5 0.8 %shard_map.67.refs_0_ = bf16[96,4096]{1,0:T(8,128)(2,1)} custom-call(bf16[96,1024]{1,0:T(8,128)(2,1)S(1)} %collective-permute-done.19.arrived_ref, f32[192,1024]{1,0:T(8,128)S(1)} %get-tuple-element.42.kept_ref), custom_call_target="tpu_custom_call" | custom-call | tf_op jit(solution)/shard_map/pallas_call | solution.py:337
  59.2 3.3 %collective-permute-done.16.arrived_ref = bf16[96,1024]{1,0:T(8,128)(2,1)S(1)} collective-permute-done((bf16[96,1024]{1,0:T(8,128)(2,1)S(1)}, bf16[96,1024]{1,0:T(8,128)(2,1)S(1)}, u32[]{:S(2)}, u32[]{:S(2)}) %collective-permute-start.16) | collective-permute-done | bytes 196640 | tf_op jit(solution)/shard_map/ppermute | solution.py:215
  62.5 0.8 %shard_map.68.refs_0_ = bf16[96,4096]{1,0:T(8,128)(2,1)} custom-call(bf16[96,1024]{1,0:T(8,128)(2,1)S(1)} %collective-permute-done.16.arrived_ref, f32[192,1024]{1,0:T(8,128)S(1)} %get-tuple-element.39.kept_ref, bf16[96,4096]{1,0:T(8,128)(2,1)} %shard_map.67.refs_0_), custom_call_target="tpu_custom_call", output_to_operand_aliasing={{}: (2, {})} | custom-call | tf_op jit(solution)/shard_map/pallas_call | solution.py:337
  63.3 3.4 %collective-permute-done.13.arrived_ref = bf16[96,1024]{1,0:T(8,128)(2,1)S(1)} collective-permute-done((bf16[96,1024]{1,0:T(8,128)(2,1)S(1)}, bf16[96,1024]{1,0:T(8,128)(2,1)S(1)}, u32[]{:S(2)}, u32[]{:S(2)}) %collective-permute-start.13) | collective-permute-done | bytes 196640 | tf_op jit(solution)/shard_map/ppermute | solution.py:215
  66.7 0.8 %shard_map.69.refs_0_ = bf16[96,4096]{1,0:T(8,128)(2,1)} custom-call(bf16[96,1024]{1,0:T(8,128)(2,1)S(1)} %collective-permute-done.13.arrived_ref, f32[192,1024]{1,0:T(8,128)S(1)} %get-tuple-element.37.kept_ref, bf16[96,4096]{1,0:T(8,128)(2,1)} %shard_map.68.refs_0_), custom_call_target="tpu_custom_call", output_to_operand_aliasing={{}: (2, {})} | custom-call | tf_op jit(solution)/shard_map/pallas_call | solution.py:337
  67.5 2.8 %collective-permute-done.10.arrived_ref = bf16[96,1024]{1,0:T(8,128)(2,1)S(1)} collective-permute-done((bf16[96,1024]{1,0:T(8,128)(2,1)S(1)}, bf16[96,1024]{1,0:T(8,128)(2,1)S(1)}, u32[]{:S(2)}, u32[]{:S(2)}) %collective-permute-start.10) | collective-permute-done | bytes 196640 | tf_op jit(solution)/shard_map/ppermute | solution.py:215
  70.3 0.8 %shard_map.70 = bf16[96,4096]{1,0:T(8,128)(2,1)} custom-call(bf16[96,1024]{1,0:T(8,128)(2,1)S(1)} %collective-permute-done.10.arrived_ref, f32[192,1024]{1,0:T(8,128)S(1)} %get-tuple-element.35.kept_ref, bf16[96,4096]{1,0:T(8,128)(2,1)} %shard_map.69.refs_0_), custom_call_target="tpu_custom_call", output_to_operand_aliasing={{}: (2, {})} | custom-call | tf_op jit(solution)/shard_map/pallas_call | solution.py:337
  (27 shorter events, 0.3 us)
Async XLA Ops:
  0.0 14.1 %slice-start = ((s8[8388608]{0:T(1024)(128)(4,1)}), s8[4194304]{0:T(1024)(128)(4,1)S(1)}, s32[]{:S(2)}) async-start(s8[8388608]{0:T(1024)(128)(4,1)} %bitcast.1), calls=%async_computation | async-start | bytes 8388608
  0.0 1.2 %copy-start.3 = (f32[64,32,32]{0,2,1:T(8,128)S(1)}, f32[64,32,32]{0,2,1:T(8,128)}, u32[]{:S(2)}) copy-start(f32[64,32,32]{0,2,1:T(8,128)} %param.5) | copy-start | bytes 786436
  1.2 7.0 %copy-start = (f32[9,64,64]{2,1,0:T(8,128)S(1)}, f32[9,64,64]{2,1,0:T(8,128)}, u32[]{:S(2)}) copy-start(f32[9,64,64]{2,1,0:T(8,128)} %first_ref.1) | copy-start | bytes 442372
  1.2 7.0 %copy-start.1 = (f32[9,64,64]{2,1,0:T(8,128)S(1)}, f32[9,64,64]{2,1,0:T(8,128)}, u32[]{:S(2)}) copy-start(f32[9,64,64]{2,1,0:T(8,128)} %second_ref.1) | copy-start | bytes 442372
  1.2 7.0 %copy-start.2 = (bf16[256,384]{1,0:T(8,128)(2,1)S(1)}, bf16[256,384]{1,0:T(8,128)(2,1)}, u32[]{:S(2)}) copy-start(bf16[256,384]{1,0:T(8,128)(2,1)} %embed_ref.1) | copy-start | bytes 589828
  1.2 12.9 %slice-start.1 = ((s8[8388608]{0:T(1024)(128)(4,1)}), s8[4194304]{0:T(1024)(128)(4,1)S(1)}, s32[]{:S(2)}) async-start(s8[8388608]{0:T(1024)(128)(4,1)} %bitcast.1), calls=%async_computation.1 | async-start | bytes 8388608
  1.3 7.4 %collective-permute-start.1 = (bf16[16,32,128]{2,1,0:T(8,128)(2,1)S(1)}, bf16[16,32,128]{2,1,0:T(8,128)(2,1)S(1)}, u32[]{:S(2)}, u32[]{:S(2)}) collective-permute-start(bf16[16,32,128]{2,1,0:T(8,128)(2,1)S(1)} %get-tuple-element.24.refs_0_), channel_id=1, source_target_pairs={{0,2},{2,0},{1,3},{3,1},{4,6},{6,4},{5,7},{7,5},{8,10},{10,8},{9,1... | collective-permute-start | bytes 393224 | tf_op jit(solution)/shard_map/ppermute | solution.py:215
  4.3 5.4 %collective-permute-start.3 = (bf16[1,32,128]{2,1,0:T(8,128)(2,1)S(1)}, bf16[1,32,128]{2,1,0:T(8,128)(2,1)S(1)}, u32[]{:S(2)}, u32[]{:S(2)}) collective-permute-start(bf16[1,32,128]{2,1,0:T(8,128)(2,1)S(1)} %get-tuple-element.25), channel_id=1, source_target_pairs={{0,4},{4,8},{8,12},{12,0},{1,5},{5,9},{9,13},{13,1},{2,6},{6,10},{... | collective-permute-start | bytes 24584 | tf_op jit(solution)/shard_map/ppermute | solution.py:215
  5.9 5.8 %collective-permute-start = (bf16[16,32,128]{2,1,0:T(8,128)(2,1)S(1)}, bf16[16,32,128]{2,1,0:T(8,128)(2,1)S(1)}, u32[]{:S(2)}, u32[]{:S(2)}) collective-permute-start(bf16[16,32,128]{2,1,0:T(8,128)(2,1)S(1)} %get-tuple-element.24.refs_0_), channel_id=1, source_target_pairs={{0,1},{1,0},{2,3},{3,2},{4,5},{5,4},{6,7},{7,6},{8,9},{9,8},{10,11... | collective-permute-start | bytes 393224 | tf_op jit(solution)/shard_map/ppermute | solution.py:215
  5.9 3.9 %collective-permute-start.4 = (bf16[1,32,128]{2,1,0:T(8,128)(2,1)S(1)}, bf16[1,32,128]{2,1,0:T(8,128)(2,1)S(1)}, u32[]{:S(2)}, u32[]{:S(2)}) collective-permute-start(bf16[1,32,128]{2,1,0:T(8,128)(2,1)S(1)} %get-tuple-element.26), channel_id=1, source_target_pairs={{0,12},{4,0},{8,4},{12,8},{1,13},{5,1},{9,5},{13,9},{2,14},{6,2},{... | collective-permute-start | bytes 24584 | tf_op jit(solution)/shard_map/ppermute | solution.py:215
  8.8 3.0 %collective-permute-start.2 = (bf16[16,32,128]{2,1,0:T(8,128)(2,1)S(1)}, bf16[16,32,128]{2,1,0:T(8,128)(2,1)S(1)}, u32[]{:S(2)}, u32[]{:S(2)}) collective-permute-start(bf16[16,32,128]{2,1,0:T(8,128)(2,1)S(1)} %collective-permute-done.1.refs_2_), channel_id=1, source_target_pairs={{0,1},{1,0},{2,3},{3,2},{4,5},{5,4},{6,7},{7,6},{8,9},{9,8},{10,11... | collective-permute-start | bytes 393224 | tf_op jit(solution)/shard_map/ppermute | solution.py:215
  9.8 4.3 %collective-permute-start.5 = (bf16[2,32,128]{2,1,0:T(8,128)(2,1)S(1)}, bf16[2,32,128]{2,1,0:T(8,128)(2,1)S(1)}, u32[]{:S(2)}, u32[]{:S(2)}) collective-permute-start(bf16[2,32,128]{2,1,0:T(8,128)(2,1)S(1)} %constant_dynamic-update-slice_fusion.refs_0_), channel_id=1, source_target_pairs={{0,1},{1,0},{2,3},{3,2},{4,5},{5,4},{6,7},{7,6},{8,9},{9,8},{10,11... | collective-permute-start | bytes 49160 | tf_op jit(solution)/shard_map/ppermute | solution.py:234
  9.9 4.2 %collective-permute-start.6 = (bf16[2,32,128]{2,1,0:T(8,128)(2,1)S(1)}, bf16[2,32,128]{2,1,0:T(8,128)(2,1)S(1)}, u32[]{:S(2)}, u32[]{:S(2)}) collective-permute-start(bf16[2,32,128]{2,1,0:T(8,128)(2,1)S(1)} %constant_dynamic-update-slice_fusion.refs_0_), channel_id=1, source_target_pairs={{0,2},{1,3},{2,0},{3,1},{4,6},{5,7},{6,4},{7,5},{8,10},{9,11},{10,... | collective-permute-start | bytes 49160 | tf_op jit(solution)/shard_map/ppermute | solution.py:234
  10.2 3.8 %collective-permute-start.7 = (bf16[2,32,128]{2,1,0:T(8,128)(2,1)S(1)}, bf16[2,32,128]{2,1,0:T(8,128)(2,1)S(1)}, u32[]{:S(2)}, u32[]{:S(2)}) collective-permute-start(bf16[2,32,128]{2,1,0:T(8,128)(2,1)S(1)} %constant_dynamic-update-slice_fusion.refs_0_), channel_id=1, source_target_pairs={{0,3},{1,2},{2,1},{3,0},{4,7},{5,6},{6,5},{7,4},{8,11},{9,10},{10,... | collective-permute-start | bytes 49160 | tf_op jit(solution)/shard_map/ppermute | solution.py:234
  15.6 9.1 %collective-permute-start.17 = (bf16[96,1024]{1,0:T(8,128)(2,1)S(1)}, bf16[96,1024]{1,0:T(8,128)(2,1)S(1)}, u32[]{:S(2)}, u32[]{:S(2)}) collective-permute-start(bf16[96,1024]{1,0:T(8,128)(2,1)S(1)} %get-tuple-element.40), channel_id=1, source_target_pairs={{0,12},{4,0},{8,4},{12,8},{1,13},{5,1},{9,5},{13,9},{2,14},{6,2},{... | collective-permute-start | bytes 589832 | tf_op jit(solution)/shard_map/ppermute | solution.py:215
  19.8 9.9 %collective-permute-start.14 = (bf16[96,1024]{1,0:T(8,128)(2,1)S(1)}, bf16[96,1024]{1,0:T(8,128)(2,1)S(1)}, u32[]{:S(2)}, u32[]{:S(2)}) collective-permute-start(bf16[96,1024]{1,0:T(8,128)(2,1)S(1)} %shard_map.64), channel_id=1, source_target_pairs={{0,12},{4,0},{8,4},{12,8},{1,13},{5,1},{9,5},{13,9},{2,14},{6,2},{... | collective-permute-start | bytes 589832 | tf_op jit(solution)/shard_map/ppermute | solution.py:215
  20.4 13.6 %collective-permute-start.11 = (bf16[96,1024]{1,0:T(8,128)(2,1)S(1)}, bf16[96,1024]{1,0:T(8,128)(2,1)S(1)}, u32[]{:S(2)}, u32[]{:S(2)}) collective-permute-start(bf16[96,1024]{1,0:T(8,128)(2,1)S(1)} %shard_map.62), channel_id=1, source_target_pairs={{0,12},{4,0},{8,4},{12,8},{1,13},{5,1},{9,5},{13,9},{2,14},{6,2},{... | collective-permute-start | bytes 589832 | tf_op jit(solution)/shard_map/ppermute | solution.py:215
  21.3 16.8 %collective-permute-start.8 = (bf16[96,1024]{1,0:T(8,128)(2,1)S(1)}, bf16[96,1024]{1,0:T(8,128)(2,1)S(1)}, u32[]{:S(2)}, u32[]{:S(2)}) collective-permute-start(bf16[96,1024]{1,0:T(8,128)(2,1)S(1)} %shard_map.60), channel_id=1, source_target_pairs={{0,12},{4,0},{8,4},{12,8},{1,13},{5,1},{9,5},{13,9},{2,14},{6,2},{... | collective-permute-start | bytes 589832 | tf_op jit(solution)/shard_map/ppermute | solution.py:215
  25.4 17.0 %collective-permute-start.18 = (bf16[96,1024]{1,0:T(8,128)(2,1)S(1)}, bf16[96,1024]{1,0:T(8,128)(2,1)S(1)}, u32[]{:S(2)}, u32[]{:S(2)}) collective-permute-start(bf16[96,1024]{1,0:T(8,128)(2,1)S(1)} %get-tuple-element.41), channel_id=1, source_target_pairs={{0,12},{4,0},{8,4},{12,8},{1,13},{5,1},{9,5},{13,9},{2,14},{6,2},{... | collective-permute-start | bytes 589832 | tf_op jit(solution)/shard_map/ppermute | solution.py:215
  30.5 15.3 %collective-permute-start.15 = (bf16[96,1024]{1,0:T(8,128)(2,1)S(1)}, bf16[96,1024]{1,0:T(8,128)(2,1)S(1)}, u32[]{:S(2)}, u32[]{:S(2)}) collective-permute-start(bf16[96,1024]{1,0:T(8,128)(2,1)S(1)} %get-tuple-element.38), channel_id=1, source_target_pairs={{0,12},{4,0},{8,4},{12,8},{1,13},{5,1},{9,5},{13,9},{2,14},{6,2},{... | collective-permute-start | bytes 589832 | tf_op jit(solution)/shard_map/ppermute | solution.py:215
  34.7 15.3 %collective-permute-start.12 = (bf16[96,1024]{1,0:T(8,128)(2,1)S(1)}, bf16[96,1024]{1,0:T(8,128)(2,1)S(1)}, u32[]{:S(2)}, u32[]{:S(2)}) collective-permute-start(bf16[96,1024]{1,0:T(8,128)(2,1)S(1)} %get-tuple-element.36), channel_id=1, source_target_pairs={{0,12},{4,0},{8,4},{12,8},{1,13},{5,1},{9,5},{13,9},{2,14},{6,2},{... | collective-permute-start | bytes 589832 | tf_op jit(solution)/shard_map/ppermute | solution.py:215
  38.9 15.3 %collective-permute-start.9 = (bf16[96,1024]{1,0:T(8,128)(2,1)S(1)}, bf16[96,1024]{1,0:T(8,128)(2,1)S(1)}, u32[]{:S(2)}, u32[]{:S(2)}) collective-permute-start(bf16[96,1024]{1,0:T(8,128)(2,1)S(1)} %get-tuple-element.34), channel_id=1, source_target_pairs={{0,12},{4,0},{8,4},{12,8},{1,13},{5,1},{9,5},{13,9},{2,14},{6,2},{... | collective-permute-start | bytes 589832 | tf_op jit(solution)/shard_map/ppermute | solution.py:215
  42.4 16.1 %collective-permute-start.19 = (bf16[96,1024]{1,0:T(8,128)(2,1)S(1)}, bf16[96,1024]{1,0:T(8,128)(2,1)S(1)}, u32[]{:S(2)}, u32[]{:S(2)}) collective-permute-start(bf16[96,1024]{1,0:T(8,128)(2,1)S(1)} %add_convert_fusion), channel_id=1, source_target_pairs={{0,12},{4,0},{8,4},{12,8},{1,13},{5,1},{9,5},{13,9},{2,14},{6,2},{... | collective-permute-start | bytes 589832 | tf_op jit(solution)/shard_map/ppermute | solution.py:215
  45.9 16.6 %collective-permute-start.16 = (bf16[96,1024]{1,0:T(8,128)(2,1)S(1)}, bf16[96,1024]{1,0:T(8,128)(2,1)S(1)}, u32[]{:S(2)}, u32[]{:S(2)}) collective-permute-start(bf16[96,1024]{1,0:T(8,128)(2,1)S(1)} %add_convert_fusion.1), channel_id=1, source_target_pairs={{0,12},{4,0},{8,4},{12,8},{1,13},{5,1},{9,5},{13,9},{2,14},{6,2},{... | collective-permute-start | bytes 589832 | tf_op jit(solution)/shard_map/ppermute | solution.py:215
  50.1 16.6 %collective-permute-start.13 = (bf16[96,1024]{1,0:T(8,128)(2,1)S(1)}, bf16[96,1024]{1,0:T(8,128)(2,1)S(1)}, u32[]{:S(2)}, u32[]{:S(2)}) collective-permute-start(bf16[96,1024]{1,0:T(8,128)(2,1)S(1)} %add_convert_fusion.2), channel_id=1, source_target_pairs={{0,12},{4,0},{8,4},{12,8},{1,13},{5,1},{9,5},{13,9},{2,14},{6,2},{... | collective-permute-start | bytes 589832 | tf_op jit(solution)/shard_map/ppermute | solution.py:215
  54.3 16.0 %collective-permute-start.10 = (bf16[96,1024]{1,0:T(8,128)(2,1)S(1)}, bf16[96,1024]{1,0:T(8,128)(2,1)S(1)}, u32[]{:S(2)}, u32[]{:S(2)}) collective-permute-start(bf16[96,1024]{1,0:T(8,128)(2,1)S(1)} %add_convert_fusion.3), channel_id=1, source_target_pairs={{0,12},{4,0},{8,4},{12,8},{1,13},{5,1},{9,5},{13,9},{2,14},{6,2},{... | collective-permute-start | bytes 589832 | tf_op jit(solution)/shard_map/ppermute | solution.py:215
